TPU v7x, 32 devices: a whole 2x2x4 slice. The times are simulated.
32 devices in a mesh: grp: 2 (over x), tpl: 16 (over z, y, core).
Axes of the slice: x: 2, y: 2, z: 4, core: 2. Of those that a mesh axis runs over, the one named last changes fastest.
Arguments:
- strain_slots: bfloat16 [32, 3, 2, 262144], P(('grp', 'tpl')), parts along dimension 0, may hold values from -6 to 6
- templates: bfloat16 [32, 2, 262144], P(None, None, 'tpl'), may hold values from -6 to 6
- cutoffs: int32 [32], replicated, may hold values from 32768 to 262144
- lists: int32 [16, 2], replicated, may hold values from 0 to 31, as said below
- owner: int32 [2], P('grp'), parts along dimension 0, may hold values from 0 to 15
- slides: int32 [6], P('grp'), parts along dimension 0, may hold values from 0 to 262143
Outputs:
- peaks: float32 [64], P(('grp', 'tpl')), parts along dimension 0
- norms: float32 [64], P(('grp', 'tpl')), parts along dimension 0
There are 2 independent parts, one for each index of `grp`. A program takes and returns all parts, laid end to end along the dimension named above; an argument that names none is the same for every part. Nothing has to cross between parts.
Inputs may be any that keep to these rules, and one draw needn't show every extreme that they name: Every template appears once in lists; list positions in row-major order run through the templates by falling cutoffs. One template has cutoff 262144, one has 32768.
All inputs are finite; a program needn't handle non-finite values.
Results may differ from a plain program's by a relative error of at most 0.0021.
Values may be sent and summed in bfloat16 or wider, within the bound.
No kernel may reach another device: no remote copies, remote signals or barrier semaphores. Data moves between devices by JAX's collectives and lax.ppermute only.
A program may use at most 128 MiB of HBM per device.

v0:
```python
import jax
import jax.numpy as jnp
from jax import lax
from jax.sharding import PartitionSpec as P

DET = 3
ROWS = 512
COLS = 512
BLOCK_ROWS = 64


two_pi = 6.283185307179586
eps_norm = 1e-06


def spread(block, axis, owner):
    block = jnp.where(lax.axis_index(axis) == owner, block, jnp.zeros_like(block))
    return lax.psum(block, axis)


def turn_table(left_ids, right_ids, period):
    product_idx = left_ids[:, None] * right_ids[None, :] % period
    angles = product_idx.astype(jnp.float32) * (two_pi / period)
    return (jnp.cos(angles), jnp.sin(angles))


def slide_phases(slides):
    total = ROWS * COLS
    bin_ids = jnp.arange(total, dtype=jnp.int32)
    row_ids = bin_ids // COLS
    col_ids = bin_ids % COLS
    stride = COLS * slides % total
    turns = (
        row_ids[None, :] * stride[:, None] % total + col_ids[None, :] * slides[:, None] % total
    ) % total
    angles = turns.astype(jnp.float32) * (two_pi / total)
    return (jnp.cos(angles), jnp.sin(angles))


def body(strain_slots, templates, cutoffs, lists, owner, slides):
    total = ROWS * COLS
    block_count_all = ROWS // BLOCK_ROWS
    devices = lax.axis_size("tpl")
    own_index = lax.axis_index("tpl")
    per_device = lists.shape[1]
    strain = spread(strain_slots[0], "tpl", owner[0])
    flat_list = lists.reshape(-1)
    device_ids = jnp.arange(devices, dtype=jnp.int32)[:, None]
    slot_ids = jnp.arange(per_device, dtype=jnp.int32)[None, :]
    positions = device_ids * per_device + slot_ids
    chosen = flat_list[positions]
    picked = templates[chosen.reshape(-1)]
    picked = picked.reshape(devices, per_device, 2, templates.shape[2])
    arrived = lax.all_to_all(picked, "tpl", split_axis=0, concat_axis=3, tiled=True)[0]
    own_ids = lax.dynamic_index_in_dim(chosen, own_index, 0, keepdims=False)
    cutoff_bins = cutoffs[own_ids]
    row_ids = jnp.arange(ROWS, dtype=jnp.int32)
    col_ids = jnp.arange(COLS, dtype=jnp.int32)
    row_cos, row_sin = turn_table(row_ids, row_ids, ROWS)
    cos_blocks = row_cos.reshape(ROWS, block_count_all, BLOCK_ROWS).transpose(1, 0, 2)
    sin_blocks = row_sin.reshape(ROWS, block_count_all, BLOCK_ROWS).transpose(1, 0, 2)
    row_blocks = jnp.concatenate(
        [
            jnp.concatenate([cos_blocks, -sin_blocks], 2),
            jnp.concatenate([sin_blocks, cos_blocks], 2),
        ],
        1,
    ).astype(jnp.bfloat16)
    twiddle_cos, twiddle_sin = turn_table(row_ids, col_ids, total)
    col_cos, col_sin = turn_table(col_ids, col_ids, COLS)
    col_table = jnp.concatenate(
        [jnp.concatenate([col_cos, col_sin], 1), jnp.concatenate([-col_sin, col_cos], 1)], 0
    ).astype(jnp.bfloat16)
    phase_cos, phase_sin = slide_phases(slides)
    data_re = strain[:, 0].astype(jnp.float32)
    data_im = strain[:, 1].astype(jnp.float32)

    def filter_one(packed):
        waveform, cutoff = packed
        inside = jnp.arange(total, dtype=jnp.int32) < cutoff
        wave_re = waveform[0].astype(jnp.float32)
        wave_im = waveform[1].astype(jnp.float32)
        real_part = data_re * wave_re + data_im * wave_im
        imag_part = data_im * wave_re - data_re * wave_im
        prod_re = jnp.where(inside, real_part * phase_cos - imag_part * phase_sin, 0.0)
        prod_im = jnp.where(inside, real_part * phase_sin + imag_part * phase_cos, 0.0)
        stacked = jnp.concatenate(
            [
                prod_re.reshape(DET, block_count_all, BLOCK_ROWS, COLS),
                prod_im.reshape(DET, block_count_all, BLOCK_ROWS, COLS),
            ],
            2,
        ).astype(jnp.bfloat16)
        section_one = jnp.einsum(
            "bai,dbic->dac", row_blocks, stacked, preferred_element_type=jnp.float32
        )
        first_re = section_one[:, :ROWS]
        first_im = section_one[:, ROWS:]
        twisted = jnp.concatenate(
            [
                first_re * twiddle_cos - first_im * twiddle_sin,
                first_re * twiddle_sin + first_im * twiddle_cos,
            ],
            2,
        ).astype(jnp.bfloat16)
        series = jnp.einsum("dab,bc->dac", twisted, col_table, preferred_element_type=jnp.float32)
        squares = jnp.sum(series * series, axis=0)
        power_sum = squares[:, :COLS] + squares[:, COLS:]
        sigmasq = jnp.sum(jnp.where(inside, wave_re * wave_re + wave_im * wave_im, 0.0))
        return (jnp.max(power_sum) / (2.0 * (sigmasq + eps_norm)), sigmasq / total)

    peaks, norms = lax.map(filter_one, (arrived, cutoff_bins))
    return (peaks, norms)


def solution(mesh):
    in_specs = (
        P(("grp", "tpl"), None, None, None),
        P(None, None, "tpl"),
        P(),
        P(),
        P("grp"),
        P("grp"),
    )
    out_specs = (P(("grp", "tpl")), P(("grp", "tpl")))
    return jax.shard_map(body, mesh=mesh, in_specs=in_specs, out_specs=out_specs, check_vma=False)
```

profile of v0, /device:TPU:0, one launch (start us, length us, event | category | flops | bytes accessed | tf_op | source)
XLA Modules:
  0.0 477.4 jit_solution(1903081071991389454)
XLA Ops:
  8.0 10.3 %fusion.41 = bf16[3,2,262144]{2,0,1:T(4,128)(2,1)} fusion(bf16[1,3,2,262144]{3,2,1,0:T(2,128)(2,1)} %param.8, pred[]{:T(512)S(6)} %eq.15), kind=kLoop, calls=%fused_computation.69 | loop fusion | flops 1572864 | bytes 6291457 | tf_op jit(solution)/shard_map/jit(_where)/select_n | solution.py:17
  19.9 6.1 %gather_fusion.2 = bf16[32,2,16384]{2,1,0:T(2,128)(2,1)} fusion(bf16[32,2,16384]{2,1,0:T(2,128)(2,1)S(1)} %copy-done, s32[1024]{0:T(1024)S(1)} %pad_clamp_fusion), kind=kCustom, calls=%fused_computation.2 | custom fusion | bytes 4194432 | tf_op jit(solution)/shard_map/gather | solution.py:52
  26.0 7.9 %all-to-all-start = ((bf16[16,2,2,16384]{3,2,1,0:T(2,128)(2,1)}), bf16[16,2,2,16384]{3,2,1,0:T(2,128)(2,1)}, u32[]{:S(2)}, u32[]{:S(2)}) async-start(bf16[16,2,2,16384]{3,2,1,0:T(2,128)(2,1)} %bitcast.96), calls=%async_computation | async-start | bytes 4194304 | tf_op jit(solution)/shard_map/all_to_all | solution.py:54
  33.9 1.5 fusion.49
  36.2 4.0 fusion.66
  40.2 4.3 negate_convert_fusion.1
  44.5 8.7 %negate_convert_fusion = (bf16[8,512,64]{2,1,0:T(8,128)(2,1)S(1)}, bf16[8,512,64]{2,1,0:T(8,128)(2,1)S(1)}, bf16[8,512,64]{2,1,0:T(8,128)(2,1)S(1)}) fusion(s32[8,64]{1,0:T(8,128)S(1)} %multiply_add_fusion.2), kind=kLoop, calls=%fused_computation.82 | loop fusion | flops 4718592 | bytes 1574912 | tf_op jit(solution)/shard_map/convert.19
  53.2 2.5 maximum_maximum_fusion
  55.7 1.6 maximum_maximum_fusion.1
  57.3 115.2 %all-reduce.2.cloned.1.call-done = bf16[3,2,262144]{2,0,1:T(4,128)(2,1)} async-done(((bf16[3,2,262144]{2,0,1:T(4,128)(2,1)}), bf16[3,2,262144]{2,0,1:T(4,128)(2,1)}) %all-reduce.2.cloned.1.call-update) | async-done | bytes 3145744 | tf_op jit(solution)/shard_map/psum | solution.py:18
  172.5 5.0 %fusion.45 = (f32[3,262144]{1,0:T(4,128)}, f32[3,262144]{1,0:T(4,128)}) fusion(bf16[3,2,262144]{2,0,1:T(4,128)(2,1)} %all-reduce.2.cloned.1.call-done), kind=kLoop, calls=%fused_computation.77 | loop fusion | flops 1572864 | bytes 9437184 | tf_op jit(solution)/shard_map/convert_element_type | solution.py:76
  177.5 2.7 copy.68
  180.2 2.5 squeeze.23
  182.8 286.2 %while.15 = (s32[]{:T(128)}, f32[2]{0:T(128)S(1)}, f32[2]{0:T(128)S(1)}, s32[2]{0:T(128)S(1)}, f32[3,262144]{1,0:T(4,128)}, /*index=5*/bf16[2,2,262144]{2,1,0:T(...) while((s32[]{:T(128)}, f32[2]{0:T(128)S(1)}, ...), condition=%wide.region_5.6_spmd.clone.clone.clone, body=%wide.region_1.5_spmd.clone.clone.clone.sunk | while | flops 6514016256 | bytes 146276784 | solution.py:112
  202.2 16.5 %fusion.84 = (f32[262144]{0:T(1024)}, f32[262144]{0:T(1024)S(1)}, f32[1,1,262144]{2,1,0:T(1,128)}) fusion(bf16[2,2,262144]{2,1,0:T(2,128)(2,1)} %get-tuple-element.387, s32[]{:T(128)} %get-tuple-element.363, s32[]{:T(128)S(6)} %add.959), kind=kLoop, calls=%fused_computation.62.clone.1 | loop fusion | flops 1310720 | bytes 4194312 | tf_op jit(solution)/shard_map/while/body/eval_jaxpr/convert_element_type | solution.py:81
  219.4 1.4 reshape.324
  220.8 1.9 copy.97
  224.4 42.2 %fusion.83 = (f32[3,262144]{1,0:T(4,128)S(1)}, f32[3,262144]{1,0:T(4,128)}) fusion(s32[3]{0:T(128)S(1)} %get-tuple-element.393, s32[262144]{0:T(1024)} %get-tuple-element.394, s32[3]{0:T(128)S(1)} %get-tuple-element.391, s32[262144]{0:T(1024)} %get-tuple-element.392), kind=kLoop, calls=%fused_computation.43.clone.1 | loop fusion | flops 29884416 | bytes 8388632 | tf_op jit(solution)/shard_map/sin | solution.py:37
  266.6 2.7 copy.88
  269.3 5.8 %copy.89 = f32[3,8,64,512]{2,3,1,0:T(8,128)} copy(f32[3,8,64,512]{3,2,1,0:T(8,128)} %bitcast.89) | data formatting | bytes 6291456 | tf_op jit(solution)/shard_map/reshape.31
  275.1 4.8 %copy.90 = f32[1,3,512,512]{3,2,1,0:T(8,128)} copy(f32[1,3,512,512]{3,1,2,0:T(4,128)} %bitcast.87) | data formatting | bytes 6291456 | tf_op jit(solution)/shard_map/while
  279.9 5.8 %copy.91 = f32[3,8,64,512]{2,3,1,0:T(8,128)} copy(f32[3,8,64,512]{3,2,1,0:T(8,128)} %bitcast.90) | data formatting | bytes 6291456 | tf_op jit(solution)/shard_map/reshape.26
  285.7 4.9 %copy.92 = f32[1,3,512,512]{3,2,1,0:T(8,128)} copy(f32[1,3,512,512]{3,1,2,0:T(4,128)} %bitcast.93) | data formatting | bytes 6291456 | tf_op jit(solution)/shard_map/while
  290.5 5.8 %copy.93 = f32[3,8,64,512]{2,3,1,0:T(8,128)} copy(f32[3,8,64,512]{3,2,1,0:T(8,128)} %bitcast.91) | data formatting | bytes 6291456 | tf_op jit(solution)/shard_map/reshape.23
  296.3 4.8 %copy.95 = f32[1,3,512,512]{3,2,1,0:T(8,128)} copy(f32[1,3,512,512]{3,1,2,0:T(4,128)} %bitcast.94) | data formatting | bytes 6291456 | tf_op jit(solution)/shard_map/while
  301.1 5.8 %copy.96 = f32[3,8,64,512]{2,3,1,0:T(8,128)} copy(f32[3,8,64,512]{3,2,1,0:T(8,128)} %bitcast.92) | data formatting | bytes 6291456 | tf_op jit(solution)/shard_map/reshape.20
  306.9 10.7 %select_convert_fusion.3 = (bf16[3,8,64,512]{2,3,1,0:T(8,128)(2,1)S(1)}, bf16[3,8,64,512]{2,3,1,0:T(8,128)(2,1)S(1)}) fusion(f32[3,8,64,512]{2,3,1,0:T(8,128)} %copy.89, f32[3,8,64,512]{2,3,1,0:T(8,128)} %copy.91, pred[8,64,512]{1,2,0:T(8,128)(4,1)S(1)} %add_compare_fusion.2, f32[3,8,64,512]{2,3,1,0:T(8,128)} %copy.93, f32[8,64,512]{1,2,0:T(8,128)S(1)} %copy.94, ...), kind=kLoop, calls=%fused_computation.22.clone.1 | loop fusion | flops 12582912 | bytes 18087936 | tf_op jit(solution)/shard_map/convert.4
  317.6 3.6 fusion.85
  321.3 4.1 fusion.86
  326.9 3.9 multiply_reduce_fusion.2
  331.8 1.6 select_reduce_fusion.2
  335.5 16.6 %fusion.84 = (f32[262144]{0:T(1024)}, f32[262144]{0:T(1024)S(1)}, f32[1,1,262144]{2,1,0:T(1,128)}) fusion(bf16[2,2,262144]{2,1,0:T(2,128)(2,1)} %get-tuple-element.387, s32[]{:T(128)} %get-tuple-element.363, s32[]{:T(128)S(6)} %add.959), kind=kLoop, calls=%fused_computation.62.clone.1 | loop fusion | flops 1310720 | bytes 4194312 | tf_op jit(solution)/shard_map/while/body/eval_jaxpr/convert_element_type | solution.py:81
  352.9 1.4 reshape.324
  354.3 1.9 copy.97
  357.8 42.2 %fusion.83 = (f32[3,262144]{1,0:T(4,128)S(1)}, f32[3,262144]{1,0:T(4,128)}) fusion(s32[3]{0:T(128)S(1)} %get-tuple-element.393, s32[262144]{0:T(1024)} %get-tuple-element.394, s32[3]{0:T(128)S(1)} %get-tuple-element.391, s32[262144]{0:T(1024)} %get-tuple-element.392), kind=kLoop, calls=%fused_computation.43.clone.1 | loop fusion | flops 29884416 | bytes 8388632 | tf_op jit(solution)/shard_map/sin | solution.py:37
  400.1 2.7 copy.88
  402.8 5.8 %copy.89 = f32[3,8,64,512]{2,3,1,0:T(8,128)} copy(f32[3,8,64,512]{3,2,1,0:T(8,128)} %bitcast.89) | data formatting | bytes 6291456 | tf_op jit(solution)/shard_map/reshape.31
  408.5 4.8 %copy.90 = f32[1,3,512,512]{3,2,1,0:T(8,128)} copy(f32[1,3,512,512]{3,1,2,0:T(4,128)} %bitcast.87) | data formatting | bytes 6291456 | tf_op jit(solution)/shard_map/while
  413.4 5.8 %copy.91 = f32[3,8,64,512]{2,3,1,0:T(8,128)} copy(f32[3,8,64,512]{3,2,1,0:T(8,128)} %bitcast.90) | data formatting | bytes 6291456 | tf_op jit(solution)/shard_map/reshape.26
  419.1 4.9 %copy.92 = f32[1,3,512,512]{3,2,1,0:T(8,128)} copy(f32[1,3,512,512]{3,1,2,0:T(4,128)} %bitcast.93) | data formatting | bytes 6291456 | tf_op jit(solution)/shard_map/while
  424.0 5.8 %copy.93 = f32[3,8,64,512]{2,3,1,0:T(8,128)} copy(f32[3,8,64,512]{3,2,1,0:T(8,128)} %bitcast.91) | data formatting | bytes 6291456 | tf_op jit(solution)/shard_map/reshape.23
  429.8 4.8 %copy.95 = f32[1,3,512,512]{3,2,1,0:T(8,128)} copy(f32[1,3,512,512]{3,1,2,0:T(4,128)} %bitcast.94) | data formatting | bytes 6291456 | tf_op jit(solution)/shard_map/while
  434.6 5.8 %copy.96 = f32[3,8,64,512]{2,3,1,0:T(8,128)} copy(f32[3,8,64,512]{3,2,1,0:T(8,128)} %bitcast.92) | data formatting | bytes 6291456 | tf_op jit(solution)/shard_map/reshape.20
  440.4 10.7 %select_convert_fusion.3 = (bf16[3,8,64,512]{2,3,1,0:T(8,128)(2,1)S(1)}, bf16[3,8,64,512]{2,3,1,0:T(8,128)(2,1)S(1)}) fusion(f32[3,8,64,512]{2,3,1,0:T(8,128)} %copy.89, f32[3,8,64,512]{2,3,1,0:T(8,128)} %copy.91, pred[8,64,512]{1,2,0:T(8,128)(4,1)S(1)} %add_compare_fusion.2, f32[3,8,64,512]{2,3,1,0:T(8,128)} %copy.93, f32[8,64,512]{1,2,0:T(8,128)S(1)} %copy.94, ...), kind=kLoop, calls=%fused_computation.22.clone.1 | loop fusion | flops 12582912 | bytes 18087936 | tf_op jit(solution)/shard_map/convert.4
  451.1 3.6 fusion.85
  454.7 4.1 fusion.86
  460.4 3.9 multiply_reduce_fusion.2
  465.2 1.6 select_reduce_fusion.2
  (62 shorter events, 14.0 us)
Async XLA Ops:
  7.2 12.7 %copy-start = (bf16[32,2,16384]{2,1,0:T(2,128)(2,1)S(1)}, bf16[32,2,16384]{2,1,0:T(2,128)(2,1)}, u32[]{:S(2)}) copy-start(bf16[32,2,16384]{2,1,0:T(2,128)(2,1)} %param.9) | copy-start | bytes 6291460
  7.2 165.3 %all-reduce.2.cloned.1.call-start = ((), (), s32[]{:S(2)}) async-start(), calls=%async_computation.1 | async-start | bytes 8388608 | tf_op jit(solution)/shard_map/psum | solution.py:18
  18.3 0.7 copy-start.7
  26.0 9.5 %copy-start.2 = (s32[32]{0:T(128)S(1)}, s32[32]{0:T(128)}, u32[]{:S(2)}) copy-start(s32[32]{0:T(128)} %param.10) | copy-start | bytes 388
  26.0 151.4 %all-to-all-start = ((bf16[16,2,2,16384]{3,2,1,0:T(2,128)(2,1)}), bf16[16,2,2,16384]{3,2,1,0:T(2,128)(2,1)}, u32[]{:S(2)}, u32[]{:S(2)}) async-start(bf16[16,2,2,16384]{3,2,1,0:T(2,128)(2,1)} %bitcast.96), calls=%async_computation | async-start | bytes 4194304 | tf_op jit(solution)/shard_map/all_to_all | solution.py:54
  55.7 1.6 copy-start.6
  306.9 10.7 %copy-start.5 = (bf16[8,1024,128]{2,1,0:T(8,128)(2,1)S(1)}, bf16[8,1024,128]{2,1,0:T(8,128)(2,1)}, u32[]{:S(2)}) copy-start(bf16[8,1024,128]{2,1,0:T(8,128)(2,1)} %get-tuple-element.389) | copy-start | bytes 6291460 | tf_op jit(solution)/shard_map/while
  325.3 1.6 copy-start.4
  326.9 4.8 %copy-start.3 = (f32[1,1,262144]{2,1,0:T(1,128)S(1)}, f32[1,1,262144]{2,1,0:T(1,128)}, u32[]{:S(2)}) copy-start(f32[1,1,262144]{2,1,0:T(1,128)} %get-tuple-element.343) | copy-start | bytes 3145732 | tf_op jit(solution)/shard_map/while
  440.4 10.7 %copy-start.5 = (bf16[8,1024,128]{2,1,0:T(8,128)(2,1)S(1)}, bf16[8,1024,128]{2,1,0:T(8,128)(2,1)}, u32[]{:S(2)}) copy-start(bf16[8,1024,128]{2,1,0:T(8,128)(2,1)} %get-tuple-element.389) | copy-start | bytes 6291460 | tf_op jit(solution)/shard_map/while
  458.8 1.6 copy-start.4
  460.4 4.8 %copy-start.3 = (f32[1,1,262144]{2,1,0:T(1,128)S(1)}, f32[1,1,262144]{2,1,0:T(1,128)}, u32[]{:S(2)}) copy-start(f32[1,1,262144]{2,1,0:T(1,128)} %get-tuple-element.343) | copy-start | bytes 3145732 | tf_op jit(solution)/shard_map/while
  469.0 0.5 copy-start.8
  469.0 0.5 copy-start.9
  469.0 1.6 copy-start.1
Sparse Core Ops, SparseCore 0:
  18.5 153.9 all-reduce.1
where the time goes:
time: 474 us; the launch traced here: 477 us
  other arithmetic  195 us (41%)
  waiting for transfers between devices  115 us (24%)
  local copies, waits for them, and re-layouts  106 us (22%)
  loops' own time  23.4 us (5%)
  matrix products  15.1 us (3%)
  between operations  14.9 us (3%)
  starting transfers between devices  7.94 us (2%)
    psum x1, waiting for transfers between devices, spread(): return lax.psum(block, axis)  115 us
    sin x2, other arithmetic, slide_phases(): return (jnp.cos(angles), jnp.sin(angles))  84.5 us
    another operation x8, local copies, waits for them, and re-layouts  46.1 us
    another operation x9, other arithmetic  40.9 us
    while x20, local copies, waits for them, and re-layouts  35.1 us
    convert_element_type x2, other arithmetic, filter_one(): wave_re = waveform[0].astype(jnp.float32)  33.1 us
    another operation x1, loops' own time, body(): peaks, norms = lax.map(filter_one, (arrived, cutoff_bins))  23.4 us
    select_n x1, other arithmetic, spread(): jnp.where(lax.axis_index(axis) == owner, block, jnp.zeros_like(block))  10.3 us
  transfers between devices with their start and end apart: 2, of which 1 were waited for; matrix products, arithmetic and copies ran while one was open for 7% of the time, Pallas kernels for 0%

commit v1 on v0

v1 whole, which is shorter than its diff:
```python
import functools

import jax
import jax.numpy as jnp
import numpy as np
from jax import lax
from jax.experimental import pallas as pl
from jax.experimental.pallas import tpu as pltpu
from jax.sharding import PartitionSpec as P

DET = 3
ROWS = 512
COLS = 512
COL_BLOCK = 256
ROW_BLOCK = 128


two_pi = 6.283185307179586
eps_norm = 1e-06


def turn_table(left_ids, right_ids, period):
    angles = (left_ids[:, None] * right_ids[None, :] % period).astype(np.float64) * (2 * np.pi / period)
    return np.cos(angles), np.sin(angles)


def tables():
    row_ids, col_ids = np.arange(ROWS), np.arange(COLS)
    row_cos, row_sin = turn_table(row_ids, row_ids, ROWS)
    row_table = np.block([[row_cos, -row_sin], [row_sin, row_cos]])
    col_cos, col_sin = turn_table(col_ids, col_ids, COLS)
    col_table = np.block([[col_cos, col_sin], [-col_sin, col_cos]])
    twiddle = np.stack(turn_table(row_ids, col_ids, ROWS * COLS))
    return (
        jnp.asarray(row_table, jnp.float32).astype(jnp.bfloat16),
        jnp.asarray(col_table, jnp.float32).astype(jnp.bfloat16),
        jnp.asarray(twiddle, jnp.float32),
    )


def spread(block, axis, owner):
    block = jnp.where(lax.axis_index(axis) == owner, block, jnp.zeros_like(block))
    return lax.psum(block, axis)


def slide_turns(slides):
    total = ROWS * COLS
    row_turns = (jnp.arange(ROWS, dtype=jnp.int32)[None, :] * (COLS * slides % total)[:, None]) % total
    col_turns = (jnp.arange(COLS, dtype=jnp.int32)[None, :] * slides[:, None]) % total
    row_angles = row_turns.astype(jnp.float32) * (two_pi / total)
    col_angles = col_turns.astype(jnp.float32) * (two_pi / total)
    rows = jnp.stack([jnp.cos(row_angles), jnp.sin(row_angles)], 1)[..., None]
    cols = jnp.stack([jnp.cos(col_angles), jnp.sin(col_angles)], 1)[:, :, None, :]
    return rows, cols


def filter_kernel(cut_ref, strain_ref, wave_ref, rphase_ref, cphase_ref, row_ref, col_ref, twiddle_ref,
                  peaks_ref, norms_ref, slid, stacked, twisted, power, sigma):
    det, tpl = pl.program_id(0), pl.program_id(1)
    cutoff = cut_ref[tpl]

    @pl.when(tpl == 0)
    def _():
        rc, rs = rphase_ref[0, 0], rphase_ref[0, 1]
        cc, cs = cphase_ref[0, 0], cphase_ref[0, 1]
        for at in range(0, ROWS, ROW_BLOCK):
            rows = slice(at, at + ROW_BLOCK)
            turn_re = rc[rows] * cc - rs[rows] * cs
            turn_im = rc[rows] * cs + rs[rows] * cc
            data_re = strain_ref[0, 0, rows, :].astype(jnp.float32)
            data_im = strain_ref[0, 1, rows, :].astype(jnp.float32)
            slid[0, rows, :] = data_re * turn_re - data_im * turn_im
            slid[1, rows, :] = data_re * turn_im + data_im * turn_re

    def masked(rows, cols):
        bins = (lax.broadcasted_iota(jnp.int32, (ROW_BLOCK, COL_BLOCK), 0) + rows.start) * COLS
        bins = bins + lax.broadcasted_iota(jnp.int32, (ROW_BLOCK, COL_BLOCK), 1) + cols.start
        inside = bins < cutoff
        wave_re = jnp.where(inside, wave_ref[0, 0, rows, cols].astype(jnp.float32), 0.0)
        wave_im = jnp.where(inside, wave_ref[0, 1, rows, cols].astype(jnp.float32), 0.0)
        return wave_re, wave_im

    @pl.when(det == 0)
    def _():
        total = jnp.zeros((8, COL_BLOCK), jnp.float32)
        for row_at in range(0, ROWS, ROW_BLOCK):
            for col_at in range(0, COLS, COL_BLOCK):
                wave_re, wave_im = masked(slice(row_at, row_at + ROW_BLOCK), slice(col_at, col_at + COL_BLOCK))
                squares = wave_re * wave_re + wave_im * wave_im
                total = total + jnp.sum(squares.reshape(-1, 8, COL_BLOCK), axis=0)
        sigma[tpl] = jnp.sum(total)

    for col_at in range(0, COLS, COL_BLOCK):
        cols = slice(col_at, col_at + COL_BLOCK)
        for row_at in range(0, ROWS, ROW_BLOCK):
            rows = slice(row_at, row_at + ROW_BLOCK)
            wave_re, wave_im = masked(rows, cols)
            data_re, data_im = slid[0, rows, cols], slid[1, rows, cols]
            stacked[rows, cols] = (data_re * wave_re + data_im * wave_im).astype(jnp.bfloat16)
            low = slice(ROWS + row_at, ROWS + row_at + ROW_BLOCK)
            stacked[low, cols] = (data_im * wave_re - data_re * wave_im).astype(jnp.bfloat16)
        for row_at in range(0, ROWS, ROW_BLOCK):
            rows = slice(row_at, row_at + ROW_BLOCK)
            low = slice(ROWS + row_at, ROWS + row_at + ROW_BLOCK)
            first_re = jnp.dot(row_ref[rows, :], stacked[:, cols], preferred_element_type=jnp.float32)
            first_im = jnp.dot(row_ref[low, :], stacked[:, cols], preferred_element_type=jnp.float32)
            turn_re, turn_im = twiddle_ref[0, rows, cols], twiddle_ref[1, rows, cols]
            twisted[rows, cols] = (first_re * turn_re - first_im * turn_im).astype(jnp.bfloat16)
            right = slice(COLS + col_at, COLS + col_at + COL_BLOCK)
            twisted[rows, right] = (first_re * turn_im + first_im * turn_re).astype(jnp.bfloat16)

    for row_at in range(0, ROWS, ROW_BLOCK):
        rows = slice(row_at, row_at + ROW_BLOCK)
        series = jnp.dot(twisted[rows, :], col_ref[...], preferred_element_type=jnp.float32)
        series_re, series_im = series[:, :COLS], series[:, COLS:]
        squares = series_re * series_re + series_im * series_im

        @pl.when(det == 0)
        def _():
            power[tpl, rows, :] = squares

        @pl.when(det > 0)
        def _():
            power[tpl, rows, :] += squares

    @pl.when(det == DET - 1)
    def _():
        largest = jnp.max(power[tpl])
        peaks_ref[tpl] = largest / (2.0 * (sigma[tpl] + eps_norm))
        norms_ref[tpl] = sigma[tpl] / (ROWS * COLS)


def filtered(strain, waves, cutoffs, slides):
    count = waves.shape[0]
    rows, cols = slide_turns(slides)
    row_table, col_table, twiddle = tables()
    whole = lambda *shape: pl.BlockSpec(shape, lambda det, tpl: (0,) * len(shape))
    return pl.pallas_call(
        filter_kernel,
        grid=(DET, count),
        out_shape=(jax.ShapeDtypeStruct((count,), jnp.float32),) * 2,
        in_specs=[
            pl.BlockSpec(memory_space=pltpu.SMEM),
            pl.BlockSpec((1, 2, ROWS, COLS), lambda det, tpl: (det, 0, 0, 0)),
            pl.BlockSpec((1, 2, ROWS, COLS), lambda det, tpl: (tpl, 0, 0, 0)),
            pl.BlockSpec((1, 2, ROWS, 1), lambda det, tpl: (det, 0, 0, 0)),
            pl.BlockSpec((1, 2, 1, COLS), lambda det, tpl: (det, 0, 0, 0)),
            whole(2 * ROWS, 2 * ROWS),
            whole(2 * COLS, 2 * COLS),
            whole(2, ROWS, COLS),
        ],
        out_specs=(pl.BlockSpec(memory_space=pltpu.SMEM),) * 2,
        scratch_shapes=[
            pltpu.VMEM((2, ROWS, COLS), jnp.float32),
            pltpu.VMEM((2 * ROWS, COLS), jnp.bfloat16),
            pltpu.VMEM((ROWS, 2 * COLS), jnp.bfloat16),
            pltpu.VMEM((count, ROWS, COLS), jnp.float32),
            pltpu.SMEM((count,), jnp.float32),
        ],
        compiler_params=pltpu.CompilerParams(vmem_limit_bytes=48 * 1024 * 1024),
    )(cutoffs, strain, waves, rows, cols, row_table, col_table, twiddle)


def body(strain_slots, templates, cutoffs, lists, owner, slides):
    devices = lax.axis_size("tpl")
    own_index = lax.axis_index("tpl")
    per_device = lists.shape[1]
    strain = spread(strain_slots[0], "tpl", owner[0])
    picked = templates[lists.reshape(-1)]
    picked = picked.reshape(devices, per_device, 2, templates.shape[2])
    arrived = lax.all_to_all(picked, "tpl", split_axis=0, concat_axis=3, tiled=True)[0]
    own_ids = lax.dynamic_index_in_dim(lists, own_index, 0, keepdims=False)
    return filtered(
        strain.reshape(DET, 2, ROWS, COLS),
        arrived.reshape(per_device, 2, ROWS, COLS),
        cutoffs[own_ids],
        slides,
    )


def solution(mesh):
    in_specs = (
        P(("grp", "tpl"), None, None, None),
        P(None, None, "tpl"),
        P(),
        P(),
        P("grp"),
        P("grp"),
    )
    out_specs = (P(("grp", "tpl")), P(("grp", "tpl")))
    return jax.shard_map(body, mesh=mesh, in_specs=in_specs, out_specs=out_specs, check_vma=False)
```

time: 474 us -> 202 us (0.43)
  other arithmetic: 195 us -> 4.78 us
  local copies, waits for them, and re-layouts: 106 us -> 29.6 us
  Pallas kernels: 0 us -> 27.3 us
  loops' own time: 23.4 us -> 0 us
  matrix products: 15.1 us -> 0 us
    sin x4 -> x0, other arithmetic: 92.7 us -> none  [the longest x2 84.5 us: slide_phases(): return (jnp.cos(angles), jnp.sin(angles))]
    another operation x8 -> x1, local copies, waits for them, and re-layouts: 46.1 us -> 4.27 us  [body(): arrived.reshape(per_device, 2, ROWS, COLS)]
    another operation x9 -> x1, other arithmetic: 40.9 us -> 0.02 us  [slide_turns(): jnp.stack([jnp.cos(col_angles), jnp.sin(col_angles)], 1)[:, :, None, :]]
    convert_element_type x3 -> x0, other arithmetic: 38.1 us -> none  [the longest x2 33.1 us: filter_one(): wave_re = waveform[0].astype(jnp.float32)]
    all_to_all x1, waiting for transfers between devices: 0.01 us -> 35.5 us  [body(): lax.all_to_all(picked, 'tpl', split_axis=0, concat_axis=3, tiled=True)[0]]
    while x20 -> x0, local copies, waits for them, and re-layouts: 35.1 us -> none
    psum x1, waiting for transfers between devices: 115 us -> 81.5 us  [spread(): return lax.psum(block, axis)]
    pallas_call x0 -> x1, Pallas kernels: none -> 27.3 us  [filtered(): pl.pallas_call(filter_kernel, grid=(DET, count), out_shape=(jax.ShapeDtyp...]
  transfers between devices with their start and end apart: 2 -> 2, of which waited for: 1 -> 2; matrix products, arithmetic and copies ran while one was open for 7% -> 11% of each run, Pallas kernels for 0% -> 0%
where the time goes in v1:
time: 202 us; the launch traced here: 201 us
  waiting for transfers between devices  117 us (58%)
  local copies, waits for them, and re-layouts  29.6 us (15%)
  Pallas kernels  27.3 us (14%)
  between operations  14.8 us (7%)
  starting transfers between devices  7.48 us (4%)
  other arithmetic  4.78 us (2%)
    psum x1, waiting for transfers between devices, spread(): return lax.psum(block, axis)  81.5 us
    all_to_all x1, waiting for transfers between devices, body(): lax.all_to_all(picked, 'tpl', split_axis=0, concat_axis=3, tiled=True)[0]  35.5 us
    pallas_call x1, Pallas kernels, filtered(): pl.pallas_call(filter_kernel, grid=(DET, count), out_shape=(jax.ShapeDtyp...  27.3 us
    all_to_all x1, starting transfers between devices, body(): lax.all_to_all(picked, 'tpl', split_axis=0, concat_axis=3, tiled=True)[0]  7.44 us
    unnamed x15, local copies, waits for them, and re-layouts  6.74 us
    gather x1, local copies, waits for them, and re-layouts, body(): picked = templates[lists.reshape(-1)]  6.13 us
    reshape x1, local copies, waits for them, and re-layouts, body(): strain.reshape(DET, 2, ROWS, COLS)  5.79 us
    another operation x1, local copies, waits for them, and re-layouts, body(): arrived.reshape(per_device, 2, ROWS, COLS)  4.27 us
  transfers between devices with their start and end apart: 2, of which 2 were waited for; matrix products, arithmetic and copies ran while one was open for 11% of the time, Pallas kernels for 0%

profile of v1, /device:TPU:0, one launch (start us, length us, event | category | flops | bytes accessed | tf_op | source)
XLA Modules:
  0.0 201.0 jit_solution(3014167581943154262)
XLA Ops:
  7.2 0.0 copy-start
  7.2 0.9 copy.17
  8.1 0.1 reshape.256
  8.2 0.6 copy-done
  8.8 6.1 %gather_fusion.1 = bf16[32,2,16384]{2,1,0:T(2,128)(2,1)} fusion(bf16[32,2,16384]{2,1,0:T(2,128)(2,1)S(1)} %copy-done, s32[1024]{0:T(1024)S(1)} %pad_clamp_fusion), kind=kCustom, calls=%fused_computation.1 | custom fusion | bytes 4194432 | tf_op jit(solution)/shard_map/gather | solution.py:169
  14.9 7.4 %all-to-all-start = ((bf16[16,2,2,16384]{3,2,1,0:T(2,128)(2,1)}), bf16[16,2,2,16384]{3,2,1,0:T(2,128)(2,1)}, u32[]{:S(2)}, u32[]{:S(2)}) async-start(bf16[16,2,2,16384]{3,2,1,0:T(2,128)(2,1)} %bitcast.16), calls=%async_computation | async-start | bytes 4194304 | tf_op jit(solution)/shard_map/all_to_all | solution.py:171
  22.4 0.0 all-reduce.2.cloned.1.call-start
  23.1 4.2 %broadcast_select_fusion = bf16[1,3,2,262144]{3,2,1,0:T(2,128)(2,1)} fusion(bf16[1,3,2,262144]{3,2,1,0:T(2,128)(2,1)} %param.9, pred[]{:T(512)S(6)} %eq.8), kind=kLoop, calls=%fused_computation.2 | loop fusion | flops 1572864 | bytes 6291457 | tf_op jit(solution)/shard_map/jit(_where)/select_n | solution.py:42
  27.2 5.8 %reshape.255 = bf16[3,2,512,512]{3,2,1,0:T(8,128)(2,1)} reshape(bf16[1,3,2,262144]{3,2,1,0:T(2,128)(2,1)} %broadcast_select_fusion) | data formatting | bytes 6291456 | tf_op jit(solution)/shard_map/reshape | solution.py:174
  33.0 0.0 copy-start.5
  33.0 0.0 copy-start.6
  33.0 0.0 copy-start.4
  33.0 0.0 all-reduce.2.cloned.1.call-update
  33.0 0.6 copy-done.5
  33.7 0.2 dynamic-slice_reduce_fusion
  33.9 0.0 copy-done.6
  33.9 0.3 fusion.9
  34.2 1.7 copy.19.rphase_ref
  35.9 0.3 fusion.7
  36.2 0.0 copy-done.4
  36.2 0.6 gather_fusion
  36.9 35.5 %all-to-all-done = bf16[16,2,2,16384]{3,2,1,0:T(2,128)(2,1)} async-done(((bf16[16,2,2,16384]{3,2,1,0:T(2,128)(2,1)}), bf16[16,2,2,16384]{3,2,1,0:T(2,128)(2,1)}, u32[]{:S(2)}, u32[]{:S(2)}) %all-to-all-start) | async-done | bytes 2097184 | tf_op jit(solution)/shard_map/all_to_all | solution.py:171
  72.4 4.1 %copy.18 = bf16[1,2,2,16,16384]{4,3,2,1,0:T(8,128)(2,1)} copy(bf16[1,2,2,16,16384]{4,2,1,3,0:T(2,128)(2,1)} %bitcast.5) | data formatting | bytes 4194304 | tf_op jit(solution)/shard_map/all_to_all | solution.py:171
  76.5 4.3 %reshape_squeeze.3.wave_ref = bf16[2,2,512,512]{3,2,1,0:T(8,128)(2,1)} reshape(bf16[1,2,2,16,16384]{4,3,2,1,0:T(8,128)(2,1)} %copy.18) | data formatting | bytes 4194304 | tf_op jit(solution)/shard_map/reshape;squeeze | solution.py:175
  80.8 81.5 %all-reduce.2.cloned.1.call-done.strain_ref = bf16[3,2,512,512]{3,2,1,0:T(8,128)(2,1)} async-done(((bf16[3,2,512,512]{3,2,1,0:T(8,128)(2,1)}), bf16[3,2,512,512]{3,2,1,0:T(8,128)(2,1)}) %all-reduce.2.cloned.1.call-update) | async-done | bytes 3145744 | tf_op jit(solution)/shard_map/psum | solution.py:43
  162.3 0.0 copy-start.1
  162.3 1.6 copy-done.1
  163.9 0.0 copy-start.2
  163.9 1.4 copy-done.2
  165.3 0.0 copy-start.3
  165.3 1.6 copy-done.3
  166.9 27.3 %shard_map.104 = (f32[2]{0:T(128)}, f32[2]{0:T(128)}) custom-call(s32[2]{0:T(128)S(1)} %gather_fusion, bf16[3,2,512,512]{3,2,1,0:T(8,128)(2,1)} %all-reduce.2.cloned.1.call-done.strain_ref, bf16[2,2,512,512]{3,2,1,0:T(8,128)(2,1)S(1)} %copy-done.1, f32[3,2,512,1]{3,2,1,0:T(8,128)S(1)} %copy-done.2, f32[3,2,1,512]{3,2,1,0:T(1,128)S(1)} %broadcast_in_dim.8.cphase_ref, ...), custom_call_target="tpu_custom_call" | custom-call | tf_op jit(solution)/shard_map/pallas_call | solution.py:138
  (8 shorter events, 0.1 us)
Async XLA Ops:
  7.2 1.6 copy-start
  14.9 57.5 %all-to-all-start = ((bf16[16,2,2,16384]{3,2,1,0:T(2,128)(2,1)}), bf16[16,2,2,16384]{3,2,1,0:T(2,128)(2,1)}, u32[]{:S(2)}, u32[]{:S(2)}) async-start(bf16[16,2,2,16384]{3,2,1,0:T(2,128)(2,1)} %bitcast.16), calls=%async_computation | async-start | bytes 4194304 | tf_op jit(solution)/shard_map/all_to_all | solution.py:171
  22.4 139.9 %all-reduce.2.cloned.1.call-start = ((), (), s32[]{:S(2)}) async-start(), calls=%async_computation.1 | async-start | bytes 6291456 | tf_op jit(solution)/shard_map/psum | solution.py:43
  33.0 0.7 copy-start.5
  33.0 0.9 copy-start.6
  33.0 3.2 %copy-start.4 = (s32[32]{0:T(128)S(1)}, s32[32]{0:T(128)}, u32[]{:S(2)}) copy-start(s32[32]{0:T(128)} %param.11) | copy-start | bytes 388
  162.3 1.6 copy-start.1
  163.9 1.4 copy-start.2
  165.3 1.6 copy-start.3
Sparse Core Ops, SparseCore 0:
  33.2 129.0 all-reduce.1

commit v2 on v1

v2 whole, which is shorter than its diff:
```python
import functools

import jax
import jax.numpy as jnp
import numpy as np
from jax import lax
from jax.experimental import pallas as pl
from jax.experimental.pallas import tpu as pltpu
from jax.sharding import PartitionSpec as P

DET = 3
ROWS = 512
COLS = 512
COL_BLOCK = 256
ROW_BLOCK = 128
WAVE_ROWS = 32
HALF_CHUNKS = 4
LAG = 2
CORES = 2


two_pi = 6.283185307179586
eps_norm = 1e-06


def turn_table(left_ids, right_ids, period):
    angles = (left_ids[:, None] * right_ids[None, :] % period).astype(np.float64) * (2 * np.pi / period)
    return np.cos(angles), np.sin(angles)


def tables():
    row_ids, col_ids = np.arange(ROWS), np.arange(COLS)
    row_cos, row_sin = turn_table(row_ids, row_ids, ROWS)
    row_table = np.block([[row_cos, -row_sin], [row_sin, row_cos]])
    col_cos, col_sin = turn_table(col_ids, col_ids, COLS)
    col_table = np.block([[col_cos, col_sin], [-col_sin, col_cos]])
    twiddle = np.stack(turn_table(row_ids, col_ids, ROWS * COLS))
    return (
        jnp.asarray(row_table, jnp.float32).astype(jnp.bfloat16),
        jnp.asarray(col_table, jnp.float32).astype(jnp.bfloat16),
        jnp.asarray(twiddle, jnp.float32),
    )


def slide_turns(slides):
    total = ROWS * COLS
    row_turns = (jnp.arange(ROWS, dtype=jnp.int32)[None, :] * (COLS * slides % total)[:, None]) % total
    col_turns = (jnp.arange(COLS, dtype=jnp.int32)[None, :] * slides[:, None]) % total
    row_angles = row_turns.astype(jnp.float32) * (two_pi / total)
    col_angles = col_turns.astype(jnp.float32) * (two_pi / total)
    rows = jnp.stack([jnp.cos(row_angles), jnp.sin(row_angles)], 1)[..., None]
    cols = jnp.stack([jnp.cos(col_angles), jnp.sin(col_angles)], 1)[:, :, None, :]
    return rows, cols


def ring_order(chips):
    return list(range(0, chips, 2)) + list(range(chips - 1 - chips % 2, 0, -2))


def spread(own, owner):
    devices = lax.axis_size("tpl")
    chips = devices // CORES
    order = ring_order(chips)
    chip, core = lax.axis_index("tpl") // CORES, lax.axis_index("tpl") % CORES
    half = ROWS // CORES
    rows = half // HALF_CHUNKS
    to_partner = [(i, i ^ 1) for i in range(devices)]
    along = []
    for at in range(chips):
        along.append((order[at] * CORES, order[(at + 1) % chips] * CORES))
        along.append((order[(at + 1) % chips] * CORES + 1, order[at] * CORES + 1))
    on_owner_core = core == owner % CORES
    on_owner_chip = chip == owner // CORES
    chunks = []
    for det in range(DET):
        mine = lax.dynamic_slice_in_dim(own[det], core * half, half, 1)
        theirs = lax.dynamic_slice_in_dim(own[det], (1 - core) * half, half, 1)
        got = lax.ppermute(theirs, "tpl", to_partner)
        first = jnp.where(on_owner_core, mine, got)
        chunks += [first[:, rows * at : rows * (at + 1)] for at in range(HALF_CHUNKS)]
    sent, arrived = [], []
    count = len(chunks)
    for slot in range(count + LAG * (chips - 1)):
        if slot < LAG:
            here = chunks[slot]
        elif slot < count:
            here = jnp.where(on_owner_chip, chunks[slot], arrived[slot - LAG])
        else:
            here = arrived[slot - LAG]
        sent.append(here)
        if slot < count + LAG * (chips - 2):
            arrived.append(lax.ppermute(here, "tpl", along))
    shared = [lax.ppermute(here, "tpl", to_partner) for here in sent]
    place = lambda at: jnp.where(at % 2 == 0, at // 2, chips - 1 - at // 2)
    forward = (place(chip) - place(owner // CORES)) % chips
    backward = (place(owner // CORES) - place(chip)) % chips
    near = jnp.where(core == 0, forward, backward)
    far = jnp.where(core == 0, backward, forward)
    return sent, shared, jnp.stack([core, near, far]).astype(jnp.int32)


def collect(templates, lists):
    devices, groups = lax.axis_size("tpl"), lax.axis_size("grp")
    own_group = lax.axis_index("grp")
    per_device = lists.shape[1]
    bins = templates.shape[2]
    rows = bins // COLS
    pieces = per_device * 2
    if pieces % groups:
        groups, own_group = 1, 0
    size = pieces // groups
    whole_waves = size % 2 == 0
    if whole_waves:
        each = size // 2
        ids = lax.dynamic_slice_in_dim(lists, own_group * each, each, 1)
        picked = templates[ids.reshape(-1)].reshape(devices, each * 2, rows, COLS)
    else:
        picked = templates[lists.reshape(-1)].reshape(devices, pieces, rows, COLS)
        picked = lax.dynamic_slice_in_dim(picked, own_group * size, size, 1)
    own = lax.all_to_all(picked, "tpl", split_axis=0, concat_axis=0, tiled=True)
    found = [own]
    for turn in range(1, groups):
        found.append(lax.ppermute(own, "grp", [(i, (i + turn) % groups) for i in range(groups)]))
    if whole_waves and rows == WAVE_ROWS:
        waves, places = [], []
        for turn, block in enumerate(found):
            for at in range(each):
                waves.append(block[:, 2 * at : 2 * at + 2])
                places.append((own_group - turn) % groups * each + at)
        return waves, jnp.stack([jnp.asarray(place, jnp.int32) for place in places])
    found = jnp.stack(found)[(own_group - jnp.arange(groups)) % groups]
    found = found.transpose(0, 2, 1, 3, 4).reshape(per_device, 2, ROWS // WAVE_ROWS, WAVE_ROWS, COLS)
    return [found[at].transpose(1, 0, 2, 3) for at in range(per_device)], jnp.arange(per_device, dtype=jnp.int32)


def filter_kernel(chips, count, cut_ref, where_ref, *refs):
    slots = DET * HALF_CHUNKS + LAG * (chips - 1)
    near_refs, refs = refs[:slots], refs[slots:]
    far_refs, refs = refs[:slots], refs[slots:]
    wave_refs, refs = refs[:count], refs[count:]
    (rphase_ref, cphase_ref, row_hbm, col_hbm, twiddle_hbm, peaks_ref, norms_ref,
     strain_ref, wave_ref, row_ref, col_ref, twiddle_ref, slid, stacked, twisted, power, sigma,
     strain_sem, wave_sem, table_sem) = refs
    core, near, far = where_ref[0], where_ref[1], where_ref[2]
    half = ROWS // CORES
    rows = half // HALF_CHUNKS

    table_copies = [
        pltpu.make_async_copy(row_hbm, row_ref, table_sem.at[0]),
        pltpu.make_async_copy(twiddle_hbm, twiddle_ref, table_sem.at[1]),
        pltpu.make_async_copy(col_hbm, col_ref, table_sem.at[2]),
    ]
    wave_copies = [pltpu.make_async_copy(wave_refs[at], wave_ref.at[at], wave_sem.at[at]) for at in range(count)]

    def start_chunks(det):
        for slot_refs, distance, side in ((near_refs, near, core), (far_refs, far, 1 - core)):
            for away in range(chips):
                @pl.when(distance == away)
                def _():
                    for at in range(HALF_CHUNKS):
                        into = pl.ds(pl.multiple_of(side * half + at * rows, rows), rows)
                        copy = pltpu.make_async_copy(
                            slot_refs[det * HALF_CHUNKS + at + LAG * away],
                            strain_ref.at[det, :, into, :],
                            strain_sem.at[det],
                        )
                        copy.start()

    start_chunks(0)
    wave_copies[0].start()
    table_copies[0].start()
    table_copies[1].start()
    table_copies[2].start()
    for copy in wave_copies[1:]:
        copy.start()
    for det in range(1, DET):
        start_chunks(det)
    for copy in wave_copies:
        copy.wait()

    def wave(tpl, block, cutoff):
        bins = (lax.broadcasted_iota(jnp.int32, (WAVE_ROWS, COLS), 0) + block * WAVE_ROWS) * COLS
        bins = bins + lax.broadcasted_iota(jnp.int32, (WAVE_ROWS, COLS), 1)
        inside = bins < cutoff
        wave_re = jnp.where(inside, wave_ref[tpl, block, 0].astype(jnp.float32), 0.0)
        wave_im = jnp.where(inside, wave_ref[tpl, block, 1].astype(jnp.float32), 0.0)
        return wave_re, wave_im

    @pl.loop(0, count)
    def _(tpl):
        cutoff = cut_ref[tpl]
        total = jnp.zeros((8, COLS), jnp.float32)
        for block in range(ROWS // WAVE_ROWS):
            wave_re, wave_im = wave(tpl, block, cutoff)
            squares = wave_re * wave_re + wave_im * wave_im
            total = total + jnp.sum(squares.reshape(-1, 8, COLS), axis=0)
        sigma[tpl] = jnp.sum(total)
        power[tpl] = jnp.zeros((ROWS, COLS), jnp.float32)

    for copy in table_copies:
        copy.wait()

    @pl.loop(0, DET)
    def _(det):
        pltpu.make_async_copy(strain_ref.at[det], strain_ref.at[det], strain_sem.at[det]).wait()
        rc, rs = rphase_ref[det, 0], rphase_ref[det, 1]
        cc, cs = cphase_ref[det, 0], cphase_ref[det, 1]
        for at in range(0, ROWS, ROW_BLOCK):
            part = slice(at, at + ROW_BLOCK)
            turn_re = rc[part] * cc - rs[part] * cs
            turn_im = rc[part] * cs + rs[part] * cc
            data_re = strain_ref[det, 0, part, :].astype(jnp.float32)
            data_im = strain_ref[det, 1, part, :].astype(jnp.float32)
            slid[0, part, :] = data_re * turn_re - data_im * turn_im
            slid[1, part, :] = data_re * turn_im + data_im * turn_re

        @pl.loop(0, count)
        def _(tpl):
            cutoff = cut_ref[tpl]
            for block in range(ROWS // WAVE_ROWS):
                part = slice(block * WAVE_ROWS, block * WAVE_ROWS + WAVE_ROWS)
                wave_re, wave_im = wave(tpl, block, cutoff)
                data_re, data_im = slid[0, part, :], slid[1, part, :]
                stacked[part, :] = (data_re * wave_re + data_im * wave_im).astype(jnp.bfloat16)
                low = slice(ROWS + part.start, ROWS + part.stop)
                stacked[low, :] = (data_im * wave_re - data_re * wave_im).astype(jnp.bfloat16)
            for col_at in range(0, COLS, COL_BLOCK):
                cols = slice(col_at, col_at + COL_BLOCK)
                for row_at in range(0, ROWS, ROW_BLOCK):
                    part = slice(row_at, row_at + ROW_BLOCK)
                    low = slice(ROWS + row_at, ROWS + row_at + ROW_BLOCK)
                    first_re = jnp.dot(row_ref[part, :], stacked[:, cols], preferred_element_type=jnp.float32)
                    first_im = jnp.dot(row_ref[low, :], stacked[:, cols], preferred_element_type=jnp.float32)
                    turn_re, turn_im = twiddle_ref[0, part, cols], twiddle_ref[1, part, cols]
                    twisted[part, cols] = (first_re * turn_re - first_im * turn_im).astype(jnp.bfloat16)
                    right = slice(COLS + col_at, COLS + col_at + COL_BLOCK)
                    twisted[part, right] = (first_re * turn_im + first_im * turn_re).astype(jnp.bfloat16)
            for row_at in range(0, ROWS, ROW_BLOCK):
                part = slice(row_at, row_at + ROW_BLOCK)
                series = jnp.dot(twisted[part, :], col_ref[...], preferred_element_type=jnp.float32)
                series_re, series_im = series[:, :COLS], series[:, COLS:]
                power[tpl, part, :] += series_re * series_re + series_im * series_im

    for tpl in range(count):
        largest = jnp.max(power[tpl])
        peaks_ref[tpl] = largest / (2.0 * (sigma[tpl] + eps_norm))
        norms_ref[tpl] = sigma[tpl] / (ROWS * COLS)


def filtered(sent, shared, where, chips, waves, cutoffs, slides):
    count = len(waves)
    rows, cols = slide_turns(slides)
    row_table, col_table, twiddle = tables()
    smem = pl.BlockSpec(memory_space=pltpu.SMEM)
    vmem = pl.BlockSpec(memory_space=pltpu.VMEM)
    hbm = pl.BlockSpec(memory_space=pl.ANY)
    operands = [*sent, *shared, *waves]
    return pl.pallas_call(
        functools.partial(filter_kernel, chips, count),
        out_shape=(jax.ShapeDtypeStruct((count,), jnp.float32),) * 2,
        in_specs=[smem, smem] + [hbm] * len(operands) + [vmem, vmem, hbm, hbm, hbm],
        out_specs=(smem, smem),
        scratch_shapes=[
            pltpu.VMEM((DET, 2, ROWS, COLS), jnp.bfloat16),
            pltpu.VMEM((count, ROWS // WAVE_ROWS, 2, WAVE_ROWS, COLS), jnp.bfloat16),
            pltpu.VMEM((2 * ROWS, 2 * ROWS), jnp.bfloat16),
            pltpu.VMEM((2 * COLS, 2 * COLS), jnp.bfloat16),
            pltpu.VMEM((2, ROWS, COLS), jnp.float32),
            pltpu.VMEM((2, ROWS, COLS), jnp.float32),
            pltpu.VMEM((2 * ROWS, COLS), jnp.bfloat16),
            pltpu.VMEM((ROWS, 2 * COLS), jnp.bfloat16),
            pltpu.VMEM((count, ROWS, COLS), jnp.float32),
            pltpu.SMEM((count,), jnp.float32),
            pltpu.SemaphoreType.DMA((DET,)),
            pltpu.SemaphoreType.DMA((count,)),
            pltpu.SemaphoreType.DMA((3,)),
        ],
        compiler_params=pltpu.CompilerParams(vmem_limit_bytes=56 * 1024 * 1024),
    )(cutoffs, where, *operands, rows, cols, row_table, col_table, twiddle)


def body(strain_slots, templates, cutoffs, lists, owner, slides):
    devices = lax.axis_size("tpl")
    own_index = lax.axis_index("tpl")
    own = strain_slots[0].reshape(DET, 2, ROWS, COLS)
    sent, shared, where = spread(own, owner[0])
    waves, places = collect(templates, lists)
    own_ids = lax.dynamic_index_in_dim(lists, own_index, 0, keepdims=False)
    peaks, norms = filtered(sent, shared, where, devices // CORES, waves, cutoffs[own_ids[places]], slides)
    spot = places[:, None] == jnp.arange(len(waves))[None, :]
    return tuple(jnp.sum(jnp.where(spot, values[:, None], 0.0), axis=0) for values in (peaks, norms))


def solution(mesh):
    in_specs = (
        P(("grp", "tpl"), None, None, None),
        P(None, None, "tpl"),
        P(),
        P(),
        P("grp"),
        P("grp"),
    )
    out_specs = (P(("grp", "tpl")), P(("grp", "tpl")))
    return jax.shard_map(body, mesh=mesh, in_specs=in_specs, out_specs=out_specs, check_vma=False)
```

time: 202 us -> 150 us (0.74)
  waiting for transfers between devices: 117 us -> 31.2 us
  starting transfers between devices: 7.48 us -> 54.8 us
  between operations: 14.8 us -> 1.94 us
  other arithmetic: 4.78 us -> 12.7 us
  local copies, waits for them, and re-layouts: 29.6 us -> 21.9 us
    psum x1 -> x0, waiting for transfers between devices: 81.5 us -> none  [spread(): return lax.psum(block, axis)]
    ppermute x0 -> x54, starting transfers between devices: none -> 50.9 us  [the longest x24 42.4 us: spread(): arrived.append(lax.ppermute(here, 'tpl', along))]
    all_to_all x1, waiting for transfers between devices: 35.5 us -> 0.01 us  [collect(): own = lax.all_to_all(picked, 'tpl', split_axis=0, concat_axis=0, tiled=True)]
    ppermute x0 -> x54, waiting for transfers between devices: none -> 31.2 us  [the longest x24 31.1 us: spread(): arrived.append(lax.ppermute(here, 'tpl', along))]
    slice x0 -> x2, local copies, waits for them, and re-layouts: none -> 4.67 us  [the longest x1 4.65 us: spread(): mine = lax.dynamic_slice_in_dim(own[det], core * half, half, 1)]
    reshape x2 -> x1, local copies, waits for them, and re-layouts: 5.87 us -> 1.54 us  [collect(): picked = templates[ids.reshape(-1)].reshape(devices, each * 2, rows, COLS)]
    another operation x1 -> x0, local copies, waits for them, and re-layouts: 4.27 us -> none  [body(): arrived.reshape(per_device, 2, ROWS, COLS)]
    all_to_all x1 -> x0, local copies, waits for them, and re-layouts: 4.12 us -> none  [body(): lax.all_to_all(picked, 'tpl', split_axis=0, concat_axis=3, tiled=True)[0]]
  transfers between devices with their start and end apart: 2 -> 55, of which waited for: 2 -> 19; matrix products, arithmetic and copies ran while one was open for 11% -> 17% of each run, Pallas kernels for 0% -> 0%
where the time goes in v2:
time: 150 us; the launch traced here: 149 us
  starting transfers between devices  54.8 us (37%)
  waiting for transfers between devices  31.2 us (21%)
  Pallas kernels  26.5 us (18%)
  local copies, waits for them, and re-layouts  21.9 us (15%)
  other arithmetic  12.7 us (8%)
  between operations  1.94 us (1%)
    ppermute x24, starting transfers between devices, spread(): arrived.append(lax.ppermute(here, 'tpl', along))  42.4 us
    ppermute x24, waiting for transfers between devices, spread(): arrived.append(lax.ppermute(here, 'tpl', along))  31.1 us
    pallas_call x1, Pallas kernels, filtered(): pl.pallas_call(functools.partial(filter_kernel, chips, count), out_shape=...  26.5 us
    ppermute x26, starting transfers between devices, spread(): shared = [lax.ppermute(here, 'tpl', to_partner) for here in sent]  6.19 us
    slice x1, local copies, waits for them, and re-layouts, spread(): mine = lax.dynamic_slice_in_dim(own[det], core * half, half, 1)  4.65 us
    all_to_all x1, starting transfers between devices, collect(): own = lax.all_to_all(picked, 'tpl', split_axis=0, concat_axis=0, tiled=True)  3.91 us
    unnamed x81, local copies, waits for them, and re-layouts  3.48 us
    select_n x2, other arithmetic, spread(): first = jnp.where(on_owner_core, mine, got)  3.15 us
  transfers between devices with their start and end apart: 55, of which 19 were waited for; matrix products, arithmetic and copies ran while one was open for 17% of the time, Pallas kernels for 0%

profile of v2, /device:TPU:0, one launch (start us, length us, event | category | flops | bytes accessed | tf_op | source)
XLA Modules:
  0.0 149.2 jit_solution(6579749075620334139)
XLA Ops:
  0.7 4.7 %fusion.15 = (bf16[1,1,2,262144]{3,2,1,0:T(2,128)(2,1)}, bf16[1,1,2,262144]{3,2,1,0:T(2,128)(2,1)S(1)}, bf16[1,1,2,262144]{3,2,1,0:T(2,128)(2,1)}) fusion(bf16[1,3,2,262144]{3,2,1,0:T(2,128)(2,1)} %param.9), kind=kLoop, calls=%fused_computation.61 | loop fusion | bytes 6291456 | tf_op jit(solution)/shard_map/slice | solution.py:76
  6.8 1.4 copy.20
  12.3 1.3 dynamic-slice_select_fusion.2
  13.7 2.9 %collective-permute-start.2 = (bf16[2,64,512]{2,1,0:T(8,128)(2,1)S(1)}, bf16[2,64,512]{2,1,0:T(8,128)(2,1)S(1)}, u32[]{:S(2)}, u32[]{:S(2)}) collective-permute-start(bf16[2,64,512]{2,1,0:T(8,128)(2,1)S(1)} %get-tuple-element.21.refs_1_), channel_id=1, source_target_pairs={{0,4},{5,1},{4,8},{9,5},{8,12},{13,9},{12,14},{15,13},{14,10},{11,... | collective-permute-start | bytes 393224 | tf_op jit(solution)/shard_map/ppermute | solution.py:92
  16.6 1.6 %collective-permute-start.1 = (bf16[2,64,512]{2,1,0:T(8,128)(2,1)S(1)}, bf16[2,64,512]{2,1,0:T(8,128)(2,1)}, u32[]{:S(2)}, u32[]{:S(2)}) collective-permute-start(bf16[2,64,512]{2,1,0:T(8,128)(2,1)S(1)} %get-tuple-element.22.refs_0_), channel_id=1, source_target_pairs={{0,4},{5,1},{4,8},{9,5},{8,12},{13,9},{12,14},{15,13},{14,10},{11,... | collective-permute-start | bytes 393224 | tf_op jit(solution)/shard_map/ppermute | solution.py:92
  18.2 2.7 %gather_fusion.2 = bf16[16,2,16384]{2,1,0:T(2,128)(2,1)S(1)} fusion(bf16[32,2,16384]{2,1,0:T(2,128)(2,1)S(1)} %copy-done, s32[1024]{0:T(1024)S(1)} %pad_clamp_fusion), kind=kCustom, calls=%fused_computation.2 | custom fusion | bytes 2097216 | tf_op jit(solution)/shard_map/gather | solution.py:116
  20.9 1.5 %reshape.297 = bf16[16,2,32,512]{3,2,1,0:T(8,128)(2,1)} reshape(bf16[16,2,16384]{2,1,0:T(2,128)(2,1)S(1)} %gather_fusion.2) | data formatting | bytes 2097152 | tf_op jit(solution)/shard_map/reshape | solution.py:116
  22.4 3.9 %all-to-all-start = ((bf16[16,2,32,512]{3,2,1,0:T(8,128)(2,1)}), bf16[16,2,32,512]{3,2,1,0:T(8,128)(2,1)S(1)}, u32[]{:S(2)}, u32[]{:S(2)}) async-start(bf16[16,2,32,512]{3,2,1,0:T(8,128)(2,1)} %reshape.297), calls=%async_computation | async-start | bytes 2097152 | tf_op jit(solution)/shard_map/all_to_all | solution.py:120
  27.1 1.1 slice_select_fusion.8
  28.2 1.9 %collective-permute-start.5 = (bf16[2,64,512]{2,1,0:T(8,128)(2,1)S(1)}, bf16[2,64,512]{2,1,0:T(8,128)(2,1)S(1)}, u32[]{:S(2)}, u32[]{:S(2)}) collective-permute-start(bf16[2,64,512]{2,1,0:T(8,128)(2,1)S(1)} %get-tuple-element.19.refs_3_), channel_id=1, source_target_pairs={{0,4},{5,1},{4,8},{9,5},{8,12},{13,9},{12,14},{15,13},{14,10},{11,... | collective-permute-start | bytes 393224 | tf_op jit(solution)/shard_map/ppermute | solution.py:92
  30.1 1.5 collective-permute-start.4
  31.6 1.8 %dynamic-slice_select_fusion = (bf16[2,256,512]{2,1,0:T(8,128)(2,1)S(1)}, bf16[2,256,512]{2,1,0:T(8,128)(2,1)S(1)}) fusion(bf16[2,256,512]{2,1,0:T(8,128)(2,1)} %collective-permute-done.8, bf16[2,512,512]{2,1,0:T(8,128)(2,1)} %bitcast.38, s32[]{:T(128)S(6)} %select_n.240, pred[]{:T(512)S(6)} %eq.53, bf16[2,256,512]{2,1,0:T(8,128)(2,1)} %collective-permute-done.3, ...), kind=kLoop, calls=%fused_computation.6 | loop fusion | flops 524288 | bytes 3145733 | tf_op jit(solution)/shard_map/jit(_where)/select_n | solution.py:79
  33.4 12.4 %collective-permute-done.5 = bf16[2,64,512]{2,1,0:T(8,128)(2,1)S(1)} collective-permute-done((bf16[2,64,512]{2,1,0:T(8,128)(2,1)S(1)}, bf16[2,64,512]{2,1,0:T(8,128)(2,1)S(1)}, u32[]{:S(2)}, u32[]{:S(2)}) %collective-permute-start.5) | collective-permute-done | bytes 131104 | tf_op jit(solution)/shard_map/ppermute | solution.py:92
  45.8 1.4 collective-permute-done.4
  47.3 7.2 %collective-permute-start.7 = (bf16[2,64,512]{2,1,0:T(8,128)(2,1)S(1)}, bf16[2,64,512]{2,1,0:T(8,128)(2,1)S(1)}, u32[]{:S(2)}, u32[]{:S(2)}) collective-permute-start(bf16[2,64,512]{2,1,0:T(8,128)(2,1)S(1)} %get-tuple-element.17.refs_5_), channel_id=1, source_target_pairs={{0,4},{5,1},{4,8},{9,5},{8,12},{13,9},{12,14},{15,13},{14,10},{11,... | collective-permute-start | bytes 393224 | tf_op jit(solution)/shard_map/ppermute | solution.py:92
  54.5 2.5 %collective-permute-start.6 = (bf16[2,64,512]{2,1,0:T(8,128)(2,1)S(1)}, bf16[2,64,512]{2,1,0:T(8,128)(2,1)S(1)}, u32[]{:S(2)}, u32[]{:S(2)}) collective-permute-start(bf16[2,64,512]{2,1,0:T(8,128)(2,1)S(1)} %get-tuple-element.18.refs_4_), channel_id=1, source_target_pairs={{0,4},{5,1},{4,8},{9,5},{8,12},{13,9},{12,14},{15,13},{14,10},{11,... | collective-permute-start | bytes 393224 | tf_op jit(solution)/shard_map/ppermute | solution.py:92
  57.0 2.5 %collective-permute-done.6 = bf16[2,64,512]{2,1,0:T(8,128)(2,1)S(1)} collective-permute-done((bf16[2,64,512]{2,1,0:T(8,128)(2,1)S(1)}, bf16[2,64,512]{2,1,0:T(8,128)(2,1)S(1)}, u32[]{:S(2)}, u32[]{:S(2)}) %collective-permute-start.6) | collective-permute-done | bytes 131104 | tf_op jit(solution)/shard_map/ppermute | solution.py:92
  59.5 2.5 %collective-permute-start.10 = (bf16[2,64,512]{2,1,0:T(8,128)(2,1)S(1)}, bf16[2,64,512]{2,1,0:T(8,128)(2,1)S(1)}, u32[]{:S(2)}, u32[]{:S(2)}) collective-permute-start(bf16[2,64,512]{2,1,0:T(8,128)(2,1)S(1)} %get-tuple-element.15.refs_7_), channel_id=1, source_target_pairs={{0,4},{5,1},{4,8},{9,5},{8,12},{13,9},{12,14},{15,13},{14,10},{11,... | collective-permute-start | bytes 393224 | tf_op jit(solution)/shard_map/ppermute | solution.py:92
  62.0 1.4 collective-permute-start.9
  63.4 1.9 %collective-permute-done.10 = bf16[2,64,512]{2,1,0:T(8,128)(2,1)S(1)} collective-permute-done((bf16[2,64,512]{2,1,0:T(8,128)(2,1)S(1)}, bf16[2,64,512]{2,1,0:T(8,128)(2,1)S(1)}, u32[]{:S(2)}, u32[]{:S(2)}) %collective-permute-start.10) | collective-permute-done | bytes 131104 | tf_op jit(solution)/shard_map/ppermute | solution.py:92
  65.3 1.7 %collective-permute-done.9 = bf16[2,64,512]{2,1,0:T(8,128)(2,1)S(1)} collective-permute-done((bf16[2,64,512]{2,1,0:T(8,128)(2,1)S(1)}, bf16[2,64,512]{2,1,0:T(8,128)(2,1)S(1)}, u32[]{:S(2)}, u32[]{:S(2)}) %collective-permute-start.9) | collective-permute-done | bytes 131104 | tf_op jit(solution)/shard_map/ppermute | solution.py:92
  67.1 1.5 collective-permute-start.12
  68.5 1.4 collective-permute-start.11
  70.5 1.6 %collective-permute-done.12 = bf16[2,64,512]{2,1,0:T(8,128)(2,1)S(1)} collective-permute-done((bf16[2,64,512]{2,1,0:T(8,128)(2,1)S(1)}, bf16[2,64,512]{2,1,0:T(8,128)(2,1)S(1)}, u32[]{:S(2)}, u32[]{:S(2)}) %collective-permute-start.12) | collective-permute-done | bytes 131104 | tf_op jit(solution)/shard_map/ppermute | solution.py:92
  72.1 1.4 collective-permute-done.11
  75.2 1.5 collective-permute-start.14
  76.7 1.5 collective-permute-start.13
  80.4 1.4 collective-permute-start.16
  82.0 1.4 collective-permute-start.15
  85.6 1.4 collective-permute-start.18
  87.3 1.4 collective-permute-start.17
  90.9 1.4 collective-permute-start.20
  92.6 1.4 collective-permute-start.19
  94.1 1.4 collective-permute-start.53
  97.0 1.3 gather_fusion
  98.8 1.1 collective-permute-start.22
  102.5 1.5 collective-permute-done.22.refs_21_
  104.0 1.1 collective-permute-start.24
  105.4 1.1 collective-permute-start.23
  109.1 1.1 collective-permute-start.26
  110.5 1.1 collective-permute-start.25
  111.6 1.3 pad_maximum_fusion
  114.4 1.4 collective-permute-done.25.refs_24_
  115.9 1.3 broadcast_in_dim.36.refs_55_
  117.2 2.4 %copy.13.refs_54_ = f32[3,2,512,1]{3,2,1,0:T(8,128)} copy(f32[3,2,512,1]{2,1,0,3:T(2,128)} %maximum_bitcast_fusion) | data formatting | bytes 24576 | tf_op jit(solution)/shard_map/broadcast_in_dim | solution.py:51
  119.6 1.1 gather_fusion.1
  121.4 26.5 %shard_map.104 = (f32[2]{0:T(128)}, f32[2]{0:T(128)}) custom-call(s32[2]{0:T(128)} %gather_fusion.1, s32[3]{0:T(128)} %pad_add_fusion.1.where_ref, bf16[2,64,512]{2,1,0:T(8,128)(2,1)} %copy-done.9, bf16[2,64,512]{2,1,0:T(8,128)(2,1)} %copy-done.8, bf16[2,64,512]{2,1,0:T(8,128)(2,1)} %copy-done.11, bf16[2,64,512]{2,1,0:T(8,128)(2,1)} %copy-done.10, ...), custom_call_target="tpu_custom_call" | custom-call | tf_op jit(solution)/shard_map/pallas_call | solution.py:258
  147.9 1.3 select_reduce_fusion
  (177 shorter events, 25.2 us)
Async XLA Ops:
  6.3 6.0 %collective-permute-start = (bf16[2,256,512]{2,1,0:T(8,128)(2,1)}, bf16[2,256,512]{2,1,0:T(8,128)(2,1)}, u32[]{:S(2)}, u32[]{:S(2)}) collective-permute-start(bf16[2,256,512]{2,1,0:T(8,128)(2,1)} %constant_dynamic-slice_fusion.3), channel_id=1, source_target_pairs={{0,1},{1,0},{2,3},{3,2},{4,5},{5,4},{6,7},{7,6},{8,9},{9,8},{10,11... | collective-permute-start | bytes 1572872 | tf_op jit(solution)/shard_map/ppermute | solution.py:78
  9.1 22.5 %collective-permute-start.8 = (bf16[2,256,512]{2,1,0:T(8,128)(2,1)}, bf16[2,256,512]{2,1,0:T(8,128)(2,1)}, u32[]{:S(2)}, u32[]{:S(2)}) collective-permute-start(bf16[2,256,512]{2,1,0:T(8,128)(2,1)} %constant_dynamic-slice_fusion.1), channel_id=1, source_target_pairs={{0,1},{1,0},{2,3},{3,2},{4,5},{5,4},{6,7},{7,6},{8,9},{9,8},{10,11... | collective-permute-start | bytes 1572872 | tf_op jit(solution)/shard_map/ppermute | solution.py:78
  11.4 20.2 %collective-permute-start.3 = (bf16[2,256,512]{2,1,0:T(8,128)(2,1)}, bf16[2,256,512]{2,1,0:T(8,128)(2,1)}, u32[]{:S(2)}, u32[]{:S(2)}) collective-permute-start(bf16[2,256,512]{2,1,0:T(8,128)(2,1)} %constant_dynamic-slice_fusion.2), channel_id=1, source_target_pairs={{0,1},{1,0},{2,3},{3,2},{4,5},{5,4},{6,7},{7,6},{8,9},{9,8},{10,11... | collective-permute-start | bytes 1572872 | tf_op jit(solution)/shard_map/ppermute | solution.py:78
  13.7 12.7 %collective-permute-start.2 = (bf16[2,64,512]{2,1,0:T(8,128)(2,1)S(1)}, bf16[2,64,512]{2,1,0:T(8,128)(2,1)S(1)}, u32[]{:S(2)}, u32[]{:S(2)}) collective-permute-start(bf16[2,64,512]{2,1,0:T(8,128)(2,1)S(1)} %get-tuple-element.21.refs_1_), channel_id=1, source_target_pairs={{0,4},{5,1},{4,8},{9,5},{8,12},{13,9},{12,14},{15,13},{14,10},{11,... | collective-permute-start | bytes 393224 | tf_op jit(solution)/shard_map/ppermute | solution.py:92
  16.6 10.5 %collective-permute-start.1 = (bf16[2,64,512]{2,1,0:T(8,128)(2,1)S(1)}, bf16[2,64,512]{2,1,0:T(8,128)(2,1)}, u32[]{:S(2)}, u32[]{:S(2)}) collective-permute-start(bf16[2,64,512]{2,1,0:T(8,128)(2,1)S(1)} %get-tuple-element.22.refs_0_), channel_id=1, source_target_pairs={{0,4},{5,1},{4,8},{9,5},{8,12},{13,9},{12,14},{15,13},{14,10},{11,... | collective-permute-start | bytes 393224 | tf_op jit(solution)/shard_map/ppermute | solution.py:92
  22.4 71.6 %all-to-all-start = ((bf16[16,2,32,512]{3,2,1,0:T(8,128)(2,1)}), bf16[16,2,32,512]{3,2,1,0:T(8,128)(2,1)S(1)}, u32[]{:S(2)}, u32[]{:S(2)}) async-start(bf16[16,2,32,512]{3,2,1,0:T(8,128)(2,1)} %reshape.297), calls=%async_computation | async-start | bytes 2097152 | tf_op jit(solution)/shard_map/all_to_all | solution.py:120
  28.2 17.6 %collective-permute-start.5 = (bf16[2,64,512]{2,1,0:T(8,128)(2,1)S(1)}, bf16[2,64,512]{2,1,0:T(8,128)(2,1)S(1)}, u32[]{:S(2)}, u32[]{:S(2)}) collective-permute-start(bf16[2,64,512]{2,1,0:T(8,128)(2,1)S(1)} %get-tuple-element.19.refs_3_), channel_id=1, source_target_pairs={{0,4},{5,1},{4,8},{9,5},{8,12},{13,9},{12,14},{15,13},{14,10},{11,... | collective-permute-start | bytes 393224 | tf_op jit(solution)/shard_map/ppermute | solution.py:92
  30.1 17.1 %collective-permute-start.4 = (bf16[2,64,512]{2,1,0:T(8,128)(2,1)S(1)}, bf16[2,64,512]{2,1,0:T(8,128)(2,1)S(1)}, u32[]{:S(2)}, u32[]{:S(2)}) collective-permute-start(bf16[2,64,512]{2,1,0:T(8,128)(2,1)S(1)} %get-tuple-element.20.refs_2_), channel_id=1, source_target_pairs={{0,4},{5,1},{4,8},{9,5},{8,12},{13,9},{12,14},{15,13},{14,10},{11,... | collective-permute-start | bytes 393224 | tf_op jit(solution)/shard_map/ppermute | solution.py:92
  47.3 9.7 %collective-permute-start.7 = (bf16[2,64,512]{2,1,0:T(8,128)(2,1)S(1)}, bf16[2,64,512]{2,1,0:T(8,128)(2,1)S(1)}, u32[]{:S(2)}, u32[]{:S(2)}) collective-permute-start(bf16[2,64,512]{2,1,0:T(8,128)(2,1)S(1)} %get-tuple-element.17.refs_5_), channel_id=1, source_target_pairs={{0,4},{5,1},{4,8},{9,5},{8,12},{13,9},{12,14},{15,13},{14,10},{11,... | collective-permute-start | bytes 393224 | tf_op jit(solution)/shard_map/ppermute | solution.py:92
  54.5 5.0 %collective-permute-start.6 = (bf16[2,64,512]{2,1,0:T(8,128)(2,1)S(1)}, bf16[2,64,512]{2,1,0:T(8,128)(2,1)S(1)}, u32[]{:S(2)}, u32[]{:S(2)}) collective-permute-start(bf16[2,64,512]{2,1,0:T(8,128)(2,1)S(1)} %get-tuple-element.18.refs_4_), channel_id=1, source_target_pairs={{0,4},{5,1},{4,8},{9,5},{8,12},{13,9},{12,14},{15,13},{14,10},{11,... | collective-permute-start | bytes 393224 | tf_op jit(solution)/shard_map/ppermute | solution.py:92
  59.5 5.8 %collective-permute-start.10 = (bf16[2,64,512]{2,1,0:T(8,128)(2,1)S(1)}, bf16[2,64,512]{2,1,0:T(8,128)(2,1)S(1)}, u32[]{:S(2)}, u32[]{:S(2)}) collective-permute-start(bf16[2,64,512]{2,1,0:T(8,128)(2,1)S(1)} %get-tuple-element.15.refs_7_), channel_id=1, source_target_pairs={{0,4},{5,1},{4,8},{9,5},{8,12},{13,9},{12,14},{15,13},{14,10},{11,... | collective-permute-start | bytes 393224 | tf_op jit(solution)/shard_map/ppermute | solution.py:92
  62.0 5.0 %collective-permute-start.9 = (bf16[2,64,512]{2,1,0:T(8,128)(2,1)S(1)}, bf16[2,64,512]{2,1,0:T(8,128)(2,1)S(1)}, u32[]{:S(2)}, u32[]{:S(2)}) collective-permute-start(bf16[2,64,512]{2,1,0:T(8,128)(2,1)S(1)} %get-tuple-element.16.refs_6_), channel_id=1, source_target_pairs={{0,4},{5,1},{4,8},{9,5},{8,12},{13,9},{12,14},{15,13},{14,10},{11,... | collective-permute-start | bytes 393224 | tf_op jit(solution)/shard_map/ppermute | solution.py:92
  67.1 5.0 %collective-permute-start.12 = (bf16[2,64,512]{2,1,0:T(8,128)(2,1)S(1)}, bf16[2,64,512]{2,1,0:T(8,128)(2,1)S(1)}, u32[]{:S(2)}, u32[]{:S(2)}) collective-permute-start(bf16[2,64,512]{2,1,0:T(8,128)(2,1)S(1)} %get-tuple-element.13.refs_9_), channel_id=1, source_target_pairs={{0,4},{5,1},{4,8},{9,5},{8,12},{13,9},{12,14},{15,13},{14,10},{11,... | collective-permute-start | bytes 393224 | tf_op jit(solution)/shard_map/ppermute | solution.py:92
  68.5 5.0 %collective-permute-start.11 = (bf16[2,64,512]{2,1,0:T(8,128)(2,1)S(1)}, bf16[2,64,512]{2,1,0:T(8,128)(2,1)S(1)}, u32[]{:S(2)}, u32[]{:S(2)}) collective-permute-start(bf16[2,64,512]{2,1,0:T(8,128)(2,1)S(1)} %get-tuple-element.14.refs_8_), channel_id=1, source_target_pairs={{0,4},{5,1},{4,8},{9,5},{8,12},{13,9},{12,14},{15,13},{14,10},{11,... | collective-permute-start | bytes 393224 | tf_op jit(solution)/shard_map/ppermute | solution.py:92
  69.9 4.3 %collective-permute-start.28 = (bf16[2,64,512]{2,1,0:T(8,128)(2,1)S(1)}, bf16[2,64,512]{2,1,0:T(8,128)(2,1)S(1)}, u32[]{:S(2)}, u32[]{:S(2)}) collective-permute-start(bf16[2,64,512]{2,1,0:T(8,128)(2,1)S(1)} %get-tuple-element.21.refs_1_), channel_id=1, source_target_pairs={{0,1},{1,0},{2,3},{3,2},{4,5},{5,4},{6,7},{7,6},{8,9},{9,8},{10,11... | collective-permute-start | bytes 393224 | tf_op jit(solution)/shard_map/ppermute | solution.py:93
  69.9 4.8 %collective-permute-start.27 = (bf16[2,64,512]{2,1,0:T(8,128)(2,1)S(1)}, bf16[2,64,512]{2,1,0:T(8,128)(2,1)S(1)}, u32[]{:S(2)}, u32[]{:S(2)}) collective-permute-start(bf16[2,64,512]{2,1,0:T(8,128)(2,1)S(1)} %get-tuple-element.22.refs_0_), channel_id=1, source_target_pairs={{0,1},{1,0},{2,3},{3,2},{4,5},{5,4},{6,7},{7,6},{8,9},{9,8},{10,11... | collective-permute-start | bytes 393224 | tf_op jit(solution)/shard_map/ppermute | solution.py:93
  70.4 4.4 %collective-permute-start.30 = (bf16[2,64,512]{2,1,0:T(8,128)(2,1)S(1)}, bf16[2,64,512]{2,1,0:T(8,128)(2,1)S(1)}, u32[]{:S(2)}, u32[]{:S(2)}) collective-permute-start(bf16[2,64,512]{2,1,0:T(8,128)(2,1)S(1)} %get-tuple-element.19.refs_3_), channel_id=1, source_target_pairs={{0,1},{1,0},{2,3},{3,2},{4,5},{5,4},{6,7},{7,6},{8,9},{9,8},{10,11... | collective-permute-start | bytes 393224 | tf_op jit(solution)/shard_map/ppermute | solution.py:93
  75.2 5.1 %collective-permute-start.14 = (bf16[2,64,512]{2,1,0:T(8,128)(2,1)S(1)}, bf16[2,64,512]{2,1,0:T(8,128)(2,1)}, u32[]{:S(2)}, u32[]{:S(2)}) collective-permute-start(bf16[2,64,512]{2,1,0:T(8,128)(2,1)S(1)} %get-tuple-element.11.refs_11_), channel_id=1, source_target_pairs={{0,4},{5,1},{4,8},{9,5},{8,12},{13,9},{12,14},{15,13},{14,10},{11,... | collective-permute-start | bytes 393224 | tf_op jit(solution)/shard_map/ppermute | solution.py:92
  76.7 5.3 %collective-permute-start.13 = (bf16[2,64,512]{2,1,0:T(8,128)(2,1)}, bf16[2,64,512]{2,1,0:T(8,128)(2,1)}, u32[]{:S(2)}, u32[]{:S(2)}) collective-permute-start(bf16[2,64,512]{2,1,0:T(8,128)(2,1)} %get-tuple-element.12.refs_10_), channel_id=1, source_target_pairs={{0,4},{5,1},{4,8},{9,5},{8,12},{13,9},{12,14},{15,13},{14,10},{11,... | collective-permute-start | bytes 393224 | tf_op jit(solution)/shard_map/ppermute | solution.py:92
  78.2 6.1 %collective-permute-start.36 = (bf16[2,64,512]{2,1,0:T(8,128)(2,1)S(1)}, bf16[2,64,512]{2,1,0:T(8,128)(2,1)S(1)}, u32[]{:S(2)}, u32[]{:S(2)}) collective-permute-start(bf16[2,64,512]{2,1,0:T(8,128)(2,1)S(1)} %get-tuple-element.13.refs_9_), channel_id=1, source_target_pairs={{0,1},{1,0},{2,3},{3,2},{4,5},{5,4},{6,7},{7,6},{8,9},{9,8},{10,11... | collective-permute-start | bytes 393224 | tf_op jit(solution)/shard_map/ppermute | solution.py:93
  78.7 5.7 %collective-permute-start.35 = (bf16[2,64,512]{2,1,0:T(8,128)(2,1)S(1)}, bf16[2,64,512]{2,1,0:T(8,128)(2,1)S(1)}, u32[]{:S(2)}, u32[]{:S(2)}) collective-permute-start(bf16[2,64,512]{2,1,0:T(8,128)(2,1)S(1)} %get-tuple-element.14.refs_8_), channel_id=1, source_target_pairs={{0,1},{1,0},{2,3},{3,2},{4,5},{5,4},{6,7},{7,6},{8,9},{9,8},{10,11... | collective-permute-start | bytes 393224 | tf_op jit(solution)/shard_map/ppermute | solution.py:93
  78.8 6.1 %collective-permute-start.38 = (bf16[2,64,512]{2,1,0:T(8,128)(2,1)S(1)}, bf16[2,64,512]{2,1,0:T(8,128)(2,1)S(1)}, u32[]{:S(2)}, u32[]{:S(2)}) collective-permute-start(bf16[2,64,512]{2,1,0:T(8,128)(2,1)S(1)} %get-tuple-element.11.refs_11_), channel_id=1, source_target_pairs={{0,1},{1,0},{2,3},{3,2},{4,5},{5,4},{6,7},{7,6},{8,9},{9,8},{10,11... | collective-permute-start | bytes 393224 | tf_op jit(solution)/shard_map/ppermute | solution.py:93
  80.4 5.3 %collective-permute-start.16 = (bf16[2,64,512]{2,1,0:T(8,128)(2,1)}, bf16[2,64,512]{2,1,0:T(8,128)(2,1)}, u32[]{:S(2)}, u32[]{:S(2)}) collective-permute-start(bf16[2,64,512]{2,1,0:T(8,128)(2,1)} %collective-permute-done.14.refs_13_), channel_id=1, source_target_pairs={{0,4},{5,1},{4,8},{9,5},{8,12},{13,9},{12,14},{15,13},{14,10},{11,... | collective-permute-start | bytes 393224 | tf_op jit(solution)/shard_map/ppermute | solution.py:92
  82.0 5.3 %collective-permute-start.15 = (bf16[2,64,512]{2,1,0:T(8,128)(2,1)}, bf16[2,64,512]{2,1,0:T(8,128)(2,1)}, u32[]{:S(2)}, u32[]{:S(2)}) collective-permute-start(bf16[2,64,512]{2,1,0:T(8,128)(2,1)} %collective-permute-done.13.refs_12_), channel_id=1, source_target_pairs={{0,4},{5,1},{4,8},{9,5},{8,12},{13,9},{12,14},{15,13},{14,10},{11,... | collective-permute-start | bytes 393224 | tf_op jit(solution)/shard_map/ppermute | solution.py:92
  84.3 5.0 %collective-permute-start.37 = (bf16[2,64,512]{2,1,0:T(8,128)(2,1)}, bf16[2,64,512]{2,1,0:T(8,128)(2,1)}, u32[]{:S(2)}, u32[]{:S(2)}) collective-permute-start(bf16[2,64,512]{2,1,0:T(8,128)(2,1)} %get-tuple-element.12.refs_10_), channel_id=1, source_target_pairs={{0,1},{1,0},{2,3},{3,2},{4,5},{5,4},{6,7},{7,6},{8,9},{9,8},{10,11... | collective-permute-start | bytes 393224 | tf_op jit(solution)/shard_map/ppermute | solution.py:93
  84.4 4.9 %collective-permute-start.40 = (bf16[2,64,512]{2,1,0:T(8,128)(2,1)}, bf16[2,64,512]{2,1,0:T(8,128)(2,1)}, u32[]{:S(2)}, u32[]{:S(2)}) collective-permute-start(bf16[2,64,512]{2,1,0:T(8,128)(2,1)} %collective-permute-done.14.refs_13_), channel_id=1, source_target_pairs={{0,1},{1,0},{2,3},{3,2},{4,5},{5,4},{6,7},{7,6},{8,9},{9,8},{10,11... | collective-permute-start | bytes 393224 | tf_op jit(solution)/shard_map/ppermute | solution.py:93
  85.0 9.1 %collective-permute-start.39 = (bf16[2,64,512]{2,1,0:T(8,128)(2,1)}, bf16[2,64,512]{2,1,0:T(8,128)(2,1)}, u32[]{:S(2)}, u32[]{:S(2)}) collective-permute-start(bf16[2,64,512]{2,1,0:T(8,128)(2,1)} %collective-permute-done.13.refs_12_), channel_id=1, source_target_pairs={{0,1},{1,0},{2,3},{3,2},{4,5},{5,4},{6,7},{7,6},{8,9},{9,8},{10,11... | collective-permute-start | bytes 393224 | tf_op jit(solution)/shard_map/ppermute | solution.py:93
  85.6 5.3 %collective-permute-start.18 = (bf16[2,64,512]{2,1,0:T(8,128)(2,1)}, bf16[2,64,512]{2,1,0:T(8,128)(2,1)}, u32[]{:S(2)}, u32[]{:S(2)}) collective-permute-start(bf16[2,64,512]{2,1,0:T(8,128)(2,1)} %collective-permute-done.16.refs_15_), channel_id=1, source_target_pairs={{0,4},{5,1},{4,8},{9,5},{8,12},{13,9},{12,14},{15,13},{14,10},{11,... | collective-permute-start | bytes 393224 | tf_op jit(solution)/shard_map/ppermute | solution.py:92
  87.3 5.3 %collective-permute-start.17 = (bf16[2,64,512]{2,1,0:T(8,128)(2,1)}, bf16[2,64,512]{2,1,0:T(8,128)(2,1)}, u32[]{:S(2)}, u32[]{:S(2)}) collective-permute-start(bf16[2,64,512]{2,1,0:T(8,128)(2,1)} %collective-permute-done.15.refs_14_), channel_id=1, source_target_pairs={{0,4},{5,1},{4,8},{9,5},{8,12},{13,9},{12,14},{15,13},{14,10},{11,... | collective-permute-start | bytes 393224 | tf_op jit(solution)/shard_map/ppermute | solution.py:92
  89.3 9.0 %collective-permute-start.42 = (bf16[2,64,512]{2,1,0:T(8,128)(2,1)}, bf16[2,64,512]{2,1,0:T(8,128)(2,1)}, u32[]{:S(2)}, u32[]{:S(2)}) collective-permute-start(bf16[2,64,512]{2,1,0:T(8,128)(2,1)} %collective-permute-done.16.refs_15_), channel_id=1, source_target_pairs={{0,1},{1,0},{2,3},{3,2},{4,5},{5,4},{6,7},{7,6},{8,9},{9,8},{10,11... | collective-permute-start | bytes 393224 | tf_op jit(solution)/shard_map/ppermute | solution.py:93
  89.3 8.9 %collective-permute-start.41 = (bf16[2,64,512]{2,1,0:T(8,128)(2,1)}, bf16[2,64,512]{2,1,0:T(8,128)(2,1)}, u32[]{:S(2)}, u32[]{:S(2)}) collective-permute-start(bf16[2,64,512]{2,1,0:T(8,128)(2,1)} %collective-permute-done.15.refs_14_), channel_id=1, source_target_pairs={{0,1},{1,0},{2,3},{3,2},{4,5},{5,4},{6,7},{7,6},{8,9},{9,8},{10,11... | collective-permute-start | bytes 393224 | tf_op jit(solution)/shard_map/ppermute | solution.py:93
  90.9 7.9 %collective-permute-start.20 = (bf16[2,64,512]{2,1,0:T(8,128)(2,1)}, bf16[2,64,512]{2,1,0:T(8,128)(2,1)}, u32[]{:S(2)}, u32[]{:S(2)}) collective-permute-start(bf16[2,64,512]{2,1,0:T(8,128)(2,1)} %collective-permute-done.18.refs_17_), channel_id=1, source_target_pairs={{0,4},{5,1},{4,8},{9,5},{8,12},{13,9},{12,14},{15,13},{14,10},{11,... | collective-permute-start | bytes 393224 | tf_op jit(solution)/shard_map/ppermute | solution.py:92
  92.6 7.3 %collective-permute-start.19 = (bf16[2,64,512]{2,1,0:T(8,128)(2,1)}, bf16[2,64,512]{2,1,0:T(8,128)(2,1)}, u32[]{:S(2)}, u32[]{:S(2)}) collective-permute-start(bf16[2,64,512]{2,1,0:T(8,128)(2,1)} %collective-permute-done.17.refs_16_), channel_id=1, source_target_pairs={{0,4},{5,1},{4,8},{9,5},{8,12},{13,9},{12,14},{15,13},{14,10},{11,... | collective-permute-start | bytes 393224 | tf_op jit(solution)/shard_map/ppermute | solution.py:92
  94.1 27.2 %collective-permute-start.53 = (bf16[16,2,32,512]{3,2,1,0:T(8,128)(2,1)S(1)}, bf16[16,2,32,512]{3,2,1,0:T(8,128)(2,1)}, u32[]{:S(2)}, u32[]{:S(2)}) collective-permute-start(bf16[16,2,32,512]{3,2,1,0:T(8,128)(2,1)S(1)} %all-to-all-done.refs_52_), channel_id=1, source_target_pairs={{0,16},{16,0},{1,17},{17,1},{2,18},{18,2},{3,19},{19,3},{4,20},{20... | collective-permute-start | bytes 3145736 | tf_op jit(solution)/shard_map/ppermute | solution.py:123
  98.8 5.2 %collective-permute-start.22 = (bf16[2,64,512]{2,1,0:T(8,128)(2,1)}, bf16[2,64,512]{2,1,0:T(8,128)(2,1)S(1)}, u32[]{:S(2)}, u32[]{:S(2)}) collective-permute-start(bf16[2,64,512]{2,1,0:T(8,128)(2,1)} %collective-permute-done.20.refs_19_), channel_id=1, source_target_pairs={{0,4},{5,1},{4,8},{9,5},{8,12},{13,9},{12,14},{15,13},{14,10},{11,... | collective-permute-start | bytes 393224 | tf_op jit(solution)/shard_map/ppermute | solution.py:92
  99.9 5.4 %collective-permute-start.21 = (bf16[2,64,512]{2,1,0:T(8,128)(2,1)}, bf16[2,64,512]{2,1,0:T(8,128)(2,1)S(1)}, u32[]{:S(2)}, u32[]{:S(2)}) collective-permute-start(bf16[2,64,512]{2,1,0:T(8,128)(2,1)} %collective-permute-done.19.refs_18_), channel_id=1, source_target_pairs={{0,4},{5,1},{4,8},{9,5},{8,12},{13,9},{12,14},{15,13},{14,10},{11,... | collective-permute-start | bytes 393224 | tf_op jit(solution)/shard_map/ppermute | solution.py:92
  101.9 5.9 %collective-permute-start.46 = (bf16[2,64,512]{2,1,0:T(8,128)(2,1)}, bf16[2,64,512]{2,1,0:T(8,128)(2,1)S(1)}, u32[]{:S(2)}, u32[]{:S(2)}) collective-permute-start(bf16[2,64,512]{2,1,0:T(8,128)(2,1)} %collective-permute-done.20.refs_19_), channel_id=1, source_target_pairs={{0,1},{1,0},{2,3},{3,2},{4,5},{5,4},{6,7},{7,6},{8,9},{9,8},{10,11... | collective-permute-start | bytes 393224 | tf_op jit(solution)/shard_map/ppermute | solution.py:93
  102.0 5.9 %collective-permute-start.45 = (bf16[2,64,512]{2,1,0:T(8,128)(2,1)}, bf16[2,64,512]{2,1,0:T(8,128)(2,1)S(1)}, u32[]{:S(2)}, u32[]{:S(2)}) collective-permute-start(bf16[2,64,512]{2,1,0:T(8,128)(2,1)} %collective-permute-done.19.refs_18_), channel_id=1, source_target_pairs={{0,1},{1,0},{2,3},{3,2},{4,5},{5,4},{6,7},{7,6},{8,9},{9,8},{10,11... | collective-permute-start | bytes 393224 | tf_op jit(solution)/shard_map/ppermute | solution.py:93
  104.0 5.1 %collective-permute-start.24 = (bf16[2,64,512]{2,1,0:T(8,128)(2,1)S(1)}, bf16[2,64,512]{2,1,0:T(8,128)(2,1)}, u32[]{:S(2)}, u32[]{:S(2)}) collective-permute-start(bf16[2,64,512]{2,1,0:T(8,128)(2,1)S(1)} %collective-permute-done.22.refs_21_), channel_id=1, source_target_pairs={{0,4},{5,1},{4,8},{9,5},{8,12},{13,9},{12,14},{15,13},{14,10},{11,... | collective-permute-start | bytes 393224 | tf_op jit(solution)/shard_map/ppermute | solution.py:92
  105.4 5.1 %collective-permute-start.23 = (bf16[2,64,512]{2,1,0:T(8,128)(2,1)S(1)}, bf16[2,64,512]{2,1,0:T(8,128)(2,1)}, u32[]{:S(2)}, u32[]{:S(2)}) collective-permute-start(bf16[2,64,512]{2,1,0:T(8,128)(2,1)S(1)} %collective-permute-done.21.refs_20_), channel_id=1, source_target_pairs={{0,4},{5,1},{4,8},{9,5},{8,12},{13,9},{12,14},{15,13},{14,10},{11,... | collective-permute-start | bytes 393224 | tf_op jit(solution)/shard_map/ppermute | solution.py:92
  107.8 5.1 %collective-permute-start.48 = (bf16[2,64,512]{2,1,0:T(8,128)(2,1)S(1)}, bf16[2,64,512]{2,1,0:T(8,128)(2,1)S(1)}, u32[]{:S(2)}, u32[]{:S(2)}) collective-permute-start(bf16[2,64,512]{2,1,0:T(8,128)(2,1)S(1)} %collective-permute-done.22.refs_21_), channel_id=1, source_target_pairs={{0,1},{1,0},{2,3},{3,2},{4,5},{5,4},{6,7},{7,6},{8,9},{9,8},{10,11... | collective-permute-start | bytes 393224 | tf_op jit(solution)/shard_map/ppermute | solution.py:93
  107.9 5.1 %collective-permute-start.47 = (bf16[2,64,512]{2,1,0:T(8,128)(2,1)S(1)}, bf16[2,64,512]{2,1,0:T(8,128)(2,1)S(1)}, u32[]{:S(2)}, u32[]{:S(2)}) collective-permute-start(bf16[2,64,512]{2,1,0:T(8,128)(2,1)S(1)} %collective-permute-done.21.refs_20_), channel_id=1, source_target_pairs={{0,1},{1,0},{2,3},{3,2},{4,5},{5,4},{6,7},{7,6},{8,9},{9,8},{10,11... | collective-permute-start | bytes 393224 | tf_op jit(solution)/shard_map/ppermute | solution.py:93
  109.1 5.3 %collective-permute-start.26 = (bf16[2,64,512]{2,1,0:T(8,128)(2,1)}, bf16[2,64,512]{2,1,0:T(8,128)(2,1)}, u32[]{:S(2)}, u32[]{:S(2)}) collective-permute-start(bf16[2,64,512]{2,1,0:T(8,128)(2,1)} %collective-permute-done.24.refs_23_), channel_id=1, source_target_pairs={{0,4},{5,1},{4,8},{9,5},{8,12},{13,9},{12,14},{15,13},{14,10},{11,... | collective-permute-start | bytes 393224 | tf_op jit(solution)/shard_map/ppermute | solution.py:92
  110.5 5.3 %collective-permute-start.25 = (bf16[2,64,512]{2,1,0:T(8,128)(2,1)}, bf16[2,64,512]{2,1,0:T(8,128)(2,1)}, u32[]{:S(2)}, u32[]{:S(2)}) collective-permute-start(bf16[2,64,512]{2,1,0:T(8,128)(2,1)} %collective-permute-done.23.refs_22_), channel_id=1, source_target_pairs={{0,4},{5,1},{4,8},{9,5},{8,12},{13,9},{12,14},{15,13},{14,10},{11,... | collective-permute-start | bytes 393224 | tf_op jit(solution)/shard_map/ppermute | solution.py:92
  112.9 8.4 %collective-permute-start.50 = (bf16[2,64,512]{2,1,0:T(8,128)(2,1)}, bf16[2,64,512]{2,1,0:T(8,128)(2,1)}, u32[]{:S(2)}, u32[]{:S(2)}) collective-permute-start(bf16[2,64,512]{2,1,0:T(8,128)(2,1)} %collective-permute-done.24.refs_23_), channel_id=1, source_target_pairs={{0,1},{1,0},{2,3},{3,2},{4,5},{5,4},{6,7},{7,6},{8,9},{9,8},{10,11... | collective-permute-start | bytes 393224 | tf_op jit(solution)/shard_map/ppermute | solution.py:93
  113.0 8.3 %collective-permute-start.49 = (bf16[2,64,512]{2,1,0:T(8,128)(2,1)}, bf16[2,64,512]{2,1,0:T(8,128)(2,1)}, u32[]{:S(2)}, u32[]{:S(2)}) collective-permute-start(bf16[2,64,512]{2,1,0:T(8,128)(2,1)} %collective-permute-done.23.refs_22_), channel_id=1, source_target_pairs={{0,1},{1,0},{2,3},{3,2},{4,5},{5,4},{6,7},{7,6},{8,9},{9,8},{10,11... | collective-permute-start | bytes 393224 | tf_op jit(solution)/shard_map/ppermute | solution.py:93
  114.3 7.0 %collective-permute-start.52 = (bf16[2,64,512]{2,1,0:T(8,128)(2,1)}, bf16[2,64,512]{2,1,0:T(8,128)(2,1)}, u32[]{:S(2)}, u32[]{:S(2)}) collective-permute-start(bf16[2,64,512]{2,1,0:T(8,128)(2,1)} %collective-permute-done.26.refs_25_), channel_id=1, source_target_pairs={{0,1},{1,0},{2,3},{3,2},{4,5},{5,4},{6,7},{7,6},{8,9},{9,8},{10,11... | collective-permute-start | bytes 393224 | tf_op jit(solution)/shard_map/ppermute | solution.py:93
  115.7 5.6 %collective-permute-start.51 = (bf16[2,64,512]{2,1,0:T(8,128)(2,1)}, bf16[2,64,512]{2,1,0:T(8,128)(2,1)}, u32[]{:S(2)}, u32[]{:S(2)}) collective-permute-start(bf16[2,64,512]{2,1,0:T(8,128)(2,1)} %collective-permute-done.25.refs_24_), channel_id=1, source_target_pairs={{0,1},{1,0},{2,3},{3,2},{4,5},{5,4},{6,7},{7,6},{8,9},{9,8},{10,11... | collective-permute-start | bytes 393224 | tf_op jit(solution)/shard_map/ppermute | solution.py:93
  (46 other events, 757.1 us)

commit v3 on v2

v3 whole, which is shorter than its diff:
```python
import functools

import jax
import jax.numpy as jnp
import numpy as np
from jax import lax
from jax.experimental import pallas as pl
from jax.experimental.pallas import tpu as pltpu
from jax.sharding import PartitionSpec as P

DET = 3
ROWS = 512
COLS = 512
RADIX = 4
PART = 128
ROW_STEP = 16
WAVE_ROWS = 32
HALF_CHUNKS = 2
LAG = 2
CORES = 2


two_pi = 6.283185307179586
eps_norm = 1e-06


def turn_table(left_ids, right_ids, period):
    angles = (left_ids[:, None] * right_ids[None, :] % period).astype(np.float64) * (2 * np.pi / period)
    return np.cos(angles), np.sin(angles)


def tables():
    part_ids, col_ids = np.arange(PART), np.arange(COLS)
    row_tables, col_tables, turns = [], [], []
    for residue in range(RADIX):
        cos, sin = turn_table(RADIX * part_ids + residue, part_ids, ROWS)
        row_tables.append(np.block([[cos, -sin], [sin, cos]]))
        col_tables.append(np.block([[cos.T, sin.T], [-sin.T, cos.T]]))
        turns.append(np.stack(turn_table(RADIX * part_ids + residue, col_ids, ROWS * COLS)))
    return (
        jnp.asarray(np.stack(row_tables), jnp.float32).astype(jnp.bfloat16),
        jnp.asarray(np.stack(col_tables), jnp.float32).astype(jnp.bfloat16),
        jnp.asarray(np.stack(turns), jnp.float32),
    )


def slide_turns(slides):
    total = ROWS * COLS
    row_turns = (jnp.arange(ROWS, dtype=jnp.int32)[None, :] * (COLS * slides % total)[:, None]) % total
    col_turns = (jnp.arange(COLS, dtype=jnp.int32)[None, :] * slides[:, None]) % total
    row_angles = row_turns.astype(jnp.float32) * (two_pi / total)
    col_angles = col_turns.astype(jnp.float32) * (two_pi / total)
    rows = jnp.stack([jnp.cos(row_angles), jnp.sin(row_angles)], 1)[..., None]
    cols = jnp.stack([jnp.cos(col_angles), jnp.sin(col_angles)], 1)[:, :, None, :]
    return rows, cols


def ring_order(chips):
    return list(range(0, chips, 2)) + list(range(chips - 1 - chips % 2, 0, -2))


def spread(strain_slots, owner):
    devices = lax.axis_size("tpl")
    chips = devices // CORES
    order = ring_order(chips)
    chip, core = lax.axis_index("tpl") // CORES, lax.axis_index("tpl") % CORES
    half = ROWS * COLS // CORES
    bins = half // HALF_CHUNKS
    to_partner = [(i, i ^ 1) for i in range(devices)]
    along = []
    for at in range(chips):
        along.append((order[at] * CORES, order[(at + 1) % chips] * CORES))
        along.append((order[(at + 1) % chips] * CORES + 1, order[at] * CORES + 1))
    on_owner_core = core == owner % CORES
    on_owner_chip = chip == owner // CORES
    chunks = []
    for det in range(DET):
        side = lambda which: lax.dynamic_slice(strain_slots, (0, det, 0, which * half), (1, 1, 2, half))[0, 0]
        got = lax.ppermute(side(1 - core), "tpl", to_partner)
        first = jnp.where(on_owner_core, side(core), got)
        strain_slots, first = lax.optimization_barrier((strain_slots, first))
        for at in range(HALF_CHUNKS):
            chunks.append(first[:, bins * at : bins * (at + 1)].reshape(2, bins // COLS, COLS))
    sent, arrived = [], []
    count = len(chunks)
    for slot in range(count + LAG * (chips - 1)):
        if slot < LAG:
            here = chunks[slot]
        elif slot < count:
            here = jnp.where(on_owner_chip, chunks[slot], arrived[slot - LAG])
        else:
            here = arrived[slot - LAG]
        sent.append(here)
        if slot < count + LAG * (chips - 2):
            arrived.append(lax.ppermute(here, "tpl", along))
    shared = [lax.ppermute(here, "tpl", to_partner) for here in sent]
    place = lambda at: jnp.where(at % 2 == 0, at // 2, chips - 1 - at // 2)
    forward = (place(chip) - place(owner // CORES)) % chips
    backward = (place(owner // CORES) - place(chip)) % chips
    near = jnp.where(core == 0, forward, backward)
    far = jnp.where(core == 0, backward, forward)
    return sent, shared, [core, near, far]


def pick_kernel(list_ref, group_ref, templates_ref, picked_ref, sem):
    devices = picked_ref.shape[0]
    for device in range(devices):
        which = list_ref[device, group_ref[0]]
        pltpu.make_async_copy(templates_ref.at[which], picked_ref.at[device], sem).start()
    pltpu.make_async_copy(picked_ref, picked_ref, sem).wait()


def pick(templates, lists, own_group):
    devices = lists.shape[0]
    smem, hbm = pl.BlockSpec(memory_space=pltpu.SMEM), pl.BlockSpec(memory_space=pl.ANY)
    return pl.pallas_call(
        pick_kernel,
        out_shape=jax.ShapeDtypeStruct((devices, *templates.shape[1:]), templates.dtype),
        in_specs=[smem, smem, hbm],
        out_specs=hbm,
        scratch_shapes=[pltpu.SemaphoreType.DMA],
        compiler_params=pltpu.CompilerParams(vmem_limit_bytes=56 * 1024 * 1024),
    )(lists, own_group.reshape(1).astype(jnp.int32), templates)


def collect(templates, lists):
    devices, groups = lax.axis_size("tpl"), lax.axis_size("grp")
    own_group = lax.axis_index("grp")
    per_device = lists.shape[1]
    rows = templates.shape[2] // COLS
    pieces = per_device * 2
    if pieces % groups:
        groups, own_group = 1, jnp.int32(0)
    size = pieces // groups
    direct = size == 2 and rows == WAVE_ROWS
    if direct:
        picked = pick(templates, lists, own_group).reshape(devices, size, rows, COLS)
    else:
        picked = templates[lists.reshape(-1)].reshape(devices, pieces, rows, COLS)
        picked = lax.dynamic_slice_in_dim(picked, own_group * size, size, 1)
    own = lax.all_to_all(picked, "tpl", split_axis=0, concat_axis=0, tiled=True)
    found = [own]
    for turn in range(1, groups):
        found.append(lax.ppermute(own, "grp", [(i, (i + turn) % groups) for i in range(groups)]))
    if direct:
        return found, [(own_group - turn) % groups for turn in range(groups)]
    found = jnp.stack(found)[(own_group - jnp.arange(groups)) % groups]
    found = found.transpose(0, 2, 1, 3, 4).reshape(per_device, 2, ROWS // WAVE_ROWS, WAVE_ROWS, COLS)
    return [found[at].transpose(1, 0, 2, 3) for at in range(per_device)], [jnp.int32(at) for at in range(per_device)]


def held(values):
    return values.astype(jnp.bfloat16).astype(jnp.float32)


def quarters(parts):
    (re0, im0), (re1, im1), (re2, im2), (re3, im3) = parts
    even_re, even_im, odd_re, odd_im = re0 + re2, im0 + im2, re1 + re3, im1 + im3
    left_re, left_im, right_re, right_im = re0 - re2, im0 - im2, re1 - re3, im1 - im3
    return (
        (even_re + odd_re, even_im + odd_im),
        (left_re - right_im, left_im + right_re),
        (even_re - odd_re, even_im - odd_im),
        (left_re + right_im, left_im - right_re),
    )


def filter_kernel(chips, count, cut_ref, list_ref, where_ref, *refs):
    slots = DET * HALF_CHUNKS + LAG * (chips - 1)
    near_refs, refs = refs[:slots], refs[slots:]
    far_refs, refs = refs[:slots], refs[slots:]
    wave_refs, refs = refs[:count], refs[count:]
    (rphase_ref, cphase_ref, row_hbm, col_hbm, twiddle_hbm, peaks_ref, norms_ref,
     strain_ref, wave_ref, row_ref, col_ref, twiddle_ref, slid, masked, stacked, twisted, power, sigma,
     strain_sem, wave_sem, table_sem) = refs
    core, near, far, own = where_ref[0], where_ref[1], where_ref[2], where_ref[3]
    half = ROWS // CORES
    rows = half // HALF_CHUNKS

    table_copies = [
        pltpu.make_async_copy(row_hbm, row_ref, table_sem.at[0]),
        pltpu.make_async_copy(twiddle_hbm, twiddle_ref, table_sem.at[1]),
        pltpu.make_async_copy(col_hbm, col_ref, table_sem.at[2]),
    ]
    wave_copies = [pltpu.make_async_copy(wave_refs[at], wave_ref.at[at], wave_sem.at[at]) for at in range(count)]

    def start_chunks(det):
        for slot_refs, distance, side in ((near_refs, near, core), (far_refs, far, 1 - core)):
            for away in range(chips):
                @pl.when(distance == away)
                def _():
                    for at in range(HALF_CHUNKS):
                        into = pl.ds(pl.multiple_of(side * half + at * rows, rows), rows)
                        copy = pltpu.make_async_copy(
                            slot_refs[det * HALF_CHUNKS + at + LAG * away],
                            strain_ref.at[det, :, into, :],
                            strain_sem.at[det],
                        )
                        copy.start()

    for copy in wave_copies:
        copy.start()
    start_chunks(0)
    for copy in table_copies:
        copy.start()
    for det in range(1, DET):
        start_chunks(det)

    for tpl in range(count):
        wave_copies[tpl].wait()
        cutoff = cut_ref[list_ref[own, where_ref[4 + tpl]]]
        total = jnp.zeros((8, COLS), jnp.float32)
        for block in range(ROWS // WAVE_ROWS):
            bins = (lax.broadcasted_iota(jnp.int32, (WAVE_ROWS, COLS), 0) + block * WAVE_ROWS) * COLS
            bins = bins + lax.broadcasted_iota(jnp.int32, (WAVE_ROWS, COLS), 1)
            inside = bins < cutoff
            wave_re = jnp.where(inside, wave_ref[tpl, block, 0].astype(jnp.float32), 0.0)
            wave_im = jnp.where(inside, wave_ref[tpl, block, 1].astype(jnp.float32), 0.0)
            part = slice(block * WAVE_ROWS, (block + 1) * WAVE_ROWS)
            masked[tpl, 0, part, :] = wave_re.astype(jnp.bfloat16)
            masked[tpl, 1, part, :] = wave_im.astype(jnp.bfloat16)
            squares = wave_re * wave_re + wave_im * wave_im
            total = total + jnp.sum(squares.reshape(-1, 8, COLS), axis=0)
        sigma[tpl] = jnp.sum(total)

    for copy in table_copies:
        copy.wait()

    def one(det, tpl):
        for at in range(0, PART, ROW_STEP):
            for col_at in range(0, COLS, PART):
                cols = slice(col_at, col_at + PART)
                parts = []
                for quarter in range(RADIX):
                    spot = slice(quarter * PART + at, quarter * PART + at + ROW_STEP)
                    wave_re = masked[tpl, 0, spot, cols].astype(jnp.float32)
                    wave_im = masked[tpl, 1, spot, cols].astype(jnp.float32)
                    data_re, data_im = slid[0, spot, cols], slid[1, spot, cols]
                    parts.append((held(data_re * wave_re + data_im * wave_im), held(data_im * wave_re - data_re * wave_im)))
                for residue, (re, im) in enumerate(quarters(parts)):
                    stacked[residue, at : at + ROW_STEP, cols] = re.astype(jnp.bfloat16)
                    stacked[residue, PART + at : PART + at + ROW_STEP, cols] = im.astype(jnp.bfloat16)
        for residue in range(RADIX):
            section = jnp.dot(row_ref[residue], stacked[residue], preferred_element_type=jnp.float32)
            for at in range(0, PART, ROW_STEP):
                parts = []
                for quarter in range(RADIX):
                    cols = slice(quarter * PART, (quarter + 1) * PART)
                    re, im = section[at : at + ROW_STEP, cols], section[PART + at : PART + at + ROW_STEP, cols]
                    turn_re = twiddle_ref[residue, 0, at : at + ROW_STEP, cols]
                    turn_im = twiddle_ref[residue, 1, at : at + ROW_STEP, cols]
                    parts.append((held(re * turn_re - im * turn_im), held(re * turn_im + im * turn_re)))
                spot = slice(residue * PART + at, residue * PART + at + ROW_STEP)
                for other, (re, im) in enumerate(quarters(parts)):
                    twisted[other, spot, :PART] = re.astype(jnp.bfloat16)
                    twisted[other, spot, PART:] = im.astype(jnp.bfloat16)
        for other in range(RADIX):
            series = jnp.dot(twisted[other], col_ref[other], preferred_element_type=jnp.float32)
            squares = series[:, :PART] * series[:, :PART] + series[:, PART:] * series[:, PART:]
            cols = slice(other * PART, (other + 1) * PART)
            power[tpl, :, cols] = jnp.where(det == 0, squares, power[tpl, :, cols] + squares)

    @pl.loop(0, DET)
    def _(det):
        pltpu.make_async_copy(strain_ref.at[det], strain_ref.at[det], strain_sem.at[det]).wait()
        rc, rs = rphase_ref[det, 0], rphase_ref[det, 1]
        cc, cs = cphase_ref[det, 0], cphase_ref[det, 1]
        for at in range(0, ROWS, PART):
            part = slice(at, at + PART)
            turn_re = rc[part] * cc - rs[part] * cs
            turn_im = rc[part] * cs + rs[part] * cc
            data_re = strain_ref[det, 0, part, :].astype(jnp.float32)
            data_im = strain_ref[det, 1, part, :].astype(jnp.float32)
            slid[0, part, :] = data_re * turn_re - data_im * turn_im
            slid[1, part, :] = data_re * turn_im + data_im * turn_re

        @pl.loop(0, count)
        def _(tpl):
            one(det, tpl)

    for tpl in range(count):
        largest = jnp.max(power[tpl])
        place = where_ref[4 + tpl]
        peaks_ref[place] = largest / (2.0 * (sigma[tpl] + eps_norm))
        norms_ref[place] = sigma[tpl] / (ROWS * COLS)


def filtered(sent, shared, where, chips, waves, cutoffs, lists, turns):
    count = len(waves)
    rows, cols = turns
    row_table, col_table, twiddle = tables()
    smem = pl.BlockSpec(memory_space=pltpu.SMEM)
    vmem = pl.BlockSpec(memory_space=pltpu.VMEM)
    hbm = pl.BlockSpec(memory_space=pl.ANY)
    operands = [*sent, *shared, *waves]
    return pl.pallas_call(
        functools.partial(filter_kernel, chips, count),
        out_shape=(jax.ShapeDtypeStruct((count,), jnp.float32),) * 2,
        in_specs=[smem, smem, smem] + [hbm] * len(operands) + [vmem, vmem, hbm, hbm, hbm],
        out_specs=(smem, smem),
        scratch_shapes=[
            pltpu.VMEM((DET, 2, ROWS, COLS), jnp.bfloat16),
            pltpu.VMEM((count, ROWS // WAVE_ROWS, 2, WAVE_ROWS, COLS), jnp.bfloat16),
            pltpu.VMEM(row_table.shape, jnp.bfloat16),
            pltpu.VMEM(col_table.shape, jnp.bfloat16),
            pltpu.VMEM(twiddle.shape, jnp.float32),
            pltpu.VMEM((2, ROWS, COLS), jnp.float32),
            pltpu.VMEM((count, 2, ROWS, COLS), jnp.bfloat16),
            pltpu.VMEM((RADIX, 2 * PART, COLS), jnp.bfloat16),
            pltpu.VMEM((RADIX, ROWS, 2 * PART), jnp.bfloat16),
            pltpu.VMEM((count, ROWS, COLS), jnp.float32),
            pltpu.SMEM((count,), jnp.float32),
            pltpu.SemaphoreType.DMA((DET,)),
            pltpu.SemaphoreType.DMA((count,)),
            pltpu.SemaphoreType.DMA((3,)),
        ],
        compiler_params=pltpu.CompilerParams(vmem_limit_bytes=56 * 1024 * 1024),
    )(cutoffs, lists, where, *operands, rows, cols, row_table, col_table, twiddle)


def body(strain_slots, templates, cutoffs, lists, owner, slides):
    devices = lax.axis_size("tpl")
    sent, shared, where = spread(strain_slots, owner[0])
    waves, places = collect(templates, lists)
    where = jnp.stack([jnp.asarray(at, jnp.int32) for at in (*where, lax.axis_index("tpl"), *places)])
    return filtered(sent, shared, where, devices // CORES, waves, cutoffs, lists, slide_turns(slides))


def solution(mesh):
    in_specs = (
        P(("grp", "tpl"), None, None, None),
        P(None, None, "tpl"),
        P(),
        P(),
        P("grp"),
        P("grp"),
    )
    out_specs = (P(("grp", "tpl")), P(("grp", "tpl")))
    return jax.shard_map(body, mesh=mesh, in_specs=in_specs, out_specs=out_specs, check_vma=False)
```

time: 150 us -> 153 us (1.020)
  Pallas kernels: 26.5 us -> 52.1 us
  starting transfers between devices: 54.8 us -> 43.1 us
  local copies, waits for them, and re-layouts: 21.9 us -> 12.7 us
  other arithmetic: 12.7 us -> 3.57 us
  waiting for transfers between devices: 31.2 us -> 38.6 us
    pallas_call x0 -> x1, Pallas kernels: none -> 33.7 us  [pick(): pl.pallas_call(pick_kernel, out_shape=jax.ShapeDtypeStruct((devices, *tem...]
    ppermute x24 -> x18, starting transfers between devices: 42.4 us -> 29.5 us  [spread(): arrived.append(lax.ppermute(here, 'tpl', along))]
    pallas_call x1, Pallas kernels: 26.5 us -> 18.4 us  [filtered(): pl.pallas_call(functools.partial(filter_kernel, chips, count), out_shape=...]
    ppermute x24 -> x18, waiting for transfers between devices: 31.1 us -> 37.6 us  [spread(): arrived.append(lax.ppermute(here, 'tpl', along))]
    gather x3 -> x0, local copies, waits for them, and re-layouts: 5.13 us -> none  [the longest x1 2.66 us: collect(): picked = templates[ids.reshape(-1)].reshape(devices, each * 2, rows, COLS)]
    slice x2 -> x3, local copies, waits for them, and re-layouts: 4.67 us -> 1.09 us  [spread(): first[:, bins * at:bins * (at + 1)].reshape(2, bins // COLS, COLS)]
    dynamic_slice x4 -> x0, local copies, waits for them, and re-layouts: 3.43 us -> none  [the longest x3 2.57 us: spread(): theirs = lax.dynamic_slice_in_dim(own[det], (1 - core) * half, half, 1)]
    squeeze x0 -> x3, local copies, waits for them, and re-layouts: none -> 3.19 us  [spread(): lax.dynamic_slice(strain_slots, (0, det, 0, which * half), (1, 1, 2, half))]
  transfers between devices with their start and end apart: 55 -> 43, of which waited for: 19 -> 17; matrix products, arithmetic and copies ran while one was open for 17% -> 9% of each run, Pallas kernels for 0% -> 22%
where the time goes in v3:
time: 153 us; the launch traced here: 152 us
  Pallas kernels  52.1 us (34%)
  starting transfers between devices  43.1 us (28%)
  waiting for transfers between devices  38.6 us (25%)
  local copies, waits for them, and re-layouts  12.7 us (8%)
  other arithmetic  3.57 us (2%)
  between operations  2.07 us (1%)
    ppermute x18, waiting for transfers between devices, spread(): arrived.append(lax.ppermute(here, 'tpl', along))  37.6 us
    pallas_call x1, Pallas kernels, pick(): pl.pallas_call(pick_kernel, out_shape=jax.ShapeDtypeStruct((devices, *tem...  33.7 us
    ppermute x18, starting transfers between devices, spread(): arrived.append(lax.ppermute(here, 'tpl', along))  29.5 us
    pallas_call x1, Pallas kernels, filtered(): pl.pallas_call(functools.partial(filter_kernel, chips, count), out_shape=...  18.4 us
    all_to_all x1, starting transfers between devices, collect(): own = lax.all_to_all(picked, 'tpl', split_axis=0, concat_axis=0, tiled=True)  7.05 us
    ppermute x20, starting transfers between devices, spread(): shared = [lax.ppermute(here, 'tpl', to_partner) for here in sent]  3.96 us
    squeeze x3, local copies, waits for them, and re-layouts, spread(): lax.dynamic_slice(strain_slots, (0, det, 0, which * half), (1, 1, 2, half))  3.19 us
  transfers between devices with their start and end apart: 43, of which 17 were waited for; matrix products, arithmetic and copies ran while one was open for 9% of the time, Pallas kernels for 22%

profile of v3, /device:TPU:0, one launch (start us, length us, event | category | flops | bytes accessed | tf_op | source)
XLA Modules:
  0.0 152.1 jit_solution(2557125840703416468)
XLA Ops:
  0.6 1.4 dynamic-slice_bitcast_fusion.2
  2.6 1.3 copy.12.list_ref
  3.9 33.7 %shard_map.104 = bf16[16,2,16384]{2,1,0:T(2,128)(2,1)} custom-call(s32[16,2]{1,0:T(8,128)} %copy.12.list_ref, s32[1]{0:T(128)} %bitcast.13.group_ref, bf16[32,2,16384]{2,1,0:T(2,128)(2,1)} %templates_ref.1), custom_call_target="tpu_custom_call" | custom-call | tf_op jit(solution)/shard_map/pallas_call | solution.py:116
  37.6 2.6 %reshape.217 = bf16[16,2,32,512]{3,2,1,0:T(8,128)(2,1)} reshape(bf16[16,2,16384]{2,1,0:T(2,128)(2,1)} %shard_map.104) | data formatting | bytes 2097152 | tf_op jit(solution)/shard_map/reshape | solution.py:137
  40.2 7.0 %all-to-all-start = ((bf16[16,2,32,512]{3,2,1,0:T(8,128)(2,1)}), bf16[16,2,32,512]{3,2,1,0:T(8,128)(2,1)S(1)}, u32[]{:S(2)}, u32[]{:S(2)}) async-start(bf16[16,2,32,512]{3,2,1,0:T(8,128)(2,1)} %reshape.217), calls=%async_computation | async-start | bytes 2097152 | tf_op jit(solution)/shard_map/all_to_all | solution.py:141
  48.0 1.7 %broadcast_select_fusion.2 = bf16[2,131072]{1,0:T(2,128)(2,1)S(1)} fusion(bf16[2,131072]{1,0:T(2,128)(2,1)S(1)} %collective-permute-done, pred[]{:T(512)S(6)} %eq.37, bf16[1,3,2,262144]{3,2,1,0:T(2,128)(2,1)} %param.9, s32[]{:T(128)S(6)} %select_n.175), kind=kLoop, calls=%fused_computation.2 | loop fusion | flops 262144 | bytes 1572869 | tf_op jit(solution)/shard_map/jit(_where)/select_n | solution.py:80
  49.7 1.4 dynamic-slice_bitcast_fusion.1
  52.0 1.7 %collective-permute-start.2 = (bf16[2,128,512]{2,1,0:T(8,128)(2,1)S(1)}, bf16[2,128,512]{2,1,0:T(8,128)(2,1)S(1)}, u32[]{:S(2)}, u32[]{:S(2)}) collective-permute-start(bf16[2,128,512]{2,1,0:T(8,128)(2,1)S(1)} %bitcast.49), channel_id=1, source_target_pairs={{0,4},{5,1},{4,8},{9,5},{8,12},{13,9},{12,14},{15,13},{14,10},{11,... | collective-permute-start | bytes 786440 | tf_op jit(solution)/shard_map/ppermute | solution.py:95
  53.8 1.5 collective-permute-start.3
  55.2 0.5 broadcast_select_fusion.1
  56.6 11.5 %collective-permute-done.2 = bf16[2,128,512]{2,1,0:T(8,128)(2,1)S(1)} collective-permute-done((bf16[2,128,512]{2,1,0:T(8,128)(2,1)S(1)}, bf16[2,128,512]{2,1,0:T(8,128)(2,1)S(1)}, u32[]{:S(2)}, u32[]{:S(2)}) %collective-permute-start.2) | collective-permute-done | bytes 262176 | tf_op jit(solution)/shard_map/ppermute | solution.py:95
  68.2 7.2 %collective-permute-start.5 = (bf16[2,128,512]{2,1,0:T(8,128)(2,1)S(1)}, bf16[2,128,512]{2,1,0:T(8,128)(2,1)S(1)}, u32[]{:S(2)}, u32[]{:S(2)}) collective-permute-start(bf16[2,128,512]{2,1,0:T(8,128)(2,1)S(1)} %bitcast_select_fusion.3.refs_2_), channel_id=1, source_target_pairs={{0,4},{5,1},{4,8},{9,5},{8,12},{13,9},{12,14},{15,13},{14,10},{11,... | collective-permute-start | bytes 786440 | tf_op jit(solution)/shard_map/ppermute | solution.py:95
  75.4 2.8 %collective-permute-start.6 = (bf16[2,128,512]{2,1,0:T(8,128)(2,1)S(1)}, bf16[2,128,512]{2,1,0:T(8,128)(2,1)S(1)}, u32[]{:S(2)}, u32[]{:S(2)}) collective-permute-start(bf16[2,128,512]{2,1,0:T(8,128)(2,1)S(1)} %bitcast_select_fusion.2.refs_3_), channel_id=1, source_target_pairs={{0,4},{5,1},{4,8},{9,5},{8,12},{13,9},{12,14},{15,13},{14,10},{11,... | collective-permute-start | bytes 786440 | tf_op jit(solution)/shard_map/ppermute | solution.py:95
  79.3 2.5 %collective-permute-start.7 = (bf16[2,128,512]{2,1,0:T(8,128)(2,1)S(1)}, bf16[2,128,512]{2,1,0:T(8,128)(2,1)S(1)}, u32[]{:S(2)}, u32[]{:S(2)}) collective-permute-start(bf16[2,128,512]{2,1,0:T(8,128)(2,1)S(1)} %bitcast_select_fusion.1.refs_4_), channel_id=1, source_target_pairs={{0,4},{5,1},{4,8},{9,5},{8,12},{13,9},{12,14},{15,13},{14,10},{11,... | collective-permute-start | bytes 786440 | tf_op jit(solution)/shard_map/ppermute | solution.py:95
  82.1 2.5 %collective-permute-start.8 = (bf16[2,128,512]{2,1,0:T(8,128)(2,1)S(1)}, bf16[2,128,512]{2,1,0:T(8,128)(2,1)S(1)}, u32[]{:S(2)}, u32[]{:S(2)}) collective-permute-start(bf16[2,128,512]{2,1,0:T(8,128)(2,1)S(1)} %bitcast_select_fusion.refs_5_), channel_id=1, source_target_pairs={{0,4},{5,1},{4,8},{9,5},{8,12},{13,9},{12,14},{15,13},{14,10},{11,... | collective-permute-start | bytes 786440 | tf_op jit(solution)/shard_map/ppermute | solution.py:95
  85.2 2.3 %collective-permute-done.7.refs_6_ = bf16[2,128,512]{2,1,0:T(8,128)(2,1)S(1)} collective-permute-done((bf16[2,128,512]{2,1,0:T(8,128)(2,1)S(1)}, bf16[2,128,512]{2,1,0:T(8,128)(2,1)S(1)}, u32[]{:S(2)}, u32[]{:S(2)}) %collective-permute-start.7) | collective-permute-done | bytes 262176 | tf_op jit(solution)/shard_map/ppermute | solution.py:95
  87.6 0.6 collective-permute-start.9
  88.2 2.2 %collective-permute-done.8.refs_7_ = bf16[2,128,512]{2,1,0:T(8,128)(2,1)S(1)} collective-permute-done((bf16[2,128,512]{2,1,0:T(8,128)(2,1)S(1)}, bf16[2,128,512]{2,1,0:T(8,128)(2,1)S(1)}, u32[]{:S(2)}, u32[]{:S(2)}) %collective-permute-start.8) | collective-permute-done | bytes 262176 | tf_op jit(solution)/shard_map/ppermute | solution.py:95
  90.4 0.6 collective-permute-start.10
  91.6 2.4 %collective-permute-done.9.refs_8_ = bf16[2,128,512]{2,1,0:T(8,128)(2,1)} collective-permute-done((bf16[2,128,512]{2,1,0:T(8,128)(2,1)S(1)}, bf16[2,128,512]{2,1,0:T(8,128)(2,1)}, u32[]{:S(2)}, u32[]{:S(2)}) %collective-permute-start.9) | collective-permute-done | bytes 262176 | tf_op jit(solution)/shard_map/ppermute | solution.py:95
  94.1 0.6 collective-permute-start.11
  94.7 2.1 %collective-permute-done.10.refs_9_ = bf16[2,128,512]{2,1,0:T(8,128)(2,1)S(1)} collective-permute-done((bf16[2,128,512]{2,1,0:T(8,128)(2,1)S(1)}, bf16[2,128,512]{2,1,0:T(8,128)(2,1)S(1)}, u32[]{:S(2)}, u32[]{:S(2)}) %collective-permute-start.10) | collective-permute-done | bytes 262176 | tf_op jit(solution)/shard_map/ppermute | solution.py:95
  96.8 0.6 collective-permute-start.12
  98.0 2.7 %collective-permute-done.11.refs_10_ = bf16[2,128,512]{2,1,0:T(8,128)(2,1)} collective-permute-done((bf16[2,128,512]{2,1,0:T(8,128)(2,1)}, bf16[2,128,512]{2,1,0:T(8,128)(2,1)}, u32[]{:S(2)}, u32[]{:S(2)}) %collective-permute-start.11) | collective-permute-done | bytes 262176 | tf_op jit(solution)/shard_map/ppermute | solution.py:95
  100.8 0.6 collective-permute-start.13
  101.4 2.2 %collective-permute-done.12.refs_11_ = bf16[2,128,512]{2,1,0:T(8,128)(2,1)} collective-permute-done((bf16[2,128,512]{2,1,0:T(8,128)(2,1)S(1)}, bf16[2,128,512]{2,1,0:T(8,128)(2,1)}, u32[]{:S(2)}, u32[]{:S(2)}) %collective-permute-start.12) | collective-permute-done | bytes 262176 | tf_op jit(solution)/shard_map/ppermute | solution.py:95
  103.6 0.7 collective-permute-start.14
  104.3 1.6 %collective-permute-start.41 = (bf16[16,2,32,512]{3,2,1,0:T(8,128)(2,1)S(1)}, bf16[16,2,32,512]{3,2,1,0:T(8,128)(2,1)}, u32[]{:S(2)}, u32[]{:S(2)}) collective-permute-start(bf16[16,2,32,512]{3,2,1,0:T(8,128)(2,1)S(1)} %all-to-all-done.refs_40_), channel_id=1, source_target_pairs={{0,16},{16,0},{1,17},{17,1},{2,18},{18,2},{3,19},{19,3},{4,20},{20... | collective-permute-start | bytes 3145736 | tf_op jit(solution)/shard_map/ppermute | solution.py:144
  106.4 1.1 collective-permute-done.13.refs_12_
  107.5 1.4 collective-permute-start.15
  108.8 1.5 collective-permute-done.14.refs_13_
  110.3 0.6 collective-permute-start.16
  111.0 0.7 copy-done.17
  112.2 1.9 %collective-permute-done.15.refs_14_ = bf16[2,128,512]{2,1,0:T(8,128)(2,1)} collective-permute-done((bf16[2,128,512]{2,1,0:T(8,128)(2,1)}, bf16[2,128,512]{2,1,0:T(8,128)(2,1)}, u32[]{:S(2)}, u32[]{:S(2)}) %collective-permute-start.15) | collective-permute-done | bytes 262176 | tf_op jit(solution)/shard_map/ppermute | solution.py:95
  114.1 1.4 collective-permute-start.17
  115.5 1.4 collective-permute-done.16.refs_15_
  116.9 0.7 copy-done.18
  117.6 1.3 collective-permute-start.18
  119.8 1.0 collective-permute-done.17.refs_16_
  120.8 1.4 collective-permute-start.19
  122.2 1.9 %collective-permute-done.18.refs_17_ = bf16[2,128,512]{2,1,0:T(8,128)(2,1)} collective-permute-done((bf16[2,128,512]{2,1,0:T(8,128)(2,1)S(1)}, bf16[2,128,512]{2,1,0:T(8,128)(2,1)}, u32[]{:S(2)}, u32[]{:S(2)}) %collective-permute-start.18) | collective-permute-done | bytes 262176 | tf_op jit(solution)/shard_map/ppermute | solution.py:95
  124.1 1.3 collective-permute-start.20
  125.6 0.6 broadcast_in_dim.5.refs_43_
  126.3 0.9 collective-permute-done.41.refs_41_
  127.8 3.0 %collective-permute-done.20.refs_19_ = bf16[2,128,512]{2,1,0:T(8,128)(2,1)} collective-permute-done((bf16[2,128,512]{2,1,0:T(8,128)(2,1)}, bf16[2,128,512]{2,1,0:T(8,128)(2,1)}, u32[]{:S(2)}, u32[]{:S(2)}) %collective-permute-start.20) | collective-permute-done | bytes 262176 | tf_op jit(solution)/shard_map/ppermute | solution.py:95
  131.1 1.7 %copy.13.refs_42_ = f32[3,2,512,1]{3,2,1,0:T(8,128)} copy(f32[3,2,512,1]{2,1,0,3:T(2,128)S(1)} %maximum_bitcast_fusion) | data formatting | bytes 24576 | tf_op jit(solution)/shard_map/broadcast_in_dim | solution.py:53
  132.8 0.6 stack.37.where_ref
  133.6 18.4 %shard_map.105 = (f32[2]{0:T(128)}, f32[2]{0:T(128)}) custom-call(s32[32]{0:T(128)} %cut_ref.1, s32[16,2]{1,0:T(8,128)} %copy.12.list_ref, s32[6]{0:T(128)} %stack.37.where_ref, bf16[2,128,512]{2,1,0:T(8,128)(2,1)} %bitcast.51, bf16[2,128,512]{2,1,0:T(8,128)(2,1)} %bitcast.48, bf16[2,128,512]{2,1,0:T(8,128)(2,1)} %copy-done.4, ...), custom_call_target="tpu_custom_call" | custom-call | tf_op jit(solution)/shard_map/pallas_call | solution.py:296
  (109 shorter events, 8.4 us)
Async XLA Ops:
  2.1 45.9 %collective-permute-start = (bf16[2,131072]{1,0:T(2,128)(2,1)S(1)}, bf16[2,131072]{1,0:T(2,128)(2,1)S(1)}, u32[]{:S(2)}, u32[]{:S(2)}) collective-permute-start(bf16[2,131072]{1,0:T(2,128)(2,1)S(1)} %dynamic-slice_bitcast_fusion.2), channel_id=1, source_target_pairs={{0,1},{1,0},{2,3},{3,2},{4,5},{5,4},{6,7},{7,6},{8,9},{9,8},{10,11... | collective-permute-start | bytes 1572872 | tf_op jit(solution)/shard_map/ppermute | solution.py:79
  40.2 64.1 %all-to-all-start = ((bf16[16,2,32,512]{3,2,1,0:T(8,128)(2,1)}), bf16[16,2,32,512]{3,2,1,0:T(8,128)(2,1)S(1)}, u32[]{:S(2)}, u32[]{:S(2)}) async-start(bf16[16,2,32,512]{3,2,1,0:T(8,128)(2,1)} %reshape.217), calls=%async_computation | async-start | bytes 2097152 | tf_op jit(solution)/shard_map/all_to_all | solution.py:141
  51.1 4.1 %collective-permute-start.1 = (bf16[2,131072]{1,0:T(2,128)(2,1)S(1)}, bf16[2,131072]{1,0:T(2,128)(2,1)S(1)}, u32[]{:S(2)}, u32[]{:S(2)}) collective-permute-start(bf16[2,131072]{1,0:T(2,128)(2,1)S(1)} %dynamic-slice_bitcast_fusion.1), channel_id=1, source_target_pairs={{0,1},{1,0},{2,3},{3,2},{4,5},{5,4},{6,7},{7,6},{8,9},{9,8},{10,11... | collective-permute-start | bytes 1572872 | tf_op jit(solution)/shard_map/ppermute | solution.py:79
  52.0 16.1 %collective-permute-start.2 = (bf16[2,128,512]{2,1,0:T(8,128)(2,1)S(1)}, bf16[2,128,512]{2,1,0:T(8,128)(2,1)S(1)}, u32[]{:S(2)}, u32[]{:S(2)}) collective-permute-start(bf16[2,128,512]{2,1,0:T(8,128)(2,1)S(1)} %bitcast.49), channel_id=1, source_target_pairs={{0,4},{5,1},{4,8},{9,5},{8,12},{13,9},{12,14},{15,13},{14,10},{11,... | collective-permute-start | bytes 786440 | tf_op jit(solution)/shard_map/ppermute | solution.py:95
  53.8 21.6 %collective-permute-start.3 = (bf16[2,128,512]{2,1,0:T(8,128)(2,1)S(1)}, bf16[2,128,512]{2,1,0:T(8,128)(2,1)S(1)}, u32[]{:S(2)}, u32[]{:S(2)}) collective-permute-start(bf16[2,128,512]{2,1,0:T(8,128)(2,1)S(1)} %bitcast.46), channel_id=1, source_target_pairs={{0,4},{5,1},{4,8},{9,5},{8,12},{13,9},{12,14},{15,13},{14,10},{11,... | collective-permute-start | bytes 786440 | tf_op jit(solution)/shard_map/ppermute | solution.py:95
  56.2 22.0 %collective-permute-start.4 = (bf16[2,131072]{1,0:T(2,128)(2,1)S(1)}, bf16[2,131072]{1,0:T(2,128)(2,1)S(1)}, u32[]{:S(2)}, u32[]{:S(2)}) collective-permute-start(bf16[2,131072]{1,0:T(2,128)(2,1)S(1)} %dynamic-slice_bitcast_fusion), channel_id=1, source_target_pairs={{0,1},{1,0},{2,3},{3,2},{4,5},{5,4},{6,7},{7,6},{8,9},{9,8},{10,11... | collective-permute-start | bytes 1572872 | tf_op jit(solution)/shard_map/ppermute | solution.py:79
  56.6 62.3 %copy-start.21 = (s32[3]{0:T(128)S(1)}, s32[3]{0:T(128)}, u32[]{:S(2)}) copy-start(s32[3]{0:T(128)} %param.14) | copy-start | bytes 40
  68.2 64.7 %copy-start.4 = (bf16[2,128,512]{2,1,0:T(8,128)(2,1)}, bf16[2,128,512]{2,1,0:T(8,128)(2,1)S(1)}, u32[]{:S(2)}) copy-start(bf16[2,128,512]{2,1,0:T(8,128)(2,1)S(1)} %bitcast_select_fusion.3.refs_2_) | copy-start | bytes 786436
  68.2 11.1 %collective-permute-start.5 = (bf16[2,128,512]{2,1,0:T(8,128)(2,1)S(1)}, bf16[2,128,512]{2,1,0:T(8,128)(2,1)S(1)}, u32[]{:S(2)}, u32[]{:S(2)}) collective-permute-start(bf16[2,128,512]{2,1,0:T(8,128)(2,1)S(1)} %bitcast_select_fusion.3.refs_2_), channel_id=1, source_target_pairs={{0,4},{5,1},{4,8},{9,5},{8,12},{13,9},{12,14},{15,13},{14,10},{11,... | collective-permute-start | bytes 786440 | tf_op jit(solution)/shard_map/ppermute | solution.py:95
  75.4 58.1 %copy-start.5 = (bf16[2,128,512]{2,1,0:T(8,128)(2,1)}, bf16[2,128,512]{2,1,0:T(8,128)(2,1)S(1)}, u32[]{:S(2)}) copy-start(bf16[2,128,512]{2,1,0:T(8,128)(2,1)S(1)} %bitcast_select_fusion.2.refs_3_) | copy-start | bytes 786436
  75.4 6.6 %collective-permute-start.6 = (bf16[2,128,512]{2,1,0:T(8,128)(2,1)S(1)}, bf16[2,128,512]{2,1,0:T(8,128)(2,1)S(1)}, u32[]{:S(2)}, u32[]{:S(2)}) collective-permute-start(bf16[2,128,512]{2,1,0:T(8,128)(2,1)S(1)} %bitcast_select_fusion.2.refs_3_), channel_id=1, source_target_pairs={{0,4},{5,1},{4,8},{9,5},{8,12},{13,9},{12,14},{15,13},{14,10},{11,... | collective-permute-start | bytes 786440 | tf_op jit(solution)/shard_map/ppermute | solution.py:95
  79.3 54.2 %copy-start.6 = (bf16[2,128,512]{2,1,0:T(8,128)(2,1)}, bf16[2,128,512]{2,1,0:T(8,128)(2,1)S(1)}, u32[]{:S(2)}) copy-start(bf16[2,128,512]{2,1,0:T(8,128)(2,1)S(1)} %bitcast_select_fusion.1.refs_4_) | copy-start | bytes 786436
  79.3 8.3 %collective-permute-start.7 = (bf16[2,128,512]{2,1,0:T(8,128)(2,1)S(1)}, bf16[2,128,512]{2,1,0:T(8,128)(2,1)S(1)}, u32[]{:S(2)}, u32[]{:S(2)}) collective-permute-start(bf16[2,128,512]{2,1,0:T(8,128)(2,1)S(1)} %bitcast_select_fusion.1.refs_4_), channel_id=1, source_target_pairs={{0,4},{5,1},{4,8},{9,5},{8,12},{13,9},{12,14},{15,13},{14,10},{11,... | collective-permute-start | bytes 786440 | tf_op jit(solution)/shard_map/ppermute | solution.py:95
  82.1 51.4 %copy-start.7 = (bf16[2,128,512]{2,1,0:T(8,128)(2,1)}, bf16[2,128,512]{2,1,0:T(8,128)(2,1)S(1)}, u32[]{:S(2)}) copy-start(bf16[2,128,512]{2,1,0:T(8,128)(2,1)S(1)} %bitcast_select_fusion.refs_5_) | copy-start | bytes 786436
  82.1 8.3 %collective-permute-start.8 = (bf16[2,128,512]{2,1,0:T(8,128)(2,1)S(1)}, bf16[2,128,512]{2,1,0:T(8,128)(2,1)S(1)}, u32[]{:S(2)}, u32[]{:S(2)}) collective-permute-start(bf16[2,128,512]{2,1,0:T(8,128)(2,1)S(1)} %bitcast_select_fusion.refs_5_), channel_id=1, source_target_pairs={{0,4},{5,1},{4,8},{9,5},{8,12},{13,9},{12,14},{15,13},{14,10},{11,... | collective-permute-start | bytes 786440 | tf_op jit(solution)/shard_map/ppermute | solution.py:95
  84.7 6.4 %collective-permute-start.21 = (bf16[2,128,512]{2,1,0:T(8,128)(2,1)S(1)}, bf16[2,128,512]{2,1,0:T(8,128)(2,1)S(1)}, u32[]{:S(2)}, u32[]{:S(2)}) collective-permute-start(bf16[2,128,512]{2,1,0:T(8,128)(2,1)S(1)} %bitcast.50), channel_id=1, source_target_pairs={{0,1},{1,0},{2,3},{3,2},{4,5},{5,4},{6,7},{7,6},{8,9},{9,8},{10,11... | collective-permute-start | bytes 786440 | tf_op jit(solution)/shard_map/ppermute | solution.py:96
  84.7 6.4 %collective-permute-start.22 = (bf16[2,128,512]{2,1,0:T(8,128)(2,1)S(1)}, bf16[2,128,512]{2,1,0:T(8,128)(2,1)S(1)}, u32[]{:S(2)}, u32[]{:S(2)}) collective-permute-start(bf16[2,128,512]{2,1,0:T(8,128)(2,1)S(1)} %bitcast.47), channel_id=1, source_target_pairs={{0,1},{1,0},{2,3},{3,2},{4,5},{5,4},{6,7},{7,6},{8,9},{9,8},{10,11... | collective-permute-start | bytes 786440 | tf_op jit(solution)/shard_map/ppermute | solution.py:96
  85.2 6.4 %collective-permute-start.23 = (bf16[2,128,512]{2,1,0:T(8,128)(2,1)S(1)}, bf16[2,128,512]{2,1,0:T(8,128)(2,1)S(1)}, u32[]{:S(2)}, u32[]{:S(2)}) collective-permute-start(bf16[2,128,512]{2,1,0:T(8,128)(2,1)S(1)} %bitcast_select_fusion.3.refs_2_), channel_id=1, source_target_pairs={{0,1},{1,0},{2,3},{3,2},{4,5},{5,4},{6,7},{7,6},{8,9},{9,8},{10,11... | collective-permute-start | bytes 786440 | tf_op jit(solution)/shard_map/ppermute | solution.py:96
  87.6 6.5 %collective-permute-start.9 = (bf16[2,128,512]{2,1,0:T(8,128)(2,1)S(1)}, bf16[2,128,512]{2,1,0:T(8,128)(2,1)}, u32[]{:S(2)}, u32[]{:S(2)}) collective-permute-start(bf16[2,128,512]{2,1,0:T(8,128)(2,1)S(1)} %collective-permute-done.7.refs_6_), channel_id=1, source_target_pairs={{0,4},{5,1},{4,8},{9,5},{8,12},{13,9},{12,14},{15,13},{14,10},{11,... | collective-permute-start | bytes 786440 | tf_op jit(solution)/shard_map/ppermute | solution.py:95
  90.4 6.4 %collective-permute-start.10 = (bf16[2,128,512]{2,1,0:T(8,128)(2,1)S(1)}, bf16[2,128,512]{2,1,0:T(8,128)(2,1)S(1)}, u32[]{:S(2)}, u32[]{:S(2)}) collective-permute-start(bf16[2,128,512]{2,1,0:T(8,128)(2,1)S(1)} %collective-permute-done.8.refs_7_), channel_id=1, source_target_pairs={{0,4},{5,1},{4,8},{9,5},{8,12},{13,9},{12,14},{15,13},{14,10},{11,... | collective-permute-start | bytes 786440 | tf_op jit(solution)/shard_map/ppermute | solution.py:95
  91.0 6.4 %collective-permute-start.24 = (bf16[2,128,512]{2,1,0:T(8,128)(2,1)S(1)}, bf16[2,128,512]{2,1,0:T(8,128)(2,1)S(1)}, u32[]{:S(2)}, u32[]{:S(2)}) collective-permute-start(bf16[2,128,512]{2,1,0:T(8,128)(2,1)S(1)} %bitcast_select_fusion.2.refs_3_), channel_id=1, source_target_pairs={{0,1},{1,0},{2,3},{3,2},{4,5},{5,4},{6,7},{7,6},{8,9},{9,8},{10,11... | collective-permute-start | bytes 786440 | tf_op jit(solution)/shard_map/ppermute | solution.py:96
  91.1 6.4 %collective-permute-start.25 = (bf16[2,128,512]{2,1,0:T(8,128)(2,1)S(1)}, bf16[2,128,512]{2,1,0:T(8,128)(2,1)S(1)}, u32[]{:S(2)}, u32[]{:S(2)}) collective-permute-start(bf16[2,128,512]{2,1,0:T(8,128)(2,1)S(1)} %bitcast_select_fusion.1.refs_4_), channel_id=1, source_target_pairs={{0,1},{1,0},{2,3},{3,2},{4,5},{5,4},{6,7},{7,6},{8,9},{9,8},{10,11... | collective-permute-start | bytes 786440 | tf_op jit(solution)/shard_map/ppermute | solution.py:96
  91.6 6.4 %collective-permute-start.26 = (bf16[2,128,512]{2,1,0:T(8,128)(2,1)S(1)}, bf16[2,128,512]{2,1,0:T(8,128)(2,1)S(1)}, u32[]{:S(2)}, u32[]{:S(2)}) collective-permute-start(bf16[2,128,512]{2,1,0:T(8,128)(2,1)S(1)} %bitcast_select_fusion.refs_5_), channel_id=1, source_target_pairs={{0,1},{1,0},{2,3},{3,2},{4,5},{5,4},{6,7},{7,6},{8,9},{9,8},{10,11... | collective-permute-start | bytes 786440 | tf_op jit(solution)/shard_map/ppermute | solution.py:96
  94.1 6.7 %collective-permute-start.11 = (bf16[2,128,512]{2,1,0:T(8,128)(2,1)}, bf16[2,128,512]{2,1,0:T(8,128)(2,1)}, u32[]{:S(2)}, u32[]{:S(2)}) collective-permute-start(bf16[2,128,512]{2,1,0:T(8,128)(2,1)} %collective-permute-done.9.refs_8_), channel_id=1, source_target_pairs={{0,4},{5,1},{4,8},{9,5},{8,12},{13,9},{12,14},{15,13},{14,10},{11,... | collective-permute-start | bytes 786440 | tf_op jit(solution)/shard_map/ppermute | solution.py:95
  96.8 6.8 %collective-permute-start.12 = (bf16[2,128,512]{2,1,0:T(8,128)(2,1)S(1)}, bf16[2,128,512]{2,1,0:T(8,128)(2,1)}, u32[]{:S(2)}, u32[]{:S(2)}) collective-permute-start(bf16[2,128,512]{2,1,0:T(8,128)(2,1)S(1)} %collective-permute-done.10.refs_9_), channel_id=1, source_target_pairs={{0,4},{5,1},{4,8},{9,5},{8,12},{13,9},{12,14},{15,13},{14,10},{11,... | collective-permute-start | bytes 786440 | tf_op jit(solution)/shard_map/ppermute | solution.py:95
  97.4 6.9 %collective-permute-start.27 = (bf16[2,128,512]{2,1,0:T(8,128)(2,1)S(1)}, bf16[2,128,512]{2,1,0:T(8,128)(2,1)}, u32[]{:S(2)}, u32[]{:S(2)}) collective-permute-start(bf16[2,128,512]{2,1,0:T(8,128)(2,1)S(1)} %collective-permute-done.7.refs_6_), channel_id=1, source_target_pairs={{0,1},{1,0},{2,3},{3,2},{4,5},{5,4},{6,7},{7,6},{8,9},{9,8},{10,11... | collective-permute-start | bytes 786440 | tf_op jit(solution)/shard_map/ppermute | solution.py:96
  97.4 8.4 %collective-permute-start.28 = (bf16[2,128,512]{2,1,0:T(8,128)(2,1)S(1)}, bf16[2,128,512]{2,1,0:T(8,128)(2,1)}, u32[]{:S(2)}, u32[]{:S(2)}) collective-permute-start(bf16[2,128,512]{2,1,0:T(8,128)(2,1)S(1)} %collective-permute-done.8.refs_7_), channel_id=1, source_target_pairs={{0,1},{1,0},{2,3},{3,2},{4,5},{5,4},{6,7},{7,6},{8,9},{9,8},{10,11... | collective-permute-start | bytes 786440 | tf_op jit(solution)/shard_map/ppermute | solution.py:96
  97.9 7.9 %collective-permute-start.29 = (bf16[2,128,512]{2,1,0:T(8,128)(2,1)}, bf16[2,128,512]{2,1,0:T(8,128)(2,1)}, u32[]{:S(2)}, u32[]{:S(2)}) collective-permute-start(bf16[2,128,512]{2,1,0:T(8,128)(2,1)} %collective-permute-done.9.refs_8_), channel_id=1, source_target_pairs={{0,1},{1,0},{2,3},{3,2},{4,5},{5,4},{6,7},{7,6},{8,9},{9,8},{10,11... | collective-permute-start | bytes 786440 | tf_op jit(solution)/shard_map/ppermute | solution.py:96
  100.8 6.7 %collective-permute-start.13 = (bf16[2,128,512]{2,1,0:T(8,128)(2,1)}, bf16[2,128,512]{2,1,0:T(8,128)(2,1)}, u32[]{:S(2)}, u32[]{:S(2)}) collective-permute-start(bf16[2,128,512]{2,1,0:T(8,128)(2,1)} %collective-permute-done.11.refs_10_), channel_id=1, source_target_pairs={{0,4},{5,1},{4,8},{9,5},{8,12},{13,9},{12,14},{15,13},{14,10},{11,... | collective-permute-start | bytes 786440 | tf_op jit(solution)/shard_map/ppermute | solution.py:95
  103.6 6.7 %collective-permute-start.14 = (bf16[2,128,512]{2,1,0:T(8,128)(2,1)}, bf16[2,128,512]{2,1,0:T(8,128)(2,1)}, u32[]{:S(2)}, u32[]{:S(2)}) collective-permute-start(bf16[2,128,512]{2,1,0:T(8,128)(2,1)} %collective-permute-done.12.refs_11_), channel_id=1, source_target_pairs={{0,4},{5,1},{4,8},{9,5},{8,12},{13,9},{12,14},{15,13},{14,10},{11,... | collective-permute-start | bytes 786440 | tf_op jit(solution)/shard_map/ppermute | solution.py:95
  104.3 22.9 %collective-permute-start.41 = (bf16[16,2,32,512]{3,2,1,0:T(8,128)(2,1)S(1)}, bf16[16,2,32,512]{3,2,1,0:T(8,128)(2,1)}, u32[]{:S(2)}, u32[]{:S(2)}) collective-permute-start(bf16[16,2,32,512]{3,2,1,0:T(8,128)(2,1)S(1)} %all-to-all-done.refs_40_), channel_id=1, source_target_pairs={{0,16},{16,0},{1,17},{17,1},{2,18},{18,2},{3,19},{19,3},{4,20},{20... | collective-permute-start | bytes 3145736 | tf_op jit(solution)/shard_map/ppermute | solution.py:144
  105.8 5.1 %collective-permute-start.30 = (bf16[2,128,512]{2,1,0:T(8,128)(2,1)S(1)}, bf16[2,128,512]{2,1,0:T(8,128)(2,1)S(1)}, u32[]{:S(2)}, u32[]{:S(2)}) collective-permute-start(bf16[2,128,512]{2,1,0:T(8,128)(2,1)S(1)} %collective-permute-done.10.refs_9_), channel_id=1, source_target_pairs={{0,1},{1,0},{2,3},{3,2},{4,5},{5,4},{6,7},{7,6},{8,9},{9,8},{10,11... | collective-permute-start | bytes 786440 | tf_op jit(solution)/shard_map/ppermute | solution.py:96
  105.9 5.8 %collective-permute-start.31 = (bf16[2,128,512]{2,1,0:T(8,128)(2,1)}, bf16[2,128,512]{2,1,0:T(8,128)(2,1)}, u32[]{:S(2)}, u32[]{:S(2)}) collective-permute-start(bf16[2,128,512]{2,1,0:T(8,128)(2,1)} %collective-permute-done.11.refs_10_), channel_id=1, source_target_pairs={{0,1},{1,0},{2,3},{3,2},{4,5},{5,4},{6,7},{7,6},{8,9},{9,8},{10,11... | collective-permute-start | bytes 786440 | tf_op jit(solution)/shard_map/ppermute | solution.py:96
  107.5 6.7 %collective-permute-start.15 = (bf16[2,128,512]{2,1,0:T(8,128)(2,1)}, bf16[2,128,512]{2,1,0:T(8,128)(2,1)}, u32[]{:S(2)}, u32[]{:S(2)}) collective-permute-start(bf16[2,128,512]{2,1,0:T(8,128)(2,1)} %collective-permute-done.13.refs_12_), channel_id=1, source_target_pairs={{0,4},{5,1},{4,8},{9,5},{8,12},{13,9},{12,14},{15,13},{14,10},{11,... | collective-permute-start | bytes 786440 | tf_op jit(solution)/shard_map/ppermute | solution.py:95
  110.3 6.6 %collective-permute-start.16 = (bf16[2,128,512]{2,1,0:T(8,128)(2,1)}, bf16[2,128,512]{2,1,0:T(8,128)(2,1)S(1)}, u32[]{:S(2)}, u32[]{:S(2)}) collective-permute-start(bf16[2,128,512]{2,1,0:T(8,128)(2,1)} %collective-permute-done.14.refs_13_), channel_id=1, source_target_pairs={{0,4},{5,1},{4,8},{9,5},{8,12},{13,9},{12,14},{15,13},{14,10},{11,... | collective-permute-start | bytes 786440 | tf_op jit(solution)/shard_map/ppermute | solution.py:95
  111.7 7.6 %collective-permute-start.32 = (bf16[2,128,512]{2,1,0:T(8,128)(2,1)}, bf16[2,128,512]{2,1,0:T(8,128)(2,1)S(1)}, u32[]{:S(2)}, u32[]{:S(2)}) collective-permute-start(bf16[2,128,512]{2,1,0:T(8,128)(2,1)} %collective-permute-done.12.refs_11_), channel_id=1, source_target_pairs={{0,1},{1,0},{2,3},{3,2},{4,5},{5,4},{6,7},{7,6},{8,9},{9,8},{10,11... | collective-permute-start | bytes 786440 | tf_op jit(solution)/shard_map/ppermute | solution.py:96
  111.7 7.7 %collective-permute-start.33 = (bf16[2,128,512]{2,1,0:T(8,128)(2,1)}, bf16[2,128,512]{2,1,0:T(8,128)(2,1)S(1)}, u32[]{:S(2)}, u32[]{:S(2)}) collective-permute-start(bf16[2,128,512]{2,1,0:T(8,128)(2,1)} %collective-permute-done.13.refs_12_), channel_id=1, source_target_pairs={{0,1},{1,0},{2,3},{3,2},{4,5},{5,4},{6,7},{7,6},{8,9},{9,8},{10,11... | collective-permute-start | bytes 786440 | tf_op jit(solution)/shard_map/ppermute | solution.py:96
  114.1 6.7 %collective-permute-start.17 = (bf16[2,128,512]{2,1,0:T(8,128)(2,1)}, bf16[2,128,512]{2,1,0:T(8,128)(2,1)}, u32[]{:S(2)}, u32[]{:S(2)}) collective-permute-start(bf16[2,128,512]{2,1,0:T(8,128)(2,1)} %collective-permute-done.15.refs_14_), channel_id=1, source_target_pairs={{0,4},{5,1},{4,8},{9,5},{8,12},{13,9},{12,14},{15,13},{14,10},{11,... | collective-permute-start | bytes 786440 | tf_op jit(solution)/shard_map/ppermute | solution.py:95
  117.6 6.5 %collective-permute-start.18 = (bf16[2,128,512]{2,1,0:T(8,128)(2,1)S(1)}, bf16[2,128,512]{2,1,0:T(8,128)(2,1)}, u32[]{:S(2)}, u32[]{:S(2)}) collective-permute-start(bf16[2,128,512]{2,1,0:T(8,128)(2,1)S(1)} %collective-permute-done.16.refs_15_), channel_id=1, source_target_pairs={{0,4},{5,1},{4,8},{9,5},{8,12},{13,9},{12,14},{15,13},{14,10},{11,... | collective-permute-start | bytes 786440 | tf_op jit(solution)/shard_map/ppermute | solution.py:95
  119.3 7.0 %collective-permute-start.34 = (bf16[2,128,512]{2,1,0:T(8,128)(2,1)}, bf16[2,128,512]{2,1,0:T(8,128)(2,1)}, u32[]{:S(2)}, u32[]{:S(2)}) collective-permute-start(bf16[2,128,512]{2,1,0:T(8,128)(2,1)} %collective-permute-done.14.refs_13_), channel_id=1, source_target_pairs={{0,1},{1,0},{2,3},{3,2},{4,5},{5,4},{6,7},{7,6},{8,9},{9,8},{10,11... | collective-permute-start | bytes 786440 | tf_op jit(solution)/shard_map/ppermute | solution.py:96
  119.4 7.9 %collective-permute-start.35 = (bf16[2,128,512]{2,1,0:T(8,128)(2,1)}, bf16[2,128,512]{2,1,0:T(8,128)(2,1)}, u32[]{:S(2)}, u32[]{:S(2)}) collective-permute-start(bf16[2,128,512]{2,1,0:T(8,128)(2,1)} %collective-permute-done.15.refs_14_), channel_id=1, source_target_pairs={{0,1},{1,0},{2,3},{3,2},{4,5},{5,4},{6,7},{7,6},{8,9},{9,8},{10,11... | collective-permute-start | bytes 786440 | tf_op jit(solution)/shard_map/ppermute | solution.py:96
  120.8 6.9 %collective-permute-start.19 = (bf16[2,128,512]{2,1,0:T(8,128)(2,1)}, bf16[2,128,512]{2,1,0:T(8,128)(2,1)}, u32[]{:S(2)}, u32[]{:S(2)}) collective-permute-start(bf16[2,128,512]{2,1,0:T(8,128)(2,1)} %collective-permute-done.17.refs_16_), channel_id=1, source_target_pairs={{0,4},{5,1},{4,8},{9,5},{8,12},{13,9},{12,14},{15,13},{14,10},{11,... | collective-permute-start | bytes 786440 | tf_op jit(solution)/shard_map/ppermute | solution.py:95
  124.1 6.7 %collective-permute-start.20 = (bf16[2,128,512]{2,1,0:T(8,128)(2,1)}, bf16[2,128,512]{2,1,0:T(8,128)(2,1)}, u32[]{:S(2)}, u32[]{:S(2)}) collective-permute-start(bf16[2,128,512]{2,1,0:T(8,128)(2,1)} %collective-permute-done.18.refs_17_), channel_id=1, source_target_pairs={{0,4},{5,1},{4,8},{9,5},{8,12},{13,9},{12,14},{15,13},{14,10},{11,... | collective-permute-start | bytes 786440 | tf_op jit(solution)/shard_map/ppermute | solution.py:95
  126.2 7.2 %collective-permute-start.36 = (bf16[2,128,512]{2,1,0:T(8,128)(2,1)}, bf16[2,128,512]{2,1,0:T(8,128)(2,1)}, u32[]{:S(2)}, u32[]{:S(2)}) collective-permute-start(bf16[2,128,512]{2,1,0:T(8,128)(2,1)} %copy-done.18), channel_id=1, source_target_pairs={{0,1},{1,0},{2,3},{3,2},{4,5},{5,4},{6,7},{7,6},{8,9},{9,8},{10,11... | collective-permute-start | bytes 786440 | tf_op jit(solution)/shard_map/ppermute | solution.py:96
  127.2 6.2 %collective-permute-start.37 = (bf16[2,128,512]{2,1,0:T(8,128)(2,1)}, bf16[2,128,512]{2,1,0:T(8,128)(2,1)}, u32[]{:S(2)}, u32[]{:S(2)}) collective-permute-start(bf16[2,128,512]{2,1,0:T(8,128)(2,1)} %collective-permute-done.17.refs_16_), channel_id=1, source_target_pairs={{0,1},{1,0},{2,3},{3,2},{4,5},{5,4},{6,7},{7,6},{8,9},{9,8},{10,11... | collective-permute-start | bytes 786440 | tf_op jit(solution)/shard_map/ppermute | solution.py:96
  127.2 6.2 %collective-permute-start.38 = (bf16[2,128,512]{2,1,0:T(8,128)(2,1)}, bf16[2,128,512]{2,1,0:T(8,128)(2,1)}, u32[]{:S(2)}, u32[]{:S(2)}) collective-permute-start(bf16[2,128,512]{2,1,0:T(8,128)(2,1)} %collective-permute-done.18.refs_17_), channel_id=1, source_target_pairs={{0,1},{1,0},{2,3},{3,2},{4,5},{5,4},{6,7},{7,6},{8,9},{9,8},{10,11... | collective-permute-start | bytes 786440 | tf_op jit(solution)/shard_map/ppermute | solution.py:96
  127.7 5.7 %collective-permute-start.39 = (bf16[2,128,512]{2,1,0:T(8,128)(2,1)}, bf16[2,128,512]{2,1,0:T(8,128)(2,1)}, u32[]{:S(2)}, u32[]{:S(2)}) collective-permute-start(bf16[2,128,512]{2,1,0:T(8,128)(2,1)} %collective-permute-done.19.refs_18_), channel_id=1, source_target_pairs={{0,1},{1,0},{2,3},{3,2},{4,5},{5,4},{6,7},{7,6},{8,9},{9,8},{10,11... | collective-permute-start | bytes 786440 | tf_op jit(solution)/shard_map/ppermute | solution.py:96
  130.8 2.7 %collective-permute-start.40 = (bf16[2,128,512]{2,1,0:T(8,128)(2,1)}, bf16[2,128,512]{2,1,0:T(8,128)(2,1)}, u32[]{:S(2)}, u32[]{:S(2)}) collective-permute-start(bf16[2,128,512]{2,1,0:T(8,128)(2,1)} %collective-permute-done.20.refs_19_), channel_id=1, source_target_pairs={{0,1},{1,0},{2,3},{3,2},{4,5},{5,4},{6,7},{7,6},{8,9},{9,8},{10,11... | collective-permute-start | bytes 786440 | tf_op jit(solution)/shard_map/ppermute | solution.py:96
  (17 other events, 355.0 us)

commit v4 on v3

--- a/solution.py
+++ b/solution.py
@@ -16,7 +16,7 @@
 ROW_STEP = 16
 WAVE_ROWS = 32
 HALF_CHUNKS = 2
-LAG = 2
+LAG = 1
 CORES = 2
 
 
@@ -59,28 +59,36 @@
     return list(range(0, chips, 2)) + list(range(chips - 1 - chips % 2, 0, -2))
 
 
-def spread(strain_slots, owner):
+def to_partner():
+    return [(i, i ^ 1) for i in range(lax.axis_size("tpl"))]
+
+
+def halves(strain_slots, owner):
+    core = lax.axis_index("tpl") % CORES
+    half = ROWS * COLS // CORES
+    bins = half // HALF_CHUNKS
+    on_owner_core = core == owner % CORES
+    chunks = []
+    for det in range(DET):
+        side = lambda which: lax.dynamic_slice(strain_slots, (0, det, 0, which * half), (1, 1, 2, half))[0, 0]
+        got = lax.ppermute(side(1 - core), "tpl", to_partner())
+        first = jnp.where(on_owner_core, side(core), got)
+        strain_slots, first = lax.optimization_barrier((strain_slots, first))
+        for at in range(HALF_CHUNKS):
+            chunks.append(first[:, bins * at : bins * (at + 1)].reshape(2, bins // COLS, COLS))
+    return chunks
+
+
+def spread(chunks, owner, early):
     devices = lax.axis_size("tpl")
     chips = devices // CORES
     order = ring_order(chips)
     chip, core = lax.axis_index("tpl") // CORES, lax.axis_index("tpl") % CORES
-    half = ROWS * COLS // CORES
-    bins = half // HALF_CHUNKS
-    to_partner = [(i, i ^ 1) for i in range(devices)]
+    on_owner_chip = chip == owner // CORES
     along = []
     for at in range(chips):
         along.append((order[at] * CORES, order[(at + 1) % chips] * CORES))
         along.append((order[(at + 1) % chips] * CORES + 1, order[at] * CORES + 1))
-    on_owner_core = core == owner % CORES
-    on_owner_chip = chip == owner // CORES
-    chunks = []
-    for det in range(DET):
-        side = lambda which: lax.dynamic_slice(strain_slots, (0, det, 0, which * half), (1, 1, 2, half))[0, 0]
-        got = lax.ppermute(side(1 - core), "tpl", to_partner)
-        first = jnp.where(on_owner_core, side(core), got)
-        strain_slots, first = lax.optimization_barrier((strain_slots, first))
-        for at in range(HALF_CHUNKS):
-            chunks.append(first[:, bins * at : bins * (at + 1)].reshape(2, bins // COLS, COLS))
     sent, arrived = [], []
     count = len(chunks)
     for slot in range(count + LAG * (chips - 1)):
@@ -90,40 +98,21 @@
             here = jnp.where(on_owner_chip, chunks[slot], arrived[slot - LAG])
         else:
             here = arrived[slot - LAG]
+        if slot == count // 2:
+            here, early = lax.optimization_barrier((here, early))
         sent.append(here)
         if slot < count + LAG * (chips - 2):
             arrived.append(lax.ppermute(here, "tpl", along))
-    shared = [lax.ppermute(here, "tpl", to_partner) for here in sent]
+    shared = [lax.ppermute(here, "tpl", to_partner()) for here in sent]
     place = lambda at: jnp.where(at % 2 == 0, at // 2, chips - 1 - at // 2)
     forward = (place(chip) - place(owner // CORES)) % chips
     backward = (place(owner // CORES) - place(chip)) % chips
     near = jnp.where(core == 0, forward, backward)
     far = jnp.where(core == 0, backward, forward)
-    return sent, shared, [core, near, far]
-
-
-def pick_kernel(list_ref, group_ref, templates_ref, picked_ref, sem):
-    devices = picked_ref.shape[0]
-    for device in range(devices):
-        which = list_ref[device, group_ref[0]]
-        pltpu.make_async_copy(templates_ref.at[which], picked_ref.at[device], sem).start()
-    pltpu.make_async_copy(picked_ref, picked_ref, sem).wait()
-
-
-def pick(templates, lists, own_group):
-    devices = lists.shape[0]
-    smem, hbm = pl.BlockSpec(memory_space=pltpu.SMEM), pl.BlockSpec(memory_space=pl.ANY)
-    return pl.pallas_call(
-        pick_kernel,
-        out_shape=jax.ShapeDtypeStruct((devices, *templates.shape[1:]), templates.dtype),
-        in_specs=[smem, smem, hbm],
-        out_specs=hbm,
-        scratch_shapes=[pltpu.SemaphoreType.DMA],
-        compiler_params=pltpu.CompilerParams(vmem_limit_bytes=56 * 1024 * 1024),
-    )(lists, own_group.reshape(1).astype(jnp.int32), templates)
-
-
-def collect(templates, lists):
+    return sent, shared, [core, near, far], early
+
+
+def collect(templates, lists, first):
     devices, groups = lax.axis_size("tpl"), lax.axis_size("grp")
     own_group = lax.axis_index("grp")
     per_device = lists.shape[1]
@@ -134,7 +123,8 @@
     size = pieces // groups
     direct = size == 2 and rows == WAVE_ROWS
     if direct:
-        picked = pick(templates, lists, own_group).reshape(devices, size, rows, COLS)
+        picked = templates[lax.dynamic_index_in_dim(lists, own_group, 1, keepdims=False)]
+        picked, first = lax.optimization_barrier((picked.reshape(devices, size, rows, COLS), first))
     else:
         picked = templates[lists.reshape(-1)].reshape(devices, pieces, rows, COLS)
         picked = lax.dynamic_slice_in_dim(picked, own_group * size, size, 1)
@@ -143,14 +133,16 @@
     for turn in range(1, groups):
         found.append(lax.ppermute(own, "grp", [(i, (i + turn) % groups) for i in range(groups)]))
     if direct:
-        return found, [(own_group - turn) % groups for turn in range(groups)]
+        return found, [(own_group - turn) % groups for turn in range(groups)], first
     found = jnp.stack(found)[(own_group - jnp.arange(groups)) % groups]
     found = found.transpose(0, 2, 1, 3, 4).reshape(per_device, 2, ROWS // WAVE_ROWS, WAVE_ROWS, COLS)
-    return [found[at].transpose(1, 0, 2, 3) for at in range(per_device)], [jnp.int32(at) for at in range(per_device)]
+    found = [found[at].transpose(1, 0, 2, 3) for at in range(per_device)]
+    return found, [jnp.int32(at) for at in range(per_device)], first
 
 
 def held(values):
-    return values.astype(jnp.bfloat16).astype(jnp.float32)
+    scaled = values * 65537.0
+    return scaled - (scaled - values)
 
 
 def quarters(parts):
@@ -320,10 +312,11 @@
 
 def body(strain_slots, templates, cutoffs, lists, owner, slides):
     devices = lax.axis_size("tpl")
-    sent, shared, where = spread(strain_slots, owner[0])
-    waves, places = collect(templates, lists)
+    chunks = halves(strain_slots, owner[0])
+    waves, places, chunks[1] = collect(templates, lists, chunks[1])
+    sent, shared, where, turns = spread(chunks, owner[0], slide_turns(slides))
     where = jnp.stack([jnp.asarray(at, jnp.int32) for at in (*where, lax.axis_index("tpl"), *places)])
-    return filtered(sent, shared, where, devices // CORES, waves, cutoffs, lists, slide_turns(slides))
+    return filtered(sent, shared, where, devices // CORES, waves, cutoffs, lists, turns)
 
 
 def solution(mesh):

time: 153 us -> 138 us (0.902)
  Pallas kernels: 52.1 us -> 20.1 us
  waiting for transfers between devices: 38.6 us -> 58.3 us
  starting transfers between devices: 43.1 us -> 29 us
  other arithmetic: 3.57 us -> 10.3 us
  local copies, waits for them, and re-layouts: 12.7 us -> 17.4 us
    pallas_call x1 -> x0, Pallas kernels: 33.7 us -> none  [pick(): pl.pallas_call(pick_kernel, out_shape=jax.ShapeDtypeStruct((devices, *tem...]
    ppermute x18 -> x12, waiting for transfers between devices: 37.6 us -> 58.3 us  [spread(): arrived.append(lax.ppermute(here, 'tpl', along))]
    ppermute x18 -> x12, starting transfers between devices: 29.5 us -> 20.2 us  [spread(): arrived.append(lax.ppermute(here, 'tpl', along))]
    select_n x4 -> x5, other arithmetic: 0.15 us -> 3.6 us  [spread(): here = jnp.where(on_owner_chip, chunks[slot], arrived[slot - LAG])]
    all_to_all x1, starting transfers between devices: 7.05 us -> 4.07 us  [collect(): own = lax.all_to_all(picked, 'tpl', split_axis=0, concat_axis=0, tiled=True)]
    squeeze x3, local copies, waits for them, and re-layouts: 3.19 us -> 5.99 us  [halves(): lax.dynamic_slice(strain_slots, (0, det, 0, which * half), (1, 1, 2, half))]
    gather x0 -> x1, local copies, waits for them, and re-layouts: none -> 2.66 us  [collect(): templates[lax.dynamic_index_in_dim(lists, own_group, 1, keepdims=False)]]
    select_n x3 -> x4, other arithmetic: 2.83 us -> 5.46 us  [the longest x3 4.76 us: halves(): first = jnp.where(on_owner_core, side(core), got)]
  transfers between devices with their start and end apart: 43 -> 30, of which waited for: 17 -> 11; matrix products, arithmetic and copies ran while one was open for 9% -> 16% of each run, Pallas kernels for 22% -> 0%
where the time goes in v4:
time: 138 us; the launch traced here: 137 us
  waiting for transfers between devices  58.3 us (42%)
  starting transfers between devices  29 us (21%)
  Pallas kernels  20.1 us (15%)
  local copies, waits for them, and re-layouts  17.4 us (13%)
  other arithmetic  10.3 us (7%)
  between operations  1.75 us (1%)
    ppermute x12, waiting for transfers between devices, spread(): arrived.append(lax.ppermute(here, 'tpl', along))  58.3 us
    ppermute x12, starting transfers between devices, spread(): arrived.append(lax.ppermute(here, 'tpl', along))  20.2 us
    pallas_call x1, Pallas kernels, filtered(): pl.pallas_call(functools.partial(filter_kernel, chips, count), out_shape=...  20.1 us
    squeeze x3, local copies, waits for them, and re-layouts, halves(): lax.dynamic_slice(strain_slots, (0, det, 0, which * half), (1, 1, 2, half))  5.99 us
    select_n x3, other arithmetic, halves(): first = jnp.where(on_owner_core, side(core), got)  4.76 us
    all_to_all x1, starting transfers between devices, collect(): own = lax.all_to_all(picked, 'tpl', split_axis=0, concat_axis=0, tiled=True)  4.07 us
    select_n x5, other arithmetic, spread(): here = jnp.where(on_owner_chip, chunks[slot], arrived[slot - LAG])  3.6 us
  transfers between devices with their start and end apart: 30, of which 11 were waited for; matrix products, arithmetic and copies ran while one was open for 16% of the time, Pallas kernels for 0%

profile of v4, /device:TPU:0, one launch (start us, length us, event | category | flops | bytes accessed | tf_op | source)
XLA Modules:
  0.0 136.9 jit_solution(6036777102210380644)
XLA Ops:
  0.7 1.6 %dynamic-slice_bitcast_fusion.2 = bf16[2,131072]{1,0:T(2,128)(2,1)S(1)} fusion(bf16[1,3,2,262144]{3,2,1,0:T(2,128)(2,1)} %param.9, s32[]{:T(128)S(6)} %select_n.190), kind=kLoop, calls=%fused_computation.6 | loop fusion | bytes 1048580 | tf_op jit(solution)/shard_map/squeeze | solution.py:73
  2.2 0.5 collective-permute-start
  3.4 0.7 fusion.11
  4.1 0.9 fusion.7
  5.1 1.6 %broadcast_select_fusion.2 = bf16[2,131072]{1,0:T(2,128)(2,1)S(1)} fusion(bf16[2,131072]{1,0:T(2,128)(2,1)S(1)} %collective-permute-done, pred[]{:T(512)S(6)} %eq.38, bf16[1,3,2,262144]{3,2,1,0:T(2,128)(2,1)} %param.9, s32[]{:T(128)S(6)} %select_n.189), kind=kLoop, calls=%fused_computation.3 | loop fusion | flops 262144 | bytes 1572869 | tf_op jit(solution)/shard_map/jit(_where)/select_n | solution.py:75
  6.7 2.2 %dynamic-slice_bitcast_fusion.1 = bf16[2,131072]{1,0:T(2,128)(2,1)} fusion(bf16[1,3,2,262144]{3,2,1,0:T(2,128)(2,1)} %param.9, s32[]{:T(128)S(6)} %select_n.190), kind=kLoop, calls=%fused_computation.5 | loop fusion | bytes 1048580 | tf_op jit(solution)/shard_map/squeeze | solution.py:73
  9.0 1.1 fusion.14
  10.1 3.1 %collective-permute-start.1 = (bf16[2,128,512]{2,1,0:T(8,128)(2,1)S(1)}, bf16[2,128,512]{2,1,0:T(8,128)(2,1)}, u32[]{:S(2)}, u32[]{:S(2)}) collective-permute-start(bf16[2,128,512]{2,1,0:T(8,128)(2,1)S(1)} %bitcast.47), channel_id=1, source_target_pairs={{0,4},{5,1},{4,8},{9,5},{8,12},{13,9},{12,14},{15,13},{14,10},{11,... | collective-permute-start | bytes 786440 | tf_op jit(solution)/shard_map/ppermute | solution.py:105
  13.2 2.7 %gather_fusion = bf16[16,2,16384]{2,1,0:T(2,128)(2,1)S(1)} fusion(bf16[32,2,16384]{2,1,0:T(2,128)(2,1)S(1)} %copy-done, s32[1024]{0:T(1024)S(1)} %pad_clamp_fusion), kind=kCustom, calls=%fused_computation | custom fusion | bytes 2097216 | tf_op jit(solution)/shard_map/gather | solution.py:126
  15.8 1.6 %reshape.208 = bf16[16,2,32,512]{3,2,1,0:T(8,128)(2,1)} reshape(bf16[16,2,16384]{2,1,0:T(2,128)(2,1)S(1)} %gather_fusion) | data formatting | bytes 2097152 | tf_op jit(solution)/shard_map/reshape | solution.py:127
  17.4 0.6 broadcast_in_dim.5.refs_29_
  18.0 1.0 copy.25
  19.0 1.7 %broadcast_select_fusion.3.refs_1_ = bf16[2,128,512]{2,1,0:T(8,128)(2,1)} fusion(bf16[2,128,512]{2,1,0:T(8,128)(2,1)S(1)} %bitcast.51, bf16[2,128,512]{2,1,0:T(8,128)(2,1)} %collective-permute-done.1, pred[]{:T(512)S(6)} %eq.39), kind=kLoop, calls=%fused_computation.13 | loop fusion | flops 131072 | bytes 786433 | tf_op jit(solution)/shard_map/jit(_where)/select_n | solution.py:98
  20.7 0.6 collective-permute-start.3
  21.3 1.6 %broadcast_select_fusion.1 = bf16[2,131072]{1,0:T(2,128)(2,1)S(1)} fusion(bf16[2,131072]{1,0:T(2,128)(2,1)} %collective-permute-done.2, pred[]{:T(512)S(6)} %eq.38, bf16[1,3,2,262144]{3,2,1,0:T(2,128)(2,1)} %param.9, s32[]{:T(128)S(6)} %select_n.189), kind=kLoop, calls=%fused_computation.2 | loop fusion | flops 262144 | bytes 1572869 | tf_op jit(solution)/shard_map/jit(_where)/select_n | solution.py:75
  22.9 2.2 %dynamic-slice_bitcast_fusion = bf16[2,131072]{1,0:T(2,128)(2,1)} fusion(bf16[1,3,2,262144]{3,2,1,0:T(2,128)(2,1)} %param.9, s32[]{:T(128)S(6)} %select_n.190), kind=kLoop, calls=%fused_computation.4 | loop fusion | bytes 1048580 | tf_op jit(solution)/shard_map/squeeze | solution.py:73
  25.7 1.1 fusion.13
  26.7 0.6 collective-permute-done.3
  27.3 0.8 bitcast_select_fusion.3.refs_2_
  28.1 1.5 %collective-permute-start.4 = (bf16[2,128,512]{2,1,0:T(8,128)(2,1)}, bf16[2,128,512]{2,1,0:T(8,128)(2,1)}, u32[]{:S(2)}, u32[]{:S(2)}) collective-permute-start(bf16[2,128,512]{2,1,0:T(8,128)(2,1)} %bitcast_select_fusion.3.refs_2_), channel_id=1, source_target_pairs={{0,4},{5,1},{4,8},{9,5},{8,12},{13,9},{12,14},{15,13},{14,10},{11,... | collective-permute-start | bytes 786440 | tf_op jit(solution)/shard_map/ppermute | solution.py:105
  29.8 4.1 %all-to-all-start = ((bf16[16,2,32,512]{3,2,1,0:T(8,128)(2,1)}), bf16[16,2,32,512]{3,2,1,0:T(8,128)(2,1)S(1)}, u32[]{:S(2)}, u32[]{:S(2)}) async-start(bf16[16,2,32,512]{3,2,1,0:T(8,128)(2,1)} %reshape.208), calls=%async_computation | async-start | bytes 2097152 | tf_op jit(solution)/shard_map/all_to_all | solution.py:131
  33.9 0.8 collective-permute-done.4
  34.7 1.1 bitcast_select_fusion.2.refs_3_
  35.8 1.4 %collective-permute-start.6 = (bf16[2,128,512]{2,1,0:T(8,128)(2,1)S(1)}, bf16[2,128,512]{2,1,0:T(8,128)(2,1)S(1)}, u32[]{:S(2)}, u32[]{:S(2)}) collective-permute-start(bf16[2,128,512]{2,1,0:T(8,128)(2,1)S(1)} %bitcast_select_fusion.2.refs_3_), channel_id=1, source_target_pairs={{0,4},{5,1},{4,8},{9,5},{8,12},{13,9},{12,14},{15,13},{14,10},{11,... | collective-permute-start | bytes 786440 | tf_op jit(solution)/shard_map/ppermute | solution.py:105
  37.3 1.6 %broadcast_select_fusion = bf16[2,131072]{1,0:T(2,128)(2,1)S(1)} fusion(bf16[2,131072]{1,0:T(2,128)(2,1)} %collective-permute-done.5, pred[]{:T(512)S(6)} %eq.38, bf16[1,3,2,262144]{3,2,1,0:T(2,128)(2,1)} %param.9, s32[]{:T(128)S(6)} %select_n.189), kind=kLoop, calls=%fused_computation.1 | loop fusion | flops 262144 | bytes 1572869 | tf_op jit(solution)/shard_map/jit(_where)/select_n | solution.py:75
  39.2 15.5 %collective-permute-done.6 = bf16[2,128,512]{2,1,0:T(8,128)(2,1)S(1)} collective-permute-done((bf16[2,128,512]{2,1,0:T(8,128)(2,1)S(1)}, bf16[2,128,512]{2,1,0:T(8,128)(2,1)S(1)}, u32[]{:S(2)}, u32[]{:S(2)}) %collective-permute-start.6) | collective-permute-done | bytes 262176 | tf_op jit(solution)/shard_map/ppermute | solution.py:105
  54.8 7.2 %collective-permute-start.7 = (bf16[2,128,512]{2,1,0:T(8,128)(2,1)S(1)}, bf16[2,128,512]{2,1,0:T(8,128)(2,1)S(1)}, u32[]{:S(2)}, u32[]{:S(2)}) collective-permute-start(bf16[2,128,512]{2,1,0:T(8,128)(2,1)S(1)} %bitcast_select_fusion.1.refs_4_), channel_id=1, source_target_pairs={{0,4},{5,1},{4,8},{9,5},{8,12},{13,9},{12,14},{15,13},{14,10},{11,... | collective-permute-start | bytes 786440 | tf_op jit(solution)/shard_map/ppermute | solution.py:105
  62.0 3.9 %collective-permute-done.7 = bf16[2,128,512]{2,1,0:T(8,128)(2,1)S(1)} collective-permute-done((bf16[2,128,512]{2,1,0:T(8,128)(2,1)S(1)}, bf16[2,128,512]{2,1,0:T(8,128)(2,1)S(1)}, u32[]{:S(2)}, u32[]{:S(2)}) %collective-permute-start.7) | collective-permute-done | bytes 262176 | tf_op jit(solution)/shard_map/ppermute | solution.py:105
  66.0 2.5 %collective-permute-start.8 = (bf16[2,128,512]{2,1,0:T(8,128)(2,1)S(1)}, bf16[2,128,512]{2,1,0:T(8,128)(2,1)S(1)}, u32[]{:S(2)}, u32[]{:S(2)}) collective-permute-start(bf16[2,128,512]{2,1,0:T(8,128)(2,1)S(1)} %bitcast_select_fusion.refs_5_), channel_id=1, source_target_pairs={{0,4},{5,1},{4,8},{9,5},{8,12},{13,9},{12,14},{15,13},{14,10},{11,... | collective-permute-start | bytes 786440 | tf_op jit(solution)/shard_map/ppermute | solution.py:105
  68.5 5.7 %collective-permute-done.8.refs_6_ = bf16[2,128,512]{2,1,0:T(8,128)(2,1)S(1)} collective-permute-done((bf16[2,128,512]{2,1,0:T(8,128)(2,1)S(1)}, bf16[2,128,512]{2,1,0:T(8,128)(2,1)S(1)}, u32[]{:S(2)}, u32[]{:S(2)}) %collective-permute-start.8) | collective-permute-done | bytes 262176 | tf_op jit(solution)/shard_map/ppermute | solution.py:105
  74.2 0.6 collective-permute-start.9
  74.9 5.7 %collective-permute-done.9.refs_7_ = bf16[2,128,512]{2,1,0:T(8,128)(2,1)S(1)} collective-permute-done((bf16[2,128,512]{2,1,0:T(8,128)(2,1)S(1)}, bf16[2,128,512]{2,1,0:T(8,128)(2,1)S(1)}, u32[]{:S(2)}, u32[]{:S(2)}) %collective-permute-start.9) | collective-permute-done | bytes 262176 | tf_op jit(solution)/shard_map/ppermute | solution.py:105
  80.6 0.6 collective-permute-start.10
  81.2 5.7 %collective-permute-done.10.refs_8_ = bf16[2,128,512]{2,1,0:T(8,128)(2,1)S(1)} collective-permute-done((bf16[2,128,512]{2,1,0:T(8,128)(2,1)S(1)}, bf16[2,128,512]{2,1,0:T(8,128)(2,1)S(1)}, u32[]{:S(2)}, u32[]{:S(2)}) %collective-permute-start.10) | collective-permute-done | bytes 262176 | tf_op jit(solution)/shard_map/ppermute | solution.py:105
  87.0 0.6 collective-permute-start.11
  87.6 0.5 collective-permute-start.16
  88.1 5.3 %collective-permute-done.11.refs_9_ = bf16[2,128,512]{2,1,0:T(8,128)(2,1)} collective-permute-done((bf16[2,128,512]{2,1,0:T(8,128)(2,1)S(1)}, bf16[2,128,512]{2,1,0:T(8,128)(2,1)}, u32[]{:S(2)}, u32[]{:S(2)}) %collective-permute-start.11) | collective-permute-done | bytes 262176 | tf_op jit(solution)/shard_map/ppermute | solution.py:105
  93.5 0.7 collective-permute-start.12
  94.2 1.5 %collective-permute-start.28 = (bf16[16,2,32,512]{3,2,1,0:T(8,128)(2,1)S(1)}, bf16[16,2,32,512]{3,2,1,0:T(8,128)(2,1)}, u32[]{:S(2)}, u32[]{:S(2)}) collective-permute-start(bf16[16,2,32,512]{3,2,1,0:T(8,128)(2,1)S(1)} %all-to-all-done.refs_26_), channel_id=1, source_target_pairs={{0,16},{16,0},{1,17},{17,1},{2,18},{18,2},{3,19},{19,3},{4,20},{20... | collective-permute-start | bytes 3145736 | tf_op jit(solution)/shard_map/ppermute | solution.py:134
  96.2 4.0 %collective-permute-done.12.refs_10_ = bf16[2,128,512]{2,1,0:T(8,128)(2,1)} collective-permute-done((bf16[2,128,512]{2,1,0:T(8,128)(2,1)}, bf16[2,128,512]{2,1,0:T(8,128)(2,1)}, u32[]{:S(2)}, u32[]{:S(2)}) %collective-permute-start.12) | collective-permute-done | bytes 262176 | tf_op jit(solution)/shard_map/ppermute | solution.py:105
  100.2 0.6 collective-permute-start.13
  101.5 5.5 %collective-permute-done.13.refs_11_ = bf16[2,128,512]{2,1,0:T(8,128)(2,1)} collective-permute-done((bf16[2,128,512]{2,1,0:T(8,128)(2,1)}, bf16[2,128,512]{2,1,0:T(8,128)(2,1)}, u32[]{:S(2)}, u32[]{:S(2)}) %collective-permute-start.13) | collective-permute-done | bytes 262176 | tf_op jit(solution)/shard_map/ppermute | solution.py:105
  106.9 0.6 collective-permute-start.14
  108.2 5.5 %collective-permute-done.14.refs_12_ = bf16[2,128,512]{2,1,0:T(8,128)(2,1)} collective-permute-done((bf16[2,128,512]{2,1,0:T(8,128)(2,1)}, bf16[2,128,512]{2,1,0:T(8,128)(2,1)}, u32[]{:S(2)}, u32[]{:S(2)}) %collective-permute-start.14) | collective-permute-done | bytes 262176 | tf_op jit(solution)/shard_map/ppermute | solution.py:105
  113.6 0.7 copy.11.list_ref
  114.3 0.6 stack.37.where_ref
  114.9 1.7 %copy.12.refs_28_ = f32[3,2,512,1]{3,2,1,0:T(8,128)} copy(f32[3,2,512,1]{2,1,0,3:T(2,128)S(1)} %maximum_bitcast_fusion) | data formatting | bytes 24576 | tf_op jit(solution)/shard_map/optimization_barrier | solution.py:102
  116.7 20.1 %shard_map.104 = (f32[2]{0:T(128)}, f32[2]{0:T(128)}) custom-call(s32[32]{0:T(128)} %cut_ref.1, s32[16,2]{1,0:T(8,128)} %copy.11.list_ref, s32[6]{0:T(128)} %stack.37.where_ref, bf16[2,128,512]{2,1,0:T(8,128)(2,1)} %bitcast.49, bf16[2,128,512]{2,1,0:T(8,128)(2,1)} %broadcast_select_fusion.3.refs_1_, bf16[2,128,512]{2,1,0:T(8,128)(2,1)} %bitcast_select_fusion.3.refs_2_, ...), custom_call_target="tpu_custom_call" | custom-call | tf_op jit(solution)/shard_map/pallas_call | solution.py:288
  (66 shorter events, 3.2 us)
Async XLA Ops:
  0.6 12.5 %copy-start = (bf16[32,2,16384]{2,1,0:T(2,128)(2,1)S(1)}, bf16[32,2,16384]{2,1,0:T(2,128)(2,1)}, u32[]{:S(2)}) copy-start(bf16[32,2,16384]{2,1,0:T(2,128)(2,1)} %param.10) | copy-start | bytes 6291460
  2.2 2.9 %collective-permute-start = (bf16[2,131072]{1,0:T(2,128)(2,1)S(1)}, bf16[2,131072]{1,0:T(2,128)(2,1)S(1)}, u32[]{:S(2)}, u32[]{:S(2)}) collective-permute-start(bf16[2,131072]{1,0:T(2,128)(2,1)S(1)} %dynamic-slice_bitcast_fusion.2), channel_id=1, source_target_pairs={{0,1},{1,0},{2,3},{3,2},{4,5},{5,4},{6,7},{7,6},{8,9},{9,8},{10,11... | collective-permute-start | bytes 1572872 | tf_op jit(solution)/shard_map/ppermute | solution.py:74
  8.9 9.1 %copy-start.11 = (s32[3]{0:T(128)S(1)}, s32[3]{0:T(128)}, u32[]{:S(2)}) copy-start(s32[3]{0:T(128)} %param.14) | copy-start | bytes 40
  8.9 12.5 %collective-permute-start.2 = (bf16[2,131072]{1,0:T(2,128)(2,1)}, bf16[2,131072]{1,0:T(2,128)(2,1)}, u32[]{:S(2)}, u32[]{:S(2)}) collective-permute-start(bf16[2,131072]{1,0:T(2,128)(2,1)} %dynamic-slice_bitcast_fusion.1), channel_id=1, source_target_pairs={{0,1},{1,0},{2,3},{3,2},{4,5},{5,4},{6,7},{7,6},{8,9},{9,8},{10,11... | collective-permute-start | bytes 1572872 | tf_op jit(solution)/shard_map/ppermute | solution.py:74
  10.1 77.6 %copy-start.2 = (bf16[1,2,128,512]{3,2,1,0:T(8,128)(2,1)}, bf16[1,2,128,512]{3,2,1,0:T(8,128)(2,1)S(1)}, u32[]{:S(2)}) copy-start(bf16[1,2,128,512]{3,2,1,0:T(8,128)(2,1)S(1)} %copy.26) | copy-start | bytes 786436
  10.1 8.9 %collective-permute-start.1 = (bf16[2,128,512]{2,1,0:T(8,128)(2,1)S(1)}, bf16[2,128,512]{2,1,0:T(8,128)(2,1)}, u32[]{:S(2)}, u32[]{:S(2)}) collective-permute-start(bf16[2,128,512]{2,1,0:T(8,128)(2,1)S(1)} %bitcast.47), channel_id=1, source_target_pairs={{0,4},{5,1},{4,8},{9,5},{8,12},{13,9},{12,14},{15,13},{14,10},{11,... | collective-permute-start | bytes 786440 | tf_op jit(solution)/shard_map/ppermute | solution.py:105
  20.7 6.6 %collective-permute-start.3 = (bf16[2,128,512]{2,1,0:T(8,128)(2,1)}, bf16[2,128,512]{2,1,0:T(8,128)(2,1)S(1)}, u32[]{:S(2)}, u32[]{:S(2)}) collective-permute-start(bf16[2,128,512]{2,1,0:T(8,128)(2,1)} %broadcast_select_fusion.3.refs_1_), channel_id=1, source_target_pairs={{0,4},{5,1},{4,8},{9,5},{8,12},{13,9},{12,14},{15,13},{14,10},{11,... | collective-permute-start | bytes 786440 | tf_op jit(solution)/shard_map/ppermute | solution.py:105
  25.2 12.1 %collective-permute-start.5 = (bf16[2,131072]{1,0:T(2,128)(2,1)}, bf16[2,131072]{1,0:T(2,128)(2,1)}, u32[]{:S(2)}, u32[]{:S(2)}) collective-permute-start(bf16[2,131072]{1,0:T(2,128)(2,1)} %dynamic-slice_bitcast_fusion), channel_id=1, source_target_pairs={{0,1},{1,0},{2,3},{3,2},{4,5},{5,4},{6,7},{7,6},{8,9},{9,8},{10,11... | collective-permute-start | bytes 1572872 | tf_op jit(solution)/shard_map/ppermute | solution.py:74
  28.1 6.7 %collective-permute-start.4 = (bf16[2,128,512]{2,1,0:T(8,128)(2,1)}, bf16[2,128,512]{2,1,0:T(8,128)(2,1)}, u32[]{:S(2)}, u32[]{:S(2)}) collective-permute-start(bf16[2,128,512]{2,1,0:T(8,128)(2,1)} %bitcast_select_fusion.3.refs_2_), channel_id=1, source_target_pairs={{0,4},{5,1},{4,8},{9,5},{8,12},{13,9},{12,14},{15,13},{14,10},{11,... | collective-permute-start | bytes 786440 | tf_op jit(solution)/shard_map/ppermute | solution.py:105
  29.8 83.8 %copy-start.10 = (s32[16,2]{0,1:T(2,128)S(1)}, s32[16,2]{0,1:T(2,128)}, u32[]{:S(2)}) copy-start(s32[16,2]{0,1:T(2,128)} %param.12) | copy-start | bytes 388
  29.8 64.4 %all-to-all-start = ((bf16[16,2,32,512]{3,2,1,0:T(8,128)(2,1)}), bf16[16,2,32,512]{3,2,1,0:T(8,128)(2,1)S(1)}, u32[]{:S(2)}, u32[]{:S(2)}) async-start(bf16[16,2,32,512]{3,2,1,0:T(8,128)(2,1)} %reshape.208), calls=%async_computation | async-start | bytes 2097152 | tf_op jit(solution)/shard_map/all_to_all | solution.py:131
  35.8 57.6 %copy-start.3 = (bf16[2,128,512]{2,1,0:T(8,128)(2,1)}, bf16[2,128,512]{2,1,0:T(8,128)(2,1)S(1)}, u32[]{:S(2)}) copy-start(bf16[2,128,512]{2,1,0:T(8,128)(2,1)S(1)} %bitcast_select_fusion.2.refs_3_) | copy-start | bytes 786436
  35.8 18.9 %collective-permute-start.6 = (bf16[2,128,512]{2,1,0:T(8,128)(2,1)S(1)}, bf16[2,128,512]{2,1,0:T(8,128)(2,1)S(1)}, u32[]{:S(2)}, u32[]{:S(2)}) collective-permute-start(bf16[2,128,512]{2,1,0:T(8,128)(2,1)S(1)} %bitcast_select_fusion.2.refs_3_), channel_id=1, source_target_pairs={{0,4},{5,1},{4,8},{9,5},{8,12},{13,9},{12,14},{15,13},{14,10},{11,... | collective-permute-start | bytes 786440 | tf_op jit(solution)/shard_map/ppermute | solution.py:105
  54.8 38.7 %copy-start.4 = (bf16[2,128,512]{2,1,0:T(8,128)(2,1)}, bf16[2,128,512]{2,1,0:T(8,128)(2,1)S(1)}, u32[]{:S(2)}) copy-start(bf16[2,128,512]{2,1,0:T(8,128)(2,1)S(1)} %bitcast_select_fusion.1.refs_4_) | copy-start | bytes 786436
  54.8 11.1 %collective-permute-start.7 = (bf16[2,128,512]{2,1,0:T(8,128)(2,1)S(1)}, bf16[2,128,512]{2,1,0:T(8,128)(2,1)S(1)}, u32[]{:S(2)}, u32[]{:S(2)}) collective-permute-start(bf16[2,128,512]{2,1,0:T(8,128)(2,1)S(1)} %bitcast_select_fusion.1.refs_4_), channel_id=1, source_target_pairs={{0,4},{5,1},{4,8},{9,5},{8,12},{13,9},{12,14},{15,13},{14,10},{11,... | collective-permute-start | bytes 786440 | tf_op jit(solution)/shard_map/ppermute | solution.py:105
  65.9 27.5 %copy-start.5 = (bf16[2,128,512]{2,1,0:T(8,128)(2,1)}, bf16[2,128,512]{2,1,0:T(8,128)(2,1)S(1)}, u32[]{:S(2)}) copy-start(bf16[2,128,512]{2,1,0:T(8,128)(2,1)S(1)} %bitcast_select_fusion.refs_5_) | copy-start | bytes 786436
  66.0 8.3 %collective-permute-start.8 = (bf16[2,128,512]{2,1,0:T(8,128)(2,1)S(1)}, bf16[2,128,512]{2,1,0:T(8,128)(2,1)S(1)}, u32[]{:S(2)}, u32[]{:S(2)}) collective-permute-start(bf16[2,128,512]{2,1,0:T(8,128)(2,1)S(1)} %bitcast_select_fusion.refs_5_), channel_id=1, source_target_pairs={{0,4},{5,1},{4,8},{9,5},{8,12},{13,9},{12,14},{15,13},{14,10},{11,... | collective-permute-start | bytes 786440 | tf_op jit(solution)/shard_map/ppermute | solution.py:105
  74.2 19.2 %copy-start.6 = (bf16[2,128,512]{2,1,0:T(8,128)(2,1)}, bf16[2,128,512]{2,1,0:T(8,128)(2,1)S(1)}, u32[]{:S(2)}) copy-start(bf16[2,128,512]{2,1,0:T(8,128)(2,1)S(1)} %collective-permute-done.8.refs_6_) | copy-start | bytes 786436
  74.2 6.4 %collective-permute-start.9 = (bf16[2,128,512]{2,1,0:T(8,128)(2,1)S(1)}, bf16[2,128,512]{2,1,0:T(8,128)(2,1)S(1)}, u32[]{:S(2)}, u32[]{:S(2)}) collective-permute-start(bf16[2,128,512]{2,1,0:T(8,128)(2,1)S(1)} %collective-permute-done.8.refs_6_), channel_id=1, source_target_pairs={{0,4},{5,1},{4,8},{9,5},{8,12},{13,9},{12,14},{15,13},{14,10},{11,... | collective-permute-start | bytes 786440 | tf_op jit(solution)/shard_map/ppermute | solution.py:105
  80.6 12.9 %copy-start.7 = (bf16[2,128,512]{2,1,0:T(8,128)(2,1)}, bf16[2,128,512]{2,1,0:T(8,128)(2,1)S(1)}, u32[]{:S(2)}) copy-start(bf16[2,128,512]{2,1,0:T(8,128)(2,1)S(1)} %collective-permute-done.9.refs_7_) | copy-start | bytes 786436
  80.6 6.4 %collective-permute-start.10 = (bf16[2,128,512]{2,1,0:T(8,128)(2,1)S(1)}, bf16[2,128,512]{2,1,0:T(8,128)(2,1)S(1)}, u32[]{:S(2)}, u32[]{:S(2)}) collective-permute-start(bf16[2,128,512]{2,1,0:T(8,128)(2,1)S(1)} %collective-permute-done.9.refs_7_), channel_id=1, source_target_pairs={{0,4},{5,1},{4,8},{9,5},{8,12},{13,9},{12,14},{15,13},{14,10},{11,... | collective-permute-start | bytes 786440 | tf_op jit(solution)/shard_map/ppermute | solution.py:105
  87.0 6.5 %copy-start.8 = (bf16[2,128,512]{2,1,0:T(8,128)(2,1)}, bf16[2,128,512]{2,1,0:T(8,128)(2,1)S(1)}, u32[]{:S(2)}) copy-start(bf16[2,128,512]{2,1,0:T(8,128)(2,1)S(1)} %collective-permute-done.10.refs_8_) | copy-start | bytes 786436
  87.0 6.5 %collective-permute-start.11 = (bf16[2,128,512]{2,1,0:T(8,128)(2,1)S(1)}, bf16[2,128,512]{2,1,0:T(8,128)(2,1)}, u32[]{:S(2)}, u32[]{:S(2)}) collective-permute-start(bf16[2,128,512]{2,1,0:T(8,128)(2,1)S(1)} %collective-permute-done.10.refs_8_), channel_id=1, source_target_pairs={{0,4},{5,1},{4,8},{9,5},{8,12},{13,9},{12,14},{15,13},{14,10},{11,... | collective-permute-start | bytes 786440 | tf_op jit(solution)/shard_map/ppermute | solution.py:105
  87.6 8.0 %collective-permute-start.15 = (bf16[2,128,512]{2,1,0:T(8,128)(2,1)S(1)}, bf16[2,128,512]{2,1,0:T(8,128)(2,1)}, u32[]{:S(2)}, u32[]{:S(2)}) collective-permute-start(bf16[2,128,512]{2,1,0:T(8,128)(2,1)S(1)} %bitcast.48), channel_id=1, source_target_pairs={{0,1},{1,0},{2,3},{3,2},{4,5},{5,4},{6,7},{7,6},{8,9},{9,8},{10,11... | collective-permute-start | bytes 786440 | tf_op jit(solution)/shard_map/ppermute | solution.py:106
  87.6 8.0 %collective-permute-start.16 = (bf16[2,128,512]{2,1,0:T(8,128)(2,1)}, bf16[2,128,512]{2,1,0:T(8,128)(2,1)}, u32[]{:S(2)}, u32[]{:S(2)}) collective-permute-start(bf16[2,128,512]{2,1,0:T(8,128)(2,1)} %broadcast_select_fusion.3.refs_1_), channel_id=1, source_target_pairs={{0,1},{1,0},{2,3},{3,2},{4,5},{5,4},{6,7},{7,6},{8,9},{9,8},{10,11... | collective-permute-start | bytes 786440 | tf_op jit(solution)/shard_map/ppermute | solution.py:106
  88.1 8.0 %collective-permute-start.17 = (bf16[2,128,512]{2,1,0:T(8,128)(2,1)}, bf16[2,128,512]{2,1,0:T(8,128)(2,1)}, u32[]{:S(2)}, u32[]{:S(2)}) collective-permute-start(bf16[2,128,512]{2,1,0:T(8,128)(2,1)} %bitcast_select_fusion.3.refs_2_), channel_id=1, source_target_pairs={{0,1},{1,0},{2,3},{3,2},{4,5},{5,4},{6,7},{7,6},{8,9},{9,8},{10,11... | collective-permute-start | bytes 786440 | tf_op jit(solution)/shard_map/ppermute | solution.py:106
  93.5 6.7 %collective-permute-start.12 = (bf16[2,128,512]{2,1,0:T(8,128)(2,1)}, bf16[2,128,512]{2,1,0:T(8,128)(2,1)}, u32[]{:S(2)}, u32[]{:S(2)}) collective-permute-start(bf16[2,128,512]{2,1,0:T(8,128)(2,1)} %collective-permute-done.11.refs_9_), channel_id=1, source_target_pairs={{0,4},{5,1},{4,8},{9,5},{8,12},{13,9},{12,14},{15,13},{14,10},{11,... | collective-permute-start | bytes 786440 | tf_op jit(solution)/shard_map/ppermute | solution.py:105
  94.2 22.5 %copy-start.1 = (bf16[16,2,32,512]{3,2,1,0:T(8,128)(2,1)}, bf16[16,2,32,512]{3,2,1,0:T(8,128)(2,1)S(1)}, u32[]{:S(2)}) copy-start(bf16[16,2,32,512]{3,2,1,0:T(8,128)(2,1)S(1)} %all-to-all-done.refs_26_) | copy-start | bytes 3145732
  94.2 22.4 %collective-permute-start.28 = (bf16[16,2,32,512]{3,2,1,0:T(8,128)(2,1)S(1)}, bf16[16,2,32,512]{3,2,1,0:T(8,128)(2,1)}, u32[]{:S(2)}, u32[]{:S(2)}) collective-permute-start(bf16[16,2,32,512]{3,2,1,0:T(8,128)(2,1)S(1)} %all-to-all-done.refs_26_), channel_id=1, source_target_pairs={{0,16},{16,0},{1,17},{17,1},{2,18},{18,2},{3,19},{19,3},{4,20},{20... | collective-permute-start | bytes 3145736 | tf_op jit(solution)/shard_map/ppermute | solution.py:134
  95.6 5.2 %collective-permute-start.18 = (bf16[2,128,512]{2,1,0:T(8,128)(2,1)}, bf16[2,128,512]{2,1,0:T(8,128)(2,1)S(1)}, u32[]{:S(2)}, u32[]{:S(2)}) collective-permute-start(bf16[2,128,512]{2,1,0:T(8,128)(2,1)} %copy-done.3), channel_id=1, source_target_pairs={{0,1},{1,0},{2,3},{3,2},{4,5},{5,4},{6,7},{7,6},{8,9},{9,8},{10,11... | collective-permute-start | bytes 786440 | tf_op jit(solution)/shard_map/ppermute | solution.py:106
  95.7 5.2 %collective-permute-start.19 = (bf16[2,128,512]{2,1,0:T(8,128)(2,1)}, bf16[2,128,512]{2,1,0:T(8,128)(2,1)}, u32[]{:S(2)}, u32[]{:S(2)}) collective-permute-start(bf16[2,128,512]{2,1,0:T(8,128)(2,1)} %copy-done.4), channel_id=1, source_target_pairs={{0,1},{1,0},{2,3},{3,2},{4,5},{5,4},{6,7},{7,6},{8,9},{9,8},{10,11... | collective-permute-start | bytes 786440 | tf_op jit(solution)/shard_map/ppermute | solution.py:106
  96.2 5.2 %collective-permute-start.20 = (bf16[2,128,512]{2,1,0:T(8,128)(2,1)}, bf16[2,128,512]{2,1,0:T(8,128)(2,1)}, u32[]{:S(2)}, u32[]{:S(2)}) collective-permute-start(bf16[2,128,512]{2,1,0:T(8,128)(2,1)} %copy-done.5), channel_id=1, source_target_pairs={{0,1},{1,0},{2,3},{3,2},{4,5},{5,4},{6,7},{7,6},{8,9},{9,8},{10,11... | collective-permute-start | bytes 786440 | tf_op jit(solution)/shard_map/ppermute | solution.py:106
  100.2 6.7 %collective-permute-start.13 = (bf16[2,128,512]{2,1,0:T(8,128)(2,1)}, bf16[2,128,512]{2,1,0:T(8,128)(2,1)}, u32[]{:S(2)}, u32[]{:S(2)}) collective-permute-start(bf16[2,128,512]{2,1,0:T(8,128)(2,1)} %collective-permute-done.12.refs_10_), channel_id=1, source_target_pairs={{0,4},{5,1},{4,8},{9,5},{8,12},{13,9},{12,14},{15,13},{14,10},{11,... | collective-permute-start | bytes 786440 | tf_op jit(solution)/shard_map/ppermute | solution.py:105
  100.9 15.8 %copy-start.9 = (bf16[2,128,512]{2,1,0:T(8,128)(2,1)}, bf16[2,128,512]{2,1,0:T(8,128)(2,1)S(1)}, u32[]{:S(2)}) copy-start(bf16[2,128,512]{2,1,0:T(8,128)(2,1)S(1)} %collective-permute-done.18.refs_16_) | copy-start | bytes 786436
  100.9 6.7 %collective-permute-start.21 = (bf16[2,128,512]{2,1,0:T(8,128)(2,1)}, bf16[2,128,512]{2,1,0:T(8,128)(2,1)}, u32[]{:S(2)}, u32[]{:S(2)}) collective-permute-start(bf16[2,128,512]{2,1,0:T(8,128)(2,1)} %copy-done.6), channel_id=1, source_target_pairs={{0,1},{1,0},{2,3},{3,2},{4,5},{5,4},{6,7},{7,6},{8,9},{9,8},{10,11... | collective-permute-start | bytes 786440 | tf_op jit(solution)/shard_map/ppermute | solution.py:106
  100.9 6.7 %collective-permute-start.22 = (bf16[2,128,512]{2,1,0:T(8,128)(2,1)}, bf16[2,128,512]{2,1,0:T(8,128)(2,1)}, u32[]{:S(2)}, u32[]{:S(2)}) collective-permute-start(bf16[2,128,512]{2,1,0:T(8,128)(2,1)} %copy-done.7), channel_id=1, source_target_pairs={{0,1},{1,0},{2,3},{3,2},{4,5},{5,4},{6,7},{7,6},{8,9},{9,8},{10,11... | collective-permute-start | bytes 786440 | tf_op jit(solution)/shard_map/ppermute | solution.py:106
  101.4 6.7 %collective-permute-start.23 = (bf16[2,128,512]{2,1,0:T(8,128)(2,1)}, bf16[2,128,512]{2,1,0:T(8,128)(2,1)}, u32[]{:S(2)}, u32[]{:S(2)}) collective-permute-start(bf16[2,128,512]{2,1,0:T(8,128)(2,1)} %copy-done.8), channel_id=1, source_target_pairs={{0,1},{1,0},{2,3},{3,2},{4,5},{5,4},{6,7},{7,6},{8,9},{9,8},{10,11... | collective-permute-start | bytes 786440 | tf_op jit(solution)/shard_map/ppermute | solution.py:106
  106.9 6.7 %collective-permute-start.14 = (bf16[2,128,512]{2,1,0:T(8,128)(2,1)}, bf16[2,128,512]{2,1,0:T(8,128)(2,1)}, u32[]{:S(2)}, u32[]{:S(2)}) collective-permute-start(bf16[2,128,512]{2,1,0:T(8,128)(2,1)} %collective-permute-done.13.refs_11_), channel_id=1, source_target_pairs={{0,4},{5,1},{4,8},{9,5},{8,12},{13,9},{12,14},{15,13},{14,10},{11,... | collective-permute-start | bytes 786440 | tf_op jit(solution)/shard_map/ppermute | solution.py:105
  107.6 9.0 %collective-permute-start.24 = (bf16[2,128,512]{2,1,0:T(8,128)(2,1)}, bf16[2,128,512]{2,1,0:T(8,128)(2,1)}, u32[]{:S(2)}, u32[]{:S(2)}) collective-permute-start(bf16[2,128,512]{2,1,0:T(8,128)(2,1)} %collective-permute-done.11.refs_9_), channel_id=1, source_target_pairs={{0,1},{1,0},{2,3},{3,2},{4,5},{5,4},{6,7},{7,6},{8,9},{9,8},{10,11... | collective-permute-start | bytes 786440 | tf_op jit(solution)/shard_map/ppermute | solution.py:106
  107.6 9.0 %collective-permute-start.25 = (bf16[2,128,512]{2,1,0:T(8,128)(2,1)}, bf16[2,128,512]{2,1,0:T(8,128)(2,1)}, u32[]{:S(2)}, u32[]{:S(2)}) collective-permute-start(bf16[2,128,512]{2,1,0:T(8,128)(2,1)} %collective-permute-done.12.refs_10_), channel_id=1, source_target_pairs={{0,1},{1,0},{2,3},{3,2},{4,5},{5,4},{6,7},{7,6},{8,9},{9,8},{10,11... | collective-permute-start | bytes 786440 | tf_op jit(solution)/shard_map/ppermute | solution.py:106
  108.1 8.5 %collective-permute-start.26 = (bf16[2,128,512]{2,1,0:T(8,128)(2,1)}, bf16[2,128,512]{2,1,0:T(8,128)(2,1)}, u32[]{:S(2)}, u32[]{:S(2)}) collective-permute-start(bf16[2,128,512]{2,1,0:T(8,128)(2,1)} %collective-permute-done.13.refs_11_), channel_id=1, source_target_pairs={{0,1},{1,0},{2,3},{3,2},{4,5},{5,4},{6,7},{7,6},{8,9},{9,8},{10,11... | collective-permute-start | bytes 786440 | tf_op jit(solution)/shard_map/ppermute | solution.py:106
  113.6 3.0 %collective-permute-start.27 = (bf16[2,128,512]{2,1,0:T(8,128)(2,1)}, bf16[2,128,512]{2,1,0:T(8,128)(2,1)}, u32[]{:S(2)}, u32[]{:S(2)}) collective-permute-start(bf16[2,128,512]{2,1,0:T(8,128)(2,1)} %collective-permute-done.14.refs_12_), channel_id=1, source_target_pairs={{0,1},{1,0},{2,3},{3,2},{4,5},{5,4},{6,7},{7,6},{8,9},{9,8},{10,11... | collective-permute-start | bytes 786440 | tf_op jit(solution)/shard_map/ppermute | solution.py:106

commit v5 on v4

v5 whole, which is shorter than its diff:
```python
import functools

import jax
import jax.numpy as jnp
import numpy as np
from jax import lax
from jax.experimental import pallas as pl
from jax.experimental.pallas import tpu as pltpu
from jax.sharding import PartitionSpec as P

DET = 3
ROWS = 512
COLS = 512
RADIX = 4
PART = 128
ROW_STEP = 16
WAVE_ROWS = 32
CORES = 2
PAIR = 2
QUAD = CORES * PAIR
VMEM_LIMIT = 24 * 1024 * 1024


two_pi = 6.283185307179586
eps_norm = 1e-06


def turn_table(left_ids, right_ids, period):
    angles = (left_ids[:, None] * right_ids[None, :] % period).astype(np.float64) * (2 * np.pi / period)
    return np.cos(angles), np.sin(angles)


def tables():
    part_ids, col_ids = np.arange(PART), np.arange(COLS)
    row_tables, col_tables, turns = [], [], []
    for residue in range(RADIX):
        cos, sin = turn_table(RADIX * part_ids + residue, part_ids, ROWS)
        row_tables.append(np.block([[cos, -sin], [sin, cos]]))
        col_tables.append(np.block([[cos.T, sin.T], [-sin.T, cos.T]]))
        turns.append(np.stack(turn_table(RADIX * part_ids + residue, col_ids, ROWS * COLS)))
    return (
        jnp.asarray(np.stack(row_tables), jnp.float32).astype(jnp.bfloat16),
        jnp.asarray(np.stack(col_tables), jnp.float32).astype(jnp.bfloat16),
        jnp.asarray(np.stack(turns), jnp.float32),
    )


def slide_turns(slides):
    total = ROWS * COLS
    row_turns = (jnp.arange(ROWS, dtype=jnp.int32)[None, :] * (COLS * slides % total)[:, None]) % total
    col_turns = (jnp.arange(COLS, dtype=jnp.int32)[None, :] * slides[:, None]) % total
    row_angles = row_turns.astype(jnp.float32) * (two_pi / total)
    col_angles = col_turns.astype(jnp.float32) * (two_pi / total)
    rows = jnp.stack([jnp.cos(row_angles), jnp.sin(row_angles)], 1)[..., None]
    cols = jnp.stack([jnp.cos(col_angles), jnp.sin(col_angles)], 1)[:, :, None, :]
    return rows, cols


def partner(flip):
    return [(at, at ^ flip) for at in range(lax.axis_size("tpl"))]


def swap(block, flip):
    return lax.ppermute(block, "tpl", partner(flip))


def quarter_of(strain_slots, det, owner):
    me = lax.axis_index("tpl")
    core, chip = me % CORES, me // CORES % PAIR
    half = ROWS * COLS // CORES
    bins = half // PAIR
    side = lambda which: lax.dynamic_slice(strain_slots, (0, det, 0, which * half), (1, 1, 2, half))[0, 0]
    got = swap(side(1 - core), 1)
    kept = jnp.where(core == owner % CORES, side(core), got)
    got = swap(jnp.where(chip == 0, kept[:, bins:], kept[:, :bins]), CORES)
    kept = jnp.where(chip == 0, kept[:, :bins], kept[:, bins:])
    return jnp.where(chip == owner // CORES % PAIR, kept, got).reshape(2, ROWS // QUAD, COLS)


def along_line(quarter, owner):
    lines = lax.axis_size("tpl") // QUAD
    line, from_line = lax.axis_index("tpl") // QUAD, owner // QUAD
    if lines == 1:
        return quarter
    odd = line % 2 == 1
    quarter = jnp.where(line % 2 == from_line % 2, quarter, swap(quarter, QUAD))
    if lines == 2:
        return quarter
    rows = quarter.shape[1] // 2
    piece = jnp.where(odd, quarter[:, rows:], quarter[:, :rows])
    bit = 2
    while bit < lines:
        piece = jnp.where(line // bit % 2 == from_line // bit % 2, piece, swap(piece, bit * QUAD))
        bit *= 2
    other = swap(piece, QUAD)
    return jnp.concatenate([jnp.where(odd, other, piece), jnp.where(odd, piece, other)], 1)


def all_quarters(quarter):
    beside = swap(quarter, CORES)
    return quarter, beside, swap(quarter, 1), swap(beside, 1)


def collect(templates, lists, first):
    devices, groups = lax.axis_size("tpl"), lax.axis_size("grp")
    own_group = lax.axis_index("grp")
    per_device = lists.shape[1]
    rows = templates.shape[2] // COLS
    pieces = per_device * 2
    if pieces % groups:
        groups, own_group = 1, jnp.int32(0)
    size = pieces // groups
    direct = size == 2 and rows == WAVE_ROWS
    if direct:
        picked = templates[lax.dynamic_index_in_dim(lists, own_group, 1, keepdims=False)]
        picked, first = lax.optimization_barrier((picked.reshape(devices, size, rows, COLS), first))
    else:
        picked = templates[lists.reshape(-1)].reshape(devices, pieces, rows, COLS)
        picked = lax.dynamic_slice_in_dim(picked, own_group * size, size, 1)
    own = lax.all_to_all(picked, "tpl", split_axis=0, concat_axis=0, tiled=True)
    found = [own]
    for turn in range(1, groups):
        found.append(lax.ppermute(own, "grp", [(i, (i + turn) % groups) for i in range(groups)]))
    if direct:
        return found, [(own_group - turn) % groups for turn in range(groups)], first
    found = jnp.stack(found)[(own_group - jnp.arange(groups)) % groups]
    found = found.transpose(0, 2, 1, 3, 4).reshape(per_device, 2, ROWS // WAVE_ROWS, WAVE_ROWS, COLS)
    found = [found[at].transpose(1, 0, 2, 3) for at in range(per_device)]
    return found, [jnp.int32(at) for at in range(per_device)], first


def held(values):
    scaled = values * 65537.0
    return scaled - (scaled - values)


def quarters(parts):
    (re0, im0), (re1, im1), (re2, im2), (re3, im3) = parts
    even_re, even_im, odd_re, odd_im = re0 + re2, im0 + im2, re1 + re3, im1 + im3
    left_re, left_im, right_re, right_im = re0 - re2, im0 - im2, re1 - re3, im1 - im3
    return (
        (even_re + odd_re, even_im + odd_im),
        (left_re - right_im, left_im + right_re),
        (even_re - odd_re, even_im - odd_im),
        (left_re + right_im, left_im - right_re),
    )


def prepare_kernel(cut_ref, list_ref, where_ref, *refs):
    count = where_ref.shape[0] - 3
    wave_refs, (masked_ref, sigma_ref) = refs[:count], refs[count:]
    for tpl in range(count):
        cutoff = cut_ref[list_ref[where_ref[2], where_ref[3 + tpl]]]
        total = jnp.zeros((8, COLS), jnp.float32)
        for block in range(ROWS // WAVE_ROWS):
            bins = (lax.broadcasted_iota(jnp.int32, (WAVE_ROWS, COLS), 0) + block * WAVE_ROWS) * COLS
            bins = bins + lax.broadcasted_iota(jnp.int32, (WAVE_ROWS, COLS), 1)
            inside = bins < cutoff
            wave_re = jnp.where(inside, wave_refs[tpl][block, 0].astype(jnp.float32), 0.0)
            wave_im = jnp.where(inside, wave_refs[tpl][block, 1].astype(jnp.float32), 0.0)
            part = slice(block * WAVE_ROWS, (block + 1) * WAVE_ROWS)
            masked_ref[tpl, 0, part, :] = wave_re.astype(jnp.bfloat16)
            masked_ref[tpl, 1, part, :] = wave_im.astype(jnp.bfloat16)
            squares = wave_re * wave_re + wave_im * wave_im
            total = total + jnp.sum(squares.reshape(-1, 8, COLS), axis=0)
        sigma_ref[tpl] = jnp.sum(total)


def detector_kernel(det, where_ref, sigma_ref, *refs):
    first, last = det == 0, det == DET - 1
    quarter_refs, refs = refs[:QUAD], refs[QUAD:]
    masked, rphase_ref, cphase_ref, row_ref, col_ref, twiddle_ref = refs[:6]
    refs = refs[6:]
    before, refs = (None, refs) if first else (refs[0], refs[1:])
    outputs, (slid, stacked, twisted) = refs[:-3], refs[-3:]
    count = masked.shape[0]
    core, chip = where_ref[0], where_ref[1]
    half, rows = ROWS // CORES, ROWS // QUAD

    rc, rs = rphase_ref.at[det, 0], rphase_ref.at[det, 1]
    cc, cs = cphase_ref[det, 0], cphase_ref[det, 1]
    for which, quarter in enumerate(quarter_refs):
        of_core, of_chip = (core if which < 2 else 1 - core), (chip if which % 2 == 0 else 1 - chip)
        part = pl.ds(pl.multiple_of(of_core * half + of_chip * rows, rows), rows)
        turn_re = rc[part] * cc - rs[part] * cs
        turn_im = rc[part] * cs + rs[part] * cc
        data_re, data_im = quarter[0].astype(jnp.float32), quarter[1].astype(jnp.float32)
        slid[0, part, :] = data_re * turn_re - data_im * turn_im
        slid[1, part, :] = data_re * turn_im + data_im * turn_re

    largest = []
    for tpl in range(count):
        for at in range(0, PART, ROW_STEP):
            for col_at in range(0, COLS, PART):
                cols = slice(col_at, col_at + PART)
                parts = []
                for quarter in range(RADIX):
                    spot = slice(quarter * PART + at, quarter * PART + at + ROW_STEP)
                    wave_re = masked[tpl, 0, spot, cols].astype(jnp.float32)
                    wave_im = masked[tpl, 1, spot, cols].astype(jnp.float32)
                    data_re, data_im = slid[0, spot, cols], slid[1, spot, cols]
                    parts.append((held(data_re * wave_re + data_im * wave_im), held(data_im * wave_re - data_re * wave_im)))
                for residue, (re, im) in enumerate(quarters(parts)):
                    stacked[tpl, residue, at : at + ROW_STEP, cols] = re.astype(jnp.bfloat16)
                    stacked[tpl, residue, PART + at : PART + at + ROW_STEP, cols] = im.astype(jnp.bfloat16)
        for residue in range(RADIX):
            section = jnp.dot(row_ref[residue], stacked[tpl, residue], preferred_element_type=jnp.float32)
            for at in range(0, PART, ROW_STEP):
                parts = []
                for quarter in range(RADIX):
                    cols = slice(quarter * PART, (quarter + 1) * PART)
                    re, im = section[at : at + ROW_STEP, cols], section[PART + at : PART + at + ROW_STEP, cols]
                    turn_re = twiddle_ref[residue, 0, at : at + ROW_STEP, cols]
                    turn_im = twiddle_ref[residue, 1, at : at + ROW_STEP, cols]
                    parts.append((held(re * turn_re - im * turn_im), held(re * turn_im + im * turn_re)))
                spot = slice(residue * PART + at, residue * PART + at + ROW_STEP)
                for other, (re, im) in enumerate(quarters(parts)):
                    twisted[tpl, other, spot, :PART] = re.astype(jnp.bfloat16)
                    twisted[tpl, other, spot, PART:] = im.astype(jnp.bfloat16)
        peak = jnp.zeros((8, PART), jnp.float32)
        for other in range(RADIX):
            series = jnp.dot(twisted[tpl, other], col_ref[other], preferred_element_type=jnp.float32)
            squares = series[:, :PART] * series[:, :PART] + series[:, PART:] * series[:, PART:]
            cols = slice(other * PART, (other + 1) * PART)
            if not first:
                squares = squares + before[tpl, :, cols]
            if last:
                peak = jnp.maximum(peak, jnp.max(squares.reshape(-1, 8, PART), axis=0))
            else:
                outputs[0][tpl, :, cols] = squares
        largest.append(peak)

    if last:
        for tpl in range(count):
            place = where_ref[3 + tpl]
            outputs[0][place] = jnp.max(largest[tpl]) / (2.0 * (sigma_ref[tpl] + eps_norm))
            outputs[1][place] = sigma_ref[tpl] / (ROWS * COLS)


smem = pl.BlockSpec(memory_space=pltpu.SMEM)
vmem = pl.BlockSpec(memory_space=pltpu.VMEM)


def prepare(cutoffs, lists, where, waves):
    count = len(waves)
    return pl.pallas_call(
        prepare_kernel,
        out_shape=(
            jax.ShapeDtypeStruct((count, 2, ROWS, COLS), jnp.bfloat16),
            jax.ShapeDtypeStruct((count,), jnp.float32),
        ),
        in_specs=[smem, smem, smem] + [vmem] * count,
        out_specs=(vmem, smem),
        compiler_params=pltpu.CompilerParams(vmem_limit_bytes=VMEM_LIMIT),
        cost_estimate=pl.CostEstimate(flops=2_000_000_000, bytes_accessed=6_000_000, transcendentals=0),
    )(cutoffs, lists, where, *waves)


def detector(det, where, sigma, found, masked, turns, before):
    count = masked.shape[0]
    last = det == DET - 1
    scalars = jax.ShapeDtypeStruct((count,), jnp.float32)
    operands = [*found, masked, *turns, *tables(), *before]
    return pl.pallas_call(
        functools.partial(detector_kernel, det),
        out_shape=(scalars, scalars) if last else (jax.ShapeDtypeStruct((count, ROWS, COLS), jnp.float32),),
        in_specs=[smem, smem] + [vmem] * len(operands),
        out_specs=(smem, smem) if last else (vmem,),
        scratch_shapes=[
            pltpu.VMEM((2, ROWS, COLS), jnp.float32),
            pltpu.VMEM((count, RADIX, 2 * PART, COLS), jnp.bfloat16),
            pltpu.VMEM((count, RADIX, ROWS, 2 * PART), jnp.bfloat16),
        ],
        compiler_params=pltpu.CompilerParams(vmem_limit_bytes=VMEM_LIMIT),
        cost_estimate=pl.CostEstimate(flops=5_000_000_000, bytes_accessed=10_000_000, transcendentals=0),
    )(where, sigma, *operands)


def body(strain_slots, templates, cutoffs, lists, owner, slides):
    me, owner = lax.axis_index("tpl"), owner[0]
    quarter = [None] * DET
    turns = slide_turns(slides)
    for det in range(DET):
        quarter[det] = quarter_of(strain_slots, det, owner)
        if det == 0:
            waves, places, quarter[0] = collect(templates, lists, quarter[0])
        strain_slots, quarter[det] = lax.optimization_barrier((strain_slots, quarter[det]))
        if det == 1:
            turns, quarter[1] = lax.optimization_barrier((turns, quarter[1]))
    found = [all_quarters(along_line(part, owner)) for part in quarter]
    where = jnp.stack([jnp.asarray(at, jnp.int32) for at in (me % CORES, me // CORES % PAIR, me, *places)])
    masked, sigma = prepare(cutoffs, lists, where, waves)
    result = ()
    for det in range(DET):
        result = detector(det, where, sigma, found[det], masked, turns, result)
    return result


def solution(mesh):
    in_specs = (
        P(("grp", "tpl"), None, None, None),
        P(None, None, "tpl"),
        P(),
        P(),
        P("grp"),
        P("grp"),
    )
    out_specs = (P(("grp", "tpl")), P(("grp", "tpl")))
    return jax.shard_map(body, mesh=mesh, in_specs=in_specs, out_specs=out_specs, check_vma=False)
```

time: 138 us -> 132 us (0.957)
  waiting for transfers between devices: 58.3 us -> 47.1 us
  other arithmetic: 10.3 us -> 16.9 us
  local copies, waits for them, and re-layouts: 17.4 us -> 14.8 us
    ppermute x28 -> x24, waiting for transfers between devices: 58.3 us -> 43.2 us  [swap(): return lax.ppermute(block, 'tpl', partner(flip))]
    select_n x8 -> x21, other arithmetic: 8.36 us -> 12.3 us  [the longest x3 4.76 us: quarter_of(): kept = jnp.where(core == owner % CORES, side(core), got)]
    ppermute x1, waiting for transfers between devices: 0.01 us -> 3.85 us  [collect(): lax.ppermute(own, 'grp', [(i, (i + turn) % groups) for i in range(groups)])]
    slice x3 -> x0, local copies, waits for them, and re-layouts: 2.52 us -> none  [halves(): first[:, bins * at:bins * (at + 1)].reshape(2, bins // COLS, COLS)]
    concatenate x0 -> x3, other arithmetic: none -> 1.5 us  [along_line(): jnp.concatenate([jnp.where(odd, other, piece), jnp.where(odd, piece, othe...]
    ppermute x28 -> x24, starting transfers between devices: 23.5 us -> 24.4 us  [swap(): return lax.ppermute(block, 'tpl', partner(flip))]
    pallas_call x1 -> x4, Pallas kernels: 20.1 us -> 20.9 us  [the longest x3 18.1 us: detector(): pl.pallas_call(functools.partial(detector_kernel, det), out_shape=(scalar...]
  transfers between devices with their start and end apart: 30 -> 26, of which waited for: 11 -> 13; matrix products, arithmetic and copies ran while one was open for 16% -> 18% of each run, Pallas kernels for 0% -> 11%
where the time goes in v5:
time: 132 us; the launch traced here: 131 us
  waiting for transfers between devices  47.1 us (36%)
  starting transfers between devices  29.7 us (22%)
  Pallas kernels  20.9 us (16%)
  other arithmetic  16.9 us (13%)
  local copies, waits for them, and re-layouts  14.8 us (11%)
  between operations  1.98 us (2%)
    ppermute x24, waiting for transfers between devices, swap(): return lax.ppermute(block, 'tpl', partner(flip))  43.2 us
    ppermute x24, starting transfers between devices, swap(): return lax.ppermute(block, 'tpl', partner(flip))  24.4 us
    pallas_call x3, Pallas kernels, detector(): pl.pallas_call(functools.partial(detector_kernel, det), out_shape=(scalar...  18.1 us
    squeeze x3, local copies, waits for them, and re-layouts, quarter_of(): lax.dynamic_slice(strain_slots, (0, det, 0, which * half), (1, 1, 2, half))  5.16 us
    select_n x3, other arithmetic, quarter_of(): kept = jnp.where(core == owner % CORES, side(core), got)  4.76 us
    ppermute x1, waiting for transfers between devices, collect(): lax.ppermute(own, 'grp', [(i, (i + turn) % groups) for i in range(groups)])  3.85 us
    all_to_all x1, starting transfers between devices, collect(): own = lax.all_to_all(picked, 'tpl', split_axis=0, concat_axis=0, tiled=True)  3.83 us
    gather x1, local copies, waits for them, and re-layouts, collect(): templates[lax.dynamic_index_in_dim(lists, own_group, 1, keepdims=False)]  3.56 us
  transfers between devices with their start and end apart: 26, of which 13 were waited for; matrix products, arithmetic and copies ran while one was open for 18% of the time, Pallas kernels for 11%

profile of v5, /device:TPU:0, one launch (start us, length us, event | category | flops | bytes accessed | tf_op | source)
XLA Modules:
  0.0 131.3 jit_solution(18333092774301700389)
XLA Ops:
  0.7 1.5 %dynamic-slice_bitcast_fusion.2 = bf16[2,131072]{1,0:T(2,128)(2,1)S(1)} fusion(bf16[1,3,2,262144]{3,2,1,0:T(2,128)(2,1)} %param.15, s32[]{:T(128)S(6)} %select_n.315), kind=kLoop, calls=%fused_computation.6 | loop fusion | bytes 1048580 | tf_op jit(solution)/shard_map/squeeze | solution.py:72
  3.5 0.8 collective-permute-done
  4.3 1.6 %broadcast_select_fusion.2 = bf16[2,131072]{1,0:T(2,128)(2,1)S(1)} fusion(bf16[2,131072]{1,0:T(2,128)(2,1)S(1)} %collective-permute-done, pred[]{:T(512)S(6)} %eq.72, bf16[1,3,2,262144]{3,2,1,0:T(2,128)(2,1)} %param.15, s32[]{:T(128)S(6)} %select_n.314), kind=kLoop, calls=%fused_computation.3 | loop fusion | flops 262144 | bytes 1572869 | tf_op jit(solution)/shard_map/jit(_where)/select_n | solution.py:74
  6.2 3.0 %collective-permute-start.1 = (bf16[2,65536]{1,0:T(2,128)(2,1)S(1)}, bf16[2,65536]{1,0:T(2,128)(2,1)S(1)}, u32[]{:S(2)}, u32[]{:S(2)}) collective-permute-start(bf16[2,65536]{1,0:T(2,128)(2,1)S(1)} %broadcast_select_fusion.7), channel_id=1, source_target_pairs={{0,2},{1,3},{2,0},{3,1},{4,6},{5,7},{6,4},{7,5},{8,10},{9,11},{10,... | collective-permute-start | bytes 786440 | tf_op jit(solution)/shard_map/ppermute | solution.py:64
  9.2 3.6 %gather_fusion = bf16[16,2,16384]{2,1,0:T(2,128)(2,1)} fusion(bf16[32,2,16384]{2,1,0:T(2,128)(2,1)S(1)} %copy-done, s32[1024]{0:T(1024)S(1)} %pad_clamp_fusion), kind=kCustom, calls=%fused_computation | custom fusion | bytes 2097216 | tf_op jit(solution)/shard_map/gather | solution.py:115
  12.7 2.6 %reshape.198 = bf16[16,2,32,512]{3,2,1,0:T(8,128)(2,1)} reshape(bf16[16,2,16384]{2,1,0:T(2,128)(2,1)} %gather_fusion) | data formatting | bytes 2097152 | tf_op jit(solution)/shard_map/reshape | solution.py:116
  16.1 1.4 %dynamic-slice_bitcast_fusion.1 = bf16[2,131072]{1,0:T(2,128)(2,1)S(1)} fusion(bf16[1,3,2,262144]{3,2,1,0:T(2,128)(2,1)} %param.15, s32[]{:T(128)S(6)} %select_n.315), kind=kLoop, calls=%fused_computation.5 | loop fusion | bytes 1048580 | tf_op jit(solution)/shard_map/squeeze | solution.py:72
  17.6 0.9 fusion.7
  18.5 1.8 %collective-permute-start.19 = (bf16[2,128,512]{2,1,0:T(8,128)(2,1)S(1)}, bf16[2,128,512]{2,1,0:T(8,128)(2,1)}, u32[]{:S(2)}, u32[]{:S(2)}) collective-permute-start(bf16[2,128,512]{2,1,0:T(8,128)(2,1)S(1)} %bitcast.43), channel_id=1, source_target_pairs={{0,4},{1,5},{2,6},{3,7},{4,0},{5,1},{6,2},{7,3},{8,12},{9,13},{10,... | collective-permute-start | bytes 786440 | tf_op jit(solution)/shard_map/ppermute | solution.py:64
  20.3 1.6 %broadcast_select_fusion.1 = bf16[2,131072]{1,0:T(2,128)(2,1)S(1)} fusion(bf16[2,131072]{1,0:T(2,128)(2,1)S(1)} %collective-permute-done.3, pred[]{:T(512)S(6)} %eq.72, bf16[1,3,2,262144]{3,2,1,0:T(2,128)(2,1)} %param.15, s32[]{:T(128)S(6)} %select_n.314), kind=kLoop, calls=%fused_computation.2 | loop fusion | flops 262144 | bytes 1572869 | tf_op jit(solution)/shard_map/jit(_where)/select_n | solution.py:74
  21.9 1.0 broadcast_select_fusion.5
  22.9 1.5 %collective-permute-start.4 = (bf16[2,65536]{1,0:T(2,128)(2,1)}, bf16[2,65536]{1,0:T(2,128)(2,1)S(1)}, u32[]{:S(2)}, u32[]{:S(2)}) collective-permute-start(bf16[2,65536]{1,0:T(2,128)(2,1)} %broadcast_select_fusion.5), channel_id=1, source_target_pairs={{0,2},{1,3},{2,0},{3,1},{4,6},{5,7},{6,4},{7,5},{8,10},{9,11},{10,... | collective-permute-start | bytes 786440 | tf_op jit(solution)/shard_map/ppermute | solution.py:64
  24.4 0.9 fusion.9
  25.3 2.1 %collective-permute-done.19 = bf16[2,128,512]{2,1,0:T(8,128)(2,1)} collective-permute-done((bf16[2,128,512]{2,1,0:T(8,128)(2,1)S(1)}, bf16[2,128,512]{2,1,0:T(8,128)(2,1)}, u32[]{:S(2)}, u32[]{:S(2)}) %collective-permute-start.19) | collective-permute-done | bytes 262176 | tf_op jit(solution)/shard_map/ppermute | solution.py:64
  27.4 1.0 broadcast_select_fusion.12
  28.4 3.2 %collective-permute-done.4 = bf16[2,65536]{1,0:T(2,128)(2,1)S(1)} collective-permute-done((bf16[2,65536]{1,0:T(2,128)(2,1)}, bf16[2,65536]{1,0:T(2,128)(2,1)S(1)}, u32[]{:S(2)}, u32[]{:S(2)}) %collective-permute-start.4) | collective-permute-done | bytes 262176 | tf_op jit(solution)/shard_map/ppermute | solution.py:64
  31.9 0.7 copy.28
  32.6 2.2 %dynamic-slice_bitcast_fusion = bf16[2,131072]{1,0:T(2,128)(2,1)} fusion(bf16[1,3,2,262144]{3,2,1,0:T(2,128)(2,1)} %param.15, s32[]{:T(128)S(6)} %select_n.315), kind=kLoop, calls=%fused_computation.4 | loop fusion | bytes 1048580 | tf_op jit(solution)/shard_map/squeeze | solution.py:72
  34.8 2.7 %collective-permute-start.20 = (bf16[2,64,512]{2,1,0:T(8,128)(2,1)S(1)}, bf16[2,64,512]{2,1,0:T(8,128)(2,1)}, u32[]{:S(2)}, u32[]{:S(2)}) collective-permute-start(bf16[2,64,512]{2,1,0:T(8,128)(2,1)S(1)} %slice_select_fusion), channel_id=1, source_target_pairs={{0,8},{1,9},{2,10},{3,11},{4,12},{5,13},{6,14},{7,15},{8,0},{9,1},... | collective-permute-start | bytes 393224 | tf_op jit(solution)/shard_map/ppermute | solution.py:64
  37.6 1.3 maximum_bitcast_fusion
  38.9 3.8 %all-to-all-start = ((bf16[16,2,32,512]{3,2,1,0:T(8,128)(2,1)}), bf16[16,2,32,512]{3,2,1,0:T(8,128)(2,1)S(1)}, u32[]{:S(2)}, u32[]{:S(2)}) async-start(bf16[16,2,32,512]{3,2,1,0:T(8,128)(2,1)} %reshape.198), calls=%async_computation | async-start | bytes 2097152 | tf_op jit(solution)/shard_map/all_to_all | solution.py:120
  42.8 1.8 %collective-permute-done.20 = bf16[2,64,512]{2,1,0:T(8,128)(2,1)} collective-permute-done((bf16[2,64,512]{2,1,0:T(8,128)(2,1)S(1)}, bf16[2,64,512]{2,1,0:T(8,128)(2,1)}, u32[]{:S(2)}, u32[]{:S(2)}) %collective-permute-start.20) | collective-permute-done | bytes 131104 | tf_op jit(solution)/shard_map/ppermute | solution.py:64
  44.6 0.9 broadcast_select_fusion.15
  45.7 1.6 %broadcast_select_fusion = bf16[2,131072]{1,0:T(2,128)(2,1)S(1)} fusion(bf16[2,131072]{1,0:T(2,128)(2,1)} %collective-permute-done.5, pred[]{:T(512)S(6)} %eq.72, bf16[1,3,2,262144]{3,2,1,0:T(2,128)(2,1)} %param.15, s32[]{:T(128)S(6)} %select_n.314), kind=kLoop, calls=%fused_computation.1 | loop fusion | flops 262144 | bytes 1572869 | tf_op jit(solution)/shard_map/jit(_where)/select_n | solution.py:74
  47.5 1.6 %collective-permute-start.6 = (bf16[2,65536]{1,0:T(2,128)(2,1)S(1)}, bf16[2,65536]{1,0:T(2,128)(2,1)S(1)}, u32[]{:S(2)}, u32[]{:S(2)}) collective-permute-start(bf16[2,65536]{1,0:T(2,128)(2,1)S(1)} %broadcast_select_fusion.3), channel_id=1, source_target_pairs={{0,2},{1,3},{2,0},{3,1},{4,6},{5,7},{6,4},{7,5},{8,10},{9,11},{10,... | collective-permute-start | bytes 786440 | tf_op jit(solution)/shard_map/ppermute | solution.py:64
  49.1 14.2 %collective-permute-done.21 = bf16[2,64,512]{2,1,0:T(8,128)(2,1)S(1)} collective-permute-done((bf16[2,64,512]{2,1,0:T(8,128)(2,1)S(1)}, bf16[2,64,512]{2,1,0:T(8,128)(2,1)S(1)}, u32[]{:S(2)}, u32[]{:S(2)}) %collective-permute-start.21) | collective-permute-done | bytes 131104 | tf_op jit(solution)/shard_map/ppermute | solution.py:64
  63.3 1.7 %collective-permute-start.22 = (bf16[2,128,512]{2,1,0:T(8,128)(2,1)S(1)}, bf16[2,128,512]{2,1,0:T(8,128)(2,1)}, u32[]{:S(2)}, u32[]{:S(2)}) collective-permute-start(bf16[2,128,512]{2,1,0:T(8,128)(2,1)S(1)} %pad_maximum_fusion.2.refs_0_), channel_id=1, source_target_pairs={{0,2},{1,3},{2,0},{3,1},{4,6},{5,7},{6,4},{7,5},{8,10},{9,11},{10,... | collective-permute-start | bytes 786440 | tf_op jit(solution)/shard_map/ppermute | solution.py:64
  65.0 2.5 %collective-permute-start.13 = (bf16[2,128,512]{2,1,0:T(8,128)(2,1)S(1)}, bf16[2,128,512]{2,1,0:T(8,128)(2,1)S(1)}, u32[]{:S(2)}, u32[]{:S(2)}) collective-permute-start(bf16[2,128,512]{2,1,0:T(8,128)(2,1)S(1)} %bitcast.41), channel_id=1, source_target_pairs={{0,4},{1,5},{2,6},{3,7},{4,0},{5,1},{6,2},{7,3},{8,12},{9,13},{10,... | collective-permute-start | bytes 786440 | tf_op jit(solution)/shard_map/ppermute | solution.py:64
  68.0 6.7 %collective-permute-done.13 = bf16[2,128,512]{2,1,0:T(8,128)(2,1)S(1)} collective-permute-done((bf16[2,128,512]{2,1,0:T(8,128)(2,1)S(1)}, bf16[2,128,512]{2,1,0:T(8,128)(2,1)S(1)}, u32[]{:S(2)}, u32[]{:S(2)}) %collective-permute-start.13) | collective-permute-done | bytes 262176 | tf_op jit(solution)/shard_map/ppermute | solution.py:64
  74.8 3.9 %collective-permute-start.14 = (bf16[2,64,512]{2,1,0:T(8,128)(2,1)S(1)}, bf16[2,64,512]{2,1,0:T(8,128)(2,1)}, u32[]{:S(2)}, u32[]{:S(2)}) collective-permute-start(bf16[2,64,512]{2,1,0:T(8,128)(2,1)S(1)} %slice_select_fusion.1), channel_id=1, source_target_pairs={{0,8},{1,9},{2,10},{3,11},{4,12},{5,13},{6,14},{7,15},{8,0},{9,1},... | collective-permute-start | bytes 393224 | tf_op jit(solution)/shard_map/ppermute | solution.py:64
  78.7 4.2 %collective-permute-done.7 = bf16[2,128,512]{2,1,0:T(8,128)(2,1)S(1)} collective-permute-done((bf16[2,128,512]{2,1,0:T(8,128)(2,1)S(1)}, bf16[2,128,512]{2,1,0:T(8,128)(2,1)S(1)}, u32[]{:S(2)}, u32[]{:S(2)}) %collective-permute-start.7) | collective-permute-done | bytes 262176 | tf_op jit(solution)/shard_map/ppermute | solution.py:64
  83.7 1.3 collective-permute-start.8
  85.0 1.5 %collective-permute-start.2 = (bf16[16,2,32,512]{3,2,1,0:T(8,128)(2,1)S(1)}, bf16[16,2,32,512]{3,2,1,0:T(8,128)(2,1)}, u32[]{:S(2)}, u32[]{:S(2)}) collective-permute-start(bf16[16,2,32,512]{3,2,1,0:T(8,128)(2,1)S(1)} %all-to-all-done.refs_0_), channel_id=1, source_target_pairs={{0,16},{16,0},{1,17},{17,1},{2,18},{18,2},{3,19},{19,3},{4,20},{20... | collective-permute-start | bytes 3145736 | tf_op jit(solution)/shard_map/ppermute | solution.py:123
  86.5 1.1 broadcast_select_fusion.16
  87.5 2.2 %collective-permute-start.15 = (bf16[2,64,512]{2,1,0:T(8,128)(2,1)S(1)}, bf16[2,64,512]{2,1,0:T(8,128)(2,1)S(1)}, u32[]{:S(2)}, u32[]{:S(2)}) collective-permute-start(bf16[2,64,512]{2,1,0:T(8,128)(2,1)S(1)} %broadcast_select_fusion.16), channel_id=1, source_target_pairs={{0,4},{1,5},{2,6},{3,7},{4,0},{5,1},{6,2},{7,3},{8,12},{9,13},{10,... | collective-permute-start | bytes 393224 | tf_op jit(solution)/shard_map/ppermute | solution.py:64
  89.7 3.4 %collective-permute-done.8 = bf16[2,64,512]{2,1,0:T(8,128)(2,1)} collective-permute-done((bf16[2,64,512]{2,1,0:T(8,128)(2,1)}, bf16[2,64,512]{2,1,0:T(8,128)(2,1)}, u32[]{:S(2)}, u32[]{:S(2)}) %collective-permute-start.8) | collective-permute-done | bytes 131104 | tf_op jit(solution)/shard_map/ppermute | solution.py:64
  93.2 1.1 broadcast_select_fusion.17
  94.3 1.0 collective-permute-done.15
  96.4 2.9 %collective-permute-done.9 = bf16[2,64,512]{2,1,0:T(8,128)(2,1)S(1)} collective-permute-done((bf16[2,64,512]{2,1,0:T(8,128)(2,1)S(1)}, bf16[2,64,512]{2,1,0:T(8,128)(2,1)S(1)}, u32[]{:S(2)}, u32[]{:S(2)}) %collective-permute-start.9) | collective-permute-done | bytes 131104 | tf_op jit(solution)/shard_map/ppermute | solution.py:64
  99.4 0.8 pad_maximum_fusion.refs_0_
  100.5 0.8 copy.17.list_ref
  101.4 1.7 %copy.20.refs_5_ = f32[3,2,512,1]{3,2,1,0:T(8,128)} copy(f32[3,2,512,1]{2,1,0,3:T(2,128)S(1)} %copy-done.9) | data formatting | bytes 24576 | tf_op jit(solution)/shard_map/optimization_barrier | solution.py:289
  103.1 2.5 %collective-permute-done.16.refs_1_ = bf16[2,128,512]{2,1,0:T(8,128)(2,1)} collective-permute-done((bf16[2,128,512]{2,1,0:T(8,128)(2,1)}, bf16[2,128,512]{2,1,0:T(8,128)(2,1)}, u32[]{:S(2)}, u32[]{:S(2)}) %collective-permute-start.16) | collective-permute-done | bytes 262176 | tf_op jit(solution)/shard_map/ppermute | solution.py:64
  105.6 3.9 %collective-permute-done.2.refs_1_ = bf16[16,2,32,512]{3,2,1,0:T(8,128)(2,1)} collective-permute-done((bf16[16,2,32,512]{3,2,1,0:T(8,128)(2,1)S(1)}, bf16[16,2,32,512]{3,2,1,0:T(8,128)(2,1)}, u32[]{:S(2)}, u32[]{:S(2)}) %collective-permute-start.2) | collective-permute-done | bytes 1048608 | tf_op jit(solution)/shard_map/ppermute | solution.py:123
  109.4 2.8 %shard_map.158 = (bf16[2,2,512,512]{3,2,1,0:T(8,128)(2,1)S(1)}, f32[2]{0:T(128)S(1)}) custom-call(s32[32]{0:T(128)S(1)} %copy-done.2, s32[16,2]{1,0:T(8,128)S(1)} %copy.17.list_ref, s32[5]{0:T(128)S(1)} %stack.33.where_ref, bf16[16,2,32,512]{3,2,1,0:T(8,128)(2,1)S(1)} %all-to-all-done.refs_0_, bf16[16,2,32,512]{3,2,1,0:T(8,128)(2,1)} %collective-permute-done.2.refs_1_), custom_call_target="tpu_custom_call" | custom-call | flops 2000000000 | bytes 6000000 | tf_op jit(solution)/shard_map/pallas_call | solution.py:246
  112.9 5.7 %shard_map.159.refs_10_ = f32[2,512,512]{2,1,0:T(8,128)S(1)} custom-call(s32[5]{0:T(128)S(1)} %stack.33.where_ref, f32[2]{0:T(128)S(1)} %get-tuple-element.15.sigma_ref, bf16[2,128,512]{2,1,0:T(8,128)(2,1)S(1)} %pad_maximum_fusion.2.refs_0_, bf16[2,128,512]{2,1,0:T(8,128)(2,1)} %collective-permute-done.22.refs_1_, ...), custom_call_target="tpu_custom_call" | custom-call | flops 5000000000 | bytes 10000000 | tf_op jit(solution)/shard_map/pallas_call | solution.py:264
  118.7 6.0 %shard_map.160.refs_10_ = f32[2,512,512]{2,1,0:T(8,128)S(1)} custom-call(s32[5]{0:T(128)S(1)} %stack.33.where_ref, f32[2]{0:T(128)S(1)} %get-tuple-element.15.sigma_ref, bf16[2,128,512]{2,1,0:T(8,128)(2,1)} %pad_maximum_fusion.1.refs_0_, bf16[2,128,512]{2,1,0:T(8,128)(2,1)} %collective-permute-done.16.refs_1_, ...), custom_call_target="tpu_custom_call" | custom-call | flops 5000000000 | bytes 10000000 | tf_op jit(solution)/shard_map/pallas_call | solution.py:264
  124.7 6.4 %shard_map.161 = (f32[2]{0:T(128)}, f32[2]{0:T(128)}) custom-call(s32[5]{0:T(128)S(1)} %stack.33.where_ref, f32[2]{0:T(128)S(1)} %get-tuple-element.15.sigma_ref, bf16[2,128,512]{2,1,0:T(8,128)(2,1)} %pad_maximum_fusion.refs_0_, bf16[2,128,512]{2,1,0:T(8,128)(2,1)} %collective-permute-done.10.refs_1_, ...), custom_call_target="tpu_custom_call" | custom-call | flops 5000000000 | bytes 10000000 | tf_op jit(solution)/shard_map/pallas_call | solution.py:264
  (79 shorter events, 6.3 us)
Async XLA Ops:
  0.6 8.5 %copy-start = (bf16[32,2,16384]{2,1,0:T(2,128)(2,1)S(1)}, bf16[32,2,16384]{2,1,0:T(2,128)(2,1)}, u32[]{:S(2)}) copy-start(bf16[32,2,16384]{2,1,0:T(2,128)(2,1)} %param.16) | copy-start | bytes 6291460
  0.6 8.5 %copy-start.12 = (s32[16,2]{0,1:T(2,128)S(1)}, s32[16,2]{0,1:T(2,128)}, u32[]{:S(2)}) copy-start(s32[16,2]{0,1:T(2,128)} %param.18) | copy-start | bytes 388
  2.2 2.1 %collective-permute-start = (bf16[2,131072]{1,0:T(2,128)(2,1)S(1)}, bf16[2,131072]{1,0:T(2,128)(2,1)S(1)}, u32[]{:S(2)}, u32[]{:S(2)}) collective-permute-start(bf16[2,131072]{1,0:T(2,128)(2,1)S(1)} %dynamic-slice_bitcast_fusion.2), channel_id=1, source_target_pairs={{0,1},{1,0},{2,3},{3,2},{4,5},{5,4},{6,7},{7,6},{8,9},{9,8},{10,11... | collective-permute-start | bytes 1572872 | tf_op jit(solution)/shard_map/ppermute | solution.py:64
  6.2 9.6 %collective-permute-start.1 = (bf16[2,65536]{1,0:T(2,128)(2,1)S(1)}, bf16[2,65536]{1,0:T(2,128)(2,1)S(1)}, u32[]{:S(2)}, u32[]{:S(2)}) collective-permute-start(bf16[2,65536]{1,0:T(2,128)(2,1)S(1)} %broadcast_select_fusion.7), channel_id=1, source_target_pairs={{0,2},{1,3},{2,0},{3,1},{4,6},{5,7},{6,4},{7,5},{8,10},{9,11},{10,... | collective-permute-start | bytes 786440 | tf_op jit(solution)/shard_map/ppermute | solution.py:64
  9.1 8.5 %copy-start.13 = (s32[3]{0:T(128)S(1)}, s32[3]{0:T(128)}, u32[]{:S(2)}) copy-start(s32[3]{0:T(128)} %param.20) | copy-start | bytes 40
  17.5 2.8 %collective-permute-start.3 = (bf16[2,131072]{1,0:T(2,128)(2,1)S(1)}, bf16[2,131072]{1,0:T(2,128)(2,1)S(1)}, u32[]{:S(2)}, u32[]{:S(2)}) collective-permute-start(bf16[2,131072]{1,0:T(2,128)(2,1)S(1)} %dynamic-slice_bitcast_fusion.1), channel_id=1, source_target_pairs={{0,1},{1,0},{2,3},{3,2},{4,5},{5,4},{6,7},{7,6},{8,9},{9,8},{10,11... | collective-permute-start | bytes 1572872 | tf_op jit(solution)/shard_map/ppermute | solution.py:64
  18.5 8.9 %collective-permute-start.19 = (bf16[2,128,512]{2,1,0:T(8,128)(2,1)S(1)}, bf16[2,128,512]{2,1,0:T(8,128)(2,1)}, u32[]{:S(2)}, u32[]{:S(2)}) collective-permute-start(bf16[2,128,512]{2,1,0:T(8,128)(2,1)S(1)} %bitcast.43), channel_id=1, source_target_pairs={{0,4},{1,5},{2,6},{3,7},{4,0},{5,1},{6,2},{7,3},{8,12},{9,13},{10,... | collective-permute-start | bytes 786440 | tf_op jit(solution)/shard_map/ppermute | solution.py:64
  22.9 8.6 %collective-permute-start.4 = (bf16[2,65536]{1,0:T(2,128)(2,1)}, bf16[2,65536]{1,0:T(2,128)(2,1)S(1)}, u32[]{:S(2)}, u32[]{:S(2)}) collective-permute-start(bf16[2,65536]{1,0:T(2,128)(2,1)} %broadcast_select_fusion.5), channel_id=1, source_target_pairs={{0,2},{1,3},{2,0},{3,1},{4,6},{5,7},{6,4},{7,5},{8,10},{9,11},{10,... | collective-permute-start | bytes 786440 | tf_op jit(solution)/shard_map/ppermute | solution.py:64
  25.3 12.2 %copy-start.10 = (f32[3,1,512]{2,1,0:T(1,128)S(1)}, f32[3,1,512]{2,1,0:T(1,128)}, u32[]{:S(2)}) copy-start(f32[3,1,512]{2,1,0:T(1,128)} %get-tuple-element.32) | copy-start | bytes 18436
  25.3 12.2 %copy-start.11 = (f32[3,1,512]{2,1,0:T(1,128)S(1)}, f32[3,1,512]{2,1,0:T(1,128)}, u32[]{:S(2)}) copy-start(f32[3,1,512]{2,1,0:T(1,128)} %get-tuple-element.33) | copy-start | bytes 18436
  34.8 10.8 %collective-permute-start.5 = (bf16[2,131072]{1,0:T(2,128)(2,1)}, bf16[2,131072]{1,0:T(2,128)(2,1)}, u32[]{:S(2)}, u32[]{:S(2)}) collective-permute-start(bf16[2,131072]{1,0:T(2,128)(2,1)} %dynamic-slice_bitcast_fusion), channel_id=1, source_target_pairs={{0,1},{1,0},{2,3},{3,2},{4,5},{5,4},{6,7},{7,6},{8,9},{9,8},{10,11... | collective-permute-start | bytes 1572872 | tf_op jit(solution)/shard_map/ppermute | solution.py:64
  34.8 9.8 %collective-permute-start.20 = (bf16[2,64,512]{2,1,0:T(8,128)(2,1)S(1)}, bf16[2,64,512]{2,1,0:T(8,128)(2,1)}, u32[]{:S(2)}, u32[]{:S(2)}) collective-permute-start(bf16[2,64,512]{2,1,0:T(8,128)(2,1)S(1)} %slice_select_fusion), channel_id=1, source_target_pairs={{0,8},{1,9},{2,10},{3,11},{4,12},{5,13},{6,14},{7,15},{8,0},{9,1},... | collective-permute-start | bytes 393224 | tf_op jit(solution)/shard_map/ppermute | solution.py:64
  38.9 46.0 %all-to-all-start = ((bf16[16,2,32,512]{3,2,1,0:T(8,128)(2,1)}), bf16[16,2,32,512]{3,2,1,0:T(8,128)(2,1)S(1)}, u32[]{:S(2)}, u32[]{:S(2)}) async-start(bf16[16,2,32,512]{3,2,1,0:T(8,128)(2,1)} %reshape.198), calls=%async_computation | async-start | bytes 2097152 | tf_op jit(solution)/shard_map/all_to_all | solution.py:120
  42.8 22.3 %copy-start.8 = (bf16[1,2,128,512]{3,2,1,0:T(8,128)(2,1)S(1)}, bf16[1,2,128,512]{3,2,1,0:T(8,128)(2,1)}, u32[]{:S(2)}) copy-start(bf16[1,2,128,512]{3,2,1,0:T(8,128)(2,1)} %copy.28) | copy-start | bytes 786436
  45.6 17.7 %collective-permute-start.21 = (bf16[2,64,512]{2,1,0:T(8,128)(2,1)S(1)}, bf16[2,64,512]{2,1,0:T(8,128)(2,1)S(1)}, u32[]{:S(2)}, u32[]{:S(2)}) collective-permute-start(bf16[2,64,512]{2,1,0:T(8,128)(2,1)S(1)} %broadcast_select_fusion.15), channel_id=1, source_target_pairs={{0,4},{1,5},{2,6},{3,7},{4,0},{5,1},{6,2},{7,3},{8,12},{9,13},{10,... | collective-permute-start | bytes 393224 | tf_op jit(solution)/shard_map/ppermute | solution.py:64
  47.5 20.0 %collective-permute-start.6 = (bf16[2,65536]{1,0:T(2,128)(2,1)S(1)}, bf16[2,65536]{1,0:T(2,128)(2,1)S(1)}, u32[]{:S(2)}, u32[]{:S(2)}) collective-permute-start(bf16[2,65536]{1,0:T(2,128)(2,1)S(1)} %broadcast_select_fusion.3), channel_id=1, source_target_pairs={{0,2},{1,3},{2,0},{3,1},{4,6},{5,7},{6,4},{7,5},{8,10},{9,11},{10,... | collective-permute-start | bytes 786440 | tf_op jit(solution)/shard_map/ppermute | solution.py:64
  63.3 37.2 %collective-permute-start.22 = (bf16[2,128,512]{2,1,0:T(8,128)(2,1)S(1)}, bf16[2,128,512]{2,1,0:T(8,128)(2,1)}, u32[]{:S(2)}, u32[]{:S(2)}) collective-permute-start(bf16[2,128,512]{2,1,0:T(8,128)(2,1)S(1)} %pad_maximum_fusion.2.refs_0_), channel_id=1, source_target_pairs={{0,2},{1,3},{2,0},{3,1},{4,6},{5,7},{6,4},{7,5},{8,10},{9,11},{10,... | collective-permute-start | bytes 786440 | tf_op jit(solution)/shard_map/ppermute | solution.py:64
  65.0 47.2 %collective-permute-start.23 = (bf16[2,128,512]{2,1,0:T(8,128)(2,1)S(1)}, bf16[2,128,512]{2,1,0:T(8,128)(2,1)}, u32[]{:S(2)}, u32[]{:S(2)}) collective-permute-start(bf16[2,128,512]{2,1,0:T(8,128)(2,1)S(1)} %pad_maximum_fusion.2.refs_0_), channel_id=1, source_target_pairs={{0,1},{1,0},{2,3},{3,2},{4,5},{5,4},{6,7},{7,6},{8,9},{9,8},{10,11... | collective-permute-start | bytes 786440 | tf_op jit(solution)/shard_map/ppermute | solution.py:64
  65.0 9.6 %collective-permute-start.13 = (bf16[2,128,512]{2,1,0:T(8,128)(2,1)S(1)}, bf16[2,128,512]{2,1,0:T(8,128)(2,1)S(1)}, u32[]{:S(2)}, u32[]{:S(2)}) collective-permute-start(bf16[2,128,512]{2,1,0:T(8,128)(2,1)S(1)} %bitcast.41), channel_id=1, source_target_pairs={{0,4},{1,5},{2,6},{3,7},{4,0},{5,1},{6,2},{7,3},{8,12},{9,13},{10,... | collective-permute-start | bytes 786440 | tf_op jit(solution)/shard_map/ppermute | solution.py:64
  67.9 15.0 %collective-permute-start.7 = (bf16[2,128,512]{2,1,0:T(8,128)(2,1)S(1)}, bf16[2,128,512]{2,1,0:T(8,128)(2,1)S(1)}, u32[]{:S(2)}, u32[]{:S(2)}) collective-permute-start(bf16[2,128,512]{2,1,0:T(8,128)(2,1)S(1)} %bitcast.45), channel_id=1, source_target_pairs={{0,4},{1,5},{2,6},{3,7},{4,0},{5,1},{6,2},{7,3},{8,12},{9,13},{10,... | collective-permute-start | bytes 786440 | tf_op jit(solution)/shard_map/ppermute | solution.py:64
  74.7 4.0 %copy-start.7 = (bf16[2,128,512]{2,1,0:T(8,128)(2,1)}, bf16[2,128,512]{2,1,0:T(8,128)(2,1)S(1)}, u32[]{:S(2)}) copy-start(bf16[2,128,512]{2,1,0:T(8,128)(2,1)S(1)} %broadcast_select_fusion.13) | copy-start | bytes 786436
  74.7 34.7 %copy-start.2 = (s32[32]{0:T(128)S(1)}, s32[32]{0:T(128)}, u32[]{:S(2)}) copy-start(s32[32]{0:T(128)} %cut_ref.1) | copy-start | bytes 388
  74.8 11.7 %collective-permute-start.14 = (bf16[2,64,512]{2,1,0:T(8,128)(2,1)S(1)}, bf16[2,64,512]{2,1,0:T(8,128)(2,1)}, u32[]{:S(2)}, u32[]{:S(2)}) collective-permute-start(bf16[2,64,512]{2,1,0:T(8,128)(2,1)S(1)} %slice_select_fusion.1), channel_id=1, source_target_pairs={{0,8},{1,9},{2,10},{3,11},{4,12},{5,13},{6,14},{7,15},{8,0},{9,1},... | collective-permute-start | bytes 393224 | tf_op jit(solution)/shard_map/ppermute | solution.py:64
  83.0 0.8 copy-start.6
  83.7 9.5 %collective-permute-start.8 = (bf16[2,64,512]{2,1,0:T(8,128)(2,1)}, bf16[2,64,512]{2,1,0:T(8,128)(2,1)}, u32[]{:S(2)}, u32[]{:S(2)}) collective-permute-start(bf16[2,64,512]{2,1,0:T(8,128)(2,1)} %slice_select_fusion.2), channel_id=1, source_target_pairs={{0,8},{1,9},{2,10},{3,11},{4,12},{5,13},{6,14},{7,15},{8,0},{9,1},... | collective-permute-start | bytes 393224 | tf_op jit(solution)/shard_map/ppermute | solution.py:64
  85.0 24.5 %collective-permute-start.2 = (bf16[16,2,32,512]{3,2,1,0:T(8,128)(2,1)S(1)}, bf16[16,2,32,512]{3,2,1,0:T(8,128)(2,1)}, u32[]{:S(2)}, u32[]{:S(2)}) collective-permute-start(bf16[16,2,32,512]{3,2,1,0:T(8,128)(2,1)S(1)} %all-to-all-done.refs_0_), channel_id=1, source_target_pairs={{0,16},{16,0},{1,17},{17,1},{2,18},{18,2},{3,19},{19,3},{4,20},{20... | collective-permute-start | bytes 3145736 | tf_op jit(solution)/shard_map/ppermute | solution.py:123
  86.5 14.9 %copy-start.9 = (f32[3,2,512,1]{2,1,0,3:T(2,128)S(1)}, f32[3,2,512,1]{2,1,0,3:T(2,128)}, u32[]{:S(2)}) copy-start(f32[3,2,512,1]{2,1,0,3:T(2,128)} %maximum_bitcast_fusion) | copy-start | bytes 36868
  87.5 7.8 %collective-permute-start.15 = (bf16[2,64,512]{2,1,0:T(8,128)(2,1)S(1)}, bf16[2,64,512]{2,1,0:T(8,128)(2,1)S(1)}, u32[]{:S(2)}, u32[]{:S(2)}) collective-permute-start(bf16[2,64,512]{2,1,0:T(8,128)(2,1)S(1)} %broadcast_select_fusion.16), channel_id=1, source_target_pairs={{0,4},{1,5},{2,6},{3,7},{4,0},{5,1},{6,2},{7,3},{8,12},{9,13},{10,... | collective-permute-start | bytes 393224 | tf_op jit(solution)/shard_map/ppermute | solution.py:64
  94.2 5.1 %collective-permute-start.9 = (bf16[2,64,512]{2,1,0:T(8,128)(2,1)S(1)}, bf16[2,64,512]{2,1,0:T(8,128)(2,1)S(1)}, u32[]{:S(2)}, u32[]{:S(2)}) collective-permute-start(bf16[2,64,512]{2,1,0:T(8,128)(2,1)S(1)} %broadcast_select_fusion.17), channel_id=1, source_target_pairs={{0,4},{1,5},{2,6},{3,7},{4,0},{5,1},{6,2},{7,3},{8,12},{9,13},{10,... | collective-permute-start | bytes 393224 | tf_op jit(solution)/shard_map/ppermute | solution.py:64
  96.0 9.5 %collective-permute-start.16 = (bf16[2,128,512]{2,1,0:T(8,128)(2,1)}, bf16[2,128,512]{2,1,0:T(8,128)(2,1)}, u32[]{:S(2)}, u32[]{:S(2)}) collective-permute-start(bf16[2,128,512]{2,1,0:T(8,128)(2,1)} %pad_maximum_fusion.1.refs_0_), channel_id=1, source_target_pairs={{0,2},{1,3},{2,0},{3,1},{4,6},{5,7},{6,4},{7,5},{8,10},{9,11},{10,... | collective-permute-start | bytes 786440 | tf_op jit(solution)/shard_map/ppermute | solution.py:64
  100.1 12.7 %collective-permute-start.10 = (bf16[2,128,512]{2,1,0:T(8,128)(2,1)}, bf16[2,128,512]{2,1,0:T(8,128)(2,1)}, u32[]{:S(2)}, u32[]{:S(2)}) collective-permute-start(bf16[2,128,512]{2,1,0:T(8,128)(2,1)} %pad_maximum_fusion.refs_0_), channel_id=1, source_target_pairs={{0,2},{1,3},{2,0},{3,1},{4,6},{5,7},{6,4},{7,5},{8,10},{9,11},{10,... | collective-permute-start | bytes 786440 | tf_op jit(solution)/shard_map/ppermute | solution.py:64
  100.5 12.4 %collective-permute-start.24 = (bf16[2,128,512]{2,1,0:T(8,128)(2,1)}, bf16[2,128,512]{2,1,0:T(8,128)(2,1)}, u32[]{:S(2)}, u32[]{:S(2)}) collective-permute-start(bf16[2,128,512]{2,1,0:T(8,128)(2,1)} %collective-permute-done.22.refs_1_), channel_id=1, source_target_pairs={{0,1},{1,0},{2,3},{3,2},{4,5},{5,4},{6,7},{7,6},{8,9},{9,8},{10,11... | collective-permute-start | bytes 786440 | tf_op jit(solution)/shard_map/ppermute | solution.py:64
  103.1 9.8 %copy-start.1 = (f32[3,2,512,1]{3,2,1,0:T(8,128)S(1)}, f32[3,2,512,1]{3,2,1,0:T(8,128)}, u32[]{:S(2)}) copy-start(f32[3,2,512,1]{3,2,1,0:T(8,128)} %copy.20.refs_5_) | copy-start | bytes 36868
  103.1 9.8 %copy-start.3 = (f32[4,2,128,512]{3,2,1,0:T(8,128)S(1)}, f32[4,2,128,512]{3,2,1,0:T(8,128)}, u32[]{:S(2)}) copy-start(f32[4,2,128,512]{3,2,1,0:T(8,128)} %constant.226.clone.refs_9_) | copy-start | bytes 6291460
  103.1 9.9 %copy-start.4 = (bf16[4,256,256]{2,1,0:T(8,128)(2,1)S(1)}, bf16[4,256,256]{2,1,0:T(8,128)(2,1)}, u32[]{:S(2)}) copy-start(bf16[4,256,256]{2,1,0:T(8,128)(2,1)} %constant.230.refs_7_) | copy-start | bytes 1572868
  103.1 9.9 %copy-start.5 = (bf16[4,256,256]{2,1,0:T(8,128)(2,1)S(1)}, bf16[4,256,256]{2,1,0:T(8,128)(2,1)}, u32[]{:S(2)}) copy-start(bf16[4,256,256]{2,1,0:T(8,128)(2,1)} %constant.231.refs_8_) | copy-start | bytes 1572868
  105.6 13.1 %collective-permute-start.17 = (bf16[2,128,512]{2,1,0:T(8,128)(2,1)}, bf16[2,128,512]{2,1,0:T(8,128)(2,1)S(1)}, u32[]{:S(2)}, u32[]{:S(2)}) collective-permute-start(bf16[2,128,512]{2,1,0:T(8,128)(2,1)} %pad_maximum_fusion.1.refs_0_), channel_id=1, source_target_pairs={{0,1},{1,0},{2,3},{3,2},{4,5},{5,4},{6,7},{7,6},{8,9},{9,8},{10,11... | collective-permute-start | bytes 786440 | tf_op jit(solution)/shard_map/ppermute | solution.py:64
  109.4 9.2 %collective-permute-start.18 = (bf16[2,128,512]{2,1,0:T(8,128)(2,1)}, bf16[2,128,512]{2,1,0:T(8,128)(2,1)S(1)}, u32[]{:S(2)}, u32[]{:S(2)}) collective-permute-start(bf16[2,128,512]{2,1,0:T(8,128)(2,1)} %collective-permute-done.16.refs_1_), channel_id=1, source_target_pairs={{0,1},{1,0},{2,3},{3,2},{4,5},{5,4},{6,7},{7,6},{8,9},{9,8},{10,11... | collective-permute-start | bytes 786440 | tf_op jit(solution)/shard_map/ppermute | solution.py:64
  112.3 12.4 %collective-permute-start.11 = (bf16[2,128,512]{2,1,0:T(8,128)(2,1)}, bf16[2,128,512]{2,1,0:T(8,128)(2,1)S(1)}, u32[]{:S(2)}, u32[]{:S(2)}) collective-permute-start(bf16[2,128,512]{2,1,0:T(8,128)(2,1)} %pad_maximum_fusion.refs_0_), channel_id=1, source_target_pairs={{0,1},{1,0},{2,3},{3,2},{4,5},{5,4},{6,7},{7,6},{8,9},{9,8},{10,11... | collective-permute-start | bytes 786440 | tf_op jit(solution)/shard_map/ppermute | solution.py:64
  112.8 11.8 %collective-permute-start.12 = (bf16[2,128,512]{2,1,0:T(8,128)(2,1)}, bf16[2,128,512]{2,1,0:T(8,128)(2,1)S(1)}, u32[]{:S(2)}, u32[]{:S(2)}) collective-permute-start(bf16[2,128,512]{2,1,0:T(8,128)(2,1)} %collective-permute-done.10.refs_1_), channel_id=1, source_target_pairs={{0,1},{1,0},{2,3},{3,2},{4,5},{5,4},{6,7},{7,6},{8,9},{9,8},{10,11... | collective-permute-start | bytes 786440 | tf_op jit(solution)/shard_map/ppermute | solution.py:64

commit v6 on v5

--- a/solution.py
+++ b/solution.py
@@ -15,6 +15,7 @@
 PART = 128
 ROW_STEP = 16
 WAVE_ROWS = 32
+SEND_ROWS = 16
 CORES = 2
 PAIR = 2
 QUAD = CORES * PAIR
@@ -36,7 +37,7 @@
     for residue in range(RADIX):
         cos, sin = turn_table(RADIX * part_ids + residue, part_ids, ROWS)
         row_tables.append(np.block([[cos, -sin], [sin, cos]]))
-        col_tables.append(np.block([[cos.T, sin.T], [-sin.T, cos.T]]))
+        col_tables.append(np.block([[cos.T, sin.T], [-sin.T, cos.T]] * 2))
         turns.append(np.stack(turn_table(RADIX * part_ids + residue, col_ids, ROWS * COLS)))
     return (
         jnp.asarray(np.stack(row_tables), jnp.float32).astype(jnp.bfloat16),
@@ -51,8 +52,8 @@
     col_turns = (jnp.arange(COLS, dtype=jnp.int32)[None, :] * slides[:, None]) % total
     row_angles = row_turns.astype(jnp.float32) * (two_pi / total)
     col_angles = col_turns.astype(jnp.float32) * (two_pi / total)
-    rows = jnp.stack([jnp.cos(row_angles), jnp.sin(row_angles)], 1)[..., None]
-    cols = jnp.stack([jnp.cos(col_angles), jnp.sin(col_angles)], 1)[:, :, None, :]
+    rows = jnp.concatenate([jnp.cos(row_angles)[:, None], jnp.sin(row_angles)[:, None]] * 4, 1)
+    cols = jnp.concatenate([jnp.cos(col_angles)[:, None], jnp.sin(col_angles)[:, None]] * 4, 1)
     return rows, cols
 
 
@@ -101,7 +102,7 @@
     return quarter, beside, swap(quarter, 1), swap(beside, 1)
 
 
-def collect(templates, lists, first):
+def pick(templates, lists):
     devices, groups = lax.axis_size("tpl"), lax.axis_size("grp")
     own_group = lax.axis_index("grp")
     per_device = lists.shape[1]
@@ -110,23 +111,32 @@
     if pieces % groups:
         groups, own_group = 1, jnp.int32(0)
     size = pieces // groups
-    direct = size == 2 and rows == WAVE_ROWS
-    if direct:
+    if size == 2 and rows == WAVE_ROWS:
         picked = templates[lax.dynamic_index_in_dim(lists, own_group, 1, keepdims=False)]
-        picked, first = lax.optimization_barrier((picked.reshape(devices, size, rows, COLS), first))
-    else:
-        picked = templates[lists.reshape(-1)].reshape(devices, pieces, rows, COLS)
-        picked = lax.dynamic_slice_in_dim(picked, own_group * size, size, 1)
-    own = lax.all_to_all(picked, "tpl", split_axis=0, concat_axis=0, tiled=True)
-    found = [own]
-    for turn in range(1, groups):
-        found.append(lax.ppermute(own, "grp", [(i, (i + turn) % groups) for i in range(groups)]))
-    if direct:
-        return found, [(own_group - turn) % groups for turn in range(groups)], first
-    found = jnp.stack(found)[(own_group - jnp.arange(groups)) % groups]
+        picked = picked.reshape(devices, size, rows, COLS)
+        parts = [picked[:, :, at : at + SEND_ROWS] for at in range(0, rows, SEND_ROWS)]
+        return parts, [(own_group - turn) % groups for turn in range(groups)]
+    picked = templates[lists.reshape(-1)].reshape(devices, pieces, rows, COLS)
+    return [lax.dynamic_slice_in_dim(picked, own_group * size, size, 1)], None
+
+
+def exchange(block):
+    return lax.all_to_all(block, "tpl", split_axis=0, concat_axis=0, tiled=True)
+
+
+def across(own):
+    groups = lax.axis_size("grp")
+    return [own] + [
+        lax.ppermute(own, "grp", [(at, (at + turn) % groups) for at in range(groups)]) for turn in range(1, groups)
+    ]
+
+
+def assemble(own, per_device):
+    groups = lax.axis_size("grp")
+    found = jnp.stack(across(own) if per_device * 2 % groups == 0 else [own])
+    found = found[(lax.axis_index("grp") - jnp.arange(found.shape[0])) % found.shape[0]]
     found = found.transpose(0, 2, 1, 3, 4).reshape(per_device, 2, ROWS // WAVE_ROWS, WAVE_ROWS, COLS)
-    found = [found[at].transpose(1, 0, 2, 3) for at in range(per_device)]
-    return found, [jnp.int32(at) for at in range(per_device)], first
+    return [[found[at].transpose(1, 0, 2, 3)] for at in range(per_device)]
 
 
 def held(values):
@@ -146,23 +156,25 @@
     )
 
 
-def prepare_kernel(cut_ref, list_ref, where_ref, *refs):
-    count = where_ref.shape[0] - 3
-    wave_refs, (masked_ref, sigma_ref) = refs[:count], refs[count:]
+def prepare_kernel(count, cut_ref, list_ref, where_ref, *refs):
+    piece_refs, (masked_ref, sigma_ref) = refs[:-2], refs[-2:]
+    pieces = len(piece_refs) // count
+    rows = WAVE_ROWS // pieces
     for tpl in range(count):
-        cutoff = cut_ref[list_ref[where_ref[2], where_ref[3 + tpl]]]
+        cutoff = cut_ref[list_ref[where_ref[2] * count + where_ref[3 + tpl]]]
         total = jnp.zeros((8, COLS), jnp.float32)
-        for block in range(ROWS // WAVE_ROWS):
-            bins = (lax.broadcasted_iota(jnp.int32, (WAVE_ROWS, COLS), 0) + block * WAVE_ROWS) * COLS
-            bins = bins + lax.broadcasted_iota(jnp.int32, (WAVE_ROWS, COLS), 1)
-            inside = bins < cutoff
-            wave_re = jnp.where(inside, wave_refs[tpl][block, 0].astype(jnp.float32), 0.0)
-            wave_im = jnp.where(inside, wave_refs[tpl][block, 1].astype(jnp.float32), 0.0)
-            part = slice(block * WAVE_ROWS, (block + 1) * WAVE_ROWS)
-            masked_ref[tpl, 0, part, :] = wave_re.astype(jnp.bfloat16)
-            masked_ref[tpl, 1, part, :] = wave_im.astype(jnp.bfloat16)
-            squares = wave_re * wave_re + wave_im * wave_im
-            total = total + jnp.sum(squares.reshape(-1, 8, COLS), axis=0)
+        for piece in range(pieces):
+            wave_ref = piece_refs[tpl * pieces + piece]
+            for block in range(ROWS // WAVE_ROWS):
+                start = block * WAVE_ROWS + piece * rows
+                bins = (lax.broadcasted_iota(jnp.int32, (rows, COLS), 0) + start) * COLS
+                inside = bins + lax.broadcasted_iota(jnp.int32, (rows, COLS), 1) < cutoff
+                wave_re = jnp.where(inside, wave_ref[block, 0].astype(jnp.float32), 0.0)
+                wave_im = jnp.where(inside, wave_ref[block, 1].astype(jnp.float32), 0.0)
+                masked_ref[tpl, 0, start : start + rows, :] = wave_re.astype(jnp.bfloat16)
+                masked_ref[tpl, 1, start : start + rows, :] = wave_im.astype(jnp.bfloat16)
+                squares = wave_re * wave_re + wave_im * wave_im
+                total = total + jnp.sum(squares.reshape(-1, 8, COLS), axis=0)
         sigma_ref[tpl] = jnp.sum(total)
 
 
@@ -172,18 +184,19 @@
     masked, rphase_ref, cphase_ref, row_ref, col_ref, twiddle_ref = refs[:6]
     refs = refs[6:]
     before, refs = (None, refs) if first else (refs[0], refs[1:])
-    outputs, (slid, stacked, twisted) = refs[:-3], refs[-3:]
+    outputs, (turned_ref, slid, stacked, twisted) = refs[:-4], refs[-4:]
     count = masked.shape[0]
     core, chip = where_ref[0], where_ref[1]
     half, rows = ROWS // CORES, ROWS // QUAD
 
-    rc, rs = rphase_ref.at[det, 0], rphase_ref.at[det, 1]
-    cc, cs = cphase_ref[det, 0], cphase_ref[det, 1]
+    turned_ref[...] = rphase_ref[det].T
+    cc, cs = cphase_ref[det, 0:1, :], cphase_ref[det, 1:2, :]
     for which, quarter in enumerate(quarter_refs):
         of_core, of_chip = (core if which < 2 else 1 - core), (chip if which % 2 == 0 else 1 - chip)
         part = pl.ds(pl.multiple_of(of_core * half + of_chip * rows, rows), rows)
-        turn_re = rc[part] * cc - rs[part] * cs
-        turn_im = rc[part] * cs + rs[part] * cc
+        rc, rs = turned_ref[part, 0:1], turned_ref[part, 1:2]
+        turn_re = rc * cc - rs * cs
+        turn_im = rc * cs + rs * cc
         data_re, data_im = quarter[0].astype(jnp.float32), quarter[1].astype(jnp.float32)
         slid[0, part, :] = data_re * turn_re - data_im * turn_im
         slid[1, part, :] = data_re * turn_im + data_im * turn_re
@@ -214,9 +227,12 @@
                     turn_im = twiddle_ref[residue, 1, at : at + ROW_STEP, cols]
                     parts.append((held(re * turn_re - im * turn_im), held(re * turn_im + im * turn_re)))
                 spot = slice(residue * PART + at, residue * PART + at + ROW_STEP)
-                for other, (re, im) in enumerate(quarters(parts)):
-                    twisted[tpl, other, spot, :PART] = re.astype(jnp.bfloat16)
-                    twisted[tpl, other, spot, PART:] = im.astype(jnp.bfloat16)
+                for other, sums in enumerate(quarters(parts)):
+                    for which, value in enumerate(sums):
+                        high = value.astype(jnp.bfloat16)
+                        low = (value - high.astype(jnp.float32)).astype(jnp.bfloat16)
+                        twisted[tpl, other, spot, which * PART : (which + 1) * PART] = high
+                        twisted[tpl, other, spot, (which + 2) * PART : (which + 3) * PART] = low
         peak = jnp.zeros((8, PART), jnp.float32)
         for other in range(RADIX):
             series = jnp.dot(twisted[tpl, other], col_ref[other], preferred_element_type=jnp.float32)
@@ -243,17 +259,18 @@
 
 def prepare(cutoffs, lists, where, waves):
     count = len(waves)
+    operands = [piece for wave in waves for piece in wave]
     return pl.pallas_call(
-        prepare_kernel,
+        functools.partial(prepare_kernel, count),
         out_shape=(
             jax.ShapeDtypeStruct((count, 2, ROWS, COLS), jnp.bfloat16),
             jax.ShapeDtypeStruct((count,), jnp.float32),
         ),
-        in_specs=[smem, smem, smem] + [vmem] * count,
+        in_specs=[smem, smem, smem] + [vmem] * len(operands),
         out_specs=(vmem, smem),
         compiler_params=pltpu.CompilerParams(vmem_limit_bytes=VMEM_LIMIT),
         cost_estimate=pl.CostEstimate(flops=2_000_000_000, bytes_accessed=6_000_000, transcendentals=0),
-    )(cutoffs, lists, where, *waves)
+    )(cutoffs, lists, where, *operands)
 
 
 def detector(det, where, sigma, found, masked, turns, before):
@@ -267,9 +284,10 @@
         in_specs=[smem, smem] + [vmem] * len(operands),
         out_specs=(smem, smem) if last else (vmem,),
         scratch_shapes=[
+            pltpu.VMEM((ROWS, 8), jnp.float32),
             pltpu.VMEM((2, ROWS, COLS), jnp.float32),
             pltpu.VMEM((count, RADIX, 2 * PART, COLS), jnp.bfloat16),
-            pltpu.VMEM((count, RADIX, ROWS, 2 * PART), jnp.bfloat16),
+            pltpu.VMEM((count, RADIX, ROWS, 4 * PART), jnp.bfloat16),
         ],
         compiler_params=pltpu.CompilerParams(vmem_limit_bytes=VMEM_LIMIT),
         cost_estimate=pl.CostEstimate(flops=5_000_000_000, bytes_accessed=10_000_000, transcendentals=0),
@@ -278,18 +296,29 @@
 
 def body(strain_slots, templates, cutoffs, lists, owner, slides):
     me, owner = lax.axis_index("tpl"), owner[0]
-    quarter = [None] * DET
-    turns = slide_turns(slides)
-    for det in range(DET):
-        quarter[det] = quarter_of(strain_slots, det, owner)
-        if det == 0:
-            waves, places, quarter[0] = collect(templates, lists, quarter[0])
+    per_device = lists.shape[1]
+    parts, places = pick(templates, lists)
+    (strain_slots, parts) = lax.optimization_barrier((strain_slots, parts))
+    ids = list(range(per_device)) if places is None else places
+    where = jnp.stack([jnp.asarray(at, jnp.int32) for at in (me % CORES, me // CORES % PAIR, me, *ids)])
+    small = (*slide_turns(slides), where, lists.reshape(-1))
+
+    quarter = [quarter_of(strain_slots, 0, owner)]
+    arrived = [exchange(parts[0])]
+    strain_slots, quarter[0], small, arrived[0] = lax.optimization_barrier((strain_slots, quarter[0], small, arrived[0]))
+    arrived += [exchange(part) for part in parts[1:]]
+    for det in range(1, DET):
+        quarter.append(quarter_of(strain_slots, det, owner))
         strain_slots, quarter[det] = lax.optimization_barrier((strain_slots, quarter[det]))
-        if det == 1:
-            turns, quarter[1] = lax.optimization_barrier((turns, quarter[1]))
+    quarter[1:], arrived[1:] = lax.optimization_barrier((quarter[1:], arrived[1:]))
+    *turns, where, flat_list = small
+
     found = [all_quarters(along_line(part, owner)) for part in quarter]
-    where = jnp.stack([jnp.asarray(at, jnp.int32) for at in (me % CORES, me // CORES % PAIR, me, *places)])
-    masked, sigma = prepare(cutoffs, lists, where, waves)
+    if places is None:
+        waves = assemble(arrived[0], per_device)
+    else:
+        waves = [list(wave) for wave in zip(*[across(own) for own in arrived])]
+    masked, sigma = prepare(cutoffs, flat_list, where, waves)
     result = ()
     for det in range(DET):
         result = detector(det, where, sigma, found[det], masked, turns, result)

time: 132 us -> 150 us (1.14)
  waiting for transfers between devices: 47.1 us -> 58.9 us
  starting transfers between devices: 29.7 us -> 39.8 us
  other arithmetic: 16.9 us -> 10.8 us
    ppermute x24, waiting for transfers between devices: 43.2 us -> 58.8 us  [swap(): return lax.ppermute(block, 'tpl', partner(flip))]
    all_to_all x1 -> x2, starting transfers between devices: 3.83 us -> 12.5 us  [exchange(): return lax.all_to_all(block, 'tpl', split_axis=0, concat_axis=0, tiled=True)]
    ppermute x1 -> x2, waiting for transfers between devices: 3.85 us -> 0.01 us  [across(): lax.ppermute(own, 'grp', [(at, (at + turn) % groups) for at in range(grou...]
    select_n x3, other arithmetic: 3.06 us -> 0.06 us  [along_line(): jnp.where(line // bit % 2 == from_line // bit % 2, piece, swap(piece, bit...]
    slice x0 -> x1, local copies, waits for them, and re-layouts: none -> 2.3 us  [pick(): picked[:, :, at:at + SEND_ROWS]]
    pallas_call x3, Pallas kernels: 18.1 us -> 20 us  [detector(): pl.pallas_call(functools.partial(detector_kernel, det), out_shape=(scalar...]
    cos x2 -> x0, other arithmetic: 1.73 us -> none  [the longest x1 0.88 us: slide_turns(): jnp.cos(col_angles)]
    optimization_barrier x1 -> x0, local copies, waits for them, and re-layouts: 1.7 us -> none  [body(): turns, quarter[1] = lax.optimization_barrier((turns, quarter[1]))]
  transfers between devices with their start and end apart: 26 -> 28, of which waited for: 13 -> 13; matrix products, arithmetic and copies ran while one was open for 18% -> 8% of each run, Pallas kernels for 11% -> 10%
where the time goes in v6:
time: 150 us; the launch traced here: 149 us
  waiting for transfers between devices  58.9 us (39%)
  starting transfers between devices  39.8 us (27%)
  Pallas kernels  22.1 us (15%)
  local copies, waits for them, and re-layouts  14.9 us (10%)
  other arithmetic  10.8 us (7%)
  between operations  2.06 us (1%)
    ppermute x24, waiting for transfers between devices, swap(): return lax.ppermute(block, 'tpl', partner(flip))  58.8 us
    ppermute x24, starting transfers between devices, swap(): return lax.ppermute(block, 'tpl', partner(flip))  24.4 us
    pallas_call x3, Pallas kernels, detector(): pl.pallas_call(functools.partial(detector_kernel, det), out_shape=(scalar...  20 us
    all_to_all x2, starting transfers between devices, exchange(): return lax.all_to_all(block, 'tpl', split_axis=0, concat_axis=0, tiled=True)  12.5 us
    squeeze x3, local copies, waits for them, and re-layouts, quarter_of(): lax.dynamic_slice(strain_slots, (0, det, 0, which * half), (1, 1, 2, half))  4.99 us
    select_n x3, other arithmetic, quarter_of(): kept = jnp.where(core == owner % CORES, side(core), got)  4.78 us
    unnamed x18, local copies, waits for them, and re-layouts  3.05 us
  transfers between devices with their start and end apart: 28, of which 13 were waited for; matrix products, arithmetic and copies ran while one was open for 8% of the time, Pallas kernels for 10%

profile of v6, /device:TPU:0, one launch (start us, length us, event | category | flops | bytes accessed | tf_op | source)
XLA Modules:
  0.0 148.6 jit_solution(17023642411515571943)
XLA Ops:
  0.7 0.8 fusion.11
  1.5 0.7 copy-done
  2.2 2.7 %gather_fusion = bf16[16,2,16384]{2,1,0:T(2,128)(2,1)S(1)} fusion(bf16[32,2,16384]{2,1,0:T(2,128)(2,1)S(1)} %copy-done, s32[1024]{0:T(1024)S(1)} %pad_clamp_fusion), kind=kCustom, calls=%fused_computation | custom fusion | bytes 2097216 | tf_op jit(solution)/shard_map/gather | solution.py:115
  4.9 1.6 %reshape.201 = bf16[16,2,32,512]{3,2,1,0:T(8,128)(2,1)} reshape(bf16[16,2,16384]{2,1,0:T(2,128)(2,1)S(1)} %gather_fusion) | data formatting | bytes 2097152 | tf_op jit(solution)/shard_map/reshape | solution.py:116
  6.5 2.3 %fusion.12 = (bf16[16,2,16,512]{3,2,1,0:T(8,128)(2,1)}, bf16[16,2,16,512]{3,2,1,0:T(8,128)(2,1)}) fusion(bf16[16,2,32,512]{3,2,1,0:T(8,128)(2,1)} %reshape.201), kind=kLoop, calls=%fused_computation.61 | loop fusion | bytes 2097152 | tf_op jit(solution)/shard_map/slice | solution.py:117
  8.8 1.4 dynamic-slice_bitcast_fusion.2
  10.7 7.0 %all-to-all-start = ((bf16[16,2,16,512]{3,2,1,0:T(8,128)(2,1)}), bf16[16,2,16,512]{3,2,1,0:T(8,128)(2,1)S(1)}, u32[]{:S(2)}, u32[]{:S(2)}) async-start(bf16[16,2,16,512]{3,2,1,0:T(8,128)(2,1)} %get-tuple-element.21), calls=%async_computation | async-start | bytes 1048576 | tf_op jit(solution)/shard_map/all_to_all | solution.py:124
  18.5 1.6 %broadcast_select_fusion.2 = bf16[2,131072]{1,0:T(2,128)(2,1)S(1)} fusion(bf16[2,131072]{1,0:T(2,128)(2,1)} %collective-permute-done, pred[]{:T(512)S(6)} %eq.72, bf16[1,3,2,262144]{3,2,1,0:T(2,128)(2,1)} %param.15, s32[]{:T(128)S(6)} %select_n.312), kind=kLoop, calls=%fused_computation.3 | loop fusion | flops 262144 | bytes 1572869 | tf_op jit(solution)/shard_map/jit(_where)/select_n | solution.py:75
  20.4 2.0 %collective-permute-start.1 = (bf16[2,65536]{1,0:T(2,128)(2,1)S(1)}, bf16[2,65536]{1,0:T(2,128)(2,1)}, u32[]{:S(2)}, u32[]{:S(2)}) collective-permute-start(bf16[2,65536]{1,0:T(2,128)(2,1)S(1)} %broadcast_select_fusion.7), channel_id=1, source_target_pairs={{0,2},{1,3},{2,0},{3,1},{4,6},{5,7},{6,4},{7,5},{8,10},{9,11},{10,... | collective-permute-start | bytes 786440 | tf_op jit(solution)/shard_map/ppermute | solution.py:65
  23.5 8.5 %collective-permute-done.1 = bf16[2,65536]{1,0:T(2,128)(2,1)} collective-permute-done((bf16[2,65536]{1,0:T(2,128)(2,1)S(1)}, bf16[2,65536]{1,0:T(2,128)(2,1)}, u32[]{:S(2)}, u32[]{:S(2)}) %collective-permute-start.1) | collective-permute-done | bytes 262176 | tf_op jit(solution)/shard_map/ppermute | solution.py:65
  32.4 0.7 copy.27
  33.1 1.4 dynamic-slice_bitcast_fusion.1
  34.6 2.9 %collective-permute-start.20 = (bf16[2,128,512]{2,1,0:T(8,128)(2,1)}, bf16[2,128,512]{2,1,0:T(8,128)(2,1)}, u32[]{:S(2)}, u32[]{:S(2)}) collective-permute-start(bf16[2,128,512]{2,1,0:T(8,128)(2,1)} %bitcast.31), channel_id=1, source_target_pairs={{0,4},{1,5},{2,6},{3,7},{4,0},{5,1},{6,2},{7,3},{8,12},{9,13},{10,... | collective-permute-start | bytes 786440 | tf_op jit(solution)/shard_map/ppermute | solution.py:65
  37.5 1.6 %broadcast_select_fusion.1 = bf16[2,131072]{1,0:T(2,128)(2,1)S(1)} fusion(bf16[2,131072]{1,0:T(2,128)(2,1)S(1)} %collective-permute-done.2, pred[]{:T(512)S(6)} %eq.72, bf16[1,3,2,262144]{3,2,1,0:T(2,128)(2,1)} %param.15, s32[]{:T(128)S(6)} %select_n.312), kind=kLoop, calls=%fused_computation.2 | loop fusion | flops 262144 | bytes 1572869 | tf_op jit(solution)/shard_map/jit(_where)/select_n | solution.py:75
  39.1 1.0 broadcast_select_fusion.5
  40.1 2.1 %collective-permute-start.3 = (bf16[2,65536]{1,0:T(2,128)(2,1)}, bf16[2,65536]{1,0:T(2,128)(2,1)}, u32[]{:S(2)}, u32[]{:S(2)}) collective-permute-start(bf16[2,65536]{1,0:T(2,128)(2,1)} %broadcast_select_fusion.5), channel_id=1, source_target_pairs={{0,2},{1,3},{2,0},{3,1},{4,6},{5,7},{6,4},{7,5},{8,10},{9,11},{10,... | collective-permute-start | bytes 786440 | tf_op jit(solution)/shard_map/ppermute | solution.py:65
  42.2 2.5 %collective-permute-done.20 = bf16[2,128,512]{2,1,0:T(8,128)(2,1)} collective-permute-done((bf16[2,128,512]{2,1,0:T(8,128)(2,1)}, bf16[2,128,512]{2,1,0:T(8,128)(2,1)}, u32[]{:S(2)}, u32[]{:S(2)}) %collective-permute-start.20) | collective-permute-done | bytes 262176 | tf_op jit(solution)/shard_map/ppermute | solution.py:65
  44.7 1.0 broadcast_select_fusion.12
  45.7 3.4 %collective-permute-done.3 = bf16[2,65536]{1,0:T(2,128)(2,1)} collective-permute-done((bf16[2,65536]{1,0:T(2,128)(2,1)}, bf16[2,65536]{1,0:T(2,128)(2,1)}, u32[]{:S(2)}, u32[]{:S(2)}) %collective-permute-start.3) | collective-permute-done | bytes 262176 | tf_op jit(solution)/shard_map/ppermute | solution.py:65
  49.5 0.7 copy.26
  50.2 2.2 %dynamic-slice_bitcast_fusion = bf16[2,131072]{1,0:T(2,128)(2,1)} fusion(bf16[1,3,2,262144]{3,2,1,0:T(2,128)(2,1)} %param.15, s32[]{:T(128)S(6)} %select_n.313), kind=kLoop, calls=%fused_computation.4 | loop fusion | bytes 1048580 | tf_op jit(solution)/shard_map/squeeze | solution.py:73
  52.4 0.7 slice_select_fusion
  53.0 2.3 %collective-permute-start.21 = (bf16[2,64,512]{2,1,0:T(8,128)(2,1)}, bf16[2,64,512]{2,1,0:T(8,128)(2,1)}, u32[]{:S(2)}, u32[]{:S(2)}) collective-permute-start(bf16[2,64,512]{2,1,0:T(8,128)(2,1)} %slice_select_fusion), channel_id=1, source_target_pairs={{0,8},{1,9},{2,10},{3,11},{4,12},{5,13},{6,14},{7,15},{8,0},{9,1},... | collective-permute-start | bytes 393224 | tf_op jit(solution)/shard_map/ppermute | solution.py:65
  55.3 5.4 %all-to-all-start.1 = ((bf16[16,2,16,512]{3,2,1,0:T(8,128)(2,1)}), bf16[16,2,16,512]{3,2,1,0:T(8,128)(2,1)S(1)}, u32[]{:S(2)}, u32[]{:S(2)}) async-start(bf16[16,2,16,512]{3,2,1,0:T(8,128)(2,1)} %get-tuple-element.29), calls=%async_computation.1 | async-start | bytes 1048576 | tf_op jit(solution)/shard_map/all_to_all | solution.py:124
  60.8 2.1 %collective-permute-done.21 = bf16[2,64,512]{2,1,0:T(8,128)(2,1)} collective-permute-done((bf16[2,64,512]{2,1,0:T(8,128)(2,1)}, bf16[2,64,512]{2,1,0:T(8,128)(2,1)}, u32[]{:S(2)}, u32[]{:S(2)}) %collective-permute-start.21) | collective-permute-done | bytes 131104 | tf_op jit(solution)/shard_map/ppermute | solution.py:65
  63.1 1.6 %broadcast_select_fusion = bf16[2,131072]{1,0:T(2,128)(2,1)S(1)} fusion(bf16[2,131072]{1,0:T(2,128)(2,1)} %collective-permute-done.4, pred[]{:T(512)S(6)} %eq.72, bf16[1,3,2,262144]{3,2,1,0:T(2,128)(2,1)} %param.15, s32[]{:T(128)S(6)} %select_n.312), kind=kLoop, calls=%fused_computation.1 | loop fusion | flops 262144 | bytes 1572869 | tf_op jit(solution)/shard_map/jit(_where)/select_n | solution.py:75
  65.0 5.4 %collective-permute-start.5 = (bf16[2,65536]{1,0:T(2,128)(2,1)S(1)}, bf16[2,65536]{1,0:T(2,128)(2,1)S(1)}, u32[]{:S(2)}, u32[]{:S(2)}) collective-permute-start(bf16[2,65536]{1,0:T(2,128)(2,1)S(1)} %broadcast_select_fusion.3), channel_id=1, source_target_pairs={{0,2},{1,3},{2,0},{3,1},{4,6},{5,7},{6,4},{7,5},{8,10},{9,11},{10,... | collective-permute-start | bytes 786440 | tf_op jit(solution)/shard_map/ppermute | solution.py:65
  70.3 4.6 %collective-permute-done.22 = bf16[2,64,512]{2,1,0:T(8,128)(2,1)S(1)} collective-permute-done((bf16[2,64,512]{2,1,0:T(8,128)(2,1)S(1)}, bf16[2,64,512]{2,1,0:T(8,128)(2,1)S(1)}, u32[]{:S(2)}, u32[]{:S(2)}) %collective-permute-start.22) | collective-permute-done | bytes 131104 | tf_op jit(solution)/shard_map/ppermute | solution.py:65
  75.0 1.9 %collective-permute-start.23 = (bf16[2,128,512]{2,1,0:T(8,128)(2,1)S(1)}, bf16[2,128,512]{2,1,0:T(8,128)(2,1)}, u32[]{:S(2)}, u32[]{:S(2)}) collective-permute-start(bf16[2,128,512]{2,1,0:T(8,128)(2,1)S(1)} %pad_maximum_fusion.2.refs_0_), channel_id=1, source_target_pairs={{0,2},{1,3},{2,0},{3,1},{4,6},{5,7},{6,4},{7,5},{8,10},{9,11},{10,... | collective-permute-start | bytes 786440 | tf_op jit(solution)/shard_map/ppermute | solution.py:65
  77.3 0.7 copy.25
  78.0 1.4 collective-permute-start.14
  79.5 1.5 %collective-permute-start.6 = (bf16[16,2,16,512]{3,2,1,0:T(8,128)(2,1)S(1)}, bf16[16,2,16,512]{3,2,1,0:T(8,128)(2,1)S(1)}, u32[]{:S(2)}, u32[]{:S(2)}) collective-permute-start(bf16[16,2,16,512]{3,2,1,0:T(8,128)(2,1)S(1)} %all-to-all-done.refs_0_), channel_id=1, source_target_pairs={{0,16},{16,0},{1,17},{17,1},{2,18},{18,2},{3,19},{19,3},{4,20},{20... | collective-permute-start | bytes 1572872 | tf_op jit(solution)/shard_map/ppermute | solution.py:130
  80.9 2.5 %collective-permute-done.23.refs_1_ = bf16[2,128,512]{2,1,0:T(8,128)(2,1)} collective-permute-done((bf16[2,128,512]{2,1,0:T(8,128)(2,1)S(1)}, bf16[2,128,512]{2,1,0:T(8,128)(2,1)}, u32[]{:S(2)}, u32[]{:S(2)}) %collective-permute-start.23) | collective-permute-done | bytes 262176 | tf_op jit(solution)/shard_map/ppermute | solution.py:65
  83.4 1.5 %collective-permute-start.7 = (bf16[16,2,16,512]{3,2,1,0:T(8,128)(2,1)S(1)}, bf16[16,2,16,512]{3,2,1,0:T(8,128)(2,1)S(1)}, u32[]{:S(2)}, u32[]{:S(2)}) collective-permute-start(bf16[16,2,16,512]{3,2,1,0:T(8,128)(2,1)S(1)} %all-to-all-done.1.refs_1_), channel_id=1, source_target_pairs={{0,16},{16,0},{1,17},{17,1},{2,18},{18,2},{3,19},{19,3},{4,20},{20... | collective-permute-start | bytes 1572872 | tf_op jit(solution)/shard_map/ppermute | solution.py:130
  84.9 1.2 collective-permute-done.14
  86.5 7.1 %collective-permute-done.8 = bf16[2,128,512]{2,1,0:T(8,128)(2,1)S(1)} collective-permute-done((bf16[2,128,512]{2,1,0:T(8,128)(2,1)}, bf16[2,128,512]{2,1,0:T(8,128)(2,1)S(1)}, u32[]{:S(2)}, u32[]{:S(2)}) %collective-permute-start.8) | collective-permute-done | bytes 262176 | tf_op jit(solution)/shard_map/ppermute | solution.py:65
  93.6 2.5 %collective-permute-start.15 = (bf16[2,64,512]{2,1,0:T(8,128)(2,1)S(1)}, bf16[2,64,512]{2,1,0:T(8,128)(2,1)S(1)}, u32[]{:S(2)}, u32[]{:S(2)}) collective-permute-start(bf16[2,64,512]{2,1,0:T(8,128)(2,1)S(1)} %slice_select_fusion.1), channel_id=1, source_target_pairs={{0,8},{1,9},{2,10},{3,11},{4,12},{5,13},{6,14},{7,15},{8,0},{9,1},... | collective-permute-start | bytes 393224 | tf_op jit(solution)/shard_map/ppermute | solution.py:65
  96.1 6.3 %collective-permute-done.15 = bf16[2,64,512]{2,1,0:T(8,128)(2,1)S(1)} collective-permute-done((bf16[2,64,512]{2,1,0:T(8,128)(2,1)S(1)}, bf16[2,64,512]{2,1,0:T(8,128)(2,1)S(1)}, u32[]{:S(2)}, u32[]{:S(2)}) %collective-permute-start.15) | collective-permute-done | bytes 131104 | tf_op jit(solution)/shard_map/ppermute | solution.py:65
  102.4 5.9 %collective-permute-done.9 = bf16[2,64,512]{2,1,0:T(8,128)(2,1)S(1)} collective-permute-done((bf16[2,64,512]{2,1,0:T(8,128)(2,1)S(1)}, bf16[2,64,512]{2,1,0:T(8,128)(2,1)S(1)}, u32[]{:S(2)}, u32[]{:S(2)}) %collective-permute-start.9) | collective-permute-done | bytes 131104 | tf_op jit(solution)/shard_map/ppermute | solution.py:65
  108.4 6.2 %collective-permute-done.16 = bf16[2,64,512]{2,1,0:T(8,128)(2,1)S(1)} collective-permute-done((bf16[2,64,512]{2,1,0:T(8,128)(2,1)S(1)}, bf16[2,64,512]{2,1,0:T(8,128)(2,1)S(1)}, u32[]{:S(2)}, u32[]{:S(2)}) %collective-permute-start.16) | collective-permute-done | bytes 131104 | tf_op jit(solution)/shard_map/ppermute | solution.py:65
  114.7 4.9 %collective-permute-done.10 = bf16[2,64,512]{2,1,0:T(8,128)(2,1)S(1)} collective-permute-done((bf16[2,64,512]{2,1,0:T(8,128)(2,1)S(1)}, bf16[2,64,512]{2,1,0:T(8,128)(2,1)S(1)}, u32[]{:S(2)}, u32[]{:S(2)}) %collective-permute-start.10) | collective-permute-done | bytes 131104 | tf_op jit(solution)/shard_map/ppermute | solution.py:65
  119.6 1.3 collective-permute-start.17
  121.1 0.8 collective-permute-start.11
  121.9 2.1 %shard_map.158 = (bf16[2,2,512,512]{3,2,1,0:T(8,128)(2,1)S(1)}, f32[2]{0:T(128)S(1)}) custom-call(s32[32]{0:T(128)S(1)} %copy-done.1, s32[32]{0:T(128)S(1)} %reshape.203.list_ref, s32[5]{0:T(128)S(1)} %stack.23.where_ref, bf16[16,2,16,512]{3,2,1,0:T(8,128)(2,1)S(1)} %all-to-all-done.refs_0_, bf16[16,2,16,512]{3,2,1,0:T(8,128)(2,1)S(1)} %all-to-all-done.1.refs_1_, ...), custom_call_target="tpu_custom_call" | custom-call | flops 2000000000 | bytes 6000000 | tf_op jit(solution)/shard_map/pallas_call | solution.py:263
  124.2 3.5 %collective-permute-done.17.refs_1_ = bf16[2,128,512]{2,1,0:T(8,128)(2,1)S(1)} collective-permute-done((bf16[2,128,512]{2,1,0:T(8,128)(2,1)S(1)}, bf16[2,128,512]{2,1,0:T(8,128)(2,1)S(1)}, u32[]{:S(2)}, u32[]{:S(2)}) %collective-permute-start.17) | collective-permute-done | bytes 262176 | tf_op jit(solution)/shard_map/ppermute | solution.py:65
  127.8 6.6 %shard_map.159.refs_10_ = f32[2,512,512]{2,1,0:T(8,128)S(1)} custom-call(s32[5]{0:T(128)S(1)} %stack.23.where_ref, f32[2]{0:T(128)S(1)} %get-tuple-element.31.sigma_ref, bf16[2,128,512]{2,1,0:T(8,128)(2,1)S(1)} %pad_maximum_fusion.2.refs_0_, bf16[2,128,512]{2,1,0:T(8,128)(2,1)} %collective-permute-done.23.refs_1_, ...), custom_call_target="tpu_custom_call" | custom-call | flops 5000000000 | bytes 10000000 | tf_op jit(solution)/shard_map/pallas_call | solution.py:281
  135.0 6.5 %shard_map.160.refs_10_ = f32[2,512,512]{2,1,0:T(8,128)S(1)} custom-call(s32[5]{0:T(128)S(1)} %stack.23.where_ref, f32[2]{0:T(128)S(1)} %get-tuple-element.31.sigma_ref, bf16[2,128,512]{2,1,0:T(8,128)(2,1)S(1)} %pad_maximum_fusion.1.refs_0_, bf16[2,128,512]{2,1,0:T(8,128)(2,1)S(1)} %collective-permute-done.17.refs_1_, ...), custom_call_target="tpu_custom_call" | custom-call | flops 5000000000 | bytes 10000000 | tf_op jit(solution)/shard_map/pallas_call | solution.py:281
  141.5 6.9 %shard_map.161 = (f32[2]{0:T(128)}, f32[2]{0:T(128)}) custom-call(s32[5]{0:T(128)S(1)} %stack.23.where_ref, f32[2]{0:T(128)S(1)} %get-tuple-element.31.sigma_ref, bf16[2,128,512]{2,1,0:T(8,128)(2,1)S(1)} %pad_maximum_fusion.refs_0_, bf16[2,128,512]{2,1,0:T(8,128)(2,1)S(1)} %collective-permute-done.11.refs_1_, ...), custom_call_target="tpu_custom_call" | custom-call | flops 5000000000 | bytes 10000000 | tf_op jit(solution)/shard_map/pallas_call | solution.py:281
  (69 shorter events, 4.9 us)
Async XLA Ops:
  0.6 1.6 %copy-start = (bf16[32,2,16384]{2,1,0:T(2,128)(2,1)S(1)}, bf16[32,2,16384]{2,1,0:T(2,128)(2,1)}, u32[]{:S(2)}) copy-start(bf16[32,2,16384]{2,1,0:T(2,128)(2,1)} %param.16) | copy-start | bytes 6291460
  4.9 13.6 %copy-start.6 = (s32[3]{0:T(128)S(1)}, s32[3]{0:T(128)}, u32[]{:S(2)}) copy-start(s32[3]{0:T(128)} %param.20) | copy-start | bytes 40
  6.5 16.2 %copy-start.5 = (s32[16,2]{0,1:T(2,128)S(1)}, s32[16,2]{0,1:T(2,128)}, u32[]{:S(2)}) copy-start(s32[16,2]{0,1:T(2,128)} %param.18) | copy-start | bytes 388
  10.2 8.3 %collective-permute-start = (bf16[2,131072]{1,0:T(2,128)(2,1)S(1)}, bf16[2,131072]{1,0:T(2,128)(2,1)}, u32[]{:S(2)}, u32[]{:S(2)}) collective-permute-start(bf16[2,131072]{1,0:T(2,128)(2,1)S(1)} %dynamic-slice_bitcast_fusion.2), channel_id=1, source_target_pairs={{0,1},{1,0},{2,3},{3,2},{4,5},{5,4},{6,7},{7,6},{8,9},{9,8},{10,11... | collective-permute-start | bytes 1572872 | tf_op jit(solution)/shard_map/ppermute | solution.py:65
  10.7 22.4 %all-to-all-start = ((bf16[16,2,16,512]{3,2,1,0:T(8,128)(2,1)}), bf16[16,2,16,512]{3,2,1,0:T(8,128)(2,1)S(1)}, u32[]{:S(2)}, u32[]{:S(2)}) async-start(bf16[16,2,16,512]{3,2,1,0:T(8,128)(2,1)} %get-tuple-element.21), calls=%async_computation | async-start | bytes 1048576 | tf_op jit(solution)/shard_map/all_to_all | solution.py:124
  20.4 11.6 %collective-permute-start.1 = (bf16[2,65536]{1,0:T(2,128)(2,1)S(1)}, bf16[2,65536]{1,0:T(2,128)(2,1)}, u32[]{:S(2)}, u32[]{:S(2)}) collective-permute-start(bf16[2,65536]{1,0:T(2,128)(2,1)S(1)} %broadcast_select_fusion.7), channel_id=1, source_target_pairs={{0,2},{1,3},{2,0},{3,1},{4,6},{5,7},{6,4},{7,5},{8,10},{9,11},{10,... | collective-permute-start | bytes 786440 | tf_op jit(solution)/shard_map/ppermute | solution.py:65
  34.5 3.0 %collective-permute-start.2 = (bf16[2,131072]{1,0:T(2,128)(2,1)S(1)}, bf16[2,131072]{1,0:T(2,128)(2,1)S(1)}, u32[]{:S(2)}, u32[]{:S(2)}) collective-permute-start(bf16[2,131072]{1,0:T(2,128)(2,1)S(1)} %dynamic-slice_bitcast_fusion.1), channel_id=1, source_target_pairs={{0,1},{1,0},{2,3},{3,2},{4,5},{5,4},{6,7},{7,6},{8,9},{9,8},{10,11... | collective-permute-start | bytes 1572872 | tf_op jit(solution)/shard_map/ppermute | solution.py:65
  34.6 10.1 %collective-permute-start.20 = (bf16[2,128,512]{2,1,0:T(8,128)(2,1)}, bf16[2,128,512]{2,1,0:T(8,128)(2,1)}, u32[]{:S(2)}, u32[]{:S(2)}) collective-permute-start(bf16[2,128,512]{2,1,0:T(8,128)(2,1)} %bitcast.31), channel_id=1, source_target_pairs={{0,4},{1,5},{2,6},{3,7},{4,0},{5,1},{6,2},{7,3},{8,12},{9,13},{10,... | collective-permute-start | bytes 786440 | tf_op jit(solution)/shard_map/ppermute | solution.py:65
  40.1 9.0 %collective-permute-start.3 = (bf16[2,65536]{1,0:T(2,128)(2,1)}, bf16[2,65536]{1,0:T(2,128)(2,1)}, u32[]{:S(2)}, u32[]{:S(2)}) collective-permute-start(bf16[2,65536]{1,0:T(2,128)(2,1)} %broadcast_select_fusion.5), channel_id=1, source_target_pairs={{0,2},{1,3},{2,0},{3,1},{4,6},{5,7},{6,4},{7,5},{8,10},{9,11},{10,... | collective-permute-start | bytes 786440 | tf_op jit(solution)/shard_map/ppermute | solution.py:65
  52.4 10.7 %collective-permute-start.4 = (bf16[2,131072]{1,0:T(2,128)(2,1)}, bf16[2,131072]{1,0:T(2,128)(2,1)}, u32[]{:S(2)}, u32[]{:S(2)}) collective-permute-start(bf16[2,131072]{1,0:T(2,128)(2,1)} %dynamic-slice_bitcast_fusion), channel_id=1, source_target_pairs={{0,1},{1,0},{2,3},{3,2},{4,5},{5,4},{6,7},{7,6},{8,9},{9,8},{10,11... | collective-permute-start | bytes 1572872 | tf_op jit(solution)/shard_map/ppermute | solution.py:65
  53.0 9.9 %collective-permute-start.21 = (bf16[2,64,512]{2,1,0:T(8,128)(2,1)}, bf16[2,64,512]{2,1,0:T(8,128)(2,1)}, u32[]{:S(2)}, u32[]{:S(2)}) collective-permute-start(bf16[2,64,512]{2,1,0:T(8,128)(2,1)} %slice_select_fusion), channel_id=1, source_target_pairs={{0,8},{1,9},{2,10},{3,11},{4,12},{5,13},{6,14},{7,15},{8,0},{9,1},... | collective-permute-start | bytes 393224 | tf_op jit(solution)/shard_map/ppermute | solution.py:65
  55.3 22.7 %all-to-all-start.1 = ((bf16[16,2,16,512]{3,2,1,0:T(8,128)(2,1)}), bf16[16,2,16,512]{3,2,1,0:T(8,128)(2,1)S(1)}, u32[]{:S(2)}, u32[]{:S(2)}) async-start(bf16[16,2,16,512]{3,2,1,0:T(8,128)(2,1)} %get-tuple-element.29), calls=%async_computation.1 | async-start | bytes 1048576 | tf_op jit(solution)/shard_map/all_to_all | solution.py:124
  63.0 12.0 %collective-permute-start.22 = (bf16[2,64,512]{2,1,0:T(8,128)(2,1)S(1)}, bf16[2,64,512]{2,1,0:T(8,128)(2,1)S(1)}, u32[]{:S(2)}, u32[]{:S(2)}) collective-permute-start(bf16[2,64,512]{2,1,0:T(8,128)(2,1)S(1)} %broadcast_select_fusion.15), channel_id=1, source_target_pairs={{0,4},{1,5},{2,6},{3,7},{4,0},{5,1},{6,2},{7,3},{8,12},{9,13},{10,... | collective-permute-start | bytes 393224 | tf_op jit(solution)/shard_map/ppermute | solution.py:65
  65.0 11.9 %collective-permute-start.5 = (bf16[2,65536]{1,0:T(2,128)(2,1)S(1)}, bf16[2,65536]{1,0:T(2,128)(2,1)S(1)}, u32[]{:S(2)}, u32[]{:S(2)}) collective-permute-start(bf16[2,65536]{1,0:T(2,128)(2,1)S(1)} %broadcast_select_fusion.3), channel_id=1, source_target_pairs={{0,2},{1,3},{2,0},{3,1},{4,6},{5,7},{6,4},{7,5},{8,10},{9,11},{10,... | collective-permute-start | bytes 786440 | tf_op jit(solution)/shard_map/ppermute | solution.py:65
  75.0 8.4 %collective-permute-start.23 = (bf16[2,128,512]{2,1,0:T(8,128)(2,1)S(1)}, bf16[2,128,512]{2,1,0:T(8,128)(2,1)}, u32[]{:S(2)}, u32[]{:S(2)}) collective-permute-start(bf16[2,128,512]{2,1,0:T(8,128)(2,1)S(1)} %pad_maximum_fusion.2.refs_0_), channel_id=1, source_target_pairs={{0,2},{1,3},{2,0},{3,1},{4,6},{5,7},{6,4},{7,5},{8,10},{9,11},{10,... | collective-permute-start | bytes 786440 | tf_op jit(solution)/shard_map/ppermute | solution.py:65
  77.3 44.6 %copy-start.1 = (s32[32]{0:T(128)S(1)}, s32[32]{0:T(128)}, u32[]{:S(2)}) copy-start(s32[32]{0:T(128)} %cut_ref.1) | copy-start | bytes 388
  78.0 8.1 %collective-permute-start.14 = (bf16[2,128,512]{2,1,0:T(8,128)(2,1)}, bf16[2,128,512]{2,1,0:T(8,128)(2,1)S(1)}, u32[]{:S(2)}, u32[]{:S(2)}) collective-permute-start(bf16[2,128,512]{2,1,0:T(8,128)(2,1)} %bitcast.39), channel_id=1, source_target_pairs={{0,4},{1,5},{2,6},{3,7},{4,0},{5,1},{6,2},{7,3},{8,12},{9,13},{10,... | collective-permute-start | bytes 786440 | tf_op jit(solution)/shard_map/ppermute | solution.py:65
  79.5 41.5 %collective-permute-start.6 = (bf16[16,2,16,512]{3,2,1,0:T(8,128)(2,1)S(1)}, bf16[16,2,16,512]{3,2,1,0:T(8,128)(2,1)S(1)}, u32[]{:S(2)}, u32[]{:S(2)}) collective-permute-start(bf16[16,2,16,512]{3,2,1,0:T(8,128)(2,1)S(1)} %all-to-all-done.refs_0_), channel_id=1, source_target_pairs={{0,16},{16,0},{1,17},{17,1},{2,18},{18,2},{3,19},{19,3},{4,20},{20... | collective-permute-start | bytes 1572872 | tf_op jit(solution)/shard_map/ppermute | solution.py:130
  80.9 43.1 %collective-permute-start.24 = (bf16[2,128,512]{2,1,0:T(8,128)(2,1)S(1)}, bf16[2,128,512]{2,1,0:T(8,128)(2,1)S(1)}, u32[]{:S(2)}, u32[]{:S(2)}) collective-permute-start(bf16[2,128,512]{2,1,0:T(8,128)(2,1)S(1)} %pad_maximum_fusion.2.refs_0_), channel_id=1, source_target_pairs={{0,1},{1,0},{2,3},{3,2},{4,5},{5,4},{6,7},{7,6},{8,9},{9,8},{10,11... | collective-permute-start | bytes 786440 | tf_op jit(solution)/shard_map/ppermute | solution.py:65
  83.4 44.3 %collective-permute-start.25 = (bf16[2,128,512]{2,1,0:T(8,128)(2,1)}, bf16[2,128,512]{2,1,0:T(8,128)(2,1)S(1)}, u32[]{:S(2)}, u32[]{:S(2)}) collective-permute-start(bf16[2,128,512]{2,1,0:T(8,128)(2,1)} %collective-permute-done.23.refs_1_), channel_id=1, source_target_pairs={{0,1},{1,0},{2,3},{3,2},{4,5},{5,4},{6,7},{7,6},{8,9},{9,8},{10,11... | collective-permute-start | bytes 786440 | tf_op jit(solution)/shard_map/ppermute | solution.py:65
  83.4 37.6 %collective-permute-start.7 = (bf16[16,2,16,512]{3,2,1,0:T(8,128)(2,1)S(1)}, bf16[16,2,16,512]{3,2,1,0:T(8,128)(2,1)S(1)}, u32[]{:S(2)}, u32[]{:S(2)}) collective-permute-start(bf16[16,2,16,512]{3,2,1,0:T(8,128)(2,1)S(1)} %all-to-all-done.1.refs_1_), channel_id=1, source_target_pairs={{0,16},{16,0},{1,17},{17,1},{2,18},{18,2},{3,19},{19,3},{4,20},{20... | collective-permute-start | bytes 1572872 | tf_op jit(solution)/shard_map/ppermute | solution.py:130
  86.1 7.5 %collective-permute-start.8 = (bf16[2,128,512]{2,1,0:T(8,128)(2,1)}, bf16[2,128,512]{2,1,0:T(8,128)(2,1)S(1)}, u32[]{:S(2)}, u32[]{:S(2)}) collective-permute-start(bf16[2,128,512]{2,1,0:T(8,128)(2,1)} %bitcast.41), channel_id=1, source_target_pairs={{0,4},{1,5},{2,6},{3,7},{4,0},{5,1},{6,2},{7,3},{8,12},{9,13},{10,... | collective-permute-start | bytes 786440 | tf_op jit(solution)/shard_map/ppermute | solution.py:65
  93.6 8.9 %collective-permute-start.15 = (bf16[2,64,512]{2,1,0:T(8,128)(2,1)S(1)}, bf16[2,64,512]{2,1,0:T(8,128)(2,1)S(1)}, u32[]{:S(2)}, u32[]{:S(2)}) collective-permute-start(bf16[2,64,512]{2,1,0:T(8,128)(2,1)S(1)} %slice_select_fusion.1), channel_id=1, source_target_pairs={{0,8},{1,9},{2,10},{3,11},{4,12},{5,13},{6,14},{7,15},{8,0},{9,1},... | collective-permute-start | bytes 393224 | tf_op jit(solution)/shard_map/ppermute | solution.py:65
  102.4 6.0 %collective-permute-start.9 = (bf16[2,64,512]{2,1,0:T(8,128)(2,1)S(1)}, bf16[2,64,512]{2,1,0:T(8,128)(2,1)S(1)}, u32[]{:S(2)}, u32[]{:S(2)}) collective-permute-start(bf16[2,64,512]{2,1,0:T(8,128)(2,1)S(1)} %slice_select_fusion.2), channel_id=1, source_target_pairs={{0,8},{1,9},{2,10},{3,11},{4,12},{5,13},{6,14},{7,15},{8,0},{9,1},... | collective-permute-start | bytes 393224 | tf_op jit(solution)/shard_map/ppermute | solution.py:65
  108.4 6.2 %collective-permute-start.16 = (bf16[2,64,512]{2,1,0:T(8,128)(2,1)S(1)}, bf16[2,64,512]{2,1,0:T(8,128)(2,1)S(1)}, u32[]{:S(2)}, u32[]{:S(2)}) collective-permute-start(bf16[2,64,512]{2,1,0:T(8,128)(2,1)S(1)} %broadcast_select_fusion.16), channel_id=1, source_target_pairs={{0,4},{1,5},{2,6},{3,7},{4,0},{5,1},{6,2},{7,3},{8,12},{9,13},{10,... | collective-permute-start | bytes 393224 | tf_op jit(solution)/shard_map/ppermute | solution.py:65
  114.6 5.0 %collective-permute-start.10 = (bf16[2,64,512]{2,1,0:T(8,128)(2,1)S(1)}, bf16[2,64,512]{2,1,0:T(8,128)(2,1)S(1)}, u32[]{:S(2)}, u32[]{:S(2)}) collective-permute-start(bf16[2,64,512]{2,1,0:T(8,128)(2,1)S(1)} %broadcast_select_fusion.17), channel_id=1, source_target_pairs={{0,4},{1,5},{2,6},{3,7},{4,0},{5,1},{6,2},{7,3},{8,12},{9,13},{10,... | collective-permute-start | bytes 393224 | tf_op jit(solution)/shard_map/ppermute | solution.py:65
  119.6 8.2 %collective-permute-start.17 = (bf16[2,128,512]{2,1,0:T(8,128)(2,1)S(1)}, bf16[2,128,512]{2,1,0:T(8,128)(2,1)S(1)}, u32[]{:S(2)}, u32[]{:S(2)}) collective-permute-start(bf16[2,128,512]{2,1,0:T(8,128)(2,1)S(1)} %pad_maximum_fusion.1.refs_0_), channel_id=1, source_target_pairs={{0,2},{1,3},{2,0},{3,1},{4,6},{5,7},{6,4},{7,5},{8,10},{9,11},{10,... | collective-permute-start | bytes 786440 | tf_op jit(solution)/shard_map/ppermute | solution.py:65
  120.9 6.8 %copy-start.2 = (f32[4,2,128,512]{3,2,1,0:T(8,128)S(1)}, f32[4,2,128,512]{3,2,1,0:T(8,128)}, u32[]{:S(2)}) copy-start(f32[4,2,128,512]{3,2,1,0:T(8,128)} %constant.226.clone.refs_9_) | copy-start | bytes 6291460
  120.9 6.8 %copy-start.3 = (bf16[4,512,256]{2,1,0:T(8,128)(2,1)S(1)}, bf16[4,512,256]{2,1,0:T(8,128)(2,1)}, u32[]{:S(2)}) copy-start(bf16[4,512,256]{2,1,0:T(8,128)(2,1)} %constant.231.refs_8_) | copy-start | bytes 3145732
  120.9 6.8 %copy-start.4 = (bf16[4,256,256]{2,1,0:T(8,128)(2,1)S(1)}, bf16[4,256,256]{2,1,0:T(8,128)(2,1)}, u32[]{:S(2)}) copy-start(bf16[4,256,256]{2,1,0:T(8,128)(2,1)} %constant.230.refs_7_) | copy-start | bytes 1572868
  121.0 14.0 %collective-permute-start.18 = (bf16[2,128,512]{2,1,0:T(8,128)(2,1)S(1)}, bf16[2,128,512]{2,1,0:T(8,128)(2,1)S(1)}, u32[]{:S(2)}, u32[]{:S(2)}) collective-permute-start(bf16[2,128,512]{2,1,0:T(8,128)(2,1)S(1)} %pad_maximum_fusion.1.refs_0_), channel_id=1, source_target_pairs={{0,1},{1,0},{2,3},{3,2},{4,5},{5,4},{6,7},{7,6},{8,9},{9,8},{10,11... | collective-permute-start | bytes 786440 | tf_op jit(solution)/shard_map/ppermute | solution.py:65
  121.1 13.4 %collective-permute-start.11 = (bf16[2,128,512]{2,1,0:T(8,128)(2,1)S(1)}, bf16[2,128,512]{2,1,0:T(8,128)(2,1)S(1)}, u32[]{:S(2)}, u32[]{:S(2)}) collective-permute-start(bf16[2,128,512]{2,1,0:T(8,128)(2,1)S(1)} %pad_maximum_fusion.refs_0_), channel_id=1, source_target_pairs={{0,2},{1,3},{2,0},{3,1},{4,6},{5,7},{6,4},{7,5},{8,10},{9,11},{10,... | collective-permute-start | bytes 786440 | tf_op jit(solution)/shard_map/ppermute | solution.py:65
  124.0 17.4 %collective-permute-start.12 = (bf16[2,128,512]{2,1,0:T(8,128)(2,1)S(1)}, bf16[2,128,512]{2,1,0:T(8,128)(2,1)S(1)}, u32[]{:S(2)}, u32[]{:S(2)}) collective-permute-start(bf16[2,128,512]{2,1,0:T(8,128)(2,1)S(1)} %pad_maximum_fusion.refs_0_), channel_id=1, source_target_pairs={{0,1},{1,0},{2,3},{3,2},{4,5},{5,4},{6,7},{7,6},{8,9},{9,8},{10,11... | collective-permute-start | bytes 786440 | tf_op jit(solution)/shard_map/ppermute | solution.py:65
  127.7 7.2 %collective-permute-start.19 = (bf16[2,128,512]{2,1,0:T(8,128)(2,1)S(1)}, bf16[2,128,512]{2,1,0:T(8,128)(2,1)S(1)}, u32[]{:S(2)}, u32[]{:S(2)}) collective-permute-start(bf16[2,128,512]{2,1,0:T(8,128)(2,1)S(1)} %collective-permute-done.17.refs_1_), channel_id=1, source_target_pairs={{0,1},{1,0},{2,3},{3,2},{4,5},{5,4},{6,7},{7,6},{8,9},{9,8},{10,11... | collective-permute-start | bytes 786440 | tf_op jit(solution)/shard_map/ppermute | solution.py:65
  134.4 7.0 %collective-permute-start.13 = (bf16[2,128,512]{2,1,0:T(8,128)(2,1)S(1)}, bf16[2,128,512]{2,1,0:T(8,128)(2,1)S(1)}, u32[]{:S(2)}, u32[]{:S(2)}) collective-permute-start(bf16[2,128,512]{2,1,0:T(8,128)(2,1)S(1)} %collective-permute-done.11.refs_1_), channel_id=1, source_target_pairs={{0,1},{1,0},{2,3},{3,2},{4,5},{5,4},{6,7},{7,6},{8,9},{9,8},{10,11... | collective-permute-start | bytes 786440 | tf_op jit(solution)/shard_map/ppermute | solution.py:65

commit v7 on v6

--- a/solution.py
+++ b/solution.py
@@ -15,10 +15,12 @@
 PART = 128
 ROW_STEP = 16
 WAVE_ROWS = 32
-SEND_ROWS = 16
+SEND_ROWS = 32
 CORES = 2
-PAIR = 2
-QUAD = CORES * PAIR
+HALF_CHUNKS = 2
+LAG = 2
+TEMPLATE_SLOT = 4
+MASKED_SLOT = 12
 VMEM_LIMIT = 24 * 1024 * 1024
 
 
@@ -57,49 +59,59 @@
     return rows, cols
 
 
-def partner(flip):
-    return [(at, at ^ flip) for at in range(lax.axis_size("tpl"))]
-
-
-def swap(block, flip):
-    return lax.ppermute(block, "tpl", partner(flip))
-
-
-def quarter_of(strain_slots, det, owner):
-    me = lax.axis_index("tpl")
-    core, chip = me % CORES, me // CORES % PAIR
+def ring_order(chips):
+    return list(range(0, chips, 2)) + list(range(chips - 1 - chips % 2, 0, -2))
+
+
+def to_partner():
+    return [(i, i ^ 1) for i in range(lax.axis_size("tpl"))]
+
+
+def half_chunks(strain_slots, det, owner):
+    core = lax.axis_index("tpl") % CORES
     half = ROWS * COLS // CORES
-    bins = half // PAIR
+    bins = half // HALF_CHUNKS
     side = lambda which: lax.dynamic_slice(strain_slots, (0, det, 0, which * half), (1, 1, 2, half))[0, 0]
-    got = swap(side(1 - core), 1)
-    kept = jnp.where(core == owner % CORES, side(core), got)
-    got = swap(jnp.where(chip == 0, kept[:, bins:], kept[:, :bins]), CORES)
-    kept = jnp.where(chip == 0, kept[:, :bins], kept[:, bins:])
-    return jnp.where(chip == owner // CORES % PAIR, kept, got).reshape(2, ROWS // QUAD, COLS)
-
-
-def along_line(quarter, owner):
-    lines = lax.axis_size("tpl") // QUAD
-    line, from_line = lax.axis_index("tpl") // QUAD, owner // QUAD
-    if lines == 1:
-        return quarter
-    odd = line % 2 == 1
-    quarter = jnp.where(line % 2 == from_line % 2, quarter, swap(quarter, QUAD))
-    if lines == 2:
-        return quarter
-    rows = quarter.shape[1] // 2
-    piece = jnp.where(odd, quarter[:, rows:], quarter[:, :rows])
-    bit = 2
-    while bit < lines:
-        piece = jnp.where(line // bit % 2 == from_line // bit % 2, piece, swap(piece, bit * QUAD))
-        bit *= 2
-    other = swap(piece, QUAD)
-    return jnp.concatenate([jnp.where(odd, other, piece), jnp.where(odd, piece, other)], 1)
-
-
-def all_quarters(quarter):
-    beside = swap(quarter, CORES)
-    return quarter, beside, swap(quarter, 1), swap(beside, 1)
+    got = lax.ppermute(side(1 - core), "tpl", to_partner())
+    first = jnp.where(core == owner % CORES, side(core), got)
+    return [first[:, at : at + bins].reshape(2, bins // COLS, COLS) for at in range(0, half, bins)]
+
+
+def spread(chunks, owner, hooks):
+    devices = lax.axis_size("tpl")
+    chips = devices // CORES
+    order = ring_order(chips)
+    chip, core = lax.axis_index("tpl") // CORES, lax.axis_index("tpl") % CORES
+    on_owner_chip = chip == owner // CORES
+    along = []
+    for at in range(chips):
+        along.append((order[at] * CORES, order[(at + 1) % chips] * CORES))
+        along.append((order[(at + 1) % chips] * CORES + 1, order[at] * CORES + 1))
+    sent, arrived = [], []
+    count = len(chunks)
+    for slot in range(count + LAG * (chips - 1)):
+        if slot < LAG:
+            here = chunks[slot]
+        elif slot < count:
+            here = jnp.where(on_owner_chip, chunks[slot], arrived[slot - LAG])
+        else:
+            here = arrived[slot - LAG]
+        if slot in hooks:
+            here = hooks[slot](here)
+        sent.append(here)
+        if slot < count + LAG * (chips - 2):
+            arrived.append(lax.ppermute(here, "tpl", along))
+    shared = [lax.ppermute(here, "tpl", to_partner()) for here in sent]
+    return sent, shared
+
+
+def distances(owner):
+    chips = lax.axis_size("tpl") // CORES
+    chip, core = lax.axis_index("tpl") // CORES, lax.axis_index("tpl") % CORES
+    place = lambda at: jnp.where(at % 2 == 0, at // 2, chips - 1 - at // 2)
+    forward = (place(chip) - place(owner // CORES)) % chips
+    backward = (place(owner // CORES) - place(chip)) % chips
+    return jnp.where(core == 0, forward, backward), jnp.where(core == 0, backward, forward)
 
 
 def pick(templates, lists):
@@ -139,11 +151,6 @@
     return [[found[at].transpose(1, 0, 2, 3)] for at in range(per_device)]
 
 
-def held(values):
-    scaled = values * 65537.0
-    return scaled - (scaled - values)
-
-
 def quarters(parts):
     (re0, im0), (re1, im1), (re2, im2), (re3, im3) = parts
     even_re, even_im, odd_re, odd_im = re0 + re2, im0 + im2, re1 + re3, im1 + im3
@@ -161,7 +168,7 @@
     pieces = len(piece_refs) // count
     rows = WAVE_ROWS // pieces
     for tpl in range(count):
-        cutoff = cut_ref[list_ref[where_ref[2] * count + where_ref[3 + tpl]]]
+        cutoff = cut_ref[list_ref[where_ref[2] * count + where_ref[4 + tpl]]]
         total = jnp.zeros((8, COLS), jnp.float32)
         for piece in range(pieces):
             wave_ref = piece_refs[tpl * pieces + piece]
@@ -178,26 +185,35 @@
         sigma_ref[tpl] = jnp.sum(total)
 
 
-def detector_kernel(det, where_ref, sigma_ref, *refs):
+def detector_kernel(det, chips, where_ref, sigma_ref, *refs):
     first, last = det == 0, det == DET - 1
-    quarter_refs, refs = refs[:QUAD], refs[QUAD:]
+    slots = HALF_CHUNKS + LAG * (chips - 1)
+    near_refs, far_refs, refs = refs[:slots], refs[slots : 2 * slots], refs[2 * slots :]
     masked, rphase_ref, cphase_ref, row_ref, col_ref, twiddle_ref = refs[:6]
     refs = refs[6:]
     before, refs = (None, refs) if first else (refs[0], refs[1:])
-    outputs, (turned_ref, slid, stacked, twisted) = refs[:-4], refs[-4:]
+    outputs, (strain_ref, strain_sem, turned_ref, slid, stacked, twisted) = refs[:-6], refs[-6:]
     count = masked.shape[0]
-    core, chip = where_ref[0], where_ref[1]
-    half, rows = ROWS // CORES, ROWS // QUAD
-
+    core, near, far = where_ref[0], where_ref[1], where_ref[3]
+    half = ROWS // CORES
+    rows = half // HALF_CHUNKS
+
+    for slot_refs, distance, side in ((near_refs, near, core), (far_refs, far, 1 - core)):
+        for away in range(chips):
+            @pl.when(distance == away)
+            def _():
+                for at in range(HALF_CHUNKS):
+                    into = pl.ds(pl.multiple_of(side * half + at * rows, rows), rows)
+                    pltpu.make_async_copy(slot_refs[at + LAG * away], strain_ref.at[:, into, :], strain_sem).start()
     turned_ref[...] = rphase_ref[det].T
     cc, cs = cphase_ref[det, 0:1, :], cphase_ref[det, 1:2, :]
-    for which, quarter in enumerate(quarter_refs):
-        of_core, of_chip = (core if which < 2 else 1 - core), (chip if which % 2 == 0 else 1 - chip)
-        part = pl.ds(pl.multiple_of(of_core * half + of_chip * rows, rows), rows)
+    pltpu.make_async_copy(strain_ref, strain_ref, strain_sem).wait()
+    for at in range(0, ROWS, PART):
+        part = slice(at, at + PART)
         rc, rs = turned_ref[part, 0:1], turned_ref[part, 1:2]
         turn_re = rc * cc - rs * cs
         turn_im = rc * cs + rs * cc
-        data_re, data_im = quarter[0].astype(jnp.float32), quarter[1].astype(jnp.float32)
+        data_re, data_im = strain_ref[0, part, :].astype(jnp.float32), strain_ref[1, part, :].astype(jnp.float32)
         slid[0, part, :] = data_re * turn_re - data_im * turn_im
         slid[1, part, :] = data_re * turn_im + data_im * turn_re
 
@@ -212,7 +228,7 @@
                     wave_re = masked[tpl, 0, spot, cols].astype(jnp.float32)
                     wave_im = masked[tpl, 1, spot, cols].astype(jnp.float32)
                     data_re, data_im = slid[0, spot, cols], slid[1, spot, cols]
-                    parts.append((held(data_re * wave_re + data_im * wave_im), held(data_im * wave_re - data_re * wave_im)))
+                    parts.append((data_re * wave_re + data_im * wave_im, data_im * wave_re - data_re * wave_im))
                 for residue, (re, im) in enumerate(quarters(parts)):
                     stacked[tpl, residue, at : at + ROW_STEP, cols] = re.astype(jnp.bfloat16)
                     stacked[tpl, residue, PART + at : PART + at + ROW_STEP, cols] = im.astype(jnp.bfloat16)
@@ -225,7 +241,7 @@
                     re, im = section[at : at + ROW_STEP, cols], section[PART + at : PART + at + ROW_STEP, cols]
                     turn_re = twiddle_ref[residue, 0, at : at + ROW_STEP, cols]
                     turn_im = twiddle_ref[residue, 1, at : at + ROW_STEP, cols]
-                    parts.append((held(re * turn_re - im * turn_im), held(re * turn_im + im * turn_re)))
+                    parts.append((re * turn_re - im * turn_im, re * turn_im + im * turn_re))
                 spot = slice(residue * PART + at, residue * PART + at + ROW_STEP)
                 for other, sums in enumerate(quarters(parts)):
                     for which, value in enumerate(sums):
@@ -248,13 +264,14 @@
 
     if last:
         for tpl in range(count):
-            place = where_ref[3 + tpl]
+            place = where_ref[4 + tpl]
             outputs[0][place] = jnp.max(largest[tpl]) / (2.0 * (sigma_ref[tpl] + eps_norm))
             outputs[1][place] = sigma_ref[tpl] / (ROWS * COLS)
 
 
 smem = pl.BlockSpec(memory_space=pltpu.SMEM)
 vmem = pl.BlockSpec(memory_space=pltpu.VMEM)
+anywhere = pl.BlockSpec(memory_space=pl.ANY)
 
 
 def prepare(cutoffs, lists, where, waves):
@@ -273,17 +290,21 @@
     )(cutoffs, lists, where, *operands)
 
 
-def detector(det, where, sigma, found, masked, turns, before):
+def detector(det, chips, where, sigma, sent, shared, masked, turns, before):
     count = masked.shape[0]
+    slots = slice(det * HALF_CHUNKS, (det + 1) * HALF_CHUNKS + LAG * (chips - 1))
+    found = [*sent[slots], *shared[slots]]
     last = det == DET - 1
     scalars = jax.ShapeDtypeStruct((count,), jnp.float32)
-    operands = [*found, masked, *turns, *tables(), *before]
+    operands = [masked, *turns, *tables(), *before]
     return pl.pallas_call(
-        functools.partial(detector_kernel, det),
+        functools.partial(detector_kernel, det, chips),
         out_shape=(scalars, scalars) if last else (jax.ShapeDtypeStruct((count, ROWS, COLS), jnp.float32),),
-        in_specs=[smem, smem] + [vmem] * len(operands),
+        in_specs=[smem, smem] + [anywhere] * len(found) + [vmem] * len(operands),
         out_specs=(smem, smem) if last else (vmem,),
         scratch_shapes=[
+            pltpu.VMEM((2, ROWS, COLS), jnp.bfloat16),
+            pltpu.SemaphoreType.DMA,
             pltpu.VMEM((ROWS, 8), jnp.float32),
             pltpu.VMEM((2, ROWS, COLS), jnp.float32),
             pltpu.VMEM((count, RADIX, 2 * PART, COLS), jnp.bfloat16),
@@ -291,37 +312,45 @@
         ],
         compiler_params=pltpu.CompilerParams(vmem_limit_bytes=VMEM_LIMIT),
         cost_estimate=pl.CostEstimate(flops=5_000_000_000, bytes_accessed=10_000_000, transcendentals=0),
-    )(where, sigma, *operands)
+    )(where, sigma, *found, *operands)
 
 
 def body(strain_slots, templates, cutoffs, lists, owner, slides):
     me, owner = lax.axis_index("tpl"), owner[0]
+    chips = lax.axis_size("tpl") // CORES
     per_device = lists.shape[1]
+    chunks = half_chunks(strain_slots, 0, owner)
+    strain_slots, templates, chunks = lax.optimization_barrier((strain_slots, templates, chunks))
     parts, places = pick(templates, lists)
-    (strain_slots, parts) = lax.optimization_barrier((strain_slots, parts))
     ids = list(range(per_device)) if places is None else places
-    where = jnp.stack([jnp.asarray(at, jnp.int32) for at in (me % CORES, me // CORES % PAIR, me, *ids)])
-    small = (*slide_turns(slides), where, lists.reshape(-1))
-
-    quarter = [quarter_of(strain_slots, 0, owner)]
-    arrived = [exchange(parts[0])]
-    strain_slots, quarter[0], small, arrived[0] = lax.optimization_barrier((strain_slots, quarter[0], small, arrived[0]))
-    arrived += [exchange(part) for part in parts[1:]]
+    near, far = distances(owner)
+    where = jnp.stack([jnp.asarray(at, jnp.int32) for at in (me % CORES, near, me, far, *ids)])
     for det in range(1, DET):
-        quarter.append(quarter_of(strain_slots, det, owner))
-        strain_slots, quarter[det] = lax.optimization_barrier((strain_slots, quarter[det]))
-    quarter[1:], arrived[1:] = lax.optimization_barrier((quarter[1:], arrived[1:]))
-    *turns, where, flat_list = small
-
-    found = [all_quarters(along_line(part, owner)) for part in quarter]
-    if places is None:
-        waves = assemble(arrived[0], per_device)
-    else:
-        waves = [list(wave) for wave in zip(*[across(own) for own in arrived])]
-    masked, sigma = prepare(cutoffs, flat_list, where, waves)
+        more = half_chunks(strain_slots, det, owner)
+        strain_slots, more = lax.optimization_barrier((strain_slots, more))
+        chunks += more
+    held = {"arrived": exchange(parts[0]), "small": (slide_turns(slides), where, lists.reshape(-1))}
+
+    def templates_here(chunk):
+        chunk, held["arrived"], held["small"] = lax.optimization_barrier((chunk, held["arrived"], held["small"]))
+        if places is None:
+            waves = assemble(held["arrived"], per_device)
+        else:
+            waves = [[wave] for wave in across(held["arrived"])]
+        _, where, flat_list = held["small"]
+        held["masked"] = prepare(cutoffs, flat_list, where, waves)
+        return chunk
+
+    def masked_here(chunk):
+        chunk, held["masked"] = lax.optimization_barrier((chunk, held["masked"]))
+        return chunk
+
+    sent, shared = spread(chunks, owner, {TEMPLATE_SLOT: templates_here, MASKED_SLOT: masked_here})
+    turns, where, _ = held["small"]
+    masked, sigma = held["masked"]
     result = ()
     for det in range(DET):
-        result = detector(det, where, sigma, found[det], masked, turns, result)
+        result = detector(det, chips, where, sigma, sent, shared, masked, turns, result)
     return result
 
 

time: 150 us -> 123 us (0.82)
  waiting for transfers between devices: 58.9 us -> 35.5 us
  starting transfers between devices: 39.8 us -> 44.4 us
  local copies, waits for them, and re-layouts: 14.9 us -> 11.2 us
  other arithmetic: 10.8 us -> 8.69 us
    ppermute x24 -> x41, waiting for transfers between devices: 58.8 us -> 35.2 us  [the longest x18 35.1 us: spread(): arrived.append(lax.ppermute(here, 'tpl', along))]
    ppermute x24 -> x41, starting transfers between devices: 24.4 us -> 39 us  [the longest x18 33.6 us: spread(): arrived.append(lax.ppermute(here, 'tpl', along))]
    all_to_all x2 -> x1, starting transfers between devices: 12.5 us -> 3.91 us  [exchange(): return lax.all_to_all(block, 'tpl', split_axis=0, concat_axis=0, tiled=True)]
    select_n x21 -> x7, other arithmetic: 9.3 us -> 7.31 us  [the longest x3 3.82 us: half_chunks(): first = jnp.where(core == owner % CORES, side(core), got)]
    squeeze x3, local copies, waits for them, and re-layouts: 4.99 us -> 3.07 us  [half_chunks(): lax.dynamic_slice(strain_slots, (0, det, 0, which * half), (1, 1, 2, half))]
    unnamed x18 -> x31, local copies, waits for them, and re-layouts: 3.05 us -> 1.65 us
  transfers between devices with their start and end apart: 28 -> 43, of which waited for: 13 -> 14; matrix products, arithmetic and copies ran while one was open for 8% -> 12% of each run, Pallas kernels for 10% -> 11%
where the time goes in v7:
time: 123 us
  starting transfers between devices  44.4 us (36%)
  waiting for transfers between devices  35.5 us (29%)
  Pallas kernels  20.8 us (17%)
  local copies, waits for them, and re-layouts  11.2 us (9%)
  other arithmetic  8.69 us (7%)
  between operations  2.04 us (2%)
    ppermute x18, waiting for transfers between devices, spread(): arrived.append(lax.ppermute(here, 'tpl', along))  35.1 us
    ppermute x18, starting transfers between devices, spread(): arrived.append(lax.ppermute(here, 'tpl', along))  33.6 us
    pallas_call x3, Pallas kernels, detector(): pl.pallas_call(functools.partial(detector_kernel, det, chips), out_shape=...  18.7 us
    ppermute x20, starting transfers between devices, spread(): shared = [lax.ppermute(here, 'tpl', to_partner()) for here in sent]  4.53 us
    all_to_all x1, starting transfers between devices, exchange(): return lax.all_to_all(block, 'tpl', split_axis=0, concat_axis=0, tiled=True)  3.91 us
    select_n x3, other arithmetic, half_chunks(): first = jnp.where(core == owner % CORES, side(core), got)  3.82 us
    select_n x4, other arithmetic, spread(): here = jnp.where(on_owner_chip, chunks[slot], arrived[slot - LAG])  3.48 us
    squeeze x3, local copies, waits for them, and re-layouts, half_chunks(): lax.dynamic_slice(strain_slots, (0, det, 0, which * half), (1, 1, 2, half))  3.07 us
  transfers between devices with their start and end apart: 43, of which 14 were waited for; matrix products, arithmetic and copies ran while one was open for 12% of the time, Pallas kernels for 11%

profile of v7, /device:TPU:0, one launch (start us, length us, event | category | flops | bytes accessed | tf_op | source)
XLA Modules:
  0.0 122.6 jit_solution(8830367034823589140)
XLA Ops:
  0.7 1.5 %dynamic-slice_bitcast_fusion.2 = bf16[2,131072]{1,0:T(2,128)(2,1)S(1)} fusion(bf16[1,3,2,262144]{3,2,1,0:T(2,128)(2,1)} %param.15, s32[]{:T(128)S(6)} %select_n.186), kind=kLoop, calls=%fused_computation.6 | loop fusion | bytes 1048580 | tf_op jit(solution)/shard_map/squeeze | solution.py:74
  3.4 0.8 and_select_fusion.2
  4.3 1.7 %broadcast_select_fusion.2 = bf16[2,131072]{1,0:T(2,128)(2,1)S(1)} fusion(bf16[2,131072]{1,0:T(2,128)(2,1)S(1)} %collective-permute-done, pred[]{:T(512)S(6)} %eq.43, bf16[1,3,2,262144]{3,2,1,0:T(2,128)(2,1)} %param.15, s32[]{:T(128)S(6)} %select_n.185), kind=kLoop, calls=%fused_computation.3 | loop fusion | flops 262144 | bytes 1572869 | tf_op jit(solution)/shard_map/jit(_where)/select_n | solution.py:76
  6.4 0.8 copy_bitcast_fusion.4
  8.4 2.9 %collective-permute-start.10 = (bf16[2,128,512]{2,1,0:T(8,128)(2,1)S(1)}, bf16[2,128,512]{2,1,0:T(8,128)(2,1)}, u32[]{:S(2)}, u32[]{:S(2)}) collective-permute-start(bf16[2,128,512]{2,1,0:T(8,128)(2,1)S(1)} %get-tuple-element.37.refs_1_), channel_id=1, source_target_pairs={{0,4},{5,1},{4,8},{9,5},{8,12},{13,9},{12,14},{15,13},{14,10},{11,... | collective-permute-start | bytes 786440 | tf_op jit(solution)/shard_map/ppermute | solution.py:103
  11.3 1.6 %collective-permute-start.3 = (bf16[2,128,512]{2,1,0:T(8,128)(2,1)}, bf16[2,128,512]{2,1,0:T(8,128)(2,1)}, u32[]{:S(2)}, u32[]{:S(2)}) collective-permute-start(bf16[2,128,512]{2,1,0:T(8,128)(2,1)} %get-tuple-element.26.refs_0_), channel_id=1, source_target_pairs={{0,4},{5,1},{4,8},{9,5},{8,12},{13,9},{12,14},{15,13},{14,10},{11,... | collective-permute-start | bytes 786440 | tf_op jit(solution)/shard_map/ppermute | solution.py:103
  15.2 1.2 dynamic-slice_bitcast_fusion
  17.0 2.7 %gather_fusion = bf16[16,2,16384]{2,1,0:T(2,128)(2,1)S(1)} fusion(bf16[32,2,16384]{2,1,0:T(2,128)(2,1)S(1)} %copy-done, s32[1024]{0:T(1024)S(1)} %pad_clamp_fusion), kind=kCustom, calls=%fused_computation | custom fusion | bytes 2097216 | tf_op jit(solution)/shard_map/gather | solution.py:127
  19.7 1.6 %reshape.216 = bf16[16,2,32,512]{3,2,1,0:T(8,128)(2,1)} reshape(bf16[16,2,16384]{2,1,0:T(2,128)(2,1)S(1)} %gather_fusion) | data formatting | bytes 2097152 | tf_op jit(solution)/shard_map/reshape | solution.py:128
  21.2 3.9 %all-to-all-start = ((bf16[16,2,32,512]{3,2,1,0:T(8,128)(2,1)}), bf16[16,2,32,512]{3,2,1,0:T(8,128)(2,1)S(1)}, u32[]{:S(2)}, u32[]{:S(2)}) async-start(bf16[16,2,32,512]{3,2,1,0:T(8,128)(2,1)} %reshape.216), calls=%async_computation | async-start | bytes 2097152 | tf_op jit(solution)/shard_map/all_to_all | solution.py:136
  25.2 1.0 broadcast_select_fusion.4.refs_3_.refs_1_
  26.2 2.0 %collective-permute-start.11 = (bf16[2,128,512]{2,1,0:T(8,128)(2,1)S(1)}, bf16[2,128,512]{2,1,0:T(8,128)(2,1)S(1)}, u32[]{:S(2)}, u32[]{:S(2)}) collective-permute-start(bf16[2,128,512]{2,1,0:T(8,128)(2,1)S(1)} %broadcast_select_fusion.4.refs_3_.refs_1_), channel_id=1, source_target_pairs={{0,4},{5,1},{4,8},{9,5},{8,12},{13,9},{12,14},{15,13},{14,10},{11,... | collective-permute-start | bytes 786440 | tf_op jit(solution)/shard_map/ppermute | solution.py:103
  28.2 1.0 broadcast_select_fusion.6.refs_2_.refs_0_
  29.2 1.5 %collective-permute-start.4 = (bf16[2,128,512]{2,1,0:T(8,128)(2,1)S(1)}, bf16[2,128,512]{2,1,0:T(8,128)(2,1)S(1)}, u32[]{:S(2)}, u32[]{:S(2)}) collective-permute-start(bf16[2,128,512]{2,1,0:T(8,128)(2,1)S(1)} %broadcast_select_fusion.6.refs_2_.refs_0_), channel_id=1, source_target_pairs={{0,4},{5,1},{4,8},{9,5},{8,12},{13,9},{12,14},{15,13},{14,10},{11,... | collective-permute-start | bytes 786440 | tf_op jit(solution)/shard_map/ppermute | solution.py:103
  30.7 1.6 %broadcast_select_fusion = bf16[2,131072]{1,0:T(2,128)(2,1)S(1)} fusion(bf16[2,131072]{1,0:T(2,128)(2,1)} %collective-permute-done.2, pred[]{:T(512)S(6)} %eq.43, bf16[1,3,2,262144]{3,2,1,0:T(2,128)(2,1)} %param.15, s32[]{:T(128)S(6)} %select_n.185), kind=kLoop, calls=%fused_computation.1 | loop fusion | flops 262144 | bytes 1572869 | tf_op jit(solution)/shard_map/jit(_where)/select_n | solution.py:76
  32.7 13.3 %collective-permute-done.11 = bf16[2,128,512]{2,1,0:T(8,128)(2,1)S(1)} collective-permute-done((bf16[2,128,512]{2,1,0:T(8,128)(2,1)S(1)}, bf16[2,128,512]{2,1,0:T(8,128)(2,1)S(1)}, u32[]{:S(2)}, u32[]{:S(2)}) %collective-permute-start.11) | collective-permute-done | bytes 262176 | tf_op jit(solution)/shard_map/ppermute | solution.py:103
  46.8 7.1 %collective-permute-start.12 = (bf16[2,128,512]{2,1,0:T(8,128)(2,1)}, bf16[2,128,512]{2,1,0:T(8,128)(2,1)}, u32[]{:S(2)}, u32[]{:S(2)}) collective-permute-start(bf16[2,128,512]{2,1,0:T(8,128)(2,1)} %broadcast_select_fusion.3.refs_5_.refs_3_.refs_1_), channel_id=1, source_target_pairs={{0,4},{5,1},{4,8},{9,5},{8,12},{13,9},{12,14},{15,13},{14,10},{11,... | collective-permute-start | bytes 786440 | tf_op jit(solution)/shard_map/ppermute | solution.py:103
  54.0 0.8 broadcast_select_fusion.5.refs_4_.refs_2_.refs_0_
  54.8 2.5 %collective-permute-start.5 = (bf16[2,128,512]{2,1,0:T(8,128)(2,1)}, bf16[2,128,512]{2,1,0:T(8,128)(2,1)S(1)}, u32[]{:S(2)}, u32[]{:S(2)}) collective-permute-start(bf16[2,128,512]{2,1,0:T(8,128)(2,1)} %broadcast_select_fusion.5.refs_4_.refs_2_.refs_0_), channel_id=1, source_target_pairs={{0,4},{5,1},{4,8},{9,5},{8,12},{13,9},{12,14},{15,13},{14,10},{11,... | collective-permute-start | bytes 786440 | tf_op jit(solution)/shard_map/ppermute | solution.py:103
  57.3 1.5 %collective-permute-start.9 = (bf16[16,2,32,512]{3,2,1,0:T(8,128)(2,1)S(1)}, bf16[16,2,32,512]{3,2,1,0:T(8,128)(2,1)S(1)}, u32[]{:S(2)}, u32[]{:S(2)}) collective-permute-start(bf16[16,2,32,512]{3,2,1,0:T(8,128)(2,1)S(1)} %all-to-all-done.refs_0_), channel_id=1, source_target_pairs={{0,16},{16,0},{1,17},{17,1},{2,18},{18,2},{3,19},{19,3},{4,20},{20... | collective-permute-start | bytes 3145736 | tf_op jit(solution)/shard_map/ppermute | solution.py:142
  58.8 2.1 %collective-permute-start.13 = (bf16[2,128,512]{2,1,0:T(8,128)(2,1)}, bf16[2,128,512]{2,1,0:T(8,128)(2,1)S(1)}, u32[]{:S(2)}, u32[]{:S(2)}) collective-permute-start(bf16[2,128,512]{2,1,0:T(8,128)(2,1)} %collective-permute-done.12.refs_7_.refs_5_.refs_3_), channel_id=1, source_target_pairs={{0,4},{5,1},{4,8},{9,5},{8,12},{13,9},{12,14},{15,13},{14,10},{11,... | collective-permute-start | bytes 786440 | tf_op jit(solution)/shard_map/ppermute | solution.py:103
  61.5 2.4 %collective-permute-start.6 = (bf16[2,128,512]{2,1,0:T(8,128)(2,1)S(1)}, bf16[2,128,512]{2,1,0:T(8,128)(2,1)S(1)}, u32[]{:S(2)}, u32[]{:S(2)}) collective-permute-start(bf16[2,128,512]{2,1,0:T(8,128)(2,1)S(1)} %collective-permute-done.5.refs_6_.refs_4_.refs_2_), channel_id=1, source_target_pairs={{0,4},{5,1},{4,8},{9,5},{8,12},{13,9},{12,14},{15,13},{14,10},{11,... | collective-permute-start | bytes 786440 | tf_op jit(solution)/shard_map/ppermute | solution.py:103
  63.9 2.7 %collective-permute-done.13.refs_9_.refs_7_.refs_5_ = bf16[2,128,512]{2,1,0:T(8,128)(2,1)S(1)} collective-permute-done((bf16[2,128,512]{2,1,0:T(8,128)(2,1)}, bf16[2,128,512]{2,1,0:T(8,128)(2,1)S(1)}, u32[]{:S(2)}, u32[]{:S(2)}) %collective-permute-start.13) | collective-permute-done | bytes 262176 | tf_op jit(solution)/shard_map/ppermute | solution.py:103
  66.6 0.9 collective-permute-start.14
  68.0 1.4 %collective-permute-done.6.refs_8_.refs_6_.refs_4_ = bf16[2,128,512]{2,1,0:T(8,128)(2,1)S(1)} collective-permute-done((bf16[2,128,512]{2,1,0:T(8,128)(2,1)S(1)}, bf16[2,128,512]{2,1,0:T(8,128)(2,1)S(1)}, u32[]{:S(2)}, u32[]{:S(2)}) %collective-permute-start.6) | collective-permute-done | bytes 262176 | tf_op jit(solution)/shard_map/ppermute | solution.py:103
  69.4 0.9 collective-permute-start.7
  70.3 2.7 %collective-permute-done.14.refs_11_.refs_9_.refs_7_ = bf16[2,128,512]{2,1,0:T(8,128)(2,1)S(1)} collective-permute-done((bf16[2,128,512]{2,1,0:T(8,128)(2,1)S(1)}, bf16[2,128,512]{2,1,0:T(8,128)(2,1)S(1)}, u32[]{:S(2)}, u32[]{:S(2)}) %collective-permute-start.14) | collective-permute-done | bytes 262176 | tf_op jit(solution)/shard_map/ppermute | solution.py:103
  73.0 0.9 collective-permute-start.15
  74.3 1.4 %collective-permute-done.7.refs_10_.refs_8_.refs_6_ = bf16[2,128,512]{2,1,0:T(8,128)(2,1)S(1)} collective-permute-done((bf16[2,128,512]{2,1,0:T(8,128)(2,1)S(1)}, bf16[2,128,512]{2,1,0:T(8,128)(2,1)S(1)}, u32[]{:S(2)}, u32[]{:S(2)}) %collective-permute-start.7) | collective-permute-done | bytes 262176 | tf_op jit(solution)/shard_map/ppermute | solution.py:103
  75.8 0.9 collective-permute-start.8
  76.6 2.7 %collective-permute-done.15.refs_13_.refs_11_.refs_9_ = bf16[2,128,512]{2,1,0:T(8,128)(2,1)S(1)} collective-permute-done((bf16[2,128,512]{2,1,0:T(8,128)(2,1)S(1)}, bf16[2,128,512]{2,1,0:T(8,128)(2,1)S(1)}, u32[]{:S(2)}, u32[]{:S(2)}) %collective-permute-start.15) | collective-permute-done | bytes 262176 | tf_op jit(solution)/shard_map/ppermute | solution.py:103
  79.3 0.9 collective-permute-start.17
  81.0 1.2 collective-permute-done.8.refs_12_.refs_10_.refs_8_
  82.2 2.1 %shard_map.158 = (bf16[2,2,512,512]{3,2,1,0:T(8,128)(2,1)S(1)}, f32[2]{0:T(128)S(1)}) custom-call(s32[32]{0:T(128)S(1)} %copy-done.6, s32[32]{0:T(128)S(1)} %reshape.217.list_ref, s32[6]{0:T(128)S(1)} %stack.27.where_ref, bf16[16,2,32,512]{3,2,1,0:T(8,128)(2,1)S(1)} %all-to-all-done.refs_0_, bf16[16,2,32,512]{3,2,1,0:T(8,128)(2,1)S(1)} %collective-permute-done.9.refs_1_), custom_call_target="tpu_custom_call" | custom-call | flops 2000000000 | bytes 6000000 | tf_op jit(solution)/shard_map/pallas_call | solution.py:280
  84.3 1.4 %collective-permute-done.17.refs_15_.refs_13_.refs_11_ = bf16[2,128,512]{2,1,0:T(8,128)(2,1)S(1)} collective-permute-done((bf16[2,128,512]{2,1,0:T(8,128)(2,1)S(1)}, bf16[2,128,512]{2,1,0:T(8,128)(2,1)S(1)}, u32[]{:S(2)}, u32[]{:S(2)}) %collective-permute-start.17) | collective-permute-done | bytes 262176 | tf_op jit(solution)/shard_map/ppermute | solution.py:103
  85.7 1.4 %collective-permute-start.19 = (bf16[2,128,512]{2,1,0:T(8,128)(2,1)S(1)}, bf16[2,128,512]{2,1,0:T(8,128)(2,1)S(1)}, u32[]{:S(2)}, u32[]{:S(2)}) collective-permute-start(bf16[2,128,512]{2,1,0:T(8,128)(2,1)S(1)} %collective-permute-done.17.refs_15_.refs_13_.refs_11_), channel_id=1, source_target_pairs={{0,4},{5,1},{4,8},{9,5},{8,12},{13,9},{12,14},{15,13},{14,10},{11,... | collective-permute-start | bytes 786440 | tf_op jit(solution)/shard_map/ppermute | solution.py:103
  87.1 1.8 %collective-permute-start.16 = (bf16[2,128,512]{2,1,0:T(8,128)(2,1)S(1)}, bf16[2,128,512]{2,1,0:T(8,128)(2,1)S(1)}, u32[]{:S(2)}, u32[]{:S(2)}) collective-permute-start(bf16[2,128,512]{2,1,0:T(8,128)(2,1)S(1)} %collective-permute-done.8.refs_12_.refs_10_.refs_8_), channel_id=1, source_target_pairs={{0,4},{5,1},{4,8},{9,5},{8,12},{13,9},{12,14},{15,13},{14,10},{11,... | collective-permute-start | bytes 786440 | tf_op jit(solution)/shard_map/ppermute | solution.py:103
  89.4 2.7 %collective-permute-done.19.refs_15_.refs_13_ = bf16[2,128,512]{2,1,0:T(8,128)(2,1)S(1)} collective-permute-done((bf16[2,128,512]{2,1,0:T(8,128)(2,1)S(1)}, bf16[2,128,512]{2,1,0:T(8,128)(2,1)S(1)}, u32[]{:S(2)}, u32[]{:S(2)}) %collective-permute-start.19) | collective-permute-done | bytes 262176 | tf_op jit(solution)/shard_map/ppermute | solution.py:103
  92.1 1.4 %collective-permute-start.21 = (bf16[2,128,512]{2,1,0:T(8,128)(2,1)S(1)}, bf16[2,128,512]{2,1,0:T(8,128)(2,1)S(1)}, u32[]{:S(2)}, u32[]{:S(2)}) collective-permute-start(bf16[2,128,512]{2,1,0:T(8,128)(2,1)S(1)} %collective-permute-done.19.refs_15_.refs_13_), channel_id=1, source_target_pairs={{0,4},{5,1},{4,8},{9,5},{8,12},{13,9},{12,14},{15,13},{14,10},{11,... | collective-permute-start | bytes 786440 | tf_op jit(solution)/shard_map/ppermute | solution.py:103
  93.4 1.4 %collective-permute-done.16.refs_14_.refs_12_.refs_10_ = bf16[2,128,512]{2,1,0:T(8,128)(2,1)S(1)} collective-permute-done((bf16[2,128,512]{2,1,0:T(8,128)(2,1)S(1)}, bf16[2,128,512]{2,1,0:T(8,128)(2,1)S(1)}, u32[]{:S(2)}, u32[]{:S(2)}) %collective-permute-start.16) | collective-permute-done | bytes 262176 | tf_op jit(solution)/shard_map/ppermute | solution.py:103
  94.9 1.4 %collective-permute-start.18 = (bf16[2,128,512]{2,1,0:T(8,128)(2,1)S(1)}, bf16[2,128,512]{2,1,0:T(8,128)(2,1)S(1)}, u32[]{:S(2)}, u32[]{:S(2)}) collective-permute-start(bf16[2,128,512]{2,1,0:T(8,128)(2,1)S(1)} %collective-permute-done.16.refs_14_.refs_12_.refs_10_), channel_id=1, source_target_pairs={{0,4},{5,1},{4,8},{9,5},{8,12},{13,9},{12,14},{15,13},{14,10},{11,... | collective-permute-start | bytes 786440 | tf_op jit(solution)/shard_map/ppermute | solution.py:103
  96.8 1.7 %collective-permute-done.21.refs_15_ = bf16[2,128,512]{2,1,0:T(8,128)(2,1)S(1)} collective-permute-done((bf16[2,128,512]{2,1,0:T(8,128)(2,1)S(1)}, bf16[2,128,512]{2,1,0:T(8,128)(2,1)S(1)}, u32[]{:S(2)}, u32[]{:S(2)}) %collective-permute-start.21) | collective-permute-done | bytes 262176 | tf_op jit(solution)/shard_map/ppermute | solution.py:103
  99.0 2.3 %collective-permute-done.18.refs_14_.refs_12_ = bf16[2,128,512]{2,1,0:T(8,128)(2,1)S(1)} collective-permute-done((bf16[2,128,512]{2,1,0:T(8,128)(2,1)S(1)}, bf16[2,128,512]{2,1,0:T(8,128)(2,1)S(1)}, u32[]{:S(2)}, u32[]{:S(2)}) %collective-permute-start.18) | collective-permute-done | bytes 262176 | tf_op jit(solution)/shard_map/ppermute | solution.py:103
  101.3 1.4 %collective-permute-start.20 = (bf16[2,128,512]{2,1,0:T(8,128)(2,1)S(1)}, bf16[2,128,512]{2,1,0:T(8,128)(2,1)S(1)}, u32[]{:S(2)}, u32[]{:S(2)}) collective-permute-start(bf16[2,128,512]{2,1,0:T(8,128)(2,1)S(1)} %collective-permute-done.18.refs_14_.refs_12_), channel_id=1, source_target_pairs={{0,4},{5,1},{4,8},{9,5},{8,12},{13,9},{12,14},{15,13},{14,10},{11,... | collective-permute-start | bytes 786440 | tf_op jit(solution)/shard_map/ppermute | solution.py:103
  102.7 6.2 %shard_map.159.refs_38_ = f32[2,512,512]{2,1,0:T(8,128)S(1)} custom-call(s32[6]{0:T(128)S(1)} %stack.27.where_ref, f32[2]{0:T(128)S(1)} %get-tuple-element.34.sigma_ref, bf16[2,128,512]{2,1,0:T(8,128)(2,1)} %get-tuple-element.26.refs_0_, bf16[2,128,512]{2,1,0:T(8,128)(2,1)S(1)} %get-tuple-element.37.refs_1_, bf16[2,128,512]{2,1,0:T(8,128)(2,1)S(1)} %copy-done.4, ...), custom_call_target="tpu_custom_call" | custom-call | flops 5000000000 | bytes 10000000 | tf_op jit(solution)/shard_map/pallas_call | solution.py:300
  108.9 1.0 collective-permute-start.36
  109.9 5.6 %shard_map.160.refs_38_ = f32[2,512,512]{2,1,0:T(8,128)S(1)} custom-call(s32[6]{0:T(128)S(1)} %stack.27.where_ref, f32[2]{0:T(128)S(1)} %get-tuple-element.34.sigma_ref, bf16[2,128,512]{2,1,0:T(8,128)(2,1)S(1)} %copy-done.4, bf16[2,128,512]{2,1,0:T(8,128)(2,1)S(1)} %copy-done.2, bf16[2,128,512]{2,1,0:T(8,128)(2,1)S(1)} %copy-done.5, ...), custom_call_target="tpu_custom_call" | custom-call | flops 5000000000 | bytes 10000000 | tf_op jit(solution)/shard_map/pallas_call | solution.py:300
  115.5 6.9 %shard_map.161 = (f32[2]{0:T(128)}, f32[2]{0:T(128)}) custom-call(s32[6]{0:T(128)S(1)} %stack.27.where_ref, f32[2]{0:T(128)S(1)} %get-tuple-element.34.sigma_ref, bf16[2,128,512]{2,1,0:T(8,128)(2,1)S(1)} %copy-done.5, bf16[2,128,512]{2,1,0:T(8,128)(2,1)} %broadcast_select_fusion.3.refs_5_.refs_3_.refs_1_, ...), custom_call_target="tpu_custom_call" | custom-call | flops 5000000000 | bytes 10000000 | tf_op jit(solution)/shard_map/pallas_call | solution.py:300
  (98 shorter events, 10.2 us)
Async XLA Ops:
  2.2 2.1 %collective-permute-start = (bf16[2,131072]{1,0:T(2,128)(2,1)S(1)}, bf16[2,131072]{1,0:T(2,128)(2,1)S(1)}, u32[]{:S(2)}, u32[]{:S(2)}) collective-permute-start(bf16[2,131072]{1,0:T(2,128)(2,1)S(1)} %dynamic-slice_bitcast_fusion.2), channel_id=1, source_target_pairs={{0,1},{1,0},{2,3},{3,2},{4,5},{5,4},{6,7},{7,6},{8,9},{9,8},{10,11... | collective-permute-start | bytes 1572872 | tf_op jit(solution)/shard_map/ppermute | solution.py:75
  7.5 5.4 %collective-permute-start.1 = (bf16[2,131072]{1,0:T(2,128)(2,1)S(1)}, bf16[2,131072]{1,0:T(2,128)(2,1)S(1)}, u32[]{:S(2)}, u32[]{:S(2)}) collective-permute-start(bf16[2,131072]{1,0:T(2,128)(2,1)S(1)} %dynamic-slice_bitcast_fusion.1), channel_id=1, source_target_pairs={{0,1},{1,0},{2,3},{3,2},{4,5},{5,4},{6,7},{7,6},{8,9},{9,8},{10,11... | collective-permute-start | bytes 1572872 | tf_op jit(solution)/shard_map/ppermute | solution.py:75
  8.4 16.8 %collective-permute-start.10 = (bf16[2,128,512]{2,1,0:T(8,128)(2,1)S(1)}, bf16[2,128,512]{2,1,0:T(8,128)(2,1)}, u32[]{:S(2)}, u32[]{:S(2)}) collective-permute-start(bf16[2,128,512]{2,1,0:T(8,128)(2,1)S(1)} %get-tuple-element.37.refs_1_), channel_id=1, source_target_pairs={{0,4},{5,1},{4,8},{9,5},{8,12},{13,9},{12,14},{15,13},{14,10},{11,... | collective-permute-start | bytes 786440 | tf_op jit(solution)/shard_map/ppermute | solution.py:103
  11.3 16.9 %collective-permute-start.3 = (bf16[2,128,512]{2,1,0:T(8,128)(2,1)}, bf16[2,128,512]{2,1,0:T(8,128)(2,1)}, u32[]{:S(2)}, u32[]{:S(2)}) collective-permute-start(bf16[2,128,512]{2,1,0:T(8,128)(2,1)} %get-tuple-element.26.refs_0_), channel_id=1, source_target_pairs={{0,4},{5,1},{4,8},{9,5},{8,12},{13,9},{12,14},{15,13},{14,10},{11,... | collective-permute-start | bytes 786440 | tf_op jit(solution)/shard_map/ppermute | solution.py:103
  16.4 14.3 %collective-permute-start.2 = (bf16[2,131072]{1,0:T(2,128)(2,1)}, bf16[2,131072]{1,0:T(2,128)(2,1)}, u32[]{:S(2)}, u32[]{:S(2)}) collective-permute-start(bf16[2,131072]{1,0:T(2,128)(2,1)} %dynamic-slice_bitcast_fusion), channel_id=1, source_target_pairs={{0,1},{1,0},{2,3},{3,2},{4,5},{5,4},{6,7},{7,6},{8,9},{9,8},{10,11... | collective-permute-start | bytes 1572872 | tf_op jit(solution)/shard_map/ppermute | solution.py:75
  21.2 33.5 %all-to-all-start = ((bf16[16,2,32,512]{3,2,1,0:T(8,128)(2,1)}), bf16[16,2,32,512]{3,2,1,0:T(8,128)(2,1)S(1)}, u32[]{:S(2)}, u32[]{:S(2)}) async-start(bf16[16,2,32,512]{3,2,1,0:T(8,128)(2,1)} %reshape.216), calls=%async_computation | async-start | bytes 2097152 | tf_op jit(solution)/shard_map/all_to_all | solution.py:136
  26.2 56.0 %copy-start.6 = (s32[32]{0:T(128)S(1)}, s32[32]{0:T(128)}, u32[]{:S(2)}) copy-start(s32[32]{0:T(128)} %cut_ref.1) | copy-start | bytes 388
  26.2 19.9 %collective-permute-start.11 = (bf16[2,128,512]{2,1,0:T(8,128)(2,1)S(1)}, bf16[2,128,512]{2,1,0:T(8,128)(2,1)S(1)}, u32[]{:S(2)}, u32[]{:S(2)}) collective-permute-start(bf16[2,128,512]{2,1,0:T(8,128)(2,1)S(1)} %broadcast_select_fusion.4.refs_3_.refs_1_), channel_id=1, source_target_pairs={{0,4},{5,1},{4,8},{9,5},{8,12},{13,9},{12,14},{15,13},{14,10},{11,... | collective-permute-start | bytes 786440 | tf_op jit(solution)/shard_map/ppermute | solution.py:103
  29.2 24.8 %collective-permute-start.4 = (bf16[2,128,512]{2,1,0:T(8,128)(2,1)S(1)}, bf16[2,128,512]{2,1,0:T(8,128)(2,1)S(1)}, u32[]{:S(2)}, u32[]{:S(2)}) collective-permute-start(bf16[2,128,512]{2,1,0:T(8,128)(2,1)S(1)} %broadcast_select_fusion.6.refs_2_.refs_0_), channel_id=1, source_target_pairs={{0,4},{5,1},{4,8},{9,5},{8,12},{13,9},{12,14},{15,13},{14,10},{11,... | collective-permute-start | bytes 786440 | tf_op jit(solution)/shard_map/ppermute | solution.py:103
  46.8 12.0 %collective-permute-start.12 = (bf16[2,128,512]{2,1,0:T(8,128)(2,1)}, bf16[2,128,512]{2,1,0:T(8,128)(2,1)}, u32[]{:S(2)}, u32[]{:S(2)}) collective-permute-start(bf16[2,128,512]{2,1,0:T(8,128)(2,1)} %broadcast_select_fusion.3.refs_5_.refs_3_.refs_1_), channel_id=1, source_target_pairs={{0,4},{5,1},{4,8},{9,5},{8,12},{13,9},{12,14},{15,13},{14,10},{11,... | collective-permute-start | bytes 786440 | tf_op jit(solution)/shard_map/ppermute | solution.py:103
  54.7 47.9 %copy-start.5 = (bf16[2,128,512]{2,1,0:T(8,128)(2,1)S(1)}, bf16[2,128,512]{2,1,0:T(8,128)(2,1)}, u32[]{:S(2)}) copy-start(bf16[2,128,512]{2,1,0:T(8,128)(2,1)} %broadcast_select_fusion.5.refs_4_.refs_2_.refs_0_) | copy-start | bytes 786436
  54.7 47.9 %copy-start.7 = (f32[4,2,128,512]{3,2,1,0:T(8,128)S(1)}, f32[4,2,128,512]{3,2,1,0:T(8,128)}, u32[]{:S(2)}) copy-start(f32[4,2,128,512]{3,2,1,0:T(8,128)} %constant.174.clone.refs_37_) | copy-start | bytes 6291460
  54.8 47.9 %copy-start.8 = (bf16[4,512,256]{2,1,0:T(8,128)(2,1)S(1)}, bf16[4,512,256]{2,1,0:T(8,128)(2,1)}, u32[]{:S(2)}) copy-start(bf16[4,512,256]{2,1,0:T(8,128)(2,1)} %constant.179.refs_36_) | copy-start | bytes 3145732
  54.8 47.9 %copy-start.9 = (bf16[4,256,256]{2,1,0:T(8,128)(2,1)S(1)}, bf16[4,256,256]{2,1,0:T(8,128)(2,1)}, u32[]{:S(2)}) copy-start(bf16[4,256,256]{2,1,0:T(8,128)(2,1)} %constant.178.refs_35_) | copy-start | bytes 1572868
  54.8 6.7 %collective-permute-start.5 = (bf16[2,128,512]{2,1,0:T(8,128)(2,1)}, bf16[2,128,512]{2,1,0:T(8,128)(2,1)S(1)}, u32[]{:S(2)}, u32[]{:S(2)}) collective-permute-start(bf16[2,128,512]{2,1,0:T(8,128)(2,1)} %broadcast_select_fusion.5.refs_4_.refs_2_.refs_0_), channel_id=1, source_target_pairs={{0,4},{5,1},{4,8},{9,5},{8,12},{13,9},{12,14},{15,13},{14,10},{11,... | collective-permute-start | bytes 786440 | tf_op jit(solution)/shard_map/ppermute | solution.py:103
  57.3 23.6 %collective-permute-start.9 = (bf16[16,2,32,512]{3,2,1,0:T(8,128)(2,1)S(1)}, bf16[16,2,32,512]{3,2,1,0:T(8,128)(2,1)S(1)}, u32[]{:S(2)}, u32[]{:S(2)}) collective-permute-start(bf16[16,2,32,512]{3,2,1,0:T(8,128)(2,1)S(1)} %all-to-all-done.refs_0_), channel_id=1, source_target_pairs={{0,16},{16,0},{1,17},{17,1},{2,18},{18,2},{3,19},{19,3},{4,20},{20... | collective-permute-start | bytes 3145736 | tf_op jit(solution)/shard_map/ppermute | solution.py:142
  58.8 7.8 %collective-permute-start.13 = (bf16[2,128,512]{2,1,0:T(8,128)(2,1)}, bf16[2,128,512]{2,1,0:T(8,128)(2,1)S(1)}, u32[]{:S(2)}, u32[]{:S(2)}) collective-permute-start(bf16[2,128,512]{2,1,0:T(8,128)(2,1)} %collective-permute-done.12.refs_7_.refs_5_.refs_3_), channel_id=1, source_target_pairs={{0,4},{5,1},{4,8},{9,5},{8,12},{13,9},{12,14},{15,13},{14,10},{11,... | collective-permute-start | bytes 786440 | tf_op jit(solution)/shard_map/ppermute | solution.py:103
  60.9 6.6 %collective-permute-start.40 = (bf16[2,128,512]{2,1,0:T(8,128)(2,1)}, bf16[2,128,512]{2,1,0:T(8,128)(2,1)S(1)}, u32[]{:S(2)}, u32[]{:S(2)}) collective-permute-start(bf16[2,128,512]{2,1,0:T(8,128)(2,1)} %get-tuple-element.26.refs_0_), channel_id=1, source_target_pairs={{0,1},{1,0},{2,3},{3,2},{4,5},{5,4},{6,7},{7,6},{8,9},{9,8},{10,11... | collective-permute-start | bytes 786440 | tf_op jit(solution)/shard_map/ppermute | solution.py:104
  60.9 6.6 %collective-permute-start.41 = (bf16[2,128,512]{2,1,0:T(8,128)(2,1)S(1)}, bf16[2,128,512]{2,1,0:T(8,128)(2,1)S(1)}, u32[]{:S(2)}, u32[]{:S(2)}) collective-permute-start(bf16[2,128,512]{2,1,0:T(8,128)(2,1)S(1)} %get-tuple-element.37.refs_1_), channel_id=1, source_target_pairs={{0,1},{1,0},{2,3},{3,2},{4,5},{5,4},{6,7},{7,6},{8,9},{9,8},{10,11... | collective-permute-start | bytes 786440 | tf_op jit(solution)/shard_map/ppermute | solution.py:104
  61.5 7.9 %collective-permute-start.6 = (bf16[2,128,512]{2,1,0:T(8,128)(2,1)S(1)}, bf16[2,128,512]{2,1,0:T(8,128)(2,1)S(1)}, u32[]{:S(2)}, u32[]{:S(2)}) collective-permute-start(bf16[2,128,512]{2,1,0:T(8,128)(2,1)S(1)} %collective-permute-done.5.refs_6_.refs_4_.refs_2_), channel_id=1, source_target_pairs={{0,4},{5,1},{4,8},{9,5},{8,12},{13,9},{12,14},{15,13},{14,10},{11,... | collective-permute-start | bytes 786440 | tf_op jit(solution)/shard_map/ppermute | solution.py:103
  66.6 6.4 %collective-permute-start.14 = (bf16[2,128,512]{2,1,0:T(8,128)(2,1)S(1)}, bf16[2,128,512]{2,1,0:T(8,128)(2,1)S(1)}, u32[]{:S(2)}, u32[]{:S(2)}) collective-permute-start(bf16[2,128,512]{2,1,0:T(8,128)(2,1)S(1)} %collective-permute-done.13.refs_9_.refs_7_.refs_5_), channel_id=1, source_target_pairs={{0,4},{5,1},{4,8},{9,5},{8,12},{13,9},{12,14},{15,13},{14,10},{11,... | collective-permute-start | bytes 786440 | tf_op jit(solution)/shard_map/ppermute | solution.py:103
  67.5 6.4 %collective-permute-start.39 = (bf16[2,128,512]{2,1,0:T(8,128)(2,1)}, bf16[2,128,512]{2,1,0:T(8,128)(2,1)S(1)}, u32[]{:S(2)}, u32[]{:S(2)}) collective-permute-start(bf16[2,128,512]{2,1,0:T(8,128)(2,1)} %copy-done.1), channel_id=1, source_target_pairs={{0,1},{1,0},{2,3},{3,2},{4,5},{5,4},{6,7},{7,6},{8,9},{9,8},{10,11... | collective-permute-start | bytes 786440 | tf_op jit(solution)/shard_map/ppermute | solution.py:104
  67.5 6.4 %collective-permute-start.38 = (bf16[2,128,512]{2,1,0:T(8,128)(2,1)}, bf16[2,128,512]{2,1,0:T(8,128)(2,1)S(1)}, u32[]{:S(2)}, u32[]{:S(2)}) collective-permute-start(bf16[2,128,512]{2,1,0:T(8,128)(2,1)} %copy-done.3), channel_id=1, source_target_pairs={{0,1},{1,0},{2,3},{3,2},{4,5},{5,4},{6,7},{7,6},{8,9},{9,8},{10,11... | collective-permute-start | bytes 786440 | tf_op jit(solution)/shard_map/ppermute | solution.py:104
  69.4 6.4 %collective-permute-start.7 = (bf16[2,128,512]{2,1,0:T(8,128)(2,1)S(1)}, bf16[2,128,512]{2,1,0:T(8,128)(2,1)S(1)}, u32[]{:S(2)}, u32[]{:S(2)}) collective-permute-start(bf16[2,128,512]{2,1,0:T(8,128)(2,1)S(1)} %collective-permute-done.6.refs_8_.refs_6_.refs_4_), channel_id=1, source_target_pairs={{0,4},{5,1},{4,8},{9,5},{8,12},{13,9},{12,14},{15,13},{14,10},{11,... | collective-permute-start | bytes 786440 | tf_op jit(solution)/shard_map/ppermute | solution.py:103
  73.0 6.4 %collective-permute-start.15 = (bf16[2,128,512]{2,1,0:T(8,128)(2,1)S(1)}, bf16[2,128,512]{2,1,0:T(8,128)(2,1)S(1)}, u32[]{:S(2)}, u32[]{:S(2)}) collective-permute-start(bf16[2,128,512]{2,1,0:T(8,128)(2,1)S(1)} %collective-permute-done.14.refs_11_.refs_9_.refs_7_), channel_id=1, source_target_pairs={{0,4},{5,1},{4,8},{9,5},{8,12},{13,9},{12,14},{15,13},{14,10},{11,... | collective-permute-start | bytes 786440 | tf_op jit(solution)/shard_map/ppermute | solution.py:103
  73.8 6.4 %collective-permute-start.23 = (bf16[2,128,512]{2,1,0:T(8,128)(2,1)}, bf16[2,128,512]{2,1,0:T(8,128)(2,1)S(1)}, u32[]{:S(2)}, u32[]{:S(2)}) collective-permute-start(bf16[2,128,512]{2,1,0:T(8,128)(2,1)} %broadcast_select_fusion.3.refs_5_.refs_3_.refs_1_), channel_id=1, source_target_pairs={{0,1},{1,0},{2,3},{3,2},{4,5},{5,4},{6,7},{7,6},{8,9},{9,8},{10,11... | collective-permute-start | bytes 786440 | tf_op jit(solution)/shard_map/ppermute | solution.py:104
  73.8 6.4 %collective-permute-start.25 = (bf16[2,128,512]{2,1,0:T(8,128)(2,1)}, bf16[2,128,512]{2,1,0:T(8,128)(2,1)S(1)}, u32[]{:S(2)}, u32[]{:S(2)}) collective-permute-start(bf16[2,128,512]{2,1,0:T(8,128)(2,1)} %collective-permute-done.12.refs_7_.refs_5_.refs_3_), channel_id=1, source_target_pairs={{0,1},{1,0},{2,3},{3,2},{4,5},{5,4},{6,7},{7,6},{8,9},{9,8},{10,11... | collective-permute-start | bytes 786440 | tf_op jit(solution)/shard_map/ppermute | solution.py:104
  75.8 6.4 %collective-permute-start.8 = (bf16[2,128,512]{2,1,0:T(8,128)(2,1)S(1)}, bf16[2,128,512]{2,1,0:T(8,128)(2,1)S(1)}, u32[]{:S(2)}, u32[]{:S(2)}) collective-permute-start(bf16[2,128,512]{2,1,0:T(8,128)(2,1)S(1)} %collective-permute-done.7.refs_10_.refs_8_.refs_6_), channel_id=1, source_target_pairs={{0,4},{5,1},{4,8},{9,5},{8,12},{13,9},{12,14},{15,13},{14,10},{11,... | collective-permute-start | bytes 786440 | tf_op jit(solution)/shard_map/ppermute | solution.py:103
  79.3 6.4 %collective-permute-start.17 = (bf16[2,128,512]{2,1,0:T(8,128)(2,1)S(1)}, bf16[2,128,512]{2,1,0:T(8,128)(2,1)S(1)}, u32[]{:S(2)}, u32[]{:S(2)}) collective-permute-start(bf16[2,128,512]{2,1,0:T(8,128)(2,1)S(1)} %collective-permute-done.15.refs_13_.refs_11_.refs_9_), channel_id=1, source_target_pairs={{0,4},{5,1},{4,8},{9,5},{8,12},{13,9},{12,14},{15,13},{14,10},{11,... | collective-permute-start | bytes 786440 | tf_op jit(solution)/shard_map/ppermute | solution.py:103
  80.2 6.9 %collective-permute-start.27 = (bf16[2,128,512]{2,1,0:T(8,128)(2,1)S(1)}, bf16[2,128,512]{2,1,0:T(8,128)(2,1)S(1)}, u32[]{:S(2)}, u32[]{:S(2)}) collective-permute-start(bf16[2,128,512]{2,1,0:T(8,128)(2,1)S(1)} %collective-permute-done.13.refs_9_.refs_7_.refs_5_), channel_id=1, source_target_pairs={{0,1},{1,0},{2,3},{3,2},{4,5},{5,4},{6,7},{7,6},{8,9},{9,8},{10,11... | collective-permute-start | bytes 786440 | tf_op jit(solution)/shard_map/ppermute | solution.py:104
  80.2 6.9 %collective-permute-start.29 = (bf16[2,128,512]{2,1,0:T(8,128)(2,1)S(1)}, bf16[2,128,512]{2,1,0:T(8,128)(2,1)S(1)}, u32[]{:S(2)}, u32[]{:S(2)}) collective-permute-start(bf16[2,128,512]{2,1,0:T(8,128)(2,1)S(1)} %collective-permute-done.14.refs_11_.refs_9_.refs_7_), channel_id=1, source_target_pairs={{0,1},{1,0},{2,3},{3,2},{4,5},{5,4},{6,7},{7,6},{8,9},{9,8},{10,11... | collective-permute-start | bytes 786440 | tf_op jit(solution)/shard_map/ppermute | solution.py:104
  81.0 7.9 %collective-permute-start.22 = (bf16[2,128,512]{2,1,0:T(8,128)(2,1)}, bf16[2,128,512]{2,1,0:T(8,128)(2,1)S(1)}, u32[]{:S(2)}, u32[]{:S(2)}) collective-permute-start(bf16[2,128,512]{2,1,0:T(8,128)(2,1)} %broadcast_select_fusion.5.refs_4_.refs_2_.refs_0_), channel_id=1, source_target_pairs={{0,1},{1,0},{2,3},{3,2},{4,5},{5,4},{6,7},{7,6},{8,9},{9,8},{10,11... | collective-permute-start | bytes 786440 | tf_op jit(solution)/shard_map/ppermute | solution.py:104
  82.1 6.8 %collective-permute-start.31 = (bf16[2,128,512]{2,1,0:T(8,128)(2,1)S(1)}, bf16[2,128,512]{2,1,0:T(8,128)(2,1)S(1)}, u32[]{:S(2)}, u32[]{:S(2)}) collective-permute-start(bf16[2,128,512]{2,1,0:T(8,128)(2,1)S(1)} %collective-permute-done.15.refs_13_.refs_11_.refs_9_), channel_id=1, source_target_pairs={{0,1},{1,0},{2,3},{3,2},{4,5},{5,4},{6,7},{7,6},{8,9},{9,8},{10,11... | collective-permute-start | bytes 786440 | tf_op jit(solution)/shard_map/ppermute | solution.py:104
  85.7 6.4 %collective-permute-start.19 = (bf16[2,128,512]{2,1,0:T(8,128)(2,1)S(1)}, bf16[2,128,512]{2,1,0:T(8,128)(2,1)S(1)}, u32[]{:S(2)}, u32[]{:S(2)}) collective-permute-start(bf16[2,128,512]{2,1,0:T(8,128)(2,1)S(1)} %collective-permute-done.17.refs_15_.refs_13_.refs_11_), channel_id=1, source_target_pairs={{0,4},{5,1},{4,8},{9,5},{8,12},{13,9},{12,14},{15,13},{14,10},{11,... | collective-permute-start | bytes 786440 | tf_op jit(solution)/shard_map/ppermute | solution.py:103
  87.1 6.4 %collective-permute-start.24 = (bf16[2,128,512]{2,1,0:T(8,128)(2,1)S(1)}, bf16[2,128,512]{2,1,0:T(8,128)(2,1)S(1)}, u32[]{:S(2)}, u32[]{:S(2)}) collective-permute-start(bf16[2,128,512]{2,1,0:T(8,128)(2,1)S(1)} %collective-permute-done.5.refs_6_.refs_4_.refs_2_), channel_id=1, source_target_pairs={{0,1},{1,0},{2,3},{3,2},{4,5},{5,4},{6,7},{7,6},{8,9},{9,8},{10,11... | collective-permute-start | bytes 786440 | tf_op jit(solution)/shard_map/ppermute | solution.py:104
  87.1 7.8 %collective-permute-start.16 = (bf16[2,128,512]{2,1,0:T(8,128)(2,1)S(1)}, bf16[2,128,512]{2,1,0:T(8,128)(2,1)S(1)}, u32[]{:S(2)}, u32[]{:S(2)}) collective-permute-start(bf16[2,128,512]{2,1,0:T(8,128)(2,1)S(1)} %collective-permute-done.8.refs_12_.refs_10_.refs_8_), channel_id=1, source_target_pairs={{0,4},{5,1},{4,8},{9,5},{8,12},{13,9},{12,14},{15,13},{14,10},{11,... | collective-permute-start | bytes 786440 | tf_op jit(solution)/shard_map/ppermute | solution.py:103
  88.9 7.4 %collective-permute-start.33 = (bf16[2,128,512]{2,1,0:T(8,128)(2,1)S(1)}, bf16[2,128,512]{2,1,0:T(8,128)(2,1)S(1)}, u32[]{:S(2)}, u32[]{:S(2)}) collective-permute-start(bf16[2,128,512]{2,1,0:T(8,128)(2,1)S(1)} %collective-permute-done.17.refs_15_.refs_13_.refs_11_), channel_id=1, source_target_pairs={{0,1},{1,0},{2,3},{3,2},{4,5},{5,4},{6,7},{7,6},{8,9},{9,8},{10,11... | collective-permute-start | bytes 786440 | tf_op jit(solution)/shard_map/ppermute | solution.py:104
  88.9 7.4 %collective-permute-start.26 = (bf16[2,128,512]{2,1,0:T(8,128)(2,1)S(1)}, bf16[2,128,512]{2,1,0:T(8,128)(2,1)S(1)}, u32[]{:S(2)}, u32[]{:S(2)}) collective-permute-start(bf16[2,128,512]{2,1,0:T(8,128)(2,1)S(1)} %collective-permute-done.6.refs_8_.refs_6_.refs_4_), channel_id=1, source_target_pairs={{0,1},{1,0},{2,3},{3,2},{4,5},{5,4},{6,7},{7,6},{8,9},{9,8},{10,11... | collective-permute-start | bytes 786440 | tf_op jit(solution)/shard_map/ppermute | solution.py:104
  92.1 6.4 %collective-permute-start.21 = (bf16[2,128,512]{2,1,0:T(8,128)(2,1)S(1)}, bf16[2,128,512]{2,1,0:T(8,128)(2,1)S(1)}, u32[]{:S(2)}, u32[]{:S(2)}) collective-permute-start(bf16[2,128,512]{2,1,0:T(8,128)(2,1)S(1)} %collective-permute-done.19.refs_15_.refs_13_), channel_id=1, source_target_pairs={{0,4},{5,1},{4,8},{9,5},{8,12},{13,9},{12,14},{15,13},{14,10},{11,... | collective-permute-start | bytes 786440 | tf_op jit(solution)/shard_map/ppermute | solution.py:103
  93.4 5.0 %collective-permute-start.28 = (bf16[2,128,512]{2,1,0:T(8,128)(2,1)S(1)}, bf16[2,128,512]{2,1,0:T(8,128)(2,1)S(1)}, u32[]{:S(2)}, u32[]{:S(2)}) collective-permute-start(bf16[2,128,512]{2,1,0:T(8,128)(2,1)S(1)} %collective-permute-done.7.refs_10_.refs_8_.refs_6_), channel_id=1, source_target_pairs={{0,1},{1,0},{2,3},{3,2},{4,5},{5,4},{6,7},{7,6},{8,9},{9,8},{10,11... | collective-permute-start | bytes 786440 | tf_op jit(solution)/shard_map/ppermute | solution.py:104
  94.9 6.4 %collective-permute-start.18 = (bf16[2,128,512]{2,1,0:T(8,128)(2,1)S(1)}, bf16[2,128,512]{2,1,0:T(8,128)(2,1)S(1)}, u32[]{:S(2)}, u32[]{:S(2)}) collective-permute-start(bf16[2,128,512]{2,1,0:T(8,128)(2,1)S(1)} %collective-permute-done.16.refs_14_.refs_12_.refs_10_), channel_id=1, source_target_pairs={{0,4},{5,1},{4,8},{9,5},{8,12},{13,9},{12,14},{15,13},{14,10},{11,... | collective-permute-start | bytes 786440 | tf_op jit(solution)/shard_map/ppermute | solution.py:103
  96.3 5.0 %collective-permute-start.30 = (bf16[2,128,512]{2,1,0:T(8,128)(2,1)S(1)}, bf16[2,128,512]{2,1,0:T(8,128)(2,1)S(1)}, u32[]{:S(2)}, u32[]{:S(2)}) collective-permute-start(bf16[2,128,512]{2,1,0:T(8,128)(2,1)S(1)} %collective-permute-done.8.refs_12_.refs_10_.refs_8_), channel_id=1, source_target_pairs={{0,1},{1,0},{2,3},{3,2},{4,5},{5,4},{6,7},{7,6},{8,9},{9,8},{10,11... | collective-permute-start | bytes 786440 | tf_op jit(solution)/shard_map/ppermute | solution.py:104
  96.3 6.4 %collective-permute-start.32 = (bf16[2,128,512]{2,1,0:T(8,128)(2,1)S(1)}, bf16[2,128,512]{2,1,0:T(8,128)(2,1)S(1)}, u32[]{:S(2)}, u32[]{:S(2)}) collective-permute-start(bf16[2,128,512]{2,1,0:T(8,128)(2,1)S(1)} %collective-permute-done.16.refs_14_.refs_12_.refs_10_), channel_id=1, source_target_pairs={{0,1},{1,0},{2,3},{3,2},{4,5},{5,4},{6,7},{7,6},{8,9},{9,8},{10,11... | collective-permute-start | bytes 786440 | tf_op jit(solution)/shard_map/ppermute | solution.py:104
  98.5 11.4 %collective-permute-start.35 = (bf16[2,128,512]{2,1,0:T(8,128)(2,1)S(1)}, bf16[2,128,512]{2,1,0:T(8,128)(2,1)S(1)}, u32[]{:S(2)}, u32[]{:S(2)}) collective-permute-start(bf16[2,128,512]{2,1,0:T(8,128)(2,1)S(1)} %collective-permute-done.19.refs_15_.refs_13_), channel_id=1, source_target_pairs={{0,1},{1,0},{2,3},{3,2},{4,5},{5,4},{6,7},{7,6},{8,9},{9,8},{10,11... | collective-permute-start | bytes 786440 | tf_op jit(solution)/shard_map/ppermute | solution.py:104
  98.5 17.0 %collective-permute-start.37 = (bf16[2,128,512]{2,1,0:T(8,128)(2,1)S(1)}, bf16[2,128,512]{2,1,0:T(8,128)(2,1)S(1)}, u32[]{:S(2)}, u32[]{:S(2)}) collective-permute-start(bf16[2,128,512]{2,1,0:T(8,128)(2,1)S(1)} %collective-permute-done.21.refs_15_), channel_id=1, source_target_pairs={{0,1},{1,0},{2,3},{3,2},{4,5},{5,4},{6,7},{7,6},{8,9},{9,8},{10,11... | collective-permute-start | bytes 786440 | tf_op jit(solution)/shard_map/ppermute | solution.py:104
  101.3 8.6 %collective-permute-start.34 = (bf16[2,128,512]{2,1,0:T(8,128)(2,1)S(1)}, bf16[2,128,512]{2,1,0:T(8,128)(2,1)S(1)}, u32[]{:S(2)}, u32[]{:S(2)}) collective-permute-start(bf16[2,128,512]{2,1,0:T(8,128)(2,1)S(1)} %collective-permute-done.18.refs_14_.refs_12_), channel_id=1, source_target_pairs={{0,1},{1,0},{2,3},{3,2},{4,5},{5,4},{6,7},{7,6},{8,9},{9,8},{10,11... | collective-permute-start | bytes 786440 | tf_op jit(solution)/shard_map/ppermute | solution.py:104
  101.3 7.6 %collective-permute-start.20 = (bf16[2,128,512]{2,1,0:T(8,128)(2,1)S(1)}, bf16[2,128,512]{2,1,0:T(8,128)(2,1)S(1)}, u32[]{:S(2)}, u32[]{:S(2)}) collective-permute-start(bf16[2,128,512]{2,1,0:T(8,128)(2,1)S(1)} %collective-permute-done.18.refs_14_.refs_12_), channel_id=1, source_target_pairs={{0,4},{5,1},{4,8},{9,5},{8,12},{13,9},{12,14},{15,13},{14,10},{11,... | collective-permute-start | bytes 786440 | tf_op jit(solution)/shard_map/ppermute | solution.py:103
  108.9 6.5 %collective-permute-start.36 = (bf16[2,128,512]{2,1,0:T(8,128)(2,1)S(1)}, bf16[2,128,512]{2,1,0:T(8,128)(2,1)S(1)}, u32[]{:S(2)}, u32[]{:S(2)}) collective-permute-start(bf16[2,128,512]{2,1,0:T(8,128)(2,1)S(1)} %collective-permute-done.20.refs_14_), channel_id=1, source_target_pairs={{0,1},{1,0},{2,3},{3,2},{4,5},{5,4},{6,7},{7,6},{8,9},{9,8},{10,11... | collective-permute-start | bytes 786440 | tf_op jit(solution)/shard_map/ppermute | solution.py:104
  (8 other events, 182.9 us)

commit v8 on v7

--- a/solution.py
+++ b/solution.py
@@ -15,12 +15,12 @@
 PART = 128
 ROW_STEP = 16
 WAVE_ROWS = 32
-SEND_ROWS = 32
 CORES = 2
 HALF_CHUNKS = 2
 LAG = 2
-TEMPLATE_SLOT = 4
-MASKED_SLOT = 12
+LINES = 4
+QUAD = 4
+STAGE_SLOTS = (6, 9, 14)
 VMEM_LIMIT = 24 * 1024 * 1024
 
 
@@ -63,8 +63,8 @@
     return list(range(0, chips, 2)) + list(range(chips - 1 - chips % 2, 0, -2))
 
 
-def to_partner():
-    return [(i, i ^ 1) for i in range(lax.axis_size("tpl"))]
+def swap(block, flip):
+    return lax.ppermute(block, "tpl", [(at, at ^ flip) for at in range(lax.axis_size("tpl"))])
 
 
 def half_chunks(strain_slots, det, owner):
@@ -72,7 +72,7 @@
     half = ROWS * COLS // CORES
     bins = half // HALF_CHUNKS
     side = lambda which: lax.dynamic_slice(strain_slots, (0, det, 0, which * half), (1, 1, 2, half))[0, 0]
-    got = lax.ppermute(side(1 - core), "tpl", to_partner())
+    got = swap(side(1 - core), 1)
     first = jnp.where(core == owner % CORES, side(core), got)
     return [first[:, at : at + bins].reshape(2, bins // COLS, COLS) for at in range(0, half, bins)]
 
@@ -87,7 +87,7 @@
     for at in range(chips):
         along.append((order[at] * CORES, order[(at + 1) % chips] * CORES))
         along.append((order[(at + 1) % chips] * CORES + 1, order[at] * CORES + 1))
-    sent, arrived = [], []
+    sent, shared, arrived = [], [], []
     count = len(chunks)
     for slot in range(count + LAG * (chips - 1)):
         if slot < LAG:
@@ -97,11 +97,11 @@
         else:
             here = arrived[slot - LAG]
         if slot in hooks:
-            here = hooks[slot](here)
+            here = hooks[slot](here, sent, shared)
         sent.append(here)
+        shared.append(swap(here, 1))
         if slot < count + LAG * (chips - 2):
             arrived.append(lax.ppermute(here, "tpl", along))
-    shared = [lax.ppermute(here, "tpl", to_partner()) for here in sent]
     return sent, shared
 
 
@@ -114,41 +114,40 @@
     return jnp.where(core == 0, forward, backward), jnp.where(core == 0, backward, forward)
 
 
-def pick(templates, lists):
+def pick_direct(templates, lists):
+    me, group = lax.axis_index("tpl"), lax.axis_index("grp")
+    ids = lax.dynamic_index_in_dim(lists, group, 1, keepdims=False)[me ^ jnp.arange(LINES * QUAD)]
+    return templates[ids].reshape(LINES, QUAD, 2, WAVE_ROWS, COLS)
+
+
+def between_lines(picked):
+    return [picked[0]] + [swap(picked[flip], flip * QUAD) for flip in range(1, LINES)]
+
+
+def inside_quad(lines):
+    blocks = [jnp.stack([line[flip] for line in lines]) for flip in range(QUAD)]
+    return [blocks[0]] + [swap(blocks[flip], flip) for flip in range(1, QUAD)]
+
+
+def across(block, turn):
+    groups = lax.axis_size("grp")
+    return lax.ppermute(block, "grp", [(at, (at + turn) % groups) for at in range(groups)]) if turn else block
+
+
+def collect_plain(templates, lists):
     devices, groups = lax.axis_size("tpl"), lax.axis_size("grp")
     own_group = lax.axis_index("grp")
     per_device = lists.shape[1]
-    rows = templates.shape[2] // COLS
     pieces = per_device * 2
     if pieces % groups:
-        groups, own_group = 1, jnp.int32(0)
+        groups, own_group = 1, 0
     size = pieces // groups
-    if size == 2 and rows == WAVE_ROWS:
-        picked = templates[lax.dynamic_index_in_dim(lists, own_group, 1, keepdims=False)]
-        picked = picked.reshape(devices, size, rows, COLS)
-        parts = [picked[:, :, at : at + SEND_ROWS] for at in range(0, rows, SEND_ROWS)]
-        return parts, [(own_group - turn) % groups for turn in range(groups)]
-    picked = templates[lists.reshape(-1)].reshape(devices, pieces, rows, COLS)
-    return [lax.dynamic_slice_in_dim(picked, own_group * size, size, 1)], None
-
-
-def exchange(block):
-    return lax.all_to_all(block, "tpl", split_axis=0, concat_axis=0, tiled=True)
-
-
-def across(own):
-    groups = lax.axis_size("grp")
-    return [own] + [
-        lax.ppermute(own, "grp", [(at, (at + turn) % groups) for at in range(groups)]) for turn in range(1, groups)
-    ]
-
-
-def assemble(own, per_device):
-    groups = lax.axis_size("grp")
-    found = jnp.stack(across(own) if per_device * 2 % groups == 0 else [own])
-    found = found[(lax.axis_index("grp") - jnp.arange(found.shape[0])) % found.shape[0]]
+    picked = templates[lists.reshape(-1)].reshape(devices, pieces, templates.shape[2] // COLS, COLS)
+    picked = lax.dynamic_slice_in_dim(picked, own_group * size, size, 1)
+    own = lax.all_to_all(picked, "tpl", split_axis=0, concat_axis=0, tiled=True)
+    found = jnp.stack([across(own, turn) for turn in range(groups)])[(own_group - jnp.arange(groups)) % groups]
     found = found.transpose(0, 2, 1, 3, 4).reshape(per_device, 2, ROWS // WAVE_ROWS, WAVE_ROWS, COLS)
-    return [[found[at].transpose(1, 0, 2, 3)] for at in range(per_device)]
+    return [found[at].transpose(1, 0, 2, 3) for at in range(per_device)]
 
 
 def quarters(parts):
@@ -166,20 +165,20 @@
 def prepare_kernel(count, cut_ref, list_ref, where_ref, *refs):
     piece_refs, (masked_ref, sigma_ref) = refs[:-2], refs[-2:]
     pieces = len(piece_refs) // count
-    rows = WAVE_ROWS // pieces
+    flips = where_ref[4]
     for tpl in range(count):
-        cutoff = cut_ref[list_ref[where_ref[2] * count + where_ref[4 + tpl]]]
+        cutoff = cut_ref[list_ref[where_ref[2] * count + where_ref[5 + tpl]]]
         total = jnp.zeros((8, COLS), jnp.float32)
         for piece in range(pieces):
             wave_ref = piece_refs[tpl * pieces + piece]
-            for block in range(ROWS // WAVE_ROWS):
-                start = block * WAVE_ROWS + piece * rows
-                bins = (lax.broadcasted_iota(jnp.int32, (rows, COLS), 0) + start) * COLS
-                inside = bins + lax.broadcasted_iota(jnp.int32, (rows, COLS), 1) < cutoff
+            for block in range(ROWS // WAVE_ROWS // pieces):
+                start = pl.multiple_of((flips ^ (block * pieces + piece)) * WAVE_ROWS, WAVE_ROWS)
+                bins = (lax.broadcasted_iota(jnp.int32, (WAVE_ROWS, COLS), 0) + start) * COLS
+                inside = bins + lax.broadcasted_iota(jnp.int32, (WAVE_ROWS, COLS), 1) < cutoff
                 wave_re = jnp.where(inside, wave_ref[block, 0].astype(jnp.float32), 0.0)
                 wave_im = jnp.where(inside, wave_ref[block, 1].astype(jnp.float32), 0.0)
-                masked_ref[tpl, 0, start : start + rows, :] = wave_re.astype(jnp.bfloat16)
-                masked_ref[tpl, 1, start : start + rows, :] = wave_im.astype(jnp.bfloat16)
+                masked_ref[tpl, 0, pl.ds(start, WAVE_ROWS), :] = wave_re.astype(jnp.bfloat16)
+                masked_ref[tpl, 1, pl.ds(start, WAVE_ROWS), :] = wave_im.astype(jnp.bfloat16)
                 squares = wave_re * wave_re + wave_im * wave_im
                 total = total + jnp.sum(squares.reshape(-1, 8, COLS), axis=0)
         sigma_ref[tpl] = jnp.sum(total)
@@ -264,7 +263,7 @@
 
     if last:
         for tpl in range(count):
-            place = where_ref[4 + tpl]
+            place = where_ref[5 + tpl]
             outputs[0][place] = jnp.max(largest[tpl]) / (2.0 * (sigma_ref[tpl] + eps_norm))
             outputs[1][place] = sigma_ref[tpl] / (ROWS * COLS)
 
@@ -317,41 +316,65 @@
 
 def body(strain_slots, templates, cutoffs, lists, owner, slides):
     me, owner = lax.axis_index("tpl"), owner[0]
-    chips = lax.axis_size("tpl") // CORES
+    devices, groups = lax.axis_size("tpl"), lax.axis_size("grp")
+    chips = devices // CORES
     per_device = lists.shape[1]
+    direct = per_device == groups and devices == LINES * QUAD and templates.shape[2] == WAVE_ROWS * COLS
+    places = [(lax.axis_index("grp") - turn) % groups if direct else turn for turn in range(per_device)]
+
     chunks = half_chunks(strain_slots, 0, owner)
     strain_slots, templates, chunks = lax.optimization_barrier((strain_slots, templates, chunks))
-    parts, places = pick(templates, lists)
-    ids = list(range(per_device)) if places is None else places
+    picked = pick_direct(templates, lists) if direct else collect_plain(templates, lists)
     near, far = distances(owner)
-    where = jnp.stack([jnp.asarray(at, jnp.int32) for at in (me % CORES, near, me, far, *ids)])
+    numbers = (me % CORES, near, me, far, me if direct else 0, *places)
+    where = jnp.stack([jnp.asarray(at, jnp.int32) for at in numbers])
+    small = (*slide_turns(slides), where, lists.reshape(-1))
     for det in range(1, DET):
         more = half_chunks(strain_slots, det, owner)
         strain_slots, more = lax.optimization_barrier((strain_slots, more))
         chunks += more
-    held = {"arrived": exchange(parts[0]), "small": (slide_turns(slides), where, lists.reshape(-1))}
-
-    def templates_here(chunk):
-        chunk, held["arrived"], held["small"] = lax.optimization_barrier((chunk, held["arrived"], held["small"]))
-        if places is None:
-            waves = assemble(held["arrived"], per_device)
-        else:
-            waves = [[wave] for wave in across(held["arrived"])]
-        _, where, flat_list = held["small"]
+
+    held = {"small": small, "lines": between_lines(picked) if direct else picked, "result": ()}
+
+    def tie(name, chunk):
+        chunk, held[name] = lax.optimization_barrier((chunk, held[name]))
+        return chunk
+
+    def after_lines(chunk, sent, shared):
+        chunk = tie("small", tie("lines", chunk))
+        held["blocks"] = inside_quad(held["lines"]) if direct else held["lines"]
+        return chunk
+
+    def after_blocks(chunk, sent, shared):
+        chunk = tie("blocks", chunk)
+        waves = [[across(block, turn) for block in held["blocks"]] for turn in range(per_device)]
+        if not direct:
+            waves = [[block] for block in held["blocks"]]
+        *_, where, flat_list = held["small"]
         held["masked"] = prepare(cutoffs, flat_list, where, waves)
         return chunk
 
-    def masked_here(chunk):
-        chunk, held["masked"] = lax.optimization_barrier((chunk, held["masked"]))
-        return chunk
-
-    sent, shared = spread(chunks, owner, {TEMPLATE_SLOT: templates_here, MASKED_SLOT: masked_here})
-    turns, where, _ = held["small"]
-    masked, sigma = held["masked"]
-    result = ()
-    for det in range(DET):
-        result = detector(det, chips, where, sigma, sent, shared, masked, turns, result)
-    return result
+    def after_masked(chunk, sent, shared):
+        return tie("masked", chunk)
+
+    def filtered(det, sent, shared):
+        *turns, where, _ = held["small"]
+        masked, sigma = held["masked"]
+        held["result"] = detector(det, chips, where, sigma, sent, shared, masked, turns, held["result"])
+
+    def after_detector(det):
+        def hook(chunk, sent, shared):
+            filtered(det, sent, shared)
+            return tie("result", chunk)
+
+        return hook
+
+    hooks = dict(zip(STAGE_SLOTS, (after_lines, after_blocks, after_masked)))
+    for det in range(DET - 1):
+        hooks[(det + 1) * HALF_CHUNKS - 1 + LAG * chips] = after_detector(det)
+    sent, shared = spread(chunks, owner, hooks)
+    filtered(DET - 1, sent, shared)
+    return tuple(held["result"])
 
 
 def solution(mesh):

time: 123 us -> 147 us (1.20)
  local copies, waits for them, and re-layouts: 11.2 us -> 24.3 us
  waiting for transfers between devices: 35.5 us -> 45.8 us
    ppermute x24 -> x33, waiting for transfers between devices: 0.33 us -> 24 us  [the longest x4 14.9 us: across(): lax.ppermute(block, 'grp', [(at, (at + turn) % groups) for at in range(gr...]
    ppermute x18, waiting for transfers between devices: 35.1 us -> 21.8 us  [spread(): arrived.append(lax.ppermute(here, 'tpl', along))]
    ppermute x24 -> x33, starting transfers between devices: 6.88 us -> 18 us  [the longest x29 13 us: swap(): lax.ppermute(block, 'tpl', [(at, at ^ flip) for at in range(lax.axis_size...]
    ppermute x18, starting transfers between devices: 33.6 us -> 26.5 us  [spread(): arrived.append(lax.ppermute(here, 'tpl', along))]
    squeeze x0 -> x5, local copies, waits for them, and re-layouts: none -> 7.01 us  [the longest x3 4.48 us: between_lines(): picked[flip]]
    slice x0 -> x5, local copies, waits for them, and re-layouts: none -> 5.36 us  [the longest x4 3.82 us: inside_quad(): blocks = [jnp.stack([line[flip] for line in lines]) for flip in range(QUAD)]]
    all_to_all x1 -> x0, starting transfers between devices: 3.91 us -> none  [exchange(): return lax.all_to_all(block, 'tpl', split_axis=0, concat_axis=0, tiled=True)]
    squeeze x3, local copies, waits for them, and re-layouts: 3.07 us -> 5.18 us  [half_chunks(): lax.dynamic_slice(strain_slots, (0, det, 0, which * half), (1, 1, 2, half))]
  transfers between devices with their start and end apart: 43 -> 51, of which waited for: 14 -> 15; matrix products, arithmetic and copies ran while one was open for 12% -> 19% of each run, Pallas kernels for 11% -> 10%
where the time goes in v8:
time: 147 us; the launch traced here: 146 us
  waiting for transfers between devices  45.8 us (31%)
  starting transfers between devices  44.4 us (30%)
  local copies, waits for them, and re-layouts  24.3 us (17%)
  Pallas kernels  20.9 us (14%)
  other arithmetic  8.88 us (6%)
  between operations  2.08 us (1%)
    ppermute x18, starting transfers between devices, spread(): arrived.append(lax.ppermute(here, 'tpl', along))  26.5 us
    ppermute x18, waiting for transfers between devices, spread(): arrived.append(lax.ppermute(here, 'tpl', along))  21.8 us
    pallas_call x3, Pallas kernels, detector(): pl.pallas_call(functools.partial(detector_kernel, det, chips), out_shape=...  18.8 us
    ppermute x4, waiting for transfers between devices, across(): lax.ppermute(block, 'grp', [(at, (at + turn) % groups) for at in range(gr...  14.9 us
    ppermute x29, starting transfers between devices, swap(): lax.ppermute(block, 'tpl', [(at, at ^ flip) for at in range(lax.axis_size...  13 us
    ppermute x29, waiting for transfers between devices, swap(): lax.ppermute(block, 'tpl', [(at, at ^ flip) for at in range(lax.axis_size...  9.11 us
    squeeze x3, local copies, waits for them, and re-layouts, half_chunks(): lax.dynamic_slice(strain_slots, (0, det, 0, which * half), (1, 1, 2, half))  5.18 us
    select_n x3, other arithmetic, half_chunks(): first = jnp.where(core == owner % CORES, side(core), got)  5.18 us
  transfers between devices with their start and end apart: 51, of which 15 were waited for; matrix products, arithmetic and copies ran while one was open for 19% of the time, Pallas kernels for 10%

profile of v8, /device:TPU:0, one launch (start us, length us, event | category | flops | bytes accessed | tf_op | source)
XLA Modules:
  0.0 146.4 jit_solution(1170034233883490829)
XLA Ops:
  0.7 1.6 %dynamic-slice_bitcast_fusion.2 = bf16[2,131072]{1,0:T(2,128)(2,1)S(1)} fusion(bf16[1,3,2,262144]{3,2,1,0:T(2,128)(2,1)} %param.15, s32[]{:T(128)S(6)} %select_n.202), kind=kLoop, calls=%fused_computation.7 | loop fusion | bytes 1048580 | tf_op jit(solution)/shard_map/squeeze | solution.py:74
  4.8 1.9 %broadcast_select_fusion.2 = bf16[2,131072]{1,0:T(2,128)(2,1)S(1)} fusion(bf16[2,131072]{1,0:T(2,128)(2,1)S(1)} %collective-permute-done, pred[]{:T(512)S(6)} %eq.43, bf16[1,3,2,262144]{3,2,1,0:T(2,128)(2,1)} %param.15, s32[]{:T(128)S(6)} %select_n.201), kind=kLoop, calls=%fused_computation.4 | loop fusion | flops 262144 | bytes 1572869 | tf_op jit(solution)/shard_map/jit(_where)/select_n | solution.py:76
  7.2 1.4 dynamic-slice_bitcast_fusion.1
  9.0 3.1 %collective-permute-start.3 = (bf16[2,128,512]{2,1,0:T(8,128)(2,1)S(1)}, bf16[2,128,512]{2,1,0:T(8,128)(2,1)}, u32[]{:S(2)}, u32[]{:S(2)}) collective-permute-start(bf16[2,128,512]{2,1,0:T(8,128)(2,1)S(1)} %get-tuple-element.39.refs_0_), channel_id=1, source_target_pairs={{0,4},{5,1},{4,8},{9,5},{8,12},{13,9},{12,14},{15,13},{14,10},{11,... | collective-permute-start | bytes 786440 | tf_op jit(solution)/shard_map/ppermute | solution.py:104
  12.1 1.6 %collective-permute-start.13 = (bf16[2,128,512]{2,1,0:T(8,128)(2,1)S(1)}, bf16[2,128,512]{2,1,0:T(8,128)(2,1)}, u32[]{:S(2)}, u32[]{:S(2)}) collective-permute-start(bf16[2,128,512]{2,1,0:T(8,128)(2,1)S(1)} %get-tuple-element.47.refs_1_), channel_id=1, source_target_pairs={{0,4},{5,1},{4,8},{9,5},{8,12},{13,9},{12,14},{15,13},{14,10},{11,... | collective-permute-start | bytes 786440 | tf_op jit(solution)/shard_map/ppermute | solution.py:104
  13.7 3.6 %gather_fusion.1 = bf16[16,2,16384]{2,1,0:T(2,128)(2,1)} fusion(bf16[32,2,16384]{2,1,0:T(2,128)(2,1)S(1)} %copy-done, s32[1024]{0:T(1024)S(1)} %pad_clamp_fusion), kind=kCustom, calls=%fused_computation.1 | custom fusion | bytes 2097216 | tf_op jit(solution)/shard_map/gather | solution.py:120
  17.3 1.7 %broadcast_select_fusion.1 = bf16[2,131072]{1,0:T(2,128)(2,1)S(1)} fusion(bf16[2,131072]{1,0:T(2,128)(2,1)} %collective-permute-done.1, pred[]{:T(512)S(6)} %eq.43, bf16[1,3,2,262144]{3,2,1,0:T(2,128)(2,1)} %param.15, s32[]{:T(128)S(6)} %select_n.201), kind=kLoop, calls=%fused_computation.3 | loop fusion | flops 262144 | bytes 1572869 | tf_op jit(solution)/shard_map/jit(_where)/select_n | solution.py:76
  19.4 2.2 %dynamic-slice_bitcast_fusion = bf16[2,131072]{1,0:T(2,128)(2,1)} fusion(bf16[1,3,2,262144]{3,2,1,0:T(2,128)(2,1)} %param.15, s32[]{:T(128)S(6)} %select_n.202), kind=kLoop, calls=%fused_computation.5 | loop fusion | bytes 1048580 | tf_op jit(solution)/shard_map/squeeze | solution.py:74
  21.7 1.5 %fusion.14 = (bf16[4,2,16384]{2,1,0:T(2,128)(2,1)S(1)}, bf16[4,2,16384]{2,1,0:T(2,128)(2,1)}, bf16[4,2,16384]{2,1,0:T(2,128)(2,1)}, bf16[4,2,16384]{2,1,0:T(2,128)(2,1)}) fusion(bf16[16,2,16384]{2,1,0:T(2,128)(2,1)S(1)} %copy-done.5), kind=kLoop, calls=%fused_computation.50 | loop fusion | bytes 2097152 | tf_op jit(solution)/shard_map/slice | solution.py:124
  23.2 1.8 %squeeze.46 = bf16[4,2,32,512]{3,2,1,0:T(8,128)(2,1)} reshape(bf16[4,2,16384]{2,1,0:T(2,128)(2,1)} %get-tuple-element.70) | data formatting | bytes 524288 | tf_op jit(solution)/shard_map/squeeze | solution.py:124
  25.0 1.6 %collective-permute-start.6 = (bf16[4,2,32,512]{3,2,1,0:T(8,128)(2,1)}, bf16[4,2,32,512]{3,2,1,0:T(8,128)(2,1)}, u32[]{:S(2)}, u32[]{:S(2)}) collective-permute-start(bf16[4,2,32,512]{3,2,1,0:T(8,128)(2,1)} %squeeze.46), channel_id=1, source_target_pairs={{0,4},{1,5},{2,6},{3,7},{4,0},{5,1},{6,2},{7,3},{8,12},{9,13},{10,... | collective-permute-start | bytes 786440 | tf_op jit(solution)/shard_map/ppermute | solution.py:67
  26.6 1.8 %squeeze.47 = bf16[4,2,32,512]{3,2,1,0:T(8,128)(2,1)} reshape(bf16[4,2,16384]{2,1,0:T(2,128)(2,1)} %get-tuple-element.69) | data formatting | bytes 524288 | tf_op jit(solution)/shard_map/squeeze | solution.py:124
  28.4 1.4 collective-permute-start.7
  30.7 1.4 collective-permute-start.8
  32.1 1.0 broadcast_select_fusion.6.refs_2_.refs_0_
  33.8 1.0 broadcast_select_fusion.4.refs_3_.refs_1_
  34.8 1.6 %collective-permute-start.14 = (bf16[2,128,512]{2,1,0:T(8,128)(2,1)S(1)}, bf16[2,128,512]{2,1,0:T(8,128)(2,1)}, u32[]{:S(2)}, u32[]{:S(2)}) collective-permute-start(bf16[2,128,512]{2,1,0:T(8,128)(2,1)S(1)} %broadcast_select_fusion.4.refs_3_.refs_1_), channel_id=1, source_target_pairs={{0,4},{5,1},{4,8},{9,5},{8,12},{13,9},{12,14},{15,13},{14,10},{11,... | collective-permute-start | bytes 786440 | tf_op jit(solution)/shard_map/ppermute | solution.py:104
  36.4 1.6 %broadcast_select_fusion = bf16[2,131072]{1,0:T(2,128)(2,1)S(1)} fusion(bf16[2,131072]{1,0:T(2,128)(2,1)} %collective-permute-done.2, pred[]{:T(512)S(6)} %eq.43, bf16[1,3,2,262144]{3,2,1,0:T(2,128)(2,1)} %param.15, s32[]{:T(128)S(6)} %select_n.201), kind=kLoop, calls=%fused_computation.2 | loop fusion | flops 262144 | bytes 1572869 | tf_op jit(solution)/shard_map/jit(_where)/select_n | solution.py:76
  39.1 8.1 %collective-permute-done.4 = bf16[2,128,512]{2,1,0:T(8,128)(2,1)S(1)} collective-permute-done((bf16[2,128,512]{2,1,0:T(8,128)(2,1)S(1)}, bf16[2,128,512]{2,1,0:T(8,128)(2,1)S(1)}, u32[]{:S(2)}, u32[]{:S(2)}) %collective-permute-start.4) | collective-permute-done | bytes 262176 | tf_op jit(solution)/shard_map/ppermute | solution.py:104
  47.2 10.2 %collective-permute-start.5 = (bf16[2,128,512]{2,1,0:T(8,128)(2,1)S(1)}, bf16[2,128,512]{2,1,0:T(8,128)(2,1)}, u32[]{:S(2)}, u32[]{:S(2)}) collective-permute-start(bf16[2,128,512]{2,1,0:T(8,128)(2,1)S(1)} %broadcast_select_fusion.5.refs_4_.refs_2_.refs_0_), channel_id=1, source_target_pairs={{0,4},{5,1},{4,8},{9,5},{8,12},{13,9},{12,14},{15,13},{14,10},{11,... | collective-permute-start | bytes 786440 | tf_op jit(solution)/shard_map/ppermute | solution.py:104
  58.3 1.8 %squeeze.45 = bf16[4,2,32,512]{3,2,1,0:T(8,128)(2,1)} reshape(bf16[4,2,16384]{2,1,0:T(2,128)(2,1)} %get-tuple-element.71) | data formatting | bytes 524288 | tf_op jit(solution)/shard_map/squeeze | solution.py:124
  60.1 1.0 broadcast_select_fusion.3.refs_5_.refs_3_.refs_1_
  61.1 2.5 %collective-permute-start.15 = (bf16[2,128,512]{2,1,0:T(8,128)(2,1)S(1)}, bf16[2,128,512]{2,1,0:T(8,128)(2,1)S(1)}, u32[]{:S(2)}, u32[]{:S(2)}) collective-permute-start(bf16[2,128,512]{2,1,0:T(8,128)(2,1)S(1)} %broadcast_select_fusion.3.refs_5_.refs_3_.refs_1_), channel_id=1, source_target_pairs={{0,4},{5,1},{4,8},{9,5},{8,12},{13,9},{12,14},{15,13},{14,10},{11,... | collective-permute-start | bytes 786440 | tf_op jit(solution)/shard_map/ppermute | solution.py:104
  67.8 1.9 %collective-permute-start.17 = (bf16[4,2,32,512]{3,2,1,0:T(8,128)(2,1)S(1)}, bf16[4,2,32,512]{3,2,1,0:T(8,128)(2,1)S(1)}, u32[]{:S(2)}, u32[]{:S(2)}) collective-permute-start(bf16[4,2,32,512]{3,2,1,0:T(8,128)(2,1)S(1)} %pad_maximum_fusion.1), channel_id=1, source_target_pairs={{0,1},{1,0},{2,3},{3,2},{4,5},{5,4},{6,7},{7,6},{8,9},{9,8},{10,11... | collective-permute-start | bytes 786440 | tf_op jit(solution)/shard_map/ppermute | solution.py:67
  70.1 2.3 %collective-permute-start.9 = (bf16[2,128,512]{2,1,0:T(8,128)(2,1)}, bf16[2,128,512]{2,1,0:T(8,128)(2,1)S(1)}, u32[]{:S(2)}, u32[]{:S(2)}) collective-permute-start(bf16[2,128,512]{2,1,0:T(8,128)(2,1)} %collective-permute-done.5.refs_6_.refs_4_.refs_2_), channel_id=1, source_target_pairs={{0,4},{5,1},{4,8},{9,5},{8,12},{13,9},{12,14},{15,13},{14,10},{11,... | collective-permute-start | bytes 786440 | tf_op jit(solution)/shard_map/ppermute | solution.py:104
  72.4 3.9 %collective-permute-done.19.refs_3_ = bf16[4,2,32,512]{3,2,1,0:T(8,128)(2,1)S(1)} collective-permute-done((bf16[4,2,32,512]{3,2,1,0:T(8,128)(2,1)S(1)}, bf16[4,2,32,512]{3,2,1,0:T(8,128)(2,1)S(1)}, u32[]{:S(2)}, u32[]{:S(2)}) %collective-permute-start.19) | collective-permute-done | bytes 262176 | tf_op jit(solution)/shard_map/ppermute | solution.py:67
  76.3 3.6 %collective-permute-done.18.refs_2_ = bf16[4,2,32,512]{3,2,1,0:T(8,128)(2,1)S(1)} collective-permute-done((bf16[4,2,32,512]{3,2,1,0:T(8,128)(2,1)S(1)}, bf16[4,2,32,512]{3,2,1,0:T(8,128)(2,1)S(1)}, u32[]{:S(2)}, u32[]{:S(2)}) %collective-permute-start.18) | collective-permute-done | bytes 262176 | tf_op jit(solution)/shard_map/ppermute | solution.py:67
  79.9 2.1 %collective-permute-start.32 = (bf16[2,128,512]{2,1,0:T(8,128)(2,1)S(1)}, bf16[2,128,512]{2,1,0:T(8,128)(2,1)S(1)}, u32[]{:S(2)}, u32[]{:S(2)}) collective-permute-start(bf16[2,128,512]{2,1,0:T(8,128)(2,1)S(1)} %broadcast_select_fusion.4.refs_3_.refs_1_), channel_id=1, source_target_pairs={{0,1},{1,0},{2,3},{3,2},{4,5},{5,4},{6,7},{7,6},{8,9},{9,8},{10,11... | collective-permute-start | bytes 786440 | tf_op jit(solution)/shard_map/ppermute | solution.py:67
  83.0 2.8 %collective-permute-done.9.refs_8_.refs_6_.refs_4_ = bf16[2,128,512]{2,1,0:T(8,128)(2,1)S(1)} collective-permute-done((bf16[2,128,512]{2,1,0:T(8,128)(2,1)}, bf16[2,128,512]{2,1,0:T(8,128)(2,1)S(1)}, u32[]{:S(2)}, u32[]{:S(2)}) %collective-permute-start.9) | collective-permute-done | bytes 262176 | tf_op jit(solution)/shard_map/ppermute | solution.py:104
  85.9 1.0 collective-permute-start.33
  87.0 1.5 %collective-permute-start.20 = (bf16[4,2,32,512]{3,2,1,0:T(8,128)(2,1)S(1)}, bf16[4,2,32,512]{3,2,1,0:T(8,128)(2,1)S(1)}, u32[]{:S(2)}, u32[]{:S(2)}) collective-permute-start(bf16[4,2,32,512]{3,2,1,0:T(8,128)(2,1)S(1)} %pad_maximum_fusion.refs_0_), channel_id=1, source_target_pairs={{0,16},{16,0},{1,17},{17,1},{2,18},{18,2},{3,19},{19,3},{4,20},{20... | collective-permute-start | bytes 786440 | tf_op jit(solution)/shard_map/ppermute | solution.py:134
  88.5 3.6 %collective-permute-done.10.refs_10_.refs_8_.refs_6_ = bf16[2,128,512]{2,1,0:T(8,128)(2,1)S(1)} collective-permute-done((bf16[2,128,512]{2,1,0:T(8,128)(2,1)S(1)}, bf16[2,128,512]{2,1,0:T(8,128)(2,1)S(1)}, u32[]{:S(2)}, u32[]{:S(2)}) %collective-permute-start.10) | collective-permute-done | bytes 262176 | tf_op jit(solution)/shard_map/ppermute | solution.py:104
  92.2 1.5 %collective-permute-start.21 = (bf16[4,2,32,512]{3,2,1,0:T(8,128)(2,1)S(1)}, bf16[4,2,32,512]{3,2,1,0:T(8,128)(2,1)S(1)}, u32[]{:S(2)}, u32[]{:S(2)}) collective-permute-start(bf16[4,2,32,512]{3,2,1,0:T(8,128)(2,1)S(1)} %collective-permute-done.17.refs_1_), channel_id=1, source_target_pairs={{0,16},{16,0},{1,17},{17,1},{2,18},{18,2},{3,19},{19,3},{4,20},{20... | collective-permute-start | bytes 786440 | tf_op jit(solution)/shard_map/ppermute | solution.py:134
  94.2 1.9 %collective-permute-done.20.refs_4_ = bf16[4,2,32,512]{3,2,1,0:T(8,128)(2,1)S(1)} collective-permute-done((bf16[4,2,32,512]{3,2,1,0:T(8,128)(2,1)S(1)}, bf16[4,2,32,512]{3,2,1,0:T(8,128)(2,1)S(1)}, u32[]{:S(2)}, u32[]{:S(2)}) %collective-permute-start.20) | collective-permute-done | bytes 262176 | tf_op jit(solution)/shard_map/ppermute | solution.py:134
  96.1 1.5 %collective-permute-start.23 = (bf16[4,2,32,512]{3,2,1,0:T(8,128)(2,1)S(1)}, bf16[4,2,32,512]{3,2,1,0:T(8,128)(2,1)S(1)}, u32[]{:S(2)}, u32[]{:S(2)}) collective-permute-start(bf16[4,2,32,512]{3,2,1,0:T(8,128)(2,1)S(1)} %collective-permute-done.19.refs_3_), channel_id=1, source_target_pairs={{0,16},{16,0},{1,17},{17,1},{2,18},{18,2},{3,19},{19,3},{4,20},{20... | collective-permute-start | bytes 786440 | tf_op jit(solution)/shard_map/ppermute | solution.py:134
  98.5 1.0 collective-permute-start.12
  99.6 2.2 %collective-permute-done.21.refs_5_ = bf16[4,2,32,512]{3,2,1,0:T(8,128)(2,1)S(1)} collective-permute-done((bf16[4,2,32,512]{3,2,1,0:T(8,128)(2,1)S(1)}, bf16[4,2,32,512]{3,2,1,0:T(8,128)(2,1)S(1)}, u32[]{:S(2)}, u32[]{:S(2)}) %collective-permute-start.21) | collective-permute-done | bytes 262176 | tf_op jit(solution)/shard_map/ppermute | solution.py:134
  101.8 5.6 %collective-permute-done.22.refs_6_ = bf16[4,2,32,512]{3,2,1,0:T(8,128)(2,1)S(1)} collective-permute-done((bf16[4,2,32,512]{3,2,1,0:T(8,128)(2,1)S(1)}, bf16[4,2,32,512]{3,2,1,0:T(8,128)(2,1)S(1)}, u32[]{:S(2)}, u32[]{:S(2)}) %collective-permute-start.22) | collective-permute-done | bytes 262176 | tf_op jit(solution)/shard_map/ppermute | solution.py:134
  107.4 5.2 %collective-permute-done.23.refs_7_ = bf16[4,2,32,512]{3,2,1,0:T(8,128)(2,1)S(1)} collective-permute-done((bf16[4,2,32,512]{3,2,1,0:T(8,128)(2,1)S(1)}, bf16[4,2,32,512]{3,2,1,0:T(8,128)(2,1)S(1)}, u32[]{:S(2)}, u32[]{:S(2)}) %collective-permute-start.23) | collective-permute-done | bytes 262176 | tf_op jit(solution)/shard_map/ppermute | solution.py:134
  113.1 2.1 %shard_map.158 = (bf16[2,2,512,512]{3,2,1,0:T(8,128)(2,1)S(1)}, f32[2]{0:T(128)S(1)}) custom-call(s32[32]{0:T(128)S(1)} %copy-done.1, s32[32]{0:T(128)S(1)} %reshape.251.list_ref, s32[7]{0:T(128)S(1)} %stack.40.where_ref, bf16[4,2,32,512]{3,2,1,0:T(8,128)(2,1)S(1)} %pad_maximum_fusion.refs_0_, bf16[4,2,32,512]{3,2,1,0:T(8,128)(2,1)S(1)} %collective-permute-done.17.refs_1_, ...), custom_call_target="tpu_custom_call" | custom-call | flops 2000000000 | bytes 6000000 | tf_op jit(solution)/shard_map/pallas_call | solution.py:279
  116.8 2.7 %collective-permute-done.26.refs_15_.refs_13_.refs_11_ = bf16[2,128,512]{2,1,0:T(8,128)(2,1)S(1)} collective-permute-done((bf16[2,128,512]{2,1,0:T(8,128)(2,1)S(1)}, bf16[2,128,512]{2,1,0:T(8,128)(2,1)S(1)}, u32[]{:S(2)}, u32[]{:S(2)}) %collective-permute-start.26) | collective-permute-done | bytes 262176 | tf_op jit(solution)/shard_map/ppermute | solution.py:104
  119.4 1.5 %collective-permute-start.28 = (bf16[2,128,512]{2,1,0:T(8,128)(2,1)S(1)}, bf16[2,128,512]{2,1,0:T(8,128)(2,1)S(1)}, u32[]{:S(2)}, u32[]{:S(2)}) collective-permute-start(bf16[2,128,512]{2,1,0:T(8,128)(2,1)S(1)} %collective-permute-done.26.refs_15_.refs_13_.refs_11_), channel_id=1, source_target_pairs={{0,4},{5,1},{4,8},{9,5},{8,12},{13,9},{12,14},{15,13},{14,10},{11,... | collective-permute-start | bytes 786440 | tf_op jit(solution)/shard_map/ppermute | solution.py:104
  121.0 6.5 %shard_map.159.refs_38_ = f32[2,512,512]{2,1,0:T(8,128)S(1)} custom-call(s32[7]{0:T(128)S(1)} %stack.40.where_ref, f32[2]{0:T(128)S(1)} %get-tuple-element.58.sigma_ref, bf16[2,128,512]{2,1,0:T(8,128)(2,1)S(1)} %get-tuple-element.39.refs_0_, bf16[2,128,512]{2,1,0:T(8,128)(2,1)S(1)} %get-tuple-element.47.refs_1_, ...), custom_call_target="tpu_custom_call" | custom-call | flops 5000000000 | bytes 10000000 | tf_op jit(solution)/shard_map/pallas_call | solution.py:299
  127.5 1.1 collective-permute-done.28.refs_15_.refs_13_
  130.7 5.9 %shard_map.160.refs_38_ = f32[2,512,512]{2,1,0:T(8,128)S(1)} custom-call(s32[7]{0:T(128)S(1)} %stack.40.where_ref, f32[2]{0:T(128)S(1)} %get-tuple-element.58.sigma_ref, bf16[2,128,512]{2,1,0:T(8,128)(2,1)S(1)} %broadcast_select_fusion.6.refs_2_.refs_0_, bf16[2,128,512]{2,1,0:T(8,128)(2,1)S(1)} %broadcast_select_fusion.4.refs_3_.refs_1_, ...), custom_call_target="tpu_custom_call" | custom-call | flops 5000000000 | bytes 10000000 | tf_op jit(solution)/shard_map/pallas_call | solution.py:299
  136.7 1.6 %collective-permute-done.45.refs_14_ = bf16[2,128,512]{2,1,0:T(8,128)(2,1)S(1)} collective-permute-done((bf16[2,128,512]{2,1,0:T(8,128)(2,1)S(1)}, bf16[2,128,512]{2,1,0:T(8,128)(2,1)S(1)}, u32[]{:S(2)}, u32[]{:S(2)}) %collective-permute-start.45) | collective-permute-done | bytes 262176 | tf_op jit(solution)/shard_map/ppermute | solution.py:104
  138.3 1.5 %collective-permute-done.49.refs_30_ = bf16[2,128,512]{2,1,0:T(8,128)(2,1)S(1)} collective-permute-done((bf16[2,128,512]{2,1,0:T(8,128)(2,1)S(1)}, bf16[2,128,512]{2,1,0:T(8,128)(2,1)S(1)}, u32[]{:S(2)}, u32[]{:S(2)}) %collective-permute-start.49) | collective-permute-done | bytes 262176 | tf_op jit(solution)/shard_map/ppermute | solution.py:67
  139.8 6.4 %shard_map.161 = (f32[2]{0:T(128)}, f32[2]{0:T(128)}) custom-call(s32[7]{0:T(128)S(1)} %stack.40.where_ref, f32[2]{0:T(128)S(1)} %get-tuple-element.58.sigma_ref, bf16[2,128,512]{2,1,0:T(8,128)(2,1)S(1)} %broadcast_select_fusion.5.refs_4_.refs_2_.refs_0_, bf16[2,128,512]{2,1,0:T(8,128)(2,1)S(1)} %broadcast_select_fusion.3.refs_5_.refs_3_.refs_1_, ...), custom_call_target="tpu_custom_call" | custom-call | flops 5000000000 | bytes 10000000 | tf_op jit(solution)/shard_map/pallas_call | solution.py:299
  (120 shorter events, 17.9 us)
Async XLA Ops:
  2.2 2.6 %collective-permute-start = (bf16[2,131072]{1,0:T(2,128)(2,1)S(1)}, bf16[2,131072]{1,0:T(2,128)(2,1)S(1)}, u32[]{:S(2)}, u32[]{:S(2)}) collective-permute-start(bf16[2,131072]{1,0:T(2,128)(2,1)S(1)} %dynamic-slice_bitcast_fusion.2), channel_id=1, source_target_pairs={{0,1},{1,0},{2,3},{3,2},{4,5},{5,4},{6,7},{7,6},{8,9},{9,8},{10,11... | collective-permute-start | bytes 1572872 | tf_op jit(solution)/shard_map/ppermute | solution.py:67
  8.6 8.7 %collective-permute-start.1 = (bf16[2,131072]{1,0:T(2,128)(2,1)S(1)}, bf16[2,131072]{1,0:T(2,128)(2,1)}, u32[]{:S(2)}, u32[]{:S(2)}) collective-permute-start(bf16[2,131072]{1,0:T(2,128)(2,1)S(1)} %dynamic-slice_bitcast_fusion.1), channel_id=1, source_target_pairs={{0,1},{1,0},{2,3},{3,2},{4,5},{5,4},{6,7},{7,6},{8,9},{9,8},{10,11... | collective-permute-start | bytes 1572872 | tf_op jit(solution)/shard_map/ppermute | solution.py:67
  9.0 21.6 %collective-permute-start.3 = (bf16[2,128,512]{2,1,0:T(8,128)(2,1)S(1)}, bf16[2,128,512]{2,1,0:T(8,128)(2,1)}, u32[]{:S(2)}, u32[]{:S(2)}) collective-permute-start(bf16[2,128,512]{2,1,0:T(8,128)(2,1)S(1)} %get-tuple-element.39.refs_0_), channel_id=1, source_target_pairs={{0,4},{5,1},{4,8},{9,5},{8,12},{13,9},{12,14},{15,13},{14,10},{11,... | collective-permute-start | bytes 786440 | tf_op jit(solution)/shard_map/ppermute | solution.py:104
  12.1 21.0 %collective-permute-start.13 = (bf16[2,128,512]{2,1,0:T(8,128)(2,1)S(1)}, bf16[2,128,512]{2,1,0:T(8,128)(2,1)}, u32[]{:S(2)}, u32[]{:S(2)}) collective-permute-start(bf16[2,128,512]{2,1,0:T(8,128)(2,1)S(1)} %get-tuple-element.47.refs_1_), channel_id=1, source_target_pairs={{0,4},{5,1},{4,8},{9,5},{8,12},{13,9},{12,14},{15,13},{14,10},{11,... | collective-permute-start | bytes 786440 | tf_op jit(solution)/shard_map/ppermute | solution.py:104
  21.7 13.1 %collective-permute-start.2 = (bf16[2,131072]{1,0:T(2,128)(2,1)}, bf16[2,131072]{1,0:T(2,128)(2,1)}, u32[]{:S(2)}, u32[]{:S(2)}) collective-permute-start(bf16[2,131072]{1,0:T(2,128)(2,1)} %dynamic-slice_bitcast_fusion), channel_id=1, source_target_pairs={{0,1},{1,0},{2,3},{3,2},{4,5},{5,4},{6,7},{7,6},{8,9},{9,8},{10,11... | collective-permute-start | bytes 1572872 | tf_op jit(solution)/shard_map/ppermute | solution.py:67
  25.0 36.1 %collective-permute-start.6 = (bf16[4,2,32,512]{3,2,1,0:T(8,128)(2,1)}, bf16[4,2,32,512]{3,2,1,0:T(8,128)(2,1)}, u32[]{:S(2)}, u32[]{:S(2)}) collective-permute-start(bf16[4,2,32,512]{3,2,1,0:T(8,128)(2,1)} %squeeze.46), channel_id=1, source_target_pairs={{0,4},{1,5},{2,6},{3,7},{4,0},{5,1},{6,2},{7,3},{8,12},{9,13},{10,... | collective-permute-start | bytes 786440 | tf_op jit(solution)/shard_map/ppermute | solution.py:67
  28.4 35.3 %collective-permute-start.7 = (bf16[4,2,32,512]{3,2,1,0:T(8,128)(2,1)}, bf16[4,2,32,512]{3,2,1,0:T(8,128)(2,1)}, u32[]{:S(2)}, u32[]{:S(2)}) collective-permute-start(bf16[4,2,32,512]{3,2,1,0:T(8,128)(2,1)} %squeeze.47), channel_id=1, source_target_pairs={{0,8},{1,9},{2,10},{3,11},{4,12},{5,13},{6,14},{7,15},{8,0},{9,1},... | collective-permute-start | bytes 786440 | tf_op jit(solution)/shard_map/ppermute | solution.py:67
  30.7 33.0 %collective-permute-start.8 = (bf16[4,2,32,512]{3,2,1,0:T(8,128)(2,1)}, bf16[4,2,32,512]{3,2,1,0:T(8,128)(2,1)}, u32[]{:S(2)}, u32[]{:S(2)}) collective-permute-start(bf16[4,2,32,512]{3,2,1,0:T(8,128)(2,1)} %squeeze.48), channel_id=1, source_target_pairs={{0,12},{1,13},{2,14},{3,15},{4,8},{5,9},{6,10},{7,11},{8,4},{9,5},... | collective-permute-start | bytes 786440 | tf_op jit(solution)/shard_map/ppermute | solution.py:67
  33.1 14.1 %collective-permute-start.4 = (bf16[2,128,512]{2,1,0:T(8,128)(2,1)S(1)}, bf16[2,128,512]{2,1,0:T(8,128)(2,1)S(1)}, u32[]{:S(2)}, u32[]{:S(2)}) collective-permute-start(bf16[2,128,512]{2,1,0:T(8,128)(2,1)S(1)} %broadcast_select_fusion.6.refs_2_.refs_0_), channel_id=1, source_target_pairs={{0,4},{5,1},{4,8},{9,5},{8,12},{13,9},{12,14},{15,13},{14,10},{11,... | collective-permute-start | bytes 786440 | tf_op jit(solution)/shard_map/ppermute | solution.py:104
  34.8 25.3 %collective-permute-start.14 = (bf16[2,128,512]{2,1,0:T(8,128)(2,1)S(1)}, bf16[2,128,512]{2,1,0:T(8,128)(2,1)}, u32[]{:S(2)}, u32[]{:S(2)}) collective-permute-start(bf16[2,128,512]{2,1,0:T(8,128)(2,1)S(1)} %broadcast_select_fusion.4.refs_3_.refs_1_), channel_id=1, source_target_pairs={{0,4},{5,1},{4,8},{9,5},{8,12},{13,9},{12,14},{15,13},{14,10},{11,... | collective-permute-start | bytes 786440 | tf_op jit(solution)/shard_map/ppermute | solution.py:104
  47.2 16.4 %collective-permute-start.5 = (bf16[2,128,512]{2,1,0:T(8,128)(2,1)S(1)}, bf16[2,128,512]{2,1,0:T(8,128)(2,1)}, u32[]{:S(2)}, u32[]{:S(2)}) collective-permute-start(bf16[2,128,512]{2,1,0:T(8,128)(2,1)S(1)} %broadcast_select_fusion.5.refs_4_.refs_2_.refs_0_), channel_id=1, source_target_pairs={{0,4},{5,1},{4,8},{9,5},{8,12},{13,9},{12,14},{15,13},{14,10},{11,... | collective-permute-start | bytes 786440 | tf_op jit(solution)/shard_map/ppermute | solution.py:104
  60.1 9.9 %collective-permute-start.29 = (bf16[2,128,512]{2,1,0:T(8,128)(2,1)S(1)}, bf16[2,128,512]{2,1,0:T(8,128)(2,1)S(1)}, u32[]{:S(2)}, u32[]{:S(2)}) collective-permute-start(bf16[2,128,512]{2,1,0:T(8,128)(2,1)S(1)} %get-tuple-element.39.refs_0_), channel_id=1, source_target_pairs={{0,1},{1,0},{2,3},{3,2},{4,5},{5,4},{6,7},{7,6},{8,9},{9,8},{10,11... | collective-permute-start | bytes 786440 | tf_op jit(solution)/shard_map/ppermute | solution.py:67
  61.1 8.6 %collective-permute-start.15 = (bf16[2,128,512]{2,1,0:T(8,128)(2,1)S(1)}, bf16[2,128,512]{2,1,0:T(8,128)(2,1)S(1)}, u32[]{:S(2)}, u32[]{:S(2)}) collective-permute-start(bf16[2,128,512]{2,1,0:T(8,128)(2,1)S(1)} %broadcast_select_fusion.3.refs_5_.refs_3_.refs_1_), channel_id=1, source_target_pairs={{0,4},{5,1},{4,8},{9,5},{8,12},{13,9},{12,14},{15,13},{14,10},{11,... | collective-permute-start | bytes 786440 | tf_op jit(solution)/shard_map/ppermute | solution.py:104
  67.5 8.7 %collective-permute-start.19 = (bf16[4,2,32,512]{3,2,1,0:T(8,128)(2,1)S(1)}, bf16[4,2,32,512]{3,2,1,0:T(8,128)(2,1)S(1)}, u32[]{:S(2)}, u32[]{:S(2)}) collective-permute-start(bf16[4,2,32,512]{3,2,1,0:T(8,128)(2,1)S(1)} %pad_maximum_fusion.3), channel_id=1, source_target_pairs={{0,3},{1,2},{2,1},{3,0},{4,7},{5,6},{6,5},{7,4},{8,11},{9,10},{10,... | collective-permute-start | bytes 786440 | tf_op jit(solution)/shard_map/ppermute | solution.py:67
  67.7 12.2 %collective-permute-start.18 = (bf16[4,2,32,512]{3,2,1,0:T(8,128)(2,1)S(1)}, bf16[4,2,32,512]{3,2,1,0:T(8,128)(2,1)S(1)}, u32[]{:S(2)}, u32[]{:S(2)}) collective-permute-start(bf16[4,2,32,512]{3,2,1,0:T(8,128)(2,1)S(1)} %pad_maximum_fusion.2), channel_id=1, source_target_pairs={{0,2},{1,3},{2,0},{3,1},{4,6},{5,7},{6,4},{7,5},{8,10},{9,11},{10,... | collective-permute-start | bytes 786440 | tf_op jit(solution)/shard_map/ppermute | solution.py:67
  67.8 14.2 %collective-permute-start.17 = (bf16[4,2,32,512]{3,2,1,0:T(8,128)(2,1)S(1)}, bf16[4,2,32,512]{3,2,1,0:T(8,128)(2,1)S(1)}, u32[]{:S(2)}, u32[]{:S(2)}) collective-permute-start(bf16[4,2,32,512]{3,2,1,0:T(8,128)(2,1)S(1)} %pad_maximum_fusion.1), channel_id=1, source_target_pairs={{0,1},{1,0},{2,3},{3,2},{4,5},{5,4},{6,7},{7,6},{8,9},{9,8},{10,11... | collective-permute-start | bytes 786440 | tf_op jit(solution)/shard_map/ppermute | solution.py:67
  69.7 13.3 %collective-permute-start.16 = (bf16[2,128,512]{2,1,0:T(8,128)(2,1)S(1)}, bf16[2,128,512]{2,1,0:T(8,128)(2,1)S(1)}, u32[]{:S(2)}, u32[]{:S(2)}) collective-permute-start(bf16[2,128,512]{2,1,0:T(8,128)(2,1)S(1)} %collective-permute-done.15.refs_7_.refs_5_.refs_3_), channel_id=1, source_target_pairs={{0,4},{5,1},{4,8},{9,5},{8,12},{13,9},{12,14},{15,13},{14,10},{11,... | collective-permute-start | bytes 786440 | tf_op jit(solution)/shard_map/ppermute | solution.py:104
  70.1 15.7 %collective-permute-start.9 = (bf16[2,128,512]{2,1,0:T(8,128)(2,1)}, bf16[2,128,512]{2,1,0:T(8,128)(2,1)S(1)}, u32[]{:S(2)}, u32[]{:S(2)}) collective-permute-start(bf16[2,128,512]{2,1,0:T(8,128)(2,1)} %collective-permute-done.5.refs_6_.refs_4_.refs_2_), channel_id=1, source_target_pairs={{0,4},{5,1},{4,8},{9,5},{8,12},{13,9},{12,14},{15,13},{14,10},{11,... | collective-permute-start | bytes 786440 | tf_op jit(solution)/shard_map/ppermute | solution.py:104
  76.3 9.6 %collective-permute-start.30 = (bf16[2,128,512]{2,1,0:T(8,128)(2,1)S(1)}, bf16[2,128,512]{2,1,0:T(8,128)(2,1)S(1)}, u32[]{:S(2)}, u32[]{:S(2)}) collective-permute-start(bf16[2,128,512]{2,1,0:T(8,128)(2,1)S(1)} %get-tuple-element.47.refs_1_), channel_id=1, source_target_pairs={{0,1},{1,0},{2,3},{3,2},{4,5},{5,4},{6,7},{7,6},{8,9},{9,8},{10,11... | collective-permute-start | bytes 786440 | tf_op jit(solution)/shard_map/ppermute | solution.py:67
  79.9 7.0 %collective-permute-start.32 = (bf16[2,128,512]{2,1,0:T(8,128)(2,1)S(1)}, bf16[2,128,512]{2,1,0:T(8,128)(2,1)S(1)}, u32[]{:S(2)}, u32[]{:S(2)}) collective-permute-start(bf16[2,128,512]{2,1,0:T(8,128)(2,1)S(1)} %broadcast_select_fusion.4.refs_3_.refs_1_), channel_id=1, source_target_pairs={{0,1},{1,0},{2,3},{3,2},{4,5},{5,4},{6,7},{7,6},{8,9},{9,8},{10,11... | collective-permute-start | bytes 786440 | tf_op jit(solution)/shard_map/ppermute | solution.py:67
  82.0 5.0 %collective-permute-start.31 = (bf16[2,128,512]{2,1,0:T(8,128)(2,1)S(1)}, bf16[2,128,512]{2,1,0:T(8,128)(2,1)S(1)}, u32[]{:S(2)}, u32[]{:S(2)}) collective-permute-start(bf16[2,128,512]{2,1,0:T(8,128)(2,1)S(1)} %broadcast_select_fusion.6.refs_2_.refs_0_), channel_id=1, source_target_pairs={{0,1},{1,0},{2,3},{3,2},{4,5},{5,4},{6,7},{7,6},{8,9},{9,8},{10,11... | collective-permute-start | bytes 786440 | tf_op jit(solution)/shard_map/ppermute | solution.py:67
  83.0 5.5 %collective-permute-start.34 = (bf16[2,128,512]{2,1,0:T(8,128)(2,1)S(1)}, bf16[2,128,512]{2,1,0:T(8,128)(2,1)S(1)}, u32[]{:S(2)}, u32[]{:S(2)}) collective-permute-start(bf16[2,128,512]{2,1,0:T(8,128)(2,1)S(1)} %broadcast_select_fusion.3.refs_5_.refs_3_.refs_1_), channel_id=1, source_target_pairs={{0,1},{1,0},{2,3},{3,2},{4,5},{5,4},{6,7},{7,6},{8,9},{9,8},{10,11... | collective-permute-start | bytes 786440 | tf_op jit(solution)/shard_map/ppermute | solution.py:67
  85.8 6.4 %collective-permute-start.10 = (bf16[2,128,512]{2,1,0:T(8,128)(2,1)S(1)}, bf16[2,128,512]{2,1,0:T(8,128)(2,1)S(1)}, u32[]{:S(2)}, u32[]{:S(2)}) collective-permute-start(bf16[2,128,512]{2,1,0:T(8,128)(2,1)S(1)} %collective-permute-done.9.refs_8_.refs_6_.refs_4_), channel_id=1, source_target_pairs={{0,4},{5,1},{4,8},{9,5},{8,12},{13,9},{12,14},{15,13},{14,10},{11,... | collective-permute-start | bytes 786440 | tf_op jit(solution)/shard_map/ppermute | solution.py:104
  85.9 6.3 %collective-permute-start.33 = (bf16[2,128,512]{2,1,0:T(8,128)(2,1)S(1)}, bf16[2,128,512]{2,1,0:T(8,128)(2,1)S(1)}, u32[]{:S(2)}, u32[]{:S(2)}) collective-permute-start(bf16[2,128,512]{2,1,0:T(8,128)(2,1)S(1)} %broadcast_select_fusion.5.refs_4_.refs_2_.refs_0_), channel_id=1, source_target_pairs={{0,1},{1,0},{2,3},{3,2},{4,5},{5,4},{6,7},{7,6},{8,9},{9,8},{10,11... | collective-permute-start | bytes 786440 | tf_op jit(solution)/shard_map/ppermute | solution.py:67
  86.9 6.8 %collective-permute-start.36 = (bf16[2,128,512]{2,1,0:T(8,128)(2,1)S(1)}, bf16[2,128,512]{2,1,0:T(8,128)(2,1)S(1)}, u32[]{:S(2)}, u32[]{:S(2)}) collective-permute-start(bf16[2,128,512]{2,1,0:T(8,128)(2,1)S(1)} %collective-permute-done.15.refs_7_.refs_5_.refs_3_), channel_id=1, source_target_pairs={{0,1},{1,0},{2,3},{3,2},{4,5},{5,4},{6,7},{7,6},{8,9},{9,8},{10,11... | collective-permute-start | bytes 786440 | tf_op jit(solution)/shard_map/ppermute | solution.py:67
  87.0 9.1 %collective-permute-start.20 = (bf16[4,2,32,512]{3,2,1,0:T(8,128)(2,1)S(1)}, bf16[4,2,32,512]{3,2,1,0:T(8,128)(2,1)S(1)}, u32[]{:S(2)}, u32[]{:S(2)}) collective-permute-start(bf16[4,2,32,512]{3,2,1,0:T(8,128)(2,1)S(1)} %pad_maximum_fusion.refs_0_), channel_id=1, source_target_pairs={{0,16},{16,0},{1,17},{17,1},{2,18},{18,2},{3,19},{19,3},{4,20},{20... | collective-permute-start | bytes 786440 | tf_op jit(solution)/shard_map/ppermute | solution.py:134
  88.5 9.1 %collective-permute-start.24 = (bf16[2,128,512]{2,1,0:T(8,128)(2,1)S(1)}, bf16[2,128,512]{2,1,0:T(8,128)(2,1)S(1)}, u32[]{:S(2)}, u32[]{:S(2)}) collective-permute-start(bf16[2,128,512]{2,1,0:T(8,128)(2,1)S(1)} %collective-permute-done.16.refs_9_.refs_7_.refs_5_), channel_id=1, source_target_pairs={{0,4},{5,1},{4,8},{9,5},{8,12},{13,9},{12,14},{15,13},{14,10},{11,... | collective-permute-start | bytes 786440 | tf_op jit(solution)/shard_map/ppermute | solution.py:104
  92.2 6.4 %collective-permute-start.11 = (bf16[2,128,512]{2,1,0:T(8,128)(2,1)S(1)}, bf16[2,128,512]{2,1,0:T(8,128)(2,1)S(1)}, u32[]{:S(2)}, u32[]{:S(2)}) collective-permute-start(bf16[2,128,512]{2,1,0:T(8,128)(2,1)S(1)} %collective-permute-done.10.refs_10_.refs_8_.refs_6_), channel_id=1, source_target_pairs={{0,4},{5,1},{4,8},{9,5},{8,12},{13,9},{12,14},{15,13},{14,10},{11,... | collective-permute-start | bytes 786440 | tf_op jit(solution)/shard_map/ppermute | solution.py:104
  92.2 9.6 %collective-permute-start.21 = (bf16[4,2,32,512]{3,2,1,0:T(8,128)(2,1)S(1)}, bf16[4,2,32,512]{3,2,1,0:T(8,128)(2,1)S(1)}, u32[]{:S(2)}, u32[]{:S(2)}) collective-permute-start(bf16[4,2,32,512]{3,2,1,0:T(8,128)(2,1)S(1)} %collective-permute-done.17.refs_1_), channel_id=1, source_target_pairs={{0,16},{16,0},{1,17},{17,1},{2,18},{18,2},{3,19},{19,3},{4,20},{20... | collective-permute-start | bytes 786440 | tf_op jit(solution)/shard_map/ppermute | solution.py:134
  93.7 13.7 %collective-permute-start.22 = (bf16[4,2,32,512]{3,2,1,0:T(8,128)(2,1)S(1)}, bf16[4,2,32,512]{3,2,1,0:T(8,128)(2,1)S(1)}, u32[]{:S(2)}, u32[]{:S(2)}) collective-permute-start(bf16[4,2,32,512]{3,2,1,0:T(8,128)(2,1)S(1)} %collective-permute-done.18.refs_2_), channel_id=1, source_target_pairs={{0,16},{16,0},{1,17},{17,1},{2,18},{18,2},{3,19},{19,3},{4,20},{20... | collective-permute-start | bytes 786440 | tf_op jit(solution)/shard_map/ppermute | solution.py:134
  96.1 16.4 %collective-permute-start.23 = (bf16[4,2,32,512]{3,2,1,0:T(8,128)(2,1)S(1)}, bf16[4,2,32,512]{3,2,1,0:T(8,128)(2,1)S(1)}, u32[]{:S(2)}, u32[]{:S(2)}) collective-permute-start(bf16[4,2,32,512]{3,2,1,0:T(8,128)(2,1)S(1)} %collective-permute-done.19.refs_3_), channel_id=1, source_target_pairs={{0,16},{16,0},{1,17},{17,1},{2,18},{18,2},{3,19},{19,3},{4,20},{20... | collective-permute-start | bytes 786440 | tf_op jit(solution)/shard_map/ppermute | solution.py:134
  97.6 14.9 %collective-permute-start.25 = (bf16[2,128,512]{2,1,0:T(8,128)(2,1)S(1)}, bf16[2,128,512]{2,1,0:T(8,128)(2,1)S(1)}, u32[]{:S(2)}, u32[]{:S(2)}) collective-permute-start(bf16[2,128,512]{2,1,0:T(8,128)(2,1)S(1)} %collective-permute-done.24.refs_11_.refs_9_.refs_7_), channel_id=1, source_target_pairs={{0,4},{5,1},{4,8},{9,5},{8,12},{13,9},{12,14},{15,13},{14,10},{11,... | collective-permute-start | bytes 786440 | tf_op jit(solution)/shard_map/ppermute | solution.py:104
  98.5 14.5 %collective-permute-start.12 = (bf16[2,128,512]{2,1,0:T(8,128)(2,1)S(1)}, bf16[2,128,512]{2,1,0:T(8,128)(2,1)S(1)}, u32[]{:S(2)}, u32[]{:S(2)}) collective-permute-start(bf16[2,128,512]{2,1,0:T(8,128)(2,1)S(1)} %collective-permute-done.11.refs_12_.refs_10_.refs_8_), channel_id=1, source_target_pairs={{0,4},{5,1},{4,8},{9,5},{8,12},{13,9},{12,14},{15,13},{14,10},{11,... | collective-permute-start | bytes 786440 | tf_op jit(solution)/shard_map/ppermute | solution.py:104
  101.8 13.4 %collective-permute-start.35 = (bf16[2,128,512]{2,1,0:T(8,128)(2,1)}, bf16[2,128,512]{2,1,0:T(8,128)(2,1)S(1)}, u32[]{:S(2)}, u32[]{:S(2)}) collective-permute-start(bf16[2,128,512]{2,1,0:T(8,128)(2,1)} %collective-permute-done.5.refs_6_.refs_4_.refs_2_), channel_id=1, source_target_pairs={{0,1},{1,0},{2,3},{3,2},{4,5},{5,4},{6,7},{7,6},{8,9},{9,8},{10,11... | collective-permute-start | bytes 786440 | tf_op jit(solution)/shard_map/ppermute | solution.py:67
  107.4 8.8 %collective-permute-start.38 = (bf16[2,128,512]{2,1,0:T(8,128)(2,1)S(1)}, bf16[2,128,512]{2,1,0:T(8,128)(2,1)S(1)}, u32[]{:S(2)}, u32[]{:S(2)}) collective-permute-start(bf16[2,128,512]{2,1,0:T(8,128)(2,1)S(1)} %collective-permute-done.16.refs_9_.refs_7_.refs_5_), channel_id=1, source_target_pairs={{0,1},{1,0},{2,3},{3,2},{4,5},{5,4},{6,7},{7,6},{8,9},{9,8},{10,11... | collective-permute-start | bytes 786440 | tf_op jit(solution)/shard_map/ppermute | solution.py:67
  112.5 3.7 %collective-permute-start.37 = (bf16[2,128,512]{2,1,0:T(8,128)(2,1)S(1)}, bf16[2,128,512]{2,1,0:T(8,128)(2,1)S(1)}, u32[]{:S(2)}, u32[]{:S(2)}) collective-permute-start(bf16[2,128,512]{2,1,0:T(8,128)(2,1)S(1)} %collective-permute-done.9.refs_8_.refs_6_.refs_4_), channel_id=1, source_target_pairs={{0,1},{1,0},{2,3},{3,2},{4,5},{5,4},{6,7},{7,6},{8,9},{9,8},{10,11... | collective-permute-start | bytes 786440 | tf_op jit(solution)/shard_map/ppermute | solution.py:67
  112.5 4.1 %collective-permute-start.40 = (bf16[2,128,512]{2,1,0:T(8,128)(2,1)S(1)}, bf16[2,128,512]{2,1,0:T(8,128)(2,1)S(1)}, u32[]{:S(2)}, u32[]{:S(2)}) collective-permute-start(bf16[2,128,512]{2,1,0:T(8,128)(2,1)S(1)} %collective-permute-done.24.refs_11_.refs_9_.refs_7_), channel_id=1, source_target_pairs={{0,1},{1,0},{2,3},{3,2},{4,5},{5,4},{6,7},{7,6},{8,9},{9,8},{10,11... | collective-permute-start | bytes 786440 | tf_op jit(solution)/shard_map/ppermute | solution.py:67
  113.0 6.4 %collective-permute-start.26 = (bf16[2,128,512]{2,1,0:T(8,128)(2,1)S(1)}, bf16[2,128,512]{2,1,0:T(8,128)(2,1)S(1)}, u32[]{:S(2)}, u32[]{:S(2)}) collective-permute-start(bf16[2,128,512]{2,1,0:T(8,128)(2,1)S(1)} %collective-permute-done.25.refs_13_.refs_11_.refs_9_), channel_id=1, source_target_pairs={{0,4},{5,1},{4,8},{9,5},{8,12},{13,9},{12,14},{15,13},{14,10},{11,... | collective-permute-start | bytes 786440 | tf_op jit(solution)/shard_map/ppermute | solution.py:104
  115.2 4.2 %collective-permute-start.39 = (bf16[2,128,512]{2,1,0:T(8,128)(2,1)S(1)}, bf16[2,128,512]{2,1,0:T(8,128)(2,1)S(1)}, u32[]{:S(2)}, u32[]{:S(2)}) collective-permute-start(bf16[2,128,512]{2,1,0:T(8,128)(2,1)S(1)} %collective-permute-done.10.refs_10_.refs_8_.refs_6_), channel_id=1, source_target_pairs={{0,1},{1,0},{2,3},{3,2},{4,5},{5,4},{6,7},{7,6},{8,9},{9,8},{10,11... | collective-permute-start | bytes 786440 | tf_op jit(solution)/shard_map/ppermute | solution.py:67
  116.2 3.3 %collective-permute-start.42 = (bf16[2,128,512]{2,1,0:T(8,128)(2,1)S(1)}, bf16[2,128,512]{2,1,0:T(8,128)(2,1)S(1)}, u32[]{:S(2)}, u32[]{:S(2)}) collective-permute-start(bf16[2,128,512]{2,1,0:T(8,128)(2,1)S(1)} %collective-permute-done.25.refs_13_.refs_11_.refs_9_), channel_id=1, source_target_pairs={{0,1},{1,0},{2,3},{3,2},{4,5},{5,4},{6,7},{7,6},{8,9},{9,8},{10,11... | collective-permute-start | bytes 786440 | tf_op jit(solution)/shard_map/ppermute | solution.py:67
  116.2 4.7 %collective-permute-start.41 = (bf16[2,128,512]{2,1,0:T(8,128)(2,1)S(1)}, bf16[2,128,512]{2,1,0:T(8,128)(2,1)S(1)}, u32[]{:S(2)}, u32[]{:S(2)}) collective-permute-start(bf16[2,128,512]{2,1,0:T(8,128)(2,1)S(1)} %collective-permute-done.11.refs_12_.refs_10_.refs_8_), channel_id=1, source_target_pairs={{0,1},{1,0},{2,3},{3,2},{4,5},{5,4},{6,7},{7,6},{8,9},{9,8},{10,11... | collective-permute-start | bytes 786440 | tf_op jit(solution)/shard_map/ppermute | solution.py:67
  116.7 4.3 %collective-permute-start.43 = (bf16[2,128,512]{2,1,0:T(8,128)(2,1)S(1)}, bf16[2,128,512]{2,1,0:T(8,128)(2,1)S(1)}, u32[]{:S(2)}, u32[]{:S(2)}) collective-permute-start(bf16[2,128,512]{2,1,0:T(8,128)(2,1)S(1)} %collective-permute-done.12.refs_14_.refs_12_.refs_10_), channel_id=1, source_target_pairs={{0,1},{1,0},{2,3},{3,2},{4,5},{5,4},{6,7},{7,6},{8,9},{9,8},{10,11... | collective-permute-start | bytes 786440 | tf_op jit(solution)/shard_map/ppermute | solution.py:67
  119.4 9.2 %collective-permute-start.27 = (bf16[2,128,512]{2,1,0:T(8,128)(2,1)S(1)}, bf16[2,128,512]{2,1,0:T(8,128)(2,1)S(1)}, u32[]{:S(2)}, u32[]{:S(2)}) collective-permute-start(bf16[2,128,512]{2,1,0:T(8,128)(2,1)S(1)} %collective-permute-done.12.refs_14_.refs_12_.refs_10_), channel_id=1, source_target_pairs={{0,4},{5,1},{4,8},{9,5},{8,12},{13,9},{12,14},{15,13},{14,10},{11,... | collective-permute-start | bytes 786440 | tf_op jit(solution)/shard_map/ppermute | solution.py:104
  119.4 9.2 %collective-permute-start.28 = (bf16[2,128,512]{2,1,0:T(8,128)(2,1)S(1)}, bf16[2,128,512]{2,1,0:T(8,128)(2,1)S(1)}, u32[]{:S(2)}, u32[]{:S(2)}) collective-permute-start(bf16[2,128,512]{2,1,0:T(8,128)(2,1)S(1)} %collective-permute-done.26.refs_15_.refs_13_.refs_11_), channel_id=1, source_target_pairs={{0,4},{5,1},{4,8},{9,5},{8,12},{13,9},{12,14},{15,13},{14,10},{11,... | collective-permute-start | bytes 786440 | tf_op jit(solution)/shard_map/ppermute | solution.py:104
  128.6 2.0 %collective-permute-start.48 = (bf16[2,128,512]{2,1,0:T(8,128)(2,1)S(1)}, bf16[2,128,512]{2,1,0:T(8,128)(2,1)S(1)}, u32[]{:S(2)}, u32[]{:S(2)}) collective-permute-start(bf16[2,128,512]{2,1,0:T(8,128)(2,1)S(1)} %collective-permute-done.28.refs_15_.refs_13_), channel_id=1, source_target_pairs={{0,1},{1,0},{2,3},{3,2},{4,5},{5,4},{6,7},{7,6},{8,9},{9,8},{10,11... | collective-permute-start | bytes 786440 | tf_op jit(solution)/shard_map/ppermute | solution.py:67
  128.6 2.0 %collective-permute-start.47 = (bf16[2,128,512]{2,1,0:T(8,128)(2,1)S(1)}, bf16[2,128,512]{2,1,0:T(8,128)(2,1)S(1)}, u32[]{:S(2)}, u32[]{:S(2)}) collective-permute-start(bf16[2,128,512]{2,1,0:T(8,128)(2,1)S(1)} %collective-permute-done.27.refs_14_.refs_12_), channel_id=1, source_target_pairs={{0,1},{1,0},{2,3},{3,2},{4,5},{5,4},{6,7},{7,6},{8,9},{9,8},{10,11... | collective-permute-start | bytes 786440 | tf_op jit(solution)/shard_map/ppermute | solution.py:67
  129.1 7.5 %collective-permute-start.46 = (bf16[2,128,512]{2,1,0:T(8,128)(2,1)S(1)}, bf16[2,128,512]{2,1,0:T(8,128)(2,1)S(1)}, u32[]{:S(2)}, u32[]{:S(2)}) collective-permute-start(bf16[2,128,512]{2,1,0:T(8,128)(2,1)S(1)} %collective-permute-done.28.refs_15_.refs_13_), channel_id=1, source_target_pairs={{0,4},{5,1},{4,8},{9,5},{8,12},{13,9},{12,14},{15,13},{14,10},{11,... | collective-permute-start | bytes 786440 | tf_op jit(solution)/shard_map/ppermute | solution.py:104
  129.8 8.5 %collective-permute-start.45 = (bf16[2,128,512]{2,1,0:T(8,128)(2,1)S(1)}, bf16[2,128,512]{2,1,0:T(8,128)(2,1)S(1)}, u32[]{:S(2)}, u32[]{:S(2)}) collective-permute-start(bf16[2,128,512]{2,1,0:T(8,128)(2,1)S(1)} %collective-permute-done.27.refs_14_.refs_12_), channel_id=1, source_target_pairs={{0,4},{5,1},{4,8},{9,5},{8,12},{13,9},{12,14},{15,13},{14,10},{11,... | collective-permute-start | bytes 786440 | tf_op jit(solution)/shard_map/ppermute | solution.py:104
  (11 other events, 228.7 us)

commit v9 on v8

--- a/solution.py
+++ b/solution.py
@@ -18,9 +18,8 @@
 CORES = 2
 HALF_CHUNKS = 2
 LAG = 2
-LINES = 4
-QUAD = 4
-STAGE_SLOTS = (6, 9, 14)
+TEMPLATE_SLOT = 4
+MASKED_SLOT = 12
 VMEM_LIMIT = 24 * 1024 * 1024
 
 
@@ -114,19 +113,13 @@
     return jnp.where(core == 0, forward, backward), jnp.where(core == 0, backward, forward)
 
 
-def pick_direct(templates, lists):
-    me, group = lax.axis_index("tpl"), lax.axis_index("grp")
-    ids = lax.dynamic_index_in_dim(lists, group, 1, keepdims=False)[me ^ jnp.arange(LINES * QUAD)]
-    return templates[ids].reshape(LINES, QUAD, 2, WAVE_ROWS, COLS)
-
-
-def between_lines(picked):
-    return [picked[0]] + [swap(picked[flip], flip * QUAD) for flip in range(1, LINES)]
-
-
-def inside_quad(lines):
-    blocks = [jnp.stack([line[flip] for line in lines]) for flip in range(QUAD)]
-    return [blocks[0]] + [swap(blocks[flip], flip) for flip in range(1, QUAD)]
+def collect(templates, lists):
+    ids = lax.dynamic_index_in_dim(lists, lax.axis_index("grp"), 1, keepdims=False)
+    return templates[ids].reshape(lists.shape[0], 2, WAVE_ROWS, COLS)
+
+
+def exchange(block):
+    return lax.all_to_all(block, "tpl", split_axis=0, concat_axis=0, tiled=True)
 
 
 def across(block, turn):
@@ -144,7 +137,7 @@
     size = pieces // groups
     picked = templates[lists.reshape(-1)].reshape(devices, pieces, templates.shape[2] // COLS, COLS)
     picked = lax.dynamic_slice_in_dim(picked, own_group * size, size, 1)
-    own = lax.all_to_all(picked, "tpl", split_axis=0, concat_axis=0, tiled=True)
+    own = exchange(picked)
     found = jnp.stack([across(own, turn) for turn in range(groups)])[(own_group - jnp.arange(groups)) % groups]
     found = found.transpose(0, 2, 1, 3, 4).reshape(per_device, 2, ROWS // WAVE_ROWS, WAVE_ROWS, COLS)
     return [found[at].transpose(1, 0, 2, 3) for at in range(per_device)]
@@ -163,24 +156,20 @@
 
 
 def prepare_kernel(count, cut_ref, list_ref, where_ref, *refs):
-    piece_refs, (masked_ref, sigma_ref) = refs[:-2], refs[-2:]
-    pieces = len(piece_refs) // count
-    flips = where_ref[4]
+    wave_refs, (masked_ref, sigma_ref) = refs[:-2], refs[-2:]
     for tpl in range(count):
-        cutoff = cut_ref[list_ref[where_ref[2] * count + where_ref[5 + tpl]]]
+        cutoff = cut_ref[list_ref[where_ref[2] * count + where_ref[4 + tpl]]]
         total = jnp.zeros((8, COLS), jnp.float32)
-        for piece in range(pieces):
-            wave_ref = piece_refs[tpl * pieces + piece]
-            for block in range(ROWS // WAVE_ROWS // pieces):
-                start = pl.multiple_of((flips ^ (block * pieces + piece)) * WAVE_ROWS, WAVE_ROWS)
-                bins = (lax.broadcasted_iota(jnp.int32, (WAVE_ROWS, COLS), 0) + start) * COLS
-                inside = bins + lax.broadcasted_iota(jnp.int32, (WAVE_ROWS, COLS), 1) < cutoff
-                wave_re = jnp.where(inside, wave_ref[block, 0].astype(jnp.float32), 0.0)
-                wave_im = jnp.where(inside, wave_ref[block, 1].astype(jnp.float32), 0.0)
-                masked_ref[tpl, 0, pl.ds(start, WAVE_ROWS), :] = wave_re.astype(jnp.bfloat16)
-                masked_ref[tpl, 1, pl.ds(start, WAVE_ROWS), :] = wave_im.astype(jnp.bfloat16)
-                squares = wave_re * wave_re + wave_im * wave_im
-                total = total + jnp.sum(squares.reshape(-1, 8, COLS), axis=0)
+        for block in range(ROWS // WAVE_ROWS):
+            part = slice(block * WAVE_ROWS, (block + 1) * WAVE_ROWS)
+            bins = (lax.broadcasted_iota(jnp.int32, (WAVE_ROWS, COLS), 0) + part.start) * COLS
+            inside = bins + lax.broadcasted_iota(jnp.int32, (WAVE_ROWS, COLS), 1) < cutoff
+            wave_re = jnp.where(inside, wave_refs[tpl][block, 0].astype(jnp.float32), 0.0)
+            wave_im = jnp.where(inside, wave_refs[tpl][block, 1].astype(jnp.float32), 0.0)
+            masked_ref[tpl, 0, part, :] = wave_re.astype(jnp.bfloat16)
+            masked_ref[tpl, 1, part, :] = wave_im.astype(jnp.bfloat16)
+            squares = wave_re * wave_re + wave_im * wave_im
+            total = total + jnp.sum(squares.reshape(-1, 8, COLS), axis=0)
         sigma_ref[tpl] = jnp.sum(total)
 
 
@@ -263,7 +252,7 @@
 
     if last:
         for tpl in range(count):
-            place = where_ref[5 + tpl]
+            place = where_ref[4 + tpl]
             outputs[0][place] = jnp.max(largest[tpl]) / (2.0 * (sigma_ref[tpl] + eps_norm))
             outputs[1][place] = sigma_ref[tpl] / (ROWS * COLS)
 
@@ -275,18 +264,17 @@
 
 def prepare(cutoffs, lists, where, waves):
     count = len(waves)
-    operands = [piece for wave in waves for piece in wave]
     return pl.pallas_call(
         functools.partial(prepare_kernel, count),
         out_shape=(
             jax.ShapeDtypeStruct((count, 2, ROWS, COLS), jnp.bfloat16),
             jax.ShapeDtypeStruct((count,), jnp.float32),
         ),
-        in_specs=[smem, smem, smem] + [vmem] * len(operands),
+        in_specs=[smem, smem, smem] + [vmem] * count,
         out_specs=(vmem, smem),
         compiler_params=pltpu.CompilerParams(vmem_limit_bytes=VMEM_LIMIT),
         cost_estimate=pl.CostEstimate(flops=2_000_000_000, bytes_accessed=6_000_000, transcendentals=0),
-    )(cutoffs, lists, where, *operands)
+    )(cutoffs, lists, where, *waves)
 
 
 def detector(det, chips, where, sigma, sent, shared, masked, turns, before):
@@ -319,37 +307,31 @@
     devices, groups = lax.axis_size("tpl"), lax.axis_size("grp")
     chips = devices // CORES
     per_device = lists.shape[1]
-    direct = per_device == groups and devices == LINES * QUAD and templates.shape[2] == WAVE_ROWS * COLS
+    direct = per_device == groups and templates.shape[2] == WAVE_ROWS * COLS
     places = [(lax.axis_index("grp") - turn) % groups if direct else turn for turn in range(per_device)]
 
-    chunks = half_chunks(strain_slots, 0, owner)
-    strain_slots, templates, chunks = lax.optimization_barrier((strain_slots, templates, chunks))
-    picked = pick_direct(templates, lists) if direct else collect_plain(templates, lists)
-    near, far = distances(owner)
-    numbers = (me % CORES, near, me, far, me if direct else 0, *places)
-    where = jnp.stack([jnp.asarray(at, jnp.int32) for at in numbers])
-    small = (*slide_turns(slides), where, lists.reshape(-1))
-    for det in range(1, DET):
+    picked = collect(templates, lists) if direct else collect_plain(templates, lists)
+    strain_slots, picked = lax.optimization_barrier((strain_slots, picked))
+    chunks = []
+    for det in range(DET):
         more = half_chunks(strain_slots, det, owner)
         strain_slots, more = lax.optimization_barrier((strain_slots, more))
         chunks += more
-
-    held = {"small": small, "lines": between_lines(picked) if direct else picked, "result": ()}
+    near, far = distances(owner)
+    where = jnp.stack([jnp.asarray(at, jnp.int32) for at in (me % CORES, near, me, far, *places)])
+    small = (*slide_turns(slides), where, lists.reshape(-1))
+
+    held = {"small": small, "arrived": exchange(picked) if direct else picked, "result": ()}
 
     def tie(name, chunk):
         chunk, held[name] = lax.optimization_barrier((chunk, held[name]))
         return chunk
 
-    def after_lines(chunk, sent, shared):
-        chunk = tie("small", tie("lines", chunk))
-        held["blocks"] = inside_quad(held["lines"]) if direct else held["lines"]
-        return chunk
-
-    def after_blocks(chunk, sent, shared):
-        chunk = tie("blocks", chunk)
-        waves = [[across(block, turn) for block in held["blocks"]] for turn in range(per_device)]
-        if not direct:
-            waves = [[block] for block in held["blocks"]]
+    def after_arrived(chunk, sent, shared):
+        chunk = tie("small", tie("arrived", chunk))
+        waves = held["arrived"]
+        if direct:
+            waves = [across(waves, turn) for turn in range(per_device)]
         *_, where, flat_list = held["small"]
         held["masked"] = prepare(cutoffs, flat_list, where, waves)
         return chunk
@@ -369,7 +351,7 @@
 
         return hook
 
-    hooks = dict(zip(STAGE_SLOTS, (after_lines, after_blocks, after_masked)))
+    hooks = {TEMPLATE_SLOT: after_arrived, MASKED_SLOT: after_masked}
     for det in range(DET - 1):
         hooks[(det + 1) * HALF_CHUNKS - 1 + LAG * chips] = after_detector(det)
     sent, shared = spread(chunks, owner, hooks)

time: 147 us -> 128 us (0.87)
  waiting for transfers between devices: 45.8 us -> 27.3 us
  local copies, waits for them, and re-layouts: 24.3 us -> 15.4 us
  starting transfers between devices: 44.4 us -> 52.1 us
  other arithmetic: 8.88 us -> 10.5 us
    ppermute x4 -> x1, waiting for transfers between devices: 14.9 us -> 0.01 us  [across(): lax.ppermute(block, 'grp', [(at, (at + turn) % groups) for at in range(gr...]
    ppermute x18, starting transfers between devices: 26.5 us -> 36.8 us  [spread(): arrived.append(lax.ppermute(here, 'tpl', along))]
    all_to_all x0 -> x1, starting transfers between devices: none -> 7.08 us  [exchange(): return lax.all_to_all(block, 'tpl', split_axis=0, concat_axis=0, tiled=True)]
    squeeze x5 -> x0, local copies, waits for them, and re-layouts: 7.01 us -> none  [the longest x3 4.48 us: between_lines(): picked[flip]]
    ppermute x29 -> x23, waiting for transfers between devices: 9.11 us -> 2.43 us  [swap(): lax.ppermute(block, 'tpl', [(at, at ^ flip) for at in range(lax.axis_size...]
    ppermute x29 -> x23, starting transfers between devices: 13 us -> 6.65 us  [swap(): lax.ppermute(block, 'tpl', [(at, at ^ flip) for at in range(lax.axis_size...]
    slice x5 -> x0, local copies, waits for them, and re-layouts: 5.36 us -> none  [the longest x4 3.82 us: inside_quad(): blocks = [jnp.stack([line[flip] for line in lines]) for flip in range(QUAD)]]
    ppermute x4 -> x1, starting transfers between devices: 5.01 us -> 1.49 us  [across(): lax.ppermute(block, 'grp', [(at, (at + turn) % groups) for at in range(gr...]
  transfers between devices with their start and end apart: 51 -> 43, of which waited for: 15 -> 16; matrix products, arithmetic and copies ran while one was open for 19% -> 11% of each run, Pallas kernels for 10% -> 10%
where the time goes in v9:
time: 128 us; the launch traced here: 127 us
  starting transfers between devices  52.1 us (41%)
  waiting for transfers between devices  27.3 us (21%)
  Pallas kernels  19.6 us (15%)
  local copies, waits for them, and re-layouts  15.4 us (12%)
  other arithmetic  10.5 us (8%)
  between operations  2.01 us (2%)
    ppermute x18, starting transfers between devices, spread(): arrived.append(lax.ppermute(here, 'tpl', along))  36.8 us
    ppermute x18, waiting for transfers between devices, spread(): arrived.append(lax.ppermute(here, 'tpl', along))  24.8 us
    pallas_call x3, Pallas kernels, detector(): pl.pallas_call(functools.partial(detector_kernel, det, chips), out_shape=...  17.5 us
    all_to_all x1, starting transfers between devices, exchange(): return lax.all_to_all(block, 'tpl', split_axis=0, concat_axis=0, tiled=True)  7.08 us
    ppermute x23, starting transfers between devices, swap(): lax.ppermute(block, 'tpl', [(at, at ^ flip) for at in range(lax.axis_size...  6.65 us
    squeeze x3, local copies, waits for them, and re-layouts, half_chunks(): lax.dynamic_slice(strain_slots, (0, det, 0, which * half), (1, 1, 2, half))  5.8 us
    select_n x3, other arithmetic, half_chunks(): first = jnp.where(core == owner % CORES, side(core), got)  4.76 us
    select_n x4, other arithmetic, spread(): here = jnp.where(on_owner_chip, chunks[slot], arrived[slot - LAG])  4.38 us
  transfers between devices with their start and end apart: 43, of which 16 were waited for; matrix products, arithmetic and copies ran while one was open for 11% of the time, Pallas kernels for 10%

profile of v9, /device:TPU:0, one launch (start us, length us, event | category | flops | bytes accessed | tf_op | source)
XLA Modules:
  0.0 126.9 jit_solution(16034247428843571137)
XLA Ops:
  2.2 2.7 %gather_fusion = bf16[16,2,16384]{2,1,0:T(2,128)(2,1)S(1)} fusion(bf16[32,2,16384]{2,1,0:T(2,128)(2,1)S(1)} %copy-done, s32[1024]{0:T(1024)S(1)} %pad_clamp_fusion), kind=kCustom, calls=%fused_computation | custom fusion | bytes 2097216 | tf_op jit(solution)/shard_map/gather | solution.py:118
  4.9 1.6 %reshape.210 = bf16[16,2,32,512]{3,2,1,0:T(8,128)(2,1)} reshape(bf16[16,2,16384]{2,1,0:T(2,128)(2,1)S(1)} %gather_fusion) | data formatting | bytes 2097152 | tf_op jit(solution)/shard_map/reshape | solution.py:118
  6.5 1.4 %dynamic-slice_bitcast_fusion.2 = bf16[2,131072]{1,0:T(2,128)(2,1)S(1)} fusion(bf16[1,3,2,262144]{3,2,1,0:T(2,128)(2,1)} %param.15, s32[]{:T(128)S(6)} %select_n.188), kind=kLoop, calls=%fused_computation.6 | loop fusion | bytes 1048580 | tf_op jit(solution)/shard_map/squeeze | solution.py:73
  9.1 0.8 collective-permute-done
  9.9 1.6 %broadcast_select_fusion.2 = bf16[2,131072]{1,0:T(2,128)(2,1)S(1)} fusion(bf16[2,131072]{1,0:T(2,128)(2,1)S(1)} %collective-permute-done, pred[]{:T(512)S(6)} %eq.43, bf16[1,3,2,262144]{3,2,1,0:T(2,128)(2,1)} %param.15, s32[]{:T(128)S(6)} %select_n.187), kind=kLoop, calls=%fused_computation.3 | loop fusion | flops 262144 | bytes 1572869 | tf_op jit(solution)/shard_map/jit(_where)/select_n | solution.py:75
  12.7 2.2 %dynamic-slice_bitcast_fusion.1 = bf16[2,131072]{1,0:T(2,128)(2,1)} fusion(bf16[1,3,2,262144]{3,2,1,0:T(2,128)(2,1)} %param.15, s32[]{:T(128)S(6)} %select_n.188), kind=kLoop, calls=%fused_computation.5 | loop fusion | bytes 1048580 | tf_op jit(solution)/shard_map/squeeze | solution.py:73
  15.2 7.1 %all-to-all-start = ((bf16[16,2,32,512]{3,2,1,0:T(8,128)(2,1)}), bf16[16,2,32,512]{3,2,1,0:T(8,128)(2,1)S(1)}, u32[]{:S(2)}, u32[]{:S(2)}) async-start(bf16[16,2,32,512]{3,2,1,0:T(8,128)(2,1)} %reshape.210), calls=%async_computation | async-start | bytes 2097152 | tf_op jit(solution)/shard_map/all_to_all | solution.py:122
  22.6 2.0 %collective-permute-start.10 = (bf16[2,128,512]{2,1,0:T(8,128)(2,1)S(1)}, bf16[2,128,512]{2,1,0:T(8,128)(2,1)}, u32[]{:S(2)}, u32[]{:S(2)}) collective-permute-start(bf16[2,128,512]{2,1,0:T(8,128)(2,1)S(1)} %get-tuple-element.45.refs_1_), channel_id=1, source_target_pairs={{0,4},{5,1},{4,8},{9,5},{8,12},{13,9},{12,14},{15,13},{14,10},{11,... | collective-permute-start | bytes 786440 | tf_op jit(solution)/shard_map/ppermute | solution.py:103
  24.6 1.5 %collective-permute-start.3 = (bf16[2,128,512]{2,1,0:T(8,128)(2,1)}, bf16[2,128,512]{2,1,0:T(8,128)(2,1)}, u32[]{:S(2)}, u32[]{:S(2)}) collective-permute-start(bf16[2,128,512]{2,1,0:T(8,128)(2,1)} %get-tuple-element.33.refs_0_), channel_id=1, source_target_pairs={{0,4},{5,1},{4,8},{9,5},{8,12},{13,9},{12,14},{15,13},{14,10},{11,... | collective-permute-start | bytes 786440 | tf_op jit(solution)/shard_map/ppermute | solution.py:103
  26.1 1.6 %broadcast_select_fusion.1 = bf16[2,131072]{1,0:T(2,128)(2,1)S(1)} fusion(bf16[2,131072]{1,0:T(2,128)(2,1)} %collective-permute-done.1, pred[]{:T(512)S(6)} %eq.43, bf16[1,3,2,262144]{3,2,1,0:T(2,128)(2,1)} %param.15, s32[]{:T(128)S(6)} %select_n.187), kind=kLoop, calls=%fused_computation.2 | loop fusion | flops 262144 | bytes 1572869 | tf_op jit(solution)/shard_map/jit(_where)/select_n | solution.py:75
  29.5 2.2 %dynamic-slice_bitcast_fusion = bf16[2,131072]{1,0:T(2,128)(2,1)} fusion(bf16[1,3,2,262144]{3,2,1,0:T(2,128)(2,1)} %param.15, s32[]{:T(128)S(6)} %select_n.188), kind=kLoop, calls=%fused_computation.4 | loop fusion | bytes 1048580 | tf_op jit(solution)/shard_map/squeeze | solution.py:73
  32.6 10.6 %collective-permute-done.10 = bf16[2,128,512]{2,1,0:T(8,128)(2,1)} collective-permute-done((bf16[2,128,512]{2,1,0:T(8,128)(2,1)S(1)}, bf16[2,128,512]{2,1,0:T(8,128)(2,1)}, u32[]{:S(2)}, u32[]{:S(2)}) %collective-permute-start.10) | collective-permute-done | bytes 262176 | tf_op jit(solution)/shard_map/ppermute | solution.py:103
  43.2 1.7 %broadcast_select_fusion.4.refs_3_.refs_1_ = bf16[2,128,512]{2,1,0:T(8,128)(2,1)} fusion(bf16[2,128,512]{2,1,0:T(8,128)(2,1)} %bitcast.48, bf16[2,128,512]{2,1,0:T(8,128)(2,1)} %collective-permute-done.10, pred[]{:T(512)S(6)} %eq.42), kind=kLoop, calls=%fused_computation.14 | loop fusion | flops 131072 | bytes 786433 | tf_op jit(solution)/shard_map/jit(_where)/select_n | solution.py:95
  44.9 7.1 %collective-permute-start.11 = (bf16[2,128,512]{2,1,0:T(8,128)(2,1)}, bf16[2,128,512]{2,1,0:T(8,128)(2,1)}, u32[]{:S(2)}, u32[]{:S(2)}) collective-permute-start(bf16[2,128,512]{2,1,0:T(8,128)(2,1)} %broadcast_select_fusion.4.refs_3_.refs_1_), channel_id=1, source_target_pairs={{0,4},{5,1},{4,8},{9,5},{8,12},{13,9},{12,14},{15,13},{14,10},{11,... | collective-permute-start | bytes 786440 | tf_op jit(solution)/shard_map/ppermute | solution.py:103
  52.0 1.0 broadcast_select_fusion.6.refs_2_.refs_0_
  53.0 2.6 %collective-permute-start.4 = (bf16[2,128,512]{2,1,0:T(8,128)(2,1)S(1)}, bf16[2,128,512]{2,1,0:T(8,128)(2,1)S(1)}, u32[]{:S(2)}, u32[]{:S(2)}) collective-permute-start(bf16[2,128,512]{2,1,0:T(8,128)(2,1)S(1)} %broadcast_select_fusion.6.refs_2_.refs_0_), channel_id=1, source_target_pairs={{0,4},{5,1},{4,8},{9,5},{8,12},{13,9},{12,14},{15,13},{14,10},{11,... | collective-permute-start | bytes 786440 | tf_op jit(solution)/shard_map/ppermute | solution.py:103
  55.7 1.6 %broadcast_select_fusion = bf16[2,131072]{1,0:T(2,128)(2,1)S(1)} fusion(bf16[2,131072]{1,0:T(2,128)(2,1)} %collective-permute-done.2, pred[]{:T(512)S(6)} %eq.43, bf16[1,3,2,262144]{3,2,1,0:T(2,128)(2,1)} %param.15, s32[]{:T(128)S(6)} %select_n.187), kind=kLoop, calls=%fused_computation.1 | loop fusion | flops 262144 | bytes 1572869 | tf_op jit(solution)/shard_map/jit(_where)/select_n | solution.py:75
  58.4 1.1 collective-permute-done.4
  60.3 2.5 %collective-permute-start.5 = (bf16[2,128,512]{2,1,0:T(8,128)(2,1)}, bf16[2,128,512]{2,1,0:T(8,128)(2,1)S(1)}, u32[]{:S(2)}, u32[]{:S(2)}) collective-permute-start(bf16[2,128,512]{2,1,0:T(8,128)(2,1)} %broadcast_select_fusion.5.refs_4_.refs_2_.refs_0_), channel_id=1, source_target_pairs={{0,4},{5,1},{4,8},{9,5},{8,12},{13,9},{12,14},{15,13},{14,10},{11,... | collective-permute-start | bytes 786440 | tf_op jit(solution)/shard_map/ppermute | solution.py:103
  62.8 1.5 %collective-permute-start.9 = (bf16[16,2,32,512]{3,2,1,0:T(8,128)(2,1)S(1)}, bf16[16,2,32,512]{3,2,1,0:T(8,128)(2,1)S(1)}, u32[]{:S(2)}, u32[]{:S(2)}) collective-permute-start(bf16[16,2,32,512]{3,2,1,0:T(8,128)(2,1)S(1)} %all-to-all-done.refs_0_), channel_id=1, source_target_pairs={{0,16},{16,0},{1,17},{17,1},{2,18},{18,2},{3,19},{19,3},{4,20},{20... | collective-permute-start | bytes 3145736 | tf_op jit(solution)/shard_map/ppermute | solution.py:127
  64.3 1.0 broadcast_select_fusion.3.refs_5_.refs_3_.refs_1_
  65.4 2.0 %collective-permute-start.12 = (bf16[2,128,512]{2,1,0:T(8,128)(2,1)S(1)}, bf16[2,128,512]{2,1,0:T(8,128)(2,1)S(1)}, u32[]{:S(2)}, u32[]{:S(2)}) collective-permute-start(bf16[2,128,512]{2,1,0:T(8,128)(2,1)S(1)} %broadcast_select_fusion.3.refs_5_.refs_3_.refs_1_), channel_id=1, source_target_pairs={{0,4},{5,1},{4,8},{9,5},{8,12},{13,9},{12,14},{15,13},{14,10},{11,... | collective-permute-start | bytes 786440 | tf_op jit(solution)/shard_map/ppermute | solution.py:103
  67.4 0.9 collective-permute-done.5.refs_6_.refs_4_.refs_2_
  68.2 1.1 collective-permute-start.6
  69.9 1.9 %collective-permute-done.12.refs_7_.refs_5_.refs_3_ = bf16[2,128,512]{2,1,0:T(8,128)(2,1)S(1)} collective-permute-done((bf16[2,128,512]{2,1,0:T(8,128)(2,1)S(1)}, bf16[2,128,512]{2,1,0:T(8,128)(2,1)S(1)}, u32[]{:S(2)}, u32[]{:S(2)}) %collective-permute-start.12) | collective-permute-done | bytes 262176 | tf_op jit(solution)/shard_map/ppermute | solution.py:103
  71.8 2.0 %collective-permute-start.13 = (bf16[2,128,512]{2,1,0:T(8,128)(2,1)S(1)}, bf16[2,128,512]{2,1,0:T(8,128)(2,1)S(1)}, u32[]{:S(2)}, u32[]{:S(2)}) collective-permute-start(bf16[2,128,512]{2,1,0:T(8,128)(2,1)S(1)} %collective-permute-done.12.refs_7_.refs_5_.refs_3_), channel_id=1, source_target_pairs={{0,4},{5,1},{4,8},{9,5},{8,12},{13,9},{12,14},{15,13},{14,10},{11,... | collective-permute-start | bytes 786440 | tf_op jit(solution)/shard_map/ppermute | solution.py:103
  73.7 0.9 collective-permute-done.6.refs_8_.refs_6_.refs_4_
  74.6 1.9 %collective-permute-start.7 = (bf16[2,128,512]{2,1,0:T(8,128)(2,1)S(1)}, bf16[2,128,512]{2,1,0:T(8,128)(2,1)S(1)}, u32[]{:S(2)}, u32[]{:S(2)}) collective-permute-start(bf16[2,128,512]{2,1,0:T(8,128)(2,1)S(1)} %collective-permute-done.6.refs_8_.refs_6_.refs_4_), channel_id=1, source_target_pairs={{0,4},{5,1},{4,8},{9,5},{8,12},{13,9},{12,14},{15,13},{14,10},{11,... | collective-permute-start | bytes 786440 | tf_op jit(solution)/shard_map/ppermute | solution.py:103
  77.1 1.1 collective-permute-done.13.refs_9_.refs_7_.refs_5_
  78.2 2.0 %collective-permute-start.14 = (bf16[2,128,512]{2,1,0:T(8,128)(2,1)S(1)}, bf16[2,128,512]{2,1,0:T(8,128)(2,1)S(1)}, u32[]{:S(2)}, u32[]{:S(2)}) collective-permute-start(bf16[2,128,512]{2,1,0:T(8,128)(2,1)S(1)} %collective-permute-done.13.refs_9_.refs_7_.refs_5_), channel_id=1, source_target_pairs={{0,4},{5,1},{4,8},{9,5},{8,12},{13,9},{12,14},{15,13},{14,10},{11,... | collective-permute-start | bytes 786440 | tf_op jit(solution)/shard_map/ppermute | solution.py:103
  80.1 0.9 collective-permute-done.7.refs_10_.refs_8_.refs_6_
  81.0 1.9 %collective-permute-start.8 = (bf16[2,128,512]{2,1,0:T(8,128)(2,1)S(1)}, bf16[2,128,512]{2,1,0:T(8,128)(2,1)S(1)}, u32[]{:S(2)}, u32[]{:S(2)}) collective-permute-start(bf16[2,128,512]{2,1,0:T(8,128)(2,1)S(1)} %collective-permute-done.7.refs_10_.refs_8_.refs_6_), channel_id=1, source_target_pairs={{0,4},{5,1},{4,8},{9,5},{8,12},{13,9},{12,14},{15,13},{14,10},{11,... | collective-permute-start | bytes 786440 | tf_op jit(solution)/shard_map/ppermute | solution.py:103
  83.4 1.1 collective-permute-done.14.refs_11_.refs_9_.refs_7_
  84.5 2.0 %collective-permute-start.15 = (bf16[2,128,512]{2,1,0:T(8,128)(2,1)S(1)}, bf16[2,128,512]{2,1,0:T(8,128)(2,1)S(1)}, u32[]{:S(2)}, u32[]{:S(2)}) collective-permute-start(bf16[2,128,512]{2,1,0:T(8,128)(2,1)S(1)} %collective-permute-done.14.refs_11_.refs_9_.refs_7_), channel_id=1, source_target_pairs={{0,4},{5,1},{4,8},{9,5},{8,12},{13,9},{12,14},{15,13},{14,10},{11,... | collective-permute-start | bytes 786440 | tf_op jit(solution)/shard_map/ppermute | solution.py:103
  86.5 0.9 collective-permute-done.8.refs_12_.refs_10_.refs_8_
  87.9 2.1 %shard_map.158 = (bf16[2,2,512,512]{3,2,1,0:T(8,128)(2,1)S(1)}, f32[2]{0:T(128)S(1)}) custom-call(s32[32]{0:T(128)S(1)} %copy-done.5, s32[32]{0:T(128)S(1)} %reshape.217.list_ref, s32[6]{0:T(128)S(1)} %stack.27.where_ref, bf16[16,2,32,512]{3,2,1,0:T(8,128)(2,1)S(1)} %all-to-all-done.refs_0_, bf16[16,2,32,512]{3,2,1,0:T(8,128)(2,1)S(1)} %collective-permute-done.9.refs_1_), custom_call_target="tpu_custom_call" | custom-call | flops 2000000000 | bytes 6000000 | tf_op jit(solution)/shard_map/pallas_call | solution.py:267
  90.9 2.0 %collective-permute-start.17 = (bf16[2,128,512]{2,1,0:T(8,128)(2,1)S(1)}, bf16[2,128,512]{2,1,0:T(8,128)(2,1)S(1)}, u32[]{:S(2)}, u32[]{:S(2)}) collective-permute-start(bf16[2,128,512]{2,1,0:T(8,128)(2,1)S(1)} %collective-permute-done.15.refs_13_.refs_11_.refs_9_), channel_id=1, source_target_pairs={{0,4},{5,1},{4,8},{9,5},{8,12},{13,9},{12,14},{15,13},{14,10},{11,... | collective-permute-start | bytes 786440 | tf_op jit(solution)/shard_map/ppermute | solution.py:103
  92.9 0.9 collective-permute-start.16
  94.5 2.8 %collective-permute-done.17.refs_15_.refs_13_.refs_11_ = bf16[2,128,512]{2,1,0:T(8,128)(2,1)S(1)} collective-permute-done((bf16[2,128,512]{2,1,0:T(8,128)(2,1)S(1)}, bf16[2,128,512]{2,1,0:T(8,128)(2,1)S(1)}, u32[]{:S(2)}, u32[]{:S(2)}) %collective-permute-start.17) | collective-permute-done | bytes 262176 | tf_op jit(solution)/shard_map/ppermute | solution.py:103
  97.8 2.3 %collective-permute-done.16.refs_14_.refs_12_.refs_10_ = bf16[2,128,512]{2,1,0:T(8,128)(2,1)S(1)} collective-permute-done((bf16[2,128,512]{2,1,0:T(8,128)(2,1)S(1)}, bf16[2,128,512]{2,1,0:T(8,128)(2,1)S(1)}, u32[]{:S(2)}, u32[]{:S(2)}) %collective-permute-start.16) | collective-permute-done | bytes 262176 | tf_op jit(solution)/shard_map/ppermute | solution.py:103
  100.1 2.0 %collective-permute-start.19 = (bf16[2,128,512]{2,1,0:T(8,128)(2,1)S(1)}, bf16[2,128,512]{2,1,0:T(8,128)(2,1)S(1)}, u32[]{:S(2)}, u32[]{:S(2)}) collective-permute-start(bf16[2,128,512]{2,1,0:T(8,128)(2,1)S(1)} %collective-permute-done.17.refs_15_.refs_13_.refs_11_), channel_id=1, source_target_pairs={{0,4},{5,1},{4,8},{9,5},{8,12},{13,9},{12,14},{15,13},{14,10},{11,... | collective-permute-start | bytes 786440 | tf_op jit(solution)/shard_map/ppermute | solution.py:103
  103.0 5.6 %shard_map.159.refs_38_ = f32[2,512,512]{2,1,0:T(8,128)S(1)} custom-call(s32[6]{0:T(128)S(1)} %stack.27.where_ref, f32[2]{0:T(128)S(1)} %get-tuple-element.42.sigma_ref, bf16[2,128,512]{2,1,0:T(8,128)(2,1)S(1)} %copy-done.1, bf16[2,128,512]{2,1,0:T(8,128)(2,1)S(1)} %get-tuple-element.45.refs_1_, bf16[2,128,512]{2,1,0:T(8,128)(2,1)S(1)} %copy-done.4, ...), custom_call_target="tpu_custom_call" | custom-call | flops 5000000000 | bytes 10000000 | tf_op jit(solution)/shard_map/pallas_call | solution.py:287
  108.5 0.9 collective-permute-start.39
  109.6 1.7 %collective-permute-start.37 = (bf16[2,128,512]{2,1,0:T(8,128)(2,1)S(1)}, bf16[2,128,512]{2,1,0:T(8,128)(2,1)S(1)}, u32[]{:S(2)}, u32[]{:S(2)}) collective-permute-start(bf16[2,128,512]{2,1,0:T(8,128)(2,1)S(1)} %collective-permute-done.19.refs_15_.refs_13_), channel_id=1, source_target_pairs={{0,4},{5,1},{4,8},{9,5},{8,12},{13,9},{12,14},{15,13},{14,10},{11,... | collective-permute-start | bytes 786440 | tf_op jit(solution)/shard_map/ppermute | solution.py:103
  112.1 5.6 %shard_map.160.refs_38_ = f32[2,512,512]{2,1,0:T(8,128)S(1)} custom-call(s32[6]{0:T(128)S(1)} %stack.27.where_ref, f32[2]{0:T(128)S(1)} %get-tuple-element.42.sigma_ref, bf16[2,128,512]{2,1,0:T(8,128)(2,1)S(1)} %copy-done.4, bf16[2,128,512]{2,1,0:T(8,128)(2,1)} %broadcast_select_fusion.4.refs_3_.refs_1_, bf16[2,128,512]{2,1,0:T(8,128)(2,1)S(1)} %copy-done.2, ...), custom_call_target="tpu_custom_call" | custom-call | flops 5000000000 | bytes 10000000 | tf_op jit(solution)/shard_map/pallas_call | solution.py:287
  117.7 0.9 collective-permute-start.41
  118.8 1.0 collective-permute-done.41.refs_31_
  120.3 6.4 %shard_map.161 = (f32[2]{0:T(128)}, f32[2]{0:T(128)}) custom-call(s32[6]{0:T(128)S(1)} %stack.27.where_ref, f32[2]{0:T(128)S(1)} %get-tuple-element.42.sigma_ref, bf16[2,128,512]{2,1,0:T(8,128)(2,1)S(1)} %copy-done.2, bf16[2,128,512]{2,1,0:T(8,128)(2,1)S(1)} %broadcast_select_fusion.3.refs_5_.refs_3_.refs_1_, ...), custom_call_target="tpu_custom_call" | custom-call | flops 5000000000 | bytes 10000000 | tf_op jit(solution)/shard_map/pallas_call | solution.py:287
  (94 shorter events, 15.0 us)
Async XLA Ops:
  7.9 2.1 %collective-permute-start = (bf16[2,131072]{1,0:T(2,128)(2,1)S(1)}, bf16[2,131072]{1,0:T(2,128)(2,1)S(1)}, u32[]{:S(2)}, u32[]{:S(2)}) collective-permute-start(bf16[2,131072]{1,0:T(2,128)(2,1)S(1)} %dynamic-slice_bitcast_fusion.2), channel_id=1, source_target_pairs={{0,1},{1,0},{2,3},{3,2},{4,5},{5,4},{6,7},{7,6},{8,9},{9,8},{10,11... | collective-permute-start | bytes 1572872 | tf_op jit(solution)/shard_map/ppermute | solution.py:66
  14.9 11.2 %collective-permute-start.1 = (bf16[2,131072]{1,0:T(2,128)(2,1)}, bf16[2,131072]{1,0:T(2,128)(2,1)}, u32[]{:S(2)}, u32[]{:S(2)}) collective-permute-start(bf16[2,131072]{1,0:T(2,128)(2,1)} %dynamic-slice_bitcast_fusion.1), channel_id=1, source_target_pairs={{0,1},{1,0},{2,3},{3,2},{4,5},{5,4},{6,7},{7,6},{8,9},{9,8},{10,11... | collective-permute-start | bytes 1572872 | tf_op jit(solution)/shard_map/ppermute | solution.py:66
  15.2 45.1 %all-to-all-start = ((bf16[16,2,32,512]{3,2,1,0:T(8,128)(2,1)}), bf16[16,2,32,512]{3,2,1,0:T(8,128)(2,1)S(1)}, u32[]{:S(2)}, u32[]{:S(2)}) async-start(bf16[16,2,32,512]{3,2,1,0:T(8,128)(2,1)} %reshape.210), calls=%async_computation | async-start | bytes 2097152 | tf_op jit(solution)/shard_map/all_to_all | solution.py:122
  22.6 20.6 %collective-permute-start.10 = (bf16[2,128,512]{2,1,0:T(8,128)(2,1)S(1)}, bf16[2,128,512]{2,1,0:T(8,128)(2,1)}, u32[]{:S(2)}, u32[]{:S(2)}) collective-permute-start(bf16[2,128,512]{2,1,0:T(8,128)(2,1)S(1)} %get-tuple-element.45.refs_1_), channel_id=1, source_target_pairs={{0,4},{5,1},{4,8},{9,5},{8,12},{13,9},{12,14},{15,13},{14,10},{11,... | collective-permute-start | bytes 786440 | tf_op jit(solution)/shard_map/ppermute | solution.py:103
  24.6 27.4 %collective-permute-start.3 = (bf16[2,128,512]{2,1,0:T(8,128)(2,1)}, bf16[2,128,512]{2,1,0:T(8,128)(2,1)}, u32[]{:S(2)}, u32[]{:S(2)}) collective-permute-start(bf16[2,128,512]{2,1,0:T(8,128)(2,1)} %get-tuple-element.33.refs_0_), channel_id=1, source_target_pairs={{0,4},{5,1},{4,8},{9,5},{8,12},{13,9},{12,14},{15,13},{14,10},{11,... | collective-permute-start | bytes 786440 | tf_op jit(solution)/shard_map/ppermute | solution.py:103
  31.7 24.0 %collective-permute-start.2 = (bf16[2,131072]{1,0:T(2,128)(2,1)}, bf16[2,131072]{1,0:T(2,128)(2,1)}, u32[]{:S(2)}, u32[]{:S(2)}) collective-permute-start(bf16[2,131072]{1,0:T(2,128)(2,1)} %dynamic-slice_bitcast_fusion), channel_id=1, source_target_pairs={{0,1},{1,0},{2,3},{3,2},{4,5},{5,4},{6,7},{7,6},{8,9},{9,8},{10,11... | collective-permute-start | bytes 1572872 | tf_op jit(solution)/shard_map/ppermute | solution.py:66
  44.9 43.0 %copy-start.5 = (s32[32]{0:T(128)S(1)}, s32[32]{0:T(128)}, u32[]{:S(2)}) copy-start(s32[32]{0:T(128)} %cut_ref.1) | copy-start | bytes 388
  44.9 19.4 %collective-permute-start.11 = (bf16[2,128,512]{2,1,0:T(8,128)(2,1)}, bf16[2,128,512]{2,1,0:T(8,128)(2,1)}, u32[]{:S(2)}, u32[]{:S(2)}) collective-permute-start(bf16[2,128,512]{2,1,0:T(8,128)(2,1)} %broadcast_select_fusion.4.refs_3_.refs_1_), channel_id=1, source_target_pairs={{0,4},{5,1},{4,8},{9,5},{8,12},{13,9},{12,14},{15,13},{14,10},{11,... | collective-permute-start | bytes 786440 | tf_op jit(solution)/shard_map/ppermute | solution.py:103
  53.0 6.5 %collective-permute-start.4 = (bf16[2,128,512]{2,1,0:T(8,128)(2,1)S(1)}, bf16[2,128,512]{2,1,0:T(8,128)(2,1)S(1)}, u32[]{:S(2)}, u32[]{:S(2)}) collective-permute-start(bf16[2,128,512]{2,1,0:T(8,128)(2,1)S(1)} %broadcast_select_fusion.6.refs_2_.refs_0_), channel_id=1, source_target_pairs={{0,4},{5,1},{4,8},{9,5},{8,12},{13,9},{12,14},{15,13},{14,10},{11,... | collective-permute-start | bytes 786440 | tf_op jit(solution)/shard_map/ppermute | solution.py:103
  60.3 7.9 %collective-permute-start.5 = (bf16[2,128,512]{2,1,0:T(8,128)(2,1)}, bf16[2,128,512]{2,1,0:T(8,128)(2,1)S(1)}, u32[]{:S(2)}, u32[]{:S(2)}) collective-permute-start(bf16[2,128,512]{2,1,0:T(8,128)(2,1)} %broadcast_select_fusion.5.refs_4_.refs_2_.refs_0_), channel_id=1, source_target_pairs={{0,4},{5,1},{4,8},{9,5},{8,12},{13,9},{12,14},{15,13},{14,10},{11,... | collective-permute-start | bytes 786440 | tf_op jit(solution)/shard_map/ppermute | solution.py:103
  62.8 24.6 %collective-permute-start.9 = (bf16[16,2,32,512]{3,2,1,0:T(8,128)(2,1)S(1)}, bf16[16,2,32,512]{3,2,1,0:T(8,128)(2,1)S(1)}, u32[]{:S(2)}, u32[]{:S(2)}) collective-permute-start(bf16[16,2,32,512]{3,2,1,0:T(8,128)(2,1)S(1)} %all-to-all-done.refs_0_), channel_id=1, source_target_pairs={{0,16},{16,0},{1,17},{17,1},{2,18},{18,2},{3,19},{19,3},{4,20},{20... | collective-permute-start | bytes 3145736 | tf_op jit(solution)/shard_map/ppermute | solution.py:127
  65.3 37.6 %copy-start.1 = (bf16[2,128,512]{2,1,0:T(8,128)(2,1)S(1)}, bf16[2,128,512]{2,1,0:T(8,128)(2,1)}, u32[]{:S(2)}) copy-start(bf16[2,128,512]{2,1,0:T(8,128)(2,1)} %get-tuple-element.33.refs_0_) | copy-start | bytes 786436
  65.3 37.6 %copy-start.2 = (bf16[2,128,512]{2,1,0:T(8,128)(2,1)S(1)}, bf16[2,128,512]{2,1,0:T(8,128)(2,1)}, u32[]{:S(2)}) copy-start(bf16[2,128,512]{2,1,0:T(8,128)(2,1)} %broadcast_select_fusion.5.refs_4_.refs_2_.refs_0_) | copy-start | bytes 786436
  65.3 37.6 %copy-start.4 = (bf16[2,128,512]{2,1,0:T(8,128)(2,1)S(1)}, bf16[2,128,512]{2,1,0:T(8,128)(2,1)}, u32[]{:S(2)}) copy-start(bf16[2,128,512]{2,1,0:T(8,128)(2,1)} %copy-done.3) | copy-start | bytes 786436
  65.3 37.6 %copy-start.6 = (f32[4,2,128,512]{3,2,1,0:T(8,128)S(1)}, f32[4,2,128,512]{3,2,1,0:T(8,128)}, u32[]{:S(2)}) copy-start(f32[4,2,128,512]{3,2,1,0:T(8,128)} %constant.174.clone.refs_37_) | copy-start | bytes 6291460
  65.4 6.4 %collective-permute-start.12 = (bf16[2,128,512]{2,1,0:T(8,128)(2,1)S(1)}, bf16[2,128,512]{2,1,0:T(8,128)(2,1)S(1)}, u32[]{:S(2)}, u32[]{:S(2)}) collective-permute-start(bf16[2,128,512]{2,1,0:T(8,128)(2,1)S(1)} %broadcast_select_fusion.3.refs_5_.refs_3_.refs_1_), channel_id=1, source_target_pairs={{0,4},{5,1},{4,8},{9,5},{8,12},{13,9},{12,14},{15,13},{14,10},{11,... | collective-permute-start | bytes 786440 | tf_op jit(solution)/shard_map/ppermute | solution.py:103
  68.2 6.4 %collective-permute-start.6 = (bf16[2,128,512]{2,1,0:T(8,128)(2,1)S(1)}, bf16[2,128,512]{2,1,0:T(8,128)(2,1)S(1)}, u32[]{:S(2)}, u32[]{:S(2)}) collective-permute-start(bf16[2,128,512]{2,1,0:T(8,128)(2,1)S(1)} %collective-permute-done.5.refs_6_.refs_4_.refs_2_), channel_id=1, source_target_pairs={{0,4},{5,1},{4,8},{9,5},{8,12},{13,9},{12,14},{15,13},{14,10},{11,... | collective-permute-start | bytes 786440 | tf_op jit(solution)/shard_map/ppermute | solution.py:103
  69.4 7.2 %collective-permute-start.20 = (bf16[2,128,512]{2,1,0:T(8,128)(2,1)}, bf16[2,128,512]{2,1,0:T(8,128)(2,1)S(1)}, u32[]{:S(2)}, u32[]{:S(2)}) collective-permute-start(bf16[2,128,512]{2,1,0:T(8,128)(2,1)} %get-tuple-element.33.refs_0_), channel_id=1, source_target_pairs={{0,1},{1,0},{2,3},{3,2},{4,5},{5,4},{6,7},{7,6},{8,9},{9,8},{10,11... | collective-permute-start | bytes 786440 | tf_op jit(solution)/shard_map/ppermute | solution.py:66
  69.4 7.2 %collective-permute-start.21 = (bf16[2,128,512]{2,1,0:T(8,128)(2,1)S(1)}, bf16[2,128,512]{2,1,0:T(8,128)(2,1)S(1)}, u32[]{:S(2)}, u32[]{:S(2)}) collective-permute-start(bf16[2,128,512]{2,1,0:T(8,128)(2,1)S(1)} %get-tuple-element.45.refs_1_), channel_id=1, source_target_pairs={{0,1},{1,0},{2,3},{3,2},{4,5},{5,4},{6,7},{7,6},{8,9},{9,8},{10,11... | collective-permute-start | bytes 786440 | tf_op jit(solution)/shard_map/ppermute | solution.py:66
  71.8 6.4 %collective-permute-start.13 = (bf16[2,128,512]{2,1,0:T(8,128)(2,1)S(1)}, bf16[2,128,512]{2,1,0:T(8,128)(2,1)S(1)}, u32[]{:S(2)}, u32[]{:S(2)}) collective-permute-start(bf16[2,128,512]{2,1,0:T(8,128)(2,1)S(1)} %collective-permute-done.12.refs_7_.refs_5_.refs_3_), channel_id=1, source_target_pairs={{0,4},{5,1},{4,8},{9,5},{8,12},{13,9},{12,14},{15,13},{14,10},{11,... | collective-permute-start | bytes 786440 | tf_op jit(solution)/shard_map/ppermute | solution.py:103
  74.6 6.4 %collective-permute-start.7 = (bf16[2,128,512]{2,1,0:T(8,128)(2,1)S(1)}, bf16[2,128,512]{2,1,0:T(8,128)(2,1)S(1)}, u32[]{:S(2)}, u32[]{:S(2)}) collective-permute-start(bf16[2,128,512]{2,1,0:T(8,128)(2,1)S(1)} %collective-permute-done.6.refs_8_.refs_6_.refs_4_), channel_id=1, source_target_pairs={{0,4},{5,1},{4,8},{9,5},{8,12},{13,9},{12,14},{15,13},{14,10},{11,... | collective-permute-start | bytes 786440 | tf_op jit(solution)/shard_map/ppermute | solution.py:103
  76.6 6.4 %collective-permute-start.23 = (bf16[2,128,512]{2,1,0:T(8,128)(2,1)}, bf16[2,128,512]{2,1,0:T(8,128)(2,1)S(1)}, u32[]{:S(2)}, u32[]{:S(2)}) collective-permute-start(bf16[2,128,512]{2,1,0:T(8,128)(2,1)} %broadcast_select_fusion.4.refs_3_.refs_1_), channel_id=1, source_target_pairs={{0,1},{1,0},{2,3},{3,2},{4,5},{5,4},{6,7},{7,6},{8,9},{9,8},{10,11... | collective-permute-start | bytes 786440 | tf_op jit(solution)/shard_map/ppermute | solution.py:66
  76.6 6.4 %collective-permute-start.22 = (bf16[2,128,512]{2,1,0:T(8,128)(2,1)}, bf16[2,128,512]{2,1,0:T(8,128)(2,1)S(1)}, u32[]{:S(2)}, u32[]{:S(2)}) collective-permute-start(bf16[2,128,512]{2,1,0:T(8,128)(2,1)} %copy-done.3), channel_id=1, source_target_pairs={{0,1},{1,0},{2,3},{3,2},{4,5},{5,4},{6,7},{7,6},{8,9},{9,8},{10,11... | collective-permute-start | bytes 786440 | tf_op jit(solution)/shard_map/ppermute | solution.py:66
  78.2 6.4 %collective-permute-start.14 = (bf16[2,128,512]{2,1,0:T(8,128)(2,1)S(1)}, bf16[2,128,512]{2,1,0:T(8,128)(2,1)S(1)}, u32[]{:S(2)}, u32[]{:S(2)}) collective-permute-start(bf16[2,128,512]{2,1,0:T(8,128)(2,1)S(1)} %collective-permute-done.13.refs_9_.refs_7_.refs_5_), channel_id=1, source_target_pairs={{0,4},{5,1},{4,8},{9,5},{8,12},{13,9},{12,14},{15,13},{14,10},{11,... | collective-permute-start | bytes 786440 | tf_op jit(solution)/shard_map/ppermute | solution.py:103
  81.0 6.4 %collective-permute-start.8 = (bf16[2,128,512]{2,1,0:T(8,128)(2,1)S(1)}, bf16[2,128,512]{2,1,0:T(8,128)(2,1)S(1)}, u32[]{:S(2)}, u32[]{:S(2)}) collective-permute-start(bf16[2,128,512]{2,1,0:T(8,128)(2,1)S(1)} %collective-permute-done.7.refs_10_.refs_8_.refs_6_), channel_id=1, source_target_pairs={{0,4},{5,1},{4,8},{9,5},{8,12},{13,9},{12,14},{15,13},{14,10},{11,... | collective-permute-start | bytes 786440 | tf_op jit(solution)/shard_map/ppermute | solution.py:103
  82.9 7.1 %collective-permute-start.25 = (bf16[2,128,512]{2,1,0:T(8,128)(2,1)S(1)}, bf16[2,128,512]{2,1,0:T(8,128)(2,1)S(1)}, u32[]{:S(2)}, u32[]{:S(2)}) collective-permute-start(bf16[2,128,512]{2,1,0:T(8,128)(2,1)S(1)} %broadcast_select_fusion.3.refs_5_.refs_3_.refs_1_), channel_id=1, source_target_pairs={{0,1},{1,0},{2,3},{3,2},{4,5},{5,4},{6,7},{7,6},{8,9},{9,8},{10,11... | collective-permute-start | bytes 786440 | tf_op jit(solution)/shard_map/ppermute | solution.py:66
  82.9 7.1 %collective-permute-start.27 = (bf16[2,128,512]{2,1,0:T(8,128)(2,1)S(1)}, bf16[2,128,512]{2,1,0:T(8,128)(2,1)S(1)}, u32[]{:S(2)}, u32[]{:S(2)}) collective-permute-start(bf16[2,128,512]{2,1,0:T(8,128)(2,1)S(1)} %collective-permute-done.12.refs_7_.refs_5_.refs_3_), channel_id=1, source_target_pairs={{0,1},{1,0},{2,3},{3,2},{4,5},{5,4},{6,7},{7,6},{8,9},{9,8},{10,11... | collective-permute-start | bytes 786440 | tf_op jit(solution)/shard_map/ppermute | solution.py:66
  84.5 6.4 %collective-permute-start.15 = (bf16[2,128,512]{2,1,0:T(8,128)(2,1)S(1)}, bf16[2,128,512]{2,1,0:T(8,128)(2,1)S(1)}, u32[]{:S(2)}, u32[]{:S(2)}) collective-permute-start(bf16[2,128,512]{2,1,0:T(8,128)(2,1)S(1)} %collective-permute-done.14.refs_11_.refs_9_.refs_7_), channel_id=1, source_target_pairs={{0,4},{5,1},{4,8},{9,5},{8,12},{13,9},{12,14},{15,13},{14,10},{11,... | collective-permute-start | bytes 786440 | tf_op jit(solution)/shard_map/ppermute | solution.py:103
  87.4 5.5 %collective-permute-start.24 = (bf16[2,128,512]{2,1,0:T(8,128)(2,1)}, bf16[2,128,512]{2,1,0:T(8,128)(2,1)S(1)}, u32[]{:S(2)}, u32[]{:S(2)}) collective-permute-start(bf16[2,128,512]{2,1,0:T(8,128)(2,1)} %broadcast_select_fusion.5.refs_4_.refs_2_.refs_0_), channel_id=1, source_target_pairs={{0,1},{1,0},{2,3},{3,2},{4,5},{5,4},{6,7},{7,6},{8,9},{9,8},{10,11... | collective-permute-start | bytes 786440 | tf_op jit(solution)/shard_map/ppermute | solution.py:66
  87.4 5.5 %collective-permute-start.29 = (bf16[2,128,512]{2,1,0:T(8,128)(2,1)S(1)}, bf16[2,128,512]{2,1,0:T(8,128)(2,1)S(1)}, u32[]{:S(2)}, u32[]{:S(2)}) collective-permute-start(bf16[2,128,512]{2,1,0:T(8,128)(2,1)S(1)} %collective-permute-done.13.refs_9_.refs_7_.refs_5_), channel_id=1, source_target_pairs={{0,1},{1,0},{2,3},{3,2},{4,5},{5,4},{6,7},{7,6},{8,9},{9,8},{10,11... | collective-permute-start | bytes 786440 | tf_op jit(solution)/shard_map/ppermute | solution.py:66
  90.0 3.8 %collective-permute-start.26 = (bf16[2,128,512]{2,1,0:T(8,128)(2,1)S(1)}, bf16[2,128,512]{2,1,0:T(8,128)(2,1)S(1)}, u32[]{:S(2)}, u32[]{:S(2)}) collective-permute-start(bf16[2,128,512]{2,1,0:T(8,128)(2,1)S(1)} %collective-permute-done.5.refs_6_.refs_4_.refs_2_), channel_id=1, source_target_pairs={{0,1},{1,0},{2,3},{3,2},{4,5},{5,4},{6,7},{7,6},{8,9},{9,8},{10,11... | collective-permute-start | bytes 786440 | tf_op jit(solution)/shard_map/ppermute | solution.py:66
  90.1 4.3 %collective-permute-start.31 = (bf16[2,128,512]{2,1,0:T(8,128)(2,1)S(1)}, bf16[2,128,512]{2,1,0:T(8,128)(2,1)S(1)}, u32[]{:S(2)}, u32[]{:S(2)}) collective-permute-start(bf16[2,128,512]{2,1,0:T(8,128)(2,1)S(1)} %collective-permute-done.14.refs_11_.refs_9_.refs_7_), channel_id=1, source_target_pairs={{0,1},{1,0},{2,3},{3,2},{4,5},{5,4},{6,7},{7,6},{8,9},{9,8},{10,11... | collective-permute-start | bytes 786440 | tf_op jit(solution)/shard_map/ppermute | solution.py:66
  90.9 6.4 %collective-permute-start.17 = (bf16[2,128,512]{2,1,0:T(8,128)(2,1)S(1)}, bf16[2,128,512]{2,1,0:T(8,128)(2,1)S(1)}, u32[]{:S(2)}, u32[]{:S(2)}) collective-permute-start(bf16[2,128,512]{2,1,0:T(8,128)(2,1)S(1)} %collective-permute-done.15.refs_13_.refs_11_.refs_9_), channel_id=1, source_target_pairs={{0,4},{5,1},{4,8},{9,5},{8,12},{13,9},{12,14},{15,13},{14,10},{11,... | collective-permute-start | bytes 786440 | tf_op jit(solution)/shard_map/ppermute | solution.py:103
  92.9 4.4 %collective-permute-start.28 = (bf16[2,128,512]{2,1,0:T(8,128)(2,1)S(1)}, bf16[2,128,512]{2,1,0:T(8,128)(2,1)S(1)}, u32[]{:S(2)}, u32[]{:S(2)}) collective-permute-start(bf16[2,128,512]{2,1,0:T(8,128)(2,1)S(1)} %collective-permute-done.6.refs_8_.refs_6_.refs_4_), channel_id=1, source_target_pairs={{0,1},{1,0},{2,3},{3,2},{4,5},{5,4},{6,7},{7,6},{8,9},{9,8},{10,11... | collective-permute-start | bytes 786440 | tf_op jit(solution)/shard_map/ppermute | solution.py:66
  92.9 7.2 %collective-permute-start.16 = (bf16[2,128,512]{2,1,0:T(8,128)(2,1)S(1)}, bf16[2,128,512]{2,1,0:T(8,128)(2,1)S(1)}, u32[]{:S(2)}, u32[]{:S(2)}) collective-permute-start(bf16[2,128,512]{2,1,0:T(8,128)(2,1)S(1)} %collective-permute-done.8.refs_12_.refs_10_.refs_8_), channel_id=1, source_target_pairs={{0,4},{5,1},{4,8},{9,5},{8,12},{13,9},{12,14},{15,13},{14,10},{11,... | collective-permute-start | bytes 786440 | tf_op jit(solution)/shard_map/ppermute | solution.py:103
  93.8 6.3 %collective-permute-start.33 = (bf16[2,128,512]{2,1,0:T(8,128)(2,1)S(1)}, bf16[2,128,512]{2,1,0:T(8,128)(2,1)S(1)}, u32[]{:S(2)}, u32[]{:S(2)}) collective-permute-start(bf16[2,128,512]{2,1,0:T(8,128)(2,1)S(1)} %collective-permute-done.15.refs_13_.refs_11_.refs_9_), channel_id=1, source_target_pairs={{0,1},{1,0},{2,3},{3,2},{4,5},{5,4},{6,7},{7,6},{8,9},{9,8},{10,11... | collective-permute-start | bytes 786440 | tf_op jit(solution)/shard_map/ppermute | solution.py:66
  94.4 7.7 %collective-permute-start.30 = (bf16[2,128,512]{2,1,0:T(8,128)(2,1)S(1)}, bf16[2,128,512]{2,1,0:T(8,128)(2,1)S(1)}, u32[]{:S(2)}, u32[]{:S(2)}) collective-permute-start(bf16[2,128,512]{2,1,0:T(8,128)(2,1)S(1)} %collective-permute-done.7.refs_10_.refs_8_.refs_6_), channel_id=1, source_target_pairs={{0,1},{1,0},{2,3},{3,2},{4,5},{5,4},{6,7},{7,6},{8,9},{9,8},{10,11... | collective-permute-start | bytes 786440 | tf_op jit(solution)/shard_map/ppermute | solution.py:66
  97.3 5.6 %collective-permute-start.35 = (bf16[2,128,512]{2,1,0:T(8,128)(2,1)S(1)}, bf16[2,128,512]{2,1,0:T(8,128)(2,1)S(1)}, u32[]{:S(2)}, u32[]{:S(2)}) collective-permute-start(bf16[2,128,512]{2,1,0:T(8,128)(2,1)S(1)} %collective-permute-done.17.refs_15_.refs_13_.refs_11_), channel_id=1, source_target_pairs={{0,1},{1,0},{2,3},{3,2},{4,5},{5,4},{6,7},{7,6},{8,9},{9,8},{10,11... | collective-permute-start | bytes 786440 | tf_op jit(solution)/shard_map/ppermute | solution.py:66
  97.3 5.6 %collective-permute-start.32 = (bf16[2,128,512]{2,1,0:T(8,128)(2,1)S(1)}, bf16[2,128,512]{2,1,0:T(8,128)(2,1)S(1)}, u32[]{:S(2)}, u32[]{:S(2)}) collective-permute-start(bf16[2,128,512]{2,1,0:T(8,128)(2,1)S(1)} %collective-permute-done.8.refs_12_.refs_10_.refs_8_), channel_id=1, source_target_pairs={{0,1},{1,0},{2,3},{3,2},{4,5},{5,4},{6,7},{7,6},{8,9},{9,8},{10,11... | collective-permute-start | bytes 786440 | tf_op jit(solution)/shard_map/ppermute | solution.py:66
  100.1 2.8 %collective-permute-start.34 = (bf16[2,128,512]{2,1,0:T(8,128)(2,1)S(1)}, bf16[2,128,512]{2,1,0:T(8,128)(2,1)S(1)}, u32[]{:S(2)}, u32[]{:S(2)}) collective-permute-start(bf16[2,128,512]{2,1,0:T(8,128)(2,1)S(1)} %collective-permute-done.16.refs_14_.refs_12_.refs_10_), channel_id=1, source_target_pairs={{0,1},{1,0},{2,3},{3,2},{4,5},{5,4},{6,7},{7,6},{8,9},{9,8},{10,11... | collective-permute-start | bytes 786440 | tf_op jit(solution)/shard_map/ppermute | solution.py:66
  100.1 8.4 %collective-permute-start.19 = (bf16[2,128,512]{2,1,0:T(8,128)(2,1)S(1)}, bf16[2,128,512]{2,1,0:T(8,128)(2,1)S(1)}, u32[]{:S(2)}, u32[]{:S(2)}) collective-permute-start(bf16[2,128,512]{2,1,0:T(8,128)(2,1)S(1)} %collective-permute-done.17.refs_15_.refs_13_.refs_11_), channel_id=1, source_target_pairs={{0,4},{5,1},{4,8},{9,5},{8,12},{13,9},{12,14},{15,13},{14,10},{11,... | collective-permute-start | bytes 786440 | tf_op jit(solution)/shard_map/ppermute | solution.py:103
  102.1 7.4 %collective-permute-start.18 = (bf16[2,128,512]{2,1,0:T(8,128)(2,1)S(1)}, bf16[2,128,512]{2,1,0:T(8,128)(2,1)S(1)}, u32[]{:S(2)}, u32[]{:S(2)}) collective-permute-start(bf16[2,128,512]{2,1,0:T(8,128)(2,1)S(1)} %collective-permute-done.16.refs_14_.refs_12_.refs_10_), channel_id=1, source_target_pairs={{0,4},{5,1},{4,8},{9,5},{8,12},{13,9},{12,14},{15,13},{14,10},{11,... | collective-permute-start | bytes 786440 | tf_op jit(solution)/shard_map/ppermute | solution.py:103
  108.5 3.5 %collective-permute-start.39 = (bf16[2,128,512]{2,1,0:T(8,128)(2,1)S(1)}, bf16[2,128,512]{2,1,0:T(8,128)(2,1)S(1)}, u32[]{:S(2)}, u32[]{:S(2)}) collective-permute-start(bf16[2,128,512]{2,1,0:T(8,128)(2,1)S(1)} %collective-permute-done.19.refs_15_.refs_13_), channel_id=1, source_target_pairs={{0,1},{1,0},{2,3},{3,2},{4,5},{5,4},{6,7},{7,6},{8,9},{9,8},{10,11... | collective-permute-start | bytes 786440 | tf_op jit(solution)/shard_map/ppermute | solution.py:66
  109.5 2.6 %collective-permute-start.38 = (bf16[2,128,512]{2,1,0:T(8,128)(2,1)S(1)}, bf16[2,128,512]{2,1,0:T(8,128)(2,1)S(1)}, u32[]{:S(2)}, u32[]{:S(2)}) collective-permute-start(bf16[2,128,512]{2,1,0:T(8,128)(2,1)S(1)} %collective-permute-done.18.refs_14_.refs_12_), channel_id=1, source_target_pairs={{0,1},{1,0},{2,3},{3,2},{4,5},{5,4},{6,7},{7,6},{8,9},{9,8},{10,11... | collective-permute-start | bytes 786440 | tf_op jit(solution)/shard_map/ppermute | solution.py:66
  109.6 8.1 %collective-permute-start.37 = (bf16[2,128,512]{2,1,0:T(8,128)(2,1)S(1)}, bf16[2,128,512]{2,1,0:T(8,128)(2,1)S(1)}, u32[]{:S(2)}, u32[]{:S(2)}) collective-permute-start(bf16[2,128,512]{2,1,0:T(8,128)(2,1)S(1)} %collective-permute-done.19.refs_15_.refs_13_), channel_id=1, source_target_pairs={{0,4},{5,1},{4,8},{9,5},{8,12},{13,9},{12,14},{15,13},{14,10},{11,... | collective-permute-start | bytes 786440 | tf_op jit(solution)/shard_map/ppermute | solution.py:103
  111.2 7.5 %collective-permute-start.36 = (bf16[2,128,512]{2,1,0:T(8,128)(2,1)S(1)}, bf16[2,128,512]{2,1,0:T(8,128)(2,1)S(1)}, u32[]{:S(2)}, u32[]{:S(2)}) collective-permute-start(bf16[2,128,512]{2,1,0:T(8,128)(2,1)S(1)} %collective-permute-done.18.refs_14_.refs_12_), channel_id=1, source_target_pairs={{0,4},{5,1},{4,8},{9,5},{8,12},{13,9},{12,14},{15,13},{14,10},{11,... | collective-permute-start | bytes 786440 | tf_op jit(solution)/shard_map/ppermute | solution.py:103
  117.7 2.1 %collective-permute-start.41 = (bf16[2,128,512]{2,1,0:T(8,128)(2,1)S(1)}, bf16[2,128,512]{2,1,0:T(8,128)(2,1)S(1)}, u32[]{:S(2)}, u32[]{:S(2)}) collective-permute-start(bf16[2,128,512]{2,1,0:T(8,128)(2,1)S(1)} %collective-permute-done.37.refs_15_), channel_id=1, source_target_pairs={{0,1},{1,0},{2,3},{3,2},{4,5},{5,4},{6,7},{7,6},{8,9},{9,8},{10,11... | collective-permute-start | bytes 786440 | tf_op jit(solution)/shard_map/ppermute | solution.py:66
  118.8 1.5 %collective-permute-start.40 = (bf16[2,128,512]{2,1,0:T(8,128)(2,1)S(1)}, bf16[2,128,512]{2,1,0:T(8,128)(2,1)S(1)}, u32[]{:S(2)}, u32[]{:S(2)}) collective-permute-start(bf16[2,128,512]{2,1,0:T(8,128)(2,1)S(1)} %collective-permute-done.36.refs_14_), channel_id=1, source_target_pairs={{0,1},{1,0},{2,3},{3,2},{4,5},{5,4},{6,7},{7,6},{8,9},{9,8},{10,11... | collective-permute-start | bytes 786440 | tf_op jit(solution)/shard_map/ppermute | solution.py:66
  (6 other events, 114.0 us)

commit v10 on v6

--- a/solution.py
+++ b/solution.py
@@ -15,7 +15,6 @@
 PART = 128
 ROW_STEP = 16
 WAVE_ROWS = 32
-SEND_ROWS = 16
 CORES = 2
 PAIR = 2
 QUAD = CORES * PAIR
@@ -102,46 +101,34 @@
     return quarter, beside, swap(quarter, 1), swap(beside, 1)
 
 
-def pick(templates, lists):
+def collect(templates, lists):
+    ids = lax.dynamic_index_in_dim(lists, lax.axis_index("grp"), 1, keepdims=False)
+    return templates[ids].reshape(lists.shape[0], 2, WAVE_ROWS, COLS)
+
+
+def exchange(block):
+    return lax.all_to_all(block, "tpl", split_axis=0, concat_axis=0, tiled=True)
+
+
+def across(block, turn):
+    groups = lax.axis_size("grp")
+    return lax.ppermute(block, "grp", [(at, (at + turn) % groups) for at in range(groups)]) if turn else block
+
+
+def collect_plain(templates, lists):
     devices, groups = lax.axis_size("tpl"), lax.axis_size("grp")
     own_group = lax.axis_index("grp")
     per_device = lists.shape[1]
-    rows = templates.shape[2] // COLS
     pieces = per_device * 2
     if pieces % groups:
-        groups, own_group = 1, jnp.int32(0)
+        groups, own_group = 1, 0
     size = pieces // groups
-    if size == 2 and rows == WAVE_ROWS:
-        picked = templates[lax.dynamic_index_in_dim(lists, own_group, 1, keepdims=False)]
-        picked = picked.reshape(devices, size, rows, COLS)
-        parts = [picked[:, :, at : at + SEND_ROWS] for at in range(0, rows, SEND_ROWS)]
-        return parts, [(own_group - turn) % groups for turn in range(groups)]
-    picked = templates[lists.reshape(-1)].reshape(devices, pieces, rows, COLS)
-    return [lax.dynamic_slice_in_dim(picked, own_group * size, size, 1)], None
-
-
-def exchange(block):
-    return lax.all_to_all(block, "tpl", split_axis=0, concat_axis=0, tiled=True)
-
-
-def across(own):
-    groups = lax.axis_size("grp")
-    return [own] + [
-        lax.ppermute(own, "grp", [(at, (at + turn) % groups) for at in range(groups)]) for turn in range(1, groups)
-    ]
-
-
-def assemble(own, per_device):
-    groups = lax.axis_size("grp")
-    found = jnp.stack(across(own) if per_device * 2 % groups == 0 else [own])
-    found = found[(lax.axis_index("grp") - jnp.arange(found.shape[0])) % found.shape[0]]
+    picked = templates[lists.reshape(-1)].reshape(devices, pieces, templates.shape[2] // COLS, COLS)
+    picked = lax.dynamic_slice_in_dim(picked, own_group * size, size, 1)
+    own = exchange(picked)
+    found = jnp.stack([across(own, turn) for turn in range(groups)])[(own_group - jnp.arange(groups)) % groups]
     found = found.transpose(0, 2, 1, 3, 4).reshape(per_device, 2, ROWS // WAVE_ROWS, WAVE_ROWS, COLS)
-    return [[found[at].transpose(1, 0, 2, 3)] for at in range(per_device)]
-
-
-def held(values):
-    scaled = values * 65537.0
-    return scaled - (scaled - values)
+    return [found[at].transpose(1, 0, 2, 3) for at in range(per_device)]
 
 
 def quarters(parts):
@@ -157,24 +144,20 @@
 
 
 def prepare_kernel(count, cut_ref, list_ref, where_ref, *refs):
-    piece_refs, (masked_ref, sigma_ref) = refs[:-2], refs[-2:]
-    pieces = len(piece_refs) // count
-    rows = WAVE_ROWS // pieces
+    wave_refs, (masked_ref, sigma_ref) = refs[:-2], refs[-2:]
     for tpl in range(count):
         cutoff = cut_ref[list_ref[where_ref[2] * count + where_ref[3 + tpl]]]
         total = jnp.zeros((8, COLS), jnp.float32)
-        for piece in range(pieces):
-            wave_ref = piece_refs[tpl * pieces + piece]
-            for block in range(ROWS // WAVE_ROWS):
-                start = block * WAVE_ROWS + piece * rows
-                bins = (lax.broadcasted_iota(jnp.int32, (rows, COLS), 0) + start) * COLS
-                inside = bins + lax.broadcasted_iota(jnp.int32, (rows, COLS), 1) < cutoff
-                wave_re = jnp.where(inside, wave_ref[block, 0].astype(jnp.float32), 0.0)
-                wave_im = jnp.where(inside, wave_ref[block, 1].astype(jnp.float32), 0.0)
-                masked_ref[tpl, 0, start : start + rows, :] = wave_re.astype(jnp.bfloat16)
-                masked_ref[tpl, 1, start : start + rows, :] = wave_im.astype(jnp.bfloat16)
-                squares = wave_re * wave_re + wave_im * wave_im
-                total = total + jnp.sum(squares.reshape(-1, 8, COLS), axis=0)
+        for block in range(ROWS // WAVE_ROWS):
+            part = slice(block * WAVE_ROWS, (block + 1) * WAVE_ROWS)
+            bins = (lax.broadcasted_iota(jnp.int32, (WAVE_ROWS, COLS), 0) + part.start) * COLS
+            inside = bins + lax.broadcasted_iota(jnp.int32, (WAVE_ROWS, COLS), 1) < cutoff
+            wave_re = jnp.where(inside, wave_refs[tpl][block, 0].astype(jnp.float32), 0.0)
+            wave_im = jnp.where(inside, wave_refs[tpl][block, 1].astype(jnp.float32), 0.0)
+            masked_ref[tpl, 0, part, :] = wave_re.astype(jnp.bfloat16)
+            masked_ref[tpl, 1, part, :] = wave_im.astype(jnp.bfloat16)
+            squares = wave_re * wave_re + wave_im * wave_im
+            total = total + jnp.sum(squares.reshape(-1, 8, COLS), axis=0)
         sigma_ref[tpl] = jnp.sum(total)
 
 
@@ -212,7 +195,7 @@
                     wave_re = masked[tpl, 0, spot, cols].astype(jnp.float32)
                     wave_im = masked[tpl, 1, spot, cols].astype(jnp.float32)
                     data_re, data_im = slid[0, spot, cols], slid[1, spot, cols]
-                    parts.append((held(data_re * wave_re + data_im * wave_im), held(data_im * wave_re - data_re * wave_im)))
+                    parts.append((data_re * wave_re + data_im * wave_im, data_im * wave_re - data_re * wave_im))
                 for residue, (re, im) in enumerate(quarters(parts)):
                     stacked[tpl, residue, at : at + ROW_STEP, cols] = re.astype(jnp.bfloat16)
                     stacked[tpl, residue, PART + at : PART + at + ROW_STEP, cols] = im.astype(jnp.bfloat16)
@@ -225,7 +208,7 @@
                     re, im = section[at : at + ROW_STEP, cols], section[PART + at : PART + at + ROW_STEP, cols]
                     turn_re = twiddle_ref[residue, 0, at : at + ROW_STEP, cols]
                     turn_im = twiddle_ref[residue, 1, at : at + ROW_STEP, cols]
-                    parts.append((held(re * turn_re - im * turn_im), held(re * turn_im + im * turn_re)))
+                    parts.append((re * turn_re - im * turn_im, re * turn_im + im * turn_re))
                 spot = slice(residue * PART + at, residue * PART + at + ROW_STEP)
                 for other, sums in enumerate(quarters(parts)):
                     for which, value in enumerate(sums):
@@ -259,18 +242,17 @@
 
 def prepare(cutoffs, lists, where, waves):
     count = len(waves)
-    operands = [piece for wave in waves for piece in wave]
     return pl.pallas_call(
         functools.partial(prepare_kernel, count),
         out_shape=(
             jax.ShapeDtypeStruct((count, 2, ROWS, COLS), jnp.bfloat16),
             jax.ShapeDtypeStruct((count,), jnp.float32),
         ),
-        in_specs=[smem, smem, smem] + [vmem] * len(operands),
+        in_specs=[smem, smem, smem] + [vmem] * count,
         out_specs=(vmem, smem),
         compiler_params=pltpu.CompilerParams(vmem_limit_bytes=VMEM_LIMIT),
         cost_estimate=pl.CostEstimate(flops=2_000_000_000, bytes_accessed=6_000_000, transcendentals=0),
-    )(cutoffs, lists, where, *operands)
+    )(cutoffs, lists, where, *waves)
 
 
 def detector(det, where, sigma, found, masked, turns, before):
@@ -296,28 +278,25 @@
 
 def body(strain_slots, templates, cutoffs, lists, owner, slides):
     me, owner = lax.axis_index("tpl"), owner[0]
+    groups = lax.axis_size("grp")
     per_device = lists.shape[1]
-    parts, places = pick(templates, lists)
-    (strain_slots, parts) = lax.optimization_barrier((strain_slots, parts))
-    ids = list(range(per_device)) if places is None else places
-    where = jnp.stack([jnp.asarray(at, jnp.int32) for at in (me % CORES, me // CORES % PAIR, me, *ids)])
+    direct = per_device == groups and templates.shape[2] == WAVE_ROWS * COLS
+    places = [(lax.axis_index("grp") - turn) % groups if direct else turn for turn in range(per_device)]
+
+    picked = collect(templates, lists) if direct else collect_plain(templates, lists)
+    strain_slots, picked = lax.optimization_barrier((strain_slots, picked))
+    arrived = exchange(picked) if direct else picked
+    where = jnp.stack([jnp.asarray(at, jnp.int32) for at in (me % CORES, me // CORES % PAIR, me, *places)])
     small = (*slide_turns(slides), where, lists.reshape(-1))
-
-    quarter = [quarter_of(strain_slots, 0, owner)]
-    arrived = [exchange(parts[0])]
-    strain_slots, quarter[0], small, arrived[0] = lax.optimization_barrier((strain_slots, quarter[0], small, arrived[0]))
-    arrived += [exchange(part) for part in parts[1:]]
-    for det in range(1, DET):
+    quarter = []
+    for det in range(DET):
         quarter.append(quarter_of(strain_slots, det, owner))
         strain_slots, quarter[det] = lax.optimization_barrier((strain_slots, quarter[det]))
-    quarter[1:], arrived[1:] = lax.optimization_barrier((quarter[1:], arrived[1:]))
+    quarter[-1], arrived, small = lax.optimization_barrier((quarter[-1], arrived, small))
     *turns, where, flat_list = small
 
     found = [all_quarters(along_line(part, owner)) for part in quarter]
-    if places is None:
-        waves = assemble(arrived[0], per_device)
-    else:
-        waves = [list(wave) for wave in zip(*[across(own) for own in arrived])]
+    waves = [across(arrived, turn) for turn in range(per_device)] if direct else arrived
     masked, sigma = prepare(cutoffs, flat_list, where, waves)
     result = ()
     for det in range(DET):

time: 150 us -> 137 us (0.913); the launches traced: 149 us -> 138 us
  starting transfers between devices: 39.8 us -> 25.5 us
  other arithmetic: 10.8 us -> 14.9 us
  waiting for transfers between devices: 58.9 us -> 62.1 us
  Pallas kernels: 22.1 us -> 19.4 us
    ppermute x24, starting transfers between devices: 24.4 us -> 17.6 us  [swap(): return lax.ppermute(block, 'tpl', partner(flip))]
    all_to_all x2 -> x1, starting transfers between devices: 12.5 us -> 6.45 us  [exchange(): return lax.all_to_all(block, 'tpl', split_axis=0, concat_axis=0, tiled=True)]
    ppermute x24, waiting for transfers between devices: 58.8 us -> 62.1 us  [swap(): return lax.ppermute(block, 'tpl', partner(flip))]
    pallas_call x3, Pallas kernels: 20 us -> 17.3 us  [detector(): pl.pallas_call(functools.partial(detector_kernel, det), out_shape=(scalar...]
    slice x1 -> x0, local copies, waits for them, and re-layouts: 2.3 us -> none  [pick(): picked[:, :, at:at + SEND_ROWS]]
    select_n x3, other arithmetic: 1.07 us -> 2.96 us  [along_line(): quarter = jnp.where(line % 2 == from_line % 2, quarter, swap(quarter, QUAD))]
    unnamed x18 -> x22, local copies, waits for them, and re-layouts: 3.05 us -> 3.14 us
  transfers between devices with their start and end apart: 28 -> 26, of which waited for: 13 -> 14; matrix products, arithmetic and copies ran while one was open for 8% -> 12% of each run, Pallas kernels for 10% -> 10%
where the time goes in v10:
time: 137 us; the launch traced here: 138 us
  waiting for transfers between devices  62.1 us (45%)
  starting transfers between devices  25.5 us (19%)
  Pallas kernels  19.4 us (14%)
  other arithmetic  14.9 us (11%)
  local copies, waits for them, and re-layouts  13.6 us (10%)
  between operations  2.09 us (2%)
    ppermute x24, waiting for transfers between devices, swap(): return lax.ppermute(block, 'tpl', partner(flip))  62.1 us
    ppermute x24, starting transfers between devices, swap(): return lax.ppermute(block, 'tpl', partner(flip))  17.6 us
    pallas_call x3, Pallas kernels, detector(): pl.pallas_call(functools.partial(detector_kernel, det), out_shape=(scalar...  17.3 us
    all_to_all x1, starting transfers between devices, exchange(): return lax.all_to_all(block, 'tpl', split_axis=0, concat_axis=0, tiled=True)  6.45 us
    squeeze x3, local copies, waits for them, and re-layouts, quarter_of(): lax.dynamic_slice(strain_slots, (0, det, 0, which * half), (1, 1, 2, half))  5.88 us
    select_n x3, other arithmetic, quarter_of(): kept = jnp.where(core == owner % CORES, side(core), got)  5.08 us
    unnamed x22, local copies, waits for them, and re-layouts  3.14 us
    select_n x3, other arithmetic, along_line(): quarter = jnp.where(line % 2 == from_line % 2, quarter, swap(quarter, QUAD))  2.96 us
  transfers between devices with their start and end apart: 26, of which 14 were waited for; matrix products, arithmetic and copies ran while one was open for 12% of the time, Pallas kernels for 10%

profile of v10, /device:TPU:0, one launch (start us, length us, event | category | flops | bytes accessed | tf_op | source)
XLA Modules:
  0.0 137.7 jit_solution(1491500977711700849)
XLA Ops:
  0.7 0.8 fusion.11
  1.5 0.7 copy-done
  2.2 2.7 %gather_fusion = bf16[16,2,16384]{2,1,0:T(2,128)(2,1)S(1)} fusion(bf16[32,2,16384]{2,1,0:T(2,128)(2,1)S(1)} %copy-done, s32[1024]{0:T(1024)S(1)} %pad_clamp_fusion), kind=kCustom, calls=%fused_computation | custom fusion | bytes 2097216 | tf_op jit(solution)/shard_map/gather | solution.py:106
  4.9 1.6 %reshape.201 = bf16[16,2,32,512]{3,2,1,0:T(8,128)(2,1)} reshape(bf16[16,2,16384]{2,1,0:T(2,128)(2,1)S(1)} %gather_fusion) | data formatting | bytes 2097152 | tf_op jit(solution)/shard_map/reshape | solution.py:106
  6.5 1.4 %dynamic-slice_bitcast_fusion.2 = bf16[2,131072]{1,0:T(2,128)(2,1)S(1)} fusion(bf16[1,3,2,262144]{3,2,1,0:T(2,128)(2,1)} %param.15, s32[]{:T(128)S(6)} %select_n.313), kind=kLoop, calls=%fused_computation.6 | loop fusion | bytes 1048580 | tf_op jit(solution)/shard_map/squeeze | solution.py:72
  9.1 0.8 collective-permute-done
  9.9 1.6 %broadcast_select_fusion.2 = bf16[2,131072]{1,0:T(2,128)(2,1)S(1)} fusion(bf16[2,131072]{1,0:T(2,128)(2,1)S(1)} %collective-permute-done, pred[]{:T(512)S(6)} %eq.72, bf16[1,3,2,262144]{3,2,1,0:T(2,128)(2,1)} %param.15, s32[]{:T(128)S(6)} %select_n.312), kind=kLoop, calls=%fused_computation.3 | loop fusion | flops 262144 | bytes 1572869 | tf_op jit(solution)/shard_map/jit(_where)/select_n | solution.py:74
  11.8 3.0 %collective-permute-start.1 = (bf16[2,65536]{1,0:T(2,128)(2,1)S(1)}, bf16[2,65536]{1,0:T(2,128)(2,1)S(1)}, u32[]{:S(2)}, u32[]{:S(2)}) collective-permute-start(bf16[2,65536]{1,0:T(2,128)(2,1)S(1)} %broadcast_select_fusion.7), channel_id=1, source_target_pairs={{0,2},{1,3},{2,0},{3,1},{4,6},{5,7},{6,4},{7,5},{8,10},{9,11},{10,... | collective-permute-start | bytes 786440 | tf_op jit(solution)/shard_map/ppermute | solution.py:64
  14.8 6.6 %collective-permute-done.1 = bf16[2,65536]{1,0:T(2,128)(2,1)S(1)} collective-permute-done((bf16[2,65536]{1,0:T(2,128)(2,1)S(1)}, bf16[2,65536]{1,0:T(2,128)(2,1)S(1)}, u32[]{:S(2)}, u32[]{:S(2)}) %collective-permute-start.1) | collective-permute-done | bytes 262176 | tf_op jit(solution)/shard_map/ppermute | solution.py:64
  21.8 2.3 %dynamic-slice_bitcast_fusion.1 = bf16[2,131072]{1,0:T(2,128)(2,1)} fusion(bf16[1,3,2,262144]{3,2,1,0:T(2,128)(2,1)} %param.15, s32[]{:T(128)S(6)} %select_n.313), kind=kLoop, calls=%fused_computation.5 | loop fusion | bytes 1048580 | tf_op jit(solution)/shard_map/squeeze | solution.py:72
  24.1 6.5 %all-to-all-start = ((bf16[16,2,32,512]{3,2,1,0:T(8,128)(2,1)}), bf16[16,2,32,512]{3,2,1,0:T(8,128)(2,1)S(1)}, u32[]{:S(2)}, u32[]{:S(2)}) async-start(bf16[16,2,32,512]{3,2,1,0:T(8,128)(2,1)} %reshape.201), calls=%async_computation | async-start | bytes 2097152 | tf_op jit(solution)/shard_map/all_to_all | solution.py:110
  30.6 1.8 %collective-permute-start.19 = (bf16[2,128,512]{2,1,0:T(8,128)(2,1)S(1)}, bf16[2,128,512]{2,1,0:T(8,128)(2,1)}, u32[]{:S(2)}, u32[]{:S(2)}) collective-permute-start(bf16[2,128,512]{2,1,0:T(8,128)(2,1)S(1)} %bitcast.39), channel_id=1, source_target_pairs={{0,4},{1,5},{2,6},{3,7},{4,0},{5,1},{6,2},{7,3},{8,12},{9,13},{10,... | collective-permute-start | bytes 786440 | tf_op jit(solution)/shard_map/ppermute | solution.py:64
  32.4 1.7 %broadcast_select_fusion.1 = bf16[2,131072]{1,0:T(2,128)(2,1)S(1)} fusion(bf16[2,131072]{1,0:T(2,128)(2,1)} %collective-permute-done.2, pred[]{:T(512)S(6)} %eq.72, bf16[1,3,2,262144]{3,2,1,0:T(2,128)(2,1)} %param.15, s32[]{:T(128)S(6)} %select_n.312), kind=kLoop, calls=%fused_computation.2 | loop fusion | flops 262144 | bytes 1572869 | tf_op jit(solution)/shard_map/jit(_where)/select_n | solution.py:74
  34.2 0.8 copy-done.5
  34.9 1.0 broadcast_select_fusion.5
  35.9 1.5 %collective-permute-start.3 = (bf16[2,65536]{1,0:T(2,128)(2,1)}, bf16[2,65536]{1,0:T(2,128)(2,1)}, u32[]{:S(2)}, u32[]{:S(2)}) collective-permute-start(bf16[2,65536]{1,0:T(2,128)(2,1)} %broadcast_select_fusion.5), channel_id=1, source_target_pairs={{0,2},{1,3},{2,0},{3,1},{4,6},{5,7},{6,4},{7,5},{8,10},{9,11},{10,... | collective-permute-start | bytes 786440 | tf_op jit(solution)/shard_map/ppermute | solution.py:64
  38.1 18.0 %collective-permute-done.19 = bf16[2,128,512]{2,1,0:T(8,128)(2,1)} collective-permute-done((bf16[2,128,512]{2,1,0:T(8,128)(2,1)S(1)}, bf16[2,128,512]{2,1,0:T(8,128)(2,1)}, u32[]{:S(2)}, u32[]{:S(2)}) %collective-permute-start.19) | collective-permute-done | bytes 262176 | tf_op jit(solution)/shard_map/ppermute | solution.py:64
  56.1 1.0 broadcast_select_fusion.12
  57.1 1.4 %broadcast_select_fusion.10 = bf16[2,65536]{1,0:T(2,128)(2,1)S(1)} fusion(bf16[2,65536]{1,0:T(2,128)(2,1)} %collective-permute-done.3, pred[]{:T(512)S(6)} %eq.70, pred[]{:T(512)S(6)} %eq.71, bf16[2,131072]{1,0:T(2,128)(2,1)} %copy-done.5), kind=kLoop, calls=%fused_computation.14 | loop fusion | flops 262144 | bytes 1048578 | tf_op jit(solution)/shard_map/jit(_where)/select_n | solution.py:77
  58.5 0.7 copy.26
  59.3 2.2 %dynamic-slice_bitcast_fusion = bf16[2,131072]{1,0:T(2,128)(2,1)} fusion(bf16[1,3,2,262144]{3,2,1,0:T(2,128)(2,1)} %param.15, s32[]{:T(128)S(6)} %select_n.313), kind=kLoop, calls=%fused_computation.4 | loop fusion | bytes 1048580 | tf_op jit(solution)/shard_map/squeeze | solution.py:72
  61.5 0.7 slice_select_fusion
  62.1 2.5 %collective-permute-start.20 = (bf16[2,64,512]{2,1,0:T(8,128)(2,1)}, bf16[2,64,512]{2,1,0:T(8,128)(2,1)}, u32[]{:S(2)}, u32[]{:S(2)}) collective-permute-start(bf16[2,64,512]{2,1,0:T(8,128)(2,1)} %slice_select_fusion), channel_id=1, source_target_pairs={{0,8},{1,9},{2,10},{3,11},{4,12},{5,13},{6,14},{7,15},{8,0},{9,1},... | collective-permute-start | bytes 393224 | tf_op jit(solution)/shard_map/ppermute | solution.py:64
  65.0 7.0 %collective-permute-done.20 = bf16[2,64,512]{2,1,0:T(8,128)(2,1)} collective-permute-done((bf16[2,64,512]{2,1,0:T(8,128)(2,1)}, bf16[2,64,512]{2,1,0:T(8,128)(2,1)}, u32[]{:S(2)}, u32[]{:S(2)}) %collective-permute-start.20) | collective-permute-done | bytes 131104 | tf_op jit(solution)/shard_map/ppermute | solution.py:64
  72.1 0.9 broadcast_select_fusion.15
  73.1 1.8 %broadcast_select_fusion = bf16[2,131072]{1,0:T(2,128)(2,1)S(1)} fusion(bf16[2,131072]{1,0:T(2,128)(2,1)} %collective-permute-done.4, pred[]{:T(512)S(6)} %eq.72, bf16[1,3,2,262144]{3,2,1,0:T(2,128)(2,1)} %param.15, s32[]{:T(128)S(6)} %select_n.312), kind=kLoop, calls=%fused_computation.1 | loop fusion | flops 262144 | bytes 1572869 | tf_op jit(solution)/shard_map/jit(_where)/select_n | solution.py:74
  75.1 1.6 %collective-permute-start.5 = (bf16[2,65536]{1,0:T(2,128)(2,1)S(1)}, bf16[2,65536]{1,0:T(2,128)(2,1)S(1)}, u32[]{:S(2)}, u32[]{:S(2)}) collective-permute-start(bf16[2,65536]{1,0:T(2,128)(2,1)S(1)} %broadcast_select_fusion.3), channel_id=1, source_target_pairs={{0,2},{1,3},{2,0},{3,1},{4,6},{5,7},{6,4},{7,5},{8,10},{9,11},{10,... | collective-permute-start | bytes 786440 | tf_op jit(solution)/shard_map/ppermute | solution.py:64
  76.7 1.7 %collective-permute-done.21 = bf16[2,64,512]{2,1,0:T(8,128)(2,1)S(1)} collective-permute-done((bf16[2,64,512]{2,1,0:T(8,128)(2,1)S(1)}, bf16[2,64,512]{2,1,0:T(8,128)(2,1)S(1)}, u32[]{:S(2)}, u32[]{:S(2)}) %collective-permute-start.21) | collective-permute-done | bytes 131104 | tf_op jit(solution)/shard_map/ppermute | solution.py:64
  78.5 1.6 %collective-permute-start.22 = (bf16[2,128,512]{2,1,0:T(8,128)(2,1)S(1)}, bf16[2,128,512]{2,1,0:T(8,128)(2,1)}, u32[]{:S(2)}, u32[]{:S(2)}) collective-permute-start(bf16[2,128,512]{2,1,0:T(8,128)(2,1)S(1)} %pad_maximum_fusion.2.refs_0_), channel_id=1, source_target_pairs={{0,2},{1,3},{2,0},{3,1},{4,6},{5,7},{6,4},{7,5},{8,10},{9,11},{10,... | collective-permute-start | bytes 786440 | tf_op jit(solution)/shard_map/ppermute | solution.py:64
  80.3 4.0 %collective-permute-done.5 = bf16[2,65536]{1,0:T(2,128)(2,1)S(1)} collective-permute-done((bf16[2,65536]{1,0:T(2,128)(2,1)S(1)}, bf16[2,65536]{1,0:T(2,128)(2,1)S(1)}, u32[]{:S(2)}, u32[]{:S(2)}) %collective-permute-start.5) | collective-permute-done | bytes 262176 | tf_op jit(solution)/shard_map/ppermute | solution.py:64
  84.8 0.7 copy.25
  85.5 2.0 %collective-permute-start.7 = (bf16[2,128,512]{2,1,0:T(8,128)(2,1)}, bf16[2,128,512]{2,1,0:T(8,128)(2,1)S(1)}, u32[]{:S(2)}, u32[]{:S(2)}) collective-permute-start(bf16[2,128,512]{2,1,0:T(8,128)(2,1)} %bitcast.41), channel_id=1, source_target_pairs={{0,4},{1,5},{2,6},{3,7},{4,0},{5,1},{6,2},{7,3},{8,12},{9,13},{10,... | collective-permute-start | bytes 786440 | tf_op jit(solution)/shard_map/ppermute | solution.py:64
  87.5 1.9 %collective-permute-done.13 = bf16[2,128,512]{2,1,0:T(8,128)(2,1)} collective-permute-done((bf16[2,128,512]{2,1,0:T(8,128)(2,1)}, bf16[2,128,512]{2,1,0:T(8,128)(2,1)}, u32[]{:S(2)}, u32[]{:S(2)}) %collective-permute-start.13) | collective-permute-done | bytes 262176 | tf_op jit(solution)/shard_map/ppermute | solution.py:64
  89.5 1.0 broadcast_select_fusion.13
  90.6 1.5 %collective-permute-start.6 = (bf16[16,2,32,512]{3,2,1,0:T(8,128)(2,1)S(1)}, bf16[16,2,32,512]{3,2,1,0:T(8,128)(2,1)S(1)}, u32[]{:S(2)}, u32[]{:S(2)}) collective-permute-start(bf16[16,2,32,512]{3,2,1,0:T(8,128)(2,1)S(1)} %all-to-all-done.refs_0_), channel_id=1, source_target_pairs={{0,16},{16,0},{1,17},{17,1},{2,18},{18,2},{3,19},{19,3},{4,20},{20... | collective-permute-start | bytes 3145736 | tf_op jit(solution)/shard_map/ppermute | solution.py:115
  92.1 3.4 %collective-permute-done.7 = bf16[2,128,512]{2,1,0:T(8,128)(2,1)S(1)} collective-permute-done((bf16[2,128,512]{2,1,0:T(8,128)(2,1)}, bf16[2,128,512]{2,1,0:T(8,128)(2,1)S(1)}, u32[]{:S(2)}, u32[]{:S(2)}) %collective-permute-start.7) | collective-permute-done | bytes 262176 | tf_op jit(solution)/shard_map/ppermute | solution.py:64
  95.5 1.0 broadcast_select_fusion.14
  96.6 5.4 %collective-permute-done.14 = bf16[2,64,512]{2,1,0:T(8,128)(2,1)S(1)} collective-permute-done((bf16[2,64,512]{2,1,0:T(8,128)(2,1)S(1)}, bf16[2,64,512]{2,1,0:T(8,128)(2,1)S(1)}, u32[]{:S(2)}, u32[]{:S(2)}) %collective-permute-start.14) | collective-permute-done | bytes 131104 | tf_op jit(solution)/shard_map/ppermute | solution.py:64
  102.1 2.5 %collective-permute-done.8 = bf16[2,64,512]{2,1,0:T(8,128)(2,1)S(1)} collective-permute-done((bf16[2,64,512]{2,1,0:T(8,128)(2,1)S(1)}, bf16[2,64,512]{2,1,0:T(8,128)(2,1)S(1)}, u32[]{:S(2)}, u32[]{:S(2)}) %collective-permute-start.8) | collective-permute-done | bytes 131104 | tf_op jit(solution)/shard_map/ppermute | solution.py:64
  104.7 2.8 %collective-permute-done.15 = bf16[2,64,512]{2,1,0:T(8,128)(2,1)S(1)} collective-permute-done((bf16[2,64,512]{2,1,0:T(8,128)(2,1)S(1)}, bf16[2,64,512]{2,1,0:T(8,128)(2,1)S(1)}, u32[]{:S(2)}, u32[]{:S(2)}) %collective-permute-start.15) | collective-permute-done | bytes 131104 | tf_op jit(solution)/shard_map/ppermute | solution.py:64
  107.6 1.1 collective-permute-start.16
  108.7 1.3 collective-permute-done.9
  110.1 0.6 collective-permute-start.10
  110.7 6.2 %collective-permute-done.16.refs_1_ = bf16[2,128,512]{2,1,0:T(8,128)(2,1)S(1)} collective-permute-done((bf16[2,128,512]{2,1,0:T(8,128)(2,1)S(1)}, bf16[2,128,512]{2,1,0:T(8,128)(2,1)S(1)}, u32[]{:S(2)}, u32[]{:S(2)}) %collective-permute-start.16) | collective-permute-done | bytes 262176 | tf_op jit(solution)/shard_map/ppermute | solution.py:64
  117.4 2.1 %shard_map.158 = (bf16[2,2,512,512]{3,2,1,0:T(8,128)(2,1)S(1)}, f32[2]{0:T(128)S(1)}) custom-call(s32[32]{0:T(128)S(1)} %copy-done.1, s32[32]{0:T(128)S(1)} %reshape.205.list_ref, s32[5]{0:T(128)S(1)} %stack.23.where_ref, bf16[16,2,32,512]{3,2,1,0:T(8,128)(2,1)S(1)} %all-to-all-done.refs_0_, bf16[16,2,32,512]{3,2,1,0:T(8,128)(2,1)S(1)} %collective-permute-done.6.refs_1_), custom_call_target="tpu_custom_call" | custom-call | flops 2000000000 | bytes 6000000 | tf_op jit(solution)/shard_map/pallas_call | solution.py:245
  120.1 5.7 %shard_map.159.refs_10_ = f32[2,512,512]{2,1,0:T(8,128)S(1)} custom-call(s32[5]{0:T(128)S(1)} %stack.23.where_ref, f32[2]{0:T(128)S(1)} %get-tuple-element.25.sigma_ref, bf16[2,128,512]{2,1,0:T(8,128)(2,1)S(1)} %pad_maximum_fusion.2.refs_0_, bf16[2,128,512]{2,1,0:T(8,128)(2,1)} %collective-permute-done.22.refs_1_, ...), custom_call_target="tpu_custom_call" | custom-call | flops 5000000000 | bytes 10000000 | tf_op jit(solution)/shard_map/pallas_call | solution.py:263
  125.9 5.6 %shard_map.160.refs_10_ = f32[2,512,512]{2,1,0:T(8,128)S(1)} custom-call(s32[5]{0:T(128)S(1)} %stack.23.where_ref, f32[2]{0:T(128)S(1)} %get-tuple-element.25.sigma_ref, bf16[2,128,512]{2,1,0:T(8,128)(2,1)S(1)} %pad_maximum_fusion.1.refs_0_, bf16[2,128,512]{2,1,0:T(8,128)(2,1)S(1)} %collective-permute-done.16.refs_1_, ...), custom_call_target="tpu_custom_call" | custom-call | flops 5000000000 | bytes 10000000 | tf_op jit(solution)/shard_map/pallas_call | solution.py:263
  131.5 6.0 %shard_map.161 = (f32[2]{0:T(128)}, f32[2]{0:T(128)}) custom-call(s32[5]{0:T(128)S(1)} %stack.23.where_ref, f32[2]{0:T(128)S(1)} %get-tuple-element.25.sigma_ref, bf16[2,128,512]{2,1,0:T(8,128)(2,1)S(1)} %pad_maximum_fusion.refs_0_, bf16[2,128,512]{2,1,0:T(8,128)(2,1)S(1)} %collective-permute-done.10.refs_1_, ...), custom_call_target="tpu_custom_call" | custom-call | flops 5000000000 | bytes 10000000 | tf_op jit(solution)/shard_map/pallas_call | solution.py:263
  (68 shorter events, 4.9 us)
Async XLA Ops:
  0.6 1.6 %copy-start = (bf16[32,2,16384]{2,1,0:T(2,128)(2,1)S(1)}, bf16[32,2,16384]{2,1,0:T(2,128)(2,1)}, u32[]{:S(2)}) copy-start(bf16[32,2,16384]{2,1,0:T(2,128)(2,1)} %param.16) | copy-start | bytes 6291460
  7.9 2.1 %collective-permute-start = (bf16[2,131072]{1,0:T(2,128)(2,1)S(1)}, bf16[2,131072]{1,0:T(2,128)(2,1)S(1)}, u32[]{:S(2)}, u32[]{:S(2)}) collective-permute-start(bf16[2,131072]{1,0:T(2,128)(2,1)S(1)} %dynamic-slice_bitcast_fusion.2), channel_id=1, source_target_pairs={{0,1},{1,0},{2,3},{3,2},{4,5},{5,4},{6,7},{7,6},{8,9},{9,8},{10,11... | collective-permute-start | bytes 1572872 | tf_op jit(solution)/shard_map/ppermute | solution.py:64
  11.5 19.0 %copy-start.8 = (s32[3]{0:T(128)S(1)}, s32[3]{0:T(128)}, u32[]{:S(2)}) copy-start(s32[3]{0:T(128)} %param.20) | copy-start | bytes 40
  11.8 9.6 %collective-permute-start.1 = (bf16[2,65536]{1,0:T(2,128)(2,1)S(1)}, bf16[2,65536]{1,0:T(2,128)(2,1)S(1)}, u32[]{:S(2)}, u32[]{:S(2)}) collective-permute-start(bf16[2,65536]{1,0:T(2,128)(2,1)S(1)} %broadcast_select_fusion.7), channel_id=1, source_target_pairs={{0,2},{1,3},{2,0},{3,1},{4,6},{5,7},{6,4},{7,5},{8,10},{9,11},{10,... | collective-permute-start | bytes 786440 | tf_op jit(solution)/shard_map/ppermute | solution.py:64
  21.8 16.0 %copy-start.7 = (s32[16,2]{0,1:T(2,128)S(1)}, s32[16,2]{0,1:T(2,128)}, u32[]{:S(2)}) copy-start(s32[16,2]{0,1:T(2,128)} %param.18) | copy-start | bytes 388
  21.8 16.3 %copy-start.6 = (bf16[1,2,128,512]{3,2,1,0:T(8,128)(2,1)}, bf16[1,2,128,512]{3,2,1,0:T(8,128)(2,1)S(1)}, u32[]{:S(2)}) copy-start(bf16[1,2,128,512]{3,2,1,0:T(8,128)(2,1)S(1)} %copy.27) | copy-start | bytes 786436
  24.1 8.3 %collective-permute-start.2 = (bf16[2,131072]{1,0:T(2,128)(2,1)}, bf16[2,131072]{1,0:T(2,128)(2,1)}, u32[]{:S(2)}, u32[]{:S(2)}) collective-permute-start(bf16[2,131072]{1,0:T(2,128)(2,1)} %dynamic-slice_bitcast_fusion.1), channel_id=1, source_target_pairs={{0,1},{1,0},{2,3},{3,2},{4,5},{5,4},{6,7},{7,6},{8,9},{9,8},{10,11... | collective-permute-start | bytes 1572872 | tf_op jit(solution)/shard_map/ppermute | solution.py:64
  24.1 61.4 %all-to-all-start = ((bf16[16,2,32,512]{3,2,1,0:T(8,128)(2,1)}), bf16[16,2,32,512]{3,2,1,0:T(8,128)(2,1)S(1)}, u32[]{:S(2)}, u32[]{:S(2)}) async-start(bf16[16,2,32,512]{3,2,1,0:T(8,128)(2,1)} %reshape.201), calls=%async_computation | async-start | bytes 2097152 | tf_op jit(solution)/shard_map/all_to_all | solution.py:110
  30.6 25.5 %collective-permute-start.19 = (bf16[2,128,512]{2,1,0:T(8,128)(2,1)S(1)}, bf16[2,128,512]{2,1,0:T(8,128)(2,1)}, u32[]{:S(2)}, u32[]{:S(2)}) collective-permute-start(bf16[2,128,512]{2,1,0:T(8,128)(2,1)S(1)} %bitcast.39), channel_id=1, source_target_pairs={{0,4},{1,5},{2,6},{3,7},{4,0},{5,1},{6,2},{7,3},{8,12},{9,13},{10,... | collective-permute-start | bytes 786440 | tf_op jit(solution)/shard_map/ppermute | solution.py:64
  34.1 0.8 copy-start.5
  35.9 21.2 %collective-permute-start.3 = (bf16[2,65536]{1,0:T(2,128)(2,1)}, bf16[2,65536]{1,0:T(2,128)(2,1)}, u32[]{:S(2)}, u32[]{:S(2)}) collective-permute-start(bf16[2,65536]{1,0:T(2,128)(2,1)} %broadcast_select_fusion.5), channel_id=1, source_target_pairs={{0,2},{1,3},{2,0},{3,1},{4,6},{5,7},{6,4},{7,5},{8,10},{9,11},{10,... | collective-permute-start | bytes 786440 | tf_op jit(solution)/shard_map/ppermute | solution.py:64
  61.5 11.6 %collective-permute-start.4 = (bf16[2,131072]{1,0:T(2,128)(2,1)}, bf16[2,131072]{1,0:T(2,128)(2,1)}, u32[]{:S(2)}, u32[]{:S(2)}) collective-permute-start(bf16[2,131072]{1,0:T(2,128)(2,1)} %dynamic-slice_bitcast_fusion), channel_id=1, source_target_pairs={{0,1},{1,0},{2,3},{3,2},{4,5},{5,4},{6,7},{7,6},{8,9},{9,8},{10,11... | collective-permute-start | bytes 1572872 | tf_op jit(solution)/shard_map/ppermute | solution.py:64
  62.1 9.9 %collective-permute-start.20 = (bf16[2,64,512]{2,1,0:T(8,128)(2,1)}, bf16[2,64,512]{2,1,0:T(8,128)(2,1)}, u32[]{:S(2)}, u32[]{:S(2)}) collective-permute-start(bf16[2,64,512]{2,1,0:T(8,128)(2,1)} %slice_select_fusion), channel_id=1, source_target_pairs={{0,8},{1,9},{2,10},{3,11},{4,12},{5,13},{6,14},{7,15},{8,0},{9,1},... | collective-permute-start | bytes 393224 | tf_op jit(solution)/shard_map/ppermute | solution.py:64
  73.0 5.4 %collective-permute-start.21 = (bf16[2,64,512]{2,1,0:T(8,128)(2,1)S(1)}, bf16[2,64,512]{2,1,0:T(8,128)(2,1)S(1)}, u32[]{:S(2)}, u32[]{:S(2)}) collective-permute-start(bf16[2,64,512]{2,1,0:T(8,128)(2,1)S(1)} %broadcast_select_fusion.15), channel_id=1, source_target_pairs={{0,4},{1,5},{2,6},{3,7},{4,0},{5,1},{6,2},{7,3},{8,12},{9,13},{10,... | collective-permute-start | bytes 393224 | tf_op jit(solution)/shard_map/ppermute | solution.py:64
  75.1 9.3 %collective-permute-start.5 = (bf16[2,65536]{1,0:T(2,128)(2,1)S(1)}, bf16[2,65536]{1,0:T(2,128)(2,1)S(1)}, u32[]{:S(2)}, u32[]{:S(2)}) collective-permute-start(bf16[2,65536]{1,0:T(2,128)(2,1)S(1)} %broadcast_select_fusion.3), channel_id=1, source_target_pairs={{0,2},{1,3},{2,0},{3,1},{4,6},{5,7},{6,4},{7,5},{8,10},{9,11},{10,... | collective-permute-start | bytes 786440 | tf_op jit(solution)/shard_map/ppermute | solution.py:64
  78.5 32.2 %collective-permute-start.22 = (bf16[2,128,512]{2,1,0:T(8,128)(2,1)S(1)}, bf16[2,128,512]{2,1,0:T(8,128)(2,1)}, u32[]{:S(2)}, u32[]{:S(2)}) collective-permute-start(bf16[2,128,512]{2,1,0:T(8,128)(2,1)S(1)} %pad_maximum_fusion.2.refs_0_), channel_id=1, source_target_pairs={{0,2},{1,3},{2,0},{3,1},{4,6},{5,7},{6,4},{7,5},{8,10},{9,11},{10,... | collective-permute-start | bytes 786440 | tf_op jit(solution)/shard_map/ppermute | solution.py:64
  80.0 39.5 %collective-permute-start.23 = (bf16[2,128,512]{2,1,0:T(8,128)(2,1)S(1)}, bf16[2,128,512]{2,1,0:T(8,128)(2,1)}, u32[]{:S(2)}, u32[]{:S(2)}) collective-permute-start(bf16[2,128,512]{2,1,0:T(8,128)(2,1)S(1)} %pad_maximum_fusion.2.refs_0_), channel_id=1, source_target_pairs={{0,1},{1,0},{2,3},{3,2},{4,5},{5,4},{6,7},{7,6},{8,9},{9,8},{10,11... | collective-permute-start | bytes 786440 | tf_op jit(solution)/shard_map/ppermute | solution.py:64
  80.1 9.4 %collective-permute-start.13 = (bf16[2,128,512]{2,1,0:T(8,128)(2,1)}, bf16[2,128,512]{2,1,0:T(8,128)(2,1)}, u32[]{:S(2)}, u32[]{:S(2)}) collective-permute-start(bf16[2,128,512]{2,1,0:T(8,128)(2,1)} %bitcast.30), channel_id=1, source_target_pairs={{0,4},{1,5},{2,6},{3,7},{4,0},{5,1},{6,2},{7,3},{8,12},{9,13},{10,... | collective-permute-start | bytes 786440 | tf_op jit(solution)/shard_map/ppermute | solution.py:64
  84.8 32.7 %copy-start.1 = (s32[32]{0:T(128)S(1)}, s32[32]{0:T(128)}, u32[]{:S(2)}) copy-start(s32[32]{0:T(128)} %cut_ref.1) | copy-start | bytes 388
  85.5 10.0 %collective-permute-start.7 = (bf16[2,128,512]{2,1,0:T(8,128)(2,1)}, bf16[2,128,512]{2,1,0:T(8,128)(2,1)S(1)}, u32[]{:S(2)}, u32[]{:S(2)}) collective-permute-start(bf16[2,128,512]{2,1,0:T(8,128)(2,1)} %bitcast.41), channel_id=1, source_target_pairs={{0,4},{1,5},{2,6},{3,7},{4,0},{5,1},{6,2},{7,3},{8,12},{9,13},{10,... | collective-permute-start | bytes 786440 | tf_op jit(solution)/shard_map/ppermute | solution.py:64
  90.5 11.5 %collective-permute-start.14 = (bf16[2,64,512]{2,1,0:T(8,128)(2,1)S(1)}, bf16[2,64,512]{2,1,0:T(8,128)(2,1)S(1)}, u32[]{:S(2)}, u32[]{:S(2)}) collective-permute-start(bf16[2,64,512]{2,1,0:T(8,128)(2,1)S(1)} %slice_select_fusion.1), channel_id=1, source_target_pairs={{0,8},{1,9},{2,10},{3,11},{4,12},{5,13},{6,14},{7,15},{8,0},{9,1},... | collective-permute-start | bytes 393224 | tf_op jit(solution)/shard_map/ppermute | solution.py:64
  90.6 26.3 %collective-permute-start.6 = (bf16[16,2,32,512]{3,2,1,0:T(8,128)(2,1)S(1)}, bf16[16,2,32,512]{3,2,1,0:T(8,128)(2,1)S(1)}, u32[]{:S(2)}, u32[]{:S(2)}) collective-permute-start(bf16[16,2,32,512]{3,2,1,0:T(8,128)(2,1)S(1)} %all-to-all-done.refs_0_), channel_id=1, source_target_pairs={{0,16},{16,0},{1,17},{17,1},{2,18},{18,2},{3,19},{19,3},{4,20},{20... | collective-permute-start | bytes 3145736 | tf_op jit(solution)/shard_map/ppermute | solution.py:115
  96.5 8.1 %collective-permute-start.8 = (bf16[2,64,512]{2,1,0:T(8,128)(2,1)S(1)}, bf16[2,64,512]{2,1,0:T(8,128)(2,1)S(1)}, u32[]{:S(2)}, u32[]{:S(2)}) collective-permute-start(bf16[2,64,512]{2,1,0:T(8,128)(2,1)S(1)} %slice_select_fusion.2), channel_id=1, source_target_pairs={{0,8},{1,9},{2,10},{3,11},{4,12},{5,13},{6,14},{7,15},{8,0},{9,1},... | collective-permute-start | bytes 393224 | tf_op jit(solution)/shard_map/ppermute | solution.py:64
  102.0 5.5 %collective-permute-start.15 = (bf16[2,64,512]{2,1,0:T(8,128)(2,1)S(1)}, bf16[2,64,512]{2,1,0:T(8,128)(2,1)S(1)}, u32[]{:S(2)}, u32[]{:S(2)}) collective-permute-start(bf16[2,64,512]{2,1,0:T(8,128)(2,1)S(1)} %broadcast_select_fusion.16), channel_id=1, source_target_pairs={{0,4},{1,5},{2,6},{3,7},{4,0},{5,1},{6,2},{7,3},{8,12},{9,13},{10,... | collective-permute-start | bytes 393224 | tf_op jit(solution)/shard_map/ppermute | solution.py:64
  104.6 5.4 %collective-permute-start.9 = (bf16[2,64,512]{2,1,0:T(8,128)(2,1)S(1)}, bf16[2,64,512]{2,1,0:T(8,128)(2,1)S(1)}, u32[]{:S(2)}, u32[]{:S(2)}) collective-permute-start(bf16[2,64,512]{2,1,0:T(8,128)(2,1)S(1)} %broadcast_select_fusion.17), channel_id=1, source_target_pairs={{0,4},{1,5},{2,6},{3,7},{4,0},{5,1},{6,2},{7,3},{8,12},{9,13},{10,... | collective-permute-start | bytes 393224 | tf_op jit(solution)/shard_map/ppermute | solution.py:64
  107.6 9.3 %collective-permute-start.16 = (bf16[2,128,512]{2,1,0:T(8,128)(2,1)S(1)}, bf16[2,128,512]{2,1,0:T(8,128)(2,1)S(1)}, u32[]{:S(2)}, u32[]{:S(2)}) collective-permute-start(bf16[2,128,512]{2,1,0:T(8,128)(2,1)S(1)} %pad_maximum_fusion.1.refs_0_), channel_id=1, source_target_pairs={{0,2},{1,3},{2,0},{3,1},{4,6},{5,7},{6,4},{7,5},{8,10},{9,11},{10,... | collective-permute-start | bytes 786440 | tf_op jit(solution)/shard_map/ppermute | solution.py:64
  110.1 10.1 %copy-start.2 = (f32[4,2,128,512]{3,2,1,0:T(8,128)S(1)}, f32[4,2,128,512]{3,2,1,0:T(8,128)}, u32[]{:S(2)}) copy-start(f32[4,2,128,512]{3,2,1,0:T(8,128)} %constant.226.clone.refs_9_) | copy-start | bytes 6291460
  110.1 10.0 %copy-start.3 = (bf16[4,512,256]{2,1,0:T(8,128)(2,1)S(1)}, bf16[4,512,256]{2,1,0:T(8,128)(2,1)}, u32[]{:S(2)}) copy-start(bf16[4,512,256]{2,1,0:T(8,128)(2,1)} %constant.231.refs_8_) | copy-start | bytes 3145732
  110.1 10.0 %copy-start.4 = (bf16[4,256,256]{2,1,0:T(8,128)(2,1)S(1)}, bf16[4,256,256]{2,1,0:T(8,128)(2,1)}, u32[]{:S(2)}) copy-start(bf16[4,256,256]{2,1,0:T(8,128)(2,1)} %constant.230.refs_7_) | copy-start | bytes 1572868
  110.1 9.9 %collective-permute-start.10 = (bf16[2,128,512]{2,1,0:T(8,128)(2,1)S(1)}, bf16[2,128,512]{2,1,0:T(8,128)(2,1)S(1)}, u32[]{:S(2)}, u32[]{:S(2)}) collective-permute-start(bf16[2,128,512]{2,1,0:T(8,128)(2,1)S(1)} %pad_maximum_fusion.refs_0_), channel_id=1, source_target_pairs={{0,2},{1,3},{2,0},{3,1},{4,6},{5,7},{6,4},{7,5},{8,10},{9,11},{10,... | collective-permute-start | bytes 786440 | tf_op jit(solution)/shard_map/ppermute | solution.py:64
  110.7 9.4 %collective-permute-start.24 = (bf16[2,128,512]{2,1,0:T(8,128)(2,1)}, bf16[2,128,512]{2,1,0:T(8,128)(2,1)S(1)}, u32[]{:S(2)}, u32[]{:S(2)}) collective-permute-start(bf16[2,128,512]{2,1,0:T(8,128)(2,1)} %collective-permute-done.22.refs_1_), channel_id=1, source_target_pairs={{0,1},{1,0},{2,3},{3,2},{4,5},{5,4},{6,7},{7,6},{8,9},{9,8},{10,11... | collective-permute-start | bytes 786440 | tf_op jit(solution)/shard_map/ppermute | solution.py:64
  116.9 9.0 %collective-permute-start.17 = (bf16[2,128,512]{2,1,0:T(8,128)(2,1)S(1)}, bf16[2,128,512]{2,1,0:T(8,128)(2,1)S(1)}, u32[]{:S(2)}, u32[]{:S(2)}) collective-permute-start(bf16[2,128,512]{2,1,0:T(8,128)(2,1)S(1)} %pad_maximum_fusion.1.refs_0_), channel_id=1, source_target_pairs={{0,1},{1,0},{2,3},{3,2},{4,5},{5,4},{6,7},{7,6},{8,9},{9,8},{10,11... | collective-permute-start | bytes 786440 | tf_op jit(solution)/shard_map/ppermute | solution.py:64
  116.9 9.0 %collective-permute-start.18 = (bf16[2,128,512]{2,1,0:T(8,128)(2,1)S(1)}, bf16[2,128,512]{2,1,0:T(8,128)(2,1)S(1)}, u32[]{:S(2)}, u32[]{:S(2)}) collective-permute-start(bf16[2,128,512]{2,1,0:T(8,128)(2,1)S(1)} %collective-permute-done.16.refs_1_), channel_id=1, source_target_pairs={{0,1},{1,0},{2,3},{3,2},{4,5},{5,4},{6,7},{7,6},{8,9},{9,8},{10,11... | collective-permute-start | bytes 786440 | tf_op jit(solution)/shard_map/ppermute | solution.py:64
  119.5 12.0 %collective-permute-start.11 = (bf16[2,128,512]{2,1,0:T(8,128)(2,1)S(1)}, bf16[2,128,512]{2,1,0:T(8,128)(2,1)S(1)}, u32[]{:S(2)}, u32[]{:S(2)}) collective-permute-start(bf16[2,128,512]{2,1,0:T(8,128)(2,1)S(1)} %pad_maximum_fusion.refs_0_), channel_id=1, source_target_pairs={{0,1},{1,0},{2,3},{3,2},{4,5},{5,4},{6,7},{7,6},{8,9},{9,8},{10,11... | collective-permute-start | bytes 786440 | tf_op jit(solution)/shard_map/ppermute | solution.py:64
  120.0 11.5 %collective-permute-start.12 = (bf16[2,128,512]{2,1,0:T(8,128)(2,1)S(1)}, bf16[2,128,512]{2,1,0:T(8,128)(2,1)S(1)}, u32[]{:S(2)}, u32[]{:S(2)}) collective-permute-start(bf16[2,128,512]{2,1,0:T(8,128)(2,1)S(1)} %collective-permute-done.10.refs_1_), channel_id=1, source_target_pairs={{0,1},{1,0},{2,3},{3,2},{4,5},{5,4},{6,7},{7,6},{8,9},{9,8},{10,11... | collective-permute-start | bytes 786440 | tf_op jit(solution)/shard_map/ppermute | solution.py:64

commit v11 on v9

--- a/solution.py
+++ b/solution.py
@@ -18,8 +18,8 @@
 CORES = 2
 HALF_CHUNKS = 2
 LAG = 2
-TEMPLATE_SLOT = 4
-MASKED_SLOT = 12
+TEMPLATE_SLOT = 2
+MASKED_SLOT = 13
 VMEM_LIMIT = 24 * 1024 * 1024
 
 
@@ -88,7 +88,8 @@
         along.append((order[(at + 1) % chips] * CORES + 1, order[at] * CORES + 1))
     sent, shared, arrived = [], [], []
     count = len(chunks)
-    for slot in range(count + LAG * (chips - 1)):
+    last = count + LAG * (chips - 1)
+    for slot in range(last):
         if slot < LAG:
             here = chunks[slot]
         elif slot < count:
@@ -98,7 +99,7 @@
         if slot in hooks:
             here = hooks[slot](here, sent, shared)
         sent.append(here)
-        shared.append(swap(here, 1))
+        shared.append(swap(hooks[last](here, sent, shared) if slot >= last - LAG else here, 1))
         if slot < count + LAG * (chips - 2):
             arrived.append(lax.ppermute(here, "tpl", along))
     return sent, shared
@@ -250,6 +251,9 @@
                 outputs[0][tpl, :, cols] = squares
         largest.append(peak)
 
+    if not last:
+        outputs[1][0] = jnp.int32(0)
+
     if last:
         for tpl in range(count):
             place = where_ref[4 + tpl]
@@ -283,12 +287,14 @@
     found = [*sent[slots], *shared[slots]]
     last = det == DET - 1
     scalars = jax.ShapeDtypeStruct((count,), jnp.float32)
-    operands = [masked, *turns, *tables(), *before]
+    operands = [masked, *turns, *tables(), *before[:1]]
     return pl.pallas_call(
         functools.partial(detector_kernel, det, chips),
-        out_shape=(scalars, scalars) if last else (jax.ShapeDtypeStruct((count, ROWS, COLS), jnp.float32),),
+        out_shape=(scalars, scalars)
+        if last
+        else (jax.ShapeDtypeStruct((count, ROWS, COLS), jnp.float32), jax.ShapeDtypeStruct((1,), jnp.int32)),
         in_specs=[smem, smem] + [anywhere] * len(found) + [vmem] * len(operands),
-        out_specs=(smem, smem) if last else (vmem,),
+        out_specs=(smem, smem) if last else (vmem, smem),
         scratch_shapes=[
             pltpu.VMEM((2, ROWS, COLS), jnp.bfloat16),
             pltpu.SemaphoreType.DMA,
@@ -321,42 +327,35 @@
     where = jnp.stack([jnp.asarray(at, jnp.int32) for at in (me % CORES, near, me, far, *places)])
     small = (*slide_turns(slides), where, lists.reshape(-1))
 
-    held = {"small": small, "arrived": exchange(picked) if direct else picked, "result": ()}
-
-    def tie(name, chunk):
-        chunk, held[name] = lax.optimization_barrier((chunk, held[name]))
-        return chunk
+    arrived = exchange(picked) if direct else picked
+    waves = [across(arrived, turn) for turn in range(per_device)] if direct else arrived
+    *turns, where, flat_list = small
+    masked, sigma = prepare(cutoffs, flat_list, where, waves)
+    results = [()]
+
+    def once(ready, chunk):
+        return jnp.where(ready, chunk, jnp.zeros_like(chunk))
 
     def after_arrived(chunk, sent, shared):
-        chunk = tie("small", tie("arrived", chunk))
-        waves = held["arrived"]
-        if direct:
-            waves = [across(waves, turn) for turn in range(per_device)]
-        *_, where, flat_list = held["small"]
-        held["masked"] = prepare(cutoffs, flat_list, where, waves)
-        return chunk
+        block = arrived if direct else arrived[0]
+        return once(block[(0,) * block.ndim].astype(jnp.float32) < 1e3, chunk)
 
     def after_masked(chunk, sent, shared):
-        return tie("masked", chunk)
-
-    def filtered(det, sent, shared):
-        *turns, where, _ = held["small"]
-        masked, sigma = held["masked"]
-        held["result"] = detector(det, chips, where, sigma, sent, shared, masked, turns, held["result"])
+        return once(sigma[0] >= 0.0, chunk)
 
     def after_detector(det):
         def hook(chunk, sent, shared):
-            filtered(det, sent, shared)
-            return tie("result", chunk)
+            if len(results) == det + 1:
+                results.append(detector(det, chips, where, sigma, sent, shared, masked, turns, results[-1]))
+            return once(results[-1][1][0] == 0, chunk)
 
         return hook
 
     hooks = {TEMPLATE_SLOT: after_arrived, MASKED_SLOT: after_masked}
     for det in range(DET - 1):
-        hooks[(det + 1) * HALF_CHUNKS - 1 + LAG * chips] = after_detector(det)
+        hooks[(det + 1) * HALF_CHUNKS + LAG * chips - (1 if det < DET - 2 else 0)] = after_detector(det)
     sent, shared = spread(chunks, owner, hooks)
-    filtered(DET - 1, sent, shared)
-    return tuple(held["result"])
+    return tuple(detector(DET - 1, chips, where, sigma, sent, shared, masked, turns, results[-1]))
 
 
 def solution(mesh):

time: 128 us -> 164 us (1.28)
  local copies, waits for them, and re-layouts: 15.4 us -> 46 us
  waiting for transfers between devices: 27.3 us -> 36.2 us
  starting transfers between devices: 52.1 us -> 44 us
  Pallas kernels: 19.6 us -> 23.1 us
  between operations: 2.01 us -> 4.07 us
    unnamed x27 -> x129, local copies, waits for them, and re-layouts: 3.13 us -> 36.2 us
    ppermute x18, waiting for transfers between devices: 24.8 us -> 32.3 us  [spread(): arrived.append(lax.ppermute(here, 'tpl', along))]
    ppermute x18, starting transfers between devices: 36.8 us -> 30.5 us  [spread(): arrived.append(lax.ppermute(here, 'tpl', along))]
    squeeze x3, local copies, waits for them, and re-layouts: 5.8 us -> 2.92 us  [half_chunks(): lax.dynamic_slice(strain_slots, (0, det, 0, which * half), (1, 1, 2, half))]
    pallas_call x3, Pallas kernels: 17.5 us -> 20.4 us  [detector(): pl.pallas_call(functools.partial(detector_kernel, det, chips), out_shape=...]
    select_n x4 -> x3, other arithmetic: 4.38 us -> 1.77 us  [spread(): here = jnp.where(on_owner_chip, chunks[slot], arrived[slot - LAG])]
    all_to_all x1, starting transfers between devices: 7.08 us -> 4.93 us  [exchange(): return lax.all_to_all(block, 'tpl', split_axis=0, concat_axis=0, tiled=True)]
    select_n x0 -> x5, other arithmetic: none -> 2.04 us  [once(): return jnp.where(ready, chunk, jnp.zeros_like(chunk))]
  transfers between devices with their start and end apart: 43 -> 43, of which waited for: 16 -> 13; matrix products, arithmetic and copies ran while one was open for 11% -> 5% of each run, Pallas kernels for 10% -> 10%
where the time goes in v11:
time: 164 us; the launch traced here: 163 us
  local copies, waits for them, and re-layouts  46 us (28%)
  starting transfers between devices  44 us (27%)
  waiting for transfers between devices  36.2 us (22%)
  Pallas kernels  23.1 us (14%)
  other arithmetic  9.18 us (6%)
  between operations  4.07 us (2%)
    unnamed x129, local copies, waits for them, and re-layouts  36.2 us
    ppermute x18, waiting for transfers between devices, spread(): arrived.append(lax.ppermute(here, 'tpl', along))  32.3 us
    ppermute x18, starting transfers between devices, spread(): arrived.append(lax.ppermute(here, 'tpl', along))  30.5 us
    pallas_call x3, Pallas kernels, detector(): pl.pallas_call(functools.partial(detector_kernel, det, chips), out_shape=...  20.4 us
    ppermute x23, starting transfers between devices, swap(): lax.ppermute(block, 'tpl', [(at, at ^ flip) for at in range(lax.axis_size...  7.16 us
    all_to_all x1, starting transfers between devices, exchange(): return lax.all_to_all(block, 'tpl', split_axis=0, concat_axis=0, tiled=True)  4.93 us
    select_n x3, other arithmetic, half_chunks(): first = jnp.where(core == owner % CORES, side(core), got)  3.96 us
    ppermute x23, waiting for transfers between devices, swap(): lax.ppermute(block, 'tpl', [(at, at ^ flip) for at in range(lax.axis_size...  3.83 us
  transfers between devices with their start and end apart: 43, of which 13 were waited for; matrix products, arithmetic and copies ran while one was open for 5% of the time, Pallas kernels for 10%

profile of v11, /device:TPU:0, one launch (start us, length us, event | category | flops | bytes accessed | tf_op | source)
XLA Modules:
  0.0 162.6 jit_solution(11449190408612065967)
XLA Ops:
  2.2 2.7 %gather_fusion = bf16[16,2,16384]{2,1,0:T(2,128)(2,1)S(1)} fusion(bf16[32,2,16384]{2,1,0:T(2,128)(2,1)S(1)} %copy-done, s32[1024]{0:T(1024)S(1)} %pad_clamp_fusion), kind=kCustom, calls=%fused_computation | custom fusion | bytes 2097216 | tf_op jit(solution)/shard_map/gather | solution.py:119
  4.9 1.6 reshape.220
  6.5 1.4 dynamic-slice_bitcast_fusion.2
  9.9 1.7 %broadcast_select_fusion.2 = bf16[2,131072]{1,0:T(2,128)(2,1)S(1)} fusion(bf16[2,131072]{1,0:T(2,128)(2,1)S(1)} %collective-permute-done.1, pred[]{:T(512)S(6)} %eq.59, bf16[1,3,2,262144]{3,2,1,0:T(2,128)(2,1)} %param.15, s32[]{:T(128)S(6)} %select_n.227), kind=kLoop, calls=%fused_computation.3 | loop fusion | flops 262144 | bytes 1572869 | tf_op jit(solution)/shard_map/jit(_where)/select_n | solution.py:75
  13.5 1.6 collective-permute-done.2
  17.5 1.2 dynamic-slice_bitcast_fusion
  18.9 2.8 %collective-permute-start.6 = (bf16[2,128,512]{2,1,0:T(8,128)(2,1)S(1)}, bf16[2,128,512]{2,1,0:T(8,128)(2,1)}, u32[]{:S(2)}, u32[]{:S(2)}) collective-permute-start(bf16[2,128,512]{2,1,0:T(8,128)(2,1)S(1)} %get-tuple-element.28.refs_1_), channel_id=1, source_target_pairs={{0,4},{5,1},{4,8},{9,5},{8,12},{13,9},{12,14},{15,13},{14,10},{11,... | collective-permute-start | bytes 786440 | tf_op jit(solution)/shard_map/ppermute | solution.py:104
  21.7 4.9 %all-to-all-start = ((bf16[16,2,32,512]{3,2,1,0:T(8,128)(2,1)}), bf16[16,2,32,512]{3,2,1,0:T(8,128)(2,1)S(1)}, u32[]{:S(2)}, u32[]{:S(2)}) async-start(bf16[16,2,32,512]{3,2,1,0:T(8,128)(2,1)} %reshape.220), calls=%async_computation | async-start | bytes 2097152 | tf_op jit(solution)/shard_map/all_to_all | solution.py:123
  26.7 1.9 %collective-permute-start.4 = (bf16[2,128,512]{2,1,0:T(8,128)(2,1)}, bf16[2,128,512]{2,1,0:T(8,128)(2,1)}, u32[]{:S(2)}, u32[]{:S(2)}) collective-permute-start(bf16[2,128,512]{2,1,0:T(8,128)(2,1)} %get-tuple-element.25.refs_0_), channel_id=1, source_target_pairs={{0,4},{5,1},{4,8},{9,5},{8,12},{13,9},{12,14},{15,13},{14,10},{11,... | collective-permute-start | bytes 786440 | tf_op jit(solution)/shard_map/ppermute | solution.py:104
  28.6 1.0 broadcast_select_fusion.8.refs_3_.refs_1_
  29.6 1.5 collective-permute-start.7
  31.1 1.7 %broadcast_select_fusion = bf16[2,131072]{1,0:T(2,128)(2,1)S(1)} fusion(bf16[2,131072]{1,0:T(2,128)(2,1)} %collective-permute-done.3, pred[]{:T(512)S(6)} %eq.59, bf16[1,3,2,262144]{3,2,1,0:T(2,128)(2,1)} %param.15, s32[]{:T(128)S(6)} %select_n.227), kind=kLoop, calls=%fused_computation.1 | loop fusion | flops 262144 | bytes 1572869 | tf_op jit(solution)/shard_map/jit(_where)/select_n | solution.py:75
  34.0 16.3 %collective-permute-done.7 = bf16[2,128,512]{2,1,0:T(8,128)(2,1)S(1)} collective-permute-done((bf16[2,128,512]{2,1,0:T(8,128)(2,1)S(1)}, bf16[2,128,512]{2,1,0:T(8,128)(2,1)S(1)}, u32[]{:S(2)}, u32[]{:S(2)}) %collective-permute-start.7) | collective-permute-done | bytes 262176 | tf_op jit(solution)/shard_map/ppermute | solution.py:104
  51.1 7.1 %collective-permute-start.9 = (bf16[2,128,512]{2,1,0:T(8,128)(2,1)}, bf16[2,128,512]{2,1,0:T(8,128)(2,1)}, u32[]{:S(2)}, u32[]{:S(2)}) collective-permute-start(bf16[2,128,512]{2,1,0:T(8,128)(2,1)} %broadcast_select_fusion.7.refs_5_.refs_3_.refs_1_), channel_id=1, source_target_pairs={{0,4},{5,1},{4,8},{9,5},{8,12},{13,9},{12,14},{15,13},{14,10},{11,... | collective-permute-start | bytes 786440 | tf_op jit(solution)/shard_map/ppermute | solution.py:104
  59.3 1.0 select_select_fusion.refs_2_.refs_0_
  60.3 2.5 %collective-permute-start.5 = (bf16[2,128,512]{2,1,0:T(8,128)(2,1)S(1)}, bf16[2,128,512]{2,1,0:T(8,128)(2,1)S(1)}, u32[]{:S(2)}, u32[]{:S(2)}) collective-permute-start(bf16[2,128,512]{2,1,0:T(8,128)(2,1)S(1)} %select_select_fusion.refs_2_.refs_0_), channel_id=1, source_target_pairs={{0,4},{5,1},{4,8},{9,5},{8,12},{13,9},{12,14},{15,13},{14,10},{11,... | collective-permute-start | bytes 786440 | tf_op jit(solution)/shard_map/ppermute | solution.py:104
  62.8 1.5 collective-permute-start
  64.9 1.8 %collective-permute-done.5 = bf16[2,128,512]{2,1,0:T(8,128)(2,1)S(1)} collective-permute-done((bf16[2,128,512]{2,1,0:T(8,128)(2,1)S(1)}, bf16[2,128,512]{2,1,0:T(8,128)(2,1)S(1)}, u32[]{:S(2)}, u32[]{:S(2)}) %collective-permute-start.5) | collective-permute-done | bytes 262176 | tf_op jit(solution)/shard_map/ppermute | solution.py:104
  67.5 2.5 %collective-permute-start.8 = (bf16[2,128,512]{2,1,0:T(8,128)(2,1)S(1)}, bf16[2,128,512]{2,1,0:T(8,128)(2,1)S(1)}, u32[]{:S(2)}, u32[]{:S(2)}) collective-permute-start(bf16[2,128,512]{2,1,0:T(8,128)(2,1)S(1)} %broadcast_select_fusion.9.refs_4_.refs_2_.refs_0_), channel_id=1, source_target_pairs={{0,4},{5,1},{4,8},{9,5},{8,12},{13,9},{12,14},{15,13},{14,10},{11,... | collective-permute-start | bytes 786440 | tf_op jit(solution)/shard_map/ppermute | solution.py:104
  70.9 1.1 collective-permute-start.13
  72.0 2.1 %collective-permute-done.8.refs_6_.refs_4_.refs_2_ = bf16[2,128,512]{2,1,0:T(8,128)(2,1)S(1)} collective-permute-done((bf16[2,128,512]{2,1,0:T(8,128)(2,1)S(1)}, bf16[2,128,512]{2,1,0:T(8,128)(2,1)S(1)}, u32[]{:S(2)}, u32[]{:S(2)}) %collective-permute-start.8) | collective-permute-done | bytes 262176 | tf_op jit(solution)/shard_map/ppermute | solution.py:104
  74.1 2.2 %collective-permute-start.10 = (bf16[2,128,512]{2,1,0:T(8,128)(2,1)S(1)}, bf16[2,128,512]{2,1,0:T(8,128)(2,1)}, u32[]{:S(2)}, u32[]{:S(2)}) collective-permute-start(bf16[2,128,512]{2,1,0:T(8,128)(2,1)S(1)} %collective-permute-done.8.refs_6_.refs_4_.refs_2_), channel_id=1, source_target_pairs={{0,4},{5,1},{4,8},{9,5},{8,12},{13,9},{12,14},{15,13},{14,10},{11,... | collective-permute-start | bytes 786440 | tf_op jit(solution)/shard_map/ppermute | solution.py:104
  79.3 2.3 %collective-permute-done.10.refs_8_.refs_6_.refs_4_ = bf16[2,128,512]{2,1,0:T(8,128)(2,1)} collective-permute-done((bf16[2,128,512]{2,1,0:T(8,128)(2,1)S(1)}, bf16[2,128,512]{2,1,0:T(8,128)(2,1)}, u32[]{:S(2)}, u32[]{:S(2)}) %collective-permute-start.10) | collective-permute-done | bytes 262176 | tf_op jit(solution)/shard_map/ppermute | solution.py:104
  81.6 1.3 collective-permute-start.12
  83.7 1.3 collective-permute-done.15
  85.0 3.2 %collective-permute-done.12.refs_10_.refs_8_.refs_6_ = bf16[2,128,512]{2,1,0:T(8,128)(2,1)} collective-permute-done((bf16[2,128,512]{2,1,0:T(8,128)(2,1)}, bf16[2,128,512]{2,1,0:T(8,128)(2,1)}, u32[]{:S(2)}, u32[]{:S(2)}) %collective-permute-start.12) | collective-permute-done | bytes 262176 | tf_op jit(solution)/shard_map/ppermute | solution.py:104
  88.2 1.3 collective-permute-start.14
  89.5 2.8 %shard_map.158 = (bf16[2,2,512,512]{3,2,1,0:T(8,128)(2,1)S(1)}, f32[2]{0:T(128)S(1)}) custom-call(s32[32]{0:T(128)S(1)} %copy-done.50, s32[32]{0:T(128)S(1)} %reshape.219.list_ref, s32[6]{0:T(128)S(1)} %stack.27.where_ref, bf16[16,2,32,512]{3,2,1,0:T(8,128)(2,1)S(1)} %all-to-all-done.refs_0_, bf16[16,2,32,512]{3,2,1,0:T(8,128)(2,1)} %collective-permute-done.refs_1_), custom_call_target="tpu_custom_call" | custom-call | flops 2000000000 | bytes 6000000 | tf_op jit(solution)/shard_map/pallas_call | solution.py:271
  92.3 1.3 copy-done.57
  93.7 1.0 broadcast_select_fusion.6.refs_13_.refs_11_.refs_9_
  95.4 1.0 collective-permute-start.30
  99.0 1.3 collective-permute-start.16
  103.4 2.0 %collective-permute-done.17.refs_15_.refs_13_.refs_11_ = bf16[2,128,512]{2,1,0:T(8,128)(2,1)} collective-permute-done((bf16[2,128,512]{2,1,0:T(8,128)(2,1)S(1)}, bf16[2,128,512]{2,1,0:T(8,128)(2,1)}, u32[]{:S(2)}, u32[]{:S(2)}) %collective-permute-start.17) | collective-permute-done | bytes 262176 | tf_op jit(solution)/shard_map/ppermute | solution.py:104
  105.4 2.8 %collective-permute-done.16.refs_14_.refs_12_.refs_10_ = bf16[2,128,512]{2,1,0:T(8,128)(2,1)} collective-permute-done((bf16[2,128,512]{2,1,0:T(8,128)(2,1)}, bf16[2,128,512]{2,1,0:T(8,128)(2,1)}, u32[]{:S(2)}, u32[]{:S(2)}) %collective-permute-start.16) | collective-permute-done | bytes 262176 | tf_op jit(solution)/shard_map/ppermute | solution.py:104
  110.4 1.3 collective-permute-start.18
  114.3 0.9 copy-done.5
  115.3 0.9 copy-done.8
  117.2 0.9 copy-done.15
  118.1 0.9 copy-done.18
  129.5 1.6 copy-done.51
  131.1 1.2 copy-done.53
  132.4 1.0 copy-done.55
  133.4 1.6 copy-done.58
  135.1 6.8 %shard_map.159 = (f32[2,512,512]{2,1,0:T(8,128)S(1)}, s32[1]{0:T(128)}) custom-call(s32[6]{0:T(128)S(1)} %stack.27.where_ref, f32[2]{0:T(128)S(1)} %get-tuple-element.19.sigma_ref, bf16[2,128,512]{2,1,0:T(8,128)(2,1)S(1)} %copy-done.3, bf16[2,128,512]{2,1,0:T(8,128)(2,1)S(1)} %copy-done.2, bf16[2,128,512]{2,1,0:T(8,128)(2,1)S(1)} %select_select_fusion.refs_2_.refs_0_, ...), custom_call_target="tpu_custom_call" | custom-call | flops 5000000000 | bytes 10000000 | tf_op jit(solution)/shard_map/pallas_call | solution.py:291
  142.6 1.2 collective-permute-start.39
  143.9 1.7 %collective-permute-start.37 = (bf16[2,128,512]{2,1,0:T(8,128)(2,1)S(1)}, bf16[2,128,512]{2,1,0:T(8,128)(2,1)S(1)}, u32[]{:S(2)}, u32[]{:S(2)}) collective-permute-start(bf16[2,128,512]{2,1,0:T(8,128)(2,1)S(1)} %broadcast_select_fusion.5.refs_15_.refs_13_), channel_id=1, source_target_pairs={{0,4},{5,1},{4,8},{9,5},{8,12},{13,9},{12,14},{15,13},{14,10},{11,... | collective-permute-start | bytes 786440 | tf_op jit(solution)/shard_map/ppermute | solution.py:104
  146.2 6.5 %shard_map.160 = (f32[2,512,512]{2,1,0:T(8,128)S(1)}, s32[1]{0:T(128)}) custom-call(s32[6]{0:T(128)S(1)} %stack.27.where_ref, f32[2]{0:T(128)S(1)} %get-tuple-element.19.sigma_ref, bf16[2,128,512]{2,1,0:T(8,128)(2,1)S(1)} %select_select_fusion.refs_2_.refs_0_, bf16[2,128,512]{2,1,0:T(8,128)(2,1)S(1)} %copy-done.6, bf16[2,128,512]{2,1,0:T(8,128)(2,1)S(1)} %copy-done.9, ...), custom_call_target="tpu_custom_call" | custom-call | flops 5000000000 | bytes 10000000 | tf_op jit(solution)/shard_map/pallas_call | solution.py:291
  155.4 7.1 %shard_map.161 = (f32[2]{0:T(128)}, f32[2]{0:T(128)}) custom-call(s32[6]{0:T(128)S(1)} %stack.27.where_ref, f32[2]{0:T(128)S(1)} %get-tuple-element.19.sigma_ref, bf16[2,128,512]{2,1,0:T(8,128)(2,1)S(1)} %copy-done.9, bf16[2,128,512]{2,1,0:T(8,128)(2,1)} %broadcast_select_fusion.7.refs_5_.refs_3_.refs_1_, bf16[2,128,512]{2,1,0:T(8,128)(2,1)S(1)} %copy-done.16, ...), custom_call_target="tpu_custom_call" | custom-call | flops 5000000000 | bytes 10000000 | tf_op jit(solution)/shard_map/pallas_call | solution.py:291
  (201 shorter events, 41.3 us)
Async XLA Ops:
  7.9 2.1 %collective-permute-start.1 = (bf16[2,131072]{1,0:T(2,128)(2,1)S(1)}, bf16[2,131072]{1,0:T(2,128)(2,1)S(1)}, u32[]{:S(2)}, u32[]{:S(2)}) collective-permute-start(bf16[2,131072]{1,0:T(2,128)(2,1)S(1)} %dynamic-slice_bitcast_fusion.2), channel_id=1, source_target_pairs={{0,1},{1,0},{2,3},{3,2},{4,5},{5,4},{6,7},{7,6},{8,9},{9,8},{10,11... | collective-permute-start | bytes 1572872 | tf_op jit(solution)/shard_map/ppermute | solution.py:66
  13.1 2.0 %collective-permute-start.2 = (bf16[2,131072]{1,0:T(2,128)(2,1)S(1)}, bf16[2,131072]{1,0:T(2,128)(2,1)S(1)}, u32[]{:S(2)}, u32[]{:S(2)}) collective-permute-start(bf16[2,131072]{1,0:T(2,128)(2,1)S(1)} %dynamic-slice_bitcast_fusion.1), channel_id=1, source_target_pairs={{0,1},{1,0},{2,3},{3,2},{4,5},{5,4},{6,7},{7,6},{8,9},{9,8},{10,11... | collective-permute-start | bytes 1572872 | tf_op jit(solution)/shard_map/ppermute | solution.py:66
  18.6 12.5 %collective-permute-start.3 = (bf16[2,131072]{1,0:T(2,128)(2,1)}, bf16[2,131072]{1,0:T(2,128)(2,1)}, u32[]{:S(2)}, u32[]{:S(2)}) collective-permute-start(bf16[2,131072]{1,0:T(2,128)(2,1)} %dynamic-slice_bitcast_fusion), channel_id=1, source_target_pairs={{0,1},{1,0},{2,3},{3,2},{4,5},{5,4},{6,7},{7,6},{8,9},{9,8},{10,11... | collective-permute-start | bytes 1572872 | tf_op jit(solution)/shard_map/ppermute | solution.py:66
  18.9 9.7 %collective-permute-start.6 = (bf16[2,128,512]{2,1,0:T(8,128)(2,1)S(1)}, bf16[2,128,512]{2,1,0:T(8,128)(2,1)}, u32[]{:S(2)}, u32[]{:S(2)}) collective-permute-start(bf16[2,128,512]{2,1,0:T(8,128)(2,1)S(1)} %get-tuple-element.28.refs_1_), channel_id=1, source_target_pairs={{0,4},{5,1},{4,8},{9,5},{8,12},{13,9},{12,14},{15,13},{14,10},{11,... | collective-permute-start | bytes 786440 | tf_op jit(solution)/shard_map/ppermute | solution.py:104
  21.7 36.5 %all-to-all-start = ((bf16[16,2,32,512]{3,2,1,0:T(8,128)(2,1)}), bf16[16,2,32,512]{3,2,1,0:T(8,128)(2,1)S(1)}, u32[]{:S(2)}, u32[]{:S(2)}) async-start(bf16[16,2,32,512]{3,2,1,0:T(8,128)(2,1)} %reshape.220), calls=%async_computation | async-start | bytes 2097152 | tf_op jit(solution)/shard_map/all_to_all | solution.py:123
  26.7 32.6 %collective-permute-start.4 = (bf16[2,128,512]{2,1,0:T(8,128)(2,1)}, bf16[2,128,512]{2,1,0:T(8,128)(2,1)}, u32[]{:S(2)}, u32[]{:S(2)}) collective-permute-start(bf16[2,128,512]{2,1,0:T(8,128)(2,1)} %get-tuple-element.25.refs_0_), channel_id=1, source_target_pairs={{0,4},{5,1},{4,8},{9,5},{8,12},{13,9},{12,14},{15,13},{14,10},{11,... | collective-permute-start | bytes 786440 | tf_op jit(solution)/shard_map/ppermute | solution.py:104
  29.6 29.7 %copy-start.4 = (bf16[2,128,512]{2,1,0:T(8,128)(2,1)}, bf16[2,128,512]{2,1,0:T(8,128)(2,1)S(1)}, u32[]{:S(2)}) copy-start(bf16[2,128,512]{2,1,0:T(8,128)(2,1)S(1)} %broadcast_select_fusion.8.refs_3_.refs_1_) | copy-start | bytes 786436
  29.6 53.3 %copy-start.60 = (s32[16,2]{0,1:T(2,128)S(1)}, s32[16,2]{0,1:T(2,128)}, u32[]{:S(2)}) copy-start(s32[16,2]{0,1:T(2,128)} %param.18) | copy-start | bytes 388
  29.6 59.9 %copy-start.50 = (s32[32]{0:T(128)S(1)}, s32[32]{0:T(128)}, u32[]{:S(2)}) copy-start(s32[32]{0:T(128)} %cut_ref.1) | copy-start | bytes 388
  29.6 20.8 %collective-permute-start.7 = (bf16[2,128,512]{2,1,0:T(8,128)(2,1)S(1)}, bf16[2,128,512]{2,1,0:T(8,128)(2,1)S(1)}, u32[]{:S(2)}, u32[]{:S(2)}) collective-permute-start(bf16[2,128,512]{2,1,0:T(8,128)(2,1)S(1)} %broadcast_select_fusion.8.refs_3_.refs_1_), channel_id=1, source_target_pairs={{0,4},{5,1},{4,8},{9,5},{8,12},{13,9},{12,14},{15,13},{14,10},{11,... | collective-permute-start | bytes 786440 | tf_op jit(solution)/shard_map/ppermute | solution.py:104
  51.1 13.2 %collective-permute-start.9 = (bf16[2,128,512]{2,1,0:T(8,128)(2,1)}, bf16[2,128,512]{2,1,0:T(8,128)(2,1)}, u32[]{:S(2)}, u32[]{:S(2)}) collective-permute-start(bf16[2,128,512]{2,1,0:T(8,128)(2,1)} %broadcast_select_fusion.7.refs_5_.refs_3_.refs_1_), channel_id=1, source_target_pairs={{0,4},{5,1},{4,8},{9,5},{8,12},{13,9},{12,14},{15,13},{14,10},{11,... | collective-permute-start | bytes 786440 | tf_op jit(solution)/shard_map/ppermute | solution.py:104
  60.3 6.4 %collective-permute-start.5 = (bf16[2,128,512]{2,1,0:T(8,128)(2,1)S(1)}, bf16[2,128,512]{2,1,0:T(8,128)(2,1)S(1)}, u32[]{:S(2)}, u32[]{:S(2)}) collective-permute-start(bf16[2,128,512]{2,1,0:T(8,128)(2,1)S(1)} %select_select_fusion.refs_2_.refs_0_), channel_id=1, source_target_pairs={{0,4},{5,1},{4,8},{9,5},{8,12},{13,9},{12,14},{15,13},{14,10},{11,... | collective-permute-start | bytes 786440 | tf_op jit(solution)/shard_map/ppermute | solution.py:104
  62.8 25.4 %collective-permute-start = (bf16[16,2,32,512]{3,2,1,0:T(8,128)(2,1)S(1)}, bf16[16,2,32,512]{3,2,1,0:T(8,128)(2,1)}, u32[]{:S(2)}, u32[]{:S(2)}) collective-permute-start(bf16[16,2,32,512]{3,2,1,0:T(8,128)(2,1)S(1)} %all-to-all-done.refs_0_), channel_id=1, source_target_pairs={{0,16},{16,0},{1,17},{17,1},{2,18},{18,2},{3,19},{19,3},{4,20},{20... | collective-permute-start | bytes 3145736 | tf_op jit(solution)/shard_map/ppermute | solution.py:128
  64.3 6.6 %collective-permute-start.11 = (bf16[2,128,512]{2,1,0:T(8,128)(2,1)}, bf16[2,128,512]{2,1,0:T(8,128)(2,1)S(1)}, u32[]{:S(2)}, u32[]{:S(2)}) collective-permute-start(bf16[2,128,512]{2,1,0:T(8,128)(2,1)} %collective-permute-done.9.refs_7_.refs_5_.refs_3_), channel_id=1, source_target_pairs={{0,4},{5,1},{4,8},{9,5},{8,12},{13,9},{12,14},{15,13},{14,10},{11,... | collective-permute-start | bytes 786440 | tf_op jit(solution)/shard_map/ppermute | solution.py:104
  67.5 6.6 %collective-permute-start.8 = (bf16[2,128,512]{2,1,0:T(8,128)(2,1)S(1)}, bf16[2,128,512]{2,1,0:T(8,128)(2,1)S(1)}, u32[]{:S(2)}, u32[]{:S(2)}) collective-permute-start(bf16[2,128,512]{2,1,0:T(8,128)(2,1)S(1)} %broadcast_select_fusion.9.refs_4_.refs_2_.refs_0_), channel_id=1, source_target_pairs={{0,4},{5,1},{4,8},{9,5},{8,12},{13,9},{12,14},{15,13},{14,10},{11,... | collective-permute-start | bytes 786440 | tf_op jit(solution)/shard_map/ppermute | solution.py:104
  70.0 6.4 %collective-permute-start.19 = (bf16[2,128,512]{2,1,0:T(8,128)(2,1)}, bf16[2,128,512]{2,1,0:T(8,128)(2,1)S(1)}, u32[]{:S(2)}, u32[]{:S(2)}) collective-permute-start(bf16[2,128,512]{2,1,0:T(8,128)(2,1)} %get-tuple-element.25.refs_0_), channel_id=1, source_target_pairs={{0,1},{1,0},{2,3},{3,2},{4,5},{5,4},{6,7},{7,6},{8,9},{9,8},{10,11... | collective-permute-start | bytes 786440 | tf_op jit(solution)/shard_map/ppermute | solution.py:66
  70.0 7.1 %collective-permute-start.20 = (bf16[2,128,512]{2,1,0:T(8,128)(2,1)}, bf16[2,128,512]{2,1,0:T(8,128)(2,1)S(1)}, u32[]{:S(2)}, u32[]{:S(2)}) collective-permute-start(bf16[2,128,512]{2,1,0:T(8,128)(2,1)} %copy-done.1), channel_id=1, source_target_pairs={{0,1},{1,0},{2,3},{3,2},{4,5},{5,4},{6,7},{7,6},{8,9},{9,8},{10,11... | collective-permute-start | bytes 786440 | tf_op jit(solution)/shard_map/ppermute | solution.py:66
  70.9 7.4 %collective-permute-start.13 = (bf16[2,128,512]{2,1,0:T(8,128)(2,1)S(1)}, bf16[2,128,512]{2,1,0:T(8,128)(2,1)}, u32[]{:S(2)}, u32[]{:S(2)}) collective-permute-start(bf16[2,128,512]{2,1,0:T(8,128)(2,1)S(1)} %collective-permute-done.11.refs_9_.refs_7_.refs_5_), channel_id=1, source_target_pairs={{0,4},{5,1},{4,8},{9,5},{8,12},{13,9},{12,14},{15,13},{14,10},{11,... | collective-permute-start | bytes 786440 | tf_op jit(solution)/shard_map/ppermute | solution.py:104
  74.1 7.4 %collective-permute-start.10 = (bf16[2,128,512]{2,1,0:T(8,128)(2,1)S(1)}, bf16[2,128,512]{2,1,0:T(8,128)(2,1)}, u32[]{:S(2)}, u32[]{:S(2)}) collective-permute-start(bf16[2,128,512]{2,1,0:T(8,128)(2,1)S(1)} %collective-permute-done.8.refs_6_.refs_4_.refs_2_), channel_id=1, source_target_pairs={{0,4},{5,1},{4,8},{9,5},{8,12},{13,9},{12,14},{15,13},{14,10},{11,... | collective-permute-start | bytes 786440 | tf_op jit(solution)/shard_map/ppermute | solution.py:104
  77.1 6.0 %collective-permute-start.22 = (bf16[2,128,512]{2,1,0:T(8,128)(2,1)}, bf16[2,128,512]{2,1,0:T(8,128)(2,1)}, u32[]{:S(2)}, u32[]{:S(2)}) collective-permute-start(bf16[2,128,512]{2,1,0:T(8,128)(2,1)} %copy-done.4), channel_id=1, source_target_pairs={{0,1},{1,0},{2,3},{3,2},{4,5},{5,4},{6,7},{7,6},{8,9},{9,8},{10,11... | collective-permute-start | bytes 786440 | tf_op jit(solution)/shard_map/ppermute | solution.py:66
  77.8 5.4 %collective-permute-start.24 = (bf16[2,128,512]{2,1,0:T(8,128)(2,1)}, bf16[2,128,512]{2,1,0:T(8,128)(2,1)}, u32[]{:S(2)}, u32[]{:S(2)}) collective-permute-start(bf16[2,128,512]{2,1,0:T(8,128)(2,1)} %broadcast_select_fusion.7.refs_5_.refs_3_.refs_1_), channel_id=1, source_target_pairs={{0,1},{1,0},{2,3},{3,2},{4,5},{5,4},{6,7},{7,6},{8,9},{9,8},{10,11... | collective-permute-start | bytes 786440 | tf_op jit(solution)/shard_map/ppermute | solution.py:66
  78.3 6.7 %collective-permute-start.15 = (bf16[2,128,512]{2,1,0:T(8,128)(2,1)}, bf16[2,128,512]{2,1,0:T(8,128)(2,1)}, u32[]{:S(2)}, u32[]{:S(2)}) collective-permute-start(bf16[2,128,512]{2,1,0:T(8,128)(2,1)} %collective-permute-done.13.refs_11_.refs_9_.refs_7_), channel_id=1, source_target_pairs={{0,4},{5,1},{4,8},{9,5},{8,12},{13,9},{12,14},{15,13},{14,10},{11,... | collective-permute-start | bytes 786440 | tf_op jit(solution)/shard_map/ppermute | solution.py:104
  81.6 6.7 %collective-permute-start.12 = (bf16[2,128,512]{2,1,0:T(8,128)(2,1)}, bf16[2,128,512]{2,1,0:T(8,128)(2,1)}, u32[]{:S(2)}, u32[]{:S(2)}) collective-permute-start(bf16[2,128,512]{2,1,0:T(8,128)(2,1)} %collective-permute-done.10.refs_8_.refs_6_.refs_4_), channel_id=1, source_target_pairs={{0,4},{5,1},{4,8},{9,5},{8,12},{13,9},{12,14},{15,13},{14,10},{11,... | collective-permute-start | bytes 786440 | tf_op jit(solution)/shard_map/ppermute | solution.py:104
  83.1 13.9 %copy-start.14 = (bf16[2,128,512]{2,1,0:T(8,128)(2,1)S(1)}, bf16[2,128,512]{2,1,0:T(8,128)(2,1)}, u32[]{:S(2)}) copy-start(bf16[2,128,512]{2,1,0:T(8,128)(2,1)} %copy-done.13) | copy-start | bytes 786436
  83.1 17.1 %copy-start.61 = (s32[3]{0:T(128)S(1)}, s32[3]{0:T(128)}, u32[]{:S(2)}) copy-start(s32[3]{0:T(128)} %param.20) | copy-start | bytes 40
  83.1 11.5 %collective-permute-start.26 = (bf16[2,128,512]{2,1,0:T(8,128)(2,1)}, bf16[2,128,512]{2,1,0:T(8,128)(2,1)S(1)}, u32[]{:S(2)}, u32[]{:S(2)}) collective-permute-start(bf16[2,128,512]{2,1,0:T(8,128)(2,1)} %collective-permute-done.9.refs_7_.refs_5_.refs_3_), channel_id=1, source_target_pairs={{0,1},{1,0},{2,3},{3,2},{4,5},{5,4},{6,7},{7,6},{8,9},{9,8},{10,11... | collective-permute-start | bytes 786440 | tf_op jit(solution)/shard_map/ppermute | solution.py:66
  83.2 13.2 %collective-permute-start.21 = (bf16[2,128,512]{2,1,0:T(8,128)(2,1)S(1)}, bf16[2,128,512]{2,1,0:T(8,128)(2,1)S(1)}, u32[]{:S(2)}, u32[]{:S(2)}) collective-permute-start(bf16[2,128,512]{2,1,0:T(8,128)(2,1)S(1)} %select_select_fusion.refs_2_.refs_0_), channel_id=1, source_target_pairs={{0,1},{1,0},{2,3},{3,2},{4,5},{5,4},{6,7},{7,6},{8,9},{9,8},{10,11... | collective-permute-start | bytes 786440 | tf_op jit(solution)/shard_map/ppermute | solution.py:66
  85.0 12.0 %collective-permute-start.28 = (bf16[2,128,512]{2,1,0:T(8,128)(2,1)}, bf16[2,128,512]{2,1,0:T(8,128)(2,1)S(1)}, u32[]{:S(2)}, u32[]{:S(2)}) collective-permute-start(bf16[2,128,512]{2,1,0:T(8,128)(2,1)} %copy-done.10), channel_id=1, source_target_pairs={{0,1},{1,0},{2,3},{3,2},{4,5},{5,4},{6,7},{7,6},{8,9},{9,8},{10,11... | collective-permute-start | bytes 786440 | tf_op jit(solution)/shard_map/ppermute | solution.py:66
  88.2 10.0 %collective-permute-start.23 = (bf16[2,128,512]{2,1,0:T(8,128)(2,1)}, bf16[2,128,512]{2,1,0:T(8,128)(2,1)S(1)}, u32[]{:S(2)}, u32[]{:S(2)}) collective-permute-start(bf16[2,128,512]{2,1,0:T(8,128)(2,1)} %copy-done.7), channel_id=1, source_target_pairs={{0,1},{1,0},{2,3},{3,2},{4,5},{5,4},{6,7},{7,6},{8,9},{9,8},{10,11... | collective-permute-start | bytes 786440 | tf_op jit(solution)/shard_map/ppermute | solution.py:66
  88.2 10.7 %collective-permute-start.14 = (bf16[2,128,512]{2,1,0:T(8,128)(2,1)}, bf16[2,128,512]{2,1,0:T(8,128)(2,1)}, u32[]{:S(2)}, u32[]{:S(2)}) collective-permute-start(bf16[2,128,512]{2,1,0:T(8,128)(2,1)} %collective-permute-done.12.refs_10_.refs_8_.refs_6_), channel_id=1, source_target_pairs={{0,4},{5,1},{4,8},{9,5},{8,12},{13,9},{12,14},{15,13},{14,10},{11,... | collective-permute-start | bytes 786440 | tf_op jit(solution)/shard_map/ppermute | solution.py:104
  95.4 4.9 %collective-permute-start.30 = (bf16[2,128,512]{2,1,0:T(8,128)(2,1)}, bf16[2,128,512]{2,1,0:T(8,128)(2,1)S(1)}, u32[]{:S(2)}, u32[]{:S(2)}) collective-permute-start(bf16[2,128,512]{2,1,0:T(8,128)(2,1)} %collective-permute-done.13.refs_11_.refs_9_.refs_7_), channel_id=1, source_target_pairs={{0,1},{1,0},{2,3},{3,2},{4,5},{5,4},{6,7},{7,6},{8,9},{9,8},{10,11... | collective-permute-start | bytes 786440 | tf_op jit(solution)/shard_map/ppermute | solution.py:66
  97.1 4.5 %collective-permute-start.25 = (bf16[2,128,512]{2,1,0:T(8,128)(2,1)S(1)}, bf16[2,128,512]{2,1,0:T(8,128)(2,1)S(1)}, u32[]{:S(2)}, u32[]{:S(2)}) collective-permute-start(bf16[2,128,512]{2,1,0:T(8,128)(2,1)S(1)} %copy-done.14), channel_id=1, source_target_pairs={{0,1},{1,0},{2,3},{3,2},{4,5},{5,4},{6,7},{7,6},{8,9},{9,8},{10,11... | collective-permute-start | bytes 786440 | tf_op jit(solution)/shard_map/ppermute | solution.py:66
  97.8 4.5 %collective-permute-start.27 = (bf16[2,128,512]{2,1,0:T(8,128)(2,1)}, bf16[2,128,512]{2,1,0:T(8,128)(2,1)S(1)}, u32[]{:S(2)}, u32[]{:S(2)}) collective-permute-start(bf16[2,128,512]{2,1,0:T(8,128)(2,1)} %collective-permute-done.10.refs_8_.refs_6_.refs_4_), channel_id=1, source_target_pairs={{0,1},{1,0},{2,3},{3,2},{4,5},{5,4},{6,7},{7,6},{8,9},{9,8},{10,11... | collective-permute-start | bytes 786440 | tf_op jit(solution)/shard_map/ppermute | solution.py:66
  99.0 6.5 %collective-permute-start.17 = (bf16[2,128,512]{2,1,0:T(8,128)(2,1)S(1)}, bf16[2,128,512]{2,1,0:T(8,128)(2,1)}, u32[]{:S(2)}, u32[]{:S(2)}) collective-permute-start(bf16[2,128,512]{2,1,0:T(8,128)(2,1)S(1)} %broadcast_select_fusion.6.refs_13_.refs_11_.refs_9_), channel_id=1, source_target_pairs={{0,4},{5,1},{4,8},{9,5},{8,12},{13,9},{12,14},{15,13},{14,10},{11,... | collective-permute-start | bytes 786440 | tf_op jit(solution)/shard_map/ppermute | solution.py:104
  99.0 9.3 %collective-permute-start.16 = (bf16[2,128,512]{2,1,0:T(8,128)(2,1)}, bf16[2,128,512]{2,1,0:T(8,128)(2,1)}, u32[]{:S(2)}, u32[]{:S(2)}) collective-permute-start(bf16[2,128,512]{2,1,0:T(8,128)(2,1)} %collective-permute-done.14.refs_12_.refs_10_.refs_8_), channel_id=1, source_target_pairs={{0,4},{5,1},{4,8},{9,5},{8,12},{13,9},{12,14},{15,13},{14,10},{11,... | collective-permute-start | bytes 786440 | tf_op jit(solution)/shard_map/ppermute | solution.py:104
  101.0 8.0 %collective-permute-start.29 = (bf16[2,128,512]{2,1,0:T(8,128)(2,1)}, bf16[2,128,512]{2,1,0:T(8,128)(2,1)S(1)}, u32[]{:S(2)}, u32[]{:S(2)}) collective-permute-start(bf16[2,128,512]{2,1,0:T(8,128)(2,1)} %collective-permute-done.12.refs_10_.refs_8_.refs_6_), channel_id=1, source_target_pairs={{0,1},{1,0},{2,3},{3,2},{4,5},{5,4},{6,7},{7,6},{8,9},{9,8},{10,11... | collective-permute-start | bytes 786440 | tf_op jit(solution)/shard_map/ppermute | solution.py:66
  102.2 7.5 %collective-permute-start.32 = (bf16[2,128,512]{2,1,0:T(8,128)(2,1)S(1)}, bf16[2,128,512]{2,1,0:T(8,128)(2,1)S(1)}, u32[]{:S(2)}, u32[]{:S(2)}) collective-permute-start(bf16[2,128,512]{2,1,0:T(8,128)(2,1)S(1)} %broadcast_select_fusion.6.refs_13_.refs_11_.refs_9_), channel_id=1, source_target_pairs={{0,1},{1,0},{2,3},{3,2},{4,5},{5,4},{6,7},{7,6},{8,9},{9,8},{10,11... | collective-permute-start | bytes 786440 | tf_op jit(solution)/shard_map/ppermute | solution.py:66
  102.9 8.8 %collective-permute-start.31 = (bf16[2,128,512]{2,1,0:T(8,128)(2,1)}, bf16[2,128,512]{2,1,0:T(8,128)(2,1)S(1)}, u32[]{:S(2)}, u32[]{:S(2)}) collective-permute-start(bf16[2,128,512]{2,1,0:T(8,128)(2,1)} %collective-permute-done.14.refs_12_.refs_10_.refs_8_), channel_id=1, source_target_pairs={{0,1},{1,0},{2,3},{3,2},{4,5},{5,4},{6,7},{7,6},{8,9},{9,8},{10,11... | collective-permute-start | bytes 786440 | tf_op jit(solution)/shard_map/ppermute | solution.py:66
  105.4 7.0 %collective-permute-start.34 = (bf16[2,128,512]{2,1,0:T(8,128)(2,1)}, bf16[2,128,512]{2,1,0:T(8,128)(2,1)}, u32[]{:S(2)}, u32[]{:S(2)}) collective-permute-start(bf16[2,128,512]{2,1,0:T(8,128)(2,1)} %collective-permute-done.17.refs_15_.refs_13_.refs_11_), channel_id=1, source_target_pairs={{0,1},{1,0},{2,3},{3,2},{4,5},{5,4},{6,7},{7,6},{8,9},{9,8},{10,11... | collective-permute-start | bytes 786440 | tf_op jit(solution)/shard_map/ppermute | solution.py:66
  108.3 4.2 %collective-permute-start.33 = (bf16[2,128,512]{2,1,0:T(8,128)(2,1)}, bf16[2,128,512]{2,1,0:T(8,128)(2,1)}, u32[]{:S(2)}, u32[]{:S(2)}) collective-permute-start(bf16[2,128,512]{2,1,0:T(8,128)(2,1)} %collective-permute-done.16.refs_14_.refs_12_.refs_10_), channel_id=1, source_target_pairs={{0,1},{1,0},{2,3},{3,2},{4,5},{5,4},{6,7},{7,6},{8,9},{9,8},{10,11... | collective-permute-start | bytes 786440 | tf_op jit(solution)/shard_map/ppermute | solution.py:66
  109.7 32.8 %collective-permute-start.35 = (bf16[2,128,512]{2,1,0:T(8,128)(2,1)}, bf16[2,128,512]{2,1,0:T(8,128)(2,1)S(1)}, u32[]{:S(2)}, u32[]{:S(2)}) collective-permute-start(bf16[2,128,512]{2,1,0:T(8,128)(2,1)} %collective-permute-done.17.refs_15_.refs_13_.refs_11_), channel_id=1, source_target_pairs={{0,4},{5,1},{4,8},{9,5},{8,12},{13,9},{12,14},{15,13},{14,10},{11,... | collective-permute-start | bytes 786440 | tf_op jit(solution)/shard_map/ppermute | solution.py:104
  110.4 33.3 %collective-permute-start.18 = (bf16[2,128,512]{2,1,0:T(8,128)(2,1)}, bf16[2,128,512]{2,1,0:T(8,128)(2,1)S(1)}, u32[]{:S(2)}, u32[]{:S(2)}) collective-permute-start(bf16[2,128,512]{2,1,0:T(8,128)(2,1)} %collective-permute-done.16.refs_14_.refs_12_.refs_10_), channel_id=1, source_target_pairs={{0,4},{5,1},{4,8},{9,5},{8,12},{13,9},{12,14},{15,13},{14,10},{11,... | collective-permute-start | bytes 786440 | tf_op jit(solution)/shard_map/ppermute | solution.py:104
  142.6 3.5 %collective-permute-start.39 = (bf16[2,128,512]{2,1,0:T(8,128)(2,1)S(1)}, bf16[2,128,512]{2,1,0:T(8,128)(2,1)S(1)}, u32[]{:S(2)}, u32[]{:S(2)}) collective-permute-start(bf16[2,128,512]{2,1,0:T(8,128)(2,1)S(1)} %broadcast_select_fusion.5.refs_15_.refs_13_), channel_id=1, source_target_pairs={{0,1},{1,0},{2,3},{3,2},{4,5},{5,4},{6,7},{7,6},{8,9},{9,8},{10,11... | collective-permute-start | bytes 786440 | tf_op jit(solution)/shard_map/ppermute | solution.py:66
  143.8 2.3 %collective-permute-start.38 = (bf16[2,128,512]{2,1,0:T(8,128)(2,1)S(1)}, bf16[2,128,512]{2,1,0:T(8,128)(2,1)S(1)}, u32[]{:S(2)}, u32[]{:S(2)}) collective-permute-start(bf16[2,128,512]{2,1,0:T(8,128)(2,1)S(1)} %collective-permute-done.18.refs_14_.refs_12_), channel_id=1, source_target_pairs={{0,1},{1,0},{2,3},{3,2},{4,5},{5,4},{6,7},{7,6},{8,9},{9,8},{10,11... | collective-permute-start | bytes 786440 | tf_op jit(solution)/shard_map/ppermute | solution.py:66
  143.9 9.5 %collective-permute-start.37 = (bf16[2,128,512]{2,1,0:T(8,128)(2,1)S(1)}, bf16[2,128,512]{2,1,0:T(8,128)(2,1)S(1)}, u32[]{:S(2)}, u32[]{:S(2)}) collective-permute-start(bf16[2,128,512]{2,1,0:T(8,128)(2,1)S(1)} %broadcast_select_fusion.5.refs_15_.refs_13_), channel_id=1, source_target_pairs={{0,4},{5,1},{4,8},{9,5},{8,12},{13,9},{12,14},{15,13},{14,10},{11,... | collective-permute-start | bytes 786440 | tf_op jit(solution)/shard_map/ppermute | solution.py:104
  145.5 8.0 %collective-permute-start.36 = (bf16[2,128,512]{2,1,0:T(8,128)(2,1)S(1)}, bf16[2,128,512]{2,1,0:T(8,128)(2,1)S(1)}, u32[]{:S(2)}, u32[]{:S(2)}) collective-permute-start(bf16[2,128,512]{2,1,0:T(8,128)(2,1)S(1)} %collective-permute-done.18.refs_14_.refs_12_), channel_id=1, source_target_pairs={{0,4},{5,1},{4,8},{9,5},{8,12},{13,9},{12,14},{15,13},{14,10},{11,... | collective-permute-start | bytes 786440 | tf_op jit(solution)/shard_map/ppermute | solution.py:104
  153.4 1.6 collective-permute-start.41
  153.5 1.9 %collective-permute-start.40 = (bf16[2,128,512]{2,1,0:T(8,128)(2,1)S(1)}, bf16[2,128,512]{2,1,0:T(8,128)(2,1)S(1)}, u32[]{:S(2)}, u32[]{:S(2)}) collective-permute-start(bf16[2,128,512]{2,1,0:T(8,128)(2,1)S(1)} %broadcast_select_fusion.4), channel_id=1, source_target_pairs={{0,1},{1,0},{2,3},{3,2},{4,5},{5,4},{6,7},{7,6},{8,9},{9,8},{10,11... | collective-permute-start | bytes 786440 | tf_op jit(solution)/shard_map/ppermute | solution.py:66
  (57 other events, 228.4 us)

commit v12 on v10

--- a/solution.py
+++ b/solution.py
@@ -16,8 +16,6 @@
 ROW_STEP = 16
 WAVE_ROWS = 32
 CORES = 2
-PAIR = 2
-QUAD = CORES * PAIR
 VMEM_LIMIT = 24 * 1024 * 1024
 
 
@@ -56,49 +54,22 @@
     return rows, cols
 
 
-def partner(flip):
-    return [(at, at ^ flip) for at in range(lax.axis_size("tpl"))]
-
-
-def swap(block, flip):
-    return lax.ppermute(block, "tpl", partner(flip))
-
-
-def quarter_of(strain_slots, det, owner):
+def swap(block):
+    return lax.ppermute(block, "tpl", [(at, at ^ 1) for at in range(lax.axis_size("tpl"))])
+
+
+def spread(strain_slots, det, owner):
+    devices = lax.axis_size("tpl")
     me = lax.axis_index("tpl")
-    core, chip = me % CORES, me // CORES % PAIR
+    core = me % CORES
     half = ROWS * COLS // CORES
-    bins = half // PAIR
     side = lambda which: lax.dynamic_slice(strain_slots, (0, det, 0, which * half), (1, 1, 2, half))[0, 0]
-    got = swap(side(1 - core), 1)
-    kept = jnp.where(core == owner % CORES, side(core), got)
-    got = swap(jnp.where(chip == 0, kept[:, bins:], kept[:, :bins]), CORES)
-    kept = jnp.where(chip == 0, kept[:, :bins], kept[:, bins:])
-    return jnp.where(chip == owner // CORES % PAIR, kept, got).reshape(2, ROWS // QUAD, COLS)
-
-
-def along_line(quarter, owner):
-    lines = lax.axis_size("tpl") // QUAD
-    line, from_line = lax.axis_index("tpl") // QUAD, owner // QUAD
-    if lines == 1:
-        return quarter
-    odd = line % 2 == 1
-    quarter = jnp.where(line % 2 == from_line % 2, quarter, swap(quarter, QUAD))
-    if lines == 2:
-        return quarter
-    rows = quarter.shape[1] // 2
-    piece = jnp.where(odd, quarter[:, rows:], quarter[:, :rows])
-    bit = 2
-    while bit < lines:
-        piece = jnp.where(line // bit % 2 == from_line // bit % 2, piece, swap(piece, bit * QUAD))
-        bit *= 2
-    other = swap(piece, QUAD)
-    return jnp.concatenate([jnp.where(odd, other, piece), jnp.where(odd, piece, other)], 1)
-
-
-def all_quarters(quarter):
-    beside = swap(quarter, CORES)
-    return quarter, beside, swap(quarter, 1), swap(beside, 1)
+    got = swap(side(1 - core))
+    kept = jnp.where(core == owner % CORES, side(core), got).reshape(2, ROWS // CORES, COLS)
+    kept = jnp.where(me // CORES == owner // CORES, kept, jnp.zeros_like(kept))
+    same_core = [list(range(first, devices, CORES)) for first in range(CORES)]
+    near = lax.psum(kept, "tpl", axis_index_groups=same_core)
+    return near, swap(near)
 
 
 def collect(templates, lists):
@@ -146,7 +117,7 @@
 def prepare_kernel(count, cut_ref, list_ref, where_ref, *refs):
     wave_refs, (masked_ref, sigma_ref) = refs[:-2], refs[-2:]
     for tpl in range(count):
-        cutoff = cut_ref[list_ref[where_ref[2] * count + where_ref[3 + tpl]]]
+        cutoff = cut_ref[list_ref[where_ref[1] * count + where_ref[2 + tpl]]]
         total = jnp.zeros((8, COLS), jnp.float32)
         for block in range(ROWS // WAVE_ROWS):
             part = slice(block * WAVE_ROWS, (block + 1) * WAVE_ROWS)
@@ -163,26 +134,27 @@
 
 def detector_kernel(det, where_ref, sigma_ref, *refs):
     first, last = det == 0, det == DET - 1
-    quarter_refs, refs = refs[:QUAD], refs[QUAD:]
+    half_refs, refs = refs[:CORES], refs[CORES:]
     masked, rphase_ref, cphase_ref, row_ref, col_ref, twiddle_ref = refs[:6]
     refs = refs[6:]
     before, refs = (None, refs) if first else (refs[0], refs[1:])
     outputs, (turned_ref, slid, stacked, twisted) = refs[:-4], refs[-4:]
     count = masked.shape[0]
-    core, chip = where_ref[0], where_ref[1]
-    half, rows = ROWS // CORES, ROWS // QUAD
+    core, half = where_ref[0], ROWS // CORES
 
     turned_ref[...] = rphase_ref[det].T
     cc, cs = cphase_ref[det, 0:1, :], cphase_ref[det, 1:2, :]
-    for which, quarter in enumerate(quarter_refs):
-        of_core, of_chip = (core if which < 2 else 1 - core), (chip if which % 2 == 0 else 1 - chip)
-        part = pl.ds(pl.multiple_of(of_core * half + of_chip * rows, rows), rows)
-        rc, rs = turned_ref[part, 0:1], turned_ref[part, 1:2]
-        turn_re = rc * cc - rs * cs
-        turn_im = rc * cs + rs * cc
-        data_re, data_im = quarter[0].astype(jnp.float32), quarter[1].astype(jnp.float32)
-        slid[0, part, :] = data_re * turn_re - data_im * turn_im
-        slid[1, part, :] = data_re * turn_im + data_im * turn_re
+    for which, half_ref in enumerate(half_refs):
+        of_core = core if which == 0 else 1 - core
+        for at in range(0, half, PART):
+            part = pl.ds(pl.multiple_of(of_core * half + at, PART), PART)
+            rc, rs = turned_ref[part, 0:1], turned_ref[part, 1:2]
+            turn_re = rc * cc - rs * cs
+            turn_im = rc * cs + rs * cc
+            data_re = half_ref[0, at : at + PART].astype(jnp.float32)
+            data_im = half_ref[1, at : at + PART].astype(jnp.float32)
+            slid[0, part, :] = data_re * turn_re - data_im * turn_im
+            slid[1, part, :] = data_re * turn_im + data_im * turn_re
 
     largest = []
     for tpl in range(count):
@@ -231,7 +203,7 @@
 
     if last:
         for tpl in range(count):
-            place = where_ref[3 + tpl]
+            place = where_ref[2 + tpl]
             outputs[0][place] = jnp.max(largest[tpl]) / (2.0 * (sigma_ref[tpl] + eps_norm))
             outputs[1][place] = sigma_ref[tpl] / (ROWS * COLS)
 
@@ -286,18 +258,13 @@
     picked = collect(templates, lists) if direct else collect_plain(templates, lists)
     strain_slots, picked = lax.optimization_barrier((strain_slots, picked))
     arrived = exchange(picked) if direct else picked
-    where = jnp.stack([jnp.asarray(at, jnp.int32) for at in (me % CORES, me // CORES % PAIR, me, *places)])
-    small = (*slide_turns(slides), where, lists.reshape(-1))
-    quarter = []
+    where = jnp.stack([jnp.asarray(at, jnp.int32) for at in (me % CORES, me, *places)])
+    found = []
     for det in range(DET):
-        quarter.append(quarter_of(strain_slots, det, owner))
-        strain_slots, quarter[det] = lax.optimization_barrier((strain_slots, quarter[det]))
-    quarter[-1], arrived, small = lax.optimization_barrier((quarter[-1], arrived, small))
-    *turns, where, flat_list = small
-
-    found = [all_quarters(along_line(part, owner)) for part in quarter]
+        found.append(spread(strain_slots, det, owner))
+    turns = slide_turns(slides)
     waves = [across(arrived, turn) for turn in range(per_device)] if direct else arrived
-    masked, sigma = prepare(cutoffs, flat_list, where, waves)
+    masked, sigma = prepare(cutoffs, lists.reshape(-1), where, waves)
     result = ()
     for det in range(DET):
         result = detector(det, where, sigma, found[det], masked, turns, result)

time: 137 us -> 162 us (1.18)
  waiting for transfers between devices: 62.1 us -> 99.7 us
  starting transfers between devices: 25.5 us -> 10.2 us
  between operations: 2.09 us -> 15 us
  other arithmetic: 14.9 us -> 4.86 us
  local copies, waits for them, and re-layouts: 13.6 us -> 10.8 us
  Pallas kernels: 19.4 us -> 21.3 us
    psum x0 -> x1, waiting for transfers between devices: none -> 77.5 us  [spread(): near = lax.psum(kept, 'tpl', axis_index_groups=same_core)]
    ppermute x24 -> x6, waiting for transfers between devices: 62.1 us -> 0.02 us  [swap(): lax.ppermute(block, 'tpl', [(at, at ^ 1) for at in range(lax.axis_size('t...]
    all_to_all x1, waiting for transfers between devices: 0.01 us -> 22.1 us  [exchange(): return lax.all_to_all(block, 'tpl', split_axis=0, concat_axis=0, tiled=True)]
    ppermute x24 -> x6, starting transfers between devices: 17.6 us -> 1.59 us  [swap(): lax.ppermute(block, 'tpl', [(at, at ^ 1) for at in range(lax.axis_size('t...]
    select_n x21 -> x1, other arithmetic: 13.4 us -> 3.38 us  [spread(): kept = jnp.where(me // CORES == owner // CORES, kept, jnp.zeros_like(kept))]
    squeeze x3 -> x1, local copies, waits for them, and re-layouts: 5.88 us -> 3.44 us  [spread(): lax.dynamic_slice(strain_slots, (0, det, 0, which * half), (1, 1, 2, half))]
  transfers between devices with their start and end apart: 26 -> 9, of which waited for: 14 -> 2; matrix products, arithmetic and copies ran while one was open for 12% -> 4% of each run, Pallas kernels for 10% -> 9%
where the time goes in v12:
time: 162 us
  waiting for transfers between devices  99.7 us (62%)
  Pallas kernels  21.3 us (13%)
  between operations  15 us (9%)
  local copies, waits for them, and re-layouts  10.8 us (7%)
  starting transfers between devices  10.2 us (6%)
  other arithmetic  4.86 us (3%)
    psum x1, waiting for transfers between devices, spread(): near = lax.psum(kept, 'tpl', axis_index_groups=same_core)  77.5 us
    all_to_all x1, waiting for transfers between devices, exchange(): return lax.all_to_all(block, 'tpl', split_axis=0, concat_axis=0, tiled=True)  22.1 us
    pallas_call x3, Pallas kernels, detector(): pl.pallas_call(functools.partial(detector_kernel, det), out_shape=(scalar...  18.4 us
    all_to_all x1, starting transfers between devices, exchange(): return lax.all_to_all(block, 'tpl', split_axis=0, concat_axis=0, tiled=True)  7.05 us
    squeeze x1, local copies, waits for them, and re-layouts, spread(): lax.dynamic_slice(strain_slots, (0, det, 0, which * half), (1, 1, 2, half))  3.44 us
    select_n x1, other arithmetic, spread(): kept = jnp.where(me // CORES == owner // CORES, kept, jnp.zeros_like(kept))  3.38 us
  transfers between devices with their start and end apart: 9, of which 2 were waited for; matrix products, arithmetic and copies ran while one was open for 4% of the time, Pallas kernels for 9%

profile of v12, /device:TPU:0, one launch (start us, length us, event | category | flops | bytes accessed | tf_op | source)
XLA Modules:
  0.0 161.8 jit_solution(53318760452890457)
XLA Ops:
  7.2 0.0 copy-start
  7.2 0.8 fusion.11
  8.0 0.7 copy-done
  8.8 2.7 %gather_fusion = bf16[16,2,16384]{2,1,0:T(2,128)(2,1)S(1)} fusion(bf16[32,2,16384]{2,1,0:T(2,128)(2,1)S(1)} %copy-done, s32[1024]{0:T(1024)S(1)} %pad_clamp_fusion), kind=kCustom, calls=%fused_computation | custom fusion | bytes 2097216 | tf_op jit(solution)/shard_map/gather | solution.py:77
  11.4 1.6 reshape.205
  13.0 3.4 %dynamic-slice_bitcast_fusion = (bf16[2,131072]{1,0:T(2,128)(2,1)}, bf16[2,131072]{1,0:T(2,128)(2,1)}, bf16[2,131072]{1,0:T(2,128)(2,1)}) fusion(bf16[1,3,2,262144]{3,2,1,0:T(2,128)(2,1)} %param.15, s32[]{:T(128)S(6)} %select_n.148), kind=kLoop, calls=%fused_computation.10 | loop fusion | bytes 3145732 | tf_op jit(solution)/shard_map/squeeze | solution.py:66
  16.4 0.5 collective-permute-start.1
  16.9 0.1 collective-permute-start.3
  17.0 0.5 collective-permute-start.5
  17.4 7.0 %all-to-all-start = ((bf16[16,2,32,512]{3,2,1,0:T(8,128)(2,1)}), bf16[16,2,32,512]{3,2,1,0:T(8,128)(2,1)S(1)}, u32[]{:S(2)}, u32[]{:S(2)}) async-start(bf16[16,2,32,512]{3,2,1,0:T(8,128)(2,1)} %reshape.205), calls=%async_computation | async-start | bytes 2097152 | tf_op jit(solution)/shard_map/all_to_all | solution.py:81
  24.5 0.0 all-reduce.3.cloned.1.call-start
  25.2 0.0 collective-permute-done.1
  25.2 0.0 collective-permute-done.3
  25.2 0.0 collective-permute-done.5
  25.2 3.4 %broadcast_select_fusion.3 = (bf16[2,131072]{1,0:T(2,128)(2,1)S(1)}, bf16[2,131072]{1,0:T(2,128)(2,1)S(1)}, bf16[2,131072]{1,0:T(2,128)(2,1)S(1)}) fusion(pred[]{:T(512)S(6)} %eq.25, bf16[2,131072]{1,0:T(2,128)(2,1)} %collective-permute-done.5, pred[]{:T(512)S(6)} %eq.26, bf16[1,3,2,262144]{3,2,1,0:T(2,128)(2,1)} %param.15, s32[]{:T(128)S(6)} %select_n.147, ...), kind=kLoop, calls=%fused_computation.4 | loop fusion | flops 1572864 | bytes 4718598 | tf_op jit(solution)/shard_map/jit(_where)/select_n | solution.py:69
  28.6 0.8 copy.25
  29.5 1.1 copy_bitcast_fusion
  30.6 0.0 all-reduce.3.cloned.1.call-update
  30.6 22.1 %all-to-all-done.refs_0_ = bf16[16,2,32,512]{3,2,1,0:T(8,128)(2,1)S(1)} async-done(((bf16[16,2,32,512]{3,2,1,0:T(8,128)(2,1)}), bf16[16,2,32,512]{3,2,1,0:T(8,128)(2,1)S(1)}, u32[]{:S(2)}, u32[]{:S(2)}) %all-to-all-start) | async-done | bytes 1048608 | tf_op jit(solution)/shard_map/all_to_all | solution.py:81
  52.7 1.5 collective-permute-start
  54.2 0.0 copy-done.8
  54.2 0.1 copy.18
  54.3 0.1 reshape.204.list_ref
  54.4 0.0 copy-done.9
  54.5 0.3 fusion.8
  54.7 0.1 concatenate.6.refs_3_
  54.8 77.5 %all-reduce.3.cloned.1.call-done = (bf16[2,256,512]{2,1,0:T(8,128)(2,1)}, bf16[2,256,512]{2,1,0:T(8,128)(2,1)}, bf16[2,256,512]{2,1,0:T(8,128)(2,1)}) async-done(((bf16[2,256,512]{2,1,0:T(8,128)(2,1)}, bf16[2,256,512]{2,1,0:T(8,128)(2,1)}, bf16[2,256,512]{2,1,0:T(8,128)(2,1)}), (bf16[2,256,512]{2,1,0:T(8,128)(2,1)}, bf16[2,256,512]{2,1,0:T(8,128)(2,1)}, ...) | async-done | bytes 1572880 | tf_op jit(solution)/shard_map/psum | solution.py:71
  132.4 0.0 collective-permute-start.6
  132.4 0.3 fusion.6
  132.7 0.1 concatenate.7.refs_4_
  132.8 0.1 pad_add_fusion.where_ref
  132.9 0.5 collective-permute-start.4
  133.3 0.1 collective-permute-start.2
  133.4 0.0 collective-permute-done.refs_1_
  133.5 0.0 copy-done.4
  133.5 2.9 %shard_map.158 = (bf16[2,2,512,512]{3,2,1,0:T(8,128)(2,1)S(1)}, f32[2]{0:T(128)S(1)}) custom-call(s32[32]{0:T(128)S(1)} %copy-done.4, s32[32]{0:T(128)S(1)} %reshape.204.list_ref, s32[4]{0:T(128)S(1)} %pad_add_fusion.where_ref, bf16[16,2,32,512]{3,2,1,0:T(8,128)(2,1)S(1)} %all-to-all-done.refs_0_, bf16[16,2,32,512]{3,2,1,0:T(8,128)(2,1)} %collective-permute-done.refs_1_), custom_call_target="tpu_custom_call" | custom-call | flops 2000000000 | bytes 6000000 | tf_op jit(solution)/shard_map/pallas_call | solution.py:217
  136.4 0.0 collective-permute-done.6.refs_1_
  136.4 0.0 copy-done.3
  136.4 0.0 copy-done.5
  136.4 0.0 copy-done.6
  136.4 0.0 copy-done.7
  136.4 0.0 copy-start.2
  136.4 6.2 %shard_map.159.refs_8_ = f32[2,512,512]{2,1,0:T(8,128)S(1)} custom-call(s32[4]{0:T(128)S(1)} %pad_add_fusion.where_ref, f32[2]{0:T(128)S(1)} %get-tuple-element.7.sigma_ref, bf16[2,256,512]{2,1,0:T(8,128)(2,1)S(1)} %copy-done.3, bf16[2,256,512]{2,1,0:T(8,128)(2,1)} %collective-permute-done.6.refs_1_, bf16[2,2,512,512]{3,2,1,0:T(8,128)(2,1)S(1)} %get-tuple-element.9.refs_2_, ...), custom_call_target="tpu_custom_call" | custom-call | flops 5000000000 | bytes 10000000 | tf_op jit(solution)/shard_map/pallas_call | solution.py:235
  142.6 0.0 copy-start.1
  142.6 0.0 collective-permute-done.4.refs_1_
  142.7 5.7 %shard_map.160.refs_8_ = f32[2,512,512]{2,1,0:T(8,128)S(1)} custom-call(s32[4]{0:T(128)S(1)} %pad_add_fusion.where_ref, f32[2]{0:T(128)S(1)} %get-tuple-element.7.sigma_ref, bf16[2,256,512]{2,1,0:T(8,128)(2,1)S(1)} %copy-done.2, bf16[2,256,512]{2,1,0:T(8,128)(2,1)S(1)} %collective-permute-done.4.refs_1_, ...), custom_call_target="tpu_custom_call" | custom-call | flops 5000000000 | bytes 10000000 | tf_op jit(solution)/shard_map/pallas_call | solution.py:235
  148.3 0.0 collective-permute-done.2.refs_1_
  148.4 6.6 %shard_map.161 = (f32[2]{0:T(128)}, f32[2]{0:T(128)}) custom-call(s32[4]{0:T(128)S(1)} %pad_add_fusion.where_ref, f32[2]{0:T(128)S(1)} %get-tuple-element.7.sigma_ref, bf16[2,256,512]{2,1,0:T(8,128)(2,1)S(1)} %copy-done.1, bf16[2,256,512]{2,1,0:T(8,128)(2,1)S(1)} %collective-permute-done.2.refs_1_, bf16[2,2,512,512]{3,2,1,0:T(8,128)(2,1)S(1)} %get-tuple-element.9.refs_2_, ...), custom_call_target="tpu_custom_call" | custom-call | flops 5000000000 | bytes 10000000 | tf_op jit(solution)/shard_map/pallas_call | solution.py:235
  (11 shorter events, 0.0 us)
Async XLA Ops:
  7.2 1.6 copy-start
  16.4 8.8 %collective-permute-start.1 = (bf16[2,131072]{1,0:T(2,128)(2,1)}, bf16[2,131072]{1,0:T(2,128)(2,1)}, u32[]{:S(2)}, u32[]{:S(2)}) collective-permute-start(bf16[2,131072]{1,0:T(2,128)(2,1)} %get-tuple-element.18), channel_id=1, source_target_pairs={{0,1},{1,0},{2,3},{3,2},{4,5},{5,4},{6,7},{7,6},{8,9},{9,8},{10,11... | collective-permute-start | bytes 1572872 | tf_op jit(solution)/shard_map/ppermute | solution.py:58
  16.9 8.3 %collective-permute-start.3 = (bf16[2,131072]{1,0:T(2,128)(2,1)}, bf16[2,131072]{1,0:T(2,128)(2,1)}, u32[]{:S(2)}, u32[]{:S(2)}) collective-permute-start(bf16[2,131072]{1,0:T(2,128)(2,1)} %get-tuple-element.17), channel_id=1, source_target_pairs={{0,1},{1,0},{2,3},{3,2},{4,5},{5,4},{6,7},{7,6},{8,9},{9,8},{10,11... | collective-permute-start | bytes 1572872 | tf_op jit(solution)/shard_map/ppermute | solution.py:58
  17.0 8.3 %collective-permute-start.5 = (bf16[2,131072]{1,0:T(2,128)(2,1)}, bf16[2,131072]{1,0:T(2,128)(2,1)}, u32[]{:S(2)}, u32[]{:S(2)}) collective-permute-start(bf16[2,131072]{1,0:T(2,128)(2,1)} %get-tuple-element.16), channel_id=1, source_target_pairs={{0,1},{1,0},{2,3},{3,2},{4,5},{5,4},{6,7},{7,6},{8,9},{9,8},{10,11... | collective-permute-start | bytes 1572872 | tf_op jit(solution)/shard_map/ppermute | solution.py:58
  17.4 35.3 %all-to-all-start = ((bf16[16,2,32,512]{3,2,1,0:T(8,128)(2,1)}), bf16[16,2,32,512]{3,2,1,0:T(8,128)(2,1)S(1)}, u32[]{:S(2)}, u32[]{:S(2)}) async-start(bf16[16,2,32,512]{3,2,1,0:T(8,128)(2,1)} %reshape.205), calls=%async_computation | async-start | bytes 2097152 | tf_op jit(solution)/shard_map/all_to_all | solution.py:81
  24.5 107.9 %all-reduce.3.cloned.1.call-start = ((), (), s32[]{:S(2)}) async-start(), calls=%async_computation.1 | async-start | bytes 3145728 | tf_op jit(solution)/shard_map/psum | solution.py:71
  29.5 24.8 %copy-start.8 = (s32[16,2]{0,1:T(2,128)S(1)}, s32[16,2]{0,1:T(2,128)}, u32[]{:S(2)}) copy-start(s32[16,2]{0,1:T(2,128)} %param.18) | copy-start | bytes 388
  29.5 25.0 %copy-start.9 = (s32[3]{0:T(128)S(1)}, s32[3]{0:T(128)}, u32[]{:S(2)}) copy-start(s32[3]{0:T(128)} %param.20) | copy-start | bytes 40
  29.5 104.0 %copy-start.4 = (s32[32]{0:T(128)S(1)}, s32[32]{0:T(128)}, u32[]{:S(2)}) copy-start(s32[32]{0:T(128)} %cut_ref.1) | copy-start | bytes 388
  52.7 80.7 %collective-permute-start = (bf16[16,2,32,512]{3,2,1,0:T(8,128)(2,1)S(1)}, bf16[16,2,32,512]{3,2,1,0:T(8,128)(2,1)}, u32[]{:S(2)}, u32[]{:S(2)}) collective-permute-start(bf16[16,2,32,512]{3,2,1,0:T(8,128)(2,1)S(1)} %all-to-all-done.refs_0_), channel_id=1, source_target_pairs={{0,16},{16,0},{1,17},{17,1},{2,18},{18,2},{3,19},{19,3},{4,20},{20... | collective-permute-start | bytes 3145736 | tf_op jit(solution)/shard_map/ppermute | solution.py:86
  132.4 4.0 %collective-permute-start.6 = (bf16[2,256,512]{2,1,0:T(8,128)(2,1)}, bf16[2,256,512]{2,1,0:T(8,128)(2,1)}, u32[]{:S(2)}, u32[]{:S(2)}) collective-permute-start(bf16[2,256,512]{2,1,0:T(8,128)(2,1)} %get-tuple-element.12.refs_0_), channel_id=1, source_target_pairs={{0,1},{1,0},{2,3},{3,2},{4,5},{5,4},{6,7},{7,6},{8,9},{9,8},{10,11... | collective-permute-start | bytes 1572872 | tf_op jit(solution)/shard_map/ppermute | solution.py:58
  132.9 9.8 %collective-permute-start.4 = (bf16[2,256,512]{2,1,0:T(8,128)(2,1)}, bf16[2,256,512]{2,1,0:T(8,128)(2,1)S(1)}, u32[]{:S(2)}, u32[]{:S(2)}) collective-permute-start(bf16[2,256,512]{2,1,0:T(8,128)(2,1)} %get-tuple-element.11.refs_0_), channel_id=1, source_target_pairs={{0,1},{1,0},{2,3},{3,2},{4,5},{5,4},{6,7},{7,6},{8,9},{9,8},{10,11... | collective-permute-start | bytes 1572872 | tf_op jit(solution)/shard_map/ppermute | solution.py:58
  133.3 3.1 %copy-start.3 = (bf16[2,256,512]{2,1,0:T(8,128)(2,1)S(1)}, bf16[2,256,512]{2,1,0:T(8,128)(2,1)}, u32[]{:S(2)}) copy-start(bf16[2,256,512]{2,1,0:T(8,128)(2,1)} %get-tuple-element.12.refs_0_) | copy-start | bytes 1572868
  133.3 3.1 %copy-start.5 = (f32[4,2,128,512]{3,2,1,0:T(8,128)S(1)}, f32[4,2,128,512]{3,2,1,0:T(8,128)}, u32[]{:S(2)}) copy-start(f32[4,2,128,512]{3,2,1,0:T(8,128)} %constant.123.clone.refs_7_) | copy-start | bytes 6291460
  133.3 3.1 %copy-start.6 = (bf16[4,512,256]{2,1,0:T(8,128)(2,1)S(1)}, bf16[4,512,256]{2,1,0:T(8,128)(2,1)}, u32[]{:S(2)}) copy-start(bf16[4,512,256]{2,1,0:T(8,128)(2,1)} %constant.128.refs_6_) | copy-start | bytes 3145732
  133.3 3.1 %copy-start.7 = (bf16[4,256,256]{2,1,0:T(8,128)(2,1)S(1)}, bf16[4,256,256]{2,1,0:T(8,128)(2,1)}, u32[]{:S(2)}) copy-start(bf16[4,256,256]{2,1,0:T(8,128)(2,1)} %constant.127.refs_5_) | copy-start | bytes 1572868
  133.3 15.0 %collective-permute-start.2 = (bf16[2,256,512]{2,1,0:T(8,128)(2,1)}, bf16[2,256,512]{2,1,0:T(8,128)(2,1)S(1)}, u32[]{:S(2)}, u32[]{:S(2)}) collective-permute-start(bf16[2,256,512]{2,1,0:T(8,128)(2,1)} %get-tuple-element.10.refs_0_), channel_id=1, source_target_pairs={{0,1},{1,0},{2,3},{3,2},{4,5},{5,4},{6,7},{7,6},{8,9},{9,8},{10,11... | collective-permute-start | bytes 1572872 | tf_op jit(solution)/shard_map/ppermute | solution.py:58
  136.4 6.2 %copy-start.2 = (bf16[2,256,512]{2,1,0:T(8,128)(2,1)S(1)}, bf16[2,256,512]{2,1,0:T(8,128)(2,1)}, u32[]{:S(2)}) copy-start(bf16[2,256,512]{2,1,0:T(8,128)(2,1)} %get-tuple-element.11.refs_0_) | copy-start | bytes 1572868
  142.6 5.7 %copy-start.1 = (bf16[2,256,512]{2,1,0:T(8,128)(2,1)S(1)}, bf16[2,256,512]{2,1,0:T(8,128)(2,1)}, u32[]{:S(2)}) copy-start(bf16[2,256,512]{2,1,0:T(8,128)(2,1)} %get-tuple-element.10.refs_0_) | copy-start | bytes 1572868
Sparse Core Ops, SparseCore 0:
  30.8 101.5 all-reduce.2

commit v13 on v7

--- a/solution.py
+++ b/solution.py
@@ -19,9 +19,8 @@
 CORES = 2
 HALF_CHUNKS = 2
 LAG = 2
-TEMPLATE_SLOT = 4
-MASKED_SLOT = 12
-VMEM_LIMIT = 24 * 1024 * 1024
+VMEM_CHIPS = 8
+VMEM_LIMIT = 32 * 1024 * 1024
 
 
 two_pi = 6.283185307179586
@@ -87,7 +86,7 @@
     for at in range(chips):
         along.append((order[at] * CORES, order[(at + 1) % chips] * CORES))
         along.append((order[(at + 1) % chips] * CORES + 1, order[at] * CORES + 1))
-    sent, arrived = [], []
+    sent, shared, arrived = [], [], []
     count = len(chunks)
     for slot in range(count + LAG * (chips - 1)):
         if slot < LAG:
@@ -97,11 +96,11 @@
         else:
             here = arrived[slot - LAG]
         if slot in hooks:
-            here = hooks[slot](here)
+            here = hooks[slot](here, sent, shared)
         sent.append(here)
+        shared.append(lax.ppermute(here, "tpl", to_partner()))
         if slot < count + LAG * (chips - 2):
             arrived.append(lax.ppermute(here, "tpl", along))
-    shared = [lax.ppermute(here, "tpl", to_partner()) for here in sent]
     return sent, shared
 
 
@@ -262,6 +261,8 @@
                 outputs[0][tpl, :, cols] = squares
         largest.append(peak)
 
+    if not last:
+        outputs[1][0] = jnp.int32(0)
     if last:
         for tpl in range(count):
             place = where_ref[4 + tpl]
@@ -296,12 +297,14 @@
     found = [*sent[slots], *shared[slots]]
     last = det == DET - 1
     scalars = jax.ShapeDtypeStruct((count,), jnp.float32)
-    operands = [masked, *turns, *tables(), *before]
+    operands = [masked, *turns, *tables(), *before[:1]]
     return pl.pallas_call(
         functools.partial(detector_kernel, det, chips),
-        out_shape=(scalars, scalars) if last else (jax.ShapeDtypeStruct((count, ROWS, COLS), jnp.float32),),
-        in_specs=[smem, smem] + [anywhere] * len(found) + [vmem] * len(operands),
-        out_specs=(smem, smem) if last else (vmem,),
+        out_shape=(scalars, scalars)
+        if last
+        else (jax.ShapeDtypeStruct((count, ROWS, COLS), jnp.float32), jax.ShapeDtypeStruct((1,), jnp.int32)),
+        in_specs=[smem, smem] + [vmem if chips <= VMEM_CHIPS else anywhere] * len(found) + [vmem] * len(operands),
+        out_specs=(smem, smem) if last else (vmem, smem),
         scratch_shapes=[
             pltpu.VMEM((2, ROWS, COLS), jnp.bfloat16),
             pltpu.SemaphoreType.DMA,
@@ -319,39 +322,31 @@
     me, owner = lax.axis_index("tpl"), owner[0]
     chips = lax.axis_size("tpl") // CORES
     per_device = lists.shape[1]
-    chunks = half_chunks(strain_slots, 0, owner)
-    strain_slots, templates, chunks = lax.optimization_barrier((strain_slots, templates, chunks))
+    chunks = [chunk for det in range(DET) for chunk in half_chunks(strain_slots, det, owner)]
     parts, places = pick(templates, lists)
     ids = list(range(per_device)) if places is None else places
     near, far = distances(owner)
     where = jnp.stack([jnp.asarray(at, jnp.int32) for at in (me % CORES, near, me, far, *ids)])
+    arrived = exchange(parts[0])
+    if places is None:
+        waves = assemble(arrived, per_device)
+    else:
+        waves = [[wave] for wave in across(arrived)]
+    turns = slide_turns(slides)
+    masked, sigma = prepare(cutoffs, lists.reshape(-1), where, waves)
+    results = [()]
+
+    def filtered(det, sent, shared):
+        results.append(detector(det, chips, where, sigma, sent, shared, masked, turns, results[-1]))
+
+    def after_first(chunk, sent, shared):
+        filtered(0, sent, shared)
+        return jnp.where(results[-1][1][0] == 0, chunk, jnp.zeros_like(chunk))
+
+    sent, shared = spread(chunks, owner, {HALF_CHUNKS - 1 + LAG * chips: after_first})
     for det in range(1, DET):
-        more = half_chunks(strain_slots, det, owner)
-        strain_slots, more = lax.optimization_barrier((strain_slots, more))
-        chunks += more
-    held = {"arrived": exchange(parts[0]), "small": (slide_turns(slides), where, lists.reshape(-1))}
-
-    def templates_here(chunk):
-        chunk, held["arrived"], held["small"] = lax.optimization_barrier((chunk, held["arrived"], held["small"]))
-        if places is None:
-            waves = assemble(held["arrived"], per_device)
-        else:
-            waves = [[wave] for wave in across(held["arrived"])]
-        _, where, flat_list = held["small"]
-        held["masked"] = prepare(cutoffs, flat_list, where, waves)
-        return chunk
-
-    def masked_here(chunk):
-        chunk, held["masked"] = lax.optimization_barrier((chunk, held["masked"]))
-        return chunk
-
-    sent, shared = spread(chunks, owner, {TEMPLATE_SLOT: templates_here, MASKED_SLOT: masked_here})
-    turns, where, _ = held["small"]
-    masked, sigma = held["masked"]
-    result = ()
-    for det in range(DET):
-        result = detector(det, chips, where, sigma, sent, shared, masked, turns, result)
-    return result
+        filtered(det, sent, shared)
+    return results[-1]
 
 
 def solution(mesh):

time: 123 us -> 130 us (1.057)
  waiting for transfers between devices: 35.5 us -> 24 us
  local copies, waits for them, and re-layouts: 11.2 us -> 21.3 us
  starting transfers between devices: 44.4 us -> 50.3 us
  Pallas kernels: 20.8 us -> 25.5 us
  other arithmetic: 8.69 us -> 5.63 us
    ppermute x18, waiting for transfers between devices: 35.1 us -> 23.9 us  [spread(): arrived.append(lax.ppermute(here, 'tpl', along))]
    unnamed x31 -> x83, local copies, waits for them, and re-layouts: 1.65 us -> 12.1 us
    pallas_call x3, Pallas kernels: 18.7 us -> 23.4 us  [detector(): pl.pallas_call(functools.partial(detector_kernel, det, chips), out_shape=...]
    ppermute x18, starting transfers between devices: 33.6 us -> 37.2 us  [spread(): arrived.append(lax.ppermute(here, 'tpl', along))]
    all_to_all x1, starting transfers between devices: 3.91 us -> 7.05 us  [exchange(): return lax.all_to_all(block, 'tpl', split_axis=0, concat_axis=0, tiled=True)]
    select_n x4, other arithmetic: 3.48 us -> 1.56 us  [spread(): here = jnp.where(on_owner_chip, chunks[slot], arrived[slot - LAG])]
    squeeze x3 -> x1, local copies, waits for them, and re-layouts: 3.07 us -> 3.59 us  [half_chunks(): lax.dynamic_slice(strain_slots, (0, det, 0, which * half), (1, 1, 2, half))]
    select_n x3 -> x1, other arithmetic: 3.82 us -> 3.46 us  [half_chunks(): first = jnp.where(core == owner % CORES, side(core), got)]
  transfers between devices with their start and end apart: 43 -> 43, of which waited for: 14 -> 10; matrix products, arithmetic and copies ran while one was open for 12% -> 9% of each run, Pallas kernels for 11% -> 13%
where the time goes in v13:
time: 130 us
  starting transfers between devices  50.3 us (39%)
  Pallas kernels  25.5 us (20%)
  waiting for transfers between devices  24 us (18%)
  local copies, waits for them, and re-layouts  21.3 us (16%)
  other arithmetic  5.63 us (4%)
  between operations  2.9 us (2%)
    ppermute x18, starting transfers between devices, spread(): arrived.append(lax.ppermute(here, 'tpl', along))  37.2 us
    ppermute x18, waiting for transfers between devices, spread(): arrived.append(lax.ppermute(here, 'tpl', along))  23.9 us
    pallas_call x3, Pallas kernels, detector(): pl.pallas_call(functools.partial(detector_kernel, det, chips), out_shape=...  23.4 us
    unnamed x83, local copies, waits for them, and re-layouts  12.1 us
    all_to_all x1, starting transfers between devices, exchange(): return lax.all_to_all(block, 'tpl', split_axis=0, concat_axis=0, tiled=True)  7.05 us
    squeeze x1, local copies, waits for them, and re-layouts, half_chunks(): lax.dynamic_slice(strain_slots, (0, det, 0, which * half), (1, 1, 2, half))  3.59 us
    ppermute x20, starting transfers between devices, spread(): shared.append(lax.ppermute(here, 'tpl', to_partner()))  3.58 us
    select_n x1, other arithmetic, half_chunks(): first = jnp.where(core == owner % CORES, side(core), got)  3.46 us
  transfers between devices with their start and end apart: 43, of which 10 were waited for; matrix products, arithmetic and copies ran while one was open for 9% of the time, Pallas kernels for 13%

profile of v13, /device:TPU:0, one launch (start us, length us, event | category | flops | bytes accessed | tf_op | source)
XLA Modules:
  0.0 129.5 jit_solution(11020808294454351740)
XLA Ops:
  0.7 3.6 %dynamic-slice_bitcast_fusion.2 = (bf16[2,131072]{1,0:T(2,128)(2,1)}, bf16[2,131072]{1,0:T(2,128)(2,1)}, bf16[2,131072]{1,0:T(2,128)(2,1)}) fusion(bf16[1,3,2,262144]{3,2,1,0:T(2,128)(2,1)} %param.15, s32[]{:T(128)S(6)} %select_n.206), kind=kLoop, calls=%fused_computation.6 | loop fusion | bytes 3145732 | tf_op jit(solution)/shard_map/squeeze | solution.py:73
  5.3 2.7 %gather_fusion = bf16[16,2,16384]{2,1,0:T(2,128)(2,1)S(1)} fusion(bf16[32,2,16384]{2,1,0:T(2,128)(2,1)S(1)} %copy-done, s32[1024]{0:T(1024)S(1)} %pad_clamp_fusion), kind=kCustom, calls=%fused_computation | custom fusion | bytes 2097216 | tf_op jit(solution)/shard_map/gather | solution.py:126
  7.9 1.5 %reshape.213 = bf16[16,2,32,512]{3,2,1,0:T(8,128)(2,1)} reshape(bf16[16,2,16384]{2,1,0:T(2,128)(2,1)S(1)} %gather_fusion) | data formatting | bytes 2097152 | tf_op jit(solution)/shard_map/reshape | solution.py:127
  9.5 7.0 %all-to-all-start = ((bf16[16,2,32,512]{3,2,1,0:T(8,128)(2,1)}), bf16[16,2,32,512]{3,2,1,0:T(8,128)(2,1)S(1)}, u32[]{:S(2)}, u32[]{:S(2)}) async-start(bf16[16,2,32,512]{3,2,1,0:T(8,128)(2,1)} %reshape.213), calls=%async_computation | async-start | bytes 2097152 | tf_op jit(solution)/shard_map/all_to_all | solution.py:135
  17.3 3.5 %broadcast_select_fusion.2 = (bf16[2,131072]{1,0:T(2,128)(2,1)S(1)}, bf16[2,131072]{1,0:T(2,128)(2,1)S(1)}, bf16[2,131072]{1,0:T(2,128)(2,1)S(1)}) fusion(bf16[2,131072]{1,0:T(2,128)(2,1)} %collective-permute-done.1, pred[]{:T(512)S(6)} %eq.52, bf16[1,3,2,262144]{3,2,1,0:T(2,128)(2,1)} %param.15, s32[]{:T(128)S(6)} %select_n.205, ...), kind=kLoop, calls=%fused_computation.3 | loop fusion | flops 786432 | bytes 4718597 | tf_op jit(solution)/shard_map/jit(_where)/select_n | solution.py:75
  21.1 2.0 %collective-permute-start.6 = (bf16[2,128,512]{2,1,0:T(8,128)(2,1)S(1)}, bf16[2,128,512]{2,1,0:T(8,128)(2,1)S(1)}, u32[]{:S(2)}, u32[]{:S(2)}) collective-permute-start(bf16[2,128,512]{2,1,0:T(8,128)(2,1)S(1)} %bitcast.46), channel_id=1, source_target_pairs={{0,4},{5,1},{4,8},{9,5},{8,12},{13,9},{12,14},{15,13},{14,10},{11,... | collective-permute-start | bytes 786440 | tf_op jit(solution)/shard_map/ppermute | solution.py:103
  23.2 1.5 %collective-permute-start.4 = (bf16[2,128,512]{2,1,0:T(8,128)(2,1)S(1)}, bf16[2,128,512]{2,1,0:T(8,128)(2,1)S(1)}, u32[]{:S(2)}, u32[]{:S(2)}) collective-permute-start(bf16[2,128,512]{2,1,0:T(8,128)(2,1)S(1)} %bitcast.49), channel_id=1, source_target_pairs={{0,4},{5,1},{4,8},{9,5},{8,12},{13,9},{12,14},{15,13},{14,10},{11,... | collective-permute-start | bytes 786440 | tf_op jit(solution)/shard_map/ppermute | solution.py:103
  24.7 0.7 fusion.12
  25.4 12.0 %collective-permute-done.6 = bf16[2,128,512]{2,1,0:T(8,128)(2,1)S(1)} collective-permute-done((bf16[2,128,512]{2,1,0:T(8,128)(2,1)S(1)}, bf16[2,128,512]{2,1,0:T(8,128)(2,1)S(1)}, u32[]{:S(2)}, u32[]{:S(2)}) %collective-permute-start.6) | collective-permute-done | bytes 262176 | tf_op jit(solution)/shard_map/ppermute | solution.py:103
  37.5 7.2 %collective-permute-start.7 = (bf16[2,128,512]{2,1,0:T(8,128)(2,1)S(1)}, bf16[2,128,512]{2,1,0:T(8,128)(2,1)S(1)}, u32[]{:S(2)}, u32[]{:S(2)}) collective-permute-start(bf16[2,128,512]{2,1,0:T(8,128)(2,1)S(1)} %bitcast_select_fusion.refs_3_.refs_1_), channel_id=1, source_target_pairs={{0,4},{5,1},{4,8},{9,5},{8,12},{13,9},{12,14},{15,13},{14,10},{11,... | collective-permute-start | bytes 786440 | tf_op jit(solution)/shard_map/ppermute | solution.py:103
  44.7 2.8 %collective-permute-start.5 = (bf16[2,128,512]{2,1,0:T(8,128)(2,1)S(1)}, bf16[2,128,512]{2,1,0:T(8,128)(2,1)S(1)}, u32[]{:S(2)}, u32[]{:S(2)}) collective-permute-start(bf16[2,128,512]{2,1,0:T(8,128)(2,1)S(1)} %bitcast_select_fusion.2.refs_2_.refs_0_), channel_id=1, source_target_pairs={{0,4},{5,1},{4,8},{9,5},{8,12},{13,9},{12,14},{15,13},{14,10},{11,... | collective-permute-start | bytes 786440 | tf_op jit(solution)/shard_map/ppermute | solution.py:103
  48.6 0.7 bitcast_select_fusion.1.refs_5_.refs_3_.refs_1_
  49.3 2.5 %collective-permute-start.9 = (bf16[2,128,512]{2,1,0:T(8,128)(2,1)}, bf16[2,128,512]{2,1,0:T(8,128)(2,1)}, u32[]{:S(2)}, u32[]{:S(2)}) collective-permute-start(bf16[2,128,512]{2,1,0:T(8,128)(2,1)} %bitcast_select_fusion.1.refs_5_.refs_3_.refs_1_), channel_id=1, source_target_pairs={{0,4},{5,1},{4,8},{9,5},{8,12},{13,9},{12,14},{15,13},{14,10},{11,... | collective-permute-start | bytes 786440 | tf_op jit(solution)/shard_map/ppermute | solution.py:103
  51.8 0.7 bitcast_select_fusion.3.refs_4_.refs_2_.refs_0_
  52.5 2.5 %collective-permute-start.8 = (bf16[2,128,512]{2,1,0:T(8,128)(2,1)}, bf16[2,128,512]{2,1,0:T(8,128)(2,1)}, u32[]{:S(2)}, u32[]{:S(2)}) collective-permute-start(bf16[2,128,512]{2,1,0:T(8,128)(2,1)} %bitcast_select_fusion.3.refs_4_.refs_2_.refs_0_), channel_id=1, source_target_pairs={{0,4},{5,1},{4,8},{9,5},{8,12},{13,9},{12,14},{15,13},{14,10},{11,... | collective-permute-start | bytes 786440 | tf_op jit(solution)/shard_map/ppermute | solution.py:103
  56.9 0.7 copy-done.9
  57.8 1.9 %collective-permute-start.11 = (bf16[2,128,512]{2,1,0:T(8,128)(2,1)}, bf16[2,128,512]{2,1,0:T(8,128)(2,1)}, u32[]{:S(2)}, u32[]{:S(2)}) collective-permute-start(bf16[2,128,512]{2,1,0:T(8,128)(2,1)} %collective-permute-done.9.refs_7_.refs_5_.refs_3_), channel_id=1, source_target_pairs={{0,4},{5,1},{4,8},{9,5},{8,12},{13,9},{12,14},{15,13},{14,10},{11,... | collective-permute-start | bytes 786440 | tf_op jit(solution)/shard_map/ppermute | solution.py:103
  59.7 0.9 collective-permute-done.8.refs_6_.refs_4_.refs_2_
  60.7 1.0 collective-permute-start.10
  61.7 0.7 copy-done.11
  62.4 1.5 %collective-permute-start = (bf16[16,2,32,512]{3,2,1,0:T(8,128)(2,1)S(1)}, bf16[16,2,32,512]{3,2,1,0:T(8,128)(2,1)S(1)}, u32[]{:S(2)}, u32[]{:S(2)}) collective-permute-start(bf16[16,2,32,512]{3,2,1,0:T(8,128)(2,1)S(1)} %all-to-all-done.refs_0_), channel_id=1, source_target_pairs={{0,16},{16,0},{1,17},{17,1},{2,18},{18,2},{3,19},{19,3},{4,20},{20... | collective-permute-start | bytes 3145736 | tf_op jit(solution)/shard_map/ppermute | solution.py:141
  64.5 2.0 %collective-permute-start.13 = (bf16[2,128,512]{2,1,0:T(8,128)(2,1)}, bf16[2,128,512]{2,1,0:T(8,128)(2,1)S(1)}, u32[]{:S(2)}, u32[]{:S(2)}) collective-permute-start(bf16[2,128,512]{2,1,0:T(8,128)(2,1)} %collective-permute-done.11.refs_9_.refs_7_.refs_5_), channel_id=1, source_target_pairs={{0,4},{5,1},{4,8},{9,5},{8,12},{13,9},{12,14},{15,13},{14,10},{11,... | collective-permute-start | bytes 786440 | tf_op jit(solution)/shard_map/ppermute | solution.py:103
  66.5 0.8 collective-permute-done.10.refs_8_.refs_6_.refs_4_
  67.3 1.9 %collective-permute-start.12 = (bf16[2,128,512]{2,1,0:T(8,128)(2,1)}, bf16[2,128,512]{2,1,0:T(8,128)(2,1)S(1)}, u32[]{:S(2)}, u32[]{:S(2)}) collective-permute-start(bf16[2,128,512]{2,1,0:T(8,128)(2,1)} %collective-permute-done.10.refs_8_.refs_6_.refs_4_), channel_id=1, source_target_pairs={{0,4},{5,1},{4,8},{9,5},{8,12},{13,9},{12,14},{15,13},{14,10},{11,... | collective-permute-start | bytes 786440 | tf_op jit(solution)/shard_map/ppermute | solution.py:103
  69.2 0.7 copy-done.17
  70.0 0.7 copy-done.19
  71.2 1.9 %collective-permute-start.15 = (bf16[2,128,512]{2,1,0:T(8,128)(2,1)S(1)}, bf16[2,128,512]{2,1,0:T(8,128)(2,1)}, u32[]{:S(2)}, u32[]{:S(2)}) collective-permute-start(bf16[2,128,512]{2,1,0:T(8,128)(2,1)S(1)} %collective-permute-done.13.refs_11_.refs_9_.refs_7_), channel_id=1, source_target_pairs={{0,4},{5,1},{4,8},{9,5},{8,12},{13,9},{12,14},{15,13},{14,10},{11,... | collective-permute-start | bytes 786440 | tf_op jit(solution)/shard_map/ppermute | solution.py:103
  73.1 0.8 collective-permute-done.12.refs_10_.refs_8_.refs_6_
  73.9 2.0 %collective-permute-start.14 = (bf16[2,128,512]{2,1,0:T(8,128)(2,1)S(1)}, bf16[2,128,512]{2,1,0:T(8,128)(2,1)}, u32[]{:S(2)}, u32[]{:S(2)}) collective-permute-start(bf16[2,128,512]{2,1,0:T(8,128)(2,1)S(1)} %collective-permute-done.12.refs_10_.refs_8_.refs_6_), channel_id=1, source_target_pairs={{0,4},{5,1},{4,8},{9,5},{8,12},{13,9},{12,14},{15,13},{14,10},{11,... | collective-permute-start | bytes 786440 | tf_op jit(solution)/shard_map/ppermute | solution.py:103
  76.6 0.7 copy-done.21
  77.3 0.7 copy-done.27
  79.3 1.1 collective-permute-start.17
  80.5 1.9 %collective-permute-start.16 = (bf16[2,128,512]{2,1,0:T(8,128)(2,1)}, bf16[2,128,512]{2,1,0:T(8,128)(2,1)}, u32[]{:S(2)}, u32[]{:S(2)}) collective-permute-start(bf16[2,128,512]{2,1,0:T(8,128)(2,1)} %collective-permute-done.14.refs_12_.refs_10_.refs_8_), channel_id=1, source_target_pairs={{0,4},{5,1},{4,8},{9,5},{8,12},{13,9},{12,14},{15,13},{14,10},{11,... | collective-permute-start | bytes 786440 | tf_op jit(solution)/shard_map/ppermute | solution.py:103
  82.7 0.7 copy-done.29
  83.4 0.7 copy-done.31
  84.6 4.1 %collective-permute-done.16.refs_14_.refs_12_.refs_10_ = bf16[2,128,512]{2,1,0:T(8,128)(2,1)} collective-permute-done((bf16[2,128,512]{2,1,0:T(8,128)(2,1)}, bf16[2,128,512]{2,1,0:T(8,128)(2,1)}, u32[]{:S(2)}, u32[]{:S(2)}) %collective-permute-start.16) | collective-permute-done | bytes 262176 | tf_op jit(solution)/shard_map/ppermute | solution.py:103
  88.8 1.1 collective-permute-start.18
  89.9 1.0 copy-done.7
  91.7 1.2 copy-done.8
  93.1 2.1 %shard_map.158 = (bf16[2,2,512,512]{3,2,1,0:T(8,128)(2,1)S(1)}, f32[2]{0:T(128)S(1)}) custom-call(s32[32]{0:T(128)S(1)} %copy-done.33, s32[32]{0:T(128)S(1)} %reshape.212.list_ref, s32[6]{0:T(128)S(1)} %stack.27.where_ref, bf16[16,2,32,512]{3,2,1,0:T(8,128)(2,1)S(1)} %all-to-all-done.refs_0_, bf16[16,2,32,512]{3,2,1,0:T(8,128)(2,1)S(1)} %copy-done.8), custom_call_target="tpu_custom_call" | custom-call | flops 2000000000 | bytes 6000000 | tf_op jit(solution)/shard_map/pallas_call | solution.py:281
  95.3 1.2 collective-permute-start.35
  96.4 1.1 collective-permute-start.36
  97.8 1.0 copy-done.36
  98.8 7.6 %shard_map.159 = (f32[2,512,512]{2,1,0:T(8,128)S(1)}, s32[1]{0:T(128)}) custom-call(s32[6]{0:T(128)S(1)} %stack.27.where_ref, f32[2]{0:T(128)S(1)} %get-tuple-element.7.sigma_ref, bf16[2,128,512]{2,1,0:T(8,128)(2,1)S(1)} %bitcast.51, bf16[2,128,512]{2,1,0:T(8,128)(2,1)S(1)} %bitcast.48, bf16[2,128,512]{2,1,0:T(8,128)(2,1)S(1)} %copy-done.6, ...), custom_call_target="tpu_custom_call" | custom-call | flops 5000000000 | bytes 10000000 | tf_op jit(solution)/shard_map/pallas_call | solution.py:301
  107.1 1.6 %collective-permute-start.37 = (bf16[2,128,512]{2,1,0:T(8,128)(2,1)S(1)}, bf16[2,128,512]{2,1,0:T(8,128)(2,1)S(1)}, u32[]{:S(2)}, u32[]{:S(2)}) collective-permute-start(bf16[2,128,512]{2,1,0:T(8,128)(2,1)S(1)} %broadcast_select_fusion.3.refs_15_.refs_13_), channel_id=1, source_target_pairs={{0,4},{5,1},{4,8},{9,5},{8,12},{13,9},{12,14},{15,13},{14,10},{11,... | collective-permute-start | bytes 786440 | tf_op jit(solution)/shard_map/ppermute | solution.py:103
  109.2 4.3 %collective-permute-done.37.refs_15_ = bf16[2,128,512]{2,1,0:T(8,128)(2,1)S(1)} collective-permute-done((bf16[2,128,512]{2,1,0:T(8,128)(2,1)S(1)}, bf16[2,128,512]{2,1,0:T(8,128)(2,1)S(1)}, u32[]{:S(2)}, u32[]{:S(2)}) %collective-permute-start.37) | collective-permute-done | bytes 262176 | tf_op jit(solution)/shard_map/ppermute | solution.py:103
  113.5 7.7 %shard_map.160 = (f32[2,512,512]{2,1,0:T(8,128)S(1)}, s32[1]{0:T(128)}) custom-call(s32[6]{0:T(128)S(1)} %stack.27.where_ref, f32[2]{0:T(128)S(1)} %get-tuple-element.7.sigma_ref, bf16[2,128,512]{2,1,0:T(8,128)(2,1)S(1)} %copy-done.6, bf16[2,128,512]{2,1,0:T(8,128)(2,1)S(1)} %copy-done.4, bf16[2,128,512]{2,1,0:T(8,128)(2,1)} %bitcast_select_fusion.3.refs_4_.refs_2_.refs_0_, ...), custom_call_target="tpu_custom_call" | custom-call | flops 5000000000 | bytes 10000000 | tf_op jit(solution)/shard_map/pallas_call | solution.py:301
  121.2 8.1 %shard_map.161 = (f32[2]{0:T(128)}, f32[2]{0:T(128)}) custom-call(s32[6]{0:T(128)S(1)} %stack.27.where_ref, f32[2]{0:T(128)S(1)} %get-tuple-element.7.sigma_ref, bf16[2,128,512]{2,1,0:T(8,128)(2,1)} %bitcast_select_fusion.3.refs_4_.refs_2_.refs_0_, bf16[2,128,512]{2,1,0:T(8,128)(2,1)} %bitcast_select_fusion.1.refs_5_.refs_3_.refs_1_, ...), custom_call_target="tpu_custom_call" | custom-call | flops 5000000000 | bytes 10000000 | tf_op jit(solution)/shard_map/pallas_call | solution.py:301
  (145 shorter events, 10.0 us)
Async XLA Ops:
  4.3 13.0 %collective-permute-start.1 = (bf16[2,131072]{1,0:T(2,128)(2,1)}, bf16[2,131072]{1,0:T(2,128)(2,1)}, u32[]{:S(2)}, u32[]{:S(2)}) collective-permute-start(bf16[2,131072]{1,0:T(2,128)(2,1)} %get-tuple-element.15), channel_id=1, source_target_pairs={{0,1},{1,0},{2,3},{3,2},{4,5},{5,4},{6,7},{7,6},{8,9},{9,8},{10,11... | collective-permute-start | bytes 1572872 | tf_op jit(solution)/shard_map/ppermute | solution.py:74
  4.7 12.5 %collective-permute-start.2 = (bf16[2,131072]{1,0:T(2,128)(2,1)}, bf16[2,131072]{1,0:T(2,128)(2,1)}, u32[]{:S(2)}, u32[]{:S(2)}) collective-permute-start(bf16[2,131072]{1,0:T(2,128)(2,1)} %get-tuple-element.16), channel_id=1, source_target_pairs={{0,1},{1,0},{2,3},{3,2},{4,5},{5,4},{6,7},{7,6},{8,9},{9,8},{10,11... | collective-permute-start | bytes 1572872 | tf_op jit(solution)/shard_map/ppermute | solution.py:74
  4.8 12.5 %collective-permute-start.3 = (bf16[2,131072]{1,0:T(2,128)(2,1)}, bf16[2,131072]{1,0:T(2,128)(2,1)}, u32[]{:S(2)}, u32[]{:S(2)}) collective-permute-start(bf16[2,131072]{1,0:T(2,128)(2,1)} %get-tuple-element.17), channel_id=1, source_target_pairs={{0,1},{1,0},{2,3},{3,2},{4,5},{5,4},{6,7},{7,6},{8,9},{9,8},{10,11... | collective-permute-start | bytes 1572872 | tf_op jit(solution)/shard_map/ppermute | solution.py:74
  9.5 53.0 %all-to-all-start = ((bf16[16,2,32,512]{3,2,1,0:T(8,128)(2,1)}), bf16[16,2,32,512]{3,2,1,0:T(8,128)(2,1)S(1)}, u32[]{:S(2)}, u32[]{:S(2)}) async-start(bf16[16,2,32,512]{3,2,1,0:T(8,128)(2,1)} %reshape.213), calls=%async_computation | async-start | bytes 2097152 | tf_op jit(solution)/shard_map/all_to_all | solution.py:135
  21.1 16.3 %collective-permute-start.6 = (bf16[2,128,512]{2,1,0:T(8,128)(2,1)S(1)}, bf16[2,128,512]{2,1,0:T(8,128)(2,1)S(1)}, u32[]{:S(2)}, u32[]{:S(2)}) collective-permute-start(bf16[2,128,512]{2,1,0:T(8,128)(2,1)S(1)} %bitcast.46), channel_id=1, source_target_pairs={{0,4},{5,1},{4,8},{9,5},{8,12},{13,9},{12,14},{15,13},{14,10},{11,... | collective-permute-start | bytes 786440 | tf_op jit(solution)/shard_map/ppermute | solution.py:103
  23.1 26.2 %copy-start.1 = (bf16[1,2,128,512]{3,2,1,0:T(8,128)(2,1)}, bf16[1,2,128,512]{3,2,1,0:T(8,128)(2,1)S(1)}, u32[]{:S(2)}) copy-start(bf16[1,2,128,512]{3,2,1,0:T(8,128)(2,1)S(1)} %copy.32) | copy-start | bytes 786436
  23.2 21.5 %collective-permute-start.4 = (bf16[2,128,512]{2,1,0:T(8,128)(2,1)S(1)}, bf16[2,128,512]{2,1,0:T(8,128)(2,1)S(1)}, u32[]{:S(2)}, u32[]{:S(2)}) collective-permute-start(bf16[2,128,512]{2,1,0:T(8,128)(2,1)S(1)} %bitcast.49), channel_id=1, source_target_pairs={{0,4},{5,1},{4,8},{9,5},{8,12},{13,9},{12,14},{15,13},{14,10},{11,... | collective-permute-start | bytes 786440 | tf_op jit(solution)/shard_map/ppermute | solution.py:103
  25.4 57.0 %copy-start.39 = (s32[3]{0:T(128)S(1)}, s32[3]{0:T(128)}, u32[]{:S(2)}) copy-start(s32[3]{0:T(128)} %param.20) | copy-start | bytes 40
  25.4 66.3 %copy-start.33 = (s32[32]{0:T(128)S(1)}, s32[32]{0:T(128)}, u32[]{:S(2)}) copy-start(s32[32]{0:T(128)} %cut_ref.1) | copy-start | bytes 388
  37.5 24.2 %copy-start.3 = (bf16[2,128,512]{2,1,0:T(8,128)(2,1)}, bf16[2,128,512]{2,1,0:T(8,128)(2,1)S(1)}, u32[]{:S(2)}) copy-start(bf16[2,128,512]{2,1,0:T(8,128)(2,1)S(1)} %bitcast_select_fusion.refs_3_.refs_1_) | copy-start | bytes 786436
  37.5 11.1 %collective-permute-start.7 = (bf16[2,128,512]{2,1,0:T(8,128)(2,1)S(1)}, bf16[2,128,512]{2,1,0:T(8,128)(2,1)S(1)}, u32[]{:S(2)}, u32[]{:S(2)}) collective-permute-start(bf16[2,128,512]{2,1,0:T(8,128)(2,1)S(1)} %bitcast_select_fusion.refs_3_.refs_1_), channel_id=1, source_target_pairs={{0,4},{5,1},{4,8},{9,5},{8,12},{13,9},{12,14},{15,13},{14,10},{11,... | collective-permute-start | bytes 786440 | tf_op jit(solution)/shard_map/ppermute | solution.py:103
  44.7 17.0 %copy-start.5 = (bf16[2,128,512]{2,1,0:T(8,128)(2,1)}, bf16[2,128,512]{2,1,0:T(8,128)(2,1)S(1)}, u32[]{:S(2)}) copy-start(bf16[2,128,512]{2,1,0:T(8,128)(2,1)S(1)} %bitcast_select_fusion.2.refs_2_.refs_0_) | copy-start | bytes 786436
  44.7 7.1 %collective-permute-start.5 = (bf16[2,128,512]{2,1,0:T(8,128)(2,1)S(1)}, bf16[2,128,512]{2,1,0:T(8,128)(2,1)S(1)}, u32[]{:S(2)}, u32[]{:S(2)}) collective-permute-start(bf16[2,128,512]{2,1,0:T(8,128)(2,1)S(1)} %bitcast_select_fusion.2.refs_2_.refs_0_), channel_id=1, source_target_pairs={{0,4},{5,1},{4,8},{9,5},{8,12},{13,9},{12,14},{15,13},{14,10},{11,... | collective-permute-start | bytes 786440 | tf_op jit(solution)/shard_map/ppermute | solution.py:103
  47.5 7.5 %collective-permute-start.19 = (bf16[2,128,512]{2,1,0:T(8,128)(2,1)S(1)}, bf16[2,128,512]{2,1,0:T(8,128)(2,1)S(1)}, u32[]{:S(2)}, u32[]{:S(2)}) collective-permute-start(bf16[2,128,512]{2,1,0:T(8,128)(2,1)S(1)} %bitcast.50), channel_id=1, source_target_pairs={{0,1},{1,0},{2,3},{3,2},{4,5},{5,4},{6,7},{7,6},{8,9},{9,8},{10,11... | collective-permute-start | bytes 786440 | tf_op jit(solution)/shard_map/ppermute | solution.py:101
  47.5 8.2 %collective-permute-start.20 = (bf16[2,128,512]{2,1,0:T(8,128)(2,1)S(1)}, bf16[2,128,512]{2,1,0:T(8,128)(2,1)S(1)}, u32[]{:S(2)}, u32[]{:S(2)}) collective-permute-start(bf16[2,128,512]{2,1,0:T(8,128)(2,1)S(1)} %bitcast.47), channel_id=1, source_target_pairs={{0,1},{1,0},{2,3},{3,2},{4,5},{5,4},{6,7},{7,6},{8,9},{9,8},{10,11... | collective-permute-start | bytes 786440 | tf_op jit(solution)/shard_map/ppermute | solution.py:101
  48.0 8.9 %collective-permute-start.22 = (bf16[2,128,512]{2,1,0:T(8,128)(2,1)S(1)}, bf16[2,128,512]{2,1,0:T(8,128)(2,1)S(1)}, u32[]{:S(2)}, u32[]{:S(2)}) collective-permute-start(bf16[2,128,512]{2,1,0:T(8,128)(2,1)S(1)} %bitcast_select_fusion.refs_3_.refs_1_), channel_id=1, source_target_pairs={{0,1},{1,0},{2,3},{3,2},{4,5},{5,4},{6,7},{7,6},{8,9},{9,8},{10,11... | collective-permute-start | bytes 786440 | tf_op jit(solution)/shard_map/ppermute | solution.py:101
  49.3 8.5 %collective-permute-start.9 = (bf16[2,128,512]{2,1,0:T(8,128)(2,1)}, bf16[2,128,512]{2,1,0:T(8,128)(2,1)}, u32[]{:S(2)}, u32[]{:S(2)}) collective-permute-start(bf16[2,128,512]{2,1,0:T(8,128)(2,1)} %bitcast_select_fusion.1.refs_5_.refs_3_.refs_1_), channel_id=1, source_target_pairs={{0,4},{5,1},{4,8},{9,5},{8,12},{13,9},{12,14},{15,13},{14,10},{11,... | collective-permute-start | bytes 786440 | tf_op jit(solution)/shard_map/ppermute | solution.py:103
  52.5 8.1 %collective-permute-start.8 = (bf16[2,128,512]{2,1,0:T(8,128)(2,1)}, bf16[2,128,512]{2,1,0:T(8,128)(2,1)}, u32[]{:S(2)}, u32[]{:S(2)}) collective-permute-start(bf16[2,128,512]{2,1,0:T(8,128)(2,1)} %bitcast_select_fusion.3.refs_4_.refs_2_.refs_0_), channel_id=1, source_target_pairs={{0,4},{5,1},{4,8},{9,5},{8,12},{13,9},{12,14},{15,13},{14,10},{11,... | collective-permute-start | bytes 786440 | tf_op jit(solution)/shard_map/ppermute | solution.py:103
  55.7 6.0 %collective-permute-start.21 = (bf16[2,128,512]{2,1,0:T(8,128)(2,1)S(1)}, bf16[2,128,512]{2,1,0:T(8,128)(2,1)S(1)}, u32[]{:S(2)}, u32[]{:S(2)}) collective-permute-start(bf16[2,128,512]{2,1,0:T(8,128)(2,1)S(1)} %bitcast_select_fusion.2.refs_2_.refs_0_), channel_id=1, source_target_pairs={{0,1},{1,0},{2,3},{3,2},{4,5},{5,4},{6,7},{7,6},{8,9},{9,8},{10,11... | collective-permute-start | bytes 786440 | tf_op jit(solution)/shard_map/ppermute | solution.py:101
  56.4 7.5 %collective-permute-start.24 = (bf16[2,128,512]{2,1,0:T(8,128)(2,1)}, bf16[2,128,512]{2,1,0:T(8,128)(2,1)}, u32[]{:S(2)}, u32[]{:S(2)}) collective-permute-start(bf16[2,128,512]{2,1,0:T(8,128)(2,1)} %bitcast_select_fusion.1.refs_5_.refs_3_.refs_1_), channel_id=1, source_target_pairs={{0,1},{1,0},{2,3},{3,2},{4,5},{5,4},{6,7},{7,6},{8,9},{9,8},{10,11... | collective-permute-start | bytes 786440 | tf_op jit(solution)/shard_map/ppermute | solution.py:101
  57.7 6.3 %collective-permute-start.23 = (bf16[2,128,512]{2,1,0:T(8,128)(2,1)}, bf16[2,128,512]{2,1,0:T(8,128)(2,1)}, u32[]{:S(2)}, u32[]{:S(2)}) collective-permute-start(bf16[2,128,512]{2,1,0:T(8,128)(2,1)} %bitcast_select_fusion.3.refs_4_.refs_2_.refs_0_), channel_id=1, source_target_pairs={{0,1},{1,0},{2,3},{3,2},{4,5},{5,4},{6,7},{7,6},{8,9},{9,8},{10,11... | collective-permute-start | bytes 786440 | tf_op jit(solution)/shard_map/ppermute | solution.py:101
  57.8 6.7 %collective-permute-start.11 = (bf16[2,128,512]{2,1,0:T(8,128)(2,1)}, bf16[2,128,512]{2,1,0:T(8,128)(2,1)}, u32[]{:S(2)}, u32[]{:S(2)}) collective-permute-start(bf16[2,128,512]{2,1,0:T(8,128)(2,1)} %collective-permute-done.9.refs_7_.refs_5_.refs_3_), channel_id=1, source_target_pairs={{0,4},{5,1},{4,8},{9,5},{8,12},{13,9},{12,14},{15,13},{14,10},{11,... | collective-permute-start | bytes 786440 | tf_op jit(solution)/shard_map/ppermute | solution.py:103
  60.7 6.7 %collective-permute-start.10 = (bf16[2,128,512]{2,1,0:T(8,128)(2,1)}, bf16[2,128,512]{2,1,0:T(8,128)(2,1)}, u32[]{:S(2)}, u32[]{:S(2)}) collective-permute-start(bf16[2,128,512]{2,1,0:T(8,128)(2,1)} %collective-permute-done.8.refs_6_.refs_4_.refs_2_), channel_id=1, source_target_pairs={{0,4},{5,1},{4,8},{9,5},{8,12},{13,9},{12,14},{15,13},{14,10},{11,... | collective-permute-start | bytes 786440 | tf_op jit(solution)/shard_map/ppermute | solution.py:103
  62.4 27.5 %collective-permute-start = (bf16[16,2,32,512]{3,2,1,0:T(8,128)(2,1)S(1)}, bf16[16,2,32,512]{3,2,1,0:T(8,128)(2,1)S(1)}, u32[]{:S(2)}, u32[]{:S(2)}) collective-permute-start(bf16[16,2,32,512]{3,2,1,0:T(8,128)(2,1)S(1)} %all-to-all-done.refs_0_), channel_id=1, source_target_pairs={{0,16},{16,0},{1,17},{17,1},{2,18},{18,2},{3,19},{19,3},{4,20},{20... | collective-permute-start | bytes 3145736 | tf_op jit(solution)/shard_map/ppermute | solution.py:141
  63.9 5.3 %collective-permute-start.26 = (bf16[2,128,512]{2,1,0:T(8,128)(2,1)}, bf16[2,128,512]{2,1,0:T(8,128)(2,1)S(1)}, u32[]{:S(2)}, u32[]{:S(2)}) collective-permute-start(bf16[2,128,512]{2,1,0:T(8,128)(2,1)} %collective-permute-done.9.refs_7_.refs_5_.refs_3_), channel_id=1, source_target_pairs={{0,1},{1,0},{2,3},{3,2},{4,5},{5,4},{6,7},{7,6},{8,9},{9,8},{10,11... | collective-permute-start | bytes 786440 | tf_op jit(solution)/shard_map/ppermute | solution.py:101
  63.9 6.0 %collective-permute-start.25 = (bf16[2,128,512]{2,1,0:T(8,128)(2,1)}, bf16[2,128,512]{2,1,0:T(8,128)(2,1)S(1)}, u32[]{:S(2)}, u32[]{:S(2)}) collective-permute-start(bf16[2,128,512]{2,1,0:T(8,128)(2,1)} %collective-permute-done.8.refs_6_.refs_4_.refs_2_), channel_id=1, source_target_pairs={{0,1},{1,0},{2,3},{3,2},{4,5},{5,4},{6,7},{7,6},{8,9},{9,8},{10,11... | collective-permute-start | bytes 786440 | tf_op jit(solution)/shard_map/ppermute | solution.py:101
  64.5 6.7 %collective-permute-start.13 = (bf16[2,128,512]{2,1,0:T(8,128)(2,1)}, bf16[2,128,512]{2,1,0:T(8,128)(2,1)S(1)}, u32[]{:S(2)}, u32[]{:S(2)}) collective-permute-start(bf16[2,128,512]{2,1,0:T(8,128)(2,1)} %collective-permute-done.11.refs_9_.refs_7_.refs_5_), channel_id=1, source_target_pairs={{0,4},{5,1},{4,8},{9,5},{8,12},{13,9},{12,14},{15,13},{14,10},{11,... | collective-permute-start | bytes 786440 | tf_op jit(solution)/shard_map/ppermute | solution.py:103
  67.3 6.6 %collective-permute-start.12 = (bf16[2,128,512]{2,1,0:T(8,128)(2,1)}, bf16[2,128,512]{2,1,0:T(8,128)(2,1)S(1)}, u32[]{:S(2)}, u32[]{:S(2)}) collective-permute-start(bf16[2,128,512]{2,1,0:T(8,128)(2,1)} %collective-permute-done.10.refs_8_.refs_6_.refs_4_), channel_id=1, source_target_pairs={{0,4},{5,1},{4,8},{9,5},{8,12},{13,9},{12,14},{15,13},{14,10},{11,... | collective-permute-start | bytes 786440 | tf_op jit(solution)/shard_map/ppermute | solution.py:103
  70.0 6.0 %collective-permute-start.28 = (bf16[2,128,512]{2,1,0:T(8,128)(2,1)}, bf16[2,128,512]{2,1,0:T(8,128)(2,1)S(1)}, u32[]{:S(2)}, u32[]{:S(2)}) collective-permute-start(bf16[2,128,512]{2,1,0:T(8,128)(2,1)} %collective-permute-done.11.refs_9_.refs_7_.refs_5_), channel_id=1, source_target_pairs={{0,1},{1,0},{2,3},{3,2},{4,5},{5,4},{6,7},{7,6},{8,9},{9,8},{10,11... | collective-permute-start | bytes 786440 | tf_op jit(solution)/shard_map/ppermute | solution.py:101
  70.7 6.7 %collective-permute-start.27 = (bf16[2,128,512]{2,1,0:T(8,128)(2,1)}, bf16[2,128,512]{2,1,0:T(8,128)(2,1)S(1)}, u32[]{:S(2)}, u32[]{:S(2)}) collective-permute-start(bf16[2,128,512]{2,1,0:T(8,128)(2,1)} %collective-permute-done.10.refs_8_.refs_6_.refs_4_), channel_id=1, source_target_pairs={{0,1},{1,0},{2,3},{3,2},{4,5},{5,4},{6,7},{7,6},{8,9},{9,8},{10,11... | collective-permute-start | bytes 786440 | tf_op jit(solution)/shard_map/ppermute | solution.py:101
  71.2 8.1 %collective-permute-start.15 = (bf16[2,128,512]{2,1,0:T(8,128)(2,1)S(1)}, bf16[2,128,512]{2,1,0:T(8,128)(2,1)}, u32[]{:S(2)}, u32[]{:S(2)}) collective-permute-start(bf16[2,128,512]{2,1,0:T(8,128)(2,1)S(1)} %collective-permute-done.13.refs_11_.refs_9_.refs_7_), channel_id=1, source_target_pairs={{0,4},{5,1},{4,8},{9,5},{8,12},{13,9},{12,14},{15,13},{14,10},{11,... | collective-permute-start | bytes 786440 | tf_op jit(solution)/shard_map/ppermute | solution.py:103
  73.9 6.6 %collective-permute-start.14 = (bf16[2,128,512]{2,1,0:T(8,128)(2,1)S(1)}, bf16[2,128,512]{2,1,0:T(8,128)(2,1)}, u32[]{:S(2)}, u32[]{:S(2)}) collective-permute-start(bf16[2,128,512]{2,1,0:T(8,128)(2,1)S(1)} %collective-permute-done.12.refs_10_.refs_8_.refs_6_), channel_id=1, source_target_pairs={{0,4},{5,1},{4,8},{9,5},{8,12},{13,9},{12,14},{15,13},{14,10},{11,... | collective-permute-start | bytes 786440 | tf_op jit(solution)/shard_map/ppermute | solution.py:103
  76.6 6.1 %collective-permute-start.30 = (bf16[2,128,512]{2,1,0:T(8,128)(2,1)S(1)}, bf16[2,128,512]{2,1,0:T(8,128)(2,1)S(1)}, u32[]{:S(2)}, u32[]{:S(2)}) collective-permute-start(bf16[2,128,512]{2,1,0:T(8,128)(2,1)S(1)} %collective-permute-done.13.refs_11_.refs_9_.refs_7_), channel_id=1, source_target_pairs={{0,1},{1,0},{2,3},{3,2},{4,5},{5,4},{6,7},{7,6},{8,9},{9,8},{10,11... | collective-permute-start | bytes 786440 | tf_op jit(solution)/shard_map/ppermute | solution.py:101
  78.1 5.4 %collective-permute-start.29 = (bf16[2,128,512]{2,1,0:T(8,128)(2,1)S(1)}, bf16[2,128,512]{2,1,0:T(8,128)(2,1)S(1)}, u32[]{:S(2)}, u32[]{:S(2)}) collective-permute-start(bf16[2,128,512]{2,1,0:T(8,128)(2,1)S(1)} %collective-permute-done.12.refs_10_.refs_8_.refs_6_), channel_id=1, source_target_pairs={{0,1},{1,0},{2,3},{3,2},{4,5},{5,4},{6,7},{7,6},{8,9},{9,8},{10,11... | collective-permute-start | bytes 786440 | tf_op jit(solution)/shard_map/ppermute | solution.py:101
  79.3 9.5 %collective-permute-start.17 = (bf16[2,128,512]{2,1,0:T(8,128)(2,1)}, bf16[2,128,512]{2,1,0:T(8,128)(2,1)}, u32[]{:S(2)}, u32[]{:S(2)}) collective-permute-start(bf16[2,128,512]{2,1,0:T(8,128)(2,1)} %collective-permute-done.15.refs_13_.refs_11_.refs_9_), channel_id=1, source_target_pairs={{0,4},{5,1},{4,8},{9,5},{8,12},{13,9},{12,14},{15,13},{14,10},{11,... | collective-permute-start | bytes 786440 | tf_op jit(solution)/shard_map/ppermute | solution.py:103
  80.5 8.3 %collective-permute-start.16 = (bf16[2,128,512]{2,1,0:T(8,128)(2,1)}, bf16[2,128,512]{2,1,0:T(8,128)(2,1)}, u32[]{:S(2)}, u32[]{:S(2)}) collective-permute-start(bf16[2,128,512]{2,1,0:T(8,128)(2,1)} %collective-permute-done.14.refs_12_.refs_10_.refs_8_), channel_id=1, source_target_pairs={{0,4},{5,1},{4,8},{9,5},{8,12},{13,9},{12,14},{15,13},{14,10},{11,... | collective-permute-start | bytes 786440 | tf_op jit(solution)/shard_map/ppermute | solution.py:103
  83.4 11.8 %collective-permute-start.32 = (bf16[2,128,512]{2,1,0:T(8,128)(2,1)}, bf16[2,128,512]{2,1,0:T(8,128)(2,1)}, u32[]{:S(2)}, u32[]{:S(2)}) collective-permute-start(bf16[2,128,512]{2,1,0:T(8,128)(2,1)} %collective-permute-done.15.refs_13_.refs_11_.refs_9_), channel_id=1, source_target_pairs={{0,1},{1,0},{2,3},{3,2},{4,5},{5,4},{6,7},{7,6},{8,9},{9,8},{10,11... | collective-permute-start | bytes 786440 | tf_op jit(solution)/shard_map/ppermute | solution.py:101
  84.1 13.4 %collective-permute-start.31 = (bf16[2,128,512]{2,1,0:T(8,128)(2,1)}, bf16[2,128,512]{2,1,0:T(8,128)(2,1)}, u32[]{:S(2)}, u32[]{:S(2)}) collective-permute-start(bf16[2,128,512]{2,1,0:T(8,128)(2,1)} %collective-permute-done.14.refs_12_.refs_10_.refs_8_), channel_id=1, source_target_pairs={{0,1},{1,0},{2,3},{3,2},{4,5},{5,4},{6,7},{7,6},{8,9},{9,8},{10,11... | collective-permute-start | bytes 786440 | tf_op jit(solution)/shard_map/ppermute | solution.py:101
  88.8 8.8 %collective-permute-start.33 = (bf16[2,128,512]{2,1,0:T(8,128)(2,1)}, bf16[2,128,512]{2,1,0:T(8,128)(2,1)}, u32[]{:S(2)}, u32[]{:S(2)}) collective-permute-start(bf16[2,128,512]{2,1,0:T(8,128)(2,1)} %collective-permute-done.16.refs_14_.refs_12_.refs_10_), channel_id=1, source_target_pairs={{0,1},{1,0},{2,3},{3,2},{4,5},{5,4},{6,7},{7,6},{8,9},{9,8},{10,11... | collective-permute-start | bytes 786440 | tf_op jit(solution)/shard_map/ppermute | solution.py:101
  88.8 7.6 %collective-permute-start.18 = (bf16[2,128,512]{2,1,0:T(8,128)(2,1)}, bf16[2,128,512]{2,1,0:T(8,128)(2,1)}, u32[]{:S(2)}, u32[]{:S(2)}) collective-permute-start(bf16[2,128,512]{2,1,0:T(8,128)(2,1)} %collective-permute-done.16.refs_14_.refs_12_.refs_10_), channel_id=1, source_target_pairs={{0,4},{5,1},{4,8},{9,5},{8,12},{13,9},{12,14},{15,13},{14,10},{11,... | collective-permute-start | bytes 786440 | tf_op jit(solution)/shard_map/ppermute | solution.py:103
  90.9 6.7 %collective-permute-start.34 = (bf16[2,128,512]{2,1,0:T(8,128)(2,1)}, bf16[2,128,512]{2,1,0:T(8,128)(2,1)}, u32[]{:S(2)}, u32[]{:S(2)}) collective-permute-start(bf16[2,128,512]{2,1,0:T(8,128)(2,1)} %collective-permute-done.17.refs_15_.refs_13_.refs_11_), channel_id=1, source_target_pairs={{0,1},{1,0},{2,3},{3,2},{4,5},{5,4},{6,7},{7,6},{8,9},{9,8},{10,11... | collective-permute-start | bytes 786440 | tf_op jit(solution)/shard_map/ppermute | solution.py:101
  95.3 11.8 %collective-permute-start.35 = (bf16[2,128,512]{2,1,0:T(8,128)(2,1)}, bf16[2,128,512]{2,1,0:T(8,128)(2,1)S(1)}, u32[]{:S(2)}, u32[]{:S(2)}) collective-permute-start(bf16[2,128,512]{2,1,0:T(8,128)(2,1)} %collective-permute-done.17.refs_15_.refs_13_.refs_11_), channel_id=1, source_target_pairs={{0,4},{5,1},{4,8},{9,5},{8,12},{13,9},{12,14},{15,13},{14,10},{11,... | collective-permute-start | bytes 786440 | tf_op jit(solution)/shard_map/ppermute | solution.py:103
  96.4 12.8 %collective-permute-start.36 = (bf16[2,128,512]{2,1,0:T(8,128)(2,1)}, bf16[2,128,512]{2,1,0:T(8,128)(2,1)S(1)}, u32[]{:S(2)}, u32[]{:S(2)}) collective-permute-start(bf16[2,128,512]{2,1,0:T(8,128)(2,1)} %collective-permute-done.18.refs_14_.refs_12_), channel_id=1, source_target_pairs={{0,4},{5,1},{4,8},{9,5},{8,12},{13,9},{12,14},{15,13},{14,10},{11,... | collective-permute-start | bytes 786440 | tf_op jit(solution)/shard_map/ppermute | solution.py:103
  107.1 6.4 %collective-permute-start.37 = (bf16[2,128,512]{2,1,0:T(8,128)(2,1)S(1)}, bf16[2,128,512]{2,1,0:T(8,128)(2,1)S(1)}, u32[]{:S(2)}, u32[]{:S(2)}) collective-permute-start(bf16[2,128,512]{2,1,0:T(8,128)(2,1)S(1)} %broadcast_select_fusion.3.refs_15_.refs_13_), channel_id=1, source_target_pairs={{0,4},{5,1},{4,8},{9,5},{8,12},{13,9},{12,14},{15,13},{14,10},{11,... | collective-permute-start | bytes 786440 | tf_op jit(solution)/shard_map/ppermute | solution.py:103
  108.7 4.8 %collective-permute-start.38 = (bf16[2,128,512]{2,1,0:T(8,128)(2,1)}, bf16[2,128,512]{2,1,0:T(8,128)(2,1)S(1)}, u32[]{:S(2)}, u32[]{:S(2)}) collective-permute-start(bf16[2,128,512]{2,1,0:T(8,128)(2,1)} %collective-permute-done.18.refs_14_.refs_12_), channel_id=1, source_target_pairs={{0,1},{1,0},{2,3},{3,2},{4,5},{5,4},{6,7},{7,6},{8,9},{9,8},{10,11... | collective-permute-start | bytes 786440 | tf_op jit(solution)/shard_map/ppermute | solution.py:101
  108.7 4.8 %collective-permute-start.39 = (bf16[2,128,512]{2,1,0:T(8,128)(2,1)S(1)}, bf16[2,128,512]{2,1,0:T(8,128)(2,1)S(1)}, u32[]{:S(2)}, u32[]{:S(2)}) collective-permute-start(bf16[2,128,512]{2,1,0:T(8,128)(2,1)S(1)} %broadcast_select_fusion.3.refs_15_.refs_13_), channel_id=1, source_target_pairs={{0,1},{1,0},{2,3},{3,2},{4,5},{5,4},{6,7},{7,6},{8,9},{9,8},{10,11... | collective-permute-start | bytes 786440 | tf_op jit(solution)/shard_map/ppermute | solution.py:101
  109.2 12.0 %collective-permute-start.40 = (bf16[2,128,512]{2,1,0:T(8,128)(2,1)S(1)}, bf16[2,128,512]{2,1,0:T(8,128)(2,1)S(1)}, u32[]{:S(2)}, u32[]{:S(2)}) collective-permute-start(bf16[2,128,512]{2,1,0:T(8,128)(2,1)S(1)} %collective-permute-done.36.refs_14_), channel_id=1, source_target_pairs={{0,1},{1,0},{2,3},{3,2},{4,5},{5,4},{6,7},{7,6},{8,9},{9,8},{10,11... | collective-permute-start | bytes 786440 | tf_op jit(solution)/shard_map/ppermute | solution.py:101
  113.5 7.7 %collective-permute-start.41 = (bf16[2,128,512]{2,1,0:T(8,128)(2,1)S(1)}, bf16[2,128,512]{2,1,0:T(8,128)(2,1)S(1)}, u32[]{:S(2)}, u32[]{:S(2)}) collective-permute-start(bf16[2,128,512]{2,1,0:T(8,128)(2,1)S(1)} %collective-permute-done.37.refs_15_), channel_id=1, source_target_pairs={{0,1},{1,0},{2,3},{3,2},{4,5},{5,4},{6,7},{7,6},{8,9},{9,8},{10,11... | collective-permute-start | bytes 786440 | tf_op jit(solution)/shard_map/ppermute | solution.py:101
  (35 other events, 114.5 us)

commit v14 on v13

--- a/solution.py
+++ b/solution.py
@@ -19,8 +19,7 @@
 CORES = 2
 HALF_CHUNKS = 2
 LAG = 2
-VMEM_CHIPS = 8
-VMEM_LIMIT = 32 * 1024 * 1024
+VMEM_LIMIT = 24 * 1024 * 1024
 
 
 two_pi = 6.283185307179586
@@ -76,7 +75,7 @@
     return [first[:, at : at + bins].reshape(2, bins // COLS, COLS) for at in range(0, half, bins)]
 
 
-def spread(chunks, owner, hooks):
+def spread(chunks, owner):
     devices = lax.axis_size("tpl")
     chips = devices // CORES
     order = ring_order(chips)
@@ -95,8 +94,6 @@
             here = jnp.where(on_owner_chip, chunks[slot], arrived[slot - LAG])
         else:
             here = arrived[slot - LAG]
-        if slot in hooks:
-            here = hooks[slot](here, sent, shared)
         sent.append(here)
         shared.append(lax.ppermute(here, "tpl", to_partner()))
         if slot < count + LAG * (chips - 2):
@@ -261,8 +258,6 @@
                 outputs[0][tpl, :, cols] = squares
         largest.append(peak)
 
-    if not last:
-        outputs[1][0] = jnp.int32(0)
     if last:
         for tpl in range(count):
             place = where_ref[4 + tpl]
@@ -297,14 +292,12 @@
     found = [*sent[slots], *shared[slots]]
     last = det == DET - 1
     scalars = jax.ShapeDtypeStruct((count,), jnp.float32)
-    operands = [masked, *turns, *tables(), *before[:1]]
+    operands = [masked, *turns, *tables(), *before]
     return pl.pallas_call(
         functools.partial(detector_kernel, det, chips),
-        out_shape=(scalars, scalars)
-        if last
-        else (jax.ShapeDtypeStruct((count, ROWS, COLS), jnp.float32), jax.ShapeDtypeStruct((1,), jnp.int32)),
-        in_specs=[smem, smem] + [vmem if chips <= VMEM_CHIPS else anywhere] * len(found) + [vmem] * len(operands),
-        out_specs=(smem, smem) if last else (vmem, smem),
+        out_shape=(scalars, scalars) if last else (jax.ShapeDtypeStruct((count, ROWS, COLS), jnp.float32),),
+        in_specs=[smem, smem] + [anywhere] * len(found) + [vmem] * len(operands),
+        out_specs=(smem, smem) if last else (vmem,),
         scratch_shapes=[
             pltpu.VMEM((2, ROWS, COLS), jnp.bfloat16),
             pltpu.SemaphoreType.DMA,
@@ -334,19 +327,11 @@
         waves = [[wave] for wave in across(arrived)]
     turns = slide_turns(slides)
     masked, sigma = prepare(cutoffs, lists.reshape(-1), where, waves)
-    results = [()]
-
-    def filtered(det, sent, shared):
-        results.append(detector(det, chips, where, sigma, sent, shared, masked, turns, results[-1]))
-
-    def after_first(chunk, sent, shared):
-        filtered(0, sent, shared)
-        return jnp.where(results[-1][1][0] == 0, chunk, jnp.zeros_like(chunk))
-
-    sent, shared = spread(chunks, owner, {HALF_CHUNKS - 1 + LAG * chips: after_first})
-    for det in range(1, DET):
-        filtered(det, sent, shared)
-    return results[-1]
+    sent, shared = spread(chunks, owner)
+    result = ()
+    for det in range(DET):
+        result = detector(det, chips, where, sigma, sent, shared, masked, turns, result)
+    return result
 
 
 def solution(mesh):

time: 130 us -> 126 us (0.969)
  Pallas kernels: 25.5 us -> 22.6 us
    pallas_call x3, Pallas kernels: 23.4 us -> 20.5 us  [detector(): pl.pallas_call(functools.partial(detector_kernel, det, chips), out_shape=...]
    unnamed x83 -> x89, local copies, waits for them, and re-layouts: 12.1 us -> 12.2 us
  transfers between devices with their start and end apart: 43 -> 43, of which waited for: 10 -> 13; matrix products, arithmetic and copies ran while one was open for 9% -> 8% of each run, Pallas kernels for 13% -> 12%
where the time goes in v14:
time: 126 us
  starting transfers between devices  50.7 us (40%)
  waiting for transfers between devices  24.9 us (20%)
  Pallas kernels  22.6 us (18%)
  local copies, waits for them, and re-layouts  21.4 us (17%)
  other arithmetic  4.41 us (4%)
  between operations  2.31 us (2%)
    ppermute x18, starting transfers between devices, spread(): arrived.append(lax.ppermute(here, 'tpl', along))  37.5 us
    ppermute x18, waiting for transfers between devices, spread(): arrived.append(lax.ppermute(here, 'tpl', along))  24.9 us
    pallas_call x3, Pallas kernels, detector(): pl.pallas_call(functools.partial(detector_kernel, det, chips), out_shape=...  20.5 us
    unnamed x89, local copies, waits for them, and re-layouts  12.2 us
    all_to_all x1, starting transfers between devices, exchange(): return lax.all_to_all(block, 'tpl', split_axis=0, concat_axis=0, tiled=True)  7.05 us
    ppermute x20, starting transfers between devices, spread(): shared.append(lax.ppermute(here, 'tpl', to_partner()))  3.72 us
    squeeze x1, local copies, waits for them, and re-layouts, half_chunks(): lax.dynamic_slice(strain_slots, (0, det, 0, which * half), (1, 1, 2, half))  3.56 us
    select_n x1, other arithmetic, half_chunks(): first = jnp.where(core == owner % CORES, side(core), got)  2.99 us
  transfers between devices with their start and end apart: 43, of which 13 were waited for; matrix products, arithmetic and copies ran while one was open for 8% of the time, Pallas kernels for 12%

profile of v14, /device:TPU:0, one launch (start us, length us, event | category | flops | bytes accessed | tf_op | source)
XLA Modules:
  0.0 126.4 jit_solution(9980913749745278622)
XLA Ops:
  0.7 3.6 %dynamic-slice_bitcast_fusion.2 = (bf16[2,131072]{1,0:T(2,128)(2,1)}, bf16[2,131072]{1,0:T(2,128)(2,1)}, bf16[2,131072]{1,0:T(2,128)(2,1)}) fusion(bf16[1,3,2,262144]{3,2,1,0:T(2,128)(2,1)} %param.15, s32[]{:T(128)S(6)} %select_n.200), kind=kLoop, calls=%fused_computation.6 | loop fusion | bytes 3145732 | tf_op jit(solution)/shard_map/squeeze | solution.py:72
  5.2 2.7 %gather_fusion = bf16[16,2,16384]{2,1,0:T(2,128)(2,1)S(1)} fusion(bf16[32,2,16384]{2,1,0:T(2,128)(2,1)S(1)} %copy-done, s32[1024]{0:T(1024)S(1)} %pad_clamp_fusion), kind=kCustom, calls=%fused_computation | custom fusion | bytes 2097216 | tf_op jit(solution)/shard_map/gather | solution.py:123
  7.9 1.6 %reshape.211 = bf16[16,2,32,512]{3,2,1,0:T(8,128)(2,1)} reshape(bf16[16,2,16384]{2,1,0:T(2,128)(2,1)S(1)} %gather_fusion) | data formatting | bytes 2097152 | tf_op jit(solution)/shard_map/reshape | solution.py:124
  9.5 7.0 %all-to-all-start = ((bf16[16,2,32,512]{3,2,1,0:T(8,128)(2,1)}), bf16[16,2,32,512]{3,2,1,0:T(8,128)(2,1)S(1)}, u32[]{:S(2)}, u32[]{:S(2)}) async-start(bf16[16,2,32,512]{3,2,1,0:T(8,128)(2,1)} %reshape.211), calls=%async_computation | async-start | bytes 2097152 | tf_op jit(solution)/shard_map/all_to_all | solution.py:132
  17.2 3.0 %broadcast_select_fusion.2 = (bf16[2,131072]{1,0:T(2,128)(2,1)S(1)}, bf16[2,131072]{1,0:T(2,128)(2,1)S(1)}, bf16[2,131072]{1,0:T(2,128)(2,1)S(1)}) fusion(bf16[2,131072]{1,0:T(2,128)(2,1)} %collective-permute-done.1, pred[]{:T(512)S(6)} %eq.46, bf16[1,3,2,262144]{3,2,1,0:T(2,128)(2,1)} %param.15, s32[]{:T(128)S(6)} %select_n.199, ...), kind=kLoop, calls=%fused_computation.3 | loop fusion | flops 786432 | bytes 4718597 | tf_op jit(solution)/shard_map/jit(_where)/select_n | solution.py:74
  20.6 2.0 %collective-permute-start.6 = (bf16[2,128,512]{2,1,0:T(8,128)(2,1)S(1)}, bf16[2,128,512]{2,1,0:T(8,128)(2,1)S(1)}, u32[]{:S(2)}, u32[]{:S(2)}) collective-permute-start(bf16[2,128,512]{2,1,0:T(8,128)(2,1)S(1)} %bitcast.45), channel_id=1, source_target_pairs={{0,4},{5,1},{4,8},{9,5},{8,12},{13,9},{12,14},{15,13},{14,10},{11,... | collective-permute-start | bytes 786440 | tf_op jit(solution)/shard_map/ppermute | solution.py:100
  22.7 1.5 %collective-permute-start.4 = (bf16[2,128,512]{2,1,0:T(8,128)(2,1)S(1)}, bf16[2,128,512]{2,1,0:T(8,128)(2,1)S(1)}, u32[]{:S(2)}, u32[]{:S(2)}) collective-permute-start(bf16[2,128,512]{2,1,0:T(8,128)(2,1)S(1)} %bitcast.48), channel_id=1, source_target_pairs={{0,4},{5,1},{4,8},{9,5},{8,12},{13,9},{12,14},{15,13},{14,10},{11,... | collective-permute-start | bytes 786440 | tf_op jit(solution)/shard_map/ppermute | solution.py:100
  24.2 0.7 fusion.12
  24.9 12.5 %collective-permute-done.6 = bf16[2,128,512]{2,1,0:T(8,128)(2,1)S(1)} collective-permute-done((bf16[2,128,512]{2,1,0:T(8,128)(2,1)S(1)}, bf16[2,128,512]{2,1,0:T(8,128)(2,1)S(1)}, u32[]{:S(2)}, u32[]{:S(2)}) %collective-permute-start.6) | collective-permute-done | bytes 262176 | tf_op jit(solution)/shard_map/ppermute | solution.py:100
  37.5 7.2 %collective-permute-start.7 = (bf16[2,128,512]{2,1,0:T(8,128)(2,1)S(1)}, bf16[2,128,512]{2,1,0:T(8,128)(2,1)S(1)}, u32[]{:S(2)}, u32[]{:S(2)}) collective-permute-start(bf16[2,128,512]{2,1,0:T(8,128)(2,1)S(1)} %bitcast_select_fusion.refs_3_.refs_1_), channel_id=1, source_target_pairs={{0,4},{5,1},{4,8},{9,5},{8,12},{13,9},{12,14},{15,13},{14,10},{11,... | collective-permute-start | bytes 786440 | tf_op jit(solution)/shard_map/ppermute | solution.py:100
  44.7 2.8 %collective-permute-start.5 = (bf16[2,128,512]{2,1,0:T(8,128)(2,1)S(1)}, bf16[2,128,512]{2,1,0:T(8,128)(2,1)S(1)}, u32[]{:S(2)}, u32[]{:S(2)}) collective-permute-start(bf16[2,128,512]{2,1,0:T(8,128)(2,1)S(1)} %bitcast_select_fusion.2.refs_2_.refs_0_), channel_id=1, source_target_pairs={{0,4},{5,1},{4,8},{9,5},{8,12},{13,9},{12,14},{15,13},{14,10},{11,... | collective-permute-start | bytes 786440 | tf_op jit(solution)/shard_map/ppermute | solution.py:100
  47.5 1.1 collective-permute-done.7
  48.6 2.5 %collective-permute-start.9 = (bf16[2,128,512]{2,1,0:T(8,128)(2,1)S(1)}, bf16[2,128,512]{2,1,0:T(8,128)(2,1)}, u32[]{:S(2)}, u32[]{:S(2)}) collective-permute-start(bf16[2,128,512]{2,1,0:T(8,128)(2,1)S(1)} %bitcast_select_fusion.1.refs_5_.refs_3_.refs_1_), channel_id=1, source_target_pairs={{0,4},{5,1},{4,8},{9,5},{8,12},{13,9},{12,14},{15,13},{14,10},{11,... | collective-permute-start | bytes 786440 | tf_op jit(solution)/shard_map/ppermute | solution.py:100
  51.4 0.7 bitcast_select_fusion.3.refs_4_.refs_2_.refs_0_
  52.1 2.5 %collective-permute-start.8 = (bf16[2,128,512]{2,1,0:T(8,128)(2,1)}, bf16[2,128,512]{2,1,0:T(8,128)(2,1)S(1)}, u32[]{:S(2)}, u32[]{:S(2)}) collective-permute-start(bf16[2,128,512]{2,1,0:T(8,128)(2,1)} %bitcast_select_fusion.3.refs_4_.refs_2_.refs_0_), channel_id=1, source_target_pairs={{0,4},{5,1},{4,8},{9,5},{8,12},{13,9},{12,14},{15,13},{14,10},{11,... | collective-permute-start | bytes 786440 | tf_op jit(solution)/shard_map/ppermute | solution.py:100
  55.1 0.7 copy-done.13
  55.8 1.2 collective-permute-done.9.refs_7_.refs_5_.refs_3_
  57.0 1.3 %collective-permute-start.11 = (bf16[2,128,512]{2,1,0:T(8,128)(2,1)}, bf16[2,128,512]{2,1,0:T(8,128)(2,1)}, u32[]{:S(2)}, u32[]{:S(2)}) collective-permute-start(bf16[2,128,512]{2,1,0:T(8,128)(2,1)} %collective-permute-done.9.refs_7_.refs_5_.refs_3_), channel_id=1, source_target_pairs={{0,4},{5,1},{4,8},{9,5},{8,12},{13,9},{12,14},{15,13},{14,10},{11,... | collective-permute-start | bytes 786440 | tf_op jit(solution)/shard_map/ppermute | solution.py:100
  58.3 2.2 %collective-permute-done.8.refs_6_.refs_4_.refs_2_ = bf16[2,128,512]{2,1,0:T(8,128)(2,1)S(1)} collective-permute-done((bf16[2,128,512]{2,1,0:T(8,128)(2,1)}, bf16[2,128,512]{2,1,0:T(8,128)(2,1)S(1)}, u32[]{:S(2)}, u32[]{:S(2)}) %collective-permute-start.8) | collective-permute-done | bytes 262176 | tf_op jit(solution)/shard_map/ppermute | solution.py:100
  60.5 0.7 collective-permute-start.10
  61.3 0.7 copy-done.17
  62.0 0.7 copy-done.15
  63.2 0.7 copy-done.19
  64.0 2.4 %collective-permute-start.13 = (bf16[2,128,512]{2,1,0:T(8,128)(2,1)}, bf16[2,128,512]{2,1,0:T(8,128)(2,1)}, u32[]{:S(2)}, u32[]{:S(2)}) collective-permute-start(bf16[2,128,512]{2,1,0:T(8,128)(2,1)} %collective-permute-done.11.refs_9_.refs_7_.refs_5_), channel_id=1, source_target_pairs={{0,4},{5,1},{4,8},{9,5},{8,12},{13,9},{12,14},{15,13},{14,10},{11,... | collective-permute-start | bytes 786440 | tf_op jit(solution)/shard_map/ppermute | solution.py:100
  67.0 0.8 collective-permute-start.12
  68.5 1.5 %collective-permute-start = (bf16[16,2,32,512]{3,2,1,0:T(8,128)(2,1)S(1)}, bf16[16,2,32,512]{3,2,1,0:T(8,128)(2,1)S(1)}, u32[]{:S(2)}, u32[]{:S(2)}) collective-permute-start(bf16[16,2,32,512]{3,2,1,0:T(8,128)(2,1)S(1)} %all-to-all-done.refs_0_), channel_id=1, source_target_pairs={{0,16},{16,0},{1,17},{17,1},{2,18},{18,2},{3,19},{19,3},{4,20},{20... | collective-permute-start | bytes 3145736 | tf_op jit(solution)/shard_map/ppermute | solution.py:138
  70.6 2.4 %collective-permute-start.15 = (bf16[2,128,512]{2,1,0:T(8,128)(2,1)}, bf16[2,128,512]{2,1,0:T(8,128)(2,1)S(1)}, u32[]{:S(2)}, u32[]{:S(2)}) collective-permute-start(bf16[2,128,512]{2,1,0:T(8,128)(2,1)} %collective-permute-done.13.refs_11_.refs_9_.refs_7_), channel_id=1, source_target_pairs={{0,4},{5,1},{4,8},{9,5},{8,12},{13,9},{12,14},{15,13},{14,10},{11,... | collective-permute-start | bytes 786440 | tf_op jit(solution)/shard_map/ppermute | solution.py:100
  73.7 2.1 %collective-permute-start.14 = (bf16[2,128,512]{2,1,0:T(8,128)(2,1)}, bf16[2,128,512]{2,1,0:T(8,128)(2,1)}, u32[]{:S(2)}, u32[]{:S(2)}) collective-permute-start(bf16[2,128,512]{2,1,0:T(8,128)(2,1)} %collective-permute-done.12.refs_10_.refs_8_.refs_6_), channel_id=1, source_target_pairs={{0,4},{5,1},{4,8},{9,5},{8,12},{13,9},{12,14},{15,13},{14,10},{11,... | collective-permute-start | bytes 786440 | tf_op jit(solution)/shard_map/ppermute | solution.py:100
  77.8 1.8 %collective-permute-start.17 = (bf16[2,128,512]{2,1,0:T(8,128)(2,1)S(1)}, bf16[2,128,512]{2,1,0:T(8,128)(2,1)}, u32[]{:S(2)}, u32[]{:S(2)}) collective-permute-start(bf16[2,128,512]{2,1,0:T(8,128)(2,1)S(1)} %collective-permute-done.15.refs_13_.refs_11_.refs_9_), channel_id=1, source_target_pairs={{0,4},{5,1},{4,8},{9,5},{8,12},{13,9},{12,14},{15,13},{14,10},{11,... | collective-permute-start | bytes 786440 | tf_op jit(solution)/shard_map/ppermute | solution.py:100
  79.6 0.8 collective-permute-done.14.refs_12_.refs_10_.refs_8_
  80.4 2.1 %collective-permute-start.16 = (bf16[2,128,512]{2,1,0:T(8,128)(2,1)}, bf16[2,128,512]{2,1,0:T(8,128)(2,1)}, u32[]{:S(2)}, u32[]{:S(2)}) collective-permute-start(bf16[2,128,512]{2,1,0:T(8,128)(2,1)} %collective-permute-done.14.refs_12_.refs_10_.refs_8_), channel_id=1, source_target_pairs={{0,4},{5,1},{4,8},{9,5},{8,12},{13,9},{12,14},{15,13},{14,10},{11,... | collective-permute-start | bytes 786440 | tf_op jit(solution)/shard_map/ppermute | solution.py:100
  82.5 0.7 copy-done.29
  83.3 0.7 copy-done.31
  84.5 0.7 copy-done.27
  85.2 1.0 collective-permute-start.19
  86.1 0.9 collective-permute-done.16.refs_14_.refs_12_.refs_10_
  87.1 2.1 %collective-permute-start.18 = (bf16[2,128,512]{2,1,0:T(8,128)(2,1)}, bf16[2,128,512]{2,1,0:T(8,128)(2,1)}, u32[]{:S(2)}, u32[]{:S(2)}) collective-permute-start(bf16[2,128,512]{2,1,0:T(8,128)(2,1)} %collective-permute-done.16.refs_14_.refs_12_.refs_10_), channel_id=1, source_target_pairs={{0,4},{5,1},{4,8},{9,5},{8,12},{13,9},{12,14},{15,13},{14,10},{11,... | collective-permute-start | bytes 786440 | tf_op jit(solution)/shard_map/ppermute | solution.py:100
  91.9 2.8 %collective-permute-done.18.refs_14_.refs_12_ = bf16[2,128,512]{2,1,0:T(8,128)(2,1)} collective-permute-done((bf16[2,128,512]{2,1,0:T(8,128)(2,1)}, bf16[2,128,512]{2,1,0:T(8,128)(2,1)}, u32[]{:S(2)}, u32[]{:S(2)}) %collective-permute-start.18) | collective-permute-done | bytes 262176 | tf_op jit(solution)/shard_map/ppermute | solution.py:100
  94.7 1.2 collective-permute-start.21
  95.9 1.0 copy-done.9
  96.9 1.0 collective-permute-start.20
  98.7 1.2 copy-done.10
  100.1 2.1 %shard_map.158 = (bf16[2,2,512,512]{3,2,1,0:T(8,128)(2,1)S(1)}, f32[2]{0:T(128)S(1)}) custom-call(s32[32]{0:T(128)S(1)} %copy-done.37, s32[32]{0:T(128)S(1)} %reshape.210.list_ref, s32[6]{0:T(128)S(1)} %stack.27.where_ref, bf16[16,2,32,512]{3,2,1,0:T(8,128)(2,1)S(1)} %all-to-all-done.refs_0_, bf16[16,2,32,512]{3,2,1,0:T(8,128)(2,1)S(1)} %copy-done.10), custom_call_target="tpu_custom_call" | custom-call | flops 2000000000 | bytes 6000000 | tf_op jit(solution)/shard_map/pallas_call | solution.py:276
  102.9 1.3 %collective-permute-done.20.refs_14_ = bf16[2,128,512]{2,1,0:T(8,128)(2,1)} collective-permute-done((bf16[2,128,512]{2,1,0:T(8,128)(2,1)}, bf16[2,128,512]{2,1,0:T(8,128)(2,1)}, u32[]{:S(2)}, u32[]{:S(2)}) %collective-permute-start.20) | collective-permute-done | bytes 262176 | tf_op jit(solution)/shard_map/ppermute | solution.py:100
  104.4 1.2 copy-done.39
  105.6 6.5 %shard_map.159.refs_38_ = f32[2,512,512]{2,1,0:T(8,128)S(1)} custom-call(s32[6]{0:T(128)S(1)} %stack.27.where_ref, f32[2]{0:T(128)S(1)} %get-tuple-element.4.sigma_ref, bf16[2,128,512]{2,1,0:T(8,128)(2,1)S(1)} %bitcast.50, bf16[2,128,512]{2,1,0:T(8,128)(2,1)S(1)} %bitcast.47, bf16[2,128,512]{2,1,0:T(8,128)(2,1)S(1)} %copy-done.8, ...), custom_call_target="tpu_custom_call" | custom-call | flops 5000000000 | bytes 10000000 | tf_op jit(solution)/shard_map/pallas_call | solution.py:296
  112.2 6.7 %shard_map.160.refs_38_ = f32[2,512,512]{2,1,0:T(8,128)S(1)} custom-call(s32[6]{0:T(128)S(1)} %stack.27.where_ref, f32[2]{0:T(128)S(1)} %get-tuple-element.4.sigma_ref, bf16[2,128,512]{2,1,0:T(8,128)(2,1)S(1)} %copy-done.8, bf16[2,128,512]{2,1,0:T(8,128)(2,1)S(1)} %copy-done.4, bf16[2,128,512]{2,1,0:T(8,128)(2,1)} %bitcast_select_fusion.3.refs_4_.refs_2_.refs_0_, ...), custom_call_target="tpu_custom_call" | custom-call | flops 5000000000 | bytes 10000000 | tf_op jit(solution)/shard_map/pallas_call | solution.py:296
  118.8 7.3 %shard_map.161 = (f32[2]{0:T(128)}, f32[2]{0:T(128)}) custom-call(s32[6]{0:T(128)S(1)} %stack.27.where_ref, f32[2]{0:T(128)S(1)} %get-tuple-element.4.sigma_ref, bf16[2,128,512]{2,1,0:T(8,128)(2,1)} %bitcast_select_fusion.3.refs_4_.refs_2_.refs_0_, bf16[2,128,512]{2,1,0:T(8,128)(2,1)S(1)} %copy-done.6, bf16[2,128,512]{2,1,0:T(8,128)(2,1)S(1)} %copy-done.12, ...), custom_call_target="tpu_custom_call" | custom-call | flops 5000000000 | bytes 10000000 | tf_op jit(solution)/shard_map/pallas_call | solution.py:296
  (150 shorter events, 12.0 us)
Async XLA Ops:
  4.2 13.0 %collective-permute-start.1 = (bf16[2,131072]{1,0:T(2,128)(2,1)}, bf16[2,131072]{1,0:T(2,128)(2,1)}, u32[]{:S(2)}, u32[]{:S(2)}) collective-permute-start(bf16[2,131072]{1,0:T(2,128)(2,1)} %get-tuple-element.9), channel_id=1, source_target_pairs={{0,1},{1,0},{2,3},{3,2},{4,5},{5,4},{6,7},{7,6},{8,9},{9,8},{10,11... | collective-permute-start | bytes 1572872 | tf_op jit(solution)/shard_map/ppermute | solution.py:73
  4.7 12.5 %collective-permute-start.2 = (bf16[2,131072]{1,0:T(2,128)(2,1)}, bf16[2,131072]{1,0:T(2,128)(2,1)}, u32[]{:S(2)}, u32[]{:S(2)}) collective-permute-start(bf16[2,131072]{1,0:T(2,128)(2,1)} %get-tuple-element.10), channel_id=1, source_target_pairs={{0,1},{1,0},{2,3},{3,2},{4,5},{5,4},{6,7},{7,6},{8,9},{9,8},{10,11... | collective-permute-start | bytes 1572872 | tf_op jit(solution)/shard_map/ppermute | solution.py:73
  4.7 12.5 %collective-permute-start.3 = (bf16[2,131072]{1,0:T(2,128)(2,1)}, bf16[2,131072]{1,0:T(2,128)(2,1)}, u32[]{:S(2)}, u32[]{:S(2)}) collective-permute-start(bf16[2,131072]{1,0:T(2,128)(2,1)} %get-tuple-element.11), channel_id=1, source_target_pairs={{0,1},{1,0},{2,3},{3,2},{4,5},{5,4},{6,7},{7,6},{8,9},{9,8},{10,11... | collective-permute-start | bytes 1572872 | tf_op jit(solution)/shard_map/ppermute | solution.py:73
  9.5 59.1 %all-to-all-start = ((bf16[16,2,32,512]{3,2,1,0:T(8,128)(2,1)}), bf16[16,2,32,512]{3,2,1,0:T(8,128)(2,1)S(1)}, u32[]{:S(2)}, u32[]{:S(2)}) async-start(bf16[16,2,32,512]{3,2,1,0:T(8,128)(2,1)} %reshape.211), calls=%async_computation | async-start | bytes 2097152 | tf_op jit(solution)/shard_map/all_to_all | solution.py:132
  20.6 16.8 %collective-permute-start.6 = (bf16[2,128,512]{2,1,0:T(8,128)(2,1)S(1)}, bf16[2,128,512]{2,1,0:T(8,128)(2,1)S(1)}, u32[]{:S(2)}, u32[]{:S(2)}) collective-permute-start(bf16[2,128,512]{2,1,0:T(8,128)(2,1)S(1)} %bitcast.45), channel_id=1, source_target_pairs={{0,4},{5,1},{4,8},{9,5},{8,12},{13,9},{12,14},{15,13},{14,10},{11,... | collective-permute-start | bytes 786440 | tf_op jit(solution)/shard_map/ppermute | solution.py:100
  22.7 25.9 %copy-start.1 = (bf16[1,2,128,512]{3,2,1,0:T(8,128)(2,1)}, bf16[1,2,128,512]{3,2,1,0:T(8,128)(2,1)S(1)}, u32[]{:S(2)}) copy-start(bf16[1,2,128,512]{3,2,1,0:T(8,128)(2,1)S(1)} %copy.32) | copy-start | bytes 786436
  22.7 22.0 %collective-permute-start.4 = (bf16[2,128,512]{2,1,0:T(8,128)(2,1)S(1)}, bf16[2,128,512]{2,1,0:T(8,128)(2,1)S(1)}, u32[]{:S(2)}, u32[]{:S(2)}) collective-permute-start(bf16[2,128,512]{2,1,0:T(8,128)(2,1)S(1)} %bitcast.48), channel_id=1, source_target_pairs={{0,4},{5,1},{4,8},{9,5},{8,12},{13,9},{12,14},{15,13},{14,10},{11,... | collective-permute-start | bytes 786440 | tf_op jit(solution)/shard_map/ppermute | solution.py:100
  24.9 64.3 %copy-start.42 = (s32[3]{0:T(128)S(1)}, s32[3]{0:T(128)}, u32[]{:S(2)}) copy-start(s32[3]{0:T(128)} %param.20) | copy-start | bytes 40
  24.9 73.8 %copy-start.37 = (s32[32]{0:T(128)S(1)}, s32[32]{0:T(128)}, u32[]{:S(2)}) copy-start(s32[32]{0:T(128)} %cut_ref.1) | copy-start | bytes 388
  37.4 30.3 %copy-start.3 = (bf16[2,128,512]{2,1,0:T(8,128)(2,1)}, bf16[2,128,512]{2,1,0:T(8,128)(2,1)S(1)}, u32[]{:S(2)}) copy-start(bf16[2,128,512]{2,1,0:T(8,128)(2,1)S(1)} %bitcast_select_fusion.refs_3_.refs_1_) | copy-start | bytes 786436
  37.5 11.1 %collective-permute-start.7 = (bf16[2,128,512]{2,1,0:T(8,128)(2,1)S(1)}, bf16[2,128,512]{2,1,0:T(8,128)(2,1)S(1)}, u32[]{:S(2)}, u32[]{:S(2)}) collective-permute-start(bf16[2,128,512]{2,1,0:T(8,128)(2,1)S(1)} %bitcast_select_fusion.refs_3_.refs_1_), channel_id=1, source_target_pairs={{0,4},{5,1},{4,8},{9,5},{8,12},{13,9},{12,14},{15,13},{14,10},{11,... | collective-permute-start | bytes 786440 | tf_op jit(solution)/shard_map/ppermute | solution.py:100
  44.7 23.1 %copy-start.7 = (bf16[2,128,512]{2,1,0:T(8,128)(2,1)}, bf16[2,128,512]{2,1,0:T(8,128)(2,1)S(1)}, u32[]{:S(2)}) copy-start(bf16[2,128,512]{2,1,0:T(8,128)(2,1)S(1)} %bitcast_select_fusion.2.refs_2_.refs_0_) | copy-start | bytes 786436
  44.7 6.6 %collective-permute-start.5 = (bf16[2,128,512]{2,1,0:T(8,128)(2,1)S(1)}, bf16[2,128,512]{2,1,0:T(8,128)(2,1)S(1)}, u32[]{:S(2)}, u32[]{:S(2)}) collective-permute-start(bf16[2,128,512]{2,1,0:T(8,128)(2,1)S(1)} %bitcast_select_fusion.2.refs_2_.refs_0_), channel_id=1, source_target_pairs={{0,4},{5,1},{4,8},{9,5},{8,12},{13,9},{12,14},{15,13},{14,10},{11,... | collective-permute-start | bytes 786440 | tf_op jit(solution)/shard_map/ppermute | solution.py:100
  47.5 7.6 %collective-permute-start.40 = (bf16[2,128,512]{2,1,0:T(8,128)(2,1)S(1)}, bf16[2,128,512]{2,1,0:T(8,128)(2,1)S(1)}, u32[]{:S(2)}, u32[]{:S(2)}) collective-permute-start(bf16[2,128,512]{2,1,0:T(8,128)(2,1)S(1)} %bitcast.49), channel_id=1, source_target_pairs={{0,1},{1,0},{2,3},{3,2},{4,5},{5,4},{6,7},{7,6},{8,9},{9,8},{10,11... | collective-permute-start | bytes 786440 | tf_op jit(solution)/shard_map/ppermute | solution.py:98
  48.6 8.4 %collective-permute-start.9 = (bf16[2,128,512]{2,1,0:T(8,128)(2,1)S(1)}, bf16[2,128,512]{2,1,0:T(8,128)(2,1)}, u32[]{:S(2)}, u32[]{:S(2)}) collective-permute-start(bf16[2,128,512]{2,1,0:T(8,128)(2,1)S(1)} %bitcast_select_fusion.1.refs_5_.refs_3_.refs_1_), channel_id=1, source_target_pairs={{0,4},{5,1},{4,8},{9,5},{8,12},{13,9},{12,14},{15,13},{14,10},{11,... | collective-permute-start | bytes 786440 | tf_op jit(solution)/shard_map/ppermute | solution.py:100
  52.1 8.4 %collective-permute-start.8 = (bf16[2,128,512]{2,1,0:T(8,128)(2,1)}, bf16[2,128,512]{2,1,0:T(8,128)(2,1)S(1)}, u32[]{:S(2)}, u32[]{:S(2)}) collective-permute-start(bf16[2,128,512]{2,1,0:T(8,128)(2,1)} %bitcast_select_fusion.3.refs_4_.refs_2_.refs_0_), channel_id=1, source_target_pairs={{0,4},{5,1},{4,8},{9,5},{8,12},{13,9},{12,14},{15,13},{14,10},{11,... | collective-permute-start | bytes 786440 | tf_op jit(solution)/shard_map/ppermute | solution.py:100
  54.6 6.7 %collective-permute-start.41 = (bf16[2,128,512]{2,1,0:T(8,128)(2,1)S(1)}, bf16[2,128,512]{2,1,0:T(8,128)(2,1)S(1)}, u32[]{:S(2)}, u32[]{:S(2)}) collective-permute-start(bf16[2,128,512]{2,1,0:T(8,128)(2,1)S(1)} %bitcast.46), channel_id=1, source_target_pairs={{0,1},{1,0},{2,3},{3,2},{4,5},{5,4},{6,7},{7,6},{8,9},{9,8},{10,11... | collective-permute-start | bytes 786440 | tf_op jit(solution)/shard_map/ppermute | solution.py:98
  54.6 7.4 %collective-permute-start.39 = (bf16[2,128,512]{2,1,0:T(8,128)(2,1)S(1)}, bf16[2,128,512]{2,1,0:T(8,128)(2,1)S(1)}, u32[]{:S(2)}, u32[]{:S(2)}) collective-permute-start(bf16[2,128,512]{2,1,0:T(8,128)(2,1)S(1)} %bitcast_select_fusion.refs_3_.refs_1_), channel_id=1, source_target_pairs={{0,1},{1,0},{2,3},{3,2},{4,5},{5,4},{6,7},{7,6},{8,9},{9,8},{10,11... | collective-permute-start | bytes 786440 | tf_op jit(solution)/shard_map/ppermute | solution.py:98
  55.8 7.4 %collective-permute-start.38 = (bf16[2,128,512]{2,1,0:T(8,128)(2,1)S(1)}, bf16[2,128,512]{2,1,0:T(8,128)(2,1)S(1)}, u32[]{:S(2)}, u32[]{:S(2)}) collective-permute-start(bf16[2,128,512]{2,1,0:T(8,128)(2,1)S(1)} %bitcast_select_fusion.2.refs_2_.refs_0_), channel_id=1, source_target_pairs={{0,1},{1,0},{2,3},{3,2},{4,5},{5,4},{6,7},{7,6},{8,9},{9,8},{10,11... | collective-permute-start | bytes 786440 | tf_op jit(solution)/shard_map/ppermute | solution.py:98
  57.0 7.0 %collective-permute-start.11 = (bf16[2,128,512]{2,1,0:T(8,128)(2,1)}, bf16[2,128,512]{2,1,0:T(8,128)(2,1)}, u32[]{:S(2)}, u32[]{:S(2)}) collective-permute-start(bf16[2,128,512]{2,1,0:T(8,128)(2,1)} %collective-permute-done.9.refs_7_.refs_5_.refs_3_), channel_id=1, source_target_pairs={{0,4},{5,1},{4,8},{9,5},{8,12},{13,9},{12,14},{15,13},{14,10},{11,... | collective-permute-start | bytes 786440 | tf_op jit(solution)/shard_map/ppermute | solution.py:100
  60.5 6.5 %collective-permute-start.10 = (bf16[2,128,512]{2,1,0:T(8,128)(2,1)S(1)}, bf16[2,128,512]{2,1,0:T(8,128)(2,1)}, u32[]{:S(2)}, u32[]{:S(2)}) collective-permute-start(bf16[2,128,512]{2,1,0:T(8,128)(2,1)S(1)} %collective-permute-done.8.refs_6_.refs_4_.refs_2_), channel_id=1, source_target_pairs={{0,4},{5,1},{4,8},{9,5},{8,12},{13,9},{12,14},{15,13},{14,10},{11,... | collective-permute-start | bytes 786440 | tf_op jit(solution)/shard_map/ppermute | solution.py:100
  62.0 5.8 %collective-permute-start.23 = (bf16[2,128,512]{2,1,0:T(8,128)(2,1)S(1)}, bf16[2,128,512]{2,1,0:T(8,128)(2,1)S(1)}, u32[]{:S(2)}, u32[]{:S(2)}) collective-permute-start(bf16[2,128,512]{2,1,0:T(8,128)(2,1)S(1)} %bitcast_select_fusion.1.refs_5_.refs_3_.refs_1_), channel_id=1, source_target_pairs={{0,1},{1,0},{2,3},{3,2},{4,5},{5,4},{6,7},{7,6},{8,9},{9,8},{10,11... | collective-permute-start | bytes 786440 | tf_op jit(solution)/shard_map/ppermute | solution.py:98
  62.7 7.3 %collective-permute-start.22 = (bf16[2,128,512]{2,1,0:T(8,128)(2,1)}, bf16[2,128,512]{2,1,0:T(8,128)(2,1)}, u32[]{:S(2)}, u32[]{:S(2)}) collective-permute-start(bf16[2,128,512]{2,1,0:T(8,128)(2,1)} %bitcast_select_fusion.3.refs_4_.refs_2_.refs_0_), channel_id=1, source_target_pairs={{0,1},{1,0},{2,3},{3,2},{4,5},{5,4},{6,7},{7,6},{8,9},{9,8},{10,11... | collective-permute-start | bytes 786440 | tf_op jit(solution)/shard_map/ppermute | solution.py:98
  64.0 6.1 %collective-permute-start.25 = (bf16[2,128,512]{2,1,0:T(8,128)(2,1)}, bf16[2,128,512]{2,1,0:T(8,128)(2,1)}, u32[]{:S(2)}, u32[]{:S(2)}) collective-permute-start(bf16[2,128,512]{2,1,0:T(8,128)(2,1)} %collective-permute-done.9.refs_7_.refs_5_.refs_3_), channel_id=1, source_target_pairs={{0,1},{1,0},{2,3},{3,2},{4,5},{5,4},{6,7},{7,6},{8,9},{9,8},{10,11... | collective-permute-start | bytes 786440 | tf_op jit(solution)/shard_map/ppermute | solution.py:98
  64.0 6.7 %collective-permute-start.13 = (bf16[2,128,512]{2,1,0:T(8,128)(2,1)}, bf16[2,128,512]{2,1,0:T(8,128)(2,1)}, u32[]{:S(2)}, u32[]{:S(2)}) collective-permute-start(bf16[2,128,512]{2,1,0:T(8,128)(2,1)} %collective-permute-done.11.refs_9_.refs_7_.refs_5_), channel_id=1, source_target_pairs={{0,4},{5,1},{4,8},{9,5},{8,12},{13,9},{12,14},{15,13},{14,10},{11,... | collective-permute-start | bytes 786440 | tf_op jit(solution)/shard_map/ppermute | solution.py:100
  67.0 6.7 %collective-permute-start.12 = (bf16[2,128,512]{2,1,0:T(8,128)(2,1)}, bf16[2,128,512]{2,1,0:T(8,128)(2,1)}, u32[]{:S(2)}, u32[]{:S(2)}) collective-permute-start(bf16[2,128,512]{2,1,0:T(8,128)(2,1)} %collective-permute-done.10.refs_8_.refs_6_.refs_4_), channel_id=1, source_target_pairs={{0,4},{5,1},{4,8},{9,5},{8,12},{13,9},{12,14},{15,13},{14,10},{11,... | collective-permute-start | bytes 786440 | tf_op jit(solution)/shard_map/ppermute | solution.py:100
  68.5 27.4 %collective-permute-start = (bf16[16,2,32,512]{3,2,1,0:T(8,128)(2,1)S(1)}, bf16[16,2,32,512]{3,2,1,0:T(8,128)(2,1)S(1)}, u32[]{:S(2)}, u32[]{:S(2)}) collective-permute-start(bf16[16,2,32,512]{3,2,1,0:T(8,128)(2,1)S(1)} %all-to-all-done.refs_0_), channel_id=1, source_target_pairs={{0,16},{16,0},{1,17},{17,1},{2,18},{18,2},{3,19},{19,3},{4,20},{20... | collective-permute-start | bytes 3145736 | tf_op jit(solution)/shard_map/ppermute | solution.py:138
  70.0 5.8 %collective-permute-start.24 = (bf16[2,128,512]{2,1,0:T(8,128)(2,1)}, bf16[2,128,512]{2,1,0:T(8,128)(2,1)S(1)}, u32[]{:S(2)}, u32[]{:S(2)}) collective-permute-start(bf16[2,128,512]{2,1,0:T(8,128)(2,1)} %copy-done.11), channel_id=1, source_target_pairs={{0,1},{1,0},{2,3},{3,2},{4,5},{5,4},{6,7},{7,6},{8,9},{9,8},{10,11... | collective-permute-start | bytes 786440 | tf_op jit(solution)/shard_map/ppermute | solution.py:98
  70.0 6.5 %collective-permute-start.27 = (bf16[2,128,512]{2,1,0:T(8,128)(2,1)}, bf16[2,128,512]{2,1,0:T(8,128)(2,1)S(1)}, u32[]{:S(2)}, u32[]{:S(2)}) collective-permute-start(bf16[2,128,512]{2,1,0:T(8,128)(2,1)} %collective-permute-done.11.refs_9_.refs_7_.refs_5_), channel_id=1, source_target_pairs={{0,1},{1,0},{2,3},{3,2},{4,5},{5,4},{6,7},{7,6},{8,9},{9,8},{10,11... | collective-permute-start | bytes 786440 | tf_op jit(solution)/shard_map/ppermute | solution.py:98
  70.6 7.1 %collective-permute-start.15 = (bf16[2,128,512]{2,1,0:T(8,128)(2,1)}, bf16[2,128,512]{2,1,0:T(8,128)(2,1)S(1)}, u32[]{:S(2)}, u32[]{:S(2)}) collective-permute-start(bf16[2,128,512]{2,1,0:T(8,128)(2,1)} %collective-permute-done.13.refs_11_.refs_9_.refs_7_), channel_id=1, source_target_pairs={{0,4},{5,1},{4,8},{9,5},{8,12},{13,9},{12,14},{15,13},{14,10},{11,... | collective-permute-start | bytes 786440 | tf_op jit(solution)/shard_map/ppermute | solution.py:100
  73.7 6.7 %collective-permute-start.14 = (bf16[2,128,512]{2,1,0:T(8,128)(2,1)}, bf16[2,128,512]{2,1,0:T(8,128)(2,1)}, u32[]{:S(2)}, u32[]{:S(2)}) collective-permute-start(bf16[2,128,512]{2,1,0:T(8,128)(2,1)} %collective-permute-done.12.refs_10_.refs_8_.refs_6_), channel_id=1, source_target_pairs={{0,4},{5,1},{4,8},{9,5},{8,12},{13,9},{12,14},{15,13},{14,10},{11,... | collective-permute-start | bytes 786440 | tf_op jit(solution)/shard_map/ppermute | solution.py:100
  76.5 6.0 %collective-permute-start.26 = (bf16[2,128,512]{2,1,0:T(8,128)(2,1)}, bf16[2,128,512]{2,1,0:T(8,128)(2,1)S(1)}, u32[]{:S(2)}, u32[]{:S(2)}) collective-permute-start(bf16[2,128,512]{2,1,0:T(8,128)(2,1)} %collective-permute-done.10.refs_8_.refs_6_.refs_4_), channel_id=1, source_target_pairs={{0,1},{1,0},{2,3},{3,2},{4,5},{5,4},{6,7},{7,6},{8,9},{9,8},{10,11... | collective-permute-start | bytes 786440 | tf_op jit(solution)/shard_map/ppermute | solution.py:98
  77.2 6.0 %collective-permute-start.29 = (bf16[2,128,512]{2,1,0:T(8,128)(2,1)}, bf16[2,128,512]{2,1,0:T(8,128)(2,1)S(1)}, u32[]{:S(2)}, u32[]{:S(2)}) collective-permute-start(bf16[2,128,512]{2,1,0:T(8,128)(2,1)} %collective-permute-done.13.refs_11_.refs_9_.refs_7_), channel_id=1, source_target_pairs={{0,1},{1,0},{2,3},{3,2},{4,5},{5,4},{6,7},{7,6},{8,9},{9,8},{10,11... | collective-permute-start | bytes 786440 | tf_op jit(solution)/shard_map/ppermute | solution.py:98
  77.8 7.4 %collective-permute-start.17 = (bf16[2,128,512]{2,1,0:T(8,128)(2,1)S(1)}, bf16[2,128,512]{2,1,0:T(8,128)(2,1)}, u32[]{:S(2)}, u32[]{:S(2)}) collective-permute-start(bf16[2,128,512]{2,1,0:T(8,128)(2,1)S(1)} %collective-permute-done.15.refs_13_.refs_11_.refs_9_), channel_id=1, source_target_pairs={{0,4},{5,1},{4,8},{9,5},{8,12},{13,9},{12,14},{15,13},{14,10},{11,... | collective-permute-start | bytes 786440 | tf_op jit(solution)/shard_map/ppermute | solution.py:100
  80.4 6.7 %collective-permute-start.16 = (bf16[2,128,512]{2,1,0:T(8,128)(2,1)}, bf16[2,128,512]{2,1,0:T(8,128)(2,1)}, u32[]{:S(2)}, u32[]{:S(2)}) collective-permute-start(bf16[2,128,512]{2,1,0:T(8,128)(2,1)} %collective-permute-done.14.refs_12_.refs_10_.refs_8_), channel_id=1, source_target_pairs={{0,4},{5,1},{4,8},{9,5},{8,12},{13,9},{12,14},{15,13},{14,10},{11,... | collective-permute-start | bytes 786440 | tf_op jit(solution)/shard_map/ppermute | solution.py:100
  83.2 6.3 %collective-permute-start.28 = (bf16[2,128,512]{2,1,0:T(8,128)(2,1)}, bf16[2,128,512]{2,1,0:T(8,128)(2,1)S(1)}, u32[]{:S(2)}, u32[]{:S(2)}) collective-permute-start(bf16[2,128,512]{2,1,0:T(8,128)(2,1)} %collective-permute-done.12.refs_10_.refs_8_.refs_6_), channel_id=1, source_target_pairs={{0,1},{1,0},{2,3},{3,2},{4,5},{5,4},{6,7},{7,6},{8,9},{9,8},{10,11... | collective-permute-start | bytes 786440 | tf_op jit(solution)/shard_map/ppermute | solution.py:98
  84.0 6.3 %collective-permute-start.31 = (bf16[2,128,512]{2,1,0:T(8,128)(2,1)S(1)}, bf16[2,128,512]{2,1,0:T(8,128)(2,1)S(1)}, u32[]{:S(2)}, u32[]{:S(2)}) collective-permute-start(bf16[2,128,512]{2,1,0:T(8,128)(2,1)S(1)} %collective-permute-done.15.refs_13_.refs_11_.refs_9_), channel_id=1, source_target_pairs={{0,1},{1,0},{2,3},{3,2},{4,5},{5,4},{6,7},{7,6},{8,9},{9,8},{10,11... | collective-permute-start | bytes 786440 | tf_op jit(solution)/shard_map/ppermute | solution.py:98
  85.2 6.7 %collective-permute-start.19 = (bf16[2,128,512]{2,1,0:T(8,128)(2,1)}, bf16[2,128,512]{2,1,0:T(8,128)(2,1)}, u32[]{:S(2)}, u32[]{:S(2)}) collective-permute-start(bf16[2,128,512]{2,1,0:T(8,128)(2,1)} %collective-permute-done.17.refs_15_.refs_13_.refs_11_), channel_id=1, source_target_pairs={{0,4},{5,1},{4,8},{9,5},{8,12},{13,9},{12,14},{15,13},{14,10},{11,... | collective-permute-start | bytes 786440 | tf_op jit(solution)/shard_map/ppermute | solution.py:100
  87.1 7.6 %collective-permute-start.18 = (bf16[2,128,512]{2,1,0:T(8,128)(2,1)}, bf16[2,128,512]{2,1,0:T(8,128)(2,1)}, u32[]{:S(2)}, u32[]{:S(2)}) collective-permute-start(bf16[2,128,512]{2,1,0:T(8,128)(2,1)} %collective-permute-done.16.refs_14_.refs_12_.refs_10_), channel_id=1, source_target_pairs={{0,4},{5,1},{4,8},{9,5},{8,12},{13,9},{12,14},{15,13},{14,10},{11,... | collective-permute-start | bytes 786440 | tf_op jit(solution)/shard_map/ppermute | solution.py:100
  90.2 12.0 %collective-permute-start.30 = (bf16[2,128,512]{2,1,0:T(8,128)(2,1)}, bf16[2,128,512]{2,1,0:T(8,128)(2,1)}, u32[]{:S(2)}, u32[]{:S(2)}) collective-permute-start(bf16[2,128,512]{2,1,0:T(8,128)(2,1)} %collective-permute-done.14.refs_12_.refs_10_.refs_8_), channel_id=1, source_target_pairs={{0,1},{1,0},{2,3},{3,2},{4,5},{5,4},{6,7},{7,6},{8,9},{9,8},{10,11... | collective-permute-start | bytes 786440 | tf_op jit(solution)/shard_map/ppermute | solution.py:98
  90.9 11.4 %collective-permute-start.33 = (bf16[2,128,512]{2,1,0:T(8,128)(2,1)}, bf16[2,128,512]{2,1,0:T(8,128)(2,1)}, u32[]{:S(2)}, u32[]{:S(2)}) collective-permute-start(bf16[2,128,512]{2,1,0:T(8,128)(2,1)} %collective-permute-done.17.refs_15_.refs_13_.refs_11_), channel_id=1, source_target_pairs={{0,1},{1,0},{2,3},{3,2},{4,5},{5,4},{6,7},{7,6},{8,9},{9,8},{10,11... | collective-permute-start | bytes 786440 | tf_op jit(solution)/shard_map/ppermute | solution.py:98
  91.9 12.3 %collective-permute-start.32 = (bf16[2,128,512]{2,1,0:T(8,128)(2,1)}, bf16[2,128,512]{2,1,0:T(8,128)(2,1)}, u32[]{:S(2)}, u32[]{:S(2)}) collective-permute-start(bf16[2,128,512]{2,1,0:T(8,128)(2,1)} %collective-permute-done.16.refs_14_.refs_12_.refs_10_), channel_id=1, source_target_pairs={{0,1},{1,0},{2,3},{3,2},{4,5},{5,4},{6,7},{7,6},{8,9},{9,8},{10,11... | collective-permute-start | bytes 786440 | tf_op jit(solution)/shard_map/ppermute | solution.py:98
  94.7 8.1 %collective-permute-start.21 = (bf16[2,128,512]{2,1,0:T(8,128)(2,1)}, bf16[2,128,512]{2,1,0:T(8,128)(2,1)}, u32[]{:S(2)}, u32[]{:S(2)}) collective-permute-start(bf16[2,128,512]{2,1,0:T(8,128)(2,1)} %collective-permute-done.19.refs_15_.refs_13_), channel_id=1, source_target_pairs={{0,4},{5,1},{4,8},{9,5},{8,12},{13,9},{12,14},{15,13},{14,10},{11,... | collective-permute-start | bytes 786440 | tf_op jit(solution)/shard_map/ppermute | solution.py:100
  96.9 7.3 %collective-permute-start.20 = (bf16[2,128,512]{2,1,0:T(8,128)(2,1)}, bf16[2,128,512]{2,1,0:T(8,128)(2,1)}, u32[]{:S(2)}, u32[]{:S(2)}) collective-permute-start(bf16[2,128,512]{2,1,0:T(8,128)(2,1)} %collective-permute-done.18.refs_14_.refs_12_), channel_id=1, source_target_pairs={{0,4},{5,1},{4,8},{9,5},{8,12},{13,9},{12,14},{15,13},{14,10},{11,... | collective-permute-start | bytes 786440 | tf_op jit(solution)/shard_map/ppermute | solution.py:100
  102.2 9.9 %collective-permute-start.35 = (bf16[2,128,512]{2,1,0:T(8,128)(2,1)}, bf16[2,128,512]{2,1,0:T(8,128)(2,1)S(1)}, u32[]{:S(2)}, u32[]{:S(2)}) collective-permute-start(bf16[2,128,512]{2,1,0:T(8,128)(2,1)} %collective-permute-done.19.refs_15_.refs_13_), channel_id=1, source_target_pairs={{0,1},{1,0},{2,3},{3,2},{4,5},{5,4},{6,7},{7,6},{8,9},{9,8},{10,11... | collective-permute-start | bytes 786440 | tf_op jit(solution)/shard_map/ppermute | solution.py:98
  102.3 9.8 %collective-permute-start.34 = (bf16[2,128,512]{2,1,0:T(8,128)(2,1)}, bf16[2,128,512]{2,1,0:T(8,128)(2,1)S(1)}, u32[]{:S(2)}, u32[]{:S(2)}) collective-permute-start(bf16[2,128,512]{2,1,0:T(8,128)(2,1)} %collective-permute-done.18.refs_14_.refs_12_), channel_id=1, source_target_pairs={{0,1},{1,0},{2,3},{3,2},{4,5},{5,4},{6,7},{7,6},{8,9},{9,8},{10,11... | collective-permute-start | bytes 786440 | tf_op jit(solution)/shard_map/ppermute | solution.py:98
  102.8 16.0 %collective-permute-start.37 = (bf16[2,128,512]{2,1,0:T(8,128)(2,1)}, bf16[2,128,512]{2,1,0:T(8,128)(2,1)S(1)}, u32[]{:S(2)}, u32[]{:S(2)}) collective-permute-start(bf16[2,128,512]{2,1,0:T(8,128)(2,1)} %collective-permute-done.21.refs_15_), channel_id=1, source_target_pairs={{0,1},{1,0},{2,3},{3,2},{4,5},{5,4},{6,7},{7,6},{8,9},{9,8},{10,11... | collective-permute-start | bytes 786440 | tf_op jit(solution)/shard_map/ppermute | solution.py:98
  104.2 14.7 %collective-permute-start.36 = (bf16[2,128,512]{2,1,0:T(8,128)(2,1)}, bf16[2,128,512]{2,1,0:T(8,128)(2,1)S(1)}, u32[]{:S(2)}, u32[]{:S(2)}) collective-permute-start(bf16[2,128,512]{2,1,0:T(8,128)(2,1)} %collective-permute-done.20.refs_14_), channel_id=1, source_target_pairs={{0,1},{1,0},{2,3},{3,2},{4,5},{5,4},{6,7},{7,6},{8,9},{9,8},{10,11... | collective-permute-start | bytes 786440 | tf_op jit(solution)/shard_map/ppermute | solution.py:98
  (38 other events, 129.0 us)

commit v15 on v7

--- a/solution.py
+++ b/solution.py
@@ -319,16 +319,11 @@
     me, owner = lax.axis_index("tpl"), owner[0]
     chips = lax.axis_size("tpl") // CORES
     per_device = lists.shape[1]
-    chunks = half_chunks(strain_slots, 0, owner)
-    strain_slots, templates, chunks = lax.optimization_barrier((strain_slots, templates, chunks))
+    chunks = [chunk for det in range(DET) for chunk in half_chunks(strain_slots, det, owner)]
     parts, places = pick(templates, lists)
     ids = list(range(per_device)) if places is None else places
     near, far = distances(owner)
     where = jnp.stack([jnp.asarray(at, jnp.int32) for at in (me % CORES, near, me, far, *ids)])
-    for det in range(1, DET):
-        more = half_chunks(strain_slots, det, owner)
-        strain_slots, more = lax.optimization_barrier((strain_slots, more))
-        chunks += more
     held = {"arrived": exchange(parts[0]), "small": (slide_turns(slides), where, lists.reshape(-1))}
 
     def templates_here(chunk):

time: 123 us -> 123 us (level)
  starting transfers between devices: 44.4 us -> 49.7 us
  waiting for transfers between devices: 35.5 us -> 31.3 us
    ppermute x18, waiting for transfers between devices: 35.1 us -> 31.2 us  [spread(): arrived.append(lax.ppermute(here, 'tpl', along))]
    all_to_all x1, starting transfers between devices: 3.91 us -> 7.05 us  [exchange(): return lax.all_to_all(block, 'tpl', split_axis=0, concat_axis=0, tiled=True)]
    ppermute x20, starting transfers between devices: 4.53 us -> 6.1 us  [spread(): shared = [lax.ppermute(here, 'tpl', to_partner()) for here in sent]]
    select_n x4, other arithmetic: 3.48 us -> 5.03 us  [spread(): here = jnp.where(on_owner_chip, chunks[slot], arrived[slot - LAG])]
    unnamed x31 -> x23, local copies, waits for them, and re-layouts: 1.65 us -> 0.2 us
    squeeze x3 -> x1, local copies, waits for them, and re-layouts: 3.07 us -> 3.58 us  [half_chunks(): lax.dynamic_slice(strain_slots, (0, det, 0, which * half), (1, 1, 2, half))]
    select_n x3 -> x1, other arithmetic: 3.82 us -> 3.47 us  [half_chunks(): first = jnp.where(core == owner % CORES, side(core), got)]
  transfers between devices with their start and end apart: 43 -> 43, of which waited for: 14 -> 15; matrix products, arithmetic and copies ran while one was open for 12% -> 13% of each run, Pallas kernels for 11% -> 11%
where the time goes in v15:
time: 123 us
  starting transfers between devices  49.7 us (40%)
  waiting for transfers between devices  31.3 us (25%)
  Pallas kernels  20.3 us (17%)
  local copies, waits for them, and re-layouts  10.2 us (8%)
  other arithmetic  9.07 us (7%)
  between operations  1.97 us (2%)
    ppermute x18, starting transfers between devices, spread(): arrived.append(lax.ppermute(here, 'tpl', along))  34.1 us
    ppermute x18, waiting for transfers between devices, spread(): arrived.append(lax.ppermute(here, 'tpl', along))  31.2 us
    pallas_call x3, Pallas kernels, detector(): pl.pallas_call(functools.partial(detector_kernel, det, chips), out_shape=...  18.2 us
    all_to_all x1, starting transfers between devices, exchange(): return lax.all_to_all(block, 'tpl', split_axis=0, concat_axis=0, tiled=True)  7.05 us
    ppermute x20, starting transfers between devices, spread(): shared = [lax.ppermute(here, 'tpl', to_partner()) for here in sent]  6.1 us
    select_n x4, other arithmetic, spread(): here = jnp.where(on_owner_chip, chunks[slot], arrived[slot - LAG])  5.03 us
    squeeze x1, local copies, waits for them, and re-layouts, half_chunks(): lax.dynamic_slice(strain_slots, (0, det, 0, which * half), (1, 1, 2, half))  3.58 us
    select_n x1, other arithmetic, half_chunks(): first = jnp.where(core == owner % CORES, side(core), got)  3.47 us
  transfers between devices with their start and end apart: 43, of which 15 were waited for; matrix products, arithmetic and copies ran while one was open for 13% of the time, Pallas kernels for 11%

profile of v15, /device:TPU:0, one launch (start us, length us, event | category | flops | bytes accessed | tf_op | source)
XLA Modules:
  0.0 122.6 jit_solution(17262593922236410354)
XLA Ops:
  0.7 3.6 %dynamic-slice_bitcast_fusion.2 = (bf16[2,131072]{1,0:T(2,128)(2,1)}, bf16[2,131072]{1,0:T(2,128)(2,1)}, bf16[2,131072]{1,0:T(2,128)(2,1)}) fusion(bf16[1,3,2,262144]{3,2,1,0:T(2,128)(2,1)} %param.15, s32[]{:T(128)S(6)} %select_n.186), kind=kLoop, calls=%fused_computation.6 | loop fusion | bytes 3145732 | tf_op jit(solution)/shard_map/squeeze | solution.py:74
  5.3 2.7 %gather_fusion = bf16[16,2,16384]{2,1,0:T(2,128)(2,1)S(1)} fusion(bf16[32,2,16384]{2,1,0:T(2,128)(2,1)S(1)} %copy-done, s32[1024]{0:T(1024)S(1)} %pad_clamp_fusion), kind=kCustom, calls=%fused_computation | custom fusion | bytes 2097216 | tf_op jit(solution)/shard_map/gather | solution.py:127
  7.9 1.5 %reshape.213 = bf16[16,2,32,512]{3,2,1,0:T(8,128)(2,1)} reshape(bf16[16,2,16384]{2,1,0:T(2,128)(2,1)S(1)} %gather_fusion) | data formatting | bytes 2097152 | tf_op jit(solution)/shard_map/reshape | solution.py:128
  9.5 7.0 %all-to-all-start = ((bf16[16,2,32,512]{3,2,1,0:T(8,128)(2,1)}), bf16[16,2,32,512]{3,2,1,0:T(8,128)(2,1)S(1)}, u32[]{:S(2)}, u32[]{:S(2)}) async-start(bf16[16,2,32,512]{3,2,1,0:T(8,128)(2,1)} %reshape.213), calls=%async_computation | async-start | bytes 2097152 | tf_op jit(solution)/shard_map/all_to_all | solution.py:136
  17.6 3.5 %broadcast_select_fusion.2 = (bf16[2,131072]{1,0:T(2,128)(2,1)S(1)}, bf16[2,131072]{1,0:T(2,128)(2,1)S(1)}, bf16[2,131072]{1,0:T(2,128)(2,1)S(1)}) fusion(bf16[2,131072]{1,0:T(2,128)(2,1)} %collective-permute-done, pred[]{:T(512)S(6)} %eq.43, bf16[1,3,2,262144]{3,2,1,0:T(2,128)(2,1)} %param.15, s32[]{:T(128)S(6)} %select_n.185, ...), kind=kLoop, calls=%fused_computation.3 | loop fusion | flops 786432 | bytes 4718597 | tf_op jit(solution)/shard_map/jit(_where)/select_n | solution.py:76
  21.4 2.0 %collective-permute-start.10 = (bf16[2,128,512]{2,1,0:T(8,128)(2,1)S(1)}, bf16[2,128,512]{2,1,0:T(8,128)(2,1)S(1)}, u32[]{:S(2)}, u32[]{:S(2)}) collective-permute-start(bf16[2,128,512]{2,1,0:T(8,128)(2,1)S(1)} %bitcast.45), channel_id=1, source_target_pairs={{0,4},{5,1},{4,8},{9,5},{8,12},{13,9},{12,14},{15,13},{14,10},{11,... | collective-permute-start | bytes 786440 | tf_op jit(solution)/shard_map/ppermute | solution.py:103
  23.5 1.5 %collective-permute-start.3 = (bf16[2,128,512]{2,1,0:T(8,128)(2,1)S(1)}, bf16[2,128,512]{2,1,0:T(8,128)(2,1)S(1)}, u32[]{:S(2)}, u32[]{:S(2)}) collective-permute-start(bf16[2,128,512]{2,1,0:T(8,128)(2,1)S(1)} %bitcast.48), channel_id=1, source_target_pairs={{0,4},{5,1},{4,8},{9,5},{8,12},{13,9},{12,14},{15,13},{14,10},{11,... | collective-permute-start | bytes 786440 | tf_op jit(solution)/shard_map/ppermute | solution.py:103
  25.0 1.5 %fusion.12 = (bf16[2,65536]{1,0:T(2,128)(2,1)}, bf16[2,65536]{1,0:T(2,128)(2,1)}, bf16[2,65536]{1,0:T(2,128)(2,1)S(1)}, bf16[2,65536]{1,0:T(2,128)(2,1)S(1)}) fusion(bf16[2,131072]{1,0:T(2,128)(2,1)S(1)} %get-tuple-element.24, bf16[2,131072]{1,0:T(2,128)(2,1)S(1)} %get-tuple-element.25), kind=kLoop, calls=%fused_computation.37 | loop fusion | bytes 2097152 | tf_op jit(solution)/shard_map/slice | solution.py:77
  26.5 10.9 %collective-permute-done.10 = bf16[2,128,512]{2,1,0:T(8,128)(2,1)S(1)} collective-permute-done((bf16[2,128,512]{2,1,0:T(8,128)(2,1)S(1)}, bf16[2,128,512]{2,1,0:T(8,128)(2,1)S(1)}, u32[]{:S(2)}, u32[]{:S(2)}) %collective-permute-start.10) | collective-permute-done | bytes 262176 | tf_op jit(solution)/shard_map/ppermute | solution.py:103
  37.4 0.7 bitcast_select_fusion.refs_3_.refs_1_
  38.2 7.1 %collective-permute-start.11 = (bf16[2,128,512]{2,1,0:T(8,128)(2,1)}, bf16[2,128,512]{2,1,0:T(8,128)(2,1)}, u32[]{:S(2)}, u32[]{:S(2)}) collective-permute-start(bf16[2,128,512]{2,1,0:T(8,128)(2,1)} %bitcast_select_fusion.refs_3_.refs_1_), channel_id=1, source_target_pairs={{0,4},{5,1},{4,8},{9,5},{8,12},{13,9},{12,14},{15,13},{14,10},{11,... | collective-permute-start | bytes 786440 | tf_op jit(solution)/shard_map/ppermute | solution.py:103
  45.3 0.7 bitcast_select_fusion.2.refs_2_.refs_0_
  46.0 2.5 %collective-permute-start.4 = (bf16[2,128,512]{2,1,0:T(8,128)(2,1)}, bf16[2,128,512]{2,1,0:T(8,128)(2,1)}, u32[]{:S(2)}, u32[]{:S(2)}) collective-permute-start(bf16[2,128,512]{2,1,0:T(8,128)(2,1)} %bitcast_select_fusion.2.refs_2_.refs_0_), channel_id=1, source_target_pairs={{0,4},{5,1},{4,8},{9,5},{8,12},{13,9},{12,14},{15,13},{14,10},{11,... | collective-permute-start | bytes 786440 | tf_op jit(solution)/shard_map/ppermute | solution.py:103
  49.5 1.8 %bitcast_select_fusion.1.refs_5_.refs_3_.refs_1_ = bf16[2,128,512]{2,1,0:T(8,128)(2,1)} fusion(bf16[2,128,512]{2,1,0:T(8,128)(2,1)} %collective-permute-done.11, bf16[1,2,128,512]{3,1,2,0:T(2,128)(2,1)} %bitcast.54, pred[]{:T(512)S(6)} %eq.42), kind=kLoop, calls=%fused_computation.9 | loop fusion | flops 131072 | bytes 786433 | tf_op jit(solution)/shard_map/jit(_where)/select_n | solution.py:96
  51.3 2.4 %collective-permute-start.12 = (bf16[2,128,512]{2,1,0:T(8,128)(2,1)}, bf16[2,128,512]{2,1,0:T(8,128)(2,1)}, u32[]{:S(2)}, u32[]{:S(2)}) collective-permute-start(bf16[2,128,512]{2,1,0:T(8,128)(2,1)} %bitcast_select_fusion.1.refs_5_.refs_3_.refs_1_), channel_id=1, source_target_pairs={{0,4},{5,1},{4,8},{9,5},{8,12},{13,9},{12,14},{15,13},{14,10},{11,... | collective-permute-start | bytes 786440 | tf_op jit(solution)/shard_map/ppermute | solution.py:103
  53.7 1.8 %bitcast_select_fusion.3.refs_4_.refs_2_.refs_0_ = bf16[2,128,512]{2,1,0:T(8,128)(2,1)} fusion(bf16[2,128,512]{2,1,0:T(8,128)(2,1)} %collective-permute-done.4, bf16[1,2,128,512]{3,1,2,0:T(2,128)(2,1)} %bitcast.53, pred[]{:T(512)S(6)} %eq.42), kind=kLoop, calls=%fused_computation.12 | loop fusion | flops 131072 | bytes 786433 | tf_op jit(solution)/shard_map/jit(_where)/select_n | solution.py:96
  55.5 2.5 %collective-permute-start.5 = (bf16[2,128,512]{2,1,0:T(8,128)(2,1)}, bf16[2,128,512]{2,1,0:T(8,128)(2,1)S(1)}, u32[]{:S(2)}, u32[]{:S(2)}) collective-permute-start(bf16[2,128,512]{2,1,0:T(8,128)(2,1)} %bitcast_select_fusion.3.refs_4_.refs_2_.refs_0_), channel_id=1, source_target_pairs={{0,4},{5,1},{4,8},{9,5},{8,12},{13,9},{12,14},{15,13},{14,10},{11,... | collective-permute-start | bytes 786440 | tf_op jit(solution)/shard_map/ppermute | solution.py:103
  58.1 1.6 %collective-permute-start.9 = (bf16[16,2,32,512]{3,2,1,0:T(8,128)(2,1)S(1)}, bf16[16,2,32,512]{3,2,1,0:T(8,128)(2,1)S(1)}, u32[]{:S(2)}, u32[]{:S(2)}) collective-permute-start(bf16[16,2,32,512]{3,2,1,0:T(8,128)(2,1)S(1)} %all-to-all-done.refs_0_), channel_id=1, source_target_pairs={{0,16},{16,0},{1,17},{17,1},{2,18},{18,2},{3,19},{19,3},{4,20},{20... | collective-permute-start | bytes 3145736 | tf_op jit(solution)/shard_map/ppermute | solution.py:142
  59.8 0.8 collective-permute-start.13
  61.2 1.5 %collective-permute-done.5.refs_6_.refs_4_.refs_2_ = bf16[2,128,512]{2,1,0:T(8,128)(2,1)S(1)} collective-permute-done((bf16[2,128,512]{2,1,0:T(8,128)(2,1)}, bf16[2,128,512]{2,1,0:T(8,128)(2,1)S(1)}, u32[]{:S(2)}, u32[]{:S(2)}) %collective-permute-start.5) | collective-permute-done | bytes 262176 | tf_op jit(solution)/shard_map/ppermute | solution.py:103
  62.6 2.0 %collective-permute-start.6 = (bf16[2,128,512]{2,1,0:T(8,128)(2,1)S(1)}, bf16[2,128,512]{2,1,0:T(8,128)(2,1)S(1)}, u32[]{:S(2)}, u32[]{:S(2)}) collective-permute-start(bf16[2,128,512]{2,1,0:T(8,128)(2,1)S(1)} %collective-permute-done.5.refs_6_.refs_4_.refs_2_), channel_id=1, source_target_pairs={{0,4},{5,1},{4,8},{9,5},{8,12},{13,9},{12,14},{15,13},{14,10},{11,... | collective-permute-start | bytes 786440 | tf_op jit(solution)/shard_map/ppermute | solution.py:103
  64.6 1.8 %collective-permute-done.13.refs_9_.refs_7_.refs_5_ = bf16[2,128,512]{2,1,0:T(8,128)(2,1)S(1)} collective-permute-done((bf16[2,128,512]{2,1,0:T(8,128)(2,1)}, bf16[2,128,512]{2,1,0:T(8,128)(2,1)S(1)}, u32[]{:S(2)}, u32[]{:S(2)}) %collective-permute-start.13) | collective-permute-done | bytes 262176 | tf_op jit(solution)/shard_map/ppermute | solution.py:103
  66.4 1.0 collective-permute-start.14
  68.0 1.3 %collective-permute-done.6.refs_8_.refs_6_.refs_4_ = bf16[2,128,512]{2,1,0:T(8,128)(2,1)S(1)} collective-permute-done((bf16[2,128,512]{2,1,0:T(8,128)(2,1)S(1)}, bf16[2,128,512]{2,1,0:T(8,128)(2,1)S(1)}, u32[]{:S(2)}, u32[]{:S(2)}) %collective-permute-start.6) | collective-permute-done | bytes 262176 | tf_op jit(solution)/shard_map/ppermute | solution.py:103
  69.2 1.8 %collective-permute-start.7 = (bf16[2,128,512]{2,1,0:T(8,128)(2,1)S(1)}, bf16[2,128,512]{2,1,0:T(8,128)(2,1)S(1)}, u32[]{:S(2)}, u32[]{:S(2)}) collective-permute-start(bf16[2,128,512]{2,1,0:T(8,128)(2,1)S(1)} %collective-permute-done.6.refs_8_.refs_6_.refs_4_), channel_id=1, source_target_pairs={{0,4},{5,1},{4,8},{9,5},{8,12},{13,9},{12,14},{15,13},{14,10},{11,... | collective-permute-start | bytes 786440 | tf_op jit(solution)/shard_map/ppermute | solution.py:103
  71.0 1.8 %collective-permute-done.14.refs_11_.refs_9_.refs_7_ = bf16[2,128,512]{2,1,0:T(8,128)(2,1)S(1)} collective-permute-done((bf16[2,128,512]{2,1,0:T(8,128)(2,1)S(1)}, bf16[2,128,512]{2,1,0:T(8,128)(2,1)S(1)}, u32[]{:S(2)}, u32[]{:S(2)}) %collective-permute-start.14) | collective-permute-done | bytes 262176 | tf_op jit(solution)/shard_map/ppermute | solution.py:103
  72.8 1.0 collective-permute-start.15
  74.3 1.3 %collective-permute-done.7.refs_10_.refs_8_.refs_6_ = bf16[2,128,512]{2,1,0:T(8,128)(2,1)S(1)} collective-permute-done((bf16[2,128,512]{2,1,0:T(8,128)(2,1)S(1)}, bf16[2,128,512]{2,1,0:T(8,128)(2,1)S(1)}, u32[]{:S(2)}, u32[]{:S(2)}) %collective-permute-start.7) | collective-permute-done | bytes 262176 | tf_op jit(solution)/shard_map/ppermute | solution.py:103
  75.6 1.8 %collective-permute-start.8 = (bf16[2,128,512]{2,1,0:T(8,128)(2,1)S(1)}, bf16[2,128,512]{2,1,0:T(8,128)(2,1)S(1)}, u32[]{:S(2)}, u32[]{:S(2)}) collective-permute-start(bf16[2,128,512]{2,1,0:T(8,128)(2,1)S(1)} %collective-permute-done.7.refs_10_.refs_8_.refs_6_), channel_id=1, source_target_pairs={{0,4},{5,1},{4,8},{9,5},{8,12},{13,9},{12,14},{15,13},{14,10},{11,... | collective-permute-start | bytes 786440 | tf_op jit(solution)/shard_map/ppermute | solution.py:103
  77.4 1.8 %collective-permute-done.15.refs_13_.refs_11_.refs_9_ = bf16[2,128,512]{2,1,0:T(8,128)(2,1)S(1)} collective-permute-done((bf16[2,128,512]{2,1,0:T(8,128)(2,1)S(1)}, bf16[2,128,512]{2,1,0:T(8,128)(2,1)S(1)}, u32[]{:S(2)}, u32[]{:S(2)}) %collective-permute-start.15) | collective-permute-done | bytes 262176 | tf_op jit(solution)/shard_map/ppermute | solution.py:103
  79.2 1.0 collective-permute-start.17
  80.7 1.3 %collective-permute-done.8.refs_12_.refs_10_.refs_8_ = bf16[2,128,512]{2,1,0:T(8,128)(2,1)S(1)} collective-permute-done((bf16[2,128,512]{2,1,0:T(8,128)(2,1)S(1)}, bf16[2,128,512]{2,1,0:T(8,128)(2,1)S(1)}, u32[]{:S(2)}, u32[]{:S(2)}) %collective-permute-start.8) | collective-permute-done | bytes 262176 | tf_op jit(solution)/shard_map/ppermute | solution.py:103
  82.0 0.5 collective-permute-start.31
  82.5 2.1 %shard_map.158 = (bf16[2,2,512,512]{3,2,1,0:T(8,128)(2,1)S(1)}, f32[2]{0:T(128)S(1)}) custom-call(s32[32]{0:T(128)S(1)} %copy-done.4, s32[32]{0:T(128)S(1)} %reshape.214.list_ref, s32[6]{0:T(128)S(1)} %stack.27.where_ref, bf16[16,2,32,512]{3,2,1,0:T(8,128)(2,1)S(1)} %all-to-all-done.refs_0_, bf16[16,2,32,512]{3,2,1,0:T(8,128)(2,1)S(1)} %collective-permute-done.9.refs_1_), custom_call_target="tpu_custom_call" | custom-call | flops 2000000000 | bytes 6000000 | tf_op jit(solution)/shard_map/pallas_call | solution.py:280
  84.6 0.9 collective-permute-done.17.refs_15_.refs_13_.refs_11_
  85.5 1.0 collective-permute-start.19
  86.6 2.3 %collective-permute-start.16 = (bf16[2,128,512]{2,1,0:T(8,128)(2,1)S(1)}, bf16[2,128,512]{2,1,0:T(8,128)(2,1)S(1)}, u32[]{:S(2)}, u32[]{:S(2)}) collective-permute-start(bf16[2,128,512]{2,1,0:T(8,128)(2,1)S(1)} %collective-permute-done.8.refs_12_.refs_10_.refs_8_), channel_id=1, source_target_pairs={{0,4},{5,1},{4,8},{9,5},{8,12},{13,9},{12,14},{15,13},{14,10},{11,... | collective-permute-start | bytes 786440 | tf_op jit(solution)/shard_map/ppermute | solution.py:103
  89.4 2.5 %collective-permute-done.19.refs_15_.refs_13_ = bf16[2,128,512]{2,1,0:T(8,128)(2,1)S(1)} collective-permute-done((bf16[2,128,512]{2,1,0:T(8,128)(2,1)S(1)}, bf16[2,128,512]{2,1,0:T(8,128)(2,1)S(1)}, u32[]{:S(2)}, u32[]{:S(2)}) %collective-permute-start.19) | collective-permute-done | bytes 262176 | tf_op jit(solution)/shard_map/ppermute | solution.py:103
  91.9 1.0 collective-permute-start.21
  92.9 1.8 %collective-permute-done.16.refs_14_.refs_12_.refs_10_ = bf16[2,128,512]{2,1,0:T(8,128)(2,1)S(1)} collective-permute-done((bf16[2,128,512]{2,1,0:T(8,128)(2,1)S(1)}, bf16[2,128,512]{2,1,0:T(8,128)(2,1)S(1)}, u32[]{:S(2)}, u32[]{:S(2)}) %collective-permute-start.16) | collective-permute-done | bytes 262176 | tf_op jit(solution)/shard_map/ppermute | solution.py:103
  94.7 1.0 collective-permute-start.18
  96.3 2.0 %collective-permute-done.21.refs_15_ = bf16[2,128,512]{2,1,0:T(8,128)(2,1)S(1)} collective-permute-done((bf16[2,128,512]{2,1,0:T(8,128)(2,1)S(1)}, bf16[2,128,512]{2,1,0:T(8,128)(2,1)S(1)}, u32[]{:S(2)}, u32[]{:S(2)}) %collective-permute-start.21) | collective-permute-done | bytes 262176 | tf_op jit(solution)/shard_map/ppermute | solution.py:103
  98.8 2.3 %collective-permute-done.18.refs_14_.refs_12_ = bf16[2,128,512]{2,1,0:T(8,128)(2,1)S(1)} collective-permute-done((bf16[2,128,512]{2,1,0:T(8,128)(2,1)S(1)}, bf16[2,128,512]{2,1,0:T(8,128)(2,1)S(1)}, u32[]{:S(2)}, u32[]{:S(2)}) %collective-permute-start.18) | collective-permute-done | bytes 262176 | tf_op jit(solution)/shard_map/ppermute | solution.py:103
  101.1 1.0 collective-permute-start.20
  102.2 5.8 %shard_map.159.refs_38_ = f32[2,512,512]{2,1,0:T(8,128)S(1)} custom-call(s32[6]{0:T(128)S(1)} %stack.27.where_ref, f32[2]{0:T(128)S(1)} %get-tuple-element.19.sigma_ref, bf16[2,128,512]{2,1,0:T(8,128)(2,1)S(1)} %bitcast.50, bf16[2,128,512]{2,1,0:T(8,128)(2,1)S(1)} %bitcast.47, bf16[2,128,512]{2,1,0:T(8,128)(2,1)} %bitcast_select_fusion.2.refs_2_.refs_0_, ...), custom_call_target="tpu_custom_call" | custom-call | flops 5000000000 | bytes 10000000 | tf_op jit(solution)/shard_map/pallas_call | solution.py:300
  108.0 2.0 %collective-permute-start.36 = (bf16[2,128,512]{2,1,0:T(8,128)(2,1)S(1)}, bf16[2,128,512]{2,1,0:T(8,128)(2,1)S(1)}, u32[]{:S(2)}, u32[]{:S(2)}) collective-permute-start(bf16[2,128,512]{2,1,0:T(8,128)(2,1)S(1)} %collective-permute-done.20.refs_14_), channel_id=1, source_target_pairs={{0,1},{1,0},{2,3},{3,2},{4,5},{5,4},{6,7},{7,6},{8,9},{9,8},{10,11... | collective-permute-start | bytes 786440 | tf_op jit(solution)/shard_map/ppermute | solution.py:104
  110.0 5.7 %shard_map.160.refs_38_ = f32[2,512,512]{2,1,0:T(8,128)S(1)} custom-call(s32[6]{0:T(128)S(1)} %stack.27.where_ref, f32[2]{0:T(128)S(1)} %get-tuple-element.19.sigma_ref, bf16[2,128,512]{2,1,0:T(8,128)(2,1)} %bitcast_select_fusion.2.refs_2_.refs_0_, bf16[2,128,512]{2,1,0:T(8,128)(2,1)} %bitcast_select_fusion.refs_3_.refs_1_, ...), custom_call_target="tpu_custom_call" | custom-call | flops 5000000000 | bytes 10000000 | tf_op jit(solution)/shard_map/pallas_call | solution.py:300
  115.8 6.7 %shard_map.161 = (f32[2]{0:T(128)}, f32[2]{0:T(128)}) custom-call(s32[6]{0:T(128)S(1)} %stack.27.where_ref, f32[2]{0:T(128)S(1)} %get-tuple-element.19.sigma_ref, bf16[2,128,512]{2,1,0:T(8,128)(2,1)S(1)} %copy-done.3, bf16[2,128,512]{2,1,0:T(8,128)(2,1)} %bitcast_select_fusion.1.refs_5_.refs_3_.refs_1_, ...), custom_call_target="tpu_custom_call" | custom-call | flops 5000000000 | bytes 10000000 | tf_op jit(solution)/shard_map/pallas_call | solution.py:300
  (84 shorter events, 6.4 us)
Async XLA Ops:
  4.3 13.3 %collective-permute-start = (bf16[2,131072]{1,0:T(2,128)(2,1)}, bf16[2,131072]{1,0:T(2,128)(2,1)}, u32[]{:S(2)}, u32[]{:S(2)}) collective-permute-start(bf16[2,131072]{1,0:T(2,128)(2,1)} %get-tuple-element.27), channel_id=1, source_target_pairs={{0,1},{1,0},{2,3},{3,2},{4,5},{5,4},{6,7},{7,6},{8,9},{9,8},{10,11... | collective-permute-start | bytes 1572872 | tf_op jit(solution)/shard_map/ppermute | solution.py:75
  4.7 12.8 %collective-permute-start.1 = (bf16[2,131072]{1,0:T(2,128)(2,1)}, bf16[2,131072]{1,0:T(2,128)(2,1)}, u32[]{:S(2)}, u32[]{:S(2)}) collective-permute-start(bf16[2,131072]{1,0:T(2,128)(2,1)} %get-tuple-element.28), channel_id=1, source_target_pairs={{0,1},{1,0},{2,3},{3,2},{4,5},{5,4},{6,7},{7,6},{8,9},{9,8},{10,11... | collective-permute-start | bytes 1572872 | tf_op jit(solution)/shard_map/ppermute | solution.py:75
  4.8 12.8 %collective-permute-start.2 = (bf16[2,131072]{1,0:T(2,128)(2,1)}, bf16[2,131072]{1,0:T(2,128)(2,1)}, u32[]{:S(2)}, u32[]{:S(2)}) collective-permute-start(bf16[2,131072]{1,0:T(2,128)(2,1)} %get-tuple-element.29), channel_id=1, source_target_pairs={{0,1},{1,0},{2,3},{3,2},{4,5},{5,4},{6,7},{7,6},{8,9},{9,8},{10,11... | collective-permute-start | bytes 1572872 | tf_op jit(solution)/shard_map/ppermute | solution.py:75
  9.5 46.0 %all-to-all-start = ((bf16[16,2,32,512]{3,2,1,0:T(8,128)(2,1)}), bf16[16,2,32,512]{3,2,1,0:T(8,128)(2,1)S(1)}, u32[]{:S(2)}, u32[]{:S(2)}) async-start(bf16[16,2,32,512]{3,2,1,0:T(8,128)(2,1)} %reshape.213), calls=%async_computation | async-start | bytes 2097152 | tf_op jit(solution)/shard_map/all_to_all | solution.py:136
  21.4 16.0 %collective-permute-start.10 = (bf16[2,128,512]{2,1,0:T(8,128)(2,1)S(1)}, bf16[2,128,512]{2,1,0:T(8,128)(2,1)S(1)}, u32[]{:S(2)}, u32[]{:S(2)}) collective-permute-start(bf16[2,128,512]{2,1,0:T(8,128)(2,1)S(1)} %bitcast.45), channel_id=1, source_target_pairs={{0,4},{5,1},{4,8},{9,5},{8,12},{13,9},{12,14},{15,13},{14,10},{11,... | collective-permute-start | bytes 786440 | tf_op jit(solution)/shard_map/ppermute | solution.py:103
  23.5 21.8 %collective-permute-start.3 = (bf16[2,128,512]{2,1,0:T(8,128)(2,1)S(1)}, bf16[2,128,512]{2,1,0:T(8,128)(2,1)S(1)}, u32[]{:S(2)}, u32[]{:S(2)}) collective-permute-start(bf16[2,128,512]{2,1,0:T(8,128)(2,1)S(1)} %bitcast.48), channel_id=1, source_target_pairs={{0,4},{5,1},{4,8},{9,5},{8,12},{13,9},{12,14},{15,13},{14,10},{11,... | collective-permute-start | bytes 786440 | tf_op jit(solution)/shard_map/ppermute | solution.py:103
  26.5 56.0 %copy-start.4 = (s32[32]{0:T(128)S(1)}, s32[32]{0:T(128)}, u32[]{:S(2)}) copy-start(s32[32]{0:T(128)} %cut_ref.1) | copy-start | bytes 388
  38.2 11.3 %collective-permute-start.11 = (bf16[2,128,512]{2,1,0:T(8,128)(2,1)}, bf16[2,128,512]{2,1,0:T(8,128)(2,1)}, u32[]{:S(2)}, u32[]{:S(2)}) collective-permute-start(bf16[2,128,512]{2,1,0:T(8,128)(2,1)} %bitcast_select_fusion.refs_3_.refs_1_), channel_id=1, source_target_pairs={{0,4},{5,1},{4,8},{9,5},{8,12},{13,9},{12,14},{15,13},{14,10},{11,... | collective-permute-start | bytes 786440 | tf_op jit(solution)/shard_map/ppermute | solution.py:103
  46.0 7.7 %collective-permute-start.4 = (bf16[2,128,512]{2,1,0:T(8,128)(2,1)}, bf16[2,128,512]{2,1,0:T(8,128)(2,1)}, u32[]{:S(2)}, u32[]{:S(2)}) collective-permute-start(bf16[2,128,512]{2,1,0:T(8,128)(2,1)} %bitcast_select_fusion.2.refs_2_.refs_0_), channel_id=1, source_target_pairs={{0,4},{5,1},{4,8},{9,5},{8,12},{13,9},{12,14},{15,13},{14,10},{11,... | collective-permute-start | bytes 786440 | tf_op jit(solution)/shard_map/ppermute | solution.py:103
  51.3 8.5 %collective-permute-start.12 = (bf16[2,128,512]{2,1,0:T(8,128)(2,1)}, bf16[2,128,512]{2,1,0:T(8,128)(2,1)}, u32[]{:S(2)}, u32[]{:S(2)}) collective-permute-start(bf16[2,128,512]{2,1,0:T(8,128)(2,1)} %bitcast_select_fusion.1.refs_5_.refs_3_.refs_1_), channel_id=1, source_target_pairs={{0,4},{5,1},{4,8},{9,5},{8,12},{13,9},{12,14},{15,13},{14,10},{11,... | collective-permute-start | bytes 786440 | tf_op jit(solution)/shard_map/ppermute | solution.py:103
  55.5 46.7 %copy-start.2 = (bf16[1,2,128,512]{3,2,1,0:T(8,128)(2,1)S(1)}, bf16[1,2,128,512]{3,2,1,0:T(8,128)(2,1)}, u32[]{:S(2)}) copy-start(bf16[1,2,128,512]{3,2,1,0:T(8,128)(2,1)} %copy-done.1) | copy-start | bytes 786436
  55.5 46.7 %copy-start.3 = (bf16[2,128,512]{2,1,0:T(8,128)(2,1)S(1)}, bf16[2,128,512]{2,1,0:T(8,128)(2,1)}, u32[]{:S(2)}) copy-start(bf16[2,128,512]{2,1,0:T(8,128)(2,1)} %bitcast_select_fusion.3.refs_4_.refs_2_.refs_0_) | copy-start | bytes 786436
  55.5 46.7 %copy-start.5 = (f32[4,2,128,512]{3,2,1,0:T(8,128)S(1)}, f32[4,2,128,512]{3,2,1,0:T(8,128)}, u32[]{:S(2)}) copy-start(f32[4,2,128,512]{3,2,1,0:T(8,128)} %constant.174.clone.refs_37_) | copy-start | bytes 6291460
  55.5 46.7 %copy-start.6 = (bf16[4,512,256]{2,1,0:T(8,128)(2,1)S(1)}, bf16[4,512,256]{2,1,0:T(8,128)(2,1)}, u32[]{:S(2)}) copy-start(bf16[4,512,256]{2,1,0:T(8,128)(2,1)} %constant.179.refs_36_) | copy-start | bytes 3145732
  55.5 7.1 %collective-permute-start.5 = (bf16[2,128,512]{2,1,0:T(8,128)(2,1)}, bf16[2,128,512]{2,1,0:T(8,128)(2,1)S(1)}, u32[]{:S(2)}, u32[]{:S(2)}) collective-permute-start(bf16[2,128,512]{2,1,0:T(8,128)(2,1)} %bitcast_select_fusion.3.refs_4_.refs_2_.refs_0_), channel_id=1, source_target_pairs={{0,4},{5,1},{4,8},{9,5},{8,12},{13,9},{12,14},{15,13},{14,10},{11,... | collective-permute-start | bytes 786440 | tf_op jit(solution)/shard_map/ppermute | solution.py:103
  58.1 23.9 %collective-permute-start.9 = (bf16[16,2,32,512]{3,2,1,0:T(8,128)(2,1)S(1)}, bf16[16,2,32,512]{3,2,1,0:T(8,128)(2,1)S(1)}, u32[]{:S(2)}, u32[]{:S(2)}) collective-permute-start(bf16[16,2,32,512]{3,2,1,0:T(8,128)(2,1)S(1)} %all-to-all-done.refs_0_), channel_id=1, source_target_pairs={{0,16},{16,0},{1,17},{17,1},{2,18},{18,2},{3,19},{19,3},{4,20},{20... | collective-permute-start | bytes 3145736 | tf_op jit(solution)/shard_map/ppermute | solution.py:142
  59.8 6.6 %collective-permute-start.13 = (bf16[2,128,512]{2,1,0:T(8,128)(2,1)}, bf16[2,128,512]{2,1,0:T(8,128)(2,1)S(1)}, u32[]{:S(2)}, u32[]{:S(2)}) collective-permute-start(bf16[2,128,512]{2,1,0:T(8,128)(2,1)} %collective-permute-done.12.refs_7_.refs_5_.refs_3_), channel_id=1, source_target_pairs={{0,4},{5,1},{4,8},{9,5},{8,12},{13,9},{12,14},{15,13},{14,10},{11,... | collective-permute-start | bytes 786440 | tf_op jit(solution)/shard_map/ppermute | solution.py:103
  60.7 6.8 %collective-permute-start.40 = (bf16[2,128,512]{2,1,0:T(8,128)(2,1)}, bf16[2,128,512]{2,1,0:T(8,128)(2,1)S(1)}, u32[]{:S(2)}, u32[]{:S(2)}) collective-permute-start(bf16[2,128,512]{2,1,0:T(8,128)(2,1)} %bitcast.49), channel_id=1, source_target_pairs={{0,1},{1,0},{2,3},{3,2},{4,5},{5,4},{6,7},{7,6},{8,9},{9,8},{10,11... | collective-permute-start | bytes 786440 | tf_op jit(solution)/shard_map/ppermute | solution.py:104
  60.7 6.8 %collective-permute-start.41 = (bf16[2,128,512]{2,1,0:T(8,128)(2,1)S(1)}, bf16[2,128,512]{2,1,0:T(8,128)(2,1)S(1)}, u32[]{:S(2)}, u32[]{:S(2)}) collective-permute-start(bf16[2,128,512]{2,1,0:T(8,128)(2,1)S(1)} %bitcast.46), channel_id=1, source_target_pairs={{0,1},{1,0},{2,3},{3,2},{4,5},{5,4},{6,7},{7,6},{8,9},{9,8},{10,11... | collective-permute-start | bytes 786440 | tf_op jit(solution)/shard_map/ppermute | solution.py:104
  62.6 6.6 %collective-permute-start.6 = (bf16[2,128,512]{2,1,0:T(8,128)(2,1)S(1)}, bf16[2,128,512]{2,1,0:T(8,128)(2,1)S(1)}, u32[]{:S(2)}, u32[]{:S(2)}) collective-permute-start(bf16[2,128,512]{2,1,0:T(8,128)(2,1)S(1)} %collective-permute-done.5.refs_6_.refs_4_.refs_2_), channel_id=1, source_target_pairs={{0,4},{5,1},{4,8},{9,5},{8,12},{13,9},{12,14},{15,13},{14,10},{11,... | collective-permute-start | bytes 786440 | tf_op jit(solution)/shard_map/ppermute | solution.py:103
  66.4 6.4 %collective-permute-start.14 = (bf16[2,128,512]{2,1,0:T(8,128)(2,1)S(1)}, bf16[2,128,512]{2,1,0:T(8,128)(2,1)S(1)}, u32[]{:S(2)}, u32[]{:S(2)}) collective-permute-start(bf16[2,128,512]{2,1,0:T(8,128)(2,1)S(1)} %collective-permute-done.13.refs_9_.refs_7_.refs_5_), channel_id=1, source_target_pairs={{0,4},{5,1},{4,8},{9,5},{8,12},{13,9},{12,14},{15,13},{14,10},{11,... | collective-permute-start | bytes 786440 | tf_op jit(solution)/shard_map/ppermute | solution.py:103
  67.5 6.4 %collective-permute-start.39 = (bf16[2,128,512]{2,1,0:T(8,128)(2,1)}, bf16[2,128,512]{2,1,0:T(8,128)(2,1)S(1)}, u32[]{:S(2)}, u32[]{:S(2)}) collective-permute-start(bf16[2,128,512]{2,1,0:T(8,128)(2,1)} %bitcast_select_fusion.refs_3_.refs_1_), channel_id=1, source_target_pairs={{0,1},{1,0},{2,3},{3,2},{4,5},{5,4},{6,7},{7,6},{8,9},{9,8},{10,11... | collective-permute-start | bytes 786440 | tf_op jit(solution)/shard_map/ppermute | solution.py:104
  67.5 6.4 %collective-permute-start.38 = (bf16[2,128,512]{2,1,0:T(8,128)(2,1)}, bf16[2,128,512]{2,1,0:T(8,128)(2,1)S(1)}, u32[]{:S(2)}, u32[]{:S(2)}) collective-permute-start(bf16[2,128,512]{2,1,0:T(8,128)(2,1)} %bitcast_select_fusion.2.refs_2_.refs_0_), channel_id=1, source_target_pairs={{0,1},{1,0},{2,3},{3,2},{4,5},{5,4},{6,7},{7,6},{8,9},{9,8},{10,11... | collective-permute-start | bytes 786440 | tf_op jit(solution)/shard_map/ppermute | solution.py:104
  69.2 6.4 %collective-permute-start.7 = (bf16[2,128,512]{2,1,0:T(8,128)(2,1)S(1)}, bf16[2,128,512]{2,1,0:T(8,128)(2,1)S(1)}, u32[]{:S(2)}, u32[]{:S(2)}) collective-permute-start(bf16[2,128,512]{2,1,0:T(8,128)(2,1)S(1)} %collective-permute-done.6.refs_8_.refs_6_.refs_4_), channel_id=1, source_target_pairs={{0,4},{5,1},{4,8},{9,5},{8,12},{13,9},{12,14},{15,13},{14,10},{11,... | collective-permute-start | bytes 786440 | tf_op jit(solution)/shard_map/ppermute | solution.py:103
  72.8 6.4 %collective-permute-start.15 = (bf16[2,128,512]{2,1,0:T(8,128)(2,1)S(1)}, bf16[2,128,512]{2,1,0:T(8,128)(2,1)S(1)}, u32[]{:S(2)}, u32[]{:S(2)}) collective-permute-start(bf16[2,128,512]{2,1,0:T(8,128)(2,1)S(1)} %collective-permute-done.14.refs_11_.refs_9_.refs_7_), channel_id=1, source_target_pairs={{0,4},{5,1},{4,8},{9,5},{8,12},{13,9},{12,14},{15,13},{14,10},{11,... | collective-permute-start | bytes 786440 | tf_op jit(solution)/shard_map/ppermute | solution.py:103
  73.8 6.4 %collective-permute-start.23 = (bf16[2,128,512]{2,1,0:T(8,128)(2,1)}, bf16[2,128,512]{2,1,0:T(8,128)(2,1)S(1)}, u32[]{:S(2)}, u32[]{:S(2)}) collective-permute-start(bf16[2,128,512]{2,1,0:T(8,128)(2,1)} %bitcast_select_fusion.1.refs_5_.refs_3_.refs_1_), channel_id=1, source_target_pairs={{0,1},{1,0},{2,3},{3,2},{4,5},{5,4},{6,7},{7,6},{8,9},{9,8},{10,11... | collective-permute-start | bytes 786440 | tf_op jit(solution)/shard_map/ppermute | solution.py:104
  73.8 6.4 %collective-permute-start.25 = (bf16[2,128,512]{2,1,0:T(8,128)(2,1)}, bf16[2,128,512]{2,1,0:T(8,128)(2,1)S(1)}, u32[]{:S(2)}, u32[]{:S(2)}) collective-permute-start(bf16[2,128,512]{2,1,0:T(8,128)(2,1)} %collective-permute-done.12.refs_7_.refs_5_.refs_3_), channel_id=1, source_target_pairs={{0,1},{1,0},{2,3},{3,2},{4,5},{5,4},{6,7},{7,6},{8,9},{9,8},{10,11... | collective-permute-start | bytes 786440 | tf_op jit(solution)/shard_map/ppermute | solution.py:104
  75.6 6.4 %collective-permute-start.8 = (bf16[2,128,512]{2,1,0:T(8,128)(2,1)S(1)}, bf16[2,128,512]{2,1,0:T(8,128)(2,1)S(1)}, u32[]{:S(2)}, u32[]{:S(2)}) collective-permute-start(bf16[2,128,512]{2,1,0:T(8,128)(2,1)S(1)} %collective-permute-done.7.refs_10_.refs_8_.refs_6_), channel_id=1, source_target_pairs={{0,4},{5,1},{4,8},{9,5},{8,12},{13,9},{12,14},{15,13},{14,10},{11,... | collective-permute-start | bytes 786440 | tf_op jit(solution)/shard_map/ppermute | solution.py:103
  79.2 6.4 %collective-permute-start.17 = (bf16[2,128,512]{2,1,0:T(8,128)(2,1)S(1)}, bf16[2,128,512]{2,1,0:T(8,128)(2,1)S(1)}, u32[]{:S(2)}, u32[]{:S(2)}) collective-permute-start(bf16[2,128,512]{2,1,0:T(8,128)(2,1)S(1)} %collective-permute-done.15.refs_13_.refs_11_.refs_9_), channel_id=1, source_target_pairs={{0,4},{5,1},{4,8},{9,5},{8,12},{13,9},{12,14},{15,13},{14,10},{11,... | collective-permute-start | bytes 786440 | tf_op jit(solution)/shard_map/ppermute | solution.py:103
  80.2 6.4 %collective-permute-start.27 = (bf16[2,128,512]{2,1,0:T(8,128)(2,1)S(1)}, bf16[2,128,512]{2,1,0:T(8,128)(2,1)S(1)}, u32[]{:S(2)}, u32[]{:S(2)}) collective-permute-start(bf16[2,128,512]{2,1,0:T(8,128)(2,1)S(1)} %collective-permute-done.13.refs_9_.refs_7_.refs_5_), channel_id=1, source_target_pairs={{0,1},{1,0},{2,3},{3,2},{4,5},{5,4},{6,7},{7,6},{8,9},{9,8},{10,11... | collective-permute-start | bytes 786440 | tf_op jit(solution)/shard_map/ppermute | solution.py:104
  80.2 6.4 %collective-permute-start.29 = (bf16[2,128,512]{2,1,0:T(8,128)(2,1)S(1)}, bf16[2,128,512]{2,1,0:T(8,128)(2,1)S(1)}, u32[]{:S(2)}, u32[]{:S(2)}) collective-permute-start(bf16[2,128,512]{2,1,0:T(8,128)(2,1)S(1)} %collective-permute-done.14.refs_11_.refs_9_.refs_7_), channel_id=1, source_target_pairs={{0,1},{1,0},{2,3},{3,2},{4,5},{5,4},{6,7},{7,6},{8,9},{9,8},{10,11... | collective-permute-start | bytes 786440 | tf_op jit(solution)/shard_map/ppermute | solution.py:104
  82.0 6.9 %collective-permute-start.22 = (bf16[2,128,512]{2,1,0:T(8,128)(2,1)}, bf16[2,128,512]{2,1,0:T(8,128)(2,1)S(1)}, u32[]{:S(2)}, u32[]{:S(2)}) collective-permute-start(bf16[2,128,512]{2,1,0:T(8,128)(2,1)} %bitcast_select_fusion.3.refs_4_.refs_2_.refs_0_), channel_id=1, source_target_pairs={{0,1},{1,0},{2,3},{3,2},{4,5},{5,4},{6,7},{7,6},{8,9},{9,8},{10,11... | collective-permute-start | bytes 786440 | tf_op jit(solution)/shard_map/ppermute | solution.py:104
  82.0 6.9 %collective-permute-start.31 = (bf16[2,128,512]{2,1,0:T(8,128)(2,1)S(1)}, bf16[2,128,512]{2,1,0:T(8,128)(2,1)S(1)}, u32[]{:S(2)}, u32[]{:S(2)}) collective-permute-start(bf16[2,128,512]{2,1,0:T(8,128)(2,1)S(1)} %collective-permute-done.15.refs_13_.refs_11_.refs_9_), channel_id=1, source_target_pairs={{0,1},{1,0},{2,3},{3,2},{4,5},{5,4},{6,7},{7,6},{8,9},{9,8},{10,11... | collective-permute-start | bytes 786440 | tf_op jit(solution)/shard_map/ppermute | solution.py:104
  85.5 6.4 %collective-permute-start.19 = (bf16[2,128,512]{2,1,0:T(8,128)(2,1)S(1)}, bf16[2,128,512]{2,1,0:T(8,128)(2,1)S(1)}, u32[]{:S(2)}, u32[]{:S(2)}) collective-permute-start(bf16[2,128,512]{2,1,0:T(8,128)(2,1)S(1)} %collective-permute-done.17.refs_15_.refs_13_.refs_11_), channel_id=1, source_target_pairs={{0,4},{5,1},{4,8},{9,5},{8,12},{13,9},{12,14},{15,13},{14,10},{11,... | collective-permute-start | bytes 786440 | tf_op jit(solution)/shard_map/ppermute | solution.py:103
  86.6 6.4 %collective-permute-start.24 = (bf16[2,128,512]{2,1,0:T(8,128)(2,1)S(1)}, bf16[2,128,512]{2,1,0:T(8,128)(2,1)S(1)}, u32[]{:S(2)}, u32[]{:S(2)}) collective-permute-start(bf16[2,128,512]{2,1,0:T(8,128)(2,1)S(1)} %collective-permute-done.5.refs_6_.refs_4_.refs_2_), channel_id=1, source_target_pairs={{0,1},{1,0},{2,3},{3,2},{4,5},{5,4},{6,7},{7,6},{8,9},{9,8},{10,11... | collective-permute-start | bytes 786440 | tf_op jit(solution)/shard_map/ppermute | solution.py:104
  86.6 8.1 %collective-permute-start.16 = (bf16[2,128,512]{2,1,0:T(8,128)(2,1)S(1)}, bf16[2,128,512]{2,1,0:T(8,128)(2,1)S(1)}, u32[]{:S(2)}, u32[]{:S(2)}) collective-permute-start(bf16[2,128,512]{2,1,0:T(8,128)(2,1)S(1)} %collective-permute-done.8.refs_12_.refs_10_.refs_8_), channel_id=1, source_target_pairs={{0,4},{5,1},{4,8},{9,5},{8,12},{13,9},{12,14},{15,13},{14,10},{11,... | collective-permute-start | bytes 786440 | tf_op jit(solution)/shard_map/ppermute | solution.py:103
  88.9 6.9 %collective-permute-start.33 = (bf16[2,128,512]{2,1,0:T(8,128)(2,1)S(1)}, bf16[2,128,512]{2,1,0:T(8,128)(2,1)S(1)}, u32[]{:S(2)}, u32[]{:S(2)}) collective-permute-start(bf16[2,128,512]{2,1,0:T(8,128)(2,1)S(1)} %collective-permute-done.17.refs_15_.refs_13_.refs_11_), channel_id=1, source_target_pairs={{0,1},{1,0},{2,3},{3,2},{4,5},{5,4},{6,7},{7,6},{8,9},{9,8},{10,11... | collective-permute-start | bytes 786440 | tf_op jit(solution)/shard_map/ppermute | solution.py:104
  88.9 6.9 %collective-permute-start.26 = (bf16[2,128,512]{2,1,0:T(8,128)(2,1)S(1)}, bf16[2,128,512]{2,1,0:T(8,128)(2,1)S(1)}, u32[]{:S(2)}, u32[]{:S(2)}) collective-permute-start(bf16[2,128,512]{2,1,0:T(8,128)(2,1)S(1)} %collective-permute-done.6.refs_8_.refs_6_.refs_4_), channel_id=1, source_target_pairs={{0,1},{1,0},{2,3},{3,2},{4,5},{5,4},{6,7},{7,6},{8,9},{9,8},{10,11... | collective-permute-start | bytes 786440 | tf_op jit(solution)/shard_map/ppermute | solution.py:104
  91.9 6.4 %collective-permute-start.21 = (bf16[2,128,512]{2,1,0:T(8,128)(2,1)S(1)}, bf16[2,128,512]{2,1,0:T(8,128)(2,1)S(1)}, u32[]{:S(2)}, u32[]{:S(2)}) collective-permute-start(bf16[2,128,512]{2,1,0:T(8,128)(2,1)S(1)} %collective-permute-done.19.refs_15_.refs_13_), channel_id=1, source_target_pairs={{0,4},{5,1},{4,8},{9,5},{8,12},{13,9},{12,14},{15,13},{14,10},{11,... | collective-permute-start | bytes 786440 | tf_op jit(solution)/shard_map/ppermute | solution.py:103
  92.9 5.3 %collective-permute-start.28 = (bf16[2,128,512]{2,1,0:T(8,128)(2,1)S(1)}, bf16[2,128,512]{2,1,0:T(8,128)(2,1)S(1)}, u32[]{:S(2)}, u32[]{:S(2)}) collective-permute-start(bf16[2,128,512]{2,1,0:T(8,128)(2,1)S(1)} %collective-permute-done.7.refs_10_.refs_8_.refs_6_), channel_id=1, source_target_pairs={{0,1},{1,0},{2,3},{3,2},{4,5},{5,4},{6,7},{7,6},{8,9},{9,8},{10,11... | collective-permute-start | bytes 786440 | tf_op jit(solution)/shard_map/ppermute | solution.py:104
  94.7 6.4 %collective-permute-start.18 = (bf16[2,128,512]{2,1,0:T(8,128)(2,1)S(1)}, bf16[2,128,512]{2,1,0:T(8,128)(2,1)S(1)}, u32[]{:S(2)}, u32[]{:S(2)}) collective-permute-start(bf16[2,128,512]{2,1,0:T(8,128)(2,1)S(1)} %collective-permute-done.16.refs_14_.refs_12_.refs_10_), channel_id=1, source_target_pairs={{0,4},{5,1},{4,8},{9,5},{8,12},{13,9},{12,14},{15,13},{14,10},{11,... | collective-permute-start | bytes 786440 | tf_op jit(solution)/shard_map/ppermute | solution.py:103
  95.8 5.3 %collective-permute-start.30 = (bf16[2,128,512]{2,1,0:T(8,128)(2,1)S(1)}, bf16[2,128,512]{2,1,0:T(8,128)(2,1)S(1)}, u32[]{:S(2)}, u32[]{:S(2)}) collective-permute-start(bf16[2,128,512]{2,1,0:T(8,128)(2,1)S(1)} %collective-permute-done.8.refs_12_.refs_10_.refs_8_), channel_id=1, source_target_pairs={{0,1},{1,0},{2,3},{3,2},{4,5},{5,4},{6,7},{7,6},{8,9},{9,8},{10,11... | collective-permute-start | bytes 786440 | tf_op jit(solution)/shard_map/ppermute | solution.py:104
  95.8 6.4 %collective-permute-start.32 = (bf16[2,128,512]{2,1,0:T(8,128)(2,1)S(1)}, bf16[2,128,512]{2,1,0:T(8,128)(2,1)S(1)}, u32[]{:S(2)}, u32[]{:S(2)}) collective-permute-start(bf16[2,128,512]{2,1,0:T(8,128)(2,1)S(1)} %collective-permute-done.16.refs_14_.refs_12_.refs_10_), channel_id=1, source_target_pairs={{0,1},{1,0},{2,3},{3,2},{4,5},{5,4},{6,7},{7,6},{8,9},{9,8},{10,11... | collective-permute-start | bytes 786440 | tf_op jit(solution)/shard_map/ppermute | solution.py:104
  98.3 11.7 %collective-permute-start.35 = (bf16[2,128,512]{2,1,0:T(8,128)(2,1)S(1)}, bf16[2,128,512]{2,1,0:T(8,128)(2,1)S(1)}, u32[]{:S(2)}, u32[]{:S(2)}) collective-permute-start(bf16[2,128,512]{2,1,0:T(8,128)(2,1)S(1)} %collective-permute-done.19.refs_15_.refs_13_), channel_id=1, source_target_pairs={{0,1},{1,0},{2,3},{3,2},{4,5},{5,4},{6,7},{7,6},{8,9},{9,8},{10,11... | collective-permute-start | bytes 786440 | tf_op jit(solution)/shard_map/ppermute | solution.py:104
  98.3 17.5 %collective-permute-start.37 = (bf16[2,128,512]{2,1,0:T(8,128)(2,1)S(1)}, bf16[2,128,512]{2,1,0:T(8,128)(2,1)S(1)}, u32[]{:S(2)}, u32[]{:S(2)}) collective-permute-start(bf16[2,128,512]{2,1,0:T(8,128)(2,1)S(1)} %collective-permute-done.21.refs_15_), channel_id=1, source_target_pairs={{0,1},{1,0},{2,3},{3,2},{4,5},{5,4},{6,7},{7,6},{8,9},{9,8},{10,11... | collective-permute-start | bytes 786440 | tf_op jit(solution)/shard_map/ppermute | solution.py:104
  101.1 8.9 %collective-permute-start.34 = (bf16[2,128,512]{2,1,0:T(8,128)(2,1)S(1)}, bf16[2,128,512]{2,1,0:T(8,128)(2,1)S(1)}, u32[]{:S(2)}, u32[]{:S(2)}) collective-permute-start(bf16[2,128,512]{2,1,0:T(8,128)(2,1)S(1)} %collective-permute-done.18.refs_14_.refs_12_), channel_id=1, source_target_pairs={{0,1},{1,0},{2,3},{3,2},{4,5},{5,4},{6,7},{7,6},{8,9},{9,8},{10,11... | collective-permute-start | bytes 786440 | tf_op jit(solution)/shard_map/ppermute | solution.py:104
  101.1 6.9 %collective-permute-start.20 = (bf16[2,128,512]{2,1,0:T(8,128)(2,1)S(1)}, bf16[2,128,512]{2,1,0:T(8,128)(2,1)S(1)}, u32[]{:S(2)}, u32[]{:S(2)}) collective-permute-start(bf16[2,128,512]{2,1,0:T(8,128)(2,1)S(1)} %collective-permute-done.18.refs_14_.refs_12_), channel_id=1, source_target_pairs={{0,4},{5,1},{4,8},{9,5},{8,12},{13,9},{12,14},{15,13},{14,10},{11,... | collective-permute-start | bytes 786440 | tf_op jit(solution)/shard_map/ppermute | solution.py:103
  108.0 7.8 %collective-permute-start.36 = (bf16[2,128,512]{2,1,0:T(8,128)(2,1)S(1)}, bf16[2,128,512]{2,1,0:T(8,128)(2,1)S(1)}, u32[]{:S(2)}, u32[]{:S(2)}) collective-permute-start(bf16[2,128,512]{2,1,0:T(8,128)(2,1)S(1)} %collective-permute-done.20.refs_14_), channel_id=1, source_target_pairs={{0,1},{1,0},{2,3},{3,2},{4,5},{5,4},{6,7},{7,6},{8,9},{9,8},{10,11... | collective-permute-start | bytes 786440 | tf_op jit(solution)/shard_map/ppermute | solution.py:104
  (5 other events, 79.1 us)

commit v16 on v15

--- a/solution.py
+++ b/solution.py
@@ -21,7 +21,7 @@
 LAG = 2
 TEMPLATE_SLOT = 4
 MASKED_SLOT = 12
-VMEM_LIMIT = 24 * 1024 * 1024
+VMEM_LIMIT = 16 * 1024 * 1024
 
 
 two_pi = 6.283185307179586

time: 123 us -> 124 us (level)
  transfers between devices with their start and end apart: 43 -> 43, of which waited for: 15 -> 15; matrix products, arithmetic and copies ran while one was open for 13% -> 12% of each run, Pallas kernels for 11% -> 11%
where the time goes in v16:
time: 124 us; the launch traced here: 123 us
  starting transfers between devices  49.7 us (40%)
  waiting for transfers between devices  31.8 us (26%)
  Pallas kernels  20.3 us (16%)
  local copies, waits for them, and re-layouts  10.2 us (8%)
  other arithmetic  8.6 us (7%)
  between operations  1.97 us (2%)
    ppermute x18, starting transfers between devices, spread(): arrived.append(lax.ppermute(here, 'tpl', along))  34.1 us
    ppermute x18, waiting for transfers between devices, spread(): arrived.append(lax.ppermute(here, 'tpl', along))  31.7 us
    pallas_call x3, Pallas kernels, detector(): pl.pallas_call(functools.partial(detector_kernel, det, chips), out_shape=...  18.2 us
    all_to_all x1, starting transfers between devices, exchange(): return lax.all_to_all(block, 'tpl', split_axis=0, concat_axis=0, tiled=True)  7.05 us
    ppermute x20, starting transfers between devices, spread(): shared = [lax.ppermute(here, 'tpl', to_partner()) for here in sent]  6.1 us
    select_n x4, other arithmetic, spread(): here = jnp.where(on_owner_chip, chunks[slot], arrived[slot - LAG])  5.03 us
    squeeze x1, local copies, waits for them, and re-layouts, half_chunks(): lax.dynamic_slice(strain_slots, (0, det, 0, which * half), (1, 1, 2, half))  3.58 us
    select_n x1, other arithmetic, half_chunks(): first = jnp.where(core == owner % CORES, side(core), got)  2.99 us
  transfers between devices with their start and end apart: 43, of which 15 were waited for; matrix products, arithmetic and copies ran while one was open for 12% of the time, Pallas kernels for 11%

profile of v16, /device:TPU:0, one launch (start us, length us, event | category | flops | bytes accessed | tf_op | source)
XLA Modules:
  0.0 122.6 jit_solution(10183979977601756591)
XLA Ops:
  0.7 3.6 %dynamic-slice_bitcast_fusion.2 = (bf16[2,131072]{1,0:T(2,128)(2,1)}, bf16[2,131072]{1,0:T(2,128)(2,1)}, bf16[2,131072]{1,0:T(2,128)(2,1)}) fusion(bf16[1,3,2,262144]{3,2,1,0:T(2,128)(2,1)} %param.15, s32[]{:T(128)S(6)} %select_n.186), kind=kLoop, calls=%fused_computation.6 | loop fusion | bytes 3145732 | tf_op jit(solution)/shard_map/squeeze | solution.py:74
  5.3 2.7 %gather_fusion = bf16[16,2,16384]{2,1,0:T(2,128)(2,1)S(1)} fusion(bf16[32,2,16384]{2,1,0:T(2,128)(2,1)S(1)} %copy-done, s32[1024]{0:T(1024)S(1)} %pad_clamp_fusion), kind=kCustom, calls=%fused_computation | custom fusion | bytes 2097216 | tf_op jit(solution)/shard_map/gather | solution.py:127
  7.9 1.5 %reshape.213 = bf16[16,2,32,512]{3,2,1,0:T(8,128)(2,1)} reshape(bf16[16,2,16384]{2,1,0:T(2,128)(2,1)S(1)} %gather_fusion) | data formatting | bytes 2097152 | tf_op jit(solution)/shard_map/reshape | solution.py:128
  9.5 7.0 %all-to-all-start = ((bf16[16,2,32,512]{3,2,1,0:T(8,128)(2,1)}), bf16[16,2,32,512]{3,2,1,0:T(8,128)(2,1)S(1)}, u32[]{:S(2)}, u32[]{:S(2)}) async-start(bf16[16,2,32,512]{3,2,1,0:T(8,128)(2,1)} %reshape.213), calls=%async_computation | async-start | bytes 2097152 | tf_op jit(solution)/shard_map/all_to_all | solution.py:136
  17.6 3.0 %broadcast_select_fusion.2 = (bf16[2,131072]{1,0:T(2,128)(2,1)S(1)}, bf16[2,131072]{1,0:T(2,128)(2,1)S(1)}, bf16[2,131072]{1,0:T(2,128)(2,1)S(1)}) fusion(bf16[2,131072]{1,0:T(2,128)(2,1)} %collective-permute-done, pred[]{:T(512)S(6)} %eq.43, bf16[1,3,2,262144]{3,2,1,0:T(2,128)(2,1)} %param.15, s32[]{:T(128)S(6)} %select_n.185, ...), kind=kLoop, calls=%fused_computation.3 | loop fusion | flops 786432 | bytes 4718597 | tf_op jit(solution)/shard_map/jit(_where)/select_n | solution.py:76
  21.0 2.0 %collective-permute-start.10 = (bf16[2,128,512]{2,1,0:T(8,128)(2,1)S(1)}, bf16[2,128,512]{2,1,0:T(8,128)(2,1)S(1)}, u32[]{:S(2)}, u32[]{:S(2)}) collective-permute-start(bf16[2,128,512]{2,1,0:T(8,128)(2,1)S(1)} %bitcast.45), channel_id=1, source_target_pairs={{0,4},{5,1},{4,8},{9,5},{8,12},{13,9},{12,14},{15,13},{14,10},{11,... | collective-permute-start | bytes 786440 | tf_op jit(solution)/shard_map/ppermute | solution.py:103
  23.0 1.5 %collective-permute-start.3 = (bf16[2,128,512]{2,1,0:T(8,128)(2,1)S(1)}, bf16[2,128,512]{2,1,0:T(8,128)(2,1)S(1)}, u32[]{:S(2)}, u32[]{:S(2)}) collective-permute-start(bf16[2,128,512]{2,1,0:T(8,128)(2,1)S(1)} %bitcast.48), channel_id=1, source_target_pairs={{0,4},{5,1},{4,8},{9,5},{8,12},{13,9},{12,14},{15,13},{14,10},{11,... | collective-permute-start | bytes 786440 | tf_op jit(solution)/shard_map/ppermute | solution.py:103
  24.5 1.5 %fusion.12 = (bf16[2,65536]{1,0:T(2,128)(2,1)}, bf16[2,65536]{1,0:T(2,128)(2,1)}, bf16[2,65536]{1,0:T(2,128)(2,1)S(1)}, bf16[2,65536]{1,0:T(2,128)(2,1)S(1)}) fusion(bf16[2,131072]{1,0:T(2,128)(2,1)S(1)} %get-tuple-element.24, bf16[2,131072]{1,0:T(2,128)(2,1)S(1)} %get-tuple-element.25), kind=kLoop, calls=%fused_computation.37 | loop fusion | bytes 2097152 | tf_op jit(solution)/shard_map/slice | solution.py:77
  26.0 11.4 %collective-permute-done.10 = bf16[2,128,512]{2,1,0:T(8,128)(2,1)S(1)} collective-permute-done((bf16[2,128,512]{2,1,0:T(8,128)(2,1)S(1)}, bf16[2,128,512]{2,1,0:T(8,128)(2,1)S(1)}, u32[]{:S(2)}, u32[]{:S(2)}) %collective-permute-start.10) | collective-permute-done | bytes 262176 | tf_op jit(solution)/shard_map/ppermute | solution.py:103
  37.4 0.7 bitcast_select_fusion.refs_3_.refs_1_
  38.2 7.1 %collective-permute-start.11 = (bf16[2,128,512]{2,1,0:T(8,128)(2,1)}, bf16[2,128,512]{2,1,0:T(8,128)(2,1)}, u32[]{:S(2)}, u32[]{:S(2)}) collective-permute-start(bf16[2,128,512]{2,1,0:T(8,128)(2,1)} %bitcast_select_fusion.refs_3_.refs_1_), channel_id=1, source_target_pairs={{0,4},{5,1},{4,8},{9,5},{8,12},{13,9},{12,14},{15,13},{14,10},{11,... | collective-permute-start | bytes 786440 | tf_op jit(solution)/shard_map/ppermute | solution.py:103
  45.3 0.7 bitcast_select_fusion.2.refs_2_.refs_0_
  46.0 2.5 %collective-permute-start.4 = (bf16[2,128,512]{2,1,0:T(8,128)(2,1)}, bf16[2,128,512]{2,1,0:T(8,128)(2,1)}, u32[]{:S(2)}, u32[]{:S(2)}) collective-permute-start(bf16[2,128,512]{2,1,0:T(8,128)(2,1)} %bitcast_select_fusion.2.refs_2_.refs_0_), channel_id=1, source_target_pairs={{0,4},{5,1},{4,8},{9,5},{8,12},{13,9},{12,14},{15,13},{14,10},{11,... | collective-permute-start | bytes 786440 | tf_op jit(solution)/shard_map/ppermute | solution.py:103
  49.5 1.8 %bitcast_select_fusion.1.refs_5_.refs_3_.refs_1_ = bf16[2,128,512]{2,1,0:T(8,128)(2,1)} fusion(bf16[2,128,512]{2,1,0:T(8,128)(2,1)} %collective-permute-done.11, bf16[1,2,128,512]{3,1,2,0:T(2,128)(2,1)} %bitcast.54, pred[]{:T(512)S(6)} %eq.42), kind=kLoop, calls=%fused_computation.9 | loop fusion | flops 131072 | bytes 786433 | tf_op jit(solution)/shard_map/jit(_where)/select_n | solution.py:96
  51.3 2.4 %collective-permute-start.12 = (bf16[2,128,512]{2,1,0:T(8,128)(2,1)}, bf16[2,128,512]{2,1,0:T(8,128)(2,1)}, u32[]{:S(2)}, u32[]{:S(2)}) collective-permute-start(bf16[2,128,512]{2,1,0:T(8,128)(2,1)} %bitcast_select_fusion.1.refs_5_.refs_3_.refs_1_), channel_id=1, source_target_pairs={{0,4},{5,1},{4,8},{9,5},{8,12},{13,9},{12,14},{15,13},{14,10},{11,... | collective-permute-start | bytes 786440 | tf_op jit(solution)/shard_map/ppermute | solution.py:103
  53.7 1.8 %bitcast_select_fusion.3.refs_4_.refs_2_.refs_0_ = bf16[2,128,512]{2,1,0:T(8,128)(2,1)} fusion(bf16[2,128,512]{2,1,0:T(8,128)(2,1)} %collective-permute-done.4, bf16[1,2,128,512]{3,1,2,0:T(2,128)(2,1)} %bitcast.53, pred[]{:T(512)S(6)} %eq.42), kind=kLoop, calls=%fused_computation.12 | loop fusion | flops 131072 | bytes 786433 | tf_op jit(solution)/shard_map/jit(_where)/select_n | solution.py:96
  55.5 2.5 %collective-permute-start.5 = (bf16[2,128,512]{2,1,0:T(8,128)(2,1)}, bf16[2,128,512]{2,1,0:T(8,128)(2,1)S(1)}, u32[]{:S(2)}, u32[]{:S(2)}) collective-permute-start(bf16[2,128,512]{2,1,0:T(8,128)(2,1)} %bitcast_select_fusion.3.refs_4_.refs_2_.refs_0_), channel_id=1, source_target_pairs={{0,4},{5,1},{4,8},{9,5},{8,12},{13,9},{12,14},{15,13},{14,10},{11,... | collective-permute-start | bytes 786440 | tf_op jit(solution)/shard_map/ppermute | solution.py:103
  58.1 1.6 %collective-permute-start.9 = (bf16[16,2,32,512]{3,2,1,0:T(8,128)(2,1)S(1)}, bf16[16,2,32,512]{3,2,1,0:T(8,128)(2,1)S(1)}, u32[]{:S(2)}, u32[]{:S(2)}) collective-permute-start(bf16[16,2,32,512]{3,2,1,0:T(8,128)(2,1)S(1)} %all-to-all-done.refs_0_), channel_id=1, source_target_pairs={{0,16},{16,0},{1,17},{17,1},{2,18},{18,2},{3,19},{19,3},{4,20},{20... | collective-permute-start | bytes 3145736 | tf_op jit(solution)/shard_map/ppermute | solution.py:142
  59.8 0.8 collective-permute-start.13
  61.2 1.5 %collective-permute-done.5.refs_6_.refs_4_.refs_2_ = bf16[2,128,512]{2,1,0:T(8,128)(2,1)S(1)} collective-permute-done((bf16[2,128,512]{2,1,0:T(8,128)(2,1)}, bf16[2,128,512]{2,1,0:T(8,128)(2,1)S(1)}, u32[]{:S(2)}, u32[]{:S(2)}) %collective-permute-start.5) | collective-permute-done | bytes 262176 | tf_op jit(solution)/shard_map/ppermute | solution.py:103
  62.6 2.0 %collective-permute-start.6 = (bf16[2,128,512]{2,1,0:T(8,128)(2,1)S(1)}, bf16[2,128,512]{2,1,0:T(8,128)(2,1)S(1)}, u32[]{:S(2)}, u32[]{:S(2)}) collective-permute-start(bf16[2,128,512]{2,1,0:T(8,128)(2,1)S(1)} %collective-permute-done.5.refs_6_.refs_4_.refs_2_), channel_id=1, source_target_pairs={{0,4},{5,1},{4,8},{9,5},{8,12},{13,9},{12,14},{15,13},{14,10},{11,... | collective-permute-start | bytes 786440 | tf_op jit(solution)/shard_map/ppermute | solution.py:103
  64.6 1.8 %collective-permute-done.13.refs_9_.refs_7_.refs_5_ = bf16[2,128,512]{2,1,0:T(8,128)(2,1)S(1)} collective-permute-done((bf16[2,128,512]{2,1,0:T(8,128)(2,1)}, bf16[2,128,512]{2,1,0:T(8,128)(2,1)S(1)}, u32[]{:S(2)}, u32[]{:S(2)}) %collective-permute-start.13) | collective-permute-done | bytes 262176 | tf_op jit(solution)/shard_map/ppermute | solution.py:103
  66.4 1.0 collective-permute-start.14
  68.0 1.3 %collective-permute-done.6.refs_8_.refs_6_.refs_4_ = bf16[2,128,512]{2,1,0:T(8,128)(2,1)S(1)} collective-permute-done((bf16[2,128,512]{2,1,0:T(8,128)(2,1)S(1)}, bf16[2,128,512]{2,1,0:T(8,128)(2,1)S(1)}, u32[]{:S(2)}, u32[]{:S(2)}) %collective-permute-start.6) | collective-permute-done | bytes 262176 | tf_op jit(solution)/shard_map/ppermute | solution.py:103
  69.2 1.8 %collective-permute-start.7 = (bf16[2,128,512]{2,1,0:T(8,128)(2,1)S(1)}, bf16[2,128,512]{2,1,0:T(8,128)(2,1)S(1)}, u32[]{:S(2)}, u32[]{:S(2)}) collective-permute-start(bf16[2,128,512]{2,1,0:T(8,128)(2,1)S(1)} %collective-permute-done.6.refs_8_.refs_6_.refs_4_), channel_id=1, source_target_pairs={{0,4},{5,1},{4,8},{9,5},{8,12},{13,9},{12,14},{15,13},{14,10},{11,... | collective-permute-start | bytes 786440 | tf_op jit(solution)/shard_map/ppermute | solution.py:103
  71.0 1.8 %collective-permute-done.14.refs_11_.refs_9_.refs_7_ = bf16[2,128,512]{2,1,0:T(8,128)(2,1)S(1)} collective-permute-done((bf16[2,128,512]{2,1,0:T(8,128)(2,1)S(1)}, bf16[2,128,512]{2,1,0:T(8,128)(2,1)S(1)}, u32[]{:S(2)}, u32[]{:S(2)}) %collective-permute-start.14) | collective-permute-done | bytes 262176 | tf_op jit(solution)/shard_map/ppermute | solution.py:103
  72.8 1.0 collective-permute-start.15
  74.3 1.3 %collective-permute-done.7.refs_10_.refs_8_.refs_6_ = bf16[2,128,512]{2,1,0:T(8,128)(2,1)S(1)} collective-permute-done((bf16[2,128,512]{2,1,0:T(8,128)(2,1)S(1)}, bf16[2,128,512]{2,1,0:T(8,128)(2,1)S(1)}, u32[]{:S(2)}, u32[]{:S(2)}) %collective-permute-start.7) | collective-permute-done | bytes 262176 | tf_op jit(solution)/shard_map/ppermute | solution.py:103
  75.6 1.8 %collective-permute-start.8 = (bf16[2,128,512]{2,1,0:T(8,128)(2,1)S(1)}, bf16[2,128,512]{2,1,0:T(8,128)(2,1)S(1)}, u32[]{:S(2)}, u32[]{:S(2)}) collective-permute-start(bf16[2,128,512]{2,1,0:T(8,128)(2,1)S(1)} %collective-permute-done.7.refs_10_.refs_8_.refs_6_), channel_id=1, source_target_pairs={{0,4},{5,1},{4,8},{9,5},{8,12},{13,9},{12,14},{15,13},{14,10},{11,... | collective-permute-start | bytes 786440 | tf_op jit(solution)/shard_map/ppermute | solution.py:103
  77.4 1.8 %collective-permute-done.15.refs_13_.refs_11_.refs_9_ = bf16[2,128,512]{2,1,0:T(8,128)(2,1)S(1)} collective-permute-done((bf16[2,128,512]{2,1,0:T(8,128)(2,1)S(1)}, bf16[2,128,512]{2,1,0:T(8,128)(2,1)S(1)}, u32[]{:S(2)}, u32[]{:S(2)}) %collective-permute-start.15) | collective-permute-done | bytes 262176 | tf_op jit(solution)/shard_map/ppermute | solution.py:103
  79.2 1.0 collective-permute-start.17
  80.7 1.3 %collective-permute-done.8.refs_12_.refs_10_.refs_8_ = bf16[2,128,512]{2,1,0:T(8,128)(2,1)S(1)} collective-permute-done((bf16[2,128,512]{2,1,0:T(8,128)(2,1)S(1)}, bf16[2,128,512]{2,1,0:T(8,128)(2,1)S(1)}, u32[]{:S(2)}, u32[]{:S(2)}) %collective-permute-start.8) | collective-permute-done | bytes 262176 | tf_op jit(solution)/shard_map/ppermute | solution.py:103
  82.0 0.5 collective-permute-start.31
  82.5 2.1 %shard_map.158 = (bf16[2,2,512,512]{3,2,1,0:T(8,128)(2,1)S(1)}, f32[2]{0:T(128)S(1)}) custom-call(s32[32]{0:T(128)S(1)} %copy-done.4, s32[32]{0:T(128)S(1)} %reshape.214.list_ref, s32[6]{0:T(128)S(1)} %stack.27.where_ref, bf16[16,2,32,512]{3,2,1,0:T(8,128)(2,1)S(1)} %all-to-all-done.refs_0_, bf16[16,2,32,512]{3,2,1,0:T(8,128)(2,1)S(1)} %collective-permute-done.9.refs_1_), custom_call_target="tpu_custom_call" | custom-call | flops 2000000000 | bytes 6000000 | tf_op jit(solution)/shard_map/pallas_call | solution.py:280
  84.6 0.9 collective-permute-done.17.refs_15_.refs_13_.refs_11_
  85.5 1.0 collective-permute-start.19
  86.6 2.3 %collective-permute-start.16 = (bf16[2,128,512]{2,1,0:T(8,128)(2,1)S(1)}, bf16[2,128,512]{2,1,0:T(8,128)(2,1)S(1)}, u32[]{:S(2)}, u32[]{:S(2)}) collective-permute-start(bf16[2,128,512]{2,1,0:T(8,128)(2,1)S(1)} %collective-permute-done.8.refs_12_.refs_10_.refs_8_), channel_id=1, source_target_pairs={{0,4},{5,1},{4,8},{9,5},{8,12},{13,9},{12,14},{15,13},{14,10},{11,... | collective-permute-start | bytes 786440 | tf_op jit(solution)/shard_map/ppermute | solution.py:103
  89.4 2.5 %collective-permute-done.19.refs_15_.refs_13_ = bf16[2,128,512]{2,1,0:T(8,128)(2,1)S(1)} collective-permute-done((bf16[2,128,512]{2,1,0:T(8,128)(2,1)S(1)}, bf16[2,128,512]{2,1,0:T(8,128)(2,1)S(1)}, u32[]{:S(2)}, u32[]{:S(2)}) %collective-permute-start.19) | collective-permute-done | bytes 262176 | tf_op jit(solution)/shard_map/ppermute | solution.py:103
  91.9 1.0 collective-permute-start.21
  92.9 1.8 %collective-permute-done.16.refs_14_.refs_12_.refs_10_ = bf16[2,128,512]{2,1,0:T(8,128)(2,1)S(1)} collective-permute-done((bf16[2,128,512]{2,1,0:T(8,128)(2,1)S(1)}, bf16[2,128,512]{2,1,0:T(8,128)(2,1)S(1)}, u32[]{:S(2)}, u32[]{:S(2)}) %collective-permute-start.16) | collective-permute-done | bytes 262176 | tf_op jit(solution)/shard_map/ppermute | solution.py:103
  94.7 1.0 collective-permute-start.18
  96.3 2.0 %collective-permute-done.21.refs_15_ = bf16[2,128,512]{2,1,0:T(8,128)(2,1)S(1)} collective-permute-done((bf16[2,128,512]{2,1,0:T(8,128)(2,1)S(1)}, bf16[2,128,512]{2,1,0:T(8,128)(2,1)S(1)}, u32[]{:S(2)}, u32[]{:S(2)}) %collective-permute-start.21) | collective-permute-done | bytes 262176 | tf_op jit(solution)/shard_map/ppermute | solution.py:103
  98.8 2.3 %collective-permute-done.18.refs_14_.refs_12_ = bf16[2,128,512]{2,1,0:T(8,128)(2,1)S(1)} collective-permute-done((bf16[2,128,512]{2,1,0:T(8,128)(2,1)S(1)}, bf16[2,128,512]{2,1,0:T(8,128)(2,1)S(1)}, u32[]{:S(2)}, u32[]{:S(2)}) %collective-permute-start.18) | collective-permute-done | bytes 262176 | tf_op jit(solution)/shard_map/ppermute | solution.py:103
  101.1 1.0 collective-permute-start.20
  102.2 5.8 %shard_map.159.refs_38_ = f32[2,512,512]{2,1,0:T(8,128)S(1)} custom-call(s32[6]{0:T(128)S(1)} %stack.27.where_ref, f32[2]{0:T(128)S(1)} %get-tuple-element.19.sigma_ref, bf16[2,128,512]{2,1,0:T(8,128)(2,1)S(1)} %bitcast.50, bf16[2,128,512]{2,1,0:T(8,128)(2,1)S(1)} %bitcast.47, bf16[2,128,512]{2,1,0:T(8,128)(2,1)} %bitcast_select_fusion.2.refs_2_.refs_0_, ...), custom_call_target="tpu_custom_call" | custom-call | flops 5000000000 | bytes 10000000 | tf_op jit(solution)/shard_map/pallas_call | solution.py:300
  108.0 2.0 %collective-permute-start.36 = (bf16[2,128,512]{2,1,0:T(8,128)(2,1)S(1)}, bf16[2,128,512]{2,1,0:T(8,128)(2,1)S(1)}, u32[]{:S(2)}, u32[]{:S(2)}) collective-permute-start(bf16[2,128,512]{2,1,0:T(8,128)(2,1)S(1)} %collective-permute-done.20.refs_14_), channel_id=1, source_target_pairs={{0,1},{1,0},{2,3},{3,2},{4,5},{5,4},{6,7},{7,6},{8,9},{9,8},{10,11... | collective-permute-start | bytes 786440 | tf_op jit(solution)/shard_map/ppermute | solution.py:104
  110.0 5.7 %shard_map.160.refs_38_ = f32[2,512,512]{2,1,0:T(8,128)S(1)} custom-call(s32[6]{0:T(128)S(1)} %stack.27.where_ref, f32[2]{0:T(128)S(1)} %get-tuple-element.19.sigma_ref, bf16[2,128,512]{2,1,0:T(8,128)(2,1)} %bitcast_select_fusion.2.refs_2_.refs_0_, bf16[2,128,512]{2,1,0:T(8,128)(2,1)} %bitcast_select_fusion.refs_3_.refs_1_, ...), custom_call_target="tpu_custom_call" | custom-call | flops 5000000000 | bytes 10000000 | tf_op jit(solution)/shard_map/pallas_call | solution.py:300
  115.8 6.7 %shard_map.161 = (f32[2]{0:T(128)}, f32[2]{0:T(128)}) custom-call(s32[6]{0:T(128)S(1)} %stack.27.where_ref, f32[2]{0:T(128)S(1)} %get-tuple-element.19.sigma_ref, bf16[2,128,512]{2,1,0:T(8,128)(2,1)S(1)} %copy-done.3, bf16[2,128,512]{2,1,0:T(8,128)(2,1)} %bitcast_select_fusion.1.refs_5_.refs_3_.refs_1_, ...), custom_call_target="tpu_custom_call" | custom-call | flops 5000000000 | bytes 10000000 | tf_op jit(solution)/shard_map/pallas_call | solution.py:300
  (84 shorter events, 6.4 us)
Async XLA Ops:
  4.3 13.3 %collective-permute-start = (bf16[2,131072]{1,0:T(2,128)(2,1)}, bf16[2,131072]{1,0:T(2,128)(2,1)}, u32[]{:S(2)}, u32[]{:S(2)}) collective-permute-start(bf16[2,131072]{1,0:T(2,128)(2,1)} %get-tuple-element.27), channel_id=1, source_target_pairs={{0,1},{1,0},{2,3},{3,2},{4,5},{5,4},{6,7},{7,6},{8,9},{9,8},{10,11... | collective-permute-start | bytes 1572872 | tf_op jit(solution)/shard_map/ppermute | solution.py:75
  4.7 12.8 %collective-permute-start.1 = (bf16[2,131072]{1,0:T(2,128)(2,1)}, bf16[2,131072]{1,0:T(2,128)(2,1)}, u32[]{:S(2)}, u32[]{:S(2)}) collective-permute-start(bf16[2,131072]{1,0:T(2,128)(2,1)} %get-tuple-element.28), channel_id=1, source_target_pairs={{0,1},{1,0},{2,3},{3,2},{4,5},{5,4},{6,7},{7,6},{8,9},{9,8},{10,11... | collective-permute-start | bytes 1572872 | tf_op jit(solution)/shard_map/ppermute | solution.py:75
  4.8 12.8 %collective-permute-start.2 = (bf16[2,131072]{1,0:T(2,128)(2,1)}, bf16[2,131072]{1,0:T(2,128)(2,1)}, u32[]{:S(2)}, u32[]{:S(2)}) collective-permute-start(bf16[2,131072]{1,0:T(2,128)(2,1)} %get-tuple-element.29), channel_id=1, source_target_pairs={{0,1},{1,0},{2,3},{3,2},{4,5},{5,4},{6,7},{7,6},{8,9},{9,8},{10,11... | collective-permute-start | bytes 1572872 | tf_op jit(solution)/shard_map/ppermute | solution.py:75
  9.5 46.0 %all-to-all-start = ((bf16[16,2,32,512]{3,2,1,0:T(8,128)(2,1)}), bf16[16,2,32,512]{3,2,1,0:T(8,128)(2,1)S(1)}, u32[]{:S(2)}, u32[]{:S(2)}) async-start(bf16[16,2,32,512]{3,2,1,0:T(8,128)(2,1)} %reshape.213), calls=%async_computation | async-start | bytes 2097152 | tf_op jit(solution)/shard_map/all_to_all | solution.py:136
  21.0 16.5 %collective-permute-start.10 = (bf16[2,128,512]{2,1,0:T(8,128)(2,1)S(1)}, bf16[2,128,512]{2,1,0:T(8,128)(2,1)S(1)}, u32[]{:S(2)}, u32[]{:S(2)}) collective-permute-start(bf16[2,128,512]{2,1,0:T(8,128)(2,1)S(1)} %bitcast.45), channel_id=1, source_target_pairs={{0,4},{5,1},{4,8},{9,5},{8,12},{13,9},{12,14},{15,13},{14,10},{11,... | collective-permute-start | bytes 786440 | tf_op jit(solution)/shard_map/ppermute | solution.py:103
  23.0 22.3 %collective-permute-start.3 = (bf16[2,128,512]{2,1,0:T(8,128)(2,1)S(1)}, bf16[2,128,512]{2,1,0:T(8,128)(2,1)S(1)}, u32[]{:S(2)}, u32[]{:S(2)}) collective-permute-start(bf16[2,128,512]{2,1,0:T(8,128)(2,1)S(1)} %bitcast.48), channel_id=1, source_target_pairs={{0,4},{5,1},{4,8},{9,5},{8,12},{13,9},{12,14},{15,13},{14,10},{11,... | collective-permute-start | bytes 786440 | tf_op jit(solution)/shard_map/ppermute | solution.py:103
  26.0 56.4 %copy-start.4 = (s32[32]{0:T(128)S(1)}, s32[32]{0:T(128)}, u32[]{:S(2)}) copy-start(s32[32]{0:T(128)} %cut_ref.1) | copy-start | bytes 388
  38.2 11.3 %collective-permute-start.11 = (bf16[2,128,512]{2,1,0:T(8,128)(2,1)}, bf16[2,128,512]{2,1,0:T(8,128)(2,1)}, u32[]{:S(2)}, u32[]{:S(2)}) collective-permute-start(bf16[2,128,512]{2,1,0:T(8,128)(2,1)} %bitcast_select_fusion.refs_3_.refs_1_), channel_id=1, source_target_pairs={{0,4},{5,1},{4,8},{9,5},{8,12},{13,9},{12,14},{15,13},{14,10},{11,... | collective-permute-start | bytes 786440 | tf_op jit(solution)/shard_map/ppermute | solution.py:103
  46.0 7.7 %collective-permute-start.4 = (bf16[2,128,512]{2,1,0:T(8,128)(2,1)}, bf16[2,128,512]{2,1,0:T(8,128)(2,1)}, u32[]{:S(2)}, u32[]{:S(2)}) collective-permute-start(bf16[2,128,512]{2,1,0:T(8,128)(2,1)} %bitcast_select_fusion.2.refs_2_.refs_0_), channel_id=1, source_target_pairs={{0,4},{5,1},{4,8},{9,5},{8,12},{13,9},{12,14},{15,13},{14,10},{11,... | collective-permute-start | bytes 786440 | tf_op jit(solution)/shard_map/ppermute | solution.py:103
  51.3 8.5 %collective-permute-start.12 = (bf16[2,128,512]{2,1,0:T(8,128)(2,1)}, bf16[2,128,512]{2,1,0:T(8,128)(2,1)}, u32[]{:S(2)}, u32[]{:S(2)}) collective-permute-start(bf16[2,128,512]{2,1,0:T(8,128)(2,1)} %bitcast_select_fusion.1.refs_5_.refs_3_.refs_1_), channel_id=1, source_target_pairs={{0,4},{5,1},{4,8},{9,5},{8,12},{13,9},{12,14},{15,13},{14,10},{11,... | collective-permute-start | bytes 786440 | tf_op jit(solution)/shard_map/ppermute | solution.py:103
  55.5 46.7 %copy-start.2 = (bf16[1,2,128,512]{3,2,1,0:T(8,128)(2,1)S(1)}, bf16[1,2,128,512]{3,2,1,0:T(8,128)(2,1)}, u32[]{:S(2)}) copy-start(bf16[1,2,128,512]{3,2,1,0:T(8,128)(2,1)} %copy-done.1) | copy-start | bytes 786436
  55.5 46.7 %copy-start.3 = (bf16[2,128,512]{2,1,0:T(8,128)(2,1)S(1)}, bf16[2,128,512]{2,1,0:T(8,128)(2,1)}, u32[]{:S(2)}) copy-start(bf16[2,128,512]{2,1,0:T(8,128)(2,1)} %bitcast_select_fusion.3.refs_4_.refs_2_.refs_0_) | copy-start | bytes 786436
  55.5 46.7 %copy-start.5 = (f32[4,2,128,512]{3,2,1,0:T(8,128)S(1)}, f32[4,2,128,512]{3,2,1,0:T(8,128)}, u32[]{:S(2)}) copy-start(f32[4,2,128,512]{3,2,1,0:T(8,128)} %constant.174.clone.refs_37_) | copy-start | bytes 6291460
  55.5 46.7 %copy-start.6 = (bf16[4,512,256]{2,1,0:T(8,128)(2,1)S(1)}, bf16[4,512,256]{2,1,0:T(8,128)(2,1)}, u32[]{:S(2)}) copy-start(bf16[4,512,256]{2,1,0:T(8,128)(2,1)} %constant.179.refs_36_) | copy-start | bytes 3145732
  55.5 7.1 %collective-permute-start.5 = (bf16[2,128,512]{2,1,0:T(8,128)(2,1)}, bf16[2,128,512]{2,1,0:T(8,128)(2,1)S(1)}, u32[]{:S(2)}, u32[]{:S(2)}) collective-permute-start(bf16[2,128,512]{2,1,0:T(8,128)(2,1)} %bitcast_select_fusion.3.refs_4_.refs_2_.refs_0_), channel_id=1, source_target_pairs={{0,4},{5,1},{4,8},{9,5},{8,12},{13,9},{12,14},{15,13},{14,10},{11,... | collective-permute-start | bytes 786440 | tf_op jit(solution)/shard_map/ppermute | solution.py:103
  58.1 23.9 %collective-permute-start.9 = (bf16[16,2,32,512]{3,2,1,0:T(8,128)(2,1)S(1)}, bf16[16,2,32,512]{3,2,1,0:T(8,128)(2,1)S(1)}, u32[]{:S(2)}, u32[]{:S(2)}) collective-permute-start(bf16[16,2,32,512]{3,2,1,0:T(8,128)(2,1)S(1)} %all-to-all-done.refs_0_), channel_id=1, source_target_pairs={{0,16},{16,0},{1,17},{17,1},{2,18},{18,2},{3,19},{19,3},{4,20},{20... | collective-permute-start | bytes 3145736 | tf_op jit(solution)/shard_map/ppermute | solution.py:142
  59.8 6.6 %collective-permute-start.13 = (bf16[2,128,512]{2,1,0:T(8,128)(2,1)}, bf16[2,128,512]{2,1,0:T(8,128)(2,1)S(1)}, u32[]{:S(2)}, u32[]{:S(2)}) collective-permute-start(bf16[2,128,512]{2,1,0:T(8,128)(2,1)} %collective-permute-done.12.refs_7_.refs_5_.refs_3_), channel_id=1, source_target_pairs={{0,4},{5,1},{4,8},{9,5},{8,12},{13,9},{12,14},{15,13},{14,10},{11,... | collective-permute-start | bytes 786440 | tf_op jit(solution)/shard_map/ppermute | solution.py:103
  60.7 6.8 %collective-permute-start.40 = (bf16[2,128,512]{2,1,0:T(8,128)(2,1)}, bf16[2,128,512]{2,1,0:T(8,128)(2,1)S(1)}, u32[]{:S(2)}, u32[]{:S(2)}) collective-permute-start(bf16[2,128,512]{2,1,0:T(8,128)(2,1)} %bitcast.49), channel_id=1, source_target_pairs={{0,1},{1,0},{2,3},{3,2},{4,5},{5,4},{6,7},{7,6},{8,9},{9,8},{10,11... | collective-permute-start | bytes 786440 | tf_op jit(solution)/shard_map/ppermute | solution.py:104
  60.7 6.8 %collective-permute-start.41 = (bf16[2,128,512]{2,1,0:T(8,128)(2,1)S(1)}, bf16[2,128,512]{2,1,0:T(8,128)(2,1)S(1)}, u32[]{:S(2)}, u32[]{:S(2)}) collective-permute-start(bf16[2,128,512]{2,1,0:T(8,128)(2,1)S(1)} %bitcast.46), channel_id=1, source_target_pairs={{0,1},{1,0},{2,3},{3,2},{4,5},{5,4},{6,7},{7,6},{8,9},{9,8},{10,11... | collective-permute-start | bytes 786440 | tf_op jit(solution)/shard_map/ppermute | solution.py:104
  62.6 6.6 %collective-permute-start.6 = (bf16[2,128,512]{2,1,0:T(8,128)(2,1)S(1)}, bf16[2,128,512]{2,1,0:T(8,128)(2,1)S(1)}, u32[]{:S(2)}, u32[]{:S(2)}) collective-permute-start(bf16[2,128,512]{2,1,0:T(8,128)(2,1)S(1)} %collective-permute-done.5.refs_6_.refs_4_.refs_2_), channel_id=1, source_target_pairs={{0,4},{5,1},{4,8},{9,5},{8,12},{13,9},{12,14},{15,13},{14,10},{11,... | collective-permute-start | bytes 786440 | tf_op jit(solution)/shard_map/ppermute | solution.py:103
  66.4 6.4 %collective-permute-start.14 = (bf16[2,128,512]{2,1,0:T(8,128)(2,1)S(1)}, bf16[2,128,512]{2,1,0:T(8,128)(2,1)S(1)}, u32[]{:S(2)}, u32[]{:S(2)}) collective-permute-start(bf16[2,128,512]{2,1,0:T(8,128)(2,1)S(1)} %collective-permute-done.13.refs_9_.refs_7_.refs_5_), channel_id=1, source_target_pairs={{0,4},{5,1},{4,8},{9,5},{8,12},{13,9},{12,14},{15,13},{14,10},{11,... | collective-permute-start | bytes 786440 | tf_op jit(solution)/shard_map/ppermute | solution.py:103
  67.5 6.4 %collective-permute-start.39 = (bf16[2,128,512]{2,1,0:T(8,128)(2,1)}, bf16[2,128,512]{2,1,0:T(8,128)(2,1)S(1)}, u32[]{:S(2)}, u32[]{:S(2)}) collective-permute-start(bf16[2,128,512]{2,1,0:T(8,128)(2,1)} %bitcast_select_fusion.refs_3_.refs_1_), channel_id=1, source_target_pairs={{0,1},{1,0},{2,3},{3,2},{4,5},{5,4},{6,7},{7,6},{8,9},{9,8},{10,11... | collective-permute-start | bytes 786440 | tf_op jit(solution)/shard_map/ppermute | solution.py:104
  67.5 6.4 %collective-permute-start.38 = (bf16[2,128,512]{2,1,0:T(8,128)(2,1)}, bf16[2,128,512]{2,1,0:T(8,128)(2,1)S(1)}, u32[]{:S(2)}, u32[]{:S(2)}) collective-permute-start(bf16[2,128,512]{2,1,0:T(8,128)(2,1)} %bitcast_select_fusion.2.refs_2_.refs_0_), channel_id=1, source_target_pairs={{0,1},{1,0},{2,3},{3,2},{4,5},{5,4},{6,7},{7,6},{8,9},{9,8},{10,11... | collective-permute-start | bytes 786440 | tf_op jit(solution)/shard_map/ppermute | solution.py:104
  69.2 6.4 %collective-permute-start.7 = (bf16[2,128,512]{2,1,0:T(8,128)(2,1)S(1)}, bf16[2,128,512]{2,1,0:T(8,128)(2,1)S(1)}, u32[]{:S(2)}, u32[]{:S(2)}) collective-permute-start(bf16[2,128,512]{2,1,0:T(8,128)(2,1)S(1)} %collective-permute-done.6.refs_8_.refs_6_.refs_4_), channel_id=1, source_target_pairs={{0,4},{5,1},{4,8},{9,5},{8,12},{13,9},{12,14},{15,13},{14,10},{11,... | collective-permute-start | bytes 786440 | tf_op jit(solution)/shard_map/ppermute | solution.py:103
  72.8 6.4 %collective-permute-start.15 = (bf16[2,128,512]{2,1,0:T(8,128)(2,1)S(1)}, bf16[2,128,512]{2,1,0:T(8,128)(2,1)S(1)}, u32[]{:S(2)}, u32[]{:S(2)}) collective-permute-start(bf16[2,128,512]{2,1,0:T(8,128)(2,1)S(1)} %collective-permute-done.14.refs_11_.refs_9_.refs_7_), channel_id=1, source_target_pairs={{0,4},{5,1},{4,8},{9,5},{8,12},{13,9},{12,14},{15,13},{14,10},{11,... | collective-permute-start | bytes 786440 | tf_op jit(solution)/shard_map/ppermute | solution.py:103
  73.8 6.4 %collective-permute-start.23 = (bf16[2,128,512]{2,1,0:T(8,128)(2,1)}, bf16[2,128,512]{2,1,0:T(8,128)(2,1)S(1)}, u32[]{:S(2)}, u32[]{:S(2)}) collective-permute-start(bf16[2,128,512]{2,1,0:T(8,128)(2,1)} %bitcast_select_fusion.1.refs_5_.refs_3_.refs_1_), channel_id=1, source_target_pairs={{0,1},{1,0},{2,3},{3,2},{4,5},{5,4},{6,7},{7,6},{8,9},{9,8},{10,11... | collective-permute-start | bytes 786440 | tf_op jit(solution)/shard_map/ppermute | solution.py:104
  73.8 6.4 %collective-permute-start.25 = (bf16[2,128,512]{2,1,0:T(8,128)(2,1)}, bf16[2,128,512]{2,1,0:T(8,128)(2,1)S(1)}, u32[]{:S(2)}, u32[]{:S(2)}) collective-permute-start(bf16[2,128,512]{2,1,0:T(8,128)(2,1)} %collective-permute-done.12.refs_7_.refs_5_.refs_3_), channel_id=1, source_target_pairs={{0,1},{1,0},{2,3},{3,2},{4,5},{5,4},{6,7},{7,6},{8,9},{9,8},{10,11... | collective-permute-start | bytes 786440 | tf_op jit(solution)/shard_map/ppermute | solution.py:104
  75.6 6.4 %collective-permute-start.8 = (bf16[2,128,512]{2,1,0:T(8,128)(2,1)S(1)}, bf16[2,128,512]{2,1,0:T(8,128)(2,1)S(1)}, u32[]{:S(2)}, u32[]{:S(2)}) collective-permute-start(bf16[2,128,512]{2,1,0:T(8,128)(2,1)S(1)} %collective-permute-done.7.refs_10_.refs_8_.refs_6_), channel_id=1, source_target_pairs={{0,4},{5,1},{4,8},{9,5},{8,12},{13,9},{12,14},{15,13},{14,10},{11,... | collective-permute-start | bytes 786440 | tf_op jit(solution)/shard_map/ppermute | solution.py:103
  79.2 6.4 %collective-permute-start.17 = (bf16[2,128,512]{2,1,0:T(8,128)(2,1)S(1)}, bf16[2,128,512]{2,1,0:T(8,128)(2,1)S(1)}, u32[]{:S(2)}, u32[]{:S(2)}) collective-permute-start(bf16[2,128,512]{2,1,0:T(8,128)(2,1)S(1)} %collective-permute-done.15.refs_13_.refs_11_.refs_9_), channel_id=1, source_target_pairs={{0,4},{5,1},{4,8},{9,5},{8,12},{13,9},{12,14},{15,13},{14,10},{11,... | collective-permute-start | bytes 786440 | tf_op jit(solution)/shard_map/ppermute | solution.py:103
  80.2 6.4 %collective-permute-start.27 = (bf16[2,128,512]{2,1,0:T(8,128)(2,1)S(1)}, bf16[2,128,512]{2,1,0:T(8,128)(2,1)S(1)}, u32[]{:S(2)}, u32[]{:S(2)}) collective-permute-start(bf16[2,128,512]{2,1,0:T(8,128)(2,1)S(1)} %collective-permute-done.13.refs_9_.refs_7_.refs_5_), channel_id=1, source_target_pairs={{0,1},{1,0},{2,3},{3,2},{4,5},{5,4},{6,7},{7,6},{8,9},{9,8},{10,11... | collective-permute-start | bytes 786440 | tf_op jit(solution)/shard_map/ppermute | solution.py:104
  80.2 6.4 %collective-permute-start.29 = (bf16[2,128,512]{2,1,0:T(8,128)(2,1)S(1)}, bf16[2,128,512]{2,1,0:T(8,128)(2,1)S(1)}, u32[]{:S(2)}, u32[]{:S(2)}) collective-permute-start(bf16[2,128,512]{2,1,0:T(8,128)(2,1)S(1)} %collective-permute-done.14.refs_11_.refs_9_.refs_7_), channel_id=1, source_target_pairs={{0,1},{1,0},{2,3},{3,2},{4,5},{5,4},{6,7},{7,6},{8,9},{9,8},{10,11... | collective-permute-start | bytes 786440 | tf_op jit(solution)/shard_map/ppermute | solution.py:104
  82.0 6.9 %collective-permute-start.22 = (bf16[2,128,512]{2,1,0:T(8,128)(2,1)}, bf16[2,128,512]{2,1,0:T(8,128)(2,1)S(1)}, u32[]{:S(2)}, u32[]{:S(2)}) collective-permute-start(bf16[2,128,512]{2,1,0:T(8,128)(2,1)} %bitcast_select_fusion.3.refs_4_.refs_2_.refs_0_), channel_id=1, source_target_pairs={{0,1},{1,0},{2,3},{3,2},{4,5},{5,4},{6,7},{7,6},{8,9},{9,8},{10,11... | collective-permute-start | bytes 786440 | tf_op jit(solution)/shard_map/ppermute | solution.py:104
  82.0 6.9 %collective-permute-start.31 = (bf16[2,128,512]{2,1,0:T(8,128)(2,1)S(1)}, bf16[2,128,512]{2,1,0:T(8,128)(2,1)S(1)}, u32[]{:S(2)}, u32[]{:S(2)}) collective-permute-start(bf16[2,128,512]{2,1,0:T(8,128)(2,1)S(1)} %collective-permute-done.15.refs_13_.refs_11_.refs_9_), channel_id=1, source_target_pairs={{0,1},{1,0},{2,3},{3,2},{4,5},{5,4},{6,7},{7,6},{8,9},{9,8},{10,11... | collective-permute-start | bytes 786440 | tf_op jit(solution)/shard_map/ppermute | solution.py:104
  85.5 6.4 %collective-permute-start.19 = (bf16[2,128,512]{2,1,0:T(8,128)(2,1)S(1)}, bf16[2,128,512]{2,1,0:T(8,128)(2,1)S(1)}, u32[]{:S(2)}, u32[]{:S(2)}) collective-permute-start(bf16[2,128,512]{2,1,0:T(8,128)(2,1)S(1)} %collective-permute-done.17.refs_15_.refs_13_.refs_11_), channel_id=1, source_target_pairs={{0,4},{5,1},{4,8},{9,5},{8,12},{13,9},{12,14},{15,13},{14,10},{11,... | collective-permute-start | bytes 786440 | tf_op jit(solution)/shard_map/ppermute | solution.py:103
  86.6 6.4 %collective-permute-start.24 = (bf16[2,128,512]{2,1,0:T(8,128)(2,1)S(1)}, bf16[2,128,512]{2,1,0:T(8,128)(2,1)S(1)}, u32[]{:S(2)}, u32[]{:S(2)}) collective-permute-start(bf16[2,128,512]{2,1,0:T(8,128)(2,1)S(1)} %collective-permute-done.5.refs_6_.refs_4_.refs_2_), channel_id=1, source_target_pairs={{0,1},{1,0},{2,3},{3,2},{4,5},{5,4},{6,7},{7,6},{8,9},{9,8},{10,11... | collective-permute-start | bytes 786440 | tf_op jit(solution)/shard_map/ppermute | solution.py:104
  86.6 8.1 %collective-permute-start.16 = (bf16[2,128,512]{2,1,0:T(8,128)(2,1)S(1)}, bf16[2,128,512]{2,1,0:T(8,128)(2,1)S(1)}, u32[]{:S(2)}, u32[]{:S(2)}) collective-permute-start(bf16[2,128,512]{2,1,0:T(8,128)(2,1)S(1)} %collective-permute-done.8.refs_12_.refs_10_.refs_8_), channel_id=1, source_target_pairs={{0,4},{5,1},{4,8},{9,5},{8,12},{13,9},{12,14},{15,13},{14,10},{11,... | collective-permute-start | bytes 786440 | tf_op jit(solution)/shard_map/ppermute | solution.py:103
  88.9 6.9 %collective-permute-start.33 = (bf16[2,128,512]{2,1,0:T(8,128)(2,1)S(1)}, bf16[2,128,512]{2,1,0:T(8,128)(2,1)S(1)}, u32[]{:S(2)}, u32[]{:S(2)}) collective-permute-start(bf16[2,128,512]{2,1,0:T(8,128)(2,1)S(1)} %collective-permute-done.17.refs_15_.refs_13_.refs_11_), channel_id=1, source_target_pairs={{0,1},{1,0},{2,3},{3,2},{4,5},{5,4},{6,7},{7,6},{8,9},{9,8},{10,11... | collective-permute-start | bytes 786440 | tf_op jit(solution)/shard_map/ppermute | solution.py:104
  88.9 6.9 %collective-permute-start.26 = (bf16[2,128,512]{2,1,0:T(8,128)(2,1)S(1)}, bf16[2,128,512]{2,1,0:T(8,128)(2,1)S(1)}, u32[]{:S(2)}, u32[]{:S(2)}) collective-permute-start(bf16[2,128,512]{2,1,0:T(8,128)(2,1)S(1)} %collective-permute-done.6.refs_8_.refs_6_.refs_4_), channel_id=1, source_target_pairs={{0,1},{1,0},{2,3},{3,2},{4,5},{5,4},{6,7},{7,6},{8,9},{9,8},{10,11... | collective-permute-start | bytes 786440 | tf_op jit(solution)/shard_map/ppermute | solution.py:104
  91.9 6.4 %collective-permute-start.21 = (bf16[2,128,512]{2,1,0:T(8,128)(2,1)S(1)}, bf16[2,128,512]{2,1,0:T(8,128)(2,1)S(1)}, u32[]{:S(2)}, u32[]{:S(2)}) collective-permute-start(bf16[2,128,512]{2,1,0:T(8,128)(2,1)S(1)} %collective-permute-done.19.refs_15_.refs_13_), channel_id=1, source_target_pairs={{0,4},{5,1},{4,8},{9,5},{8,12},{13,9},{12,14},{15,13},{14,10},{11,... | collective-permute-start | bytes 786440 | tf_op jit(solution)/shard_map/ppermute | solution.py:103
  92.9 5.3 %collective-permute-start.28 = (bf16[2,128,512]{2,1,0:T(8,128)(2,1)S(1)}, bf16[2,128,512]{2,1,0:T(8,128)(2,1)S(1)}, u32[]{:S(2)}, u32[]{:S(2)}) collective-permute-start(bf16[2,128,512]{2,1,0:T(8,128)(2,1)S(1)} %collective-permute-done.7.refs_10_.refs_8_.refs_6_), channel_id=1, source_target_pairs={{0,1},{1,0},{2,3},{3,2},{4,5},{5,4},{6,7},{7,6},{8,9},{9,8},{10,11... | collective-permute-start | bytes 786440 | tf_op jit(solution)/shard_map/ppermute | solution.py:104
  94.7 6.4 %collective-permute-start.18 = (bf16[2,128,512]{2,1,0:T(8,128)(2,1)S(1)}, bf16[2,128,512]{2,1,0:T(8,128)(2,1)S(1)}, u32[]{:S(2)}, u32[]{:S(2)}) collective-permute-start(bf16[2,128,512]{2,1,0:T(8,128)(2,1)S(1)} %collective-permute-done.16.refs_14_.refs_12_.refs_10_), channel_id=1, source_target_pairs={{0,4},{5,1},{4,8},{9,5},{8,12},{13,9},{12,14},{15,13},{14,10},{11,... | collective-permute-start | bytes 786440 | tf_op jit(solution)/shard_map/ppermute | solution.py:103
  95.8 5.3 %collective-permute-start.30 = (bf16[2,128,512]{2,1,0:T(8,128)(2,1)S(1)}, bf16[2,128,512]{2,1,0:T(8,128)(2,1)S(1)}, u32[]{:S(2)}, u32[]{:S(2)}) collective-permute-start(bf16[2,128,512]{2,1,0:T(8,128)(2,1)S(1)} %collective-permute-done.8.refs_12_.refs_10_.refs_8_), channel_id=1, source_target_pairs={{0,1},{1,0},{2,3},{3,2},{4,5},{5,4},{6,7},{7,6},{8,9},{9,8},{10,11... | collective-permute-start | bytes 786440 | tf_op jit(solution)/shard_map/ppermute | solution.py:104
  95.8 6.4 %collective-permute-start.32 = (bf16[2,128,512]{2,1,0:T(8,128)(2,1)S(1)}, bf16[2,128,512]{2,1,0:T(8,128)(2,1)S(1)}, u32[]{:S(2)}, u32[]{:S(2)}) collective-permute-start(bf16[2,128,512]{2,1,0:T(8,128)(2,1)S(1)} %collective-permute-done.16.refs_14_.refs_12_.refs_10_), channel_id=1, source_target_pairs={{0,1},{1,0},{2,3},{3,2},{4,5},{5,4},{6,7},{7,6},{8,9},{9,8},{10,11... | collective-permute-start | bytes 786440 | tf_op jit(solution)/shard_map/ppermute | solution.py:104
  98.3 11.7 %collective-permute-start.35 = (bf16[2,128,512]{2,1,0:T(8,128)(2,1)S(1)}, bf16[2,128,512]{2,1,0:T(8,128)(2,1)S(1)}, u32[]{:S(2)}, u32[]{:S(2)}) collective-permute-start(bf16[2,128,512]{2,1,0:T(8,128)(2,1)S(1)} %collective-permute-done.19.refs_15_.refs_13_), channel_id=1, source_target_pairs={{0,1},{1,0},{2,3},{3,2},{4,5},{5,4},{6,7},{7,6},{8,9},{9,8},{10,11... | collective-permute-start | bytes 786440 | tf_op jit(solution)/shard_map/ppermute | solution.py:104
  98.3 17.5 %collective-permute-start.37 = (bf16[2,128,512]{2,1,0:T(8,128)(2,1)S(1)}, bf16[2,128,512]{2,1,0:T(8,128)(2,1)S(1)}, u32[]{:S(2)}, u32[]{:S(2)}) collective-permute-start(bf16[2,128,512]{2,1,0:T(8,128)(2,1)S(1)} %collective-permute-done.21.refs_15_), channel_id=1, source_target_pairs={{0,1},{1,0},{2,3},{3,2},{4,5},{5,4},{6,7},{7,6},{8,9},{9,8},{10,11... | collective-permute-start | bytes 786440 | tf_op jit(solution)/shard_map/ppermute | solution.py:104
  101.1 8.9 %collective-permute-start.34 = (bf16[2,128,512]{2,1,0:T(8,128)(2,1)S(1)}, bf16[2,128,512]{2,1,0:T(8,128)(2,1)S(1)}, u32[]{:S(2)}, u32[]{:S(2)}) collective-permute-start(bf16[2,128,512]{2,1,0:T(8,128)(2,1)S(1)} %collective-permute-done.18.refs_14_.refs_12_), channel_id=1, source_target_pairs={{0,1},{1,0},{2,3},{3,2},{4,5},{5,4},{6,7},{7,6},{8,9},{9,8},{10,11... | collective-permute-start | bytes 786440 | tf_op jit(solution)/shard_map/ppermute | solution.py:104
  101.1 6.9 %collective-permute-start.20 = (bf16[2,128,512]{2,1,0:T(8,128)(2,1)S(1)}, bf16[2,128,512]{2,1,0:T(8,128)(2,1)S(1)}, u32[]{:S(2)}, u32[]{:S(2)}) collective-permute-start(bf16[2,128,512]{2,1,0:T(8,128)(2,1)S(1)} %collective-permute-done.18.refs_14_.refs_12_), channel_id=1, source_target_pairs={{0,4},{5,1},{4,8},{9,5},{8,12},{13,9},{12,14},{15,13},{14,10},{11,... | collective-permute-start | bytes 786440 | tf_op jit(solution)/shard_map/ppermute | solution.py:103
  108.0 7.8 %collective-permute-start.36 = (bf16[2,128,512]{2,1,0:T(8,128)(2,1)S(1)}, bf16[2,128,512]{2,1,0:T(8,128)(2,1)S(1)}, u32[]{:S(2)}, u32[]{:S(2)}) collective-permute-start(bf16[2,128,512]{2,1,0:T(8,128)(2,1)S(1)} %collective-permute-done.20.refs_14_), channel_id=1, source_target_pairs={{0,1},{1,0},{2,3},{3,2},{4,5},{5,4},{6,7},{7,6},{8,9},{9,8},{10,11... | collective-permute-start | bytes 786440 | tf_op jit(solution)/shard_map/ppermute | solution.py:104
  (5 other events, 79.6 us)

commit v17 on v7

--- a/solution.py
+++ b/solution.py
@@ -20,7 +20,7 @@
 HALF_CHUNKS = 2
 LAG = 2
 TEMPLATE_SLOT = 4
-MASKED_SLOT = 12
+MASKED_SLOT = 18
 VMEM_LIMIT = 24 * 1024 * 1024
 
 

time: 123 us -> 124 us (level)
  starting transfers between devices: 44.4 us -> 42.2 us
  waiting for transfers between devices: 35.5 us -> 36.9 us
    ppermute x20, starting transfers between devices: 4.53 us -> 2.12 us  [spread(): shared = [lax.ppermute(here, 'tpl', to_partner()) for here in sent]]
    ppermute x18, waiting for transfers between devices: 35.1 us -> 36.7 us  [spread(): arrived.append(lax.ppermute(here, 'tpl', along))]
  transfers between devices with their start and end apart: 43 -> 43, of which waited for: 14 -> 16; matrix products, arithmetic and copies ran while one was open for 12% -> 14% of each run, Pallas kernels for 11% -> 12%
where the time goes in v17:
time: 124 us; the launch traced here: 123 us
  starting transfers between devices  42.2 us (34%)
  waiting for transfers between devices  36.9 us (30%)
  Pallas kernels  20.9 us (17%)
  local copies, waits for them, and re-layouts  11.9 us (10%)
  other arithmetic  9.58 us (8%)
  between operations  2.01 us (2%)
    ppermute x18, waiting for transfers between devices, spread(): arrived.append(lax.ppermute(here, 'tpl', along))  36.7 us
    ppermute x18, starting transfers between devices, spread(): arrived.append(lax.ppermute(here, 'tpl', along))  33.8 us
    pallas_call x3, Pallas kernels, detector(): pl.pallas_call(functools.partial(detector_kernel, det, chips), out_shape=...  18.8 us
    select_n x4, other arithmetic, spread(): here = jnp.where(on_owner_chip, chunks[slot], arrived[slot - LAG])  4.38 us
    all_to_all x1, starting transfers between devices, exchange(): return lax.all_to_all(block, 'tpl', split_axis=0, concat_axis=0, tiled=True)  3.91 us
    select_n x3, other arithmetic, half_chunks(): first = jnp.where(core == owner % CORES, side(core), got)  3.82 us
    squeeze x3, local copies, waits for them, and re-layouts, half_chunks(): lax.dynamic_slice(strain_slots, (0, det, 0, which * half), (1, 1, 2, half))  3.07 us
    gather x1, local copies, waits for them, and re-layouts, pick(): templates[lax.dynamic_index_in_dim(lists, own_group, 1, keepdims=False)]  2.66 us
  transfers between devices with their start and end apart: 43, of which 16 were waited for; matrix products, arithmetic and copies ran while one was open for 14% of the time, Pallas kernels for 12%

profile of v17, /device:TPU:0, one launch (start us, length us, event | category | flops | bytes accessed | tf_op | source)
XLA Modules:
  0.0 123.4 jit_solution(15230186451481600746)
XLA Ops:
  0.7 1.5 %dynamic-slice_bitcast_fusion.2 = bf16[2,131072]{1,0:T(2,128)(2,1)S(1)} fusion(bf16[1,3,2,262144]{3,2,1,0:T(2,128)(2,1)} %param.15, s32[]{:T(128)S(6)} %select_n.186), kind=kLoop, calls=%fused_computation.6 | loop fusion | bytes 1048580 | tf_op jit(solution)/shard_map/squeeze | solution.py:74
  3.4 0.8 and_select_fusion.2
  4.3 1.7 %broadcast_select_fusion.2 = bf16[2,131072]{1,0:T(2,128)(2,1)S(1)} fusion(bf16[2,131072]{1,0:T(2,128)(2,1)S(1)} %collective-permute-done, pred[]{:T(512)S(6)} %eq.43, bf16[1,3,2,262144]{3,2,1,0:T(2,128)(2,1)} %param.15, s32[]{:T(128)S(6)} %select_n.185), kind=kLoop, calls=%fused_computation.3 | loop fusion | flops 262144 | bytes 1572869 | tf_op jit(solution)/shard_map/jit(_where)/select_n | solution.py:76
  6.4 0.8 copy_bitcast_fusion.4
  8.4 2.9 %collective-permute-start.13 = (bf16[2,128,512]{2,1,0:T(8,128)(2,1)S(1)}, bf16[2,128,512]{2,1,0:T(8,128)(2,1)}, u32[]{:S(2)}, u32[]{:S(2)}) collective-permute-start(bf16[2,128,512]{2,1,0:T(8,128)(2,1)S(1)} %get-tuple-element.37.refs_1_), channel_id=1, source_target_pairs={{0,4},{5,1},{4,8},{9,5},{8,12},{13,9},{12,14},{15,13},{14,10},{11,... | collective-permute-start | bytes 786440 | tf_op jit(solution)/shard_map/ppermute | solution.py:103
  11.3 1.6 %collective-permute-start.3 = (bf16[2,128,512]{2,1,0:T(8,128)(2,1)}, bf16[2,128,512]{2,1,0:T(8,128)(2,1)}, u32[]{:S(2)}, u32[]{:S(2)}) collective-permute-start(bf16[2,128,512]{2,1,0:T(8,128)(2,1)} %get-tuple-element.26.refs_0_), channel_id=1, source_target_pairs={{0,4},{5,1},{4,8},{9,5},{8,12},{13,9},{12,14},{15,13},{14,10},{11,... | collective-permute-start | bytes 786440 | tf_op jit(solution)/shard_map/ppermute | solution.py:103
  15.2 1.2 dynamic-slice_bitcast_fusion
  17.0 2.7 %gather_fusion = bf16[16,2,16384]{2,1,0:T(2,128)(2,1)S(1)} fusion(bf16[32,2,16384]{2,1,0:T(2,128)(2,1)S(1)} %copy-done, s32[1024]{0:T(1024)S(1)} %pad_clamp_fusion), kind=kCustom, calls=%fused_computation | custom fusion | bytes 2097216 | tf_op jit(solution)/shard_map/gather | solution.py:127
  19.7 1.6 %reshape.216 = bf16[16,2,32,512]{3,2,1,0:T(8,128)(2,1)} reshape(bf16[16,2,16384]{2,1,0:T(2,128)(2,1)S(1)} %gather_fusion) | data formatting | bytes 2097152 | tf_op jit(solution)/shard_map/reshape | solution.py:128
  21.3 3.9 %all-to-all-start = ((bf16[16,2,32,512]{3,2,1,0:T(8,128)(2,1)}), bf16[16,2,32,512]{3,2,1,0:T(8,128)(2,1)S(1)}, u32[]{:S(2)}, u32[]{:S(2)}) async-start(bf16[16,2,32,512]{3,2,1,0:T(8,128)(2,1)} %reshape.216), calls=%async_computation | async-start | bytes 2097152 | tf_op jit(solution)/shard_map/all_to_all | solution.py:136
  25.2 1.7 %broadcast_select_fusion.4.refs_3_.refs_1_ = bf16[2,128,512]{2,1,0:T(8,128)(2,1)} fusion(bf16[2,128,512]{2,1,0:T(8,128)(2,1)} %bitcast.48, bf16[2,128,512]{2,1,0:T(8,128)(2,1)} %collective-permute-done.13, pred[]{:T(512)S(6)} %eq.42), kind=kLoop, calls=%fused_computation.14 | loop fusion | flops 131072 | bytes 786433 | tf_op jit(solution)/shard_map/jit(_where)/select_n | solution.py:96
  26.9 1.9 %collective-permute-start.14 = (bf16[2,128,512]{2,1,0:T(8,128)(2,1)}, bf16[2,128,512]{2,1,0:T(8,128)(2,1)}, u32[]{:S(2)}, u32[]{:S(2)}) collective-permute-start(bf16[2,128,512]{2,1,0:T(8,128)(2,1)} %broadcast_select_fusion.4.refs_3_.refs_1_), channel_id=1, source_target_pairs={{0,4},{5,1},{4,8},{9,5},{8,12},{13,9},{12,14},{15,13},{14,10},{11,... | collective-permute-start | bytes 786440 | tf_op jit(solution)/shard_map/ppermute | solution.py:103
  28.8 1.0 broadcast_select_fusion.6.refs_2_.refs_0_
  29.8 1.5 %collective-permute-start.4 = (bf16[2,128,512]{2,1,0:T(8,128)(2,1)S(1)}, bf16[2,128,512]{2,1,0:T(8,128)(2,1)S(1)}, u32[]{:S(2)}, u32[]{:S(2)}) collective-permute-start(bf16[2,128,512]{2,1,0:T(8,128)(2,1)S(1)} %broadcast_select_fusion.6.refs_2_.refs_0_), channel_id=1, source_target_pairs={{0,4},{5,1},{4,8},{9,5},{8,12},{13,9},{12,14},{15,13},{14,10},{11,... | collective-permute-start | bytes 786440 | tf_op jit(solution)/shard_map/ppermute | solution.py:103
  31.3 1.6 %broadcast_select_fusion = bf16[2,131072]{1,0:T(2,128)(2,1)S(1)} fusion(bf16[2,131072]{1,0:T(2,128)(2,1)} %collective-permute-done.2, pred[]{:T(512)S(6)} %eq.43, bf16[1,3,2,262144]{3,2,1,0:T(2,128)(2,1)} %param.15, s32[]{:T(128)S(6)} %select_n.185), kind=kLoop, calls=%fused_computation.1 | loop fusion | flops 262144 | bytes 1572869 | tf_op jit(solution)/shard_map/jit(_where)/select_n | solution.py:76
  33.3 0.8 copy.31
  34.1 14.8 %collective-permute-done.4 = bf16[2,128,512]{2,1,0:T(8,128)(2,1)S(1)} collective-permute-done((bf16[2,128,512]{2,1,0:T(8,128)(2,1)S(1)}, bf16[2,128,512]{2,1,0:T(8,128)(2,1)S(1)}, u32[]{:S(2)}, u32[]{:S(2)}) %collective-permute-start.4) | collective-permute-done | bytes 262176 | tf_op jit(solution)/shard_map/ppermute | solution.py:103
  49.6 7.1 %collective-permute-start.5 = (bf16[2,128,512]{2,1,0:T(8,128)(2,1)}, bf16[2,128,512]{2,1,0:T(8,128)(2,1)S(1)}, u32[]{:S(2)}, u32[]{:S(2)}) collective-permute-start(bf16[2,128,512]{2,1,0:T(8,128)(2,1)} %broadcast_select_fusion.5.refs_4_.refs_2_.refs_0_), channel_id=1, source_target_pairs={{0,4},{5,1},{4,8},{9,5},{8,12},{13,9},{12,14},{15,13},{14,10},{11,... | collective-permute-start | bytes 786440 | tf_op jit(solution)/shard_map/ppermute | solution.py:103
  56.8 1.0 broadcast_select_fusion.3.refs_5_.refs_3_.refs_1_
  57.8 2.5 %collective-permute-start.15 = (bf16[2,128,512]{2,1,0:T(8,128)(2,1)S(1)}, bf16[2,128,512]{2,1,0:T(8,128)(2,1)S(1)}, u32[]{:S(2)}, u32[]{:S(2)}) collective-permute-start(bf16[2,128,512]{2,1,0:T(8,128)(2,1)S(1)} %broadcast_select_fusion.3.refs_5_.refs_3_.refs_1_), channel_id=1, source_target_pairs={{0,4},{5,1},{4,8},{9,5},{8,12},{13,9},{12,14},{15,13},{14,10},{11,... | collective-permute-start | bytes 786440 | tf_op jit(solution)/shard_map/ppermute | solution.py:103
  61.0 2.5 %collective-permute-start.6 = (bf16[2,128,512]{2,1,0:T(8,128)(2,1)S(1)}, bf16[2,128,512]{2,1,0:T(8,128)(2,1)S(1)}, u32[]{:S(2)}, u32[]{:S(2)}) collective-permute-start(bf16[2,128,512]{2,1,0:T(8,128)(2,1)S(1)} %collective-permute-done.5.refs_6_.refs_4_.refs_2_), channel_id=1, source_target_pairs={{0,4},{5,1},{4,8},{9,5},{8,12},{13,9},{12,14},{15,13},{14,10},{11,... | collective-permute-start | bytes 786440 | tf_op jit(solution)/shard_map/ppermute | solution.py:103
  63.5 0.8 collective-permute-done.15.refs_7_.refs_5_.refs_3_
  64.2 2.5 %collective-permute-start.16 = (bf16[2,128,512]{2,1,0:T(8,128)(2,1)S(1)}, bf16[2,128,512]{2,1,0:T(8,128)(2,1)S(1)}, u32[]{:S(2)}, u32[]{:S(2)}) collective-permute-start(bf16[2,128,512]{2,1,0:T(8,128)(2,1)S(1)} %collective-permute-done.15.refs_7_.refs_5_.refs_3_), channel_id=1, source_target_pairs={{0,4},{5,1},{4,8},{9,5},{8,12},{13,9},{12,14},{15,13},{14,10},{11,... | collective-permute-start | bytes 786440 | tf_op jit(solution)/shard_map/ppermute | solution.py:103
  67.2 1.9 %collective-permute-done.6.refs_8_.refs_6_.refs_4_ = bf16[2,128,512]{2,1,0:T(8,128)(2,1)S(1)} collective-permute-done((bf16[2,128,512]{2,1,0:T(8,128)(2,1)S(1)}, bf16[2,128,512]{2,1,0:T(8,128)(2,1)S(1)}, u32[]{:S(2)}, u32[]{:S(2)}) %collective-permute-start.6) | collective-permute-done | bytes 262176 | tf_op jit(solution)/shard_map/ppermute | solution.py:103
  69.8 2.1 %collective-permute-done.16.refs_9_.refs_7_.refs_5_ = bf16[2,128,512]{2,1,0:T(8,128)(2,1)S(1)} collective-permute-done((bf16[2,128,512]{2,1,0:T(8,128)(2,1)S(1)}, bf16[2,128,512]{2,1,0:T(8,128)(2,1)S(1)}, u32[]{:S(2)}, u32[]{:S(2)}) %collective-permute-start.16) | collective-permute-done | bytes 262176 | tf_op jit(solution)/shard_map/ppermute | solution.py:103
  71.9 1.2 collective-permute-start.17
  73.1 1.6 %collective-permute-start.12 = (bf16[16,2,32,512]{3,2,1,0:T(8,128)(2,1)S(1)}, bf16[16,2,32,512]{3,2,1,0:T(8,128)(2,1)S(1)}, u32[]{:S(2)}, u32[]{:S(2)}) collective-permute-start(bf16[16,2,32,512]{3,2,1,0:T(8,128)(2,1)S(1)} %all-to-all-done.refs_0_), channel_id=1, source_target_pairs={{0,16},{16,0},{1,17},{17,1},{2,18},{18,2},{3,19},{19,3},{4,20},{20... | collective-permute-start | bytes 3145736 | tf_op jit(solution)/shard_map/ppermute | solution.py:142
  74.7 0.8 collective-permute-done.7.refs_10_.refs_8_.refs_6_
  75.5 1.1 collective-permute-start.8
  76.6 1.7 %collective-permute-done.17.refs_11_.refs_9_.refs_7_ = bf16[2,128,512]{2,1,0:T(8,128)(2,1)S(1)} collective-permute-done((bf16[2,128,512]{2,1,0:T(8,128)(2,1)S(1)}, bf16[2,128,512]{2,1,0:T(8,128)(2,1)S(1)}, u32[]{:S(2)}, u32[]{:S(2)}) %collective-permute-start.17) | collective-permute-done | bytes 262176 | tf_op jit(solution)/shard_map/ppermute | solution.py:103
  78.3 1.2 collective-permute-start.18
  79.5 2.4 %collective-permute-done.8.refs_12_.refs_10_.refs_8_ = bf16[2,128,512]{2,1,0:T(8,128)(2,1)S(1)} collective-permute-done((bf16[2,128,512]{2,1,0:T(8,128)(2,1)S(1)}, bf16[2,128,512]{2,1,0:T(8,128)(2,1)S(1)}, u32[]{:S(2)}, u32[]{:S(2)}) %collective-permute-start.8) | collective-permute-done | bytes 262176 | tf_op jit(solution)/shard_map/ppermute | solution.py:103
  81.8 1.1 collective-permute-start.9
  83.0 1.7 %collective-permute-done.18.refs_13_.refs_11_.refs_9_ = bf16[2,128,512]{2,1,0:T(8,128)(2,1)S(1)} collective-permute-done((bf16[2,128,512]{2,1,0:T(8,128)(2,1)S(1)}, bf16[2,128,512]{2,1,0:T(8,128)(2,1)S(1)}, u32[]{:S(2)}, u32[]{:S(2)}) %collective-permute-start.18) | collective-permute-done | bytes 262176 | tf_op jit(solution)/shard_map/ppermute | solution.py:103
  84.6 1.2 collective-permute-start.19
  85.8 2.4 %collective-permute-done.9.refs_14_.refs_12_.refs_10_ = bf16[2,128,512]{2,1,0:T(8,128)(2,1)S(1)} collective-permute-done((bf16[2,128,512]{2,1,0:T(8,128)(2,1)S(1)}, bf16[2,128,512]{2,1,0:T(8,128)(2,1)S(1)}, u32[]{:S(2)}, u32[]{:S(2)}) %collective-permute-start.9) | collective-permute-done | bytes 262176 | tf_op jit(solution)/shard_map/ppermute | solution.py:103
  88.2 1.1 collective-permute-start.10
  89.3 1.7 %collective-permute-done.19.refs_15_.refs_13_.refs_11_ = bf16[2,128,512]{2,1,0:T(8,128)(2,1)S(1)} collective-permute-done((bf16[2,128,512]{2,1,0:T(8,128)(2,1)S(1)}, bf16[2,128,512]{2,1,0:T(8,128)(2,1)S(1)}, u32[]{:S(2)}, u32[]{:S(2)}) %collective-permute-start.19) | collective-permute-done | bytes 262176 | tf_op jit(solution)/shard_map/ppermute | solution.py:103
  91.0 1.2 collective-permute-start.20
  92.2 2.4 %collective-permute-done.10.refs_14_.refs_12_ = bf16[2,128,512]{2,1,0:T(8,128)(2,1)S(1)} collective-permute-done((bf16[2,128,512]{2,1,0:T(8,128)(2,1)S(1)}, bf16[2,128,512]{2,1,0:T(8,128)(2,1)S(1)}, u32[]{:S(2)}, u32[]{:S(2)}) %collective-permute-start.10) | collective-permute-done | bytes 262176 | tf_op jit(solution)/shard_map/ppermute | solution.py:103
  94.6 1.1 collective-permute-start.11
  95.7 1.7 %collective-permute-done.20.refs_15_.refs_13_ = bf16[2,128,512]{2,1,0:T(8,128)(2,1)S(1)} collective-permute-done((bf16[2,128,512]{2,1,0:T(8,128)(2,1)S(1)}, bf16[2,128,512]{2,1,0:T(8,128)(2,1)S(1)}, u32[]{:S(2)}, u32[]{:S(2)}) %collective-permute-start.20) | collective-permute-done | bytes 262176 | tf_op jit(solution)/shard_map/ppermute | solution.py:103
  97.4 1.2 collective-permute-start.21
  99.1 1.8 %collective-permute-done.11.refs_14_ = bf16[2,128,512]{2,1,0:T(8,128)(2,1)S(1)} collective-permute-done((bf16[2,128,512]{2,1,0:T(8,128)(2,1)S(1)}, bf16[2,128,512]{2,1,0:T(8,128)(2,1)S(1)}, u32[]{:S(2)}, u32[]{:S(2)}) %collective-permute-start.11) | collective-permute-done | bytes 262176 | tf_op jit(solution)/shard_map/ppermute | solution.py:103
  101.0 2.1 %shard_map.158 = (bf16[2,2,512,512]{3,2,1,0:T(8,128)(2,1)S(1)}, f32[2]{0:T(128)S(1)}) custom-call(s32[32]{0:T(128)S(1)} %copy-done.4, s32[32]{0:T(128)S(1)} %reshape.217.list_ref, s32[6]{0:T(128)S(1)} %stack.27.where_ref, bf16[16,2,32,512]{3,2,1,0:T(8,128)(2,1)S(1)} %all-to-all-done.refs_0_, bf16[16,2,32,512]{3,2,1,0:T(8,128)(2,1)S(1)} %collective-permute-done.12.refs_1_), custom_call_target="tpu_custom_call" | custom-call | flops 2000000000 | bytes 6000000 | tf_op jit(solution)/shard_map/pallas_call | solution.py:280
  104.4 6.2 %shard_map.159.refs_38_ = f32[2,512,512]{2,1,0:T(8,128)S(1)} custom-call(s32[6]{0:T(128)S(1)} %stack.27.where_ref, f32[2]{0:T(128)S(1)} %get-tuple-element.34.sigma_ref, bf16[2,128,512]{2,1,0:T(8,128)(2,1)} %get-tuple-element.26.refs_0_, bf16[2,128,512]{2,1,0:T(8,128)(2,1)S(1)} %get-tuple-element.37.refs_1_, bf16[2,128,512]{2,1,0:T(8,128)(2,1)S(1)} %copy-done.2, ...), custom_call_target="tpu_custom_call" | custom-call | flops 5000000000 | bytes 10000000 | tf_op jit(solution)/shard_map/pallas_call | solution.py:300
  110.6 6.3 %shard_map.160.refs_38_ = f32[2,512,512]{2,1,0:T(8,128)S(1)} custom-call(s32[6]{0:T(128)S(1)} %stack.27.where_ref, f32[2]{0:T(128)S(1)} %get-tuple-element.34.sigma_ref, bf16[2,128,512]{2,1,0:T(8,128)(2,1)S(1)} %copy-done.2, bf16[2,128,512]{2,1,0:T(8,128)(2,1)} %broadcast_select_fusion.4.refs_3_.refs_1_, bf16[2,128,512]{2,1,0:T(8,128)(2,1)S(1)} %copy-done.3, ...), custom_call_target="tpu_custom_call" | custom-call | flops 5000000000 | bytes 10000000 | tf_op jit(solution)/shard_map/pallas_call | solution.py:300
  117.0 6.3 %shard_map.161 = (f32[2]{0:T(128)}, f32[2]{0:T(128)}) custom-call(s32[6]{0:T(128)S(1)} %stack.27.where_ref, f32[2]{0:T(128)S(1)} %get-tuple-element.34.sigma_ref, bf16[2,128,512]{2,1,0:T(8,128)(2,1)S(1)} %copy-done.3, bf16[2,128,512]{2,1,0:T(8,128)(2,1)S(1)} %broadcast_select_fusion.3.refs_5_.refs_3_.refs_1_, ...), custom_call_target="tpu_custom_call" | custom-call | flops 5000000000 | bytes 10000000 | tf_op jit(solution)/shard_map/pallas_call | solution.py:300
  (94 shorter events, 9.9 us)
Async XLA Ops:
  2.2 2.1 %collective-permute-start = (bf16[2,131072]{1,0:T(2,128)(2,1)S(1)}, bf16[2,131072]{1,0:T(2,128)(2,1)S(1)}, u32[]{:S(2)}, u32[]{:S(2)}) collective-permute-start(bf16[2,131072]{1,0:T(2,128)(2,1)S(1)} %dynamic-slice_bitcast_fusion.2), channel_id=1, source_target_pairs={{0,1},{1,0},{2,3},{3,2},{4,5},{5,4},{6,7},{7,6},{8,9},{9,8},{10,11... | collective-permute-start | bytes 1572872 | tf_op jit(solution)/shard_map/ppermute | solution.py:75
  7.5 5.4 %collective-permute-start.1 = (bf16[2,131072]{1,0:T(2,128)(2,1)S(1)}, bf16[2,131072]{1,0:T(2,128)(2,1)S(1)}, u32[]{:S(2)}, u32[]{:S(2)}) collective-permute-start(bf16[2,131072]{1,0:T(2,128)(2,1)S(1)} %dynamic-slice_bitcast_fusion.1), channel_id=1, source_target_pairs={{0,1},{1,0},{2,3},{3,2},{4,5},{5,4},{6,7},{7,6},{8,9},{9,8},{10,11... | collective-permute-start | bytes 1572872 | tf_op jit(solution)/shard_map/ppermute | solution.py:75
  8.4 16.8 %collective-permute-start.13 = (bf16[2,128,512]{2,1,0:T(8,128)(2,1)S(1)}, bf16[2,128,512]{2,1,0:T(8,128)(2,1)}, u32[]{:S(2)}, u32[]{:S(2)}) collective-permute-start(bf16[2,128,512]{2,1,0:T(8,128)(2,1)S(1)} %get-tuple-element.37.refs_1_), channel_id=1, source_target_pairs={{0,4},{5,1},{4,8},{9,5},{8,12},{13,9},{12,14},{15,13},{14,10},{11,... | collective-permute-start | bytes 786440 | tf_op jit(solution)/shard_map/ppermute | solution.py:103
  11.3 17.5 %collective-permute-start.3 = (bf16[2,128,512]{2,1,0:T(8,128)(2,1)}, bf16[2,128,512]{2,1,0:T(8,128)(2,1)}, u32[]{:S(2)}, u32[]{:S(2)}) collective-permute-start(bf16[2,128,512]{2,1,0:T(8,128)(2,1)} %get-tuple-element.26.refs_0_), channel_id=1, source_target_pairs={{0,4},{5,1},{4,8},{9,5},{8,12},{13,9},{12,14},{15,13},{14,10},{11,... | collective-permute-start | bytes 786440 | tf_op jit(solution)/shard_map/ppermute | solution.py:103
  16.4 14.9 %collective-permute-start.2 = (bf16[2,131072]{1,0:T(2,128)(2,1)}, bf16[2,131072]{1,0:T(2,128)(2,1)}, u32[]{:S(2)}, u32[]{:S(2)}) collective-permute-start(bf16[2,131072]{1,0:T(2,128)(2,1)} %dynamic-slice_bitcast_fusion), channel_id=1, source_target_pairs={{0,1},{1,0},{2,3},{3,2},{4,5},{5,4},{6,7},{7,6},{8,9},{9,8},{10,11... | collective-permute-start | bytes 1572872 | tf_op jit(solution)/shard_map/ppermute | solution.py:75
  21.3 28.4 %all-to-all-start = ((bf16[16,2,32,512]{3,2,1,0:T(8,128)(2,1)}), bf16[16,2,32,512]{3,2,1,0:T(8,128)(2,1)S(1)}, u32[]{:S(2)}, u32[]{:S(2)}) async-start(bf16[16,2,32,512]{3,2,1,0:T(8,128)(2,1)} %reshape.216), calls=%async_computation | async-start | bytes 2097152 | tf_op jit(solution)/shard_map/all_to_all | solution.py:136
  26.9 74.1 %copy-start.4 = (s32[32]{0:T(128)S(1)}, s32[32]{0:T(128)}, u32[]{:S(2)}) copy-start(s32[32]{0:T(128)} %cut_ref.1) | copy-start | bytes 388
  26.9 29.9 %collective-permute-start.14 = (bf16[2,128,512]{2,1,0:T(8,128)(2,1)}, bf16[2,128,512]{2,1,0:T(8,128)(2,1)}, u32[]{:S(2)}, u32[]{:S(2)}) collective-permute-start(bf16[2,128,512]{2,1,0:T(8,128)(2,1)} %broadcast_select_fusion.4.refs_3_.refs_1_), channel_id=1, source_target_pairs={{0,4},{5,1},{4,8},{9,5},{8,12},{13,9},{12,14},{15,13},{14,10},{11,... | collective-permute-start | bytes 786440 | tf_op jit(solution)/shard_map/ppermute | solution.py:103
  29.8 19.1 %collective-permute-start.4 = (bf16[2,128,512]{2,1,0:T(8,128)(2,1)S(1)}, bf16[2,128,512]{2,1,0:T(8,128)(2,1)S(1)}, u32[]{:S(2)}, u32[]{:S(2)}) collective-permute-start(bf16[2,128,512]{2,1,0:T(8,128)(2,1)S(1)} %broadcast_select_fusion.6.refs_2_.refs_0_), channel_id=1, source_target_pairs={{0,4},{5,1},{4,8},{9,5},{8,12},{13,9},{12,14},{15,13},{14,10},{11,... | collective-permute-start | bytes 786440 | tf_op jit(solution)/shard_map/ppermute | solution.py:103
  49.6 11.3 %collective-permute-start.5 = (bf16[2,128,512]{2,1,0:T(8,128)(2,1)}, bf16[2,128,512]{2,1,0:T(8,128)(2,1)S(1)}, u32[]{:S(2)}, u32[]{:S(2)}) collective-permute-start(bf16[2,128,512]{2,1,0:T(8,128)(2,1)} %broadcast_select_fusion.5.refs_4_.refs_2_.refs_0_), channel_id=1, source_target_pairs={{0,4},{5,1},{4,8},{9,5},{8,12},{13,9},{12,14},{15,13},{14,10},{11,... | collective-permute-start | bytes 786440 | tf_op jit(solution)/shard_map/ppermute | solution.py:103
  57.8 46.6 %copy-start.2 = (bf16[2,128,512]{2,1,0:T(8,128)(2,1)S(1)}, bf16[2,128,512]{2,1,0:T(8,128)(2,1)}, u32[]{:S(2)}) copy-start(bf16[2,128,512]{2,1,0:T(8,128)(2,1)} %copy-done.1) | copy-start | bytes 786436
  57.8 46.6 %copy-start.3 = (bf16[2,128,512]{2,1,0:T(8,128)(2,1)S(1)}, bf16[2,128,512]{2,1,0:T(8,128)(2,1)}, u32[]{:S(2)}) copy-start(bf16[2,128,512]{2,1,0:T(8,128)(2,1)} %broadcast_select_fusion.5.refs_4_.refs_2_.refs_0_) | copy-start | bytes 786436
  57.8 46.6 %copy-start.5 = (f32[4,2,128,512]{3,2,1,0:T(8,128)S(1)}, f32[4,2,128,512]{3,2,1,0:T(8,128)}, u32[]{:S(2)}) copy-start(f32[4,2,128,512]{3,2,1,0:T(8,128)} %constant.174.clone.refs_37_) | copy-start | bytes 6291460
  57.8 46.6 %copy-start.6 = (bf16[4,512,256]{2,1,0:T(8,128)(2,1)S(1)}, bf16[4,512,256]{2,1,0:T(8,128)(2,1)}, u32[]{:S(2)}) copy-start(bf16[4,512,256]{2,1,0:T(8,128)(2,1)} %constant.179.refs_36_) | copy-start | bytes 3145732
  57.8 6.4 %collective-permute-start.15 = (bf16[2,128,512]{2,1,0:T(8,128)(2,1)S(1)}, bf16[2,128,512]{2,1,0:T(8,128)(2,1)S(1)}, u32[]{:S(2)}, u32[]{:S(2)}) collective-permute-start(bf16[2,128,512]{2,1,0:T(8,128)(2,1)S(1)} %broadcast_select_fusion.3.refs_5_.refs_3_.refs_1_), channel_id=1, source_target_pairs={{0,4},{5,1},{4,8},{9,5},{8,12},{13,9},{12,14},{15,13},{14,10},{11,... | collective-permute-start | bytes 786440 | tf_op jit(solution)/shard_map/ppermute | solution.py:103
  60.4 6.4 %collective-permute-start.40 = (bf16[2,128,512]{2,1,0:T(8,128)(2,1)}, bf16[2,128,512]{2,1,0:T(8,128)(2,1)S(1)}, u32[]{:S(2)}, u32[]{:S(2)}) collective-permute-start(bf16[2,128,512]{2,1,0:T(8,128)(2,1)} %get-tuple-element.26.refs_0_), channel_id=1, source_target_pairs={{0,1},{1,0},{2,3},{3,2},{4,5},{5,4},{6,7},{7,6},{8,9},{9,8},{10,11... | collective-permute-start | bytes 786440 | tf_op jit(solution)/shard_map/ppermute | solution.py:104
  61.0 8.1 %collective-permute-start.6 = (bf16[2,128,512]{2,1,0:T(8,128)(2,1)S(1)}, bf16[2,128,512]{2,1,0:T(8,128)(2,1)S(1)}, u32[]{:S(2)}, u32[]{:S(2)}) collective-permute-start(bf16[2,128,512]{2,1,0:T(8,128)(2,1)S(1)} %collective-permute-done.5.refs_6_.refs_4_.refs_2_), channel_id=1, source_target_pairs={{0,4},{5,1},{4,8},{9,5},{8,12},{13,9},{12,14},{15,13},{14,10},{11,... | collective-permute-start | bytes 786440 | tf_op jit(solution)/shard_map/ppermute | solution.py:103
  63.5 6.4 %collective-permute-start.41 = (bf16[2,128,512]{2,1,0:T(8,128)(2,1)S(1)}, bf16[2,128,512]{2,1,0:T(8,128)(2,1)S(1)}, u32[]{:S(2)}, u32[]{:S(2)}) collective-permute-start(bf16[2,128,512]{2,1,0:T(8,128)(2,1)S(1)} %get-tuple-element.37.refs_1_), channel_id=1, source_target_pairs={{0,1},{1,0},{2,3},{3,2},{4,5},{5,4},{6,7},{7,6},{8,9},{9,8},{10,11... | collective-permute-start | bytes 786440 | tf_op jit(solution)/shard_map/ppermute | solution.py:104
  64.2 7.7 %collective-permute-start.16 = (bf16[2,128,512]{2,1,0:T(8,128)(2,1)S(1)}, bf16[2,128,512]{2,1,0:T(8,128)(2,1)S(1)}, u32[]{:S(2)}, u32[]{:S(2)}) collective-permute-start(bf16[2,128,512]{2,1,0:T(8,128)(2,1)S(1)} %collective-permute-done.15.refs_7_.refs_5_.refs_3_), channel_id=1, source_target_pairs={{0,4},{5,1},{4,8},{9,5},{8,12},{13,9},{12,14},{15,13},{14,10},{11,... | collective-permute-start | bytes 786440 | tf_op jit(solution)/shard_map/ppermute | solution.py:103
  66.7 6.4 %collective-permute-start.39 = (bf16[2,128,512]{2,1,0:T(8,128)(2,1)}, bf16[2,128,512]{2,1,0:T(8,128)(2,1)S(1)}, u32[]{:S(2)}, u32[]{:S(2)}) collective-permute-start(bf16[2,128,512]{2,1,0:T(8,128)(2,1)} %broadcast_select_fusion.4.refs_3_.refs_1_), channel_id=1, source_target_pairs={{0,1},{1,0},{2,3},{3,2},{4,5},{5,4},{6,7},{7,6},{8,9},{9,8},{10,11... | collective-permute-start | bytes 786440 | tf_op jit(solution)/shard_map/ppermute | solution.py:104
  66.7 6.4 %collective-permute-start.38 = (bf16[2,128,512]{2,1,0:T(8,128)(2,1)}, bf16[2,128,512]{2,1,0:T(8,128)(2,1)S(1)}, u32[]{:S(2)}, u32[]{:S(2)}) collective-permute-start(bf16[2,128,512]{2,1,0:T(8,128)(2,1)} %copy-done.1), channel_id=1, source_target_pairs={{0,1},{1,0},{2,3},{3,2},{4,5},{5,4},{6,7},{7,6},{8,9},{9,8},{10,11... | collective-permute-start | bytes 786440 | tf_op jit(solution)/shard_map/ppermute | solution.py:104
  69.1 6.4 %collective-permute-start.7 = (bf16[2,128,512]{2,1,0:T(8,128)(2,1)S(1)}, bf16[2,128,512]{2,1,0:T(8,128)(2,1)S(1)}, u32[]{:S(2)}, u32[]{:S(2)}) collective-permute-start(bf16[2,128,512]{2,1,0:T(8,128)(2,1)S(1)} %collective-permute-done.6.refs_8_.refs_6_.refs_4_), channel_id=1, source_target_pairs={{0,4},{5,1},{4,8},{9,5},{8,12},{13,9},{12,14},{15,13},{14,10},{11,... | collective-permute-start | bytes 786440 | tf_op jit(solution)/shard_map/ppermute | solution.py:103
  69.8 6.8 %collective-permute-start.23 = (bf16[2,128,512]{2,1,0:T(8,128)(2,1)S(1)}, bf16[2,128,512]{2,1,0:T(8,128)(2,1)S(1)}, u32[]{:S(2)}, u32[]{:S(2)}) collective-permute-start(bf16[2,128,512]{2,1,0:T(8,128)(2,1)S(1)} %broadcast_select_fusion.3.refs_5_.refs_3_.refs_1_), channel_id=1, source_target_pairs={{0,1},{1,0},{2,3},{3,2},{4,5},{5,4},{6,7},{7,6},{8,9},{9,8},{10,11... | collective-permute-start | bytes 786440 | tf_op jit(solution)/shard_map/ppermute | solution.py:104
  71.9 6.4 %collective-permute-start.17 = (bf16[2,128,512]{2,1,0:T(8,128)(2,1)S(1)}, bf16[2,128,512]{2,1,0:T(8,128)(2,1)S(1)}, u32[]{:S(2)}, u32[]{:S(2)}) collective-permute-start(bf16[2,128,512]{2,1,0:T(8,128)(2,1)S(1)} %collective-permute-done.16.refs_9_.refs_7_.refs_5_), channel_id=1, source_target_pairs={{0,4},{5,1},{4,8},{9,5},{8,12},{13,9},{12,14},{15,13},{14,10},{11,... | collective-permute-start | bytes 786440 | tf_op jit(solution)/shard_map/ppermute | solution.py:103
  73.1 6.4 %collective-permute-start.25 = (bf16[2,128,512]{2,1,0:T(8,128)(2,1)S(1)}, bf16[2,128,512]{2,1,0:T(8,128)(2,1)S(1)}, u32[]{:S(2)}, u32[]{:S(2)}) collective-permute-start(bf16[2,128,512]{2,1,0:T(8,128)(2,1)S(1)} %collective-permute-done.15.refs_7_.refs_5_.refs_3_), channel_id=1, source_target_pairs={{0,1},{1,0},{2,3},{3,2},{4,5},{5,4},{6,7},{7,6},{8,9},{9,8},{10,11... | collective-permute-start | bytes 786440 | tf_op jit(solution)/shard_map/ppermute | solution.py:104
  73.1 25.6 %collective-permute-start.12 = (bf16[16,2,32,512]{3,2,1,0:T(8,128)(2,1)S(1)}, bf16[16,2,32,512]{3,2,1,0:T(8,128)(2,1)S(1)}, u32[]{:S(2)}, u32[]{:S(2)}) collective-permute-start(bf16[16,2,32,512]{3,2,1,0:T(8,128)(2,1)S(1)} %all-to-all-done.refs_0_), channel_id=1, source_target_pairs={{0,16},{16,0},{1,17},{17,1},{2,18},{18,2},{3,19},{19,3},{4,20},{20... | collective-permute-start | bytes 3145736 | tf_op jit(solution)/shard_map/ppermute | solution.py:142
  75.5 6.4 %collective-permute-start.8 = (bf16[2,128,512]{2,1,0:T(8,128)(2,1)S(1)}, bf16[2,128,512]{2,1,0:T(8,128)(2,1)S(1)}, u32[]{:S(2)}, u32[]{:S(2)}) collective-permute-start(bf16[2,128,512]{2,1,0:T(8,128)(2,1)S(1)} %collective-permute-done.7.refs_10_.refs_8_.refs_6_), channel_id=1, source_target_pairs={{0,4},{5,1},{4,8},{9,5},{8,12},{13,9},{12,14},{15,13},{14,10},{11,... | collective-permute-start | bytes 786440 | tf_op jit(solution)/shard_map/ppermute | solution.py:103
  76.6 6.4 %collective-permute-start.27 = (bf16[2,128,512]{2,1,0:T(8,128)(2,1)S(1)}, bf16[2,128,512]{2,1,0:T(8,128)(2,1)S(1)}, u32[]{:S(2)}, u32[]{:S(2)}) collective-permute-start(bf16[2,128,512]{2,1,0:T(8,128)(2,1)S(1)} %collective-permute-done.16.refs_9_.refs_7_.refs_5_), channel_id=1, source_target_pairs={{0,1},{1,0},{2,3},{3,2},{4,5},{5,4},{6,7},{7,6},{8,9},{9,8},{10,11... | collective-permute-start | bytes 786440 | tf_op jit(solution)/shard_map/ppermute | solution.py:104
  78.3 6.4 %collective-permute-start.18 = (bf16[2,128,512]{2,1,0:T(8,128)(2,1)S(1)}, bf16[2,128,512]{2,1,0:T(8,128)(2,1)S(1)}, u32[]{:S(2)}, u32[]{:S(2)}) collective-permute-start(bf16[2,128,512]{2,1,0:T(8,128)(2,1)S(1)} %collective-permute-done.17.refs_11_.refs_9_.refs_7_), channel_id=1, source_target_pairs={{0,4},{5,1},{4,8},{9,5},{8,12},{13,9},{12,14},{15,13},{14,10},{11,... | collective-permute-start | bytes 786440 | tf_op jit(solution)/shard_map/ppermute | solution.py:103
  79.5 6.4 %collective-permute-start.29 = (bf16[2,128,512]{2,1,0:T(8,128)(2,1)S(1)}, bf16[2,128,512]{2,1,0:T(8,128)(2,1)S(1)}, u32[]{:S(2)}, u32[]{:S(2)}) collective-permute-start(bf16[2,128,512]{2,1,0:T(8,128)(2,1)S(1)} %collective-permute-done.17.refs_11_.refs_9_.refs_7_), channel_id=1, source_target_pairs={{0,1},{1,0},{2,3},{3,2},{4,5},{5,4},{6,7},{7,6},{8,9},{9,8},{10,11... | collective-permute-start | bytes 786440 | tf_op jit(solution)/shard_map/ppermute | solution.py:104
  81.8 6.4 %collective-permute-start.9 = (bf16[2,128,512]{2,1,0:T(8,128)(2,1)S(1)}, bf16[2,128,512]{2,1,0:T(8,128)(2,1)S(1)}, u32[]{:S(2)}, u32[]{:S(2)}) collective-permute-start(bf16[2,128,512]{2,1,0:T(8,128)(2,1)S(1)} %collective-permute-done.8.refs_12_.refs_10_.refs_8_), channel_id=1, source_target_pairs={{0,4},{5,1},{4,8},{9,5},{8,12},{13,9},{12,14},{15,13},{14,10},{11,... | collective-permute-start | bytes 786440 | tf_op jit(solution)/shard_map/ppermute | solution.py:103
  83.0 6.4 %collective-permute-start.22 = (bf16[2,128,512]{2,1,0:T(8,128)(2,1)}, bf16[2,128,512]{2,1,0:T(8,128)(2,1)S(1)}, u32[]{:S(2)}, u32[]{:S(2)}) collective-permute-start(bf16[2,128,512]{2,1,0:T(8,128)(2,1)} %broadcast_select_fusion.5.refs_4_.refs_2_.refs_0_), channel_id=1, source_target_pairs={{0,1},{1,0},{2,3},{3,2},{4,5},{5,4},{6,7},{7,6},{8,9},{9,8},{10,11... | collective-permute-start | bytes 786440 | tf_op jit(solution)/shard_map/ppermute | solution.py:104
  84.6 6.4 %collective-permute-start.19 = (bf16[2,128,512]{2,1,0:T(8,128)(2,1)S(1)}, bf16[2,128,512]{2,1,0:T(8,128)(2,1)S(1)}, u32[]{:S(2)}, u32[]{:S(2)}) collective-permute-start(bf16[2,128,512]{2,1,0:T(8,128)(2,1)S(1)} %collective-permute-done.18.refs_13_.refs_11_.refs_9_), channel_id=1, source_target_pairs={{0,4},{5,1},{4,8},{9,5},{8,12},{13,9},{12,14},{15,13},{14,10},{11,... | collective-permute-start | bytes 786440 | tf_op jit(solution)/shard_map/ppermute | solution.py:103
  85.8 6.4 %collective-permute-start.31 = (bf16[2,128,512]{2,1,0:T(8,128)(2,1)S(1)}, bf16[2,128,512]{2,1,0:T(8,128)(2,1)S(1)}, u32[]{:S(2)}, u32[]{:S(2)}) collective-permute-start(bf16[2,128,512]{2,1,0:T(8,128)(2,1)S(1)} %collective-permute-done.18.refs_13_.refs_11_.refs_9_), channel_id=1, source_target_pairs={{0,1},{1,0},{2,3},{3,2},{4,5},{5,4},{6,7},{7,6},{8,9},{9,8},{10,11... | collective-permute-start | bytes 786440 | tf_op jit(solution)/shard_map/ppermute | solution.py:104
  88.2 6.4 %collective-permute-start.10 = (bf16[2,128,512]{2,1,0:T(8,128)(2,1)S(1)}, bf16[2,128,512]{2,1,0:T(8,128)(2,1)S(1)}, u32[]{:S(2)}, u32[]{:S(2)}) collective-permute-start(bf16[2,128,512]{2,1,0:T(8,128)(2,1)S(1)} %collective-permute-done.9.refs_14_.refs_12_.refs_10_), channel_id=1, source_target_pairs={{0,4},{5,1},{4,8},{9,5},{8,12},{13,9},{12,14},{15,13},{14,10},{11,... | collective-permute-start | bytes 786440 | tf_op jit(solution)/shard_map/ppermute | solution.py:103
  89.3 6.4 %collective-permute-start.24 = (bf16[2,128,512]{2,1,0:T(8,128)(2,1)S(1)}, bf16[2,128,512]{2,1,0:T(8,128)(2,1)S(1)}, u32[]{:S(2)}, u32[]{:S(2)}) collective-permute-start(bf16[2,128,512]{2,1,0:T(8,128)(2,1)S(1)} %collective-permute-done.5.refs_6_.refs_4_.refs_2_), channel_id=1, source_target_pairs={{0,1},{1,0},{2,3},{3,2},{4,5},{5,4},{6,7},{7,6},{8,9},{9,8},{10,11... | collective-permute-start | bytes 786440 | tf_op jit(solution)/shard_map/ppermute | solution.py:104
  91.0 6.4 %collective-permute-start.20 = (bf16[2,128,512]{2,1,0:T(8,128)(2,1)S(1)}, bf16[2,128,512]{2,1,0:T(8,128)(2,1)S(1)}, u32[]{:S(2)}, u32[]{:S(2)}) collective-permute-start(bf16[2,128,512]{2,1,0:T(8,128)(2,1)S(1)} %collective-permute-done.19.refs_15_.refs_13_.refs_11_), channel_id=1, source_target_pairs={{0,4},{5,1},{4,8},{9,5},{8,12},{13,9},{12,14},{15,13},{14,10},{11,... | collective-permute-start | bytes 786440 | tf_op jit(solution)/shard_map/ppermute | solution.py:103
  92.2 6.4 %collective-permute-start.33 = (bf16[2,128,512]{2,1,0:T(8,128)(2,1)S(1)}, bf16[2,128,512]{2,1,0:T(8,128)(2,1)S(1)}, u32[]{:S(2)}, u32[]{:S(2)}) collective-permute-start(bf16[2,128,512]{2,1,0:T(8,128)(2,1)S(1)} %collective-permute-done.19.refs_15_.refs_13_.refs_11_), channel_id=1, source_target_pairs={{0,1},{1,0},{2,3},{3,2},{4,5},{5,4},{6,7},{7,6},{8,9},{9,8},{10,11... | collective-permute-start | bytes 786440 | tf_op jit(solution)/shard_map/ppermute | solution.py:104
  94.6 6.4 %collective-permute-start.11 = (bf16[2,128,512]{2,1,0:T(8,128)(2,1)S(1)}, bf16[2,128,512]{2,1,0:T(8,128)(2,1)S(1)}, u32[]{:S(2)}, u32[]{:S(2)}) collective-permute-start(bf16[2,128,512]{2,1,0:T(8,128)(2,1)S(1)} %collective-permute-done.10.refs_14_.refs_12_), channel_id=1, source_target_pairs={{0,4},{5,1},{4,8},{9,5},{8,12},{13,9},{12,14},{15,13},{14,10},{11,... | collective-permute-start | bytes 786440 | tf_op jit(solution)/shard_map/ppermute | solution.py:103
  95.7 7.4 %collective-permute-start.26 = (bf16[2,128,512]{2,1,0:T(8,128)(2,1)S(1)}, bf16[2,128,512]{2,1,0:T(8,128)(2,1)S(1)}, u32[]{:S(2)}, u32[]{:S(2)}) collective-permute-start(bf16[2,128,512]{2,1,0:T(8,128)(2,1)S(1)} %collective-permute-done.6.refs_8_.refs_6_.refs_4_), channel_id=1, source_target_pairs={{0,1},{1,0},{2,3},{3,2},{4,5},{5,4},{6,7},{7,6},{8,9},{9,8},{10,11... | collective-permute-start | bytes 786440 | tf_op jit(solution)/shard_map/ppermute | solution.py:104
  97.4 6.4 %collective-permute-start.21 = (bf16[2,128,512]{2,1,0:T(8,128)(2,1)S(1)}, bf16[2,128,512]{2,1,0:T(8,128)(2,1)S(1)}, u32[]{:S(2)}, u32[]{:S(2)}) collective-permute-start(bf16[2,128,512]{2,1,0:T(8,128)(2,1)S(1)} %collective-permute-done.20.refs_15_.refs_13_), channel_id=1, source_target_pairs={{0,4},{5,1},{4,8},{9,5},{8,12},{13,9},{12,14},{15,13},{14,10},{11,... | collective-permute-start | bytes 786440 | tf_op jit(solution)/shard_map/ppermute | solution.py:103
  98.6 5.2 %collective-permute-start.28 = (bf16[2,128,512]{2,1,0:T(8,128)(2,1)S(1)}, bf16[2,128,512]{2,1,0:T(8,128)(2,1)S(1)}, u32[]{:S(2)}, u32[]{:S(2)}) collective-permute-start(bf16[2,128,512]{2,1,0:T(8,128)(2,1)S(1)} %collective-permute-done.7.refs_10_.refs_8_.refs_6_), channel_id=1, source_target_pairs={{0,1},{1,0},{2,3},{3,2},{4,5},{5,4},{6,7},{7,6},{8,9},{9,8},{10,11... | collective-permute-start | bytes 786440 | tf_op jit(solution)/shard_map/ppermute | solution.py:104
  98.7 5.6 %collective-permute-start.30 = (bf16[2,128,512]{2,1,0:T(8,128)(2,1)S(1)}, bf16[2,128,512]{2,1,0:T(8,128)(2,1)S(1)}, u32[]{:S(2)}, u32[]{:S(2)}) collective-permute-start(bf16[2,128,512]{2,1,0:T(8,128)(2,1)S(1)} %collective-permute-done.8.refs_12_.refs_10_.refs_8_), channel_id=1, source_target_pairs={{0,1},{1,0},{2,3},{3,2},{4,5},{5,4},{6,7},{7,6},{8,9},{9,8},{10,11... | collective-permute-start | bytes 786440 | tf_op jit(solution)/shard_map/ppermute | solution.py:104
  101.0 3.4 %collective-permute-start.32 = (bf16[2,128,512]{2,1,0:T(8,128)(2,1)S(1)}, bf16[2,128,512]{2,1,0:T(8,128)(2,1)S(1)}, u32[]{:S(2)}, u32[]{:S(2)}) collective-permute-start(bf16[2,128,512]{2,1,0:T(8,128)(2,1)S(1)} %collective-permute-done.9.refs_14_.refs_12_.refs_10_), channel_id=1, source_target_pairs={{0,1},{1,0},{2,3},{3,2},{4,5},{5,4},{6,7},{7,6},{8,9},{9,8},{10,11... | collective-permute-start | bytes 786440 | tf_op jit(solution)/shard_map/ppermute | solution.py:104
  103.1 7.5 %collective-permute-start.35 = (bf16[2,128,512]{2,1,0:T(8,128)(2,1)S(1)}, bf16[2,128,512]{2,1,0:T(8,128)(2,1)S(1)}, u32[]{:S(2)}, u32[]{:S(2)}) collective-permute-start(bf16[2,128,512]{2,1,0:T(8,128)(2,1)S(1)} %collective-permute-done.20.refs_15_.refs_13_), channel_id=1, source_target_pairs={{0,1},{1,0},{2,3},{3,2},{4,5},{5,4},{6,7},{7,6},{8,9},{9,8},{10,11... | collective-permute-start | bytes 786440 | tf_op jit(solution)/shard_map/ppermute | solution.py:104
  103.8 13.2 %collective-permute-start.37 = (bf16[2,128,512]{2,1,0:T(8,128)(2,1)S(1)}, bf16[2,128,512]{2,1,0:T(8,128)(2,1)S(1)}, u32[]{:S(2)}, u32[]{:S(2)}) collective-permute-start(bf16[2,128,512]{2,1,0:T(8,128)(2,1)S(1)} %collective-permute-done.21.refs_15_), channel_id=1, source_target_pairs={{0,1},{1,0},{2,3},{3,2},{4,5},{5,4},{6,7},{7,6},{8,9},{9,8},{10,11... | collective-permute-start | bytes 786440 | tf_op jit(solution)/shard_map/ppermute | solution.py:104
  103.8 6.8 %collective-permute-start.34 = (bf16[2,128,512]{2,1,0:T(8,128)(2,1)S(1)}, bf16[2,128,512]{2,1,0:T(8,128)(2,1)S(1)}, u32[]{:S(2)}, u32[]{:S(2)}) collective-permute-start(bf16[2,128,512]{2,1,0:T(8,128)(2,1)S(1)} %collective-permute-done.10.refs_14_.refs_12_), channel_id=1, source_target_pairs={{0,1},{1,0},{2,3},{3,2},{4,5},{5,4},{6,7},{7,6},{8,9},{9,8},{10,11... | collective-permute-start | bytes 786440 | tf_op jit(solution)/shard_map/ppermute | solution.py:104
  104.3 12.7 %collective-permute-start.36 = (bf16[2,128,512]{2,1,0:T(8,128)(2,1)S(1)}, bf16[2,128,512]{2,1,0:T(8,128)(2,1)S(1)}, u32[]{:S(2)}, u32[]{:S(2)}) collective-permute-start(bf16[2,128,512]{2,1,0:T(8,128)(2,1)S(1)} %collective-permute-done.11.refs_14_), channel_id=1, source_target_pairs={{0,1},{1,0},{2,3},{3,2},{4,5},{5,4},{6,7},{7,6},{8,9},{9,8},{10,11... | collective-permute-start | bytes 786440 | tf_op jit(solution)/shard_map/ppermute | solution.py:104
  (6 other events, 100.2 us)
